TPU v7x, 32 devices: a whole 2x2x4 slice. The times are simulated.
32 devices in a mesh: scan: 2 (over x), slab: 16 (over z, y, core).
Axes of the slice: x: 2, y: 2, z: 4, core: 2. Of those that a mesh axis runs over, the one named last changes fastest.
Arguments:
- sinogram: bfloat16 [1024, 8, 128], P(('scan', 'slab')), parts along dimension 0, may hold values from -144 to 144
- start_volume: float32 [512, 8, 128], P(('scan', 'slab')), parts along dimension 0, may hold values from -6 to 6
- slot_voxel: int32 [8192, 4], P(('scan', 'slab')), parts along dimension 0, may hold values from 0 to 15
- slot_ray: int32 [8192], P(('scan', 'slab')), parts along dimension 0, may hold values from 0 to 31
- live_count: int32 [512], P(('scan', 'slab')), parts along dimension 0, may hold values from 0 to 16, as said below
- block_slope: float32 [8192, 4], P(('scan', 'slab')), parts along dimension 0, may hold values from 0.8 to 1.25
- block_offset: float32 [8192, 4], P(('scan', 'slab')), parts along dimension 0, may hold values from -8 to 8
Outputs:
- recon_volume: float32 [512, 8, 128], P(('scan', 'slab')), parts along dimension 0
There are 2 independent parts, one for each index of `scan`. A program takes and returns all parts, laid end to end along the dimension named above; each array names one. Nothing has to cross between parts.
Inputs may be any that keep to these rules, and one draw needn't show every extreme that they name: `live_count`: every device's 16 slots to itself are all live.
All inputs are finite; a program needn't handle non-finite values.
Results may differ from a plain program's by a relative error of at most 0.0039.
Values may be sent and summed in bfloat16 or wider, within the bound.
No kernel may reach another device: no remote copies, remote signals or barrier semaphores. Data moves between devices by JAX's collectives and lax.ppermute only.
A program may use at most 64 MiB of HBM per device.

v0:
```python
import jax
import jax.numpy as jnp
from jax import lax
from jax.sharding import PartitionSpec as P

ITERS = 2


def footprint(slope_part, offset_part, alive, extent):
    position = jnp.arange(extent, dtype=jnp.float32)
    centre = offset_part[:, :, None] + slope_part[:, :, None] * position[None, None, :]
    distance = jnp.abs(position[None, None, :, None] - centre[:, :, None, :])
    weight = jnp.maximum(0.0, 1.0 - distance) * alive[:, None, None, None]
    return weight.astype(jnp.bfloat16)


def shards(sinogram, start_volume, slot_voxel, slot_ray, live_count, block_slope, block_offset):
    n_slab = lax.axis_size("slab")
    n_slots = slot_voxel.shape[0]
    depth = slot_voxel.shape[1]
    capacity = n_slots // n_slab
    ray_tiles = sinogram.shape[0]
    extent = sinogram.shape[2]
    voxel_tiles = start_volume.shape[0]
    highest = lax.Precision.HIGHEST
    alive = (
        (jnp.arange(capacity)[None, :] < live_count[:, None]).reshape(n_slots).astype(jnp.float32)
    )
    tiles = footprint(block_slope, block_offset, alive, extent)
    flat_voxel = slot_voxel.reshape(n_slots * depth)
    voxel_onehot = (flat_voxel[None, :] == jnp.arange(voxel_tiles)[:, None]).astype(jnp.float32)
    column_part = jnp.sum(tiles, axis=2, dtype=jnp.float32).reshape(n_slots * depth, extent)
    column_sum = jnp.dot(
        voxel_onehot, column_part, precision=highest, preferred_element_type=jnp.float32
    )
    column_weight = 1.0 / jnp.maximum(column_sum, 1.0)
    row_part = jnp.sum(tiles, axis=(1, 3), dtype=jnp.float32)
    got_rows, got_index = (
        lax.all_to_all(
            row_part.reshape(n_slab, capacity, extent),
            "slab",
            split_axis=0,
            concat_axis=0,
            tiled=True,
        ),
        lax.all_to_all(
            slot_ray.astype(jnp.float32).reshape(n_slab, capacity),
            "slab",
            split_axis=0,
            concat_axis=0,
            tiled=True,
        ),
    )
    ray_target = got_index.reshape(n_slots).astype(jnp.int32)
    ray_match = ray_target[None, :] == jnp.arange(ray_tiles)[:, None]
    ray_onehot = ray_match.astype(jnp.bfloat16)
    row_sum = jnp.dot(
        ray_match.astype(jnp.float32),
        got_rows.reshape(n_slots, extent),
        precision=highest,
        preferred_element_type=jnp.float32,
    )
    row_weight = 1.0 / jnp.maximum(row_sum, 1.0)
    volume = start_volume
    for sweep in range(ITERS):
        volume_bf = volume.astype(jnp.bfloat16)
        forward_count = volume_bf.shape[1]
        picked = jnp.take(volume_bf, slot_voxel, axis=0)
        forward_total = jnp.einsum(
            "sdrv,sdfv->sfr", tiles, picked, preferred_element_type=jnp.float32
        )
        terms = forward_total.astype(jnp.bfloat16).reshape(n_slab, capacity, forward_count, extent)
        received = lax.all_to_all(terms, "slab", split_axis=0, concat_axis=0, tiled=True)
        settle_count = received.shape[2]
        settle_flat = received.reshape(n_slots, settle_count * extent)
        projection = jnp.dot(ray_onehot, settle_flat, preferred_element_type=jnp.float32).reshape(
            ray_tiles, settle_count, extent
        )
        residual = ((sinogram.astype(jnp.float32) - projection) * row_weight[:, None, :]).astype(
            jnp.bfloat16
        )
        spread_back = jnp.dot(
            ray_onehot.T,
            residual.reshape(ray_tiles, settle_count * extent),
            preferred_element_type=jnp.float32,
        )
        outgoing = spread_back.astype(jnp.bfloat16).reshape(n_slab, capacity, settle_count, extent)
        returned = lax.all_to_all(outgoing, "slab", split_axis=0, concat_axis=0, tiled=True)
        count = returned.shape[2]
        flat = returned.reshape(n_slots, count, extent)
        contrib = jnp.einsum("sdrv,sfr->sdfv", tiles, flat, preferred_element_type=jnp.float32)
        total = jnp.dot(
            voxel_onehot,
            contrib.reshape(n_slots * depth, count * extent),
            precision=highest,
            preferred_element_type=jnp.float32,
        )
        back = total.reshape(voxel_tiles, count, extent)
        volume = volume + column_weight[:, None, :] * back
    return volume


def solution(mesh):
    in_specs = (
        P(("scan", "slab"), None, None),
        P(("scan", "slab"), None, None),
        P(("scan", "slab"), None),
        P(("scan", "slab")),
        P(("scan", "slab")),
        P(("scan", "slab"), None),
        P(("scan", "slab"), None),
    )
    out_specs = P(("scan", "slab"), None, None)
    return jax.shard_map(shards, mesh=mesh, in_specs=in_specs, out_specs=out_specs, check_vma=False)
```

profile of v0, /device:TPU:0, one launch (start us, length us, event | category | flops | bytes accessed | tf_op | source)
XLA Modules:
  0.0 205.9 jit_solution(1690295197460232932)
XLA Ops:
  0.0 0.7 convert_element_type.65
  0.7 0.7 all_to_all.21
  1.4 7.4 %all-to-all-start = ((f32[16,1,16]{2,1,0:T(1,128)}), f32[16,1,16]{2,1,0:T(1,128)S(1)}, u32[]{:S(2)}, u32[]{:S(2)}) async-start(f32[16,1,16]{2,1,0:T(1,128)} %all_to_all.21), calls=%async_computation | async-start | bytes 16384 | tf_op jit(solution)/shard_map/all_to_all | solution.py:46
  8.8 0.7 compare_select_fusion
  9.5 0.7 fusion.52
  10.5 0.8 copy.22
  11.4 0.8 copy.21
  12.2 0.6 multiply_add_fusion
  12.8 19.1 %convert_reduce_fusion.1 = (f32[256,4,128]{2,1,0:T(4,128)S(1)}, f32[256,128]{1,0:T(8,128)}) fusion(f32[256]{0:T(256)S(1)} %reshape.111, f32[256,4,128]{2,1,0:T(4,128)S(1)} %multiply_add_fusion), kind=kLoop, calls=%fused_computation.3 | loop fusion | flops 150831104 | bytes 1180672 | tf_op jit(solution)/shard_map/reduce_sum | solution.py:32
  31.9 0.7 compare_and_fusion
  32.8 0.8 convert_element_type.69
  33.6 3.3 %gather_fusion = bf16[1024,8,128]{2,1,0:T(8,128)(2,1)S(1)} fusion(bf16[16,8,128]{2,1,0:T(8,128)(2,1)S(1)} %convert_element_type.69, s32[1024]{0:T(1024)S(1)} %broadcast_clamp_fusion), kind=kCustom, calls=%fused_computation.clone | custom fusion | bytes 4198400 | tf_op jit(solution)/shard_map/jit(_take)/gather | solution.py:68
  37.0 6.0 %all-to-all-start.2 = ((f32[16,16,128]{2,1,0:T(8,128)}), f32[16,16,128]{2,1,0:T(8,128)S(1)}, u32[]{:S(2)}, u32[]{:S(2)}) async-start(f32[16,16,128]{2,1,0:T(8,128)} %bitcast.9), calls=%async_computation.2 | async-start | bytes 262144 | tf_op jit(solution)/shard_map/all_to_all | solution.py:39
  43.0 15.5 %fusion.17 = bf16[256,8,128]{2,1,0:T(8,128)(2,1)} fusion(f32[256]{0:T(256)S(1)} %reshape.111, f32[256,4,128]{2,1,0:T(4,128)S(1)} %multiply_add_fusion, bf16[256,4,8,128]{3,2,1,0:T(8,128)(2,1)S(1)} %bitcast.105, pred[256,4]{1,0:T(8,128)(4,1)S(1)} %copy.24), kind=kOutput, calls=%fused_computation.20 | convolution fusion | flops 370409472 | bytes 3147776 | tf_op jit(solution)/shard_map/sdrv,sdfv->sfr/dot_general | solution.py:69
  58.5 6.1 %all-to-all-start.1 = ((bf16[16,16,8,128]{3,2,1,0:T(8,128)(2,1)}), bf16[16,16,8,128]{3,2,1,0:T(8,128)(2,1)S(1)}, u32[]{:S(2)}, u32[]{:S(2)}) async-start(bf16[16,16,8,128]{3,2,1,0:T(8,128)(2,1)} %bitcast.115), calls=%async_computation.1 | async-start | bytes 1048576 | tf_op jit(solution)/shard_map/all_to_all | solution.py:73
  64.9 14.2 %all-to-all-done.1 = bf16[16,16,8,128]{3,2,1,0:T(8,128)(2,1)S(1)} async-done(((bf16[16,16,8,128]{3,2,1,0:T(8,128)(2,1)}), bf16[16,16,8,128]{3,2,1,0:T(8,128)(2,1)S(1)}, u32[]{:S(2)}, u32[]{:S(2)}) %all-to-all-start.1) | async-done | bytes 524320 | tf_op jit(solution)/shard_map/all_to_all | solution.py:73
  80.0 0.9 copy.44
  80.9 4.1 %all-to-all-start.3 = ((bf16[16,16,8,128]{3,2,1,0:T(8,128)(2,1)}), bf16[16,16,8,128]{3,2,1,0:T(8,128)(2,1)S(1)}, u32[]{:S(2)}, u32[]{:S(2)}) async-start(bf16[16,16,8,128]{3,2,1,0:T(8,128)(2,1)} %bitcast.44), calls=%async_computation.3 | async-start | bytes 1048576 | tf_op jit(solution)/shard_map/all_to_all | solution.py:88
  85.6 13.9 %all-to-all-done.3 = bf16[16,16,8,128]{3,2,1,0:T(8,128)(2,1)S(1)} async-done(((bf16[16,16,8,128]{3,2,1,0:T(8,128)(2,1)}), bf16[16,16,8,128]{3,2,1,0:T(8,128)(2,1)S(1)}, u32[]{:S(2)}, u32[]{:S(2)}) %all-to-all-start.3) | async-done | bytes 524320 | tf_op jit(solution)/shard_map/all_to_all | solution.py:88
  99.5 12.4 %fusion.2 = f32[256,8,4,128]{3,1,2,0:T(8,128)S(1)} fusion(bf16[256,8,128,1]{2,1,3,0:T(8,128)(2,1)S(1)} %bitcast.116, f32[256]{0:T(256)S(1)} %reshape.111, f32[256,4,128]{2,1,0:T(4,128)S(1)} %multiply_add_fusion), kind=kOutput, calls=%fused_computation.7 | convolution fusion | flops 369098752 | bytes 5243904 | tf_op jit(solution)/shard_map/sdrv,sfr->sdfv/dot_general | solution.py:91
  111.9 2.9 %copy.65 = f32[128,8,8,128]{3,1,2,0:T(8,128)} copy(f32[128,8,8,128]{3,2,1,0:T(8,128)S(1)} %bitcast.104) | data formatting | bytes 8388608
  114.9 5.4 %copy.28 = f32[1024,1024]{1,0:T(8,128)} copy(f32[1024,1024]{0,1:T(8,128)} %bitcast.101) | data formatting | bytes 8388608 | tf_op jit(solution)/shard_map/dot_general | solution.py:92
  120.3 4.2 %fusion.63 = (bf16[16,8,128]{2,0,1:T(8,128)(2,1)S(1)}, f32[16,8,128]{2,0,1:T(8,128)S(1)}) fusion(f32[8,128,1024]{2,1,0:T(8,128)} %bitcast.100, s32[1024]{0:T(1024)S(1)} %eq.28, f32[16,128]{1,0:T(8,128)S(1)} %fusion.31, f32[16,8,128]{2,1,0:T(8,128)S(1)} %copy-done), kind=kOutput, calls=%fused_computation.76 | convolution fusion | flops 201392128 | bytes 4370432 | tf_op jit(solution)/shard_map/dot_general | solution.py:92
  124.5 3.3 %gather_fusion.1 = bf16[1024,8,128]{2,1,0:T(8,128)(2,1)S(1)} fusion(bf16[16,8,128]{2,1,0:T(8,128)(2,1)S(1)} %copy.32, s32[1024]{0:T(1024)S(1)} %broadcast_clamp_fusion), kind=kCustom, calls=%fused_computation.1.clone | custom fusion | bytes 4198400 | tf_op jit(solution)/shard_map/jit(_take)/gather | solution.py:68
  127.8 14.8 %fusion.14 = bf16[256,8,128]{2,1,0:T(8,128)(2,1)S(1)} fusion(f32[256]{0:T(256)S(1)} %reshape.111, f32[256,4,128]{2,1,0:T(4,128)S(1)} %multiply_add_fusion, bf16[256,4,8,128]{3,2,1,0:T(8,128)(2,1)S(1)} %bitcast.106, pred[256,4]{1,0:T(8,128)(4,1)S(1)} %copy.24), kind=kOutput, calls=%fused_computation.19 | convolution fusion | flops 370409472 | bytes 3147776 | tf_op jit(solution)/shard_map/sdrv,sdfv->sfr/dot_general | solution.py:69
  142.6 18.4 %all_to_all.34 = bf16[16,16,8,128]{3,2,1,0:T(8,128)(2,1)S(1)} all-to-all(bf16[16,16,8,128]{3,2,1,0:T(8,128)(2,1)S(1)} %bitcast.118), channel_id=1, replica_groups=mesh['scan'=2,'slab'=16] {'slab'}, dimensions={0} | all-to-all | bytes 1048576 | tf_op jit(solution)/shard_map/all_to_all | solution.py:73
  162.0 18.4 %all_to_all.35 = bf16[16,16,8,128]{3,2,1,0:T(8,128)(2,1)S(1)} all-to-all(bf16[16,16,8,128]{3,2,1,0:T(8,128)(2,1)S(1)} %bitcast.114), channel_id=1, replica_groups=mesh['scan'=2,'slab'=16] {'slab'}, dimensions={0} | all-to-all | bytes 1048576 | tf_op jit(solution)/shard_map/all_to_all | solution.py:88
  180.3 12.4 %fusion = f32[256,8,4,128]{3,1,2,0:T(8,128)S(1)} fusion(bf16[256,8,128,1]{2,1,3,0:T(8,128)(2,1)S(1)} %bitcast.117, f32[256]{0:T(256)S(1)} %reshape.111, f32[256,4,128]{2,1,0:T(4,128)S(1)} %multiply_add_fusion), kind=kOutput, calls=%fused_computation.5 | convolution fusion | flops 369098752 | bytes 5243904 | tf_op jit(solution)/shard_map/sdrv,sfr->sdfv/dot_general | solution.py:91
  192.8 2.9 %copy.64 = f32[128,8,8,128]{3,1,2,0:T(8,128)} copy(f32[128,8,8,128]{3,2,1,0:T(8,128)S(1)} %bitcast.103) | data formatting | bytes 8388608
  195.7 5.4 %copy.35 = f32[1024,1024]{1,0:T(8,128)} copy(f32[1024,1024]{0,1:T(8,128)} %bitcast.102) | data formatting | bytes 8388608 | tf_op jit(solution)/shard_map/dot_general | solution.py:92
  201.1 4.2 %fusion.29 = f32[16,8,128]{2,0,1:T(8,128)S(1)} fusion(f32[16,8,128]{2,0,1:T(8,128)S(1)} %get-tuple-element.9, f32[8,128,1024]{2,1,0:T(8,128)} %bitcast.99, f32[16,128]{1,0:T(8,128)S(1)} %fusion.31, s32[1024]{0:T(1024)S(1)} %eq.28), kind=kOutput, calls=%fused_computation.34 | convolution fusion | flops 201375744 | bytes 4337664 | tf_op jit(solution)/shard_map/dot_general | solution.py:92
  205.3 0.7 copy.36
  (29 shorter events, 3.3 us)
Async XLA Ops:
  1.4 35.6 %all-to-all-start = ((f32[16,1,16]{2,1,0:T(1,128)}), f32[16,1,16]{2,1,0:T(1,128)S(1)}, u32[]{:S(2)}, u32[]{:S(2)}) async-start(f32[16,1,16]{2,1,0:T(1,128)} %all_to_all.21), calls=%async_computation | async-start | bytes 16384 | tf_op jit(solution)/shard_map/all_to_all | solution.py:46
  37.0 21.5 %all-to-all-start.2 = ((f32[16,16,128]{2,1,0:T(8,128)}), f32[16,16,128]{2,1,0:T(8,128)S(1)}, u32[]{:S(2)}, u32[]{:S(2)}) async-start(f32[16,16,128]{2,1,0:T(8,128)} %bitcast.9), calls=%async_computation.2 | async-start | bytes 262144 | tf_op jit(solution)/shard_map/all_to_all | solution.py:39
  43.0 36.4 %copy-start.1 = (bf16[32,8,128]{2,1,0:T(8,128)(2,1)S(1)}, bf16[32,8,128]{2,1,0:T(8,128)(2,1)}, u32[]{:S(2)}) copy-start(bf16[32,8,128]{2,1,0:T(8,128)(2,1)} %param.9) | copy-start | bytes 196612
  58.5 26.6 %copy-start.2 = (s32[256,4]{0,1:T(4,128)S(1)}, s32[256,4]{0,1:T(4,128)}, u32[]{:S(2)}) copy-start(s32[256,4]{0,1:T(4,128)} %param.11) | copy-start | bytes 12292
  58.5 20.6 %all-to-all-start.1 = ((bf16[16,16,8,128]{3,2,1,0:T(8,128)(2,1)}), bf16[16,16,8,128]{3,2,1,0:T(8,128)(2,1)S(1)}, u32[]{:S(2)}, u32[]{:S(2)}) async-start(bf16[16,16,8,128]{3,2,1,0:T(8,128)(2,1)} %bitcast.115), calls=%async_computation.1 | async-start | bytes 1048576 | tf_op jit(solution)/shard_map/all_to_all | solution.py:73
  80.9 18.6 %all-to-all-start.3 = ((bf16[16,16,8,128]{3,2,1,0:T(8,128)(2,1)}), bf16[16,16,8,128]{3,2,1,0:T(8,128)(2,1)S(1)}, u32[]{:S(2)}, u32[]{:S(2)}) async-start(bf16[16,16,8,128]{3,2,1,0:T(8,128)(2,1)} %bitcast.44), calls=%async_computation.3 | async-start | bytes 1048576 | tf_op jit(solution)/shard_map/all_to_all | solution.py:88
  114.9 5.4 %copy-start = (f32[16,8,128]{2,1,0:T(8,128)S(1)}, f32[16,8,128]{2,1,0:T(8,128)}, u32[]{:S(2)}) copy-start(f32[16,8,128]{2,1,0:T(8,128)} %param.10) | copy-start | bytes 196612
where the time goes:
time: 207 us; the launch traced here: 206 us
  matrix products  65.1 us (31%)
  blocking collectives  36.7 us (18%)
  local copies, waits for them, and re-layouts  28.7 us (14%)
  waiting for transfers between devices  28.1 us (14%)
  starting transfers between devices  23.7 us (11%)
  other arithmetic  23.4 us (11%)
    dot_general x2, matrix products, shards(): jnp.einsum('sdrv,sdfv->sfr', tiles, picked, preferred_element_type=jnp.fl...  30.3 us
    dot_general x2, matrix products, shards(): jnp.einsum('sdrv,sfr->sdfv', tiles, flat, preferred_element_type=jnp.floa...  24.9 us
    reduce_sum x1, other arithmetic, shards(): jnp.sum(tiles, axis=2, dtype=jnp.float32).reshape(n_slots * depth, extent)  19.1 us
    all_to_all x1, blocking collectives, shards(): lax.all_to_all(outgoing, 'slab', split_axis=0, concat_axis=0, tiled=True)  18.4 us
    all_to_all x1, blocking collectives, shards(): lax.all_to_all(terms, 'slab', split_axis=0, concat_axis=0, tiled=True)  18.4 us
    all_to_all x1, waiting for transfers between devices, shards(): lax.all_to_all(terms, 'slab', split_axis=0, concat_axis=0, tiled=True)  14.2 us
    all_to_all x1, waiting for transfers between devices, shards(): lax.all_to_all(outgoing, 'slab', split_axis=0, concat_axis=0, tiled=True)  13.9 us
    dot_general x2, local copies, waits for them, and re-layouts, shards(): jnp.dot(voxel_onehot, contrib.reshape(n_slots * depth, count * extent), p...  10.8 us
  transfers between devices with their start and end apart: 4, of which 2 were waited for; matrix products, arithmetic and copies ran while one was open for 22% of the time, Pallas kernels for 0%

commit v1 on v0

v1 whole, which is shorter than its diff:
```python
import functools

import jax
import jax.numpy as jnp
from jax import lax
from jax.experimental import pallas as pl
from jax.experimental.pallas import tpu as pltpu
from jax.sharding import PartitionSpec as P

ITERS = 2
FAR = 1.0e6
PARAMS = pltpu.CompilerParams(vmem_limit_bytes=48 * 1024 * 1024)
VMEM = pl.BlockSpec(memory_space=pltpu.VMEM)
SMEM = pl.BlockSpec(memory_space=pltpu.SMEM)


def hat(ray, offset, slope, voxel):
    return jnp.maximum(0.0, 1.0 - jnp.abs(ray - (offset + slope * voxel))).astype(jnp.bfloat16)


def row_taps(offset, slope, extent):
    shape = (offset.shape[0], extent)
    ray = lax.broadcasted_iota(jnp.int32, shape, 1).astype(jnp.float32)
    offset = jnp.broadcast_to(offset, shape)
    slope = jnp.broadcast_to(slope, shape)
    middle = jnp.floor((ray - offset) / slope + 0.5)
    middle = jnp.minimum(jnp.maximum(middle, 1.0), extent - 2.0)
    weights = [hat(ray, offset, slope, middle + step) for step in (-1.0, 0.0, 1.0)]
    return middle.astype(jnp.int32), weights


def column_taps(offset, slope, extent):
    shape = (offset.shape[0], extent)
    voxel = lax.broadcasted_iota(jnp.int32, shape, 1).astype(jnp.float32)
    centre = jnp.broadcast_to(offset, shape) + jnp.broadcast_to(slope, shape) * voxel
    first = jnp.minimum(jnp.maximum(jnp.floor(centre), 0.0), extent - 2.0)
    weights = [
        jnp.maximum(0.0, 1.0 - jnp.abs(first + step - centre)).astype(jnp.bfloat16)
        for step in (0.0, 1.0)
    ]
    return first.astype(jnp.int32), weights


def target_setup(fields, n_slab, group, capacity, extent, frames, got_ref, index_ref, *rest):
    weight_refs, row_ref = rest[:3], rest[3]
    columns = got_ref[...].T
    ray_tiles = row_ref.shape[0] // frames
    total = jnp.zeros((ray_tiles, extent), jnp.float32)
    depth = group // capacity
    for source in range(n_slab):
        offset = columns[0:group, source:source + 1]
        slope = columns[group:2 * group, source:source + 1]
        middle, weights = row_taps(offset, slope, extent)
        rows = pl.ds(source * group, group)
        index_ref[rows, :] = middle
        for ref, weight in zip(weight_refs, weights):
            ref[rows, :] = weight.astype(jnp.float32)
        summed = sum(weight.astype(jnp.float32) for weight in weights)
        tile_of = jnp.broadcast_to(
            got_ref[source:source + 1, 4 * group:5 * group], (ray_tiles, group))
        match = tile_of == lax.broadcasted_iota(
            jnp.int32, (ray_tiles, group), 0).astype(jnp.float32)
        hot = match.astype(jnp.float32)
        total += jnp.dot(hot, summed, precision=lax.Precision.HIGHEST,
                         preferred_element_type=jnp.float32)
    weight = 1.0 / jnp.maximum(total, 1.0)
    for tile in range(ray_tiles):
        row_ref[tile * frames:(tile + 1) * frames, :] = jnp.broadcast_to(
            weight[tile:tile + 1, :], (frames, extent))


def source_setup(extent, frames, offset_ref, slope_ref, voxel_ref, index_ref, first_ref, second_ref,
                 column_ref):
    offsets = offset_ref[...].T
    slopes = slope_ref[...].T
    voxel_tiles = column_ref.shape[0] // frames
    total = jnp.zeros((voxel_tiles, extent), jnp.float32)
    for part in range(offset_ref.shape[0]):
        first, weights = column_taps(offsets[:, part:part + 1], slopes[:, part:part + 1], extent)
        rows = pl.ds(part * extent, extent)
        index_ref[rows, :] = first
        first_ref[rows, :] = weights[0].astype(jnp.float32)
        second_ref[rows, :] = weights[1].astype(jnp.float32)
        summed = weights[0].astype(jnp.float32) + weights[1].astype(jnp.float32)
        tile_of = jnp.broadcast_to(voxel_ref[part:part + 1, :], (voxel_tiles, extent))
        hot = (tile_of == lax.broadcasted_iota(jnp.int32, (voxel_tiles, extent), 0)).astype(jnp.float32)
        total += jnp.dot(hot, summed, precision=lax.Precision.HIGHEST,
                         preferred_element_type=jnp.float32)
    weight = 1.0 / jnp.maximum(total, 1.0)
    for tile in range(voxel_tiles):
        column_ref[tile * frames:(tile + 1) * frames, :] = jnp.broadcast_to(
            weight[tile:tile + 1, :], (frames, extent))


def pick(values, index):
    return jnp.take_along_axis(values, index, axis=1, mode="promise_in_bounds")


def spread(ref, row, frames):
    return jnp.broadcast_to(ref[pl.ds(row, 1), :], (frames, ref.shape[1]))


def forward_kernel(n_slab, group, capacity, tiles, frames, chunk,
                   meta_ref, volume_ref, sinogram_ref, row_ref, index_ref, w0_ref, w1_ref, w2_ref,
                   out_ref, wide, projection):
    depth = group // capacity
    wide[...] = volume_ref[...].astype(jnp.float32)
    projection[...] = jnp.zeros_like(projection)

    def from_source(source, carry):
        count = meta_ref[source, 2 * group + capacity]

        def some(step, carry):
            for place in range(chunk):
                slot = step * chunk + place
                total = None
                for level in range(depth):
                    block = slot * depth + level
                    voxel = source * tiles + meta_ref[source, group + block]
                    row = source * group + block
                    values = wide[pl.ds(pl.multiple_of(voxel * frames, frames), frames), :]
                    index = spread(index_ref, row, frames)
                    for ref, shift in ((w0_ref, -1), (w1_ref, 0), (w2_ref, 1)):
                        term = spread(ref, row, frames) * pick(values, index + shift)
                        total = term if total is None else total + term
                ray = meta_ref[source, 2 * group + slot]
                at = pl.ds(pl.multiple_of(ray * frames, frames), frames)
                projection[at, :] += total.astype(jnp.bfloat16).astype(jnp.float32)
            return carry

        return lax.fori_loop(0, lax.div(count + (chunk - 1), chunk), some, carry)

    lax.fori_loop(0, n_slab, from_source, 0)
    residual = (sinogram_ref[...].astype(jnp.float32) - projection[...]) * row_ref[...]
    out_ref[...] = residual.astype(jnp.bfloat16)


def backward_kernel(n_slab, group, capacity, tiles, frames, chunk,
                    count_ref, voxel_ref, ray_ref, residual_ref, volume_ref, column_ref, index_ref,
                    w0_ref, w1_ref, out_ref, rounded_ref, wide, *banks):
    depth = group // capacity
    wide[...] = residual_ref[...].astype(jnp.float32)
    for bank in banks:
        bank[...] = jnp.zeros_like(bank)

    def to_target(target, carry):
        count = count_ref[target]

        def some(step, carry):
            for place in range(chunk):
                slot = target * capacity + step * chunk + place
                ray = target * tiles + ray_ref[slot]
                values = wide[pl.ds(pl.multiple_of(ray * frames, frames), frames), :]
                for level in range(depth):
                    row = slot * depth + level
                    index = spread(index_ref, row, frames)
                    term = (spread(w0_ref, row, frames) * pick(values, index)
                            + spread(w1_ref, row, frames) * pick(values, index + 1))
                    at = pl.ds(pl.multiple_of(voxel_ref[row] * frames, frames), frames)
                    banks[level][at, :] += term
            return carry

        return lax.fori_loop(0, lax.div(count + (chunk - 1), chunk), some, carry)

    lax.fori_loop(0, n_slab, to_target, 0)
    back = banks[0][...]
    for bank in banks[1:]:
        back = back + bank[...]
    volume = volume_ref[...] + column_ref[...] * back
    out_ref[...] = volume
    rounded_ref[...] = volume.astype(jnp.bfloat16)


def shards(sinogram, start_volume, slot_voxel, slot_ray, live_count, block_slope, block_offset):
    n_slab = lax.axis_size("slab")
    n_slots, depth = slot_voxel.shape
    capacity = n_slots // n_slab
    group = capacity * depth
    ray_tiles, frames, extent = sinogram.shape
    voxel_tiles = start_volume.shape[0]
    blocks = n_slots * depth
    chunk = min(4, capacity)
    f32, bf16 = jnp.float32, jnp.bfloat16
    shape = jax.ShapeDtypeStruct

    volume = start_volume.reshape(voxel_tiles * frames, extent)
    gathered = lax.all_gather(volume.astype(bf16), "slab", axis=0, tiled=True)

    alive = (jnp.arange(capacity)[None, :] < live_count[:, None]).reshape(n_slots, 1)
    offset = jnp.where(alive, block_offset, FAR)
    width = -(-(5 * group + capacity + 1) // extent) * extent
    used = 5 * group + capacity + 1
    packed = jnp.concatenate(
        [
            offset.reshape(n_slab, group),
            block_slope.reshape(n_slab, group),
            slot_voxel.astype(f32).reshape(n_slab, group),
            jnp.zeros((n_slab, group), f32),
            jnp.repeat(slot_ray.astype(f32), depth).reshape(n_slab, group),
            slot_ray.astype(f32).reshape(n_slab, capacity),
            live_count.astype(f32).reshape(n_slab, 1),
            jnp.zeros((n_slab, width - used), f32),
        ],
        axis=1,
    )
    got = lax.all_to_all(packed, "slab", split_axis=0, concat_axis=0, tiled=True)
    meta = jnp.concatenate(
        [got[:, 4 * group:5 * group], got[:, 2 * group:3 * group], got[:, 5 * group:used]], axis=1
    ).astype(jnp.int32)

    fwd_index, fwd0, fwd1, fwd2, row_weight = pl.pallas_call(
        functools.partial(target_setup, None, n_slab, group, capacity, extent, frames),
        out_shape=[shape((blocks, extent), jnp.int32)] + [shape((blocks, extent), f32)] * 3
        + [shape((ray_tiles * frames, extent), f32)],
        in_specs=[VMEM],
        out_specs=[VMEM] * 5,
        compiler_params=PARAMS,
        name="target_setup",
    )(got)
    meta = meta[:, :]

    voxel_flat = slot_voxel.reshape(blocks)
    bwd_index, bwd0, bwd1, column_weight = pl.pallas_call(
        functools.partial(source_setup, extent, frames),
        out_shape=[shape((blocks, extent), jnp.int32)] + [shape((blocks, extent), f32)] * 2
        + [shape((voxel_tiles * frames, extent), f32)],
        in_specs=[VMEM] * 3,
        out_specs=[VMEM] * 4,
        compiler_params=PARAMS,
        name="source_setup",
    )(
        offset.reshape(blocks // extent, extent),
        block_slope.reshape(blocks // extent, extent),
        voxel_flat.reshape(blocks // extent, extent),
    )

    forward = pl.pallas_call(
        functools.partial(forward_kernel, n_slab, group, capacity, voxel_tiles, frames, chunk),
        out_shape=shape((ray_tiles * frames, extent), bf16),
        in_specs=[SMEM] + [VMEM] * 7,
        out_specs=VMEM,
        scratch_shapes=[
            pltpu.VMEM((n_slab * voxel_tiles * frames, extent), f32),
            pltpu.VMEM((ray_tiles * frames, extent), f32),
        ],
        compiler_params=PARAMS,
        name="forward",
    )
    backward = pl.pallas_call(
        functools.partial(backward_kernel, n_slab, group, capacity, ray_tiles, frames, chunk),
        out_shape=[shape(volume.shape, f32), shape(volume.shape, bf16)],
        in_specs=[SMEM] * 3 + [VMEM] * 6,
        out_specs=[VMEM] * 2,
        scratch_shapes=[pltpu.VMEM((n_slab * ray_tiles * frames, extent), f32)]
        + [pltpu.VMEM(volume.shape, f32)] * depth,
        compiler_params=PARAMS,
        name="backward",
    )
    sino = sinogram.reshape(ray_tiles * frames, extent)
    for sweep in range(ITERS):
        residual = forward(meta, gathered, sino, row_weight, fwd_index, fwd0, fwd1, fwd2)
        spread_out = lax.all_gather(residual, "slab", axis=0, tiled=True)
        volume, rounded = backward(
            live_count, voxel_flat, slot_ray, spread_out, volume, column_weight, bwd_index, bwd0, bwd1
        )
        if sweep + 1 < ITERS:
            gathered = lax.all_gather(rounded, "slab", axis=0, tiled=True)
    return volume.reshape(start_volume.shape)


def solution(mesh):
    in_specs = (
        P(("scan", "slab"), None, None),
        P(("scan", "slab"), None, None),
        P(("scan", "slab"), None),
        P(("scan", "slab")),
        P(("scan", "slab")),
        P(("scan", "slab"), None),
        P(("scan", "slab"), None),
    )
    out_specs = P(("scan", "slab"), None, None)
    return jax.shard_map(shards, mesh=mesh, in_specs=in_specs, out_specs=out_specs, check_vma=False)
```

time: 207 us -> 183 us (0.88)
  matrix products: 65.1 us -> 0 us
  Pallas kernels: 0 us -> 38.4 us
  waiting for transfers between devices: 28.1 us -> 65.9 us
  other arithmetic: 23.4 us -> 0.9 us
  local copies, waits for them, and re-layouts: 28.7 us -> 11 us
  starting transfers between devices: 23.7 us -> 7.47 us
  between operations: 0.26 us -> 13.6 us
  blocking collectives: 36.7 us -> 46.1 us
    all_gather x0 -> x2, waiting for transfers between devices: none -> 65.9 us  [shards(): spread_out = lax.all_gather(residual, 'slab', axis=0, tiled=True)]
    dot_general x12 -> x0, matrix products: 65.1 us -> none  [the longest x2 30.3 us: shards(): jnp.einsum('sdrv,sdfv->sfr', tiles, picked, preferred_element_type=jnp.fl...]
    all_gather x0 -> x2, blocking collectives: none -> 46.1 us  [the longest x1 23.3 us: shards(): gathered = lax.all_gather(volume.astype(bf16), 'slab', axis=0, tiled=True)]
    pallas_call x0 -> x6, Pallas kernels: none -> 38.4 us  [the longest x2 22.7 us: shards(): forward(meta, gathered, sino, row_weight, fwd_index, fwd0, fwd1, fwd2)]
    all_to_all x2 -> x0, blocking collectives: 36.7 us -> none  [the longest x1 18.4 us: shards(): lax.all_to_all(outgoing, 'slab', split_axis=0, concat_axis=0, tiled=True)]
    all_to_all x4 -> x1, waiting for transfers between devices: 28.1 us -> 0.01 us  [shards(): lax.all_to_all(packed, 'slab', split_axis=0, concat_axis=0, tiled=True)]
    reduce_sum x1 -> x0, other arithmetic: 19.1 us -> none  [shards(): jnp.sum(tiles, axis=2, dtype=jnp.float32).reshape(n_slots * depth, extent)]
    all_to_all x4 -> x1, starting transfers between devices: 23.7 us -> 7.39 us  [shards(): lax.all_to_all(packed, 'slab', split_axis=0, concat_axis=0, tiled=True)]
  transfers between devices with their start and end apart: 4 -> 3, of which waited for: 2 -> 2; matrix products, arithmetic and copies ran while one was open for 22% -> 1% of each run, Pallas kernels for 0% -> 0%
where the time goes in v1:
time: 183 us
  waiting for transfers between devices  65.9 us (36%)
  blocking collectives  46.1 us (25%)
  Pallas kernels  38.4 us (21%)
  between operations  13.6 us (7%)
  local copies, waits for them, and re-layouts  11 us (6%)
  starting transfers between devices  7.47 us (4%)
    all_gather x2, waiting for transfers between devices, shards(): spread_out = lax.all_gather(residual, 'slab', axis=0, tiled=True)  65.9 us
    all_gather x1, blocking collectives, shards(): gathered = lax.all_gather(volume.astype(bf16), 'slab', axis=0, tiled=True)  23.3 us
    all_gather x1, blocking collectives, shards(): gathered = lax.all_gather(rounded, 'slab', axis=0, tiled=True)  22.8 us
    pallas_call x2, Pallas kernels, shards(): forward(meta, gathered, sino, row_weight, fwd_index, fwd0, fwd1, fwd2)  22.7 us
    pallas_call x2, Pallas kernels, shards(): backward(live_count, voxel_flat, slot_ray, spread_out, volume, column_wei...  13.7 us
    unnamed x39, local copies, waits for them, and re-layouts  8.13 us
    all_to_all x1, starting transfers between devices, shards(): lax.all_to_all(packed, 'slab', split_axis=0, concat_axis=0, tiled=True)  7.39 us
  transfers between devices with their start and end apart: 3, of which 2 were waited for; matrix products, arithmetic and copies ran while one was open for 1% of the time, Pallas kernels for 0%

profile of v1, /device:TPU:0, one launch (start us, length us, event | category | flops | bytes accessed | tf_op | source)
XLA Modules:
  0.0 183.4 jit_solution(9195849185829600828)
XLA Ops:
  6.5 0.7 convert_bitcast_fusion
  7.3 0.6 copy-done.9
  8.4 0.6 copy-done.17
  9.0 0.1 copy.26
  9.1 0.1 reshape.52
  9.2 0.1 copy.28
  9.5 0.6 copy-done.16
  10.1 0.1 copy.27
  10.2 0.1 reshape.53
  10.5 0.6 copy.32
  11.1 7.4 %all-to-all-start = ((f32[16,1,384]{2,1,0:T(1,128)}), f32[16,1,384]{2,1,0:T(1,128)S(1)}, u32[]{:S(2)}, u32[]{:S(2)}) async-start(f32[16,1,384]{2,1,0:T(1,128)} %copy.32), calls=%async_computation | async-start | bytes 49152 | tf_op jit(solution)/shard_map/all_to_all | solution.py:206
  18.6 23.3 %all_gather.12.volume_ref = bf16[2048,128]{1,0:T(8,128)(2,1)S(1)} all-gather(bf16[128,128]{1,0:T(8,128)(2,1)S(1)} %bitcast_convert_fusion), channel_id=1, replica_groups=mesh['scan'=2,'slab'=16] {'slab'}, dimensions={0}, use_global_device_ids=true | all-gather | bytes 557056 | tf_op jit(solution)/shard_map/all_gather | solution.py:187
  41.9 1.2 target_setup.1
  43.2 11.3 %forward.2 = bf16[256,128]{1,0:T(8,128)(2,1)} custom-call(s32[16,145]{1,0:T(8,128)S(1)} %maximum_convert_fusion.meta_ref, bf16[2048,128]{1,0:T(8,128)(2,1)S(1)} %all_gather.12.volume_ref, bf16[256,128]{1,0:T(8,128)(2,1)S(1)} %bitcast.11, f32[256,128]{1,0:T(8,128)S(1)} %get-tuple-element.17.row_ref, s32[1024,128]{1,0:T(8,128)S(1)} %get-tuple-element.18.index_ref, ...), custom_call_target="tpu_custom_call" | custom-call | tf_op jit(solution)/shard_map/forward/pallas_call | solution.py:261
  54.6 0.1 reshape.58.offset_ref
  54.7 0.1 reshape.59.slope_ref
  54.8 0.1 copy.25
  55.0 0.7 reshape.51.voxel_ref
  55.7 0.1 reshape_reshape.4.voxel_ref
  55.8 0.9 source_setup.1
  56.7 0.8 copy-done
  57.5 31.1 %all-gather.3.cloned.1.call-done.residual_ref = bf16[4096,128]{1,0:T(8,128)(2,1)} async-done(((bf16[256,128]{1,0:T(8,128)(2,1)}), bf16[4096,128]{1,0:T(8,128)(2,1)}) %all-gather.3.cloned.1.call-update) | async-done | bytes 1048592 | tf_op jit(solution)/shard_map/all_gather | solution.py:262
  88.6 0.7 copy-done.7
  89.3 1.0 copy-done.1
  90.3 1.2 copy-done.3
  91.5 6.5 %backward.2 = (f32[128,128]{1,0:T(8,128)S(1)}, bf16[128,128]{1,0:T(8,128)(2,1)S(1)}) custom-call(s32[16]{0:T(128)S(1)} %copy-done.13, s32[1024]{0:T(1024)S(1)} %copy-done.7, s32[256]{0:T(256)S(1)} %copy-done.10, bf16[4096,128]{1,0:T(8,128)(2,1)S(1)} %copy-done.3, f32[128,128]{1,0:T(8,128)S(1)} %bitcast.13, f32[128,128]{1,0:T(8,128)S(1)} %get-tuple-element.22.column_ref, ...), custom_call_target="tpu_custom_call" | custom-call | tf_op jit(solution)/shard_map/backward/pallas_call | solution.py:263
  98.1 22.8 %all_gather.14.volume_ref = bf16[2048,128]{1,0:T(8,128)(2,1)S(1)} all-gather(bf16[128,128]{1,0:T(8,128)(2,1)S(1)} %get-tuple-element.26), channel_id=1, replica_groups=mesh['scan'=2,'slab'=16] {'slab'}, dimensions={0}, use_global_device_ids=true | all-gather | bytes 557056 | tf_op jit(solution)/shard_map/all_gather | solution.py:267
  120.9 11.3 %forward.3 = bf16[256,128]{1,0:T(8,128)(2,1)} custom-call(s32[16,145]{1,0:T(8,128)S(1)} %maximum_convert_fusion.meta_ref, bf16[2048,128]{1,0:T(8,128)(2,1)S(1)} %all_gather.14.volume_ref, bf16[256,128]{1,0:T(8,128)(2,1)S(1)} %bitcast.12, f32[256,128]{1,0:T(8,128)S(1)} %get-tuple-element.17.row_ref, s32[1024,128]{1,0:T(8,128)S(1)} %get-tuple-element.18.index_ref, ...), custom_call_target="tpu_custom_call" | custom-call | tf_op jit(solution)/shard_map/forward/pallas_call | solution.py:261
  132.3 34.8 %all-gather.5.cloned.1.call-done.residual_ref = bf16[4096,128]{1,0:T(8,128)(2,1)} async-done(((bf16[256,128]{1,0:T(8,128)(2,1)}), bf16[4096,128]{1,0:T(8,128)(2,1)}) %all-gather.5.cloned.1.call-update) | async-done | bytes 1048592 | tf_op jit(solution)/shard_map/all_gather | solution.py:262
  167.1 1.0 copy-done.2
  168.2 1.2 copy-done.4
  169.4 7.2 %backward.3 = (f32[128,128]{1,0:T(8,128)}, bf16[128,128]{1,0:T(8,128)(2,1)}) custom-call(s32[16]{0:T(128)S(1)} %copy-done.14, s32[1024]{0:T(1024)S(1)} %copy-done.8, s32[256]{0:T(256)S(1)} %copy-done.11, bf16[4096,128]{1,0:T(8,128)(2,1)S(1)} %copy-done.4, f32[128,128]{1,0:T(8,128)S(1)} %get-tuple-element.27.volume_ref, ...), custom_call_target="tpu_custom_call" | custom-call | tf_op jit(solution)/shard_map/backward/pallas_call | solution.py:263
  (51 shorter events, 1.0 us)
Async XLA Ops:
  6.5 0.7 copy-start.12
  7.3 0.7 copy-start.9
  7.3 0.8 copy-start.15
  8.3 0.7 copy-start.17
  9.4 0.7 copy-start.16
  10.4 8.1 %copy-start.6 = (f32[16,8,128]{2,1,0:T(8,128)S(1)}, f32[16,8,128]{2,1,0:T(8,128)}, u32[]{:S(2)}) copy-start(f32[16,8,128]{2,1,0:T(8,128)} %param.8) | copy-start | bytes 196612
  11.1 30.7 %all-to-all-start = ((f32[16,1,384]{2,1,0:T(1,128)}), f32[16,1,384]{2,1,0:T(1,128)S(1)}, u32[]{:S(2)}, u32[]{:S(2)}) async-start(f32[16,1,384]{2,1,0:T(1,128)} %copy.32), calls=%async_computation | async-start | bytes 49152 | tf_op jit(solution)/shard_map/all_to_all | solution.py:206
  18.5 70.1 %all-gather.3.cloned.1.call-start = ((), (), s32[]{:S(2)}) async-start(), calls=%async_computation.1 | async-start | bytes 1114112 | tf_op jit(solution)/shard_map/all_gather | solution.py:262
  41.8 1.3 copy-start.5
  54.5 112.6 %all-gather.5.cloned.1.call-start = ((), (), s32[]{:S(2)}) async-start(), calls=%async_computation.2 | async-start | bytes 1114112 | tf_op jit(solution)/shard_map/all_gather | solution.py:262
  56.7 0.8 copy-start
  88.6 0.7 copy-start.7
  88.6 0.7 copy-start.10
  88.6 0.7 copy-start.13
  89.3 1.0 copy-start.1
  90.3 1.2 copy-start.3
  132.3 34.9 %copy-start.8 = (s32[1024]{0:T(1024)S(1)}, s32[1024]{0:T(1024)}, u32[]{:S(2)}) copy-start(s32[1024]{0:T(1024)} %reshape.51.voxel_ref) | copy-start | bytes 12292
  132.3 34.9 %copy-start.11 = (s32[256]{0:T(256)S(1)}, s32[256]{0:T(256)}, u32[]{:S(2)}) copy-start(s32[256]{0:T(256)} %ray_ref.3) | copy-start | bytes 3076
  132.3 34.8 %copy-start.14 = (s32[16]{0:T(128)S(1)}, s32[16]{0:T(128)}, u32[]{:S(2)}) copy-start(s32[16]{0:T(128)} %count_ref.3) | copy-start | bytes 196
  167.1 1.0 copy-start.2
  168.2 1.2 copy-start.4
Sparse Core Ops, SparseCore 0:
  54.7 33.8 all-gather.2
  132.4 34.6 all-gather.4

commit v2 on v1

--- a/solution.py
+++ b/solution.py
@@ -41,7 +41,7 @@
     return first.astype(jnp.int32), weights
 
 
-def target_setup(fields, n_slab, group, capacity, extent, frames, got_ref, index_ref, *rest):
+def target_setup(n_slab, group, capacity, extent, frames, got_ref, index_ref, *rest):
     weight_refs, row_ref = rest[:3], rest[3]
     columns = got_ref[...].T
     ray_tiles = row_ref.shape[0] // frames
@@ -101,10 +101,21 @@
 
 
 def forward_kernel(n_slab, group, capacity, tiles, frames, chunk,
-                   meta_ref, volume_ref, sinogram_ref, row_ref, index_ref, w0_ref, w1_ref, w2_ref,
-                   out_ref, wide, projection):
+                   me_ref, meta_ref, volume_ref, sinogram_ref, row_ref, index_ref, w0_ref, w1_ref,
+                   w2_ref, out_ref, before, wide, after, projection):
     depth = group // capacity
-    wide[...] = volume_ref[...].astype(jnp.float32)
+    me = me_ref[0]
+    rows = tiles * frames
+
+    def widen(source, carry):
+        at = pl.ds(pl.multiple_of(source * rows, rows), rows)
+        values = volume_ref[at, :].astype(jnp.float32)
+        wide[at, :] = values
+        before[at, :] = pltpu.roll(values, 1, axis=1)
+        after[at, :] = pltpu.roll(values, values.shape[1] - 1, axis=1)
+        return carry
+
+    lax.fori_loop(0, n_slab, widen, 0)
     projection[...] = jnp.zeros_like(projection)
 
     def from_source(source, carry):
@@ -116,12 +127,12 @@
                 total = None
                 for level in range(depth):
                     block = slot * depth + level
-                    voxel = source * tiles + meta_ref[source, group + block]
+                    voxel = lax.bitwise_xor(source, me) * tiles + meta_ref[source, group + block]
                     row = source * group + block
-                    values = wide[pl.ds(pl.multiple_of(voxel * frames, frames), frames), :]
+                    at = pl.ds(pl.multiple_of(voxel * frames, frames), frames)
                     index = spread(index_ref, row, frames)
-                    for ref, shift in ((w0_ref, -1), (w1_ref, 0), (w2_ref, 1)):
-                        term = spread(ref, row, frames) * pick(values, index + shift)
+                    for ref, values in ((w0_ref, before), (w1_ref, wide), (w2_ref, after)):
+                        term = spread(ref, row, frames) * pick(values[at, :], index)
                         total = term if total is None else total + term
                 ray = meta_ref[source, 2 * group + slot]
                 at = pl.ds(pl.multiple_of(ray * frames, frames), frames)
@@ -136,10 +147,20 @@
 
 
 def backward_kernel(n_slab, group, capacity, tiles, frames, chunk,
-                    count_ref, voxel_ref, ray_ref, residual_ref, volume_ref, column_ref, index_ref,
-                    w0_ref, w1_ref, out_ref, rounded_ref, wide, *banks):
+                    me_ref, count_ref, voxel_ref, ray_ref, even_ref, odd_ref, volume_ref, column_ref,
+                    index_ref, w0_ref, w1_ref, out_ref, rounded_ref, wide, *banks):
     depth = group // capacity
-    wide[...] = residual_ref[...].astype(jnp.float32)
+    me = me_ref[0]
+    rows = tiles * frames
+
+    def widen(pair, carry):
+        at = pl.ds(pl.multiple_of(pair * rows, rows), rows)
+        twice = pl.multiple_of(pair * (2 * rows), rows)
+        wide[pl.ds(twice, rows), :] = even_ref[at, :].astype(jnp.float32)
+        wide[pl.ds(twice + rows, rows), :] = odd_ref[at, :].astype(jnp.float32)
+        return carry
+
+    lax.fori_loop(0, n_slab // 2, widen, 0)
     for bank in banks:
         bank[...] = jnp.zeros_like(bank)
 
@@ -149,13 +170,14 @@
         def some(step, carry):
             for place in range(chunk):
                 slot = target * capacity + step * chunk + place
-                ray = target * tiles + ray_ref[slot]
+                ray = lax.bitwise_xor(target, me) * tiles + ray_ref[slot]
                 values = wide[pl.ds(pl.multiple_of(ray * frames, frames), frames), :]
+                after = pltpu.roll(values, values.shape[1] - 1, axis=1)
                 for level in range(depth):
                     row = slot * depth + level
                     index = spread(index_ref, row, frames)
                     term = (spread(w0_ref, row, frames) * pick(values, index)
-                            + spread(w1_ref, row, frames) * pick(values, index + 1))
+                            + spread(w1_ref, row, frames) * pick(after, index))
                     at = pl.ds(pl.multiple_of(voxel_ref[row] * frames, frames), frames)
                     banks[level][at, :] += term
             return carry
@@ -169,6 +191,28 @@
     volume = volume_ref[...] + column_ref[...] * back
     out_ref[...] = volume
     rounded_ref[...] = volume.astype(jnp.bfloat16)
+
+
+def exchange(values, n_slab, distance):
+    pairs = [(device, device ^ distance) for device in range(n_slab)]
+    return lax.ppermute(values, "slab", pairs)
+
+
+def gather_tree(values, n_slab):
+    rows, extent = values.shape
+    held = values.reshape(1, rows, extent)
+    distance = n_slab // 2
+    while distance:
+        got = exchange(held, n_slab, distance)
+        held = jnp.stack([held, got], axis=1).reshape(-1, rows, extent)
+        distance //= 2
+    return held.reshape(-1, extent)
+
+
+def gather_direct(values, n_slab):
+    even = jnp.concatenate(
+        [values] + [exchange(values, n_slab, distance) for distance in range(2, n_slab, 2)], axis=0)
+    return even, exchange(even, n_slab, 1)
 
 
 def shards(sinogram, start_volume, slot_voxel, slot_ray, live_count, block_slope, block_offset):
@@ -184,7 +228,8 @@
     shape = jax.ShapeDtypeStruct
 
     volume = start_volume.reshape(voxel_tiles * frames, extent)
-    gathered = lax.all_gather(volume.astype(bf16), "slab", axis=0, tiled=True)
+    me = lax.axis_index("slab").astype(jnp.int32).reshape(1)
+    gathered = gather_tree(volume.astype(bf16), n_slab)
 
     alive = (jnp.arange(capacity)[None, :] < live_count[:, None]).reshape(n_slots, 1)
     offset = jnp.where(alive, block_offset, FAR)
@@ -209,7 +254,7 @@
     ).astype(jnp.int32)
 
     fwd_index, fwd0, fwd1, fwd2, row_weight = pl.pallas_call(
-        functools.partial(target_setup, None, n_slab, group, capacity, extent, frames),
+        functools.partial(target_setup, n_slab, group, capacity, extent, frames),
         out_shape=[shape((blocks, extent), jnp.int32)] + [shape((blocks, extent), f32)] * 3
         + [shape((ray_tiles * frames, extent), f32)],
         in_specs=[VMEM],
@@ -217,7 +262,6 @@
         compiler_params=PARAMS,
         name="target_setup",
     )(got)
-    meta = meta[:, :]
 
     voxel_flat = slot_voxel.reshape(blocks)
     bwd_index, bwd0, bwd1, column_weight = pl.pallas_call(
@@ -237,10 +281,10 @@
     forward = pl.pallas_call(
         functools.partial(forward_kernel, n_slab, group, capacity, voxel_tiles, frames, chunk),
         out_shape=shape((ray_tiles * frames, extent), bf16),
-        in_specs=[SMEM] + [VMEM] * 7,
+        in_specs=[SMEM] * 2 + [VMEM] * 7,
         out_specs=VMEM,
-        scratch_shapes=[
-            pltpu.VMEM((n_slab * voxel_tiles * frames, extent), f32),
+        scratch_shapes=[pltpu.VMEM((n_slab * voxel_tiles * frames, extent), f32)] * 3
+        + [
             pltpu.VMEM((ray_tiles * frames, extent), f32),
         ],
         compiler_params=PARAMS,
@@ -249,7 +293,7 @@
     backward = pl.pallas_call(
         functools.partial(backward_kernel, n_slab, group, capacity, ray_tiles, frames, chunk),
         out_shape=[shape(volume.shape, f32), shape(volume.shape, bf16)],
-        in_specs=[SMEM] * 3 + [VMEM] * 6,
+        in_specs=[SMEM] * 4 + [VMEM] * 7,
         out_specs=[VMEM] * 2,
         scratch_shapes=[pltpu.VMEM((n_slab * ray_tiles * frames, extent), f32)]
         + [pltpu.VMEM(volume.shape, f32)] * depth,
@@ -258,13 +302,13 @@
     )
     sino = sinogram.reshape(ray_tiles * frames, extent)
     for sweep in range(ITERS):
-        residual = forward(meta, gathered, sino, row_weight, fwd_index, fwd0, fwd1, fwd2)
-        spread_out = lax.all_gather(residual, "slab", axis=0, tiled=True)
+        residual = forward(me, meta, gathered, sino, row_weight, fwd_index, fwd0, fwd1, fwd2)
+        even, odd = gather_direct(residual, n_slab)
         volume, rounded = backward(
-            live_count, voxel_flat, slot_ray, spread_out, volume, column_weight, bwd_index, bwd0, bwd1
+            me, live_count, voxel_flat, slot_ray, even, odd, volume, column_weight, bwd_index, bwd0, bwd1
         )
         if sweep + 1 < ITERS:
-            gathered = lax.all_gather(rounded, "slab", axis=0, tiled=True)
+            gathered = gather_tree(rounded, n_slab)
     return volume.reshape(start_volume.shape)
 
 

time: 183 us -> 129 us (0.70)
  blocking collectives: 46.1 us -> 0 us
  starting transfers between devices: 7.47 us -> 43 us
  waiting for transfers between devices: 65.9 us -> 37.5 us
  between operations: 13.6 us -> 0.4 us
    all_gather x2 -> x0, waiting for transfers between devices: 65.9 us -> none  [shards(): spread_out = lax.all_gather(residual, 'slab', axis=0, tiled=True)]
    all_gather x2 -> x0, blocking collectives: 46.1 us -> none  [the longest x1 23.3 us: shards(): gathered = lax.all_gather(volume.astype(bf16), 'slab', axis=0, tiled=True)]
    ppermute x0 -> x24, starting transfers between devices: none -> 38 us  [exchange(): return lax.ppermute(values, 'slab', pairs)]
    ppermute x0 -> x24, waiting for transfers between devices: none -> 30.9 us  [exchange(): return lax.ppermute(values, 'slab', pairs)]
    all_to_all x1, waiting for transfers between devices: 0.01 us -> 6.56 us  [shards(): lax.all_to_all(packed, 'slab', split_axis=0, concat_axis=0, tiled=True)]
    unnamed x39 -> x35, local copies, waits for them, and re-layouts: 8.13 us -> 3.68 us
    all_to_all x1, starting transfers between devices: 7.39 us -> 4.99 us  [shards(): lax.all_to_all(packed, 'slab', split_axis=0, concat_axis=0, tiled=True)]
  transfers between devices with their start and end apart: 3 -> 25, of which waited for: 2 -> 14; matrix products, arithmetic and copies ran while one was open for 1% -> 6% of each run, Pallas kernels for 0% -> 2%
where the time goes in v2:
time: 129 us
  starting transfers between devices  43 us (33%)
  waiting for transfers between devices  37.5 us (29%)
  Pallas kernels  37.2 us (29%)
  local copies, waits for them, and re-layouts  9.75 us (8%)
    ppermute x24, starting transfers between devices, exchange(): return lax.ppermute(values, 'slab', pairs)  38 us
    ppermute x24, waiting for transfers between devices, exchange(): return lax.ppermute(values, 'slab', pairs)  30.9 us
    pallas_call x2, Pallas kernels, shards(): backward(me, live_count, voxel_flat, slot_ray, even, odd, volume, column_...  18.9 us
    pallas_call x2, Pallas kernels, shards(): forward(me, meta, gathered, sino, row_weight, fwd_index, fwd0, fwd1, fwd2)  16.2 us
    all_to_all x1, waiting for transfers between devices, shards(): lax.all_to_all(packed, 'slab', split_axis=0, concat_axis=0, tiled=True)  6.56 us
    all_to_all x1, starting transfers between devices, shards(): lax.all_to_all(packed, 'slab', split_axis=0, concat_axis=0, tiled=True)  4.99 us
    unnamed x35, local copies, waits for them, and re-layouts  3.68 us
  transfers between devices with their start and end apart: 25, of which 14 were waited for; matrix products, arithmetic and copies ran while one was open for 6% of the time, Pallas kernels for 2%

profile of v2, /device:TPU:0, one launch (start us, length us, event | category | flops | bytes accessed | tf_op | source)
XLA Modules:
  0.0 129.0 jit_solution(17656213621755104303)
XLA Ops:
  0.9 4.1 %collective-permute-start = (bf16[1,128,128]{2,1,0:T(8,128)(2,1)S(1)}, bf16[1,128,128]{2,1,0:T(8,128)(2,1)S(1)}, u32[]{:S(2)}, u32[]{:S(2)}) collective-permute-start(bf16[1,128,128]{2,1,0:T(8,128)(2,1)S(1)} %get-tuple-element.34), channel_id=1, source_target_pairs={{0,8},{1,9},{2,10},{3,11},{4,12},{5,13},{6,14},{7,15},{8,0},{9,1},... | collective-permute-start | bytes 98312 | tf_op jit(solution)/shard_map/ppermute | solution.py:198
  5.1 2.1 %collective-permute-done = bf16[1,128,128]{2,1,0:T(8,128)(2,1)S(1)} collective-permute-done((bf16[1,128,128]{2,1,0:T(8,128)(2,1)S(1)}, bf16[1,128,128]{2,1,0:T(8,128)(2,1)S(1)}, u32[]{:S(2)}, u32[]{:S(2)}) %collective-permute-start) | collective-permute-done | bytes 32800 | tf_op jit(solution)/shard_map/ppermute | solution.py:198
  7.2 1.6 %collective-permute-start.1 = (bf16[2,128,128]{2,1,0:T(8,128)(2,1)S(1)}, bf16[2,128,128]{2,1,0:T(8,128)(2,1)S(1)}, u32[]{:S(2)}, u32[]{:S(2)}) collective-permute-start(bf16[2,128,128]{2,1,0:T(8,128)(2,1)S(1)} %get-tuple-element.32), channel_id=1, source_target_pairs={{0,4},{1,5},{2,6},{3,7},{4,0},{5,1},{6,2},{7,3},{8,12},{9,13},{10,... | collective-permute-start | bytes 196616 | tf_op jit(solution)/shard_map/ppermute | solution.py:198
  8.9 2.7 %collective-permute-done.1 = bf16[2,128,128]{2,1,0:T(8,128)(2,1)S(1)} collective-permute-done((bf16[2,128,128]{2,1,0:T(8,128)(2,1)S(1)}, bf16[2,128,128]{2,1,0:T(8,128)(2,1)S(1)}, u32[]{:S(2)}, u32[]{:S(2)}) %collective-permute-start.1) | collective-permute-done | bytes 65568 | tf_op jit(solution)/shard_map/ppermute | solution.py:198
  11.6 1.8 %collective-permute-start.2 = (bf16[4,128,128]{2,1,0:T(8,128)(2,1)S(1)}, bf16[4,128,128]{2,1,0:T(8,128)(2,1)S(1)}, u32[]{:S(2)}, u32[]{:S(2)}) collective-permute-start(bf16[4,128,128]{2,1,0:T(8,128)(2,1)S(1)} %bitcast.59), channel_id=1, source_target_pairs={{0,2},{1,3},{2,0},{3,1},{4,6},{5,7},{6,4},{7,5},{8,10},{9,11},{10,... | collective-permute-start | bytes 393224 | tf_op jit(solution)/shard_map/ppermute | solution.py:198
  17.0 5.0 %all-to-all-start = ((f32[16,1,384]{2,1,0:T(1,128)}), f32[16,1,384]{2,1,0:T(1,128)S(1)}, u32[]{:S(2)}, u32[]{:S(2)}) async-start(f32[16,1,384]{2,1,0:T(1,128)} %copy.54), calls=%async_computation | async-start | bytes 49152 | tf_op jit(solution)/shard_map/all_to_all | solution.py:251
  22.0 6.6 %all-to-all-done = f32[16,1,384]{2,1,0:T(1,128)S(1)} async-done(((f32[16,1,384]{2,1,0:T(1,128)}), f32[16,1,384]{2,1,0:T(1,128)S(1)}, u32[]{:S(2)}, u32[]{:S(2)}) %all-to-all-start) | async-done | bytes 24608 | tf_op jit(solution)/shard_map/all_to_all | solution.py:251
  30.1 1.4 %collective-permute-done.3 = bf16[8,128,128]{2,1,0:T(8,128)(2,1)S(1)} collective-permute-done((bf16[8,128,128]{2,1,0:T(8,128)(2,1)S(1)}, bf16[8,128,128]{2,1,0:T(8,128)(2,1)S(1)}, u32[]{:S(2)}, u32[]{:S(2)}) %collective-permute-start.3) | collective-permute-done | bytes 262176 | tf_op jit(solution)/shard_map/ppermute | solution.py:198
  32.4 8.1 %forward.2 = bf16[256,128]{1,0:T(8,128)(2,1)S(1)} custom-call(s32[1]{0:T(128)} %bitcast.me_ref, s32[16,145]{1,0:T(8,128)S(1)} %maximum_convert_fusion.meta_ref, bf16[2048,128]{1,0:T(8,128)(2,1)S(1)} %bitcast.46, bf16[256,128]{1,0:T(8,128)(2,1)S(1)} %bitcast.47, f32[256,128]{1,0:T(8,128)S(1)} %get-tuple-element.17.row_ref, ...), custom_call_target="tpu_custom_call" | custom-call | tf_op jit(solution)/shard_map/forward/pallas_call | solution.py:305
  41.5 2.0 %collective-permute-start.5 = (bf16[256,128]{1,0:T(8,128)(2,1)S(1)}, bf16[256,128]{1,0:T(8,128)(2,1)S(1)}, u32[]{:S(2)}, u32[]{:S(2)}) collective-permute-start(bf16[256,128]{1,0:T(8,128)(2,1)S(1)} %forward.2), channel_id=1, source_target_pairs={{0,4},{1,5},{2,6},{3,7},{4,0},{5,1},{6,2},{7,3},{8,12},{9,13},{10,... | collective-permute-start | bytes 196616 | tf_op jit(solution)/shard_map/ppermute | solution.py:198
  43.4 1.4 %collective-permute-start.6 = (bf16[256,128]{1,0:T(8,128)(2,1)S(1)}, bf16[256,128]{1,0:T(8,128)(2,1)S(1)}, u32[]{:S(2)}, u32[]{:S(2)}) collective-permute-start(bf16[256,128]{1,0:T(8,128)(2,1)S(1)} %forward.2), channel_id=1, source_target_pairs={{0,6},{1,7},{2,4},{3,5},{4,2},{5,3},{6,0},{7,1},{8,14},{9,15},{10,... | collective-permute-start | bytes 196616 | tf_op jit(solution)/shard_map/ppermute | solution.py:198
  44.8 1.9 %collective-permute-start.7 = (bf16[256,128]{1,0:T(8,128)(2,1)S(1)}, bf16[256,128]{1,0:T(8,128)(2,1)S(1)}, u32[]{:S(2)}, u32[]{:S(2)}) collective-permute-start(bf16[256,128]{1,0:T(8,128)(2,1)S(1)} %forward.2), channel_id=1, source_target_pairs={{0,8},{1,9},{2,10},{3,11},{4,12},{5,13},{6,14},{7,15},{8,0},{9,1},... | collective-permute-start | bytes 196616 | tf_op jit(solution)/shard_map/ppermute | solution.py:198
  47.7 2.9 %collective-permute-start.9 = (bf16[256,128]{1,0:T(8,128)(2,1)S(1)}, bf16[256,128]{1,0:T(8,128)(2,1)S(1)}, u32[]{:S(2)}, u32[]{:S(2)}) collective-permute-start(bf16[256,128]{1,0:T(8,128)(2,1)S(1)} %forward.2), channel_id=1, source_target_pairs={{0,12},{1,13},{2,14},{3,15},{4,8},{5,9},{6,10},{7,11},{8,4},{9,5},... | collective-permute-start | bytes 196616 | tf_op jit(solution)/shard_map/ppermute | solution.py:198
  50.6 2.0 %collective-permute-start.10 = (bf16[256,128]{1,0:T(8,128)(2,1)S(1)}, bf16[256,128]{1,0:T(8,128)(2,1)S(1)}, u32[]{:S(2)}, u32[]{:S(2)}) collective-permute-start(bf16[256,128]{1,0:T(8,128)(2,1)S(1)} %forward.2), channel_id=1, source_target_pairs={{0,14},{1,15},{2,12},{3,13},{4,10},{5,11},{6,8},{7,9},{8,6},{9,7},... | collective-permute-start | bytes 196616 | tf_op jit(solution)/shard_map/ppermute | solution.py:198
  52.7 2.6 %collective-permute-done.7 = bf16[256,128]{1,0:T(8,128)(2,1)S(1)} collective-permute-done((bf16[256,128]{1,0:T(8,128)(2,1)S(1)}, bf16[256,128]{1,0:T(8,128)(2,1)S(1)}, u32[]{:S(2)}, u32[]{:S(2)}) %collective-permute-start.7) | collective-permute-done | bytes 65568 | tf_op jit(solution)/shard_map/ppermute | solution.py:198
  55.3 1.5 %collective-permute-done.8 = bf16[256,128]{1,0:T(8,128)(2,1)S(1)} collective-permute-done((bf16[256,128]{1,0:T(8,128)(2,1)S(1)}, bf16[256,128]{1,0:T(8,128)(2,1)S(1)}, u32[]{:S(2)}, u32[]{:S(2)}) %collective-permute-start.8) | collective-permute-done | bytes 65568 | tf_op jit(solution)/shard_map/ppermute | solution.py:198
  63.7 9.1 %backward.2 = (f32[128,128]{1,0:T(8,128)S(1)}, bf16[128,128]{1,0:T(8,128)(2,1)S(1)}) custom-call(s32[1]{0:T(128)} %bitcast.me_ref, s32[16]{0:T(128)S(1)} %copy-done.3, s32[1024]{0:T(1024)S(1)} %reshape.99.voxel_ref, s32[256]{0:T(256)S(1)} %copy-done.2, bf16[2048,128]{1,0:T(8,128)(2,1)S(1)} %constant_dynamic-update-slice_fusion.even_ref, ...), custom_call_target="tpu_custom_call" | custom-call | tf_op jit(solution)/shard_map/backward/pallas_call | solution.py:307
  72.8 2.1 %collective-permute-start.12 = (bf16[1,128,128]{2,1,0:T(8,128)(2,1)S(1)}, bf16[1,128,128]{2,1,0:T(8,128)(2,1)S(1)}, u32[]{:S(2)}, u32[]{:S(2)}) collective-permute-start(bf16[1,128,128]{2,1,0:T(8,128)(2,1)S(1)} %bitcast.53), channel_id=1, source_target_pairs={{0,8},{1,9},{2,10},{3,11},{4,12},{5,13},{6,14},{7,15},{8,0},{9,1},... | collective-permute-start | bytes 98312 | tf_op jit(solution)/shard_map/ppermute | solution.py:198
  74.9 3.4 %collective-permute-done.12 = bf16[1,128,128]{2,1,0:T(8,128)(2,1)S(1)} collective-permute-done((bf16[1,128,128]{2,1,0:T(8,128)(2,1)S(1)}, bf16[1,128,128]{2,1,0:T(8,128)(2,1)S(1)}, u32[]{:S(2)}, u32[]{:S(2)}) %collective-permute-start.12) | collective-permute-done | bytes 32800 | tf_op jit(solution)/shard_map/ppermute | solution.py:198
  78.9 3.8 %collective-permute-done.13 = bf16[2,128,128]{2,1,0:T(8,128)(2,1)S(1)} collective-permute-done((bf16[2,128,128]{2,1,0:T(8,128)(2,1)S(1)}, bf16[2,128,128]{2,1,0:T(8,128)(2,1)S(1)}, u32[]{:S(2)}, u32[]{:S(2)}) %collective-permute-start.13) | collective-permute-done | bytes 65568 | tf_op jit(solution)/shard_map/ppermute | solution.py:198
  82.8 1.9 %collective-permute-start.14 = (bf16[4,128,128]{2,1,0:T(8,128)(2,1)S(1)}, bf16[4,128,128]{2,1,0:T(8,128)(2,1)S(1)}, u32[]{:S(2)}, u32[]{:S(2)}) collective-permute-start(bf16[4,128,128]{2,1,0:T(8,128)(2,1)S(1)} %bitcast.61), channel_id=1, source_target_pairs={{0,2},{1,3},{2,0},{3,1},{4,6},{5,7},{6,4},{7,5},{8,10},{9,11},{10,... | collective-permute-start | bytes 393224 | tf_op jit(solution)/shard_map/ppermute | solution.py:198
  84.7 3.1 %collective-permute-done.14 = bf16[4,128,128]{2,1,0:T(8,128)(2,1)S(1)} collective-permute-done((bf16[4,128,128]{2,1,0:T(8,128)(2,1)S(1)}, bf16[4,128,128]{2,1,0:T(8,128)(2,1)S(1)}, u32[]{:S(2)}, u32[]{:S(2)}) %collective-permute-start.14) | collective-permute-done | bytes 131104 | tf_op jit(solution)/shard_map/ppermute | solution.py:198
  88.0 1.5 %collective-permute-done.15 = bf16[8,128,128]{2,1,0:T(8,128)(2,1)S(1)} collective-permute-done((bf16[8,128,128]{2,1,0:T(8,128)(2,1)S(1)}, bf16[8,128,128]{2,1,0:T(8,128)(2,1)S(1)}, u32[]{:S(2)}, u32[]{:S(2)}) %collective-permute-start.15) | collective-permute-done | bytes 262176 | tf_op jit(solution)/shard_map/ppermute | solution.py:198
  89.6 8.1 %forward.3 = bf16[256,128]{1,0:T(8,128)(2,1)S(1)} custom-call(s32[1]{0:T(128)} %bitcast.me_ref, s32[16,145]{1,0:T(8,128)S(1)} %maximum_convert_fusion.meta_ref, bf16[2048,128]{1,0:T(8,128)(2,1)S(1)} %bitcast.45, bf16[256,128]{1,0:T(8,128)(2,1)S(1)} %bitcast.48, f32[256,128]{1,0:T(8,128)S(1)} %get-tuple-element.17.row_ref, ...), custom_call_target="tpu_custom_call" | custom-call | tf_op jit(solution)/shard_map/forward/pallas_call | solution.py:305
  97.7 2.4 %collective-permute-start.16 = (bf16[256,128]{1,0:T(8,128)(2,1)S(1)}, bf16[256,128]{1,0:T(8,128)(2,1)S(1)}, u32[]{:S(2)}, u32[]{:S(2)}) collective-permute-start(bf16[256,128]{1,0:T(8,128)(2,1)S(1)} %forward.3), channel_id=1, source_target_pairs={{0,2},{1,3},{2,0},{3,1},{4,6},{5,7},{6,4},{7,5},{8,10},{9,11},{10,... | collective-permute-start | bytes 196616 | tf_op jit(solution)/shard_map/ppermute | solution.py:198
  100.1 2.2 %collective-permute-start.17 = (bf16[256,128]{1,0:T(8,128)(2,1)S(1)}, bf16[256,128]{1,0:T(8,128)(2,1)S(1)}, u32[]{:S(2)}, u32[]{:S(2)}) collective-permute-start(bf16[256,128]{1,0:T(8,128)(2,1)S(1)} %forward.3), channel_id=1, source_target_pairs={{0,4},{1,5},{2,6},{3,7},{4,0},{5,1},{6,2},{7,3},{8,12},{9,13},{10,... | collective-permute-start | bytes 196616 | tf_op jit(solution)/shard_map/ppermute | solution.py:198
  103.4 2.3 %collective-permute-start.19 = (bf16[256,128]{1,0:T(8,128)(2,1)S(1)}, bf16[256,128]{1,0:T(8,128)(2,1)S(1)}, u32[]{:S(2)}, u32[]{:S(2)}) collective-permute-start(bf16[256,128]{1,0:T(8,128)(2,1)S(1)} %forward.3), channel_id=1, source_target_pairs={{0,8},{1,9},{2,10},{3,11},{4,12},{5,13},{6,14},{7,15},{8,0},{9,1},... | collective-permute-start | bytes 196616 | tf_op jit(solution)/shard_map/ppermute | solution.py:198
  106.4 3.7 %collective-permute-start.21 = (bf16[256,128]{1,0:T(8,128)(2,1)S(1)}, bf16[256,128]{1,0:T(8,128)(2,1)S(1)}, u32[]{:S(2)}, u32[]{:S(2)}) collective-permute-start(bf16[256,128]{1,0:T(8,128)(2,1)S(1)} %forward.3), channel_id=1, source_target_pairs={{0,12},{1,13},{2,14},{3,15},{4,8},{5,9},{6,10},{7,11},{8,4},{9,5},... | collective-permute-start | bytes 196616 | tf_op jit(solution)/shard_map/ppermute | solution.py:198
  111.3 3.6 %collective-permute-done.20 = bf16[256,128]{1,0:T(8,128)(2,1)S(1)} collective-permute-done((bf16[256,128]{1,0:T(8,128)(2,1)S(1)}, bf16[256,128]{1,0:T(8,128)(2,1)S(1)}, u32[]{:S(2)}, u32[]{:S(2)}) %collective-permute-start.20) | collective-permute-done | bytes 65568 | tf_op jit(solution)/shard_map/ppermute | solution.py:198
  115.0 2.2 %collective-permute-done.22 = bf16[256,128]{1,0:T(8,128)(2,1)S(1)} collective-permute-done((bf16[256,128]{1,0:T(8,128)(2,1)S(1)}, bf16[256,128]{1,0:T(8,128)(2,1)S(1)}, u32[]{:S(2)}, u32[]{:S(2)}) %collective-permute-start.22) | collective-permute-done | bytes 65568 | tf_op jit(solution)/shard_map/ppermute | solution.py:198
  117.3 1.9 %collective-permute-done.23.odd_ref = bf16[2048,128]{1,0:T(8,128)(2,1)S(1)} collective-permute-done((bf16[2048,128]{1,0:T(8,128)(2,1)S(1)}, bf16[2048,128]{1,0:T(8,128)(2,1)S(1)}, u32[]{:S(2)}, u32[]{:S(2)}) %collective-permute-start.23) | collective-permute-done | bytes 524320 | tf_op jit(solution)/shard_map/ppermute | solution.py:198
  119.2 9.8 %backward.3 = (f32[128,128]{1,0:T(8,128)}, bf16[128,128]{1,0:T(8,128)(2,1)}) custom-call(s32[1]{0:T(128)} %bitcast.me_ref, s32[16]{0:T(128)S(1)} %copy-done.3, s32[1024]{0:T(1024)S(1)} %reshape.99.voxel_ref, s32[256]{0:T(256)S(1)} %copy-done.2, bf16[2048,128]{1,0:T(8,128)(2,1)S(1)} %constant_dynamic-update-slice_fusion.8.even_ref, ...), custom_call_target="tpu_custom_call" | custom-call | tf_op jit(solution)/shard_map/backward/pallas_call | solution.py:307
  (102 shorter events, 19.9 us)
Async XLA Ops:
  0.9 4.1 %copy-start.3 = (s32[16]{0:T(128)S(1)}, s32[16]{0:T(128)}, u32[]{:S(2)}) copy-start(s32[16]{0:T(128)} %count_ref.3) | copy-start | bytes 196
  0.9 6.3 %collective-permute-start = (bf16[1,128,128]{2,1,0:T(8,128)(2,1)S(1)}, bf16[1,128,128]{2,1,0:T(8,128)(2,1)S(1)}, u32[]{:S(2)}, u32[]{:S(2)}) collective-permute-start(bf16[1,128,128]{2,1,0:T(8,128)(2,1)S(1)} %get-tuple-element.34), channel_id=1, source_target_pairs={{0,8},{1,9},{2,10},{3,11},{4,12},{5,13},{6,14},{7,15},{8,0},{9,1},... | collective-permute-start | bytes 98312 | tf_op jit(solution)/shard_map/ppermute | solution.py:198
  7.2 1.6 %copy-start.8 = (f32[256,4]{0,1:T(4,128)S(1)}, f32[256,4]{0,1:T(4,128)}, u32[]{:S(2)}) copy-start(f32[256,4]{0,1:T(4,128)} %param.13) | copy-start | bytes 12292
  7.2 4.3 %collective-permute-start.1 = (bf16[2,128,128]{2,1,0:T(8,128)(2,1)S(1)}, bf16[2,128,128]{2,1,0:T(8,128)(2,1)S(1)}, u32[]{:S(2)}, u32[]{:S(2)}) collective-permute-start(bf16[2,128,128]{2,1,0:T(8,128)(2,1)S(1)} %get-tuple-element.32), channel_id=1, source_target_pairs={{0,4},{1,5},{2,6},{3,7},{4,0},{5,1},{6,2},{7,3},{8,12},{9,13},{10,... | collective-permute-start | bytes 196616 | tf_op jit(solution)/shard_map/ppermute | solution.py:198
  11.6 18.3 %collective-permute-start.2 = (bf16[4,128,128]{2,1,0:T(8,128)(2,1)S(1)}, bf16[4,128,128]{2,1,0:T(8,128)(2,1)S(1)}, u32[]{:S(2)}, u32[]{:S(2)}) collective-permute-start(bf16[4,128,128]{2,1,0:T(8,128)(2,1)S(1)} %bitcast.59), channel_id=1, source_target_pairs={{0,2},{1,3},{2,0},{3,1},{4,6},{5,7},{6,4},{7,5},{8,10},{9,11},{10,... | collective-permute-start | bytes 393224 | tf_op jit(solution)/shard_map/ppermute | solution.py:198
  13.5 0.9 copy-start.4
  13.5 0.7 copy-start.7
  14.4 0.9 copy-start.5
  17.0 11.6 %all-to-all-start = ((f32[16,1,384]{2,1,0:T(1,128)}), f32[16,1,384]{2,1,0:T(1,128)S(1)}, u32[]{:S(2)}, u32[]{:S(2)}) async-start(f32[16,1,384]{2,1,0:T(1,128)} %copy.54), calls=%async_computation | async-start | bytes 49152 | tf_op jit(solution)/shard_map/all_to_all | solution.py:251
  29.9 1.6 %collective-permute-start.3 = (bf16[8,128,128]{2,1,0:T(8,128)(2,1)S(1)}, bf16[8,128,128]{2,1,0:T(8,128)(2,1)S(1)}, u32[]{:S(2)}, u32[]{:S(2)}) collective-permute-start(bf16[8,128,128]{2,1,0:T(8,128)(2,1)S(1)} %bitcast.55), channel_id=1, source_target_pairs={{0,1},{1,0},{2,3},{3,2},{4,5},{5,4},{6,7},{7,6},{8,9},{9,8},{10,11... | collective-permute-start | bytes 786440 | tf_op jit(solution)/shard_map/ppermute | solution.py:198
  31.6 0.8 copy-start
  40.5 7.2 %collective-permute-start.4 = (bf16[256,128]{1,0:T(8,128)(2,1)S(1)}, bf16[256,128]{1,0:T(8,128)(2,1)S(1)}, u32[]{:S(2)}, u32[]{:S(2)}) collective-permute-start(bf16[256,128]{1,0:T(8,128)(2,1)S(1)} %forward.2), channel_id=1, source_target_pairs={{0,2},{1,3},{2,0},{3,1},{4,6},{5,7},{6,4},{7,5},{8,10},{9,11},{10,... | collective-permute-start | bytes 196616 | tf_op jit(solution)/shard_map/ppermute | solution.py:198
  41.5 9.2 %collective-permute-start.5 = (bf16[256,128]{1,0:T(8,128)(2,1)S(1)}, bf16[256,128]{1,0:T(8,128)(2,1)S(1)}, u32[]{:S(2)}, u32[]{:S(2)}) collective-permute-start(bf16[256,128]{1,0:T(8,128)(2,1)S(1)} %forward.2), channel_id=1, source_target_pairs={{0,4},{1,5},{2,6},{3,7},{4,0},{5,1},{6,2},{7,3},{8,12},{9,13},{10,... | collective-permute-start | bytes 196616 | tf_op jit(solution)/shard_map/ppermute | solution.py:198
  43.4 9.2 %collective-permute-start.6 = (bf16[256,128]{1,0:T(8,128)(2,1)S(1)}, bf16[256,128]{1,0:T(8,128)(2,1)S(1)}, u32[]{:S(2)}, u32[]{:S(2)}) collective-permute-start(bf16[256,128]{1,0:T(8,128)(2,1)S(1)} %forward.2), channel_id=1, source_target_pairs={{0,6},{1,7},{2,4},{3,5},{4,2},{5,3},{6,0},{7,1},{8,14},{9,15},{10,... | collective-permute-start | bytes 196616 | tf_op jit(solution)/shard_map/ppermute | solution.py:198
  44.8 10.5 %collective-permute-start.7 = (bf16[256,128]{1,0:T(8,128)(2,1)S(1)}, bf16[256,128]{1,0:T(8,128)(2,1)S(1)}, u32[]{:S(2)}, u32[]{:S(2)}) collective-permute-start(bf16[256,128]{1,0:T(8,128)(2,1)S(1)} %forward.2), channel_id=1, source_target_pairs={{0,8},{1,9},{2,10},{3,11},{4,12},{5,13},{6,14},{7,15},{8,0},{9,1},... | collective-permute-start | bytes 196616 | tf_op jit(solution)/shard_map/ppermute | solution.py:198
  46.7 10.0 %collective-permute-start.8 = (bf16[256,128]{1,0:T(8,128)(2,1)S(1)}, bf16[256,128]{1,0:T(8,128)(2,1)S(1)}, u32[]{:S(2)}, u32[]{:S(2)}) collective-permute-start(bf16[256,128]{1,0:T(8,128)(2,1)S(1)} %forward.2), channel_id=1, source_target_pairs={{0,10},{1,11},{2,8},{3,9},{4,14},{5,15},{6,12},{7,13},{8,2},{9,3},... | collective-permute-start | bytes 196616 | tf_op jit(solution)/shard_map/ppermute | solution.py:198
  47.7 9.0 %collective-permute-start.9 = (bf16[256,128]{1,0:T(8,128)(2,1)S(1)}, bf16[256,128]{1,0:T(8,128)(2,1)S(1)}, u32[]{:S(2)}, u32[]{:S(2)}) collective-permute-start(bf16[256,128]{1,0:T(8,128)(2,1)S(1)} %forward.2), channel_id=1, source_target_pairs={{0,12},{1,13},{2,14},{3,15},{4,8},{5,9},{6,10},{7,11},{8,4},{9,5},... | collective-permute-start | bytes 196616 | tf_op jit(solution)/shard_map/ppermute | solution.py:198
  50.6 7.1 %collective-permute-start.10 = (bf16[256,128]{1,0:T(8,128)(2,1)S(1)}, bf16[256,128]{1,0:T(8,128)(2,1)S(1)}, u32[]{:S(2)}, u32[]{:S(2)}) collective-permute-start(bf16[256,128]{1,0:T(8,128)(2,1)S(1)} %forward.2), channel_id=1, source_target_pairs={{0,14},{1,15},{2,12},{3,13},{4,10},{5,11},{6,8},{7,9},{8,6},{9,7},... | collective-permute-start | bytes 196616 | tf_op jit(solution)/shard_map/ppermute | solution.py:198
  57.8 5.9 %collective-permute-start.11 = (bf16[2048,128]{1,0:T(8,128)(2,1)S(1)}, bf16[2048,128]{1,0:T(8,128)(2,1)S(1)}, u32[]{:S(2)}, u32[]{:S(2)}) collective-permute-start(bf16[2048,128]{1,0:T(8,128)(2,1)S(1)} %constant_dynamic-update-slice_fusion.even_ref), channel_id=1, source_target_pairs={{0,1},{1,0},{2,3},{3,2},{4,5},{5,4},{6,7},{7,6},{8,9},{9,8},{10,11... | collective-permute-start | bytes 1572872 | tf_op jit(solution)/shard_map/ppermute | solution.py:198
  61.7 2.0 %copy-start.1 = (f32[16,8,128]{2,1,0:T(8,128)S(1)}, f32[16,8,128]{2,1,0:T(8,128)}, u32[]{:S(2)}) copy-start(f32[16,8,128]{2,1,0:T(8,128)} %param.8) | copy-start | bytes 196612
  72.8 5.5 %collective-permute-start.12 = (bf16[1,128,128]{2,1,0:T(8,128)(2,1)S(1)}, bf16[1,128,128]{2,1,0:T(8,128)(2,1)S(1)}, u32[]{:S(2)}, u32[]{:S(2)}) collective-permute-start(bf16[1,128,128]{2,1,0:T(8,128)(2,1)S(1)} %bitcast.53), channel_id=1, source_target_pairs={{0,8},{1,9},{2,10},{3,11},{4,12},{5,13},{6,14},{7,15},{8,0},{9,1},... | collective-permute-start | bytes 98312 | tf_op jit(solution)/shard_map/ppermute | solution.py:198
  78.3 4.4 %collective-permute-start.13 = (bf16[2,128,128]{2,1,0:T(8,128)(2,1)S(1)}, bf16[2,128,128]{2,1,0:T(8,128)(2,1)S(1)}, u32[]{:S(2)}, u32[]{:S(2)}) collective-permute-start(bf16[2,128,128]{2,1,0:T(8,128)(2,1)S(1)} %get-tuple-element.30), channel_id=1, source_target_pairs={{0,4},{1,5},{2,6},{3,7},{4,0},{5,1},{6,2},{7,3},{8,12},{9,13},{10,... | collective-permute-start | bytes 196616 | tf_op jit(solution)/shard_map/ppermute | solution.py:198
  82.8 5.0 %collective-permute-start.14 = (bf16[4,128,128]{2,1,0:T(8,128)(2,1)S(1)}, bf16[4,128,128]{2,1,0:T(8,128)(2,1)S(1)}, u32[]{:S(2)}, u32[]{:S(2)}) collective-permute-start(bf16[4,128,128]{2,1,0:T(8,128)(2,1)S(1)} %bitcast.61), channel_id=1, source_target_pairs={{0,2},{1,3},{2,0},{3,1},{4,6},{5,7},{6,4},{7,5},{8,10},{9,11},{10,... | collective-permute-start | bytes 393224 | tf_op jit(solution)/shard_map/ppermute | solution.py:198
  87.9 1.6 %collective-permute-start.15 = (bf16[8,128,128]{2,1,0:T(8,128)(2,1)S(1)}, bf16[8,128,128]{2,1,0:T(8,128)(2,1)S(1)}, u32[]{:S(2)}, u32[]{:S(2)}) collective-permute-start(bf16[8,128,128]{2,1,0:T(8,128)(2,1)S(1)} %bitcast.57), channel_id=1, source_target_pairs={{0,1},{1,0},{2,3},{3,2},{4,5},{5,4},{6,7},{7,6},{8,9},{9,8},{10,11... | collective-permute-start | bytes 786440 | tf_op jit(solution)/shard_map/ppermute | solution.py:198
  97.7 8.7 %collective-permute-start.16 = (bf16[256,128]{1,0:T(8,128)(2,1)S(1)}, bf16[256,128]{1,0:T(8,128)(2,1)S(1)}, u32[]{:S(2)}, u32[]{:S(2)}) collective-permute-start(bf16[256,128]{1,0:T(8,128)(2,1)S(1)} %forward.3), channel_id=1, source_target_pairs={{0,2},{1,3},{2,0},{3,1},{4,6},{5,7},{6,4},{7,5},{8,10},{9,11},{10,... | collective-permute-start | bytes 196616 | tf_op jit(solution)/shard_map/ppermute | solution.py:198
  100.1 10.0 %collective-permute-start.17 = (bf16[256,128]{1,0:T(8,128)(2,1)S(1)}, bf16[256,128]{1,0:T(8,128)(2,1)S(1)}, u32[]{:S(2)}, u32[]{:S(2)}) collective-permute-start(bf16[256,128]{1,0:T(8,128)(2,1)S(1)} %forward.3), channel_id=1, source_target_pairs={{0,4},{1,5},{2,6},{3,7},{4,0},{5,1},{6,2},{7,3},{8,12},{9,13},{10,... | collective-permute-start | bytes 196616 | tf_op jit(solution)/shard_map/ppermute | solution.py:198
  102.3 9.0 %collective-permute-start.18 = (bf16[256,128]{1,0:T(8,128)(2,1)S(1)}, bf16[256,128]{1,0:T(8,128)(2,1)S(1)}, u32[]{:S(2)}, u32[]{:S(2)}) collective-permute-start(bf16[256,128]{1,0:T(8,128)(2,1)S(1)} %forward.3), channel_id=1, source_target_pairs={{0,6},{1,7},{2,4},{3,5},{4,2},{5,3},{6,0},{7,1},{8,14},{9,15},{10,... | collective-permute-start | bytes 196616 | tf_op jit(solution)/shard_map/ppermute | solution.py:198
  103.4 7.9 %collective-permute-start.19 = (bf16[256,128]{1,0:T(8,128)(2,1)S(1)}, bf16[256,128]{1,0:T(8,128)(2,1)S(1)}, u32[]{:S(2)}, u32[]{:S(2)}) collective-permute-start(bf16[256,128]{1,0:T(8,128)(2,1)S(1)} %forward.3), channel_id=1, source_target_pairs={{0,8},{1,9},{2,10},{3,11},{4,12},{5,13},{6,14},{7,15},{8,0},{9,1},... | collective-permute-start | bytes 196616 | tf_op jit(solution)/shard_map/ppermute | solution.py:198
  105.8 9.2 %collective-permute-start.20 = (bf16[256,128]{1,0:T(8,128)(2,1)S(1)}, bf16[256,128]{1,0:T(8,128)(2,1)S(1)}, u32[]{:S(2)}, u32[]{:S(2)}) collective-permute-start(bf16[256,128]{1,0:T(8,128)(2,1)S(1)} %forward.3), channel_id=1, source_target_pairs={{0,10},{1,11},{2,8},{3,9},{4,14},{5,15},{6,12},{7,13},{8,2},{9,3},... | collective-permute-start | bytes 196616 | tf_op jit(solution)/shard_map/ppermute | solution.py:198
  106.4 8.6 %collective-permute-start.21 = (bf16[256,128]{1,0:T(8,128)(2,1)S(1)}, bf16[256,128]{1,0:T(8,128)(2,1)S(1)}, u32[]{:S(2)}, u32[]{:S(2)}) collective-permute-start(bf16[256,128]{1,0:T(8,128)(2,1)S(1)} %forward.3), channel_id=1, source_target_pairs={{0,12},{1,13},{2,14},{3,15},{4,8},{5,9},{6,10},{7,11},{8,4},{9,5},... | collective-permute-start | bytes 196616 | tf_op jit(solution)/shard_map/ppermute | solution.py:198
  110.1 7.1 %collective-permute-start.22 = (bf16[256,128]{1,0:T(8,128)(2,1)S(1)}, bf16[256,128]{1,0:T(8,128)(2,1)S(1)}, u32[]{:S(2)}, u32[]{:S(2)}) collective-permute-start(bf16[256,128]{1,0:T(8,128)(2,1)S(1)} %forward.3), channel_id=1, source_target_pairs={{0,14},{1,15},{2,12},{3,13},{4,10},{5,11},{6,8},{7,9},{8,6},{9,7},... | collective-permute-start | bytes 196616 | tf_op jit(solution)/shard_map/ppermute | solution.py:198
  117.2 2.0 %collective-permute-start.23 = (bf16[2048,128]{1,0:T(8,128)(2,1)S(1)}, bf16[2048,128]{1,0:T(8,128)(2,1)S(1)}, u32[]{:S(2)}, u32[]{:S(2)}) collective-permute-start(bf16[2048,128]{1,0:T(8,128)(2,1)S(1)} %constant_dynamic-update-slice_fusion.8.even_ref), channel_id=1, source_target_pairs={{0,1},{1,0},{2,3},{3,2},{4,5},{5,4},{6,7},{7,6},{8,9},{9,8},{10,11... | collective-permute-start | bytes 1572872 | tf_op jit(solution)/shard_map/ppermute | solution.py:198
  (2 other events, 1.4 us)

commit v3 on v0

v3 whole, which is shorter than its diff:
```python
import functools

import jax
import jax.numpy as jnp
from jax import lax
from jax.experimental import pallas as pl
from jax.experimental.pallas import tpu as pltpu
from jax.sharding import PartitionSpec as P

ITERS = 2
FAR = 1.0e6
CHUNK = 8
F32 = jnp.float32
BF16 = jnp.bfloat16
I32 = jnp.int32
VMEM = pl.BlockSpec(memory_space=pltpu.VMEM)
SMEM = pl.BlockSpec(memory_space=pltpu.SMEM)


def params(mib):
    return pltpu.CompilerParams(vmem_limit_bytes=mib * 1024 * 1024)


def hat(ray, centre):
    return jnp.maximum(0.0, 1.0 - jnp.abs(ray - centre)).astype(BF16)


def row_taps(offset, slope, extent):
    shape = (offset.shape[0], extent)
    ray = lax.broadcasted_iota(I32, shape, 1).astype(F32)
    offset = jnp.broadcast_to(offset, shape)
    slope = jnp.broadcast_to(slope, shape)
    middle = jnp.floor((ray - offset) / slope + 0.5)
    middle = jnp.minimum(jnp.maximum(middle, 1.0), extent - 2.0)
    weights = [hat(ray, offset + slope * (middle + step)) for step in (-1.0, 0.0, 1.0)]
    return middle.astype(I32), weights


def column_taps(offset, slope, extent):
    shape = (offset.shape[0], extent)
    voxel = lax.broadcasted_iota(I32, shape, 1).astype(F32)
    centre = jnp.broadcast_to(offset, shape) + jnp.broadcast_to(slope, shape) * voxel
    first = jnp.minimum(jnp.maximum(jnp.floor(centre), 0.0), extent - 2.0)
    weights = [hat(first + step, centre) for step in (0.0, 1.0)]
    return first.astype(I32), weights


def repeat_rows(values, times):
    return jnp.concatenate(
        [jnp.broadcast_to(values[row:row + 1, :], (times, values.shape[1]))
         for row in range(values.shape[0])], axis=0)


def setup_kernel(paired, n_slab, capacity, depth, tiles, frames, extent,
                 me_ref, meta_ref, got_ref,
                 total_ref, line_ref, ray_ref, voxel_ref,
                 row_ref, fi_ref, f0_ref, f1_ref, f2_ref, bi_ref, b0_ref, b1_ref):
    group = capacity * depth
    ray_tiles = row_ref.shape[0] // frames
    tables = (fi_ref, f0_ref, f1_ref, f2_ref, bi_ref, b0_ref, b1_ref)
    me = me_ref[0]
    half = n_slab // 2

    def from_source(source, found):
        place = source
        if paired:
            entry = lax.bitwise_xor(source, me)
            place = lax.shift_right_logical(entry, 1) + lax.bitwise_and(entry, 1) * half

        def slot(k, found):
            line_ref[found] = source * group + k
            ray_ref[found] = meta_ref[source, depth * capacity + k] * frames
            for level in range(depth):
                tile = place * tiles + meta_ref[source, level * capacity + k]
                voxel_ref[found * depth + level] = tile * frames
            return found + 1

        return lax.fori_loop(0, meta_ref[source, (depth + 1) * capacity], slot, found)

    found = lax.fori_loop(0, n_slab, from_source, 0)
    total_ref[0] = found
    for spare in range(CHUNK):
        line_ref[found + spare] = n_slab * group
        ray_ref[found + spare] = 0
        for level in range(depth):
            voxel_ref[(found + spare) * depth + level] = 0

    def build(source, total):
        fields = got_ref[source]
        columns = fields.T
        summed = None
        for level in range(depth):
            offset = columns[0:capacity, level:level + 1]
            slope = columns[0:capacity, depth + level:depth + level + 1]
            middle, weights = row_taps(offset, slope, extent)
            first, pair = column_taps(offset, slope, extent)
            wide = [weight.astype(F32) for weight in weights]
            values = [middle] + wide + [first] + [weight.astype(F32) for weight in pair]
            at = source * group
            if not isinstance(at, int):
                at = pl.multiple_of(at, 8)
            at = pl.ds(at + level * capacity, capacity)
            for ref, value in zip(tables, values):
                ref[at, :] = value
            part = (wide[0] + wide[1]) + wide[2]
            summed = part if summed is None else summed + part
        tile_of = jnp.broadcast_to(fields[3 * depth:3 * depth + 1, 0:capacity], (ray_tiles, capacity))
        hot = tile_of == lax.broadcasted_iota(I32, (ray_tiles, capacity), 0).astype(F32)
        return total + jnp.dot(hot.astype(F32), summed, precision=lax.Precision.HIGHEST,
                               preferred_element_type=F32)

    total = jnp.zeros((ray_tiles, extent), F32)
    if paired:
        for source in range(n_slab):
            total = build(source, total)
    else:
        total = lax.fori_loop(0, n_slab, build, total)
    for ref in tables:
        ref[n_slab * group:, :] = jnp.zeros((group, extent), ref.dtype)
    row_ref[...] = repeat_rows(1.0 / jnp.maximum(total, 1.0), frames)


def column_kernel(frames, offset_ref, slope_ref, voxel_ref, out_ref):
    tiles = out_ref.shape[0] // frames
    depth, slots = offset_ref.shape
    extent = out_ref.shape[1]
    offsets = offset_ref[...].T
    slopes = slope_ref[...].T
    total = jnp.zeros((tiles, extent), F32)
    for level in range(depth):
        unused, pair = column_taps(
            offsets[:, level:level + 1], slopes[:, level:level + 1], extent)
        tile_of = jnp.broadcast_to(voxel_ref[level:level + 1, :], (tiles, slots))
        hot = (tile_of == lax.broadcasted_iota(I32, (tiles, slots), 0)).astype(F32).astype(BF16)
        for weight in pair:
            total += jnp.dot(hot, weight, preferred_element_type=F32)
    out_ref[...] = repeat_rows(1.0 / jnp.maximum(total, 1.0), frames)


def pick(values, index):
    return jnp.take_along_axis(values, index, axis=1, mode="promise_in_bounds")


def spread(ref, row, frames):
    return jnp.broadcast_to(ref[pl.ds(row, 1), :], (frames, ref.shape[1]))


def sweep_kernel(capacity, depth, frames, n_wide, n_bank,
                 total_ref, line_ref, ray_ref, voxel_ref, near_ref, far_ref, sinogram_ref, row_ref,
                 fi_ref, f0_ref, f1_ref, f2_ref, bi_ref, b0_ref, b1_ref,
                 near_out, far_out, projection, *scratch):
    wides, banks = scratch[:n_wide], scratch[n_wide:]
    half, extent = near_ref.shape
    step_rows = 128
    steps = half // step_rows

    def widen(step, carry):
        at = pl.multiple_of(step * step_rows, step_rows)
        for ref, base in ((near_ref, 0), (far_ref, half)):
            values = ref[pl.ds(at, step_rows), :].astype(F32)
            to = pl.ds(base + at, step_rows)
            wides[0][to, :] = values
            if n_wide == 3:
                wides[1][to, :] = pltpu.roll(values, 1, axis=1)
                wides[2][to, :] = pltpu.roll(values, extent - 1, axis=1)
            for bank in banks:
                bank[to, :] = jnp.zeros_like(values)
        return carry

    lax.fori_loop(0, steps, widen, 0)
    projection[...] = jnp.zeros_like(projection)
    rounds = lax.div(total_ref[0] + (CHUNK - 1), CHUNK)

    def tile_at(start):
        return pl.ds(pl.multiple_of(start, frames), frames)

    def forward(step, carry):
        for place in range(CHUNK):
            slot = step * CHUNK + place
            line = line_ref[slot]
            total = None
            for level in range(depth):
                at = tile_at(voxel_ref[slot * depth + level])
                row = line + level * capacity
                index = spread(fi_ref, row, frames)
                if n_wide == 3:
                    taps = [pick(ref[at, :], index) for ref in (wides[1], wides[0], wides[2])]
                else:
                    values = wides[0][at, :]
                    taps = [pick(values, index + shift) for shift in (-1, 0, 1)]
                for ref, tap in zip((f0_ref, f1_ref, f2_ref), taps):
                    term = spread(ref, row, frames) * tap
                    total = term if total is None else total + term
            projection[tile_at(ray_ref[slot]), :] += total.astype(BF16).astype(F32)
        return carry

    lax.fori_loop(0, rounds, forward, 0)
    residual = (sinogram_ref[...].astype(F32) - projection[...]) * row_ref[...]
    projection[...] = residual.astype(BF16).astype(F32)

    def backward(step, carry):
        for place in range(CHUNK):
            slot = step * CHUNK + place
            line = line_ref[slot]
            values = projection[tile_at(ray_ref[slot]), :]
            for level in range(depth):
                row = line + level * capacity
                index = spread(bi_ref, row, frames)
                term = (spread(b0_ref, row, frames) * pick(values, index)
                        + spread(b1_ref, row, frames) * pick(values, index + 1))
                bank = banks[level % n_bank]
                bank[tile_at(voxel_ref[slot * depth + level]), :] += term
        return carry

    lax.fori_loop(0, rounds, backward, 0)

    def finish(step, carry):
        at = pl.multiple_of(step * step_rows, step_rows)
        here, there = pl.ds(at, step_rows), pl.ds(half + at, step_rows)
        near_out[here, :] = sum(bank[here, :] for bank in banks[1:]) + banks[0][here, :]
        far = sum(bank[there, :] for bank in banks[1:]) + banks[0][there, :]
        far_out[here, :] = far.astype(BF16)
        return carry

    lax.fori_loop(0, steps, finish, 0)


def combine_kernel(near_ref, got_ref, own_ref, *piece_refs):
    rows = own_ref.shape[0]
    own_ref[...] = near_ref[0:rows, :] + got_ref[0:rows, :].astype(F32)
    for place, ref in enumerate(piece_refs):
        at = pl.ds((place + 1) * rows, rows)
        ref[...] = (near_ref[at, :] + got_ref[at, :].astype(F32)).astype(BF16)


def update_kernel(n_pieces, volume_ref, column_ref, own_ref, *refs):
    back = own_ref[...]
    for ref in refs[:n_pieces]:
        back = back + ref[...].astype(F32)
    volume = volume_ref[...] + column_ref[...] * back
    outs = refs[n_pieces:]
    outs[0][...] = volume
    if len(outs) > 1:
        outs[1][...] = volume.astype(BF16)


def exchange(values, n_slab, distance):
    pairs = [(device, device ^ distance) for device in range(n_slab)]
    return lax.ppermute(values, "slab", pairs)


def gather(values, n_slab, paired):
    if not paired:
        whole = lax.all_gather(values, "slab", axis=0, tiled=True)
        middle = whole.shape[0] // 2
        return whole[:middle], whole[middle:]
    near = jnp.concatenate(
        [values] + [exchange(values, n_slab, distance) for distance in range(2, n_slab, 2)], axis=0)
    return near, exchange(near, n_slab, 1)


def shards(sinogram, start_volume, slot_voxel, slot_ray, live_count, block_slope, block_offset):
    n_slab = lax.axis_size("slab")
    n_slots, depth = slot_voxel.shape
    capacity = n_slots // n_slab
    ray_tiles, frames, extent = sinogram.shape
    voxel_tiles = start_volume.shape[0]
    lines = n_slots * depth + capacity * depth
    rows = voxel_tiles * frames
    half = n_slab // 2
    paired = n_slab <= 32
    n_wide, n_bank = (3, 2) if paired else (1, 1)
    shape = jax.ShapeDtypeStruct

    volume = start_volume.reshape(rows, extent)
    near, far = gather(volume.astype(BF16), n_slab, paired)
    me = lax.axis_index("slab").astype(I32).reshape(1)

    alive = (jnp.arange(capacity)[None, :] < live_count[:, None]).reshape(1, n_slots)
    offset = jnp.where(alive, block_offset.T, FAR)
    slope = block_slope.T
    voxel = slot_voxel.T
    count = jnp.broadcast_to(live_count[:, None], (n_slab, capacity)).reshape(1, n_slots)
    fields = jnp.concatenate(
        [offset, slope, voxel.astype(F32), slot_ray.astype(F32).reshape(1, n_slots), count.astype(F32)],
        axis=0)
    n_fields = 3 * depth + 2
    packed = fields.reshape(n_fields, n_slab, capacity).transpose(1, 0, 2)
    padding = ((0, 0), (0, -n_fields % 8), (0, extent - capacity))
    got = lax.all_to_all(
        jnp.pad(packed, padding), "slab", split_axis=0, concat_axis=0, tiled=True)
    meta = got[:, 2 * depth:n_fields, :capacity].astype(I32).reshape(n_slab, (depth + 2) * capacity)

    table = [shape((lines, extent), I32)] + [shape((lines, extent), F32)] * 3
    table += [shape((lines, extent), I32)] + [shape((lines, extent), F32)] * 2
    spare = n_slots + CHUNK
    lists = [shape((1,), I32), shape((spare,), I32), shape((spare,), I32), shape((spare * depth,), I32)]
    prepared = pl.pallas_call(
        functools.partial(setup_kernel, paired, n_slab, capacity, depth, voxel_tiles, frames, extent),
        out_shape=lists + [shape((ray_tiles * frames, extent), F32)] + table,
        in_specs=[SMEM, SMEM, VMEM],
        out_specs=[SMEM] * 4 + [VMEM] * 8,
        compiler_params=params(32),
        name="setup",
    )(me, meta, got)
    lists, row_weight, table = prepared[:4], prepared[4], prepared[5:]

    column_weight = pl.pallas_call(
        functools.partial(column_kernel, frames),
        out_shape=shape((rows, extent), F32),
        in_specs=[VMEM] * 3,
        out_specs=VMEM,
        compiler_params=params(16),
        name="column_weight",
    )(offset, slope, voxel)

    sweep = pl.pallas_call(
        functools.partial(sweep_kernel, capacity, depth, frames, n_wide, n_bank),
        out_shape=[shape((half * rows, extent), F32), shape((half * rows, extent), BF16)],
        in_specs=[SMEM] * 4 + [VMEM] * 11,
        out_specs=[VMEM] * 2,
        scratch_shapes=[pltpu.VMEM((ray_tiles * frames, extent), F32)]
        + [pltpu.VMEM((n_slab * rows, extent), F32)] * (n_wide + n_bank),
        compiler_params=params(40 if n_slab > 32 else 24),
        name="sweep",
    )
    combine = pl.pallas_call(
        combine_kernel,
        out_shape=[shape((rows, extent), F32)] + [shape((rows, extent), BF16)] * (half - 1),
        in_specs=[VMEM] * 2,
        out_specs=[VMEM] * half,
        compiler_params=params(24),
        name="combine",
    )
    sino = sinogram.reshape(ray_tiles * frames, extent)
    for turn in range(ITERS):
        last = turn + 1 == ITERS
        near_sum, far_sum = sweep(*lists, near, far, sino, row_weight, *table)
        if paired:
            own, *pieces = combine(near_sum, exchange(far_sum, n_slab, 1))
            pieces = [exchange(piece, n_slab, 2 * (place + 1)) for place, piece in enumerate(pieces)]
        else:
            both = jnp.concatenate([near_sum.astype(BF16), far_sum], axis=0)
            parts = lax.all_to_all(
                both.reshape(n_slab, rows, extent), "slab", split_axis=0, concat_axis=0, tiled=True)
            own, pieces = jnp.sum(parts.astype(F32), axis=0), []
        updated = pl.pallas_call(
            functools.partial(update_kernel, len(pieces)),
            out_shape=[shape((rows, extent), F32)] + ([] if last else [shape((rows, extent), BF16)]),
            in_specs=[VMEM] * (len(pieces) + 3),
            out_specs=[VMEM] * (1 if last else 2),
            compiler_params=params(16),
            name="update",
        )(volume, column_weight, own, *pieces)
        volume = updated[0]
        if not last:
            near, far = gather(updated[1], n_slab, paired)
    return volume.reshape(start_volume.shape)


def solution(mesh):
    in_specs = (
        P(("scan", "slab"), None, None),
        P(("scan", "slab"), None, None),
        P(("scan", "slab"), None),
        P(("scan", "slab")),
        P(("scan", "slab")),
        P(("scan", "slab"), None),
        P(("scan", "slab"), None),
    )
    out_specs = P(("scan", "slab"), None, None)
    return jax.shard_map(shards, mesh=mesh, in_specs=in_specs, out_specs=out_specs, check_vma=False)
```

time: 207 us -> 119 us (0.57)
  matrix products: 65.1 us -> 0 us
  blocking collectives: 36.7 us -> 0 us
  starting transfers between devices: 23.7 us -> 54.9 us
  Pallas kernels: 0 us -> 28.4 us
  local copies, waits for them, and re-layouts: 28.7 us -> 3.54 us
  other arithmetic: 23.4 us -> 0.96 us
  waiting for transfers between devices: 28.1 us -> 30.8 us
    dot_general x12 -> x0, matrix products: 65.1 us -> none  [the longest x2 30.3 us: shards(): jnp.einsum('sdrv,sdfv->sfr', tiles, picked, preferred_element_type=jnp.fl...]
    ppermute x0 -> x32, starting transfers between devices: none -> 49.9 us  [exchange(): return lax.ppermute(values, 'slab', pairs)]
    all_to_all x2 -> x0, blocking collectives: 36.7 us -> none  [the longest x1 18.4 us: shards(): lax.all_to_all(outgoing, 'slab', split_axis=0, concat_axis=0, tiled=True)]
    ppermute x0 -> x32, waiting for transfers between devices: none -> 30.8 us  [exchange(): return lax.ppermute(values, 'slab', pairs)]
    pallas_call x0 -> x8, Pallas kernels: none -> 28.4 us  [the longest x2 21.5 us: shards(): near_sum, far_sum = sweep(*lists, near, far, sino, row_weight, *table)]
    all_to_all x4 -> x1, waiting for transfers between devices: 28.1 us -> 0.01 us  [shards(): lax.all_to_all(jnp.pad(packed, padding), 'slab', split_axis=0, concat_axi...]
    reduce_sum x1 -> x0, other arithmetic: 19.1 us -> none  [shards(): jnp.sum(tiles, axis=2, dtype=jnp.float32).reshape(n_slots * depth, extent)]
    all_to_all x4 -> x1, starting transfers between devices: 23.7 us -> 4.98 us  [shards(): lax.all_to_all(jnp.pad(packed, padding), 'slab', split_axis=0, concat_axi...]
  transfers between devices with their start and end apart: 4 -> 33, of which waited for: 2 -> 12; matrix products, arithmetic and copies ran while one was open for 22% -> 1% of each run, Pallas kernels for 0% -> 5%
where the time goes in v3:
time: 119 us
  starting transfers between devices  54.9 us (46%)
  waiting for transfers between devices  30.8 us (26%)
  Pallas kernels  28.4 us (24%)
  local copies, waits for them, and re-layouts  3.54 us (3%)
    ppermute x32, starting transfers between devices, exchange(): return lax.ppermute(values, 'slab', pairs)  49.9 us
    ppermute x32, waiting for transfers between devices, exchange(): return lax.ppermute(values, 'slab', pairs)  30.8 us
    pallas_call x2, Pallas kernels, shards(): near_sum, far_sum = sweep(*lists, near, far, sino, row_weight, *table)  21.5 us
    pallas_call x1, Pallas kernels, shards(): pl.pallas_call(functools.partial(setup_kernel, paired, n_slab, capacity,...  5.43 us
    all_to_all x1, starting transfers between devices, shards(): lax.all_to_all(jnp.pad(packed, padding), 'slab', split_axis=0, concat_axi...  4.98 us
  transfers between devices with their start and end apart: 33, of which 12 were waited for; matrix products, arithmetic and copies ran while one was open for 1% of the time, Pallas kernels for 5%

profile of v3, /device:TPU:0, one launch (start us, length us, event | category | flops | bytes accessed | tf_op | source)
XLA Modules:
  0.0 118.9 jit_solution(2677210915609053600)
XLA Ops:
  0.9 6.1 %collective-permute-start.6 = (bf16[128,128]{1,0:T(8,128)(2,1)S(1)}, bf16[128,128]{1,0:T(8,128)(2,1)S(1)}, u32[]{:S(2)}, u32[]{:S(2)}) collective-permute-start(bf16[128,128]{1,0:T(8,128)(2,1)S(1)} %get-tuple-element.74), channel_id=1, source_target_pairs={{0,14},{1,15},{2,12},{3,13},{4,10},{5,11},{6,8},{7,9},{8,6},{9,7},... | collective-permute-start | bytes 98312 | tf_op jit(solution)/shard_map/ppermute | solution.py:249
  7.9 2.0 %collective-permute-start.3 = (bf16[128,128]{1,0:T(8,128)(2,1)S(1)}, bf16[128,128]{1,0:T(8,128)(2,1)S(1)}, u32[]{:S(2)}, u32[]{:S(2)}) collective-permute-start(bf16[128,128]{1,0:T(8,128)(2,1)S(1)} %get-tuple-element.74), channel_id=1, source_target_pairs={{0,8},{1,9},{2,10},{3,11},{4,12},{5,13},{6,14},{7,15},{8,0},{9,1},... | collective-permute-start | bytes 98312 | tf_op jit(solution)/shard_map/ppermute | solution.py:249
  10.0 1.6 %collective-permute-start = (bf16[128,128]{1,0:T(8,128)(2,1)S(1)}, bf16[128,128]{1,0:T(8,128)(2,1)S(1)}, u32[]{:S(2)}, u32[]{:S(2)}) collective-permute-start(bf16[128,128]{1,0:T(8,128)(2,1)S(1)} %get-tuple-element.74), channel_id=1, source_target_pairs={{0,2},{1,3},{2,0},{3,1},{4,6},{5,7},{6,4},{7,5},{8,10},{9,11},{10,... | collective-permute-start | bytes 98312 | tf_op jit(solution)/shard_map/ppermute | solution.py:249
  15.0 5.0 %all-to-all-start = ((f32[16,16,128]{2,1,0:T(8,128)}), f32[16,16,128]{2,1,0:T(8,128)S(1)}, u32[]{:S(2)}, u32[]{:S(2)}) async-start(f32[16,16,128]{2,1,0:T(8,128)} %pad.4), calls=%async_computation | async-start | bytes 262144 | tf_op jit(solution)/shard_map/all_to_all | solution.py:290
  20.0 2.0 %collective-permute-start.1 = (bf16[128,128]{1,0:T(8,128)(2,1)S(1)}, bf16[128,128]{1,0:T(8,128)(2,1)S(1)}, u32[]{:S(2)}, u32[]{:S(2)}) collective-permute-start(bf16[128,128]{1,0:T(8,128)(2,1)S(1)} %get-tuple-element.74), channel_id=1, source_target_pairs={{0,4},{1,5},{2,6},{3,7},{4,0},{5,1},{6,2},{7,3},{8,12},{9,13},{10,... | collective-permute-start | bytes 98312 | tf_op jit(solution)/shard_map/ppermute | solution.py:249
  22.0 3.2 %collective-permute-done.1 = bf16[128,128]{1,0:T(8,128)(2,1)S(1)} collective-permute-done((bf16[128,128]{1,0:T(8,128)(2,1)S(1)}, bf16[128,128]{1,0:T(8,128)(2,1)S(1)}, u32[]{:S(2)}, u32[]{:S(2)}) %collective-permute-start.1) | collective-permute-done | bytes 32800 | tf_op jit(solution)/shard_map/ppermute | solution.py:249
  25.2 2.2 %collective-permute-start.2 = (bf16[128,128]{1,0:T(8,128)(2,1)S(1)}, bf16[128,128]{1,0:T(8,128)(2,1)S(1)}, u32[]{:S(2)}, u32[]{:S(2)}) collective-permute-start(bf16[128,128]{1,0:T(8,128)(2,1)S(1)} %get-tuple-element.74), channel_id=1, source_target_pairs={{0,6},{1,7},{2,4},{3,5},{4,2},{5,3},{6,0},{7,1},{8,14},{9,15},{10,... | collective-permute-start | bytes 98312 | tf_op jit(solution)/shard_map/ppermute | solution.py:249
  27.4 2.6 %collective-permute-done.2 = bf16[128,128]{1,0:T(8,128)(2,1)S(1)} collective-permute-done((bf16[128,128]{1,0:T(8,128)(2,1)S(1)}, bf16[128,128]{1,0:T(8,128)(2,1)S(1)}, u32[]{:S(2)}, u32[]{:S(2)}) %collective-permute-start.2) | collective-permute-done | bytes 32800 | tf_op jit(solution)/shard_map/ppermute | solution.py:249
  30.3 5.4 %setup.1 = (s32[1]{0:T(128)}, s32[264]{0:T(512)S(1)}, s32[264]{0:T(512)S(1)}, s32[1056]{0:T(1024)S(1)}, f32[256,128]{1,0:T(8,128)S(1)}, /*index=5*/s32[1088,128]...) custom-call(s32[1]{0:T(128)} %bitcast.4.me_ref, ...), custom_call_target="tpu_custom_call" | custom-call | tf_op jit(solution)/shard_map/setup/pallas_call | solution.py:298
  35.8 10.7 %sweep.2 = (f32[1024,128]{1,0:T(8,128)S(1)}, bf16[1024,128]{1,0:T(8,128)(2,1)S(1)}) custom-call(s32[1]{0:T(128)} %get-tuple-element.39.total_ref, s32[264]{0:T(512)S(1)} %get-tuple-element.40.line_ref, s32[264]{0:T(512)S(1)} %get-tuple-element.41.ray_ref, s32[1056]{0:T(1024)S(1)} %get-tuple-element.42.voxel_ref, ...), custom_call_target="tpu_custom_call" | custom-call | tf_op jit(solution)/shard_map/sweep/pallas_call | solution.py:338
  46.6 2.0 %collective-permute-start.8 = (bf16[1024,128]{1,0:T(8,128)(2,1)S(1)}, bf16[1024,128]{1,0:T(8,128)(2,1)S(1)}, u32[]{:S(2)}, u32[]{:S(2)}) collective-permute-start(bf16[1024,128]{1,0:T(8,128)(2,1)S(1)} %get-tuple-element.52), channel_id=1, source_target_pairs={{0,1},{1,0},{2,3},{3,2},{4,5},{5,4},{6,7},{7,6},{8,9},{9,8},{10,11... | collective-permute-start | bytes 786440 | tf_op jit(solution)/shard_map/ppermute | solution.py:249
  49.8 3.5 %collective-permute-start.9 = (bf16[128,128]{1,0:T(8,128)(2,1)S(1)}, bf16[128,128]{1,0:T(8,128)(2,1)S(1)}, u32[]{:S(2)}, u32[]{:S(2)}) collective-permute-start(bf16[128,128]{1,0:T(8,128)(2,1)S(1)} %get-tuple-element.54), channel_id=1, source_target_pairs={{0,2},{1,3},{2,0},{3,1},{4,6},{5,7},{6,4},{7,5},{8,10},{9,11},{10,... | collective-permute-start | bytes 98312 | tf_op jit(solution)/shard_map/ppermute | solution.py:249
  53.3 1.5 %collective-permute-start.11 = (bf16[128,128]{1,0:T(8,128)(2,1)S(1)}, bf16[128,128]{1,0:T(8,128)(2,1)S(1)}, u32[]{:S(2)}, u32[]{:S(2)}) collective-permute-start(bf16[128,128]{1,0:T(8,128)(2,1)S(1)} %get-tuple-element.56), channel_id=1, source_target_pairs={{0,6},{1,7},{2,4},{3,5},{4,2},{5,3},{6,0},{7,1},{8,14},{9,15},{10,... | collective-permute-start | bytes 98312 | tf_op jit(solution)/shard_map/ppermute | solution.py:249
  54.8 1.7 %collective-permute-start.12 = (bf16[128,128]{1,0:T(8,128)(2,1)S(1)}, bf16[128,128]{1,0:T(8,128)(2,1)S(1)}, u32[]{:S(2)}, u32[]{:S(2)}) collective-permute-start(bf16[128,128]{1,0:T(8,128)(2,1)S(1)} %get-tuple-element.57), channel_id=1, source_target_pairs={{0,8},{1,9},{2,10},{3,11},{4,12},{5,13},{6,14},{7,15},{8,0},{9,1},... | collective-permute-start | bytes 98312 | tf_op jit(solution)/shard_map/ppermute | solution.py:249
  56.5 2.6 %collective-permute-start.13 = (bf16[128,128]{1,0:T(8,128)(2,1)S(1)}, bf16[128,128]{1,0:T(8,128)(2,1)S(1)}, u32[]{:S(2)}, u32[]{:S(2)}) collective-permute-start(bf16[128,128]{1,0:T(8,128)(2,1)S(1)} %get-tuple-element.58), channel_id=1, source_target_pairs={{0,10},{1,11},{2,8},{3,9},{4,14},{5,15},{6,12},{7,13},{8,2},{9,3},... | collective-permute-start | bytes 98312 | tf_op jit(solution)/shard_map/ppermute | solution.py:249
  59.1 1.8 %collective-permute-start.14 = (bf16[128,128]{1,0:T(8,128)(2,1)S(1)}, bf16[128,128]{1,0:T(8,128)(2,1)S(1)}, u32[]{:S(2)}, u32[]{:S(2)}) collective-permute-start(bf16[128,128]{1,0:T(8,128)(2,1)S(1)} %get-tuple-element.59), channel_id=1, source_target_pairs={{0,12},{1,13},{2,14},{3,15},{4,8},{5,9},{6,10},{7,11},{8,4},{9,5},... | collective-permute-start | bytes 98312 | tf_op jit(solution)/shard_map/ppermute | solution.py:249
  60.9 1.6 %collective-permute-start.15 = (bf16[128,128]{1,0:T(8,128)(2,1)S(1)}, bf16[128,128]{1,0:T(8,128)(2,1)S(1)}, u32[]{:S(2)}, u32[]{:S(2)}) collective-permute-start(bf16[128,128]{1,0:T(8,128)(2,1)S(1)} %get-tuple-element.60), channel_id=1, source_target_pairs={{0,14},{1,15},{2,12},{3,13},{4,10},{5,11},{6,8},{7,9},{8,6},{9,7},... | collective-permute-start | bytes 98312 | tf_op jit(solution)/shard_map/ppermute | solution.py:249
  63.1 1.7 %collective-permute-done.14.refs_5_ = bf16[128,128]{1,0:T(8,128)(2,1)S(1)} collective-permute-done((bf16[128,128]{1,0:T(8,128)(2,1)S(1)}, bf16[128,128]{1,0:T(8,128)(2,1)S(1)}, u32[]{:S(2)}, u32[]{:S(2)}) %collective-permute-start.14) | collective-permute-done | bytes 32800 | tf_op jit(solution)/shard_map/ppermute | solution.py:249
  64.9 2.7 %collective-permute-done.15.refs_6_ = bf16[128,128]{1,0:T(8,128)(2,1)S(1)} collective-permute-done((bf16[128,128]{1,0:T(8,128)(2,1)S(1)}, bf16[128,128]{1,0:T(8,128)(2,1)S(1)}, u32[]{:S(2)}, u32[]{:S(2)}) %collective-permute-start.15) | collective-permute-done | bytes 32800 | tf_op jit(solution)/shard_map/ppermute | solution.py:249
  67.6 1.7 %collective-permute-start.22 = (bf16[128,128]{1,0:T(8,128)(2,1)S(1)}, bf16[128,128]{1,0:T(8,128)(2,1)S(1)}, u32[]{:S(2)}, u32[]{:S(2)}) collective-permute-start(bf16[128,128]{1,0:T(8,128)(2,1)S(1)} %get-tuple-element.62), channel_id=1, source_target_pairs={{0,14},{1,15},{2,12},{3,13},{4,10},{5,11},{6,8},{7,9},{8,6},{9,7},... | collective-permute-start | bytes 98312 | tf_op jit(solution)/shard_map/ppermute | solution.py:249
  69.3 1.7 %collective-permute-start.21 = (bf16[128,128]{1,0:T(8,128)(2,1)S(1)}, bf16[128,128]{1,0:T(8,128)(2,1)S(1)}, u32[]{:S(2)}, u32[]{:S(2)}) collective-permute-start(bf16[128,128]{1,0:T(8,128)(2,1)S(1)} %get-tuple-element.62), channel_id=1, source_target_pairs={{0,12},{1,13},{2,14},{3,15},{4,8},{5,9},{6,10},{7,11},{8,4},{9,5},... | collective-permute-start | bytes 98312 | tf_op jit(solution)/shard_map/ppermute | solution.py:249
  71.0 4.4 %collective-permute-start.19 = (bf16[128,128]{1,0:T(8,128)(2,1)S(1)}, bf16[128,128]{1,0:T(8,128)(2,1)S(1)}, u32[]{:S(2)}, u32[]{:S(2)}) collective-permute-start(bf16[128,128]{1,0:T(8,128)(2,1)S(1)} %get-tuple-element.62), channel_id=1, source_target_pairs={{0,8},{1,9},{2,10},{3,11},{4,12},{5,13},{6,14},{7,15},{8,0},{9,1},... | collective-permute-start | bytes 98312 | tf_op jit(solution)/shard_map/ppermute | solution.py:249
  75.4 3.9 %collective-permute-done.16 = bf16[128,128]{1,0:T(8,128)(2,1)S(1)} collective-permute-done((bf16[128,128]{1,0:T(8,128)(2,1)S(1)}, bf16[128,128]{1,0:T(8,128)(2,1)S(1)}, u32[]{:S(2)}, u32[]{:S(2)}) %collective-permute-start.16) | collective-permute-done | bytes 32800 | tf_op jit(solution)/shard_map/ppermute | solution.py:249
  79.3 3.9 %collective-permute-done.17 = bf16[128,128]{1,0:T(8,128)(2,1)S(1)} collective-permute-done((bf16[128,128]{1,0:T(8,128)(2,1)S(1)}, bf16[128,128]{1,0:T(8,128)(2,1)S(1)}, u32[]{:S(2)}, u32[]{:S(2)}) %collective-permute-start.17) | collective-permute-done | bytes 32800 | tf_op jit(solution)/shard_map/ppermute | solution.py:249
  83.2 4.8 %collective-permute-done.18 = bf16[128,128]{1,0:T(8,128)(2,1)S(1)} collective-permute-done((bf16[128,128]{1,0:T(8,128)(2,1)S(1)}, bf16[128,128]{1,0:T(8,128)(2,1)S(1)}, u32[]{:S(2)}, u32[]{:S(2)}) %collective-permute-start.18) | collective-permute-done | bytes 32800 | tf_op jit(solution)/shard_map/ppermute | solution.py:249
  89.7 10.7 %sweep.3 = (f32[1024,128]{1,0:T(8,128)S(1)}, bf16[1024,128]{1,0:T(8,128)(2,1)S(1)}) custom-call(s32[1]{0:T(128)} %get-tuple-element.39.total_ref, s32[264]{0:T(512)S(1)} %get-tuple-element.40.line_ref, s32[264]{0:T(512)S(1)} %get-tuple-element.41.ray_ref, s32[1056]{0:T(1024)S(1)} %get-tuple-element.42.voxel_ref, ...), custom_call_target="tpu_custom_call" | custom-call | tf_op jit(solution)/shard_map/sweep/pallas_call | solution.py:338
  103.0 1.9 %collective-permute-start.25 = (bf16[128,128]{1,0:T(8,128)(2,1)S(1)}, bf16[128,128]{1,0:T(8,128)(2,1)S(1)}, u32[]{:S(2)}, u32[]{:S(2)}) collective-permute-start(bf16[128,128]{1,0:T(8,128)(2,1)S(1)} %get-tuple-element.66), channel_id=1, source_target_pairs={{0,2},{1,3},{2,0},{3,1},{4,6},{5,7},{6,4},{7,5},{8,10},{9,11},{10,... | collective-permute-start | bytes 98312 | tf_op jit(solution)/shard_map/ppermute | solution.py:249
  104.9 1.7 %collective-permute-start.27 = (bf16[128,128]{1,0:T(8,128)(2,1)S(1)}, bf16[128,128]{1,0:T(8,128)(2,1)S(1)}, u32[]{:S(2)}, u32[]{:S(2)}) collective-permute-start(bf16[128,128]{1,0:T(8,128)(2,1)S(1)} %get-tuple-element.68), channel_id=1, source_target_pairs={{0,6},{1,7},{2,4},{3,5},{4,2},{5,3},{6,0},{7,1},{8,14},{9,15},{10,... | collective-permute-start | bytes 98312 | tf_op jit(solution)/shard_map/ppermute | solution.py:249
  106.6 4.1 %collective-permute-start.29 = (bf16[128,128]{1,0:T(8,128)(2,1)S(1)}, bf16[128,128]{1,0:T(8,128)(2,1)S(1)}, u32[]{:S(2)}, u32[]{:S(2)}) collective-permute-start(bf16[128,128]{1,0:T(8,128)(2,1)S(1)} %get-tuple-element.70), channel_id=1, source_target_pairs={{0,10},{1,11},{2,8},{3,9},{4,14},{5,15},{6,12},{7,13},{8,2},{9,3},... | collective-permute-start | bytes 98312 | tf_op jit(solution)/shard_map/ppermute | solution.py:249
  111.6 2.6 %collective-permute-start.31 = (bf16[128,128]{1,0:T(8,128)(2,1)S(1)}, bf16[128,128]{1,0:T(8,128)(2,1)S(1)}, u32[]{:S(2)}, u32[]{:S(2)}) collective-permute-start(bf16[128,128]{1,0:T(8,128)(2,1)S(1)} %get-tuple-element.72), channel_id=1, source_target_pairs={{0,14},{1,15},{2,12},{3,13},{4,10},{5,11},{6,8},{7,9},{8,6},{9,7},... | collective-permute-start | bytes 98312 | tf_op jit(solution)/shard_map/ppermute | solution.py:249
  114.3 2.1 %collective-permute-done.30.refs_5_ = bf16[128,128]{1,0:T(8,128)(2,1)S(1)} collective-permute-done((bf16[128,128]{1,0:T(8,128)(2,1)S(1)}, bf16[128,128]{1,0:T(8,128)(2,1)S(1)}, u32[]{:S(2)}, u32[]{:S(2)}) %collective-permute-start.30) | collective-permute-done | bytes 32800 | tf_op jit(solution)/shard_map/ppermute | solution.py:249
  116.4 1.8 %collective-permute-done.31.refs_6_ = bf16[128,128]{1,0:T(8,128)(2,1)S(1)} collective-permute-done((bf16[128,128]{1,0:T(8,128)(2,1)S(1)}, bf16[128,128]{1,0:T(8,128)(2,1)S(1)}, u32[]{:S(2)}, u32[]{:S(2)}) %collective-permute-start.31) | collective-permute-done | bytes 32800 | tf_op jit(solution)/shard_map/ppermute | solution.py:249
  (90 shorter events, 13.2 us)
Async XLA Ops:
  0.9 29.2 %collective-permute-start.6 = (bf16[128,128]{1,0:T(8,128)(2,1)S(1)}, bf16[128,128]{1,0:T(8,128)(2,1)S(1)}, u32[]{:S(2)}, u32[]{:S(2)}) collective-permute-start(bf16[128,128]{1,0:T(8,128)(2,1)S(1)} %get-tuple-element.74), channel_id=1, source_target_pairs={{0,14},{1,15},{2,12},{3,13},{4,10},{5,11},{6,8},{7,9},{8,6},{9,7},... | collective-permute-start | bytes 98312 | tf_op jit(solution)/shard_map/ppermute | solution.py:249
  7.0 23.2 %collective-permute-start.5 = (bf16[128,128]{1,0:T(8,128)(2,1)S(1)}, bf16[128,128]{1,0:T(8,128)(2,1)S(1)}, u32[]{:S(2)}, u32[]{:S(2)}) collective-permute-start(bf16[128,128]{1,0:T(8,128)(2,1)S(1)} %get-tuple-element.74), channel_id=1, source_target_pairs={{0,12},{1,13},{2,14},{3,15},{4,8},{5,9},{6,10},{7,11},{8,4},{9,5},... | collective-permute-start | bytes 98312 | tf_op jit(solution)/shard_map/ppermute | solution.py:249
  7.2 22.9 %collective-permute-start.4 = (bf16[128,128]{1,0:T(8,128)(2,1)S(1)}, bf16[128,128]{1,0:T(8,128)(2,1)S(1)}, u32[]{:S(2)}, u32[]{:S(2)}) collective-permute-start(bf16[128,128]{1,0:T(8,128)(2,1)S(1)} %get-tuple-element.74), channel_id=1, source_target_pairs={{0,10},{1,11},{2,8},{3,9},{4,14},{5,15},{6,12},{7,13},{8,2},{9,3},... | collective-permute-start | bytes 98312 | tf_op jit(solution)/shard_map/ppermute | solution.py:249
  7.9 22.1 %collective-permute-start.3 = (bf16[128,128]{1,0:T(8,128)(2,1)S(1)}, bf16[128,128]{1,0:T(8,128)(2,1)S(1)}, u32[]{:S(2)}, u32[]{:S(2)}) collective-permute-start(bf16[128,128]{1,0:T(8,128)(2,1)S(1)} %get-tuple-element.74), channel_id=1, source_target_pairs={{0,8},{1,9},{2,10},{3,11},{4,12},{5,13},{6,14},{7,15},{8,0},{9,1},... | collective-permute-start | bytes 98312 | tf_op jit(solution)/shard_map/ppermute | solution.py:249
  10.0 10.0 %collective-permute-start = (bf16[128,128]{1,0:T(8,128)(2,1)S(1)}, bf16[128,128]{1,0:T(8,128)(2,1)S(1)}, u32[]{:S(2)}, u32[]{:S(2)}) collective-permute-start(bf16[128,128]{1,0:T(8,128)(2,1)S(1)} %get-tuple-element.74), channel_id=1, source_target_pairs={{0,2},{1,3},{2,0},{3,1},{4,6},{5,7},{6,4},{7,5},{8,10},{9,11},{10,... | collective-permute-start | bytes 98312 | tf_op jit(solution)/shard_map/ppermute | solution.py:249
  15.0 15.2 %all-to-all-start = ((f32[16,16,128]{2,1,0:T(8,128)}), f32[16,16,128]{2,1,0:T(8,128)S(1)}, u32[]{:S(2)}, u32[]{:S(2)}) async-start(f32[16,16,128]{2,1,0:T(8,128)} %pad.4), calls=%async_computation | async-start | bytes 262144 | tf_op jit(solution)/shard_map/all_to_all | solution.py:290
  20.0 5.2 %collective-permute-start.1 = (bf16[128,128]{1,0:T(8,128)(2,1)S(1)}, bf16[128,128]{1,0:T(8,128)(2,1)S(1)}, u32[]{:S(2)}, u32[]{:S(2)}) collective-permute-start(bf16[128,128]{1,0:T(8,128)(2,1)S(1)} %get-tuple-element.74), channel_id=1, source_target_pairs={{0,4},{1,5},{2,6},{3,7},{4,0},{5,1},{6,2},{7,3},{8,12},{9,13},{10,... | collective-permute-start | bytes 98312 | tf_op jit(solution)/shard_map/ppermute | solution.py:249
  25.2 4.8 %collective-permute-start.2 = (bf16[128,128]{1,0:T(8,128)(2,1)S(1)}, bf16[128,128]{1,0:T(8,128)(2,1)S(1)}, u32[]{:S(2)}, u32[]{:S(2)}) collective-permute-start(bf16[128,128]{1,0:T(8,128)(2,1)S(1)} %get-tuple-element.74), channel_id=1, source_target_pairs={{0,6},{1,7},{2,4},{3,5},{4,2},{5,3},{6,0},{7,1},{8,14},{9,15},{10,... | collective-permute-start | bytes 98312 | tf_op jit(solution)/shard_map/ppermute | solution.py:249
  30.2 5.6 %collective-permute-start.7 = (bf16[1024,128]{1,0:T(8,128)(2,1)S(1)}, bf16[1024,128]{1,0:T(8,128)(2,1)S(1)}, u32[]{:S(2)}, u32[]{:S(2)}) collective-permute-start(bf16[1024,128]{1,0:T(8,128)(2,1)S(1)} %constant_dynamic-update-slice_fusion.near_ref), channel_id=1, source_target_pairs={{0,1},{1,0},{2,3},{3,2},{4,5},{5,4},{6,7},{7,6},{8,9},{9,8},{10,11... | collective-permute-start | bytes 786440 | tf_op jit(solution)/shard_map/ppermute | solution.py:249
  46.6 3.1 %collective-permute-start.8 = (bf16[1024,128]{1,0:T(8,128)(2,1)S(1)}, bf16[1024,128]{1,0:T(8,128)(2,1)S(1)}, u32[]{:S(2)}, u32[]{:S(2)}) collective-permute-start(bf16[1024,128]{1,0:T(8,128)(2,1)S(1)} %get-tuple-element.52), channel_id=1, source_target_pairs={{0,1},{1,0},{2,3},{3,2},{4,5},{5,4},{6,7},{7,6},{8,9},{9,8},{10,11... | collective-permute-start | bytes 786440 | tf_op jit(solution)/shard_map/ppermute | solution.py:249
  49.8 9.4 %collective-permute-start.9 = (bf16[128,128]{1,0:T(8,128)(2,1)S(1)}, bf16[128,128]{1,0:T(8,128)(2,1)S(1)}, u32[]{:S(2)}, u32[]{:S(2)}) collective-permute-start(bf16[128,128]{1,0:T(8,128)(2,1)S(1)} %get-tuple-element.54), channel_id=1, source_target_pairs={{0,2},{1,3},{2,0},{3,1},{4,6},{5,7},{6,4},{7,5},{8,10},{9,11},{10,... | collective-permute-start | bytes 98312 | tf_op jit(solution)/shard_map/ppermute | solution.py:249
  53.3 7.6 %collective-permute-start.10 = (bf16[128,128]{1,0:T(8,128)(2,1)S(1)}, bf16[128,128]{1,0:T(8,128)(2,1)S(1)}, u32[]{:S(2)}, u32[]{:S(2)}) collective-permute-start(bf16[128,128]{1,0:T(8,128)(2,1)S(1)} %get-tuple-element.55), channel_id=1, source_target_pairs={{0,4},{1,5},{2,6},{3,7},{4,0},{5,1},{6,2},{7,3},{8,12},{9,13},{10,... | collective-permute-start | bytes 98312 | tf_op jit(solution)/shard_map/ppermute | solution.py:249
  53.3 9.8 %collective-permute-start.11 = (bf16[128,128]{1,0:T(8,128)(2,1)S(1)}, bf16[128,128]{1,0:T(8,128)(2,1)S(1)}, u32[]{:S(2)}, u32[]{:S(2)}) collective-permute-start(bf16[128,128]{1,0:T(8,128)(2,1)S(1)} %get-tuple-element.56), channel_id=1, source_target_pairs={{0,6},{1,7},{2,4},{3,5},{4,2},{5,3},{6,0},{7,1},{8,14},{9,15},{10,... | collective-permute-start | bytes 98312 | tf_op jit(solution)/shard_map/ppermute | solution.py:249
  54.8 8.3 %collective-permute-start.12 = (bf16[128,128]{1,0:T(8,128)(2,1)S(1)}, bf16[128,128]{1,0:T(8,128)(2,1)S(1)}, u32[]{:S(2)}, u32[]{:S(2)}) collective-permute-start(bf16[128,128]{1,0:T(8,128)(2,1)S(1)} %get-tuple-element.57), channel_id=1, source_target_pairs={{0,8},{1,9},{2,10},{3,11},{4,12},{5,13},{6,14},{7,15},{8,0},{9,1},... | collective-permute-start | bytes 98312 | tf_op jit(solution)/shard_map/ppermute | solution.py:249
  56.5 6.6 %collective-permute-start.13 = (bf16[128,128]{1,0:T(8,128)(2,1)S(1)}, bf16[128,128]{1,0:T(8,128)(2,1)S(1)}, u32[]{:S(2)}, u32[]{:S(2)}) collective-permute-start(bf16[128,128]{1,0:T(8,128)(2,1)S(1)} %get-tuple-element.58), channel_id=1, source_target_pairs={{0,10},{1,11},{2,8},{3,9},{4,14},{5,15},{6,12},{7,13},{8,2},{9,3},... | collective-permute-start | bytes 98312 | tf_op jit(solution)/shard_map/ppermute | solution.py:249
  59.1 5.7 %collective-permute-start.14 = (bf16[128,128]{1,0:T(8,128)(2,1)S(1)}, bf16[128,128]{1,0:T(8,128)(2,1)S(1)}, u32[]{:S(2)}, u32[]{:S(2)}) collective-permute-start(bf16[128,128]{1,0:T(8,128)(2,1)S(1)} %get-tuple-element.59), channel_id=1, source_target_pairs={{0,12},{1,13},{2,14},{3,15},{4,8},{5,9},{6,10},{7,11},{8,4},{9,5},... | collective-permute-start | bytes 98312 | tf_op jit(solution)/shard_map/ppermute | solution.py:249
  60.9 6.7 %collective-permute-start.15 = (bf16[128,128]{1,0:T(8,128)(2,1)S(1)}, bf16[128,128]{1,0:T(8,128)(2,1)S(1)}, u32[]{:S(2)}, u32[]{:S(2)}) collective-permute-start(bf16[128,128]{1,0:T(8,128)(2,1)S(1)} %get-tuple-element.60), channel_id=1, source_target_pairs={{0,14},{1,15},{2,12},{3,13},{4,10},{5,11},{6,8},{7,9},{8,6},{9,7},... | collective-permute-start | bytes 98312 | tf_op jit(solution)/shard_map/ppermute | solution.py:249
  67.6 20.4 %collective-permute-start.22 = (bf16[128,128]{1,0:T(8,128)(2,1)S(1)}, bf16[128,128]{1,0:T(8,128)(2,1)S(1)}, u32[]{:S(2)}, u32[]{:S(2)}) collective-permute-start(bf16[128,128]{1,0:T(8,128)(2,1)S(1)} %get-tuple-element.62), channel_id=1, source_target_pairs={{0,14},{1,15},{2,12},{3,13},{4,10},{5,11},{6,8},{7,9},{8,6},{9,7},... | collective-permute-start | bytes 98312 | tf_op jit(solution)/shard_map/ppermute | solution.py:249
  69.3 18.7 %collective-permute-start.21 = (bf16[128,128]{1,0:T(8,128)(2,1)S(1)}, bf16[128,128]{1,0:T(8,128)(2,1)S(1)}, u32[]{:S(2)}, u32[]{:S(2)}) collective-permute-start(bf16[128,128]{1,0:T(8,128)(2,1)S(1)} %get-tuple-element.62), channel_id=1, source_target_pairs={{0,12},{1,13},{2,14},{3,15},{4,8},{5,9},{6,10},{7,11},{8,4},{9,5},... | collective-permute-start | bytes 98312 | tf_op jit(solution)/shard_map/ppermute | solution.py:249
  71.0 17.1 %collective-permute-start.20 = (bf16[128,128]{1,0:T(8,128)(2,1)S(1)}, bf16[128,128]{1,0:T(8,128)(2,1)S(1)}, u32[]{:S(2)}, u32[]{:S(2)}) collective-permute-start(bf16[128,128]{1,0:T(8,128)(2,1)S(1)} %get-tuple-element.62), channel_id=1, source_target_pairs={{0,10},{1,11},{2,8},{3,9},{4,14},{5,15},{6,12},{7,13},{8,2},{9,3},... | collective-permute-start | bytes 98312 | tf_op jit(solution)/shard_map/ppermute | solution.py:249
  71.0 17.0 %collective-permute-start.19 = (bf16[128,128]{1,0:T(8,128)(2,1)S(1)}, bf16[128,128]{1,0:T(8,128)(2,1)S(1)}, u32[]{:S(2)}, u32[]{:S(2)}) collective-permute-start(bf16[128,128]{1,0:T(8,128)(2,1)S(1)} %get-tuple-element.62), channel_id=1, source_target_pairs={{0,8},{1,9},{2,10},{3,11},{4,12},{5,13},{6,14},{7,15},{8,0},{9,1},... | collective-permute-start | bytes 98312 | tf_op jit(solution)/shard_map/ppermute | solution.py:249
  75.4 3.9 %collective-permute-start.16 = (bf16[128,128]{1,0:T(8,128)(2,1)S(1)}, bf16[128,128]{1,0:T(8,128)(2,1)S(1)}, u32[]{:S(2)}, u32[]{:S(2)}) collective-permute-start(bf16[128,128]{1,0:T(8,128)(2,1)S(1)} %get-tuple-element.62), channel_id=1, source_target_pairs={{0,2},{1,3},{2,0},{3,1},{4,6},{5,7},{6,4},{7,5},{8,10},{9,11},{10,... | collective-permute-start | bytes 98312 | tf_op jit(solution)/shard_map/ppermute | solution.py:249
  79.3 3.9 %collective-permute-start.17 = (bf16[128,128]{1,0:T(8,128)(2,1)S(1)}, bf16[128,128]{1,0:T(8,128)(2,1)S(1)}, u32[]{:S(2)}, u32[]{:S(2)}) collective-permute-start(bf16[128,128]{1,0:T(8,128)(2,1)S(1)} %get-tuple-element.62), channel_id=1, source_target_pairs={{0,4},{1,5},{2,6},{3,7},{4,0},{5,1},{6,2},{7,3},{8,12},{9,13},{10,... | collective-permute-start | bytes 98312 | tf_op jit(solution)/shard_map/ppermute | solution.py:249
  83.2 4.8 %collective-permute-start.18 = (bf16[128,128]{1,0:T(8,128)(2,1)S(1)}, bf16[128,128]{1,0:T(8,128)(2,1)S(1)}, u32[]{:S(2)}, u32[]{:S(2)}) collective-permute-start(bf16[128,128]{1,0:T(8,128)(2,1)S(1)} %get-tuple-element.62), channel_id=1, source_target_pairs={{0,6},{1,7},{2,4},{3,5},{4,2},{5,3},{6,0},{7,1},{8,14},{9,15},{10,... | collective-permute-start | bytes 98312 | tf_op jit(solution)/shard_map/ppermute | solution.py:249
  100.5 2.5 %collective-permute-start.24 = (bf16[1024,128]{1,0:T(8,128)(2,1)S(1)}, bf16[1024,128]{1,0:T(8,128)(2,1)S(1)}, u32[]{:S(2)}, u32[]{:S(2)}) collective-permute-start(bf16[1024,128]{1,0:T(8,128)(2,1)S(1)} %get-tuple-element.64), channel_id=1, source_target_pairs={{0,1},{1,0},{2,3},{3,2},{4,5},{5,4},{6,7},{7,6},{8,9},{9,8},{10,11... | collective-permute-start | bytes 786440 | tf_op jit(solution)/shard_map/ppermute | solution.py:249
  103.0 7.7 %collective-permute-start.25 = (bf16[128,128]{1,0:T(8,128)(2,1)S(1)}, bf16[128,128]{1,0:T(8,128)(2,1)S(1)}, u32[]{:S(2)}, u32[]{:S(2)}) collective-permute-start(bf16[128,128]{1,0:T(8,128)(2,1)S(1)} %get-tuple-element.66), channel_id=1, source_target_pairs={{0,2},{1,3},{2,0},{3,1},{4,6},{5,7},{6,4},{7,5},{8,10},{9,11},{10,... | collective-permute-start | bytes 98312 | tf_op jit(solution)/shard_map/ppermute | solution.py:249
  104.8 6.8 %collective-permute-start.26 = (bf16[128,128]{1,0:T(8,128)(2,1)S(1)}, bf16[128,128]{1,0:T(8,128)(2,1)S(1)}, u32[]{:S(2)}, u32[]{:S(2)}) collective-permute-start(bf16[128,128]{1,0:T(8,128)(2,1)S(1)} %get-tuple-element.67), channel_id=1, source_target_pairs={{0,4},{1,5},{2,6},{3,7},{4,0},{5,1},{6,2},{7,3},{8,12},{9,13},{10,... | collective-permute-start | bytes 98312 | tf_op jit(solution)/shard_map/ppermute | solution.py:249
  104.9 9.4 %collective-permute-start.27 = (bf16[128,128]{1,0:T(8,128)(2,1)S(1)}, bf16[128,128]{1,0:T(8,128)(2,1)S(1)}, u32[]{:S(2)}, u32[]{:S(2)}) collective-permute-start(bf16[128,128]{1,0:T(8,128)(2,1)S(1)} %get-tuple-element.68), channel_id=1, source_target_pairs={{0,6},{1,7},{2,4},{3,5},{4,2},{5,3},{6,0},{7,1},{8,14},{9,15},{10,... | collective-permute-start | bytes 98312 | tf_op jit(solution)/shard_map/ppermute | solution.py:249
  106.6 7.7 %collective-permute-start.28 = (bf16[128,128]{1,0:T(8,128)(2,1)S(1)}, bf16[128,128]{1,0:T(8,128)(2,1)S(1)}, u32[]{:S(2)}, u32[]{:S(2)}) collective-permute-start(bf16[128,128]{1,0:T(8,128)(2,1)S(1)} %get-tuple-element.69), channel_id=1, source_target_pairs={{0,8},{1,9},{2,10},{3,11},{4,12},{5,13},{6,14},{7,15},{8,0},{9,1},... | collective-permute-start | bytes 98312 | tf_op jit(solution)/shard_map/ppermute | solution.py:249
  106.6 7.7 %collective-permute-start.29 = (bf16[128,128]{1,0:T(8,128)(2,1)S(1)}, bf16[128,128]{1,0:T(8,128)(2,1)S(1)}, u32[]{:S(2)}, u32[]{:S(2)}) collective-permute-start(bf16[128,128]{1,0:T(8,128)(2,1)S(1)} %get-tuple-element.70), channel_id=1, source_target_pairs={{0,10},{1,11},{2,8},{3,9},{4,14},{5,15},{6,12},{7,13},{8,2},{9,3},... | collective-permute-start | bytes 98312 | tf_op jit(solution)/shard_map/ppermute | solution.py:249
  110.7 5.7 %collective-permute-start.30 = (bf16[128,128]{1,0:T(8,128)(2,1)S(1)}, bf16[128,128]{1,0:T(8,128)(2,1)S(1)}, u32[]{:S(2)}, u32[]{:S(2)}) collective-permute-start(bf16[128,128]{1,0:T(8,128)(2,1)S(1)} %get-tuple-element.71), channel_id=1, source_target_pairs={{0,12},{1,13},{2,14},{3,15},{4,8},{5,9},{6,10},{7,11},{8,4},{9,5},... | collective-permute-start | bytes 98312 | tf_op jit(solution)/shard_map/ppermute | solution.py:249
  111.6 6.6 %collective-permute-start.31 = (bf16[128,128]{1,0:T(8,128)(2,1)S(1)}, bf16[128,128]{1,0:T(8,128)(2,1)S(1)}, u32[]{:S(2)}, u32[]{:S(2)}) collective-permute-start(bf16[128,128]{1,0:T(8,128)(2,1)S(1)} %get-tuple-element.72), channel_id=1, source_target_pairs={{0,14},{1,15},{2,12},{3,13},{4,10},{5,11},{6,8},{7,9},{8,6},{9,7},... | collective-permute-start | bytes 98312 | tf_op jit(solution)/shard_map/ppermute | solution.py:249
  (8 other events, 49.4 us)

commit v4 on v3

v4 whole, which is shorter than its diff:
```python
import functools

import jax
import jax.numpy as jnp
from jax import lax
from jax.experimental import pallas as pl
from jax.experimental.pallas import tpu as pltpu
from jax.sharding import PartitionSpec as P

ITERS = 2
FAR = 1.0e6
CHUNK = 8
F32 = jnp.float32
BF16 = jnp.bfloat16
I32 = jnp.int32
HIGHEST = lax.Precision.HIGHEST
VMEM = pl.BlockSpec(memory_space=pltpu.VMEM)
SMEM = pl.BlockSpec(memory_space=pltpu.SMEM)


def params(mib):
    return pltpu.CompilerParams(vmem_limit_bytes=mib * 1024 * 1024)


def hat(ray, centre):
    return jnp.maximum(0.0, 1.0 - jnp.abs(ray - centre)).astype(BF16)


def row_taps(offset, slope, extent):
    shape = (offset.shape[0], extent)
    ray = lax.broadcasted_iota(I32, shape, 1).astype(F32)
    offset = jnp.broadcast_to(offset, shape)
    slope = jnp.broadcast_to(slope, shape)
    middle = jnp.floor((ray - offset) / slope + 0.5)
    middle = jnp.minimum(jnp.maximum(middle, 1.0), extent - 2.0)
    weights = [hat(ray, offset + slope * (middle + step)) for step in (-1.0, 0.0, 1.0)]
    return middle.astype(I32), weights


def column_taps(offset, slope, extent):
    shape = (offset.shape[0], extent)
    voxel = lax.broadcasted_iota(I32, shape, 1).astype(F32)
    centre = jnp.broadcast_to(offset, shape) + jnp.broadcast_to(slope, shape) * voxel
    first = jnp.minimum(jnp.maximum(jnp.floor(centre), 0.0), extent - 2.0)
    weights = [hat(first + step, centre) for step in (0.0, 1.0)]
    return first.astype(I32), weights


def repeat_rows(values, times):
    return jnp.concatenate(
        [jnp.broadcast_to(values[row:row + 1, :], (times, values.shape[1]))
         for row in range(values.shape[0])], axis=0)


def contract_lanes(left, right):
    return lax.dot_general(
        left, right, (((1,), (1,)), ((), ())), precision=HIGHEST, preferred_element_type=F32)


def setup_kernel(n_slab, capacity, depth, tiles, frames, extent,
                 me_ref, line_up_ref, got_ref,
                 near_list, far_list, row_ref, fi_ref, f0_ref, f1_ref, f2_ref, bi_ref, b0_ref, b1_ref):
    group = capacity * depth
    slots = n_slab * capacity
    dead = n_slab * group
    ray_tiles = row_ref.shape[0] // frames
    tables = (fi_ref, f0_ref, f1_ref, f2_ref, bi_ref, b0_ref, b1_ref)

    slot = lax.broadcasted_iota(I32, (1, slots), 1)
    source = lax.div(slot, capacity)
    within = lax.rem(slot, capacity)
    line = (source * group + within - dead).astype(F32)
    ray = line_up_ref[depth:depth + 1, :] * frames
    base = lax.shift_right_logical(source, 1).astype(F32) * tiles
    voxels = [(line_up_ref[level:level + 1, :] + base) * frames for level in range(depth)]
    table = jnp.concatenate(
        [line, ray] + voxels + [jnp.zeros((8 - 2 - depth, slots), F32)], axis=0)
    alive = within.astype(F32) < line_up_ref[depth + 1:depth + 2, :]
    same = lax.bitwise_and(lax.bitwise_xor(source, me_ref[0]), 1) == 0
    order = lax.broadcasted_iota(I32, (slots, slots), 0)
    earlier = (lax.broadcasted_iota(I32, (slots, slots), 1) < order).astype(F32)
    kind = lax.broadcasted_iota(I32, (8, slots), 0)
    for ref, wanted in ((near_list, same), (far_list, jnp.logical_not(same))):
        room = ref.shape[1]
        taken = jnp.logical_and(alive, wanted).astype(F32)
        position = contract_lanes(jnp.broadcast_to(taken, (8, slots)), earlier)[0:1, :]
        position = jnp.where(taken > 0.0, position, -1.0).astype(I32)
        choose = jnp.broadcast_to(position, (room, slots)) == order[:room, :]
        packed = contract_lanes(table, choose.astype(F32))
        total = jnp.sum(taken, axis=1, keepdims=True)
        extra = jnp.where(kind == 0, float(dead), jnp.where(kind == 7, total, 0.0))[:, :room]
        ref[...] = (packed + extra + 0.5).astype(I32)

    def build(source, total):
        fields = got_ref[source]
        columns = fields.T
        summed = None
        for level in range(depth):
            offset = columns[0:capacity, level:level + 1]
            slope = columns[0:capacity, depth + level:depth + level + 1]
            middle, weights = row_taps(offset, slope, extent)
            first, pair = column_taps(offset, slope, extent)
            wide = [weight.astype(F32) for weight in weights]
            values = [middle] + wide + [first] + [weight.astype(F32) for weight in pair]
            at = source * group
            if not isinstance(at, int):
                at = pl.multiple_of(at, 8)
            at = pl.ds(at + level * capacity, capacity)
            for ref, value in zip(tables, values):
                ref[at, :] = value
            part = (wide[0] + wide[1]) + wide[2]
            summed = part if summed is None else summed + part
        tile_of = jnp.broadcast_to(fields[3 * depth:3 * depth + 1, 0:capacity], (ray_tiles, capacity))
        hot = tile_of == lax.broadcasted_iota(I32, (ray_tiles, capacity), 0).astype(F32)
        return total + jnp.dot(hot.astype(F32), summed, precision=HIGHEST, preferred_element_type=F32)

    total = jnp.zeros((ray_tiles, extent), F32)
    if n_slab <= 32:
        for source in range(n_slab):
            total = build(source, total)
    else:
        total = lax.fori_loop(0, n_slab, build, total)
    for ref in tables:
        ref[dead:, :] = jnp.zeros((group, extent), ref.dtype)
    row_ref[...] = repeat_rows(1.0 / jnp.maximum(total, 1.0), frames)


def column_kernel(frames, offset_ref, slope_ref, voxel_ref, out_ref):
    tiles = out_ref.shape[0] // frames
    depth, slots = offset_ref.shape
    extent = out_ref.shape[1]
    offsets = offset_ref[...].T
    slopes = slope_ref[...].T
    total = jnp.zeros((tiles, extent), F32)
    for level in range(depth):
        unused, pair = column_taps(
            offsets[:, level:level + 1], slopes[:, level:level + 1], extent)
        tile_of = jnp.broadcast_to(voxel_ref[level:level + 1, :], (tiles, slots))
        hot = (tile_of == lax.broadcasted_iota(I32, (tiles, slots), 0)).astype(F32).astype(BF16)
        for weight in pair:
            total += jnp.dot(hot, weight, preferred_element_type=F32)
    out_ref[...] = repeat_rows(1.0 / jnp.maximum(total, 1.0), frames)


def pick(values, index):
    return jnp.take_along_axis(values, index, axis=1, mode="promise_in_bounds")


def spread(ref, row, frames):
    return jnp.broadcast_to(ref[pl.ds(row, 1), :], (frames, ref.shape[1]))


def tile_at(start, frames):
    return pl.ds(pl.multiple_of(start, frames), frames)


def for_slots(list_ref, body):
    def some(step, carry):
        for place in range(CHUNK):
            body(step * CHUNK + place)
        return carry

    lax.fori_loop(0, lax.div(list_ref[7, 0] + (CHUNK - 1), CHUNK), some, 0)


def for_rows(rows, body):
    step = 128

    def some(number, carry):
        body(pl.ds(pl.multiple_of(number * step, step), step))
        return carry

    lax.fori_loop(0, rows // step, some, 0)


def project(capacity, depth, frames, list_ref, values_ref, tables, projection, wides):
    extent = values_ref.shape[1]

    def widen(at):
        values = values_ref[at, :].astype(F32)
        wides[0][at, :] = values
        if len(wides) == 3:
            wides[1][at, :] = pltpu.roll(values, 1, axis=1)
            wides[2][at, :] = pltpu.roll(values, extent - 1, axis=1)

    for_rows(values_ref.shape[0], widen)

    def one(slot):
        line = list_ref[0, slot]
        total = None
        for level in range(depth):
            at = tile_at(list_ref[2 + level, slot], frames)
            row = line + level * capacity
            index = spread(tables[0], row, frames)
            if len(wides) == 3:
                taps = [pick(ref[at, :], index) for ref in (wides[1], wides[0], wides[2])]
            else:
                values = wides[0][at, :]
                taps = [pick(values, index + shift) for shift in (-1, 0, 1)]
            for ref, tap in zip(tables[1:], taps):
                term = spread(ref, row, frames) * tap
                total = term if total is None else total + term
        projection[tile_at(list_ref[1, slot], frames), :] += total.astype(BF16).astype(F32)

    for_slots(list_ref, one)


def backproject(capacity, depth, frames, list_ref, residual, tables, banks):
    def clear(at):
        for bank in banks:
            bank[at, :] = jnp.zeros((at.size, bank.shape[1]), F32)

    for_rows(banks[0].shape[0], clear)

    def one(slot):
        line = list_ref[0, slot]
        values = residual[tile_at(list_ref[1, slot], frames), :]
        for level in range(depth):
            row = line + level * capacity
            index = spread(tables[0], row, frames)
            term = (spread(tables[1], row, frames) * pick(values, index)
                    + spread(tables[2], row, frames) * pick(values, index + 1))
            banks[level % len(banks)][tile_at(list_ref[2 + level, slot], frames), :] += term

    for_slots(list_ref, one)


def near_forward(sizes, list_ref, values_ref, *refs):
    tables, projection, wides = refs[:4], refs[4], refs[5:]
    projection[...] = jnp.zeros_like(projection)
    project(*sizes, list_ref, values_ref, tables, projection, wides)


def far_both(sizes, n_wide, list_ref, values_ref, partial_ref, sinogram_ref, row_ref, *refs):
    forward, backward = refs[:4], refs[4:7]
    out_ref, residual, scratch = refs[7], refs[8], refs[9:]
    projection, wides, banks = scratch[0], scratch[1:1 + n_wide], scratch[1 + n_wide:]
    projection[...] = partial_ref[...]
    project(*sizes, list_ref, values_ref, forward, projection, wides)
    scaled = (sinogram_ref[...].astype(F32) - projection[...]) * row_ref[...]
    residual[...] = scaled.astype(BF16).astype(F32)
    backproject(*sizes, list_ref, residual, backward, banks)

    def finish(at):
        out_ref[at, :] = sum([bank[at, :] for bank in banks[1:]], banks[0][at, :]).astype(BF16)

    for_rows(out_ref.shape[0], finish)


def near_backward(sizes, list_ref, residual, *refs):
    tables, out_ref, banks = refs[:3], refs[3], refs[4:]
    backproject(*sizes, list_ref, residual, tables, (out_ref,) + banks)

    def finish(at):
        out_ref[at, :] = sum([bank[at, :] for bank in banks], out_ref[at, :])

    if banks:
        for_rows(out_ref.shape[0], finish)


def combine_kernel(near_ref, got_ref, out_ref):
    def add(at):
        out_ref[at, :] = (near_ref[at, :] + got_ref[at, :].astype(F32)).astype(BF16)

    for_rows(out_ref.shape[0], add)


def update_kernel(volume_ref, column_ref, parts_ref, out_ref, *copies_ref):
    rows = volume_ref.shape[0]
    pieces = parts_ref.shape[0] // rows
    back = parts_ref[0:rows, :].astype(F32)
    for piece in range(1, pieces):
        back = back + parts_ref[piece * rows:(piece + 1) * rows, :].astype(F32)
    volume = volume_ref[...] + column_ref[...] * back
    out_ref[...] = volume
    for ref in copies_ref:
        for piece in range(pieces):
            ref[piece * rows:(piece + 1) * rows, :] = volume.astype(BF16)


def exchange_cores(values, n_slab):
    return lax.ppermute(values, "slab", [(device, device ^ 1) for device in range(n_slab)])


def across(values, n_slab):
    groups = [list(range(core, n_slab, 2)) for core in (0, 1)]
    return lax.all_to_all(
        values, "slab", split_axis=0, concat_axis=0, axis_index_groups=groups, tiled=True)


def shards(sinogram, start_volume, slot_voxel, slot_ray, live_count, block_slope, block_offset):
    n_slab = lax.axis_size("slab")
    n_slots, depth = slot_voxel.shape
    capacity = n_slots // n_slab
    ray_tiles, frames, extent = sinogram.shape
    voxel_tiles = start_volume.shape[0]
    lines = n_slots * depth + capacity * depth
    rows = voxel_tiles * frames
    half = n_slab // 2
    n_wide, n_bank = (3, 2) if n_slab <= 32 else (1, 1)
    shape = jax.ShapeDtypeStruct
    sizes = (capacity, depth, frames)

    volume = start_volume.reshape(rows, extent)
    rounded = jnp.broadcast_to(volume.astype(BF16)[None], (half, rows, extent))
    near = across(rounded.reshape(half * rows, extent), n_slab)
    me = lax.axis_index("slab").astype(I32).reshape(1)

    alive = (jnp.arange(capacity)[None, :] < live_count[:, None]).reshape(1, n_slots)
    offset = jnp.where(alive, block_offset.T, FAR)
    slope = block_slope.T
    voxel = slot_voxel.T
    count = jnp.broadcast_to(live_count[:, None], (n_slab, capacity)).reshape(1, n_slots)
    fields = jnp.concatenate(
        [offset, slope, voxel.astype(F32), slot_ray.astype(F32).reshape(1, n_slots), count.astype(F32)],
        axis=0)
    n_fields = 3 * depth + 2
    packed = fields.reshape(n_fields, n_slab, capacity).transpose(1, 0, 2)
    padding = ((0, 0), (0, -n_fields % 8), (0, extent - capacity))
    got = lax.all_to_all(
        jnp.pad(packed, padding), "slab", split_axis=0, concat_axis=0, tiled=True)
    line_up = got[:, 2 * depth:n_fields, :capacity].transpose(1, 0, 2).reshape(depth + 2, n_slots)

    table = [shape((lines, extent), I32)] + [shape((lines, extent), F32)] * 3
    table += [shape((lines, extent), I32)] + [shape((lines, extent), F32)] * 2
    lists = [shape((8, n_slots // 2), I32)] * 2
    near_list, far_list, row_weight, *table = pl.pallas_call(
        functools.partial(setup_kernel, n_slab, capacity, depth, voxel_tiles, frames, extent),
        out_shape=lists + [shape((ray_tiles * frames, extent), F32)] + table,
        in_specs=[SMEM, VMEM, VMEM],
        out_specs=[VMEM] * 10,
        compiler_params=params(32),
        name="setup",
    )(me, line_up, got)

    column_weight = pl.pallas_call(
        functools.partial(column_kernel, frames),
        out_shape=shape((rows, extent), F32),
        in_specs=[VMEM] * 3,
        out_specs=VMEM,
        compiler_params=params(16),
        name="column_weight",
    )(offset, slope, voxel)

    rays = shape((ray_tiles * frames, extent), F32)
    wide = pltpu.VMEM((half * rows, extent), F32)
    forward_near = pl.pallas_call(
        functools.partial(near_forward, sizes),
        out_shape=rays,
        in_specs=[SMEM] + [VMEM] * 5,
        out_specs=VMEM,
        scratch_shapes=[wide] * n_wide,
        compiler_params=params(24),
        name="near_forward",
    )
    both_far = pl.pallas_call(
        functools.partial(far_both, sizes, n_wide),
        out_shape=[shape((half * rows, extent), BF16), rays],
        in_specs=[SMEM] + [VMEM] * 11,
        out_specs=[VMEM] * 2,
        scratch_shapes=[pltpu.VMEM(rays.shape, F32)] + [wide] * (n_wide + n_bank),
        compiler_params=params(28),
        name="far_both",
    )
    backward_near = pl.pallas_call(
        functools.partial(near_backward, sizes),
        out_shape=shape((half * rows, extent), F32),
        in_specs=[SMEM] + [VMEM] * 4,
        out_specs=VMEM,
        scratch_shapes=[wide] * (n_bank - 1),
        compiler_params=params(24),
        name="near_backward",
    )
    combine = pl.pallas_call(
        combine_kernel,
        out_shape=shape((half * rows, extent), BF16),
        in_specs=[VMEM] * 2,
        out_specs=VMEM,
        compiler_params=params(24),
        name="combine",
    )
    sino = sinogram.reshape(rays.shape)
    for turn in range(ITERS):
        copies = [shape((half * rows, extent), BF16)] if turn + 1 < ITERS else []
        far = exchange_cores(near, n_slab)
        partial = forward_near(near_list, near, *table[:4])
        far_sum, residual = both_far(far_list, far, partial, sino, row_weight, *table)
        swapped = exchange_cores(far_sum, n_slab)
        near_sum = backward_near(near_list, residual, *table[4:])
        parts = across(combine(near_sum, swapped), n_slab)
        volume, *rounded = pl.pallas_call(
            update_kernel,
            out_shape=[shape((rows, extent), F32)] + copies,
            in_specs=[VMEM] * 3,
            out_specs=[VMEM] * (1 + len(copies)),
            compiler_params=params(16),
            name="update",
        )(volume, column_weight, parts)
        if copies:
            near = across(rounded[0], n_slab)
    return volume.reshape(start_volume.shape)


def solution(mesh):
    in_specs = (
        P(("scan", "slab"), None, None),
        P(("scan", "slab"), None, None),
        P(("scan", "slab"), None),
        P(("scan", "slab")),
        P(("scan", "slab")),
        P(("scan", "slab"), None),
        P(("scan", "slab"), None),
    )
    out_specs = P(("scan", "slab"), None, None)
    return jax.shard_map(shards, mesh=mesh, in_specs=in_specs, out_specs=out_specs, check_vma=False)
```

time: 119 us -> 105 us (0.88)
  the two profiles are of different devices: /device:TPU:0 before, /device:TPU:2 now
where the time goes in v4:
time: 105 us; the launch traced here: 104 us
  Pallas kernels  36.1 us (34%)
  blocking collectives  24.9 us (24%)
  waiting for transfers between devices  21.2 us (20%)
  starting transfers between devices  14.3 us (14%)
  local copies, waits for them, and re-layouts  6.09 us (6%)
    all_to_all x2, blocking collectives, across(): lax.all_to_all(values, 'slab', split_axis=0, concat_axis=0, axis_index_gr...  24.9 us
    pallas_call x2, Pallas kernels, shards(): both_far(far_list, far, partial, sino, row_weight, *table)  14 us
    all_to_all x2, waiting for transfers between devices, across(): lax.all_to_all(values, 'slab', split_axis=0, concat_axis=0, axis_index_gr...  13.6 us
    all_to_all x2, starting transfers between devices, across(): lax.all_to_all(values, 'slab', split_axis=0, concat_axis=0, axis_index_gr...  10 us
    pallas_call x2, Pallas kernels, shards(): partial = forward_near(near_list, near, *table[:4])  9.79 us
    pallas_call x2, Pallas kernels, shards(): near_sum = backward_near(near_list, residual, *table[4:])  7.68 us
    all_to_all x1, waiting for transfers between devices, shards(): lax.all_to_all(jnp.pad(packed, padding), 'slab', split_axis=0, concat_axi...  7.52 us
    unnamed x26, local copies, waits for them, and re-layouts  3.97 us
  transfers between devices with their start and end apart: 7, of which 3 were waited for; matrix products, arithmetic and copies ran while one was open for 1% of the time, Pallas kernels for 20%

profile of v4, /device:TPU:2, one launch (start us, length us, event | category | flops | bytes accessed | tf_op | source)
XLA Modules:
  0.0 103.8 jit_solution(8680983821985566547)
XLA Ops:
  0.0 0.8 bitcast_convert_fusion.1
  0.8 0.7 broadcast_in_dim.16
  1.6 6.0 %all-to-all-start.1 = ((bf16[8,128,128]{2,1,0:T(8,128)(2,1)}), bf16[8,128,128]{2,1,0:T(8,128)(2,1)}, u32[]{:S(2)}, u32[]{:S(2)}) async-start(bf16[8,128,128]{2,1,0:T(8,128)(2,1)} %broadcast_in_dim.16), calls=%async_computation.1 | async-start | bytes 524288 | tf_op jit(solution)/shard_map/all_to_all | solution.py:287
  7.6 0.1 lt.25
  7.7 0.5 copy-done.10
  8.4 0.7 copy-done.7
  9.1 0.7 copy-done.8
  9.9 0.7 copy-done.11
  10.6 0.1 concatenate.15
  10.7 0.1 concatenate.16
  10.8 0.7 pad.4
  11.5 5.1 %all-to-all-done.1 = bf16[8,128,128]{2,1,0:T(8,128)(2,1)} async-done(((bf16[8,128,128]{2,1,0:T(8,128)(2,1)}), bf16[8,128,128]{2,1,0:T(8,128)(2,1)}, u32[]{:S(2)}, u32[]{:S(2)}) %all-to-all-start.1) | async-done | bytes 262176 | tf_op jit(solution)/shard_map/all_to_all | solution.py:287
  16.6 3.7 %all-to-all-start = ((f32[16,16,128]{2,1,0:T(8,128)}), f32[16,16,128]{2,1,0:T(8,128)S(1)}, u32[]{:S(2)}, u32[]{:S(2)}) async-start(f32[16,16,128]{2,1,0:T(8,128)} %pad.4), calls=%async_computation | async-start | bytes 262144 | tf_op jit(solution)/shard_map/all_to_all | solution.py:320
  20.3 0.4 collective-permute-start
  20.7 7.5 %all-to-all-done.got_ref = f32[16,16,128]{2,1,0:T(8,128)S(1)} async-done(((f32[16,16,128]{2,1,0:T(8,128)}), f32[16,16,128]{2,1,0:T(8,128)S(1)}, u32[]{:S(2)}, u32[]{:S(2)}) %all-to-all-start) | async-done | bytes 131104 | tf_op jit(solution)/shard_map/all_to_all | solution.py:320
  28.2 0.1 reshape.63.line_up_ref
  28.3 2.2 %setup.1 = (s32[8,128]{1,0:T(8,128)S(1)}, s32[8,128]{1,0:T(8,128)S(1)}, f32[256,128]{1,0:T(8,128)S(1)}, s32[1088,128]{1,0:T(8,128)S(1)}, f32[1088,128]{1,0:T(8,1...) custom-call(s32[1]{0:T(128)} %bitcast.4.me_ref, ...), custom_call_target="tpu_custom_call" | custom-call | tf_op jit(solution)/shard_map/setup/pallas_call | solution.py:327
  30.6 5.2 %near_forward.2.partial_ref = f32[256,128]{1,0:T(8,128)S(1)} custom-call(s32[8,128]{1,0:T(8,128)S(1)} %get-tuple-element.21.list_ref, bf16[1024,128]{1,0:T(8,128)(2,1)} %bitcast.7.values_ref, s32[1088,128]{1,0:T(8,128)S(1)} %get-tuple-element.23.refs_0_, f32[1088,128]{1,0:T(8,128)S(1)} %get-tuple-element.24.refs_1_, ...), custom_call_target="tpu_custom_call" | custom-call | tf_op jit(solution)/shard_map/near_forward/pallas_call | solution.py:386
  35.8 7.2 %far_both.2 = (bf16[1024,128]{1,0:T(8,128)(2,1)S(1)}, f32[256,128]{1,0:T(8,128)S(1)}) custom-call(s32[8,128]{1,0:T(8,128)S(1)} %get-tuple-element.22.list_ref, bf16[1024,128]{1,0:T(8,128)(2,1)} %collective-permute-done.values_ref, f32[256,128]{1,0:T(8,128)S(1)} %near_forward.2.partial_ref, bf16[256,128]{1,0:T(8,128)(2,1)S(1)} %bitcast.25, ...), custom_call_target="tpu_custom_call" | custom-call | tf_op jit(solution)/shard_map/far_both/pallas_call | solution.py:387
  43.1 3.8 %near_backward.2.near_ref = f32[1024,128]{1,0:T(8,128)S(1)} custom-call(s32[8,128]{1,0:T(8,128)S(1)} %get-tuple-element.21.list_ref, f32[256,128]{1,0:T(8,128)S(1)} %get-tuple-element.31.residual, s32[1088,128]{1,0:T(8,128)S(1)} %get-tuple-element.28.refs_4_.refs_0_, f32[1088,128]{1,0:T(8,128)S(1)} %get-tuple-element.29.refs_5_.refs_1_, ...), custom_call_target="tpu_custom_call" | custom-call | tf_op jit(solution)/shard_map/near_backward/pallas_call | solution.py:389
  47.1 0.7 copy-done.2
  47.8 4.1 %all-to-all-start.2 = ((bf16[8,128,128]{2,1,0:T(8,128)(2,1)}), bf16[8,128,128]{2,1,0:T(8,128)(2,1)}, u32[]{:S(2)}, u32[]{:S(2)}) async-start(bf16[8,128,128]{2,1,0:T(8,128)(2,1)} %bitcast.23), calls=%async_computation.2 | async-start | bytes 524288 | tf_op jit(solution)/shard_map/all_to_all | solution.py:287
  51.9 0.7 copy-done.9
  52.6 0.6 column_weight.1.column_ref
  53.2 8.5 %all-to-all-done.2 = bf16[8,128,128]{2,1,0:T(8,128)(2,1)} async-done(((bf16[8,128,128]{2,1,0:T(8,128)(2,1)}), bf16[8,128,128]{2,1,0:T(8,128)(2,1)}, u32[]{:S(2)}, u32[]{:S(2)}) %all-to-all-start.2) | async-done | bytes 262176 | tf_op jit(solution)/shard_map/all_to_all | solution.py:287
  61.7 1.0 update.2
  62.7 12.5 %all_to_all.46 = bf16[8,128,128]{2,1,0:T(8,128)(2,1)S(1)} all-to-all(bf16[8,128,128]{2,1,0:T(8,128)(2,1)S(1)} %bitcast.27), channel_id=1, replica_groups={{0,2,4,6,8,10,12,14},{1,3,5,7,9,11,13,15},{16,18,20,22,24,26,28,30},{17..., dimensions={0} | all-to-all | bytes 524288 | tf_op jit(solution)/shard_map/all_to_all | solution.py:287
  75.2 4.6 %near_forward.3.partial_ref = f32[256,128]{1,0:T(8,128)S(1)} custom-call(s32[8,128]{1,0:T(8,128)S(1)} %get-tuple-element.21.list_ref, bf16[1024,128]{1,0:T(8,128)(2,1)S(1)} %bitcast.21, s32[1088,128]{1,0:T(8,128)S(1)} %get-tuple-element.23.refs_0_, f32[1088,128]{1,0:T(8,128)S(1)} %get-tuple-element.24.refs_1_, f32[1088,128]{1,0:T(8,128)S(1)} %get-tuple-element.25.refs_2_, ...), custom_call_target="tpu_custom_call" | custom-call | tf_op jit(solution)/shard_map/near_forward/pallas_call | solution.py:386
  79.9 6.8 %far_both.3 = (bf16[1024,128]{1,0:T(8,128)(2,1)S(1)}, f32[256,128]{1,0:T(8,128)S(1)}) custom-call(s32[8,128]{1,0:T(8,128)S(1)} %get-tuple-element.22.list_ref, bf16[1024,128]{1,0:T(8,128)(2,1)S(1)} %collective-permute-done.2.values_ref, f32[256,128]{1,0:T(8,128)S(1)} %near_forward.3.partial_ref, bf16[256,128]{1,0:T(8,128)(2,1)S(1)} %bitcast.26, ...), custom_call_target="tpu_custom_call" | custom-call | tf_op jit(solution)/shard_map/far_both/pallas_call | solution.py:387
  86.8 3.8 %near_backward.3.near_ref = f32[1024,128]{1,0:T(8,128)S(1)} custom-call(s32[8,128]{1,0:T(8,128)S(1)} %get-tuple-element.21.list_ref, f32[256,128]{1,0:T(8,128)S(1)} %get-tuple-element.35.residual, s32[1088,128]{1,0:T(8,128)S(1)} %get-tuple-element.28.refs_4_.refs_0_, f32[1088,128]{1,0:T(8,128)S(1)} %get-tuple-element.29.refs_5_.refs_1_, ...), custom_call_target="tpu_custom_call" | custom-call | tf_op jit(solution)/shard_map/near_backward/pallas_call | solution.py:389
  90.7 12.4 %all_to_all.47 = bf16[8,128,128]{2,1,0:T(8,128)(2,1)S(1)} all-to-all(bf16[8,128,128]{2,1,0:T(8,128)(2,1)S(1)} %bitcast.24), channel_id=1, replica_groups={{0,2,4,6,8,10,12,14},{1,3,5,7,9,11,13,15},{16,18,20,22,24,26,28,30},{17..., dimensions={0} | all-to-all | bytes 524288 | tf_op jit(solution)/shard_map/all_to_all | solution.py:287
  103.2 0.7 update.3
  (43 shorter events, 0.8 us)
Async XLA Ops:
  1.6 6.0 %copy-start.12 = (s32[16]{0:T(128)S(1)}, s32[16]{0:T(128)}, u32[]{:S(2)}) copy-start(s32[16]{0:T(128)} %param.11) | copy-start | bytes 196
  1.6 15.0 %all-to-all-start.1 = ((bf16[8,128,128]{2,1,0:T(8,128)(2,1)}), bf16[8,128,128]{2,1,0:T(8,128)(2,1)}, u32[]{:S(2)}, u32[]{:S(2)}) async-start(bf16[8,128,128]{2,1,0:T(8,128)(2,1)} %broadcast_in_dim.16), calls=%async_computation.1 | async-start | bytes 524288 | tf_op jit(solution)/shard_map/all_to_all | solution.py:287
  7.6 0.7 copy-start.10
  8.3 0.7 copy-start.7
  9.1 0.7 copy-start.8
  9.9 0.7 copy-start.11
  16.6 11.6 %all-to-all-start = ((f32[16,16,128]{2,1,0:T(8,128)}), f32[16,16,128]{2,1,0:T(8,128)S(1)}, u32[]{:S(2)}, u32[]{:S(2)}) async-start(f32[16,16,128]{2,1,0:T(8,128)} %pad.4), calls=%async_computation | async-start | bytes 262144 | tf_op jit(solution)/shard_map/all_to_all | solution.py:320
  20.3 15.5 %collective-permute-start = (bf16[1024,128]{1,0:T(8,128)(2,1)}, bf16[1024,128]{1,0:T(8,128)(2,1)}, u32[]{:S(2)}, u32[]{:S(2)}) collective-permute-start(bf16[1024,128]{1,0:T(8,128)(2,1)} %bitcast.7.values_ref), channel_id=1, source_target_pairs={{0,1},{1,0},{2,3},{3,2},{4,5},{5,4},{6,7},{7,6},{8,9},{9,8},{10,11... | collective-permute-start | bytes 786440 | tf_op jit(solution)/shard_map/ppermute | solution.py:282
  30.6 5.3 %copy-start.3 = (f32[256,128]{1,0:T(8,128)}, f32[256,128]{1,0:T(8,128)S(1)}, u32[]{:S(2)}) copy-start(f32[256,128]{1,0:T(8,128)S(1)} %get-tuple-element.27.row_ref) | copy-start | bytes 393220
  30.6 12.5 %copy-start = (f32[1088,128]{1,0:T(8,128)}, f32[1088,128]{1,0:T(8,128)S(1)}, u32[]{:S(2)}) copy-start(f32[1088,128]{1,0:T(8,128)S(1)} %get-tuple-element.30.refs_6_.refs_2_) | copy-start | bytes 1671172
  30.6 5.2 %copy-start.5 = (bf16[32,8,128]{2,1,0:T(8,128)(2,1)S(1)}, bf16[32,8,128]{2,1,0:T(8,128)(2,1)}, u32[]{:S(2)}) copy-start(bf16[32,8,128]{2,1,0:T(8,128)(2,1)} %param.7) | copy-start | bytes 196612
  43.0 3.9 %collective-permute-start.1 = (bf16[1024,128]{1,0:T(8,128)(2,1)S(1)}, bf16[1024,128]{1,0:T(8,128)(2,1)S(1)}, u32[]{:S(2)}, u32[]{:S(2)}) collective-permute-start(bf16[1024,128]{1,0:T(8,128)(2,1)S(1)} %get-tuple-element.32), channel_id=1, source_target_pairs={{0,1},{1,0},{2,3},{3,2},{4,5},{5,4},{6,7},{7,6},{8,9},{9,8},{10,11... | collective-permute-start | bytes 786440 | tf_op jit(solution)/shard_map/ppermute | solution.py:282
  47.1 0.7 copy-start.2
  47.8 13.9 %all-to-all-start.2 = ((bf16[8,128,128]{2,1,0:T(8,128)(2,1)}), bf16[8,128,128]{2,1,0:T(8,128)(2,1)}, u32[]{:S(2)}, u32[]{:S(2)}) async-start(bf16[8,128,128]{2,1,0:T(8,128)(2,1)} %bitcast.23), calls=%async_computation.2 | async-start | bytes 524288 | tf_op jit(solution)/shard_map/all_to_all | solution.py:287
  51.8 9.9 %copy-start.6 = (f32[16,8,128]{2,1,0:T(8,128)S(1)}, f32[16,8,128]{2,1,0:T(8,128)}, u32[]{:S(2)}) copy-start(f32[16,8,128]{2,1,0:T(8,128)} %param.8) | copy-start | bytes 196612
  51.9 0.7 copy-start.9
  75.2 4.6 %copy-start.1 = (f32[1088,128]{1,0:T(8,128)S(1)}, f32[1088,128]{1,0:T(8,128)}, u32[]{:S(2)}) copy-start(f32[1088,128]{1,0:T(8,128)} %copy-done) | copy-start | bytes 1671172
  75.2 4.6 %copy-start.4 = (f32[256,128]{1,0:T(8,128)S(1)}, f32[256,128]{1,0:T(8,128)}, u32[]{:S(2)}) copy-start(f32[256,128]{1,0:T(8,128)} %copy-done.3) | copy-start | bytes 393220
  75.2 4.6 %collective-permute-start.2 = (bf16[1024,128]{1,0:T(8,128)(2,1)S(1)}, bf16[1024,128]{1,0:T(8,128)(2,1)S(1)}, u32[]{:S(2)}, u32[]{:S(2)}) collective-permute-start(bf16[1024,128]{1,0:T(8,128)(2,1)S(1)} %bitcast.20), channel_id=1, source_target_pairs={{0,1},{1,0},{2,3},{3,2},{4,5},{5,4},{6,7},{7,6},{8,9},{9,8},{10,11... | collective-permute-start | bytes 786440 | tf_op jit(solution)/shard_map/ppermute | solution.py:282
  86.7 3.9 %collective-permute-start.3 = (bf16[1024,128]{1,0:T(8,128)(2,1)S(1)}, bf16[1024,128]{1,0:T(8,128)(2,1)S(1)}, u32[]{:S(2)}, u32[]{:S(2)}) collective-permute-start(bf16[1024,128]{1,0:T(8,128)(2,1)S(1)} %get-tuple-element.36), channel_id=1, source_target_pairs={{0,1},{1,0},{2,3},{3,2},{4,5},{5,4},{6,7},{7,6},{8,9},{9,8},{10,11... | collective-permute-start | bytes 786440 | tf_op jit(solution)/shard_map/ppermute | solution.py:282

commit v5 on v4

v5 whole, which is shorter than its diff:
```python
import functools

import jax
import jax.numpy as jnp
from jax import lax
from jax.experimental import pallas as pl
from jax.experimental.pallas import tpu as pltpu
from jax.sharding import PartitionSpec as P

ITERS = 2
FAR = 1.0e6
CHUNK = 8
F32 = jnp.float32
BF16 = jnp.bfloat16
I32 = jnp.int32
HIGHEST = lax.Precision.HIGHEST
VMEM = pl.BlockSpec(memory_space=pltpu.VMEM)
SMEM = pl.BlockSpec(memory_space=pltpu.SMEM)


def hat(ray, centre):
    return jnp.maximum(0.0, 1.0 - jnp.abs(ray - centre)).astype(BF16)


def row_taps(offset, slope, extent):
    shape = (offset.shape[0], extent)
    ray = lax.broadcasted_iota(I32, shape, 1).astype(F32)
    offset = jnp.broadcast_to(offset, shape)
    slope = jnp.broadcast_to(slope, shape)
    middle = jnp.floor((ray - offset) / slope + 0.5)
    middle = jnp.minimum(jnp.maximum(middle, 1.0), extent - 2.0)
    weights = [hat(ray, offset + slope * (middle + step)) for step in (-1.0, 0.0, 1.0)]
    return middle.astype(I32), weights


def column_taps(offset, slope, extent):
    shape = (offset.shape[0], extent)
    voxel = lax.broadcasted_iota(I32, shape, 1).astype(F32)
    centre = jnp.broadcast_to(offset, shape) + jnp.broadcast_to(slope, shape) * voxel
    first = jnp.minimum(jnp.maximum(jnp.floor(centre), 0.0), extent - 2.0)
    weights = [hat(first + step, centre) for step in (0.0, 1.0)]
    return first.astype(I32), weights


def repeat_rows(values, times):
    return jnp.concatenate(
        [jnp.broadcast_to(values[row:row + 1, :], (times, values.shape[1]))
         for row in range(values.shape[0])], axis=0)


def contract_lanes(left, right):
    return lax.dot_general(
        left, right, (((1,), (1,)), ((), ())), precision=HIGHEST, preferred_element_type=F32)


def pack_kernel(capacity, volume_ref, offset_ref, slope_ref, voxel_ref, ray_ref, live_ref, out_ref):
    rows, extent = volume_ref.shape
    out_ref[0:rows, :] = volume_ref[...].astype(BF16)
    slots = ray_ref.shape[1]
    fields = []
    for ref in (offset_ref, slope_ref):
        left = ref[...]
        for addend in range(3):
            part = left.astype(BF16).astype(F32)
            fields.append(part)
            left = left - part
    fields.append(voxel_ref[...].astype(F32))
    fields.append(ray_ref[...].astype(F32))
    fields.append(per_slot(live_ref, slots, capacity))
    used = sum(field.shape[0] for field in fields)
    fields.append(jnp.zeros((-used % 16, slots), F32))
    fields = jnp.concatenate(fields, axis=0)
    height = fields.shape[0]
    for part in range(slots // extent):
        at = pl.ds(rows + part * height, height)
        out_ref[at, :] = fields[:, part * extent:(part + 1) * extent].astype(BF16)


def per_slot(live_ref, slots, capacity):
    targets = live_ref.shape[1]
    slot = lax.broadcasted_iota(I32, (targets, slots), 1)
    owner = lax.broadcasted_iota(I32, (targets, slots), 0)
    expand = (lax.div(slot, capacity) == owner).astype(F32)
    return jnp.dot(live_ref[...].astype(F32), expand, precision=HIGHEST, preferred_element_type=F32)


def setup_kernel(members, stride, sizes, tiles, me_ref, payload_ref,
                 list_ref, row_ref, fi_ref, f0_ref, f1_ref, f2_ref, bi_ref, b0_ref, b1_ref):
    capacity, depth, frames = sizes
    group = capacity * depth
    dead = members * group
    ray_tiles, extent = row_ref.shape
    height = -(-(7 * depth + 2) // 16) * 16
    tables = (fi_ref, f0_ref, f1_ref, f2_ref, bi_ref, b0_ref, b1_ref)
    lanes = list_ref.shape[1]
    first_slot = me_ref[0] * capacity
    part = lax.div(first_slot, extent)
    shift = lax.rem(extent - lax.rem(first_slot, extent), extent)

    def build(member, carry):
        total, lined = carry
        at = member * stride + tiles * frames + part * height
        raw = payload_ref[pl.ds(pl.multiple_of(at, 16), height), :].astype(F32)
        offset = (raw[0:depth] + raw[depth:2 * depth]) + raw[2 * depth:3 * depth]
        slope = (raw[3 * depth:4 * depth] + raw[4 * depth:5 * depth]) + raw[5 * depth:6 * depth]
        rest = raw[6 * depth:7 * depth + 2]
        fields = jnp.concatenate(
            [offset, slope, rest, jnp.zeros((16 - 3 * depth - 2, extent), F32)], axis=0)
        fields = pltpu.roll(fields, shift, axis=1)
        columns = fields.T
        summed = None
        for level in range(depth):
            offset = columns[0:capacity, level:level + 1]
            slope = columns[0:capacity, depth + level:depth + level + 1]
            middle, weights = row_taps(offset, slope, extent)
            first, pair = column_taps(offset, slope, extent)
            wide = [weight.astype(F32) for weight in weights]
            values = [middle] + wide + [first] + [weight.astype(F32) for weight in pair]
            at = member * group
            if not isinstance(at, int):
                at = pl.multiple_of(at, 8)
            at = pl.ds(at + level * capacity, capacity)
            for ref, value in zip(tables, values):
                ref[at, :] = value
            parts = (wide[0] + wide[1]) + wide[2]
            summed = parts if summed is None else summed + parts
        row = 3 * depth
        tile_of = jnp.broadcast_to(fields[row:row + 1, 0:capacity], (ray_tiles, capacity))
        count = jnp.broadcast_to(fields[row + 1:row + 2, 0:capacity], (ray_tiles, capacity))
        tile = lax.broadcasted_iota(I32, (ray_tiles, capacity), 0).astype(F32)
        within = lax.broadcasted_iota(I32, (ray_tiles, capacity), 1).astype(F32)
        hot = jnp.logical_and(tile_of == tile, within < count).astype(F32)
        total = total + jnp.dot(hot, summed, precision=HIGHEST, preferred_element_type=F32)
        lane = lax.broadcasted_iota(I32, fields.shape, 1)
        own = jnp.where(lane < capacity, fields, 0.0)
        if lanes > extent:
            own = jnp.concatenate(
                [own, jnp.zeros((fields.shape[0], lanes - extent), F32)], axis=1)
        return total, lined + pltpu.roll(own, member * capacity, axis=1)

    carry = jnp.zeros((ray_tiles, extent), F32), jnp.zeros((16, lanes), F32)
    if members <= 16:
        for member in range(members):
            carry = build(member, carry)
    else:
        carry = lax.fori_loop(0, members, build, carry)
    row_ref[...], lined = carry
    for ref in tables:
        ref[dead:, :] = jnp.zeros((group, extent), ref.dtype)

    slot = lax.broadcasted_iota(I32, (1, lanes), 1)
    member = lax.div(slot, capacity)
    within = lax.rem(slot, capacity)
    line = (member * group + within - dead).astype(F32)
    row = 2 * depth
    base = member.astype(F32) * tiles
    voxels = [(lined[row + level:row + level + 1] + base) * frames for level in range(depth)]
    ray = lined[3 * depth:3 * depth + 1] * frames
    table = jnp.concatenate([line, ray] + voxels + [jnp.zeros((6 - depth, lanes), F32)], axis=0)
    alive = jnp.logical_and(
        within.astype(F32) < lined[3 * depth + 1:3 * depth + 2], member < members).astype(F32)
    order = lax.broadcasted_iota(I32, (lanes, lanes), 0)
    earlier = (lax.broadcasted_iota(I32, (lanes, lanes), 1) < order).astype(F32)
    position = contract_lanes(jnp.broadcast_to(alive, (8, lanes)), earlier)[0:1]
    position = jnp.where(alive > 0.0, position, -1.0).astype(I32)
    choose = jnp.broadcast_to(position, (lanes, lanes)) == order
    packed = contract_lanes(table, choose.astype(F32))
    kind = lax.broadcasted_iota(I32, (8, lanes), 0)
    total = jnp.sum(alive, axis=1, keepdims=True)
    extra = jnp.where(kind == 0, float(dead), jnp.where(kind == 7, total, 0.0))
    list_ref[...] = (packed + extra + 0.5).astype(I32)


def column_kernel(sizes, offset_ref, slope_ref, voxel_ref, live_ref, out_ref):
    capacity, depth, frames = sizes
    tiles = out_ref.shape[0] // frames
    slots = offset_ref.shape[1]
    extent = out_ref.shape[1]
    offsets = offset_ref[...].T
    slopes = slope_ref[...].T
    within = lax.rem(lax.broadcasted_iota(I32, (1, slots), 1), capacity).astype(F32)
    alive = jnp.broadcast_to(within, (tiles, slots)) < per_slot(live_ref, slots, capacity)
    total = jnp.zeros((tiles, extent), F32)
    for level in range(depth):
        unused, pair = column_taps(
            offsets[:, level:level + 1], slopes[:, level:level + 1], extent)
        tile_of = jnp.broadcast_to(voxel_ref[level:level + 1, :], (tiles, slots))
        match = tile_of == lax.broadcasted_iota(I32, (tiles, slots), 0)
        hot = jnp.logical_and(match, alive).astype(F32).astype(BF16)
        for weight in pair:
            total += jnp.dot(hot, weight, preferred_element_type=F32)
    out_ref[...] = repeat_rows(1.0 / jnp.maximum(total, 1.0), frames)


def pick(values, index):
    return jnp.take_along_axis(values, index, axis=1, mode="promise_in_bounds")


def spread(ref, row, frames):
    return jnp.broadcast_to(ref[pl.ds(row, 1), :], (frames, ref.shape[1]))


def tile_at(start, frames):
    return pl.ds(pl.multiple_of(start, frames), frames)


def for_slots(list_ref, body):
    def some(step, carry):
        for place in range(CHUNK):
            body(step * CHUNK + place)
        return carry

    lax.fori_loop(0, lax.div(list_ref[7, 0] + (CHUNK - 1), CHUNK), some, 0)


def for_rows(rows, body):
    step = 128

    def some(number, carry):
        body(pl.ds(pl.multiple_of(number * step, step), step))
        return carry

    lax.fori_loop(0, rows // step, some, 0)


def project(sizes, stride, list_ref, values_ref, tables, projection, wides):
    capacity, depth, frames = sizes
    members = values_ref.shape[0] // stride
    rows = wides[0].shape[0] // members
    extent = values_ref.shape[1]

    def widen(member, carry):
        values = values_ref[pl.ds(pl.multiple_of(member * stride, 16), rows), :].astype(F32)
        at = pl.ds(pl.multiple_of(member * rows, rows), rows)
        wides[0][at, :] = values
        if len(wides) == 3:
            wides[1][at, :] = pltpu.roll(values, 1, axis=1)
            wides[2][at, :] = pltpu.roll(values, extent - 1, axis=1)
        return carry

    lax.fori_loop(0, members, widen, 0)

    def one(slot):
        line = list_ref[0, slot]
        total = None
        for level in range(depth):
            at = tile_at(list_ref[2 + level, slot], frames)
            row = line + level * capacity
            index = spread(tables[0], row, frames)
            if len(wides) == 3:
                taps = [pick(ref[at, :], index) for ref in (wides[1], wides[0], wides[2])]
            else:
                values = wides[0][at, :]
                taps = [pick(values, index + shift) for shift in (-1, 0, 1)]
            for ref, tap in zip(tables[1:], taps):
                term = spread(ref, row, frames) * tap
                total = term if total is None else total + term
        projection[tile_at(list_ref[1, slot], frames), :] += total.astype(BF16).astype(F32)

    for_slots(list_ref, one)


def backproject(sizes, list_ref, residual, tables, banks):
    capacity, depth, frames = sizes

    def clear(at):
        for bank in banks:
            bank[at, :] = jnp.zeros((at.size, bank.shape[1]), F32)

    for_rows(banks[0].shape[0], clear)

    def one(slot):
        line = list_ref[0, slot]
        values = residual[tile_at(list_ref[1, slot], frames), :]
        for level in range(depth):
            row = line + level * capacity
            index = spread(tables[0], row, frames)
            term = (spread(tables[1], row, frames) * pick(values, index)
                    + spread(tables[2], row, frames) * pick(values, index + 1))
            banks[level % len(banks)][tile_at(list_ref[2 + level, slot], frames), :] += term

    for_slots(list_ref, one)


def forward_kernel(sizes, stride, first, list_ref, values_ref, *refs):
    tables, refs = refs[:4], refs[4:]
    if not first:
        start_ref, refs = refs[0], refs[1:]
    projection, wides = refs[0], refs[1:]
    projection[...] = jnp.zeros_like(projection) if first else start_ref[...]
    project(sizes, stride, list_ref, values_ref, tables, projection, wides)


def residual_of(sizes, projection, sinogram_ref, row_refs):
    total = sum([ref[...] for ref in row_refs[1:]], row_refs[0][...])
    weight = repeat_rows(1.0 / jnp.maximum(total, 1.0), sizes[2])
    scaled = (sinogram_ref[...].astype(F32) - projection[...]) * weight
    return scaled.astype(BF16).astype(F32)


def turn_kernel(sizes, stride, n_rows, n_wide, first, list_ref, values_ref, *refs):
    forward, backward, refs = refs[:4], refs[4:7], refs[7:]
    sinogram_ref, row_refs, refs = refs[0], refs[1:1 + n_rows], refs[1 + n_rows:]
    if not first:
        start_ref, refs = refs[0], refs[1:]
    out_ref, residual, projection = refs[:3]
    wides, banks = refs[3:3 + n_wide], refs[3 + n_wide:]
    projection[...] = jnp.zeros_like(projection) if first else start_ref[...]
    project(sizes, stride, list_ref, values_ref, forward, projection, wides)
    residual[...] = residual_of(sizes, projection, sinogram_ref, row_refs)
    backproject(sizes, list_ref, residual, backward, banks)

    def finish(at):
        out_ref[at, :] = sum([bank[at, :] for bank in banks[1:]], banks[0][at, :]).astype(BF16)

    for_rows(out_ref.shape[0], finish)


def backward_kernel(sizes, list_ref, residual, *refs):
    tables, out_ref, banks = refs[:3], refs[3], refs[4:]
    backproject(sizes, list_ref, residual, tables, (out_ref,) + banks)

    def finish(at):
        out_ref[at, :] = sum([bank[at, :] for bank in banks], out_ref[at, :])

    if banks:
        for_rows(out_ref.shape[0], finish)


def combine_y_kernel(sum_ref, core_ref, out_ref):
    rows = sum_ref.shape[0]
    out_ref[...] = (sum_ref[...] + core_ref[rows:2 * rows, :].astype(F32)).astype(BF16)


def combine_z_kernel(sum_ref, core_ref, y_ref, own_ref, *piece_refs):
    rows = own_ref.shape[0]
    for place, ref in enumerate((own_ref,) + piece_refs):
        at = pl.ds(place * rows, rows)
        total = sum_ref[at, :] + core_ref[at, :].astype(F32) + y_ref[at, :].astype(F32)
        ref[...] = total.astype(ref.dtype)


def update_kernel(n_pieces, volume_ref, column_ref, *refs):
    back = refs[0][...]
    for ref in refs[1:n_pieces]:
        back = back + ref[...].astype(F32)
    volume = volume_ref[...] + column_ref[...] * back
    for ref in refs[n_pieces:]:
        ref[...] = volume.astype(ref.dtype)


def call(kernel, name, mib, in_specs, out_shape, *operands, scratch=()):
    one = not isinstance(out_shape, list)
    return pl.pallas_call(
        kernel,
        out_shape=out_shape,
        in_specs=in_specs,
        out_specs=VMEM if one else [VMEM] * len(out_shape),
        scratch_shapes=list(scratch),
        compiler_params=pltpu.CompilerParams(vmem_limit_bytes=mib * 1024 * 1024),
        name=name,
    )(*operands)


def exchange(values, n_slab, distance):
    return lax.ppermute(
        values, "slab", [(device, device ^ distance) for device in range(n_slab)])


def shards(sinogram, start_volume, slot_voxel, slot_ray, live_count, block_slope, block_offset):
    n_slab = lax.axis_size("slab")
    n_slots, depth = slot_voxel.shape
    capacity = n_slots // n_slab
    ray_tiles, frames, extent = sinogram.shape
    voxel_tiles = start_volume.shape[0]
    rows = voxel_tiles * frames
    sizes = (capacity, depth, frames)
    paired = n_slab == 16
    n_wide, n_bank = (3, 2) if paired else (1, 1)
    shape = jax.ShapeDtypeStruct
    rays = shape((ray_tiles * frames, extent), F32)
    volume = start_volume.reshape(rows, extent)
    sino = sinogram.reshape(rays.shape)
    me = lax.axis_index("slab").astype(I32).reshape(1)
    slots_by_depth = (block_offset.T, block_slope.T, slot_voxel.T)
    live = live_count.reshape(1, n_slab)
    height = -(-(7 * depth + 2) // 16) * 16 * (n_slots // extent)
    payload = call(
        functools.partial(pack_kernel, capacity), "pack", 16, [VMEM] * 6,
        shape((rows + height, extent), BF16),
        volume, *slots_by_depth, slot_ray.reshape(1, n_slots), live)

    def setup(values, members):
        group = capacity * depth
        lines = (members + 1) * group
        lanes = -(-members * capacity // 128) * 128
        table = [shape((lines, extent), I32)] + [shape((lines, extent), F32)] * 3
        table += [shape((lines, extent), I32)] + [shape((lines, extent), F32)] * 2
        out = [shape((8, lanes), I32), shape((ray_tiles, extent), F32)] + table
        stride = values.shape[0] // members
        found = call(
            functools.partial(setup_kernel, members, stride, sizes, voxel_tiles), "setup", 24,
            [SMEM, VMEM], out, me, values)
        return found[0], found[1], found[2:6], found[6:9]

    def wide(members):
        return pltpu.VMEM((members * rows, extent), F32)

    def forward(values, group, start, members):
        operands = [values, *group[2]] + ([] if start is None else [start])
        return call(
            functools.partial(forward_kernel, sizes, values.shape[0] // members, start is None),
            "forward", 16, [SMEM] + [VMEM] * len(operands), rays,
            group[0], *operands, scratch=[wide(members)] * n_wide)

    def turn(values, group, row_sums, start, members):
        operands = [values, *group[2], *group[3], sino, *row_sums] + ([] if start is None else [start])
        return call(
            functools.partial(turn_kernel, sizes, values.shape[0] // members, len(row_sums), n_wide,
                              start is None),
            "turn", 24 if paired else 40, [SMEM] + [VMEM] * len(operands),
            [shape((members * rows, extent), BF16), rays],
            group[0], *operands,
            scratch=[pltpu.VMEM(rays.shape, F32)] + [wide(members)] * (n_wide + n_bank))

    def backward(residual, group, members):
        return call(
            functools.partial(backward_kernel, sizes), "backward", 16, [SMEM] + [VMEM] * 4,
            shape((members * rows, extent), F32), group[0], residual, *group[3],
            scratch=[wide(members)] * (n_bank - 1))

    def update(volume, pieces, last):
        out = [shape((rows, extent), F32)] + ([] if last else [shape((rows, extent), BF16)])
        return call(
            functools.partial(update_kernel, len(pieces)), "update", 16,
            [VMEM] * (2 + len(pieces)), out, volume, column_weight, *pieces)

    column_weight = call(
        functools.partial(column_kernel, sizes), "column_weight", 16, [VMEM] * 4,
        shape((rows, extent), F32), *slots_by_depth, live)

    groups = None
    for sweep in range(ITERS):
        last = sweep + 1 == ITERS
        if paired:
            along_z = jnp.concatenate(
                [payload] + [exchange(payload, n_slab, distance) for distance in (4, 8, 12)], axis=0)
            along_y = exchange(along_z, n_slab, 2)
            other = exchange(jnp.concatenate([along_z, along_y], axis=0), n_slab, 1)
            if groups is None:
                groups = [setup(along_z, 4), setup(along_y, 4), setup(other, 8)]
                row_sums = [group[1] for group in groups]
            projection = forward(along_z, groups[0], None, 4)
            projection = forward(along_y, groups[1], projection, 4)
            other_sum, residual = turn(other, groups[2], row_sums, projection, 8)
            core_part = exchange(other_sum, n_slab, 1)
            y_sum = backward(residual, groups[1], 4)
            y_part = exchange(
                call(combine_y_kernel, "combine_y", 16, [VMEM] * 2,
                     shape((4 * rows, extent), BF16), y_sum, core_part), n_slab, 2)
            z_sum = backward(residual, groups[0], 4)
            own, *pieces = call(
                combine_z_kernel, "combine_z", 16, [VMEM] * 3,
                [shape((rows, extent), F32)] + [shape((rows, extent), BF16)] * 3,
                z_sum, core_part, y_part)
            pieces = [own] + [
                exchange(piece, n_slab, distance) for piece, distance in zip(pieces, (4, 8, 12))]
        else:
            everyone = lax.all_gather(payload, "slab", axis=0, tiled=True)
            if groups is None:
                groups = [setup(everyone, n_slab)]
                row_sums = [groups[0][1]]
            sums, residual = turn(everyone, groups[0], row_sums, None, n_slab)
            parts = lax.all_to_all(
                sums.reshape(n_slab, rows, extent), "slab", split_axis=0, concat_axis=0, tiled=True)
            pieces = [jnp.sum(parts.astype(F32), axis=0)]
        volume, *rounded = update(volume, pieces, last)
        if not last:
            payload = rounded[0]
    return volume.reshape(start_volume.shape)


def solution(mesh):
    in_specs = (
        P(("scan", "slab"), None, None),
        P(("scan", "slab"), None, None),
        P(("scan", "slab"), None),
        P(("scan", "slab")),
        P(("scan", "slab")),
        P(("scan", "slab"), None),
        P(("scan", "slab"), None),
    )
    out_specs = P(("scan", "slab"), None, None)
    return jax.shard_map(shards, mesh=mesh, in_specs=in_specs, out_specs=out_specs, check_vma=False)
```

time: 105 us -> 94.6 us (0.901)
  the two profiles are of different devices: /device:TPU:2 before, /device:TPU:0 now
where the time goes in v5:
time: 94.6 us; the launch traced here: 94.1 us
  Pallas kernels  35.9 us (38%)
  waiting for transfers between devices  32 us (34%)
  starting transfers between devices  23.5 us (25%)
  local copies, waits for them, and re-layouts  2.39 us (3%)
    pallas_call x21, Pallas kernels, call(): pl.pallas_call(kernel, out_shape=out_shape, in_specs=in_specs, out_specs=...  35.9 us
    ppermute x20, waiting for transfers between devices, exchange(): lax.ppermute(values, 'slab', [(device, device ^ distance) for device in r...  32 us
    ppermute x20, starting transfers between devices, exchange(): lax.ppermute(values, 'slab', [(device, device ^ distance) for device in r...  23.5 us
    unnamed x25, local copies, waits for them, and re-layouts  2.33 us
  transfers between devices with their start and end apart: 20, of which 11 were waited for; matrix products, arithmetic and copies ran while one was open for 0% of the time, Pallas kernels for 22%

profile of v5, /device:TPU:0, one launch (start us, length us, event | category | flops | bytes accessed | tf_op | source)
XLA Modules:
  0.0 94.1 jit_solution(11178657620545249615)
XLA Ops:
  2.4 3.0 %collective-permute-start = (bf16[192,128]{1,0:T(8,128)(2,1)S(1)}, bf16[192,128]{1,0:T(8,128)(2,1)S(1)}, u32[]{:S(2)}, u32[]{:S(2)}) collective-permute-start(bf16[192,128]{1,0:T(8,128)(2,1)S(1)} %pack.1), channel_id=1, source_target_pairs={{0,4},{1,5},{2,6},{3,7},{4,0},{5,1},{6,2},{7,3},{8,12},{9,13},{10,... | collective-permute-start | bytes 147464 | tf_op jit(solution)/shard_map/ppermute | solution.py:366
  5.4 2.6 %collective-permute-start.1 = (bf16[192,128]{1,0:T(8,128)(2,1)S(1)}, bf16[192,128]{1,0:T(8,128)(2,1)S(1)}, u32[]{:S(2)}, u32[]{:S(2)}) collective-permute-start(bf16[192,128]{1,0:T(8,128)(2,1)S(1)} %pack.1), channel_id=1, source_target_pairs={{0,8},{1,9},{2,10},{3,11},{4,12},{5,13},{6,14},{7,15},{8,0},{9,1},... | collective-permute-start | bytes 147464 | tf_op jit(solution)/shard_map/ppermute | solution.py:366
  8.0 3.3 %collective-permute-done.1 = bf16[192,128]{1,0:T(8,128)(2,1)S(1)} collective-permute-done((bf16[192,128]{1,0:T(8,128)(2,1)S(1)}, bf16[192,128]{1,0:T(8,128)(2,1)S(1)}, u32[]{:S(2)}, u32[]{:S(2)}) %collective-permute-start.1) | collective-permute-done | bytes 49184 | tf_op jit(solution)/shard_map/ppermute | solution.py:366
  11.3 2.6 %collective-permute-done.2 = bf16[192,128]{1,0:T(8,128)(2,1)S(1)} collective-permute-done((bf16[192,128]{1,0:T(8,128)(2,1)S(1)}, bf16[192,128]{1,0:T(8,128)(2,1)S(1)}, u32[]{:S(2)}, u32[]{:S(2)}) %collective-permute-start.2) | collective-permute-done | bytes 49184 | tf_op jit(solution)/shard_map/ppermute | solution.py:366
  13.9 1.6 %collective-permute-start.3 = (bf16[768,128]{1,0:T(8,128)(2,1)S(1)}, bf16[768,128]{1,0:T(8,128)(2,1)S(1)}, u32[]{:S(2)}, u32[]{:S(2)}) collective-permute-start(bf16[768,128]{1,0:T(8,128)(2,1)S(1)} %pad_maximum_fusion.payload_ref.values_ref), channel_id=1, source_target_pairs={{0,2},{1,3},{2,0},{3,1},{4,6},{5,7},{6,4},{7,5},{8,10},{9,11},{10,... | collective-permute-start | bytes 589832 | tf_op jit(solution)/shard_map/ppermute | solution.py:366
  15.5 4.1 %collective-permute-done.3.payload_ref.values_ref = bf16[768,128]{1,0:T(8,128)(2,1)S(1)} collective-permute-done((bf16[768,128]{1,0:T(8,128)(2,1)S(1)}, bf16[768,128]{1,0:T(8,128)(2,1)S(1)}, u32[]{:S(2)}, u32[]{:S(2)}) %collective-permute-start.3) | collective-permute-done | bytes 196640 | tf_op jit(solution)/shard_map/ppermute | solution.py:366
  19.8 1.1 %setup.3 = (s32[8,128]{1,0:T(8,128)S(1)}, f32[32,128]{1,0:T(8,128)S(1)}, s32[320,128]{1,0:T(8,128)S(1)}, f32[320,128]{1,0:T(8,128)S(1)}, f32[320,128]{1,0:T(8,12...) custom-call(s32[1]{0:T(128)} %bitcast.5.me_ref, ...), custom_call_target="tpu_custom_call" | custom-call | tf_op jit(solution)/shard_map/setup/pallas_call | solution.py:354
  20.9 2.3 %forward.4.refs_4_ = f32[256,128]{1,0:T(8,128)S(1)} custom-call(s32[8,128]{1,0:T(8,128)S(1)} %get-tuple-element.46.list_ref, bf16[768,128]{1,0:T(8,128)(2,1)S(1)} %pad_maximum_fusion.payload_ref.values_ref, s32[320,128]{1,0:T(8,128)S(1)} %get-tuple-element.63.refs_0_, f32[320,128]{1,0:T(8,128)S(1)} %get-tuple-element.64.refs_1_, ...), custom_call_target="tpu_custom_call" | custom-call | tf_op jit(solution)/shard_map/forward/pallas_call | solution.py:354
  23.2 1.1 %setup.5 = (s32[8,128]{1,0:T(8,128)S(1)}, f32[32,128]{1,0:T(8,128)S(1)}, s32[320,128]{1,0:T(8,128)S(1)}, f32[320,128]{1,0:T(8,128)S(1)}, f32[320,128]{1,0:T(8,12...) custom-call(s32[1]{0:T(128)} %bitcast.5.me_ref, ...), custom_call_target="tpu_custom_call" | custom-call | tf_op jit(solution)/shard_map/setup/pallas_call | solution.py:354
  24.4 2.6 %forward.5.refs_11_ = f32[256,128]{1,0:T(8,128)S(1)} custom-call(s32[8,128]{1,0:T(8,128)S(1)} %get-tuple-element.58.list_ref, bf16[768,128]{1,0:T(8,128)(2,1)S(1)} %collective-permute-done.3.payload_ref.values_ref, s32[320,128]{1,0:T(8,128)S(1)} %get-tuple-element.59.refs_0_, f32[320,128]{1,0:T(8,128)S(1)} %get-tuple-element.60.refs_1_, ...), custom_call_target="tpu_custom_call" | custom-call | tf_op jit(solution)/shard_map/forward/pallas_call | solution.py:354
  27.0 1.2 %setup.4 = (s32[8,128]{1,0:T(8,128)S(1)}, f32[32,128]{1,0:T(8,128)S(1)}, s32[576,128]{1,0:T(8,128)S(1)}, f32[576,128]{1,0:T(8,128)S(1)}, f32[576,128]{1,0:T(8,12...) custom-call(s32[1]{0:T(128)} %bitcast.5.me_ref, ...), custom_call_target="tpu_custom_call" | custom-call | tf_op jit(solution)/shard_map/setup/pallas_call | solution.py:354
  28.3 6.3 %turn.2 = (bf16[1024,128]{1,0:T(8,128)(2,1)S(1)}, f32[256,128]{1,0:T(8,128)S(1)}) custom-call(s32[8,128]{1,0:T(8,128)S(1)} %get-tuple-element.47.list_ref, bf16[1536,128]{1,0:T(8,128)(2,1)S(1)} %collective-permute-done.4.payload_ref.values_ref, s32[576,128]{1,0:T(8,128)S(1)} %get-tuple-element.48.refs_0_, f32[576,128]{1,0:T(8,128)S(1)} %get-tuple-element.49.refs_1_, ...), custom_call_target="tpu_custom_call" | custom-call | tf_op jit(solution)/shard_map/turn/pallas_call | solution.py:354
  35.4 2.2 %backward.5.sum_ref = f32[512,128]{1,0:T(8,128)S(1)} custom-call(s32[8,128]{1,0:T(8,128)S(1)} %get-tuple-element.58.list_ref, f32[256,128]{1,0:T(8,128)S(1)} %get-tuple-element.67.residual, s32[320,128]{1,0:T(8,128)S(1)} %get-tuple-element.72.refs_0_, f32[320,128]{1,0:T(8,128)S(1)} %get-tuple-element.73.refs_1_, f32[320,128]{1,0:T(8,128)S(1)} %get-tuple-element.74.refs_2_), custom_call_target="tpu_custom_call" | custom-call | tf_op jit(solution)/shard_map/backward/pallas_call | solution.py:354
  37.9 2.0 %backward.4.sum_ref = f32[512,128]{1,0:T(8,128)S(1)} custom-call(s32[8,128]{1,0:T(8,128)S(1)} %get-tuple-element.46.list_ref, f32[256,128]{1,0:T(8,128)S(1)} %get-tuple-element.67.residual, s32[320,128]{1,0:T(8,128)S(1)} %get-tuple-element.68.refs_0_, f32[320,128]{1,0:T(8,128)S(1)} %get-tuple-element.69.refs_1_, f32[320,128]{1,0:T(8,128)S(1)} %get-tuple-element.70.refs_2_), custom_call_target="tpu_custom_call" | custom-call | tf_op jit(solution)/shard_map/backward/pallas_call | solution.py:354
  39.9 3.0 %collective-permute-done.6.y_ref = bf16[512,128]{1,0:T(8,128)(2,1)S(1)} collective-permute-done((bf16[512,128]{1,0:T(8,128)(2,1)S(1)}, bf16[512,128]{1,0:T(8,128)(2,1)S(1)}, u32[]{:S(2)}, u32[]{:S(2)}) %collective-permute-start.6) | collective-permute-done | bytes 131104 | tf_op jit(solution)/shard_map/ppermute | solution.py:366
  43.0 2.2 %collective-permute-start.8 = (bf16[128,128]{1,0:T(8,128)(2,1)S(1)}, bf16[128,128]{1,0:T(8,128)(2,1)S(1)}, u32[]{:S(2)}, u32[]{:S(2)}) collective-permute-start(bf16[128,128]{1,0:T(8,128)(2,1)S(1)} %get-tuple-element.77), channel_id=1, source_target_pairs={{0,8},{1,9},{2,10},{3,11},{4,12},{5,13},{6,14},{7,15},{8,0},{9,1},... | collective-permute-start | bytes 98312 | tf_op jit(solution)/shard_map/ppermute | solution.py:366
  45.2 2.2 %collective-permute-start.9 = (bf16[128,128]{1,0:T(8,128)(2,1)S(1)}, bf16[128,128]{1,0:T(8,128)(2,1)S(1)}, u32[]{:S(2)}, u32[]{:S(2)}) collective-permute-start(bf16[128,128]{1,0:T(8,128)(2,1)S(1)} %get-tuple-element.78), channel_id=1, source_target_pairs={{0,12},{1,13},{2,14},{3,15},{4,8},{5,9},{6,10},{7,11},{8,4},{9,5},... | collective-permute-start | bytes 98312 | tf_op jit(solution)/shard_map/ppermute | solution.py:366
  48.0 2.9 %collective-permute-done.9.refs_3_ = bf16[128,128]{1,0:T(8,128)(2,1)S(1)} collective-permute-done((bf16[128,128]{1,0:T(8,128)(2,1)S(1)}, bf16[128,128]{1,0:T(8,128)(2,1)S(1)}, u32[]{:S(2)}, u32[]{:S(2)}) %collective-permute-start.9) | collective-permute-done | bytes 32800 | tf_op jit(solution)/shard_map/ppermute | solution.py:366
  51.1 2.9 %collective-permute-start.11 = (bf16[128,128]{1,0:T(8,128)(2,1)S(1)}, bf16[128,128]{1,0:T(8,128)(2,1)S(1)}, u32[]{:S(2)}, u32[]{:S(2)}) collective-permute-start(bf16[128,128]{1,0:T(8,128)(2,1)S(1)} %get-tuple-element.80), channel_id=1, source_target_pairs={{0,8},{1,9},{2,10},{3,11},{4,12},{5,13},{6,14},{7,15},{8,0},{9,1},... | collective-permute-start | bytes 98312 | tf_op jit(solution)/shard_map/ppermute | solution.py:366
  54.0 1.5 %collective-permute-start.12 = (bf16[128,128]{1,0:T(8,128)(2,1)S(1)}, bf16[128,128]{1,0:T(8,128)(2,1)S(1)}, u32[]{:S(2)}, u32[]{:S(2)}) collective-permute-start(bf16[128,128]{1,0:T(8,128)(2,1)S(1)} %get-tuple-element.80), channel_id=1, source_target_pairs={{0,12},{1,13},{2,14},{3,15},{4,8},{5,9},{6,10},{7,11},{8,4},{9,5},... | collective-permute-start | bytes 98312 | tf_op jit(solution)/shard_map/ppermute | solution.py:366
  56.0 3.7 %collective-permute-done.12 = bf16[128,128]{1,0:T(8,128)(2,1)S(1)} collective-permute-done((bf16[128,128]{1,0:T(8,128)(2,1)S(1)}, bf16[128,128]{1,0:T(8,128)(2,1)S(1)}, u32[]{:S(2)}, u32[]{:S(2)}) %collective-permute-start.12) | collective-permute-done | bytes 32800 | tf_op jit(solution)/shard_map/ppermute | solution.py:366
  59.7 0.9 collective-permute-start.13
  60.5 4.2 %collective-permute-done.13.values_ref = bf16[512,128]{1,0:T(8,128)(2,1)S(1)} collective-permute-done((bf16[512,128]{1,0:T(8,128)(2,1)S(1)}, bf16[512,128]{1,0:T(8,128)(2,1)S(1)}, u32[]{:S(2)}, u32[]{:S(2)}) %collective-permute-start.13) | collective-permute-done | bytes 131104 | tf_op jit(solution)/shard_map/ppermute | solution.py:366
  64.8 2.3 %forward.6.refs_4_ = f32[256,128]{1,0:T(8,128)S(1)} custom-call(s32[8,128]{1,0:T(8,128)S(1)} %get-tuple-element.46.list_ref, bf16[512,128]{1,0:T(8,128)(2,1)S(1)} %get-tuple-element.87.values_ref, s32[320,128]{1,0:T(8,128)S(1)} %get-tuple-element.63.refs_0_, f32[320,128]{1,0:T(8,128)S(1)} %get-tuple-element.64.refs_1_, ...), custom_call_target="tpu_custom_call" | custom-call | tf_op jit(solution)/shard_map/forward/pallas_call | solution.py:354
  67.1 2.6 %forward.7.refs_11_ = f32[256,128]{1,0:T(8,128)S(1)} custom-call(s32[8,128]{1,0:T(8,128)S(1)} %get-tuple-element.58.list_ref, bf16[512,128]{1,0:T(8,128)(2,1)S(1)} %collective-permute-done.13.values_ref, s32[320,128]{1,0:T(8,128)S(1)} %get-tuple-element.59.refs_0_, f32[320,128]{1,0:T(8,128)S(1)} %get-tuple-element.60.refs_1_, ...), custom_call_target="tpu_custom_call" | custom-call | tf_op jit(solution)/shard_map/forward/pallas_call | solution.py:354
  69.8 6.3 %turn.3 = (bf16[1024,128]{1,0:T(8,128)(2,1)S(1)}, f32[256,128]{1,0:T(8,128)S(1)}) custom-call(s32[8,128]{1,0:T(8,128)S(1)} %get-tuple-element.47.list_ref, bf16[1024,128]{1,0:T(8,128)(2,1)S(1)} %collective-permute-done.14.values_ref, s32[576,128]{1,0:T(8,128)S(1)} %get-tuple-element.48.refs_0_, f32[576,128]{1,0:T(8,128)S(1)} %get-tuple-element.49.refs_1_, ...), custom_call_target="tpu_custom_call" | custom-call | tf_op jit(solution)/shard_map/turn/pallas_call | solution.py:354
  76.8 2.2 %backward.7.sum_ref = f32[512,128]{1,0:T(8,128)S(1)} custom-call(s32[8,128]{1,0:T(8,128)S(1)} %get-tuple-element.58.list_ref, f32[256,128]{1,0:T(8,128)S(1)} %get-tuple-element.81.residual, s32[320,128]{1,0:T(8,128)S(1)} %get-tuple-element.72.refs_0_, f32[320,128]{1,0:T(8,128)S(1)} %get-tuple-element.73.refs_1_, f32[320,128]{1,0:T(8,128)S(1)} %get-tuple-element.74.refs_2_), custom_call_target="tpu_custom_call" | custom-call | tf_op jit(solution)/shard_map/backward/pallas_call | solution.py:354
  79.2 2.0 %backward.6.sum_ref = f32[512,128]{1,0:T(8,128)S(1)} custom-call(s32[8,128]{1,0:T(8,128)S(1)} %get-tuple-element.46.list_ref, f32[256,128]{1,0:T(8,128)S(1)} %get-tuple-element.81.residual, s32[320,128]{1,0:T(8,128)S(1)} %get-tuple-element.68.refs_0_, f32[320,128]{1,0:T(8,128)S(1)} %get-tuple-element.69.refs_1_, f32[320,128]{1,0:T(8,128)S(1)} %get-tuple-element.70.refs_2_), custom_call_target="tpu_custom_call" | custom-call | tf_op jit(solution)/shard_map/backward/pallas_call | solution.py:354
  81.2 3.2 %collective-permute-done.16.y_ref = bf16[512,128]{1,0:T(8,128)(2,1)S(1)} collective-permute-done((bf16[512,128]{1,0:T(8,128)(2,1)S(1)}, bf16[512,128]{1,0:T(8,128)(2,1)S(1)}, u32[]{:S(2)}, u32[]{:S(2)}) %collective-permute-start.16) | collective-permute-done | bytes 131104 | tf_op jit(solution)/shard_map/ppermute | solution.py:366
  84.5 3.2 %collective-permute-start.18 = (bf16[128,128]{1,0:T(8,128)(2,1)S(1)}, bf16[128,128]{1,0:T(8,128)(2,1)S(1)}, u32[]{:S(2)}, u32[]{:S(2)}) collective-permute-start(bf16[128,128]{1,0:T(8,128)(2,1)S(1)} %get-tuple-element.85), channel_id=1, source_target_pairs={{0,8},{1,9},{2,10},{3,11},{4,12},{5,13},{6,14},{7,15},{8,0},{9,1},... | collective-permute-start | bytes 98312 | tf_op jit(solution)/shard_map/ppermute | solution.py:366
  87.7 1.1 %collective-permute-start.19 = (bf16[128,128]{1,0:T(8,128)(2,1)S(1)}, bf16[128,128]{1,0:T(8,128)(2,1)S(1)}, u32[]{:S(2)}, u32[]{:S(2)}) collective-permute-start(bf16[128,128]{1,0:T(8,128)(2,1)S(1)} %get-tuple-element.86), channel_id=1, source_target_pairs={{0,12},{1,13},{2,14},{3,15},{4,8},{5,9},{6,10},{7,11},{8,4},{9,5},... | collective-permute-start | bytes 98312 | tf_op jit(solution)/shard_map/ppermute | solution.py:366
  89.6 3.8 %collective-permute-done.19.refs_3_ = bf16[128,128]{1,0:T(8,128)(2,1)S(1)} collective-permute-done((bf16[128,128]{1,0:T(8,128)(2,1)S(1)}, bf16[128,128]{1,0:T(8,128)(2,1)S(1)}, u32[]{:S(2)}, u32[]{:S(2)}) %collective-permute-start.19) | collective-permute-done | bytes 32800 | tf_op jit(solution)/shard_map/ppermute | solution.py:366
  (58 shorter events, 7.6 us)
Async XLA Ops:
  0.0 0.7 copy-start.8
  0.0 0.7 copy-start.4
  0.0 0.7 copy-start.3
  0.0 0.7 copy-start.7
  0.7 0.8 copy-start
  1.6 0.7 copy-start.5
  2.4 5.6 %collective-permute-start = (bf16[192,128]{1,0:T(8,128)(2,1)S(1)}, bf16[192,128]{1,0:T(8,128)(2,1)S(1)}, u32[]{:S(2)}, u32[]{:S(2)}) collective-permute-start(bf16[192,128]{1,0:T(8,128)(2,1)S(1)} %pack.1), channel_id=1, source_target_pairs={{0,4},{1,5},{2,6},{3,7},{4,0},{5,1},{6,2},{7,3},{8,12},{9,13},{10,... | collective-permute-start | bytes 147464 | tf_op jit(solution)/shard_map/ppermute | solution.py:366
  5.4 5.9 %collective-permute-start.1 = (bf16[192,128]{1,0:T(8,128)(2,1)S(1)}, bf16[192,128]{1,0:T(8,128)(2,1)S(1)}, u32[]{:S(2)}, u32[]{:S(2)}) collective-permute-start(bf16[192,128]{1,0:T(8,128)(2,1)S(1)} %pack.1), channel_id=1, source_target_pairs={{0,8},{1,9},{2,10},{3,11},{4,12},{5,13},{6,14},{7,15},{8,0},{9,1},... | collective-permute-start | bytes 147464 | tf_op jit(solution)/shard_map/ppermute | solution.py:366
  8.0 5.9 %collective-permute-start.2 = (bf16[192,128]{1,0:T(8,128)(2,1)S(1)}, bf16[192,128]{1,0:T(8,128)(2,1)S(1)}, u32[]{:S(2)}, u32[]{:S(2)}) collective-permute-start(bf16[192,128]{1,0:T(8,128)(2,1)S(1)} %pack.1), channel_id=1, source_target_pairs={{0,12},{1,13},{2,14},{3,15},{4,8},{5,9},{6,10},{7,11},{8,4},{9,5},... | collective-permute-start | bytes 147464 | tf_op jit(solution)/shard_map/ppermute | solution.py:366
  13.9 5.7 %collective-permute-start.3 = (bf16[768,128]{1,0:T(8,128)(2,1)S(1)}, bf16[768,128]{1,0:T(8,128)(2,1)S(1)}, u32[]{:S(2)}, u32[]{:S(2)}) collective-permute-start(bf16[768,128]{1,0:T(8,128)(2,1)S(1)} %pad_maximum_fusion.payload_ref.values_ref), channel_id=1, source_target_pairs={{0,2},{1,3},{2,0},{3,1},{4,6},{5,7},{6,4},{7,5},{8,10},{9,11},{10,... | collective-permute-start | bytes 589832 | tf_op jit(solution)/shard_map/ppermute | solution.py:366
  19.7 7.3 %collective-permute-start.4 = (bf16[1536,128]{1,0:T(8,128)(2,1)S(1)}, bf16[1536,128]{1,0:T(8,128)(2,1)S(1)}, u32[]{:S(2)}, u32[]{:S(2)}) collective-permute-start(bf16[1536,128]{1,0:T(8,128)(2,1)S(1)} %constant_dynamic-update-slice_fusion), channel_id=1, source_target_pairs={{0,1},{1,0},{2,3},{3,2},{4,5},{5,4},{6,7},{7,6},{8,9},{9,8},{10,11... | collective-permute-start | bytes 1179656 | tf_op jit(solution)/shard_map/ppermute | solution.py:366
  27.0 1.2 %copy-start.2 = (bf16[32,8,128]{2,1,0:T(8,128)(2,1)S(1)}, bf16[32,8,128]{2,1,0:T(8,128)(2,1)}, u32[]{:S(2)}) copy-start(bf16[32,8,128]{2,1,0:T(8,128)(2,1)} %param.7) | copy-start | bytes 196612
  34.6 3.0 %collective-permute-start.5 = (bf16[1024,128]{1,0:T(8,128)(2,1)S(1)}, bf16[1024,128]{1,0:T(8,128)(2,1)S(1)}, u32[]{:S(2)}, u32[]{:S(2)}) collective-permute-start(bf16[1024,128]{1,0:T(8,128)(2,1)S(1)} %get-tuple-element.71), channel_id=1, source_target_pairs={{0,1},{1,0},{2,3},{3,2},{4,5},{5,4},{6,7},{7,6},{8,9},{9,8},{10,11... | collective-permute-start | bytes 786440 | tf_op jit(solution)/shard_map/ppermute | solution.py:366
  37.7 5.2 %collective-permute-start.6 = (bf16[512,128]{1,0:T(8,128)(2,1)S(1)}, bf16[512,128]{1,0:T(8,128)(2,1)S(1)}, u32[]{:S(2)}, u32[]{:S(2)}) collective-permute-start(bf16[512,128]{1,0:T(8,128)(2,1)S(1)} %combine_y.2), channel_id=1, source_target_pairs={{0,2},{1,3},{2,0},{3,1},{4,6},{5,7},{6,4},{7,5},{8,10},{9,11},{10,... | collective-permute-start | bytes 393224 | tf_op jit(solution)/shard_map/ppermute | solution.py:366
  42.9 4.5 %copy-start.6 = (s32[256,4]{0,1:T(4,128)S(1)}, s32[256,4]{0,1:T(4,128)}, u32[]{:S(2)}) copy-start(s32[256,4]{0,1:T(4,128)} %param.9) | copy-start | bytes 12292
  42.9 8.0 %copy-start.1 = (f32[16,8,128]{2,1,0:T(8,128)S(1)}, f32[16,8,128]{2,1,0:T(8,128)}, u32[]{:S(2)}) copy-start(f32[16,8,128]{2,1,0:T(8,128)} %param.8) | copy-start | bytes 196612
  42.9 5.1 %collective-permute-start.7 = (bf16[128,128]{1,0:T(8,128)(2,1)S(1)}, bf16[128,128]{1,0:T(8,128)(2,1)S(1)}, u32[]{:S(2)}, u32[]{:S(2)}) collective-permute-start(bf16[128,128]{1,0:T(8,128)(2,1)S(1)} %get-tuple-element.76), channel_id=1, source_target_pairs={{0,4},{1,5},{2,6},{3,7},{4,0},{5,1},{6,2},{7,3},{8,12},{9,13},{10,... | collective-permute-start | bytes 98312 | tf_op jit(solution)/shard_map/ppermute | solution.py:366
  43.0 5.0 %collective-permute-start.8 = (bf16[128,128]{1,0:T(8,128)(2,1)S(1)}, bf16[128,128]{1,0:T(8,128)(2,1)S(1)}, u32[]{:S(2)}, u32[]{:S(2)}) collective-permute-start(bf16[128,128]{1,0:T(8,128)(2,1)S(1)} %get-tuple-element.77), channel_id=1, source_target_pairs={{0,8},{1,9},{2,10},{3,11},{4,12},{5,13},{6,14},{7,15},{8,0},{9,1},... | collective-permute-start | bytes 98312 | tf_op jit(solution)/shard_map/ppermute | solution.py:366
  45.2 5.7 %collective-permute-start.9 = (bf16[128,128]{1,0:T(8,128)(2,1)S(1)}, bf16[128,128]{1,0:T(8,128)(2,1)S(1)}, u32[]{:S(2)}, u32[]{:S(2)}) collective-permute-start(bf16[128,128]{1,0:T(8,128)(2,1)S(1)} %get-tuple-element.78), channel_id=1, source_target_pairs={{0,12},{1,13},{2,14},{3,15},{4,8},{5,9},{6,10},{7,11},{8,4},{9,5},... | collective-permute-start | bytes 98312 | tf_op jit(solution)/shard_map/ppermute | solution.py:366
  51.0 4.5 %collective-permute-start.10 = (bf16[128,128]{1,0:T(8,128)(2,1)S(1)}, bf16[128,128]{1,0:T(8,128)(2,1)S(1)}, u32[]{:S(2)}, u32[]{:S(2)}) collective-permute-start(bf16[128,128]{1,0:T(8,128)(2,1)S(1)} %get-tuple-element.80), channel_id=1, source_target_pairs={{0,4},{1,5},{2,6},{3,7},{4,0},{5,1},{6,2},{7,3},{8,12},{9,13},{10,... | collective-permute-start | bytes 98312 | tf_op jit(solution)/shard_map/ppermute | solution.py:366
  51.1 4.9 %collective-permute-start.11 = (bf16[128,128]{1,0:T(8,128)(2,1)S(1)}, bf16[128,128]{1,0:T(8,128)(2,1)S(1)}, u32[]{:S(2)}, u32[]{:S(2)}) collective-permute-start(bf16[128,128]{1,0:T(8,128)(2,1)S(1)} %get-tuple-element.80), channel_id=1, source_target_pairs={{0,8},{1,9},{2,10},{3,11},{4,12},{5,13},{6,14},{7,15},{8,0},{9,1},... | collective-permute-start | bytes 98312 | tf_op jit(solution)/shard_map/ppermute | solution.py:366
  54.0 5.7 %collective-permute-start.12 = (bf16[128,128]{1,0:T(8,128)(2,1)S(1)}, bf16[128,128]{1,0:T(8,128)(2,1)S(1)}, u32[]{:S(2)}, u32[]{:S(2)}) collective-permute-start(bf16[128,128]{1,0:T(8,128)(2,1)S(1)} %get-tuple-element.80), channel_id=1, source_target_pairs={{0,12},{1,13},{2,14},{3,15},{4,8},{5,9},{6,10},{7,11},{8,4},{9,5},... | collective-permute-start | bytes 98312 | tf_op jit(solution)/shard_map/ppermute | solution.py:366
  59.7 5.0 %collective-permute-start.13 = (bf16[512,128]{1,0:T(8,128)(2,1)S(1)}, bf16[512,128]{1,0:T(8,128)(2,1)S(1)}, u32[]{:S(2)}, u32[]{:S(2)}) collective-permute-start(bf16[512,128]{1,0:T(8,128)(2,1)S(1)} %get-tuple-element.87.values_ref), channel_id=1, source_target_pairs={{0,2},{1,3},{2,0},{3,1},{4,6},{5,7},{6,4},{7,5},{8,10},{9,11},{10,... | collective-permute-start | bytes 393224 | tf_op jit(solution)/shard_map/ppermute | solution.py:366
  64.7 5.0 %collective-permute-start.14 = (bf16[1024,128]{1,0:T(8,128)(2,1)S(1)}, bf16[1024,128]{1,0:T(8,128)(2,1)S(1)}, u32[]{:S(2)}, u32[]{:S(2)}) collective-permute-start(bf16[1024,128]{1,0:T(8,128)(2,1)S(1)} %constant_dynamic-update-slice_fusion.9), channel_id=1, source_target_pairs={{0,1},{1,0},{2,3},{3,2},{4,5},{5,4},{6,7},{7,6},{8,9},{9,8},{10,11... | collective-permute-start | bytes 786440 | tf_op jit(solution)/shard_map/ppermute | solution.py:366
  76.0 3.0 %collective-permute-start.15 = (bf16[1024,128]{1,0:T(8,128)(2,1)S(1)}, bf16[1024,128]{1,0:T(8,128)(2,1)S(1)}, u32[]{:S(2)}, u32[]{:S(2)}) collective-permute-start(bf16[1024,128]{1,0:T(8,128)(2,1)S(1)} %get-tuple-element.82), channel_id=1, source_target_pairs={{0,1},{1,0},{2,3},{3,2},{4,5},{5,4},{6,7},{7,6},{8,9},{9,8},{10,11... | collective-permute-start | bytes 786440 | tf_op jit(solution)/shard_map/ppermute | solution.py:366
  79.1 5.2 %collective-permute-start.16 = (bf16[512,128]{1,0:T(8,128)(2,1)S(1)}, bf16[512,128]{1,0:T(8,128)(2,1)S(1)}, u32[]{:S(2)}, u32[]{:S(2)}) collective-permute-start(bf16[512,128]{1,0:T(8,128)(2,1)S(1)} %combine_y.3), channel_id=1, source_target_pairs={{0,2},{1,3},{2,0},{3,1},{4,6},{5,7},{6,4},{7,5},{8,10},{9,11},{10,... | collective-permute-start | bytes 393224 | tf_op jit(solution)/shard_map/ppermute | solution.py:366
  84.4 4.5 %collective-permute-start.17 = (bf16[128,128]{1,0:T(8,128)(2,1)S(1)}, bf16[128,128]{1,0:T(8,128)(2,1)S(1)}, u32[]{:S(2)}, u32[]{:S(2)}) collective-permute-start(bf16[128,128]{1,0:T(8,128)(2,1)S(1)} %get-tuple-element.84), channel_id=1, source_target_pairs={{0,4},{1,5},{2,6},{3,7},{4,0},{5,1},{6,2},{7,3},{8,12},{9,13},{10,... | collective-permute-start | bytes 98312 | tf_op jit(solution)/shard_map/ppermute | solution.py:366
  84.5 5.1 %collective-permute-start.18 = (bf16[128,128]{1,0:T(8,128)(2,1)S(1)}, bf16[128,128]{1,0:T(8,128)(2,1)S(1)}, u32[]{:S(2)}, u32[]{:S(2)}) collective-permute-start(bf16[128,128]{1,0:T(8,128)(2,1)S(1)} %get-tuple-element.85), channel_id=1, source_target_pairs={{0,8},{1,9},{2,10},{3,11},{4,12},{5,13},{6,14},{7,15},{8,0},{9,1},... | collective-permute-start | bytes 98312 | tf_op jit(solution)/shard_map/ppermute | solution.py:366
  87.7 5.7 %collective-permute-start.19 = (bf16[128,128]{1,0:T(8,128)(2,1)S(1)}, bf16[128,128]{1,0:T(8,128)(2,1)S(1)}, u32[]{:S(2)}, u32[]{:S(2)}) collective-permute-start(bf16[128,128]{1,0:T(8,128)(2,1)S(1)} %get-tuple-element.86), channel_id=1, source_target_pairs={{0,12},{1,13},{2,14},{3,15},{4,8},{5,9},{6,10},{7,11},{8,4},{9,5},... | collective-permute-start | bytes 98312 | tf_op jit(solution)/shard_map/ppermute | solution.py:366

commit v6 on v5

--- a/solution.py
+++ b/solution.py
@@ -16,6 +16,7 @@
 HIGHEST = lax.Precision.HIGHEST
 VMEM = pl.BlockSpec(memory_space=pltpu.VMEM)
 SMEM = pl.BlockSpec(memory_space=pltpu.SMEM)
+ANY = pl.BlockSpec(memory_space=pl.ANY)
 
 
 def hat(ray, centre):
@@ -53,7 +54,16 @@
         left, right, (((1,), (1,)), ((), ())), precision=HIGHEST, preferred_element_type=F32)
 
 
-def pack_kernel(capacity, volume_ref, offset_ref, slope_ref, voxel_ref, ray_ref, live_ref, out_ref):
+def pack_kernel(capacity, *refs):
+    sources, out_ref, loaded, arrived = refs[:6], refs[6], refs[7:13], refs[13]
+    copies = [
+        pltpu.make_async_copy(source, ref, arrived.at[place])
+        for place, (source, ref) in enumerate(zip(sources, loaded))]
+    for copy in copies:
+        copy.start()
+    for copy in copies:
+        copy.wait()
+    volume_ref, offset_ref, slope_ref, voxel_ref, ray_ref, live_ref = loaded
     rows, extent = volume_ref.shape
     out_ref[0:rows, :] = volume_ref[...].astype(BF16)
     slots = ray_ref.shape[1]
@@ -332,12 +342,18 @@
     out_ref[...] = (sum_ref[...] + core_ref[rows:2 * rows, :].astype(F32)).astype(BF16)
 
 
-def combine_z_kernel(sum_ref, core_ref, y_ref, own_ref, *piece_refs):
-    rows = own_ref.shape[0]
-    for place, ref in enumerate((own_ref,) + piece_refs):
-        at = pl.ds(place * rows, rows)
-        total = sum_ref[at, :] + core_ref[at, :].astype(F32) + y_ref[at, :].astype(F32)
-        ref[...] = total.astype(ref.dtype)
+def combine_z_kernel(sum_ref, core_ref, y_ref, out_ref):
+    def add(at):
+        out_ref[at, :] = sum_ref[at, :] + core_ref[at, :].astype(F32) + y_ref[at, :].astype(F32)
+
+    for_rows(out_ref.shape[0], add)
+
+
+def join_kernel(z_ref, y_ref, after_ref, out_ref):
+    del after_ref
+    rows = z_ref.shape[0]
+    out_ref[0:rows, :] = z_ref[...]
+    out_ref[rows:2 * rows, :] = y_ref[...]
 
 
 def update_kernel(n_pieces, volume_ref, column_ref, *refs):
@@ -385,10 +401,12 @@
     slots_by_depth = (block_offset.T, block_slope.T, slot_voxel.T)
     live = live_count.reshape(1, n_slab)
     height = -(-(7 * depth + 2) // 16) * 16 * (n_slots // extent)
+    operands = (volume, *slots_by_depth, slot_ray.reshape(1, n_slots), live)
     payload = call(
-        functools.partial(pack_kernel, capacity), "pack", 16, [VMEM] * 6,
-        shape((rows + height, extent), BF16),
-        volume, *slots_by_depth, slot_ray.reshape(1, n_slots), live)
+        functools.partial(pack_kernel, capacity), "pack", 16, [ANY] * 6,
+        shape((rows + height, extent), BF16), *operands,
+        scratch=[pltpu.VMEM(operand.shape, operand.dtype) for operand in operands]
+        + [pltpu.SemaphoreType.DMA((6,))])
 
     def setup(values, members):
         group = capacity * depth
@@ -443,14 +461,20 @@
     for sweep in range(ITERS):
         last = sweep + 1 == ITERS
         if paired:
-            along_z = jnp.concatenate(
-                [payload] + [exchange(payload, n_slab, distance) for distance in (4, 8, 12)], axis=0)
+            columns = [list(range(place, n_slab, 4)) for place in range(4)]
+            along_z = lax.all_gather(
+                payload, "slab", axis=0, axis_index_groups=columns, tiled=True)
             along_y = exchange(along_z, n_slab, 2)
-            other = exchange(jnp.concatenate([along_z, along_y], axis=0), n_slab, 1)
-            if groups is None:
-                groups = [setup(along_z, 4), setup(along_y, 4), setup(other, 8)]
+            if sweep == 0:
+                groups = [setup(along_z, 4)]
+            projection = forward(along_z, groups[0], None, 4)
+            stride = along_z.shape[0]
+            other = exchange(
+                call(join_kernel, "join", 16, [VMEM, VMEM, ANY],
+                     shape((2 * stride, extent), BF16), along_z, along_y, projection), n_slab, 1)
+            if sweep == 0:
+                groups += [setup(along_y, 4), setup(other, 8)]
                 row_sums = [group[1] for group in groups]
-            projection = forward(along_z, groups[0], None, 4)
             projection = forward(along_y, groups[1], projection, 4)
             other_sum, residual = turn(other, groups[2], row_sums, projection, 8)
             core_part = exchange(other_sum, n_slab, 1)
@@ -459,12 +483,11 @@
                 call(combine_y_kernel, "combine_y", 16, [VMEM] * 2,
                      shape((4 * rows, extent), BF16), y_sum, core_part), n_slab, 2)
             z_sum = backward(residual, groups[0], 4)
-            own, *pieces = call(
-                combine_z_kernel, "combine_z", 16, [VMEM] * 3,
-                [shape((rows, extent), F32)] + [shape((rows, extent), BF16)] * 3,
+            total = call(
+                combine_z_kernel, "combine_z", 16, [VMEM] * 3, shape((4 * rows, extent), F32),
                 z_sum, core_part, y_part)
-            pieces = [own] + [
-                exchange(piece, n_slab, distance) for piece, distance in zip(pieces, (4, 8, 12))]
+            pieces = [lax.psum_scatter(
+                total, "slab", scatter_dimension=0, axis_index_groups=columns, tiled=True)]
         else:
             everyone = lax.all_gather(payload, "slab", axis=0, tiled=True)
             if groups is None:

time: 94.6 us -> 139 us (1.47)
  blocking collectives: 0 us -> 29 us
  starting transfers between devices: 23.5 us -> 5.13 us
  between operations: 0.28 us -> 13.9 us
  waiting for transfers between devices: 32 us -> 41.9 us
  local copies, waits for them, and re-layouts: 2.39 us -> 9.69 us
  Pallas kernels: 35.9 us -> 37.5 us
    reduce_scatter x0 -> x2, waiting for transfers between devices: none -> 35 us  [shards(): lax.psum_scatter(total, 'slab', scatter_dimension=0, axis_index_groups=co...]
    all_gather x0 -> x2, blocking collectives: none -> 29 us  [shards(): lax.all_gather(payload, 'slab', axis=0, axis_index_groups=columns, tiled=...]
    ppermute x20 -> x8, waiting for transfers between devices: 32 us -> 6.92 us  [exchange(): lax.ppermute(values, 'slab', [(device, device ^ distance) for device in r...]
    ppermute x20 -> x8, starting transfers between devices: 23.5 us -> 5.09 us  [exchange(): lax.ppermute(values, 'slab', [(device, device ^ distance) for device in r...]
    unnamed x25 -> x80, local copies, waits for them, and re-layouts: 2.33 us -> 9.69 us
    pallas_call x21 -> x23, Pallas kernels: 35.9 us -> 37.5 us  [call(): pl.pallas_call(kernel, out_shape=out_shape, in_specs=in_specs, out_specs=...]
  transfers between devices with their start and end apart: 20 -> 10, of which waited for: 11 -> 6; matrix products, arithmetic and copies ran while one was open for 0% -> 0% of each run, Pallas kernels for 22% -> 14%
where the time goes in v6:
time: 139 us; the launch traced here: 137 us
  waiting for transfers between devices  41.9 us (30%)
  Pallas kernels  37.5 us (27%)
  blocking collectives  29 us (21%)
  between operations  13.9 us (10%)
  local copies, waits for them, and re-layouts  9.69 us (7%)
  starting transfers between devices  5.13 us (4%)
    pallas_call x23, Pallas kernels, call(): pl.pallas_call(kernel, out_shape=out_shape, in_specs=in_specs, out_specs=...  37.5 us
    reduce_scatter x2, waiting for transfers between devices, shards(): lax.psum_scatter(total, 'slab', scatter_dimension=0, axis_index_groups=co...  35 us
    all_gather x2, blocking collectives, shards(): lax.all_gather(payload, 'slab', axis=0, axis_index_groups=columns, tiled=...  29 us
    unnamed x80, local copies, waits for them, and re-layouts  9.69 us
    ppermute x8, waiting for transfers between devices, exchange(): lax.ppermute(values, 'slab', [(device, device ^ distance) for device in r...  6.92 us
    ppermute x8, starting transfers between devices, exchange(): lax.ppermute(values, 'slab', [(device, device ^ distance) for device in r...  5.09 us
  transfers between devices with their start and end apart: 10, of which 6 were waited for; matrix products, arithmetic and copies ran while one was open for 0% of the time, Pallas kernels for 14%

profile of v6, /device:TPU:0, one launch (start us, length us, event | category | flops | bytes accessed | tf_op | source)
XLA Modules:
  0.0 137.1 jit_solution(2845613922396008720)
XLA Ops:
  7.3 0.8 copy-done.13
  8.1 0.7 copy-done.35
  9.1 15.5 %all_gather.6.payload_ref.values_ref.z_ref = bf16[768,128]{1,0:T(8,128)(2,1)S(1)} all-gather(bf16[192,128]{1,0:T(8,128)(2,1)S(1)} %pack.1), channel_id=1, replica_groups={{0,4,8,12},{1,5,9,13},{2,6,10,14},{3,7,11,15},{16,20,24,28},{17,21,25,2..., dimensions={0}, use_global_device_ids=true | all-gather | bytes 245760 | tf_op jit(solution)/shard_map/all_gather | solution.py:465
  24.5 1.5 %collective-permute-start = (bf16[768,128]{1,0:T(8,128)(2,1)S(1)}, bf16[768,128]{1,0:T(8,128)(2,1)S(1)}, u32[]{:S(2)}, u32[]{:S(2)}) collective-permute-start(bf16[768,128]{1,0:T(8,128)(2,1)S(1)} %all_gather.6.payload_ref.values_ref.z_ref), channel_id=1, source_target_pairs={{0,2},{1,3},{2,0},{3,1},{4,6},{5,7},{6,4},{7,5},{8,10},{9,11},{10,... | collective-permute-start | bytes 589832 | tf_op jit(solution)/shard_map/ppermute | solution.py:382
  26.0 1.1 setup.3
  27.2 2.6 %forward.4.after_ref.refs_4_ = f32[256,128]{1,0:T(8,128)S(1)} custom-call(s32[8,128]{1,0:T(8,128)S(1)} %get-tuple-element.38.list_ref, bf16[768,128]{1,0:T(8,128)(2,1)S(1)} %all_gather.6.payload_ref.values_ref.z_ref, s32[320,128]{1,0:T(8,128)S(1)} %get-tuple-element.39.refs_0_, f32[320,128]{1,0:T(8,128)S(1)} %get-tuple-element.40.refs_1_, ...), custom_call_target="tpu_custom_call" | custom-call | tf_op jit(solution)/shard_map/forward/pallas_call | solution.py:370
  30.3 1.1 setup.5
  31.5 1.8 %forward.5.refs_11_ = f32[256,128]{1,0:T(8,128)S(1)} custom-call(s32[8,128]{1,0:T(8,128)S(1)} %get-tuple-element.54.list_ref, bf16[768,128]{1,0:T(8,128)(2,1)S(1)} %collective-permute-done.y_ref.payload_ref.values_ref, s32[320,128]{1,0:T(8,128)S(1)} %get-tuple-element.55.refs_0_, f32[320,128]{1,0:T(8,128)S(1)} %get-tuple-element.56.refs_1_, ...), custom_call_target="tpu_custom_call" | custom-call | tf_op jit(solution)/shard_map/forward/pallas_call | solution.py:370
  33.4 1.2 setup.4
  35.2 7.3 %turn.2 = (bf16[1024,128]{1,0:T(8,128)(2,1)S(1)}, f32[256,128]{1,0:T(8,128)S(1)}) custom-call(s32[8,128]{1,0:T(8,128)S(1)} %get-tuple-element.43.list_ref, bf16[1536,128]{1,0:T(8,128)(2,1)S(1)} %collective-permute-done.1.payload_ref.values_ref, s32[576,128]{1,0:T(8,128)S(1)} %get-tuple-element.44.refs_0_, f32[576,128]{1,0:T(8,128)S(1)} %get-tuple-element.45.refs_1_, ...), custom_call_target="tpu_custom_call" | custom-call | tf_op jit(solution)/shard_map/turn/pallas_call | solution.py:370
  42.6 1.5 %backward.5.sum_ref = f32[512,128]{1,0:T(8,128)S(1)} custom-call(s32[8,128]{1,0:T(8,128)S(1)} %get-tuple-element.54.list_ref, f32[256,128]{1,0:T(8,128)S(1)} %get-tuple-element.59.residual, s32[320,128]{1,0:T(8,128)S(1)} %get-tuple-element.64.refs_0_, f32[320,128]{1,0:T(8,128)S(1)} %get-tuple-element.65.refs_1_, f32[320,128]{1,0:T(8,128)S(1)} %get-tuple-element.66.refs_2_), custom_call_target="tpu_custom_call" | custom-call | tf_op jit(solution)/shard_map/backward/pallas_call | solution.py:370
  44.2 1.0 collective-permute-start.3
  45.2 2.2 %backward.4.sum_ref = f32[512,128]{1,0:T(8,128)S(1)} custom-call(s32[8,128]{1,0:T(8,128)S(1)} %get-tuple-element.38.list_ref, f32[256,128]{1,0:T(8,128)S(1)} %get-tuple-element.59.residual, s32[320,128]{1,0:T(8,128)S(1)} %get-tuple-element.60.refs_0_, f32[320,128]{1,0:T(8,128)S(1)} %get-tuple-element.61.refs_1_, f32[320,128]{1,0:T(8,128)S(1)} %get-tuple-element.62.refs_2_), custom_call_target="tpu_custom_call" | custom-call | tf_op jit(solution)/shard_map/backward/pallas_call | solution.py:370
  47.4 2.7 %collective-permute-done.3.y_ref = bf16[512,128]{1,0:T(8,128)(2,1)S(1)} collective-permute-done((bf16[512,128]{1,0:T(8,128)(2,1)S(1)}, bf16[512,128]{1,0:T(8,128)(2,1)S(1)}, u32[]{:S(2)}, u32[]{:S(2)}) %collective-permute-start.3) | collective-permute-done | bytes 131104 | tf_op jit(solution)/shard_map/ppermute | solution.py:382
  50.2 0.8 combine_z.2
  55.0 17.1 %reduce-scatter.3.cloned.1.call-done.refs_0_ = f32[128,128]{1,0:T(8,128)} async-done(((f32[512,128]{1,0:T(8,128)}), f32[128,128]{1,0:T(8,128)}) %reduce-scatter.3.cloned.1.call-update) | async-done | bytes 65552 | tf_op jit(solution)/shard_map/reduce_scatter | solution.py:489
  72.0 0.8 copy-done.11
  72.9 0.8 copy-done.14
  73.7 0.8 copy-done.25
  74.6 13.5 %all_gather.7.values_ref.z_ref = bf16[512,128]{1,0:T(8,128)(2,1)S(1)} all-gather(bf16[128,128]{1,0:T(8,128)(2,1)S(1)} %get-tuple-element.68), channel_id=1, replica_groups={{0,4,8,12},{1,5,9,13},{2,6,10,14},{3,7,11,15},{16,20,24,28},{17,21,25,2..., dimensions={0}, use_global_device_ids=true | all-gather | bytes 163840 | tf_op jit(solution)/shard_map/all_gather | solution.py:465
  88.1 1.4 %collective-permute-start.4 = (bf16[512,128]{1,0:T(8,128)(2,1)S(1)}, bf16[512,128]{1,0:T(8,128)(2,1)S(1)}, u32[]{:S(2)}, u32[]{:S(2)}) collective-permute-start(bf16[512,128]{1,0:T(8,128)(2,1)S(1)} %all_gather.7.values_ref.z_ref), channel_id=1, source_target_pairs={{0,2},{1,3},{2,0},{3,1},{4,6},{5,7},{6,4},{7,5},{8,10},{9,11},{10,... | collective-permute-start | bytes 393224 | tf_op jit(solution)/shard_map/ppermute | solution.py:382
  89.5 2.6 %forward.6.after_ref.refs_4_ = f32[256,128]{1,0:T(8,128)S(1)} custom-call(s32[8,128]{1,0:T(8,128)S(1)} %copy-done.22, bf16[512,128]{1,0:T(8,128)(2,1)S(1)} %all_gather.7.values_ref.z_ref, s32[320,128]{1,0:T(8,128)S(1)} %get-tuple-element.39.refs_0_, f32[320,128]{1,0:T(8,128)S(1)} %get-tuple-element.40.refs_1_, f32[320,128]{1,0:T(8,128)S(1)} %get-tuple-element.41.refs_2_, ...), custom_call_target="tpu_custom_call" | custom-call | tf_op jit(solution)/shard_map/forward/pallas_call | solution.py:370
  92.2 0.9 collective-permute-done.4.y_ref.values_ref
  93.3 1.8 %forward.7.refs_11_ = f32[256,128]{1,0:T(8,128)S(1)} custom-call(s32[8,128]{1,0:T(8,128)S(1)} %copy-done.24, bf16[512,128]{1,0:T(8,128)(2,1)S(1)} %collective-permute-done.4.y_ref.values_ref, s32[320,128]{1,0:T(8,128)S(1)} %copy-done.3, f32[320,128]{1,0:T(8,128)S(1)} %copy-done.5, f32[320,128]{1,0:T(8,128)S(1)} %copy-done.7, f32[320,128]{1,0:T(8,128)S(1)} %copy-done.9, ...), custom_call_target="tpu_custom_call" | custom-call | tf_op jit(solution)/shard_map/forward/pallas_call | solution.py:370
  95.1 7.4 %turn.3 = (bf16[1024,128]{1,0:T(8,128)(2,1)S(1)}, f32[256,128]{1,0:T(8,128)S(1)}) custom-call(s32[8,128]{1,0:T(8,128)S(1)} %copy-done.30, bf16[1024,128]{1,0:T(8,128)(2,1)S(1)} %collective-permute-done.5.values_ref, s32[576,128]{1,0:T(8,128)S(1)} %get-tuple-element.44.refs_0_, f32[576,128]{1,0:T(8,128)S(1)} %get-tuple-element.45.refs_1_, ...), custom_call_target="tpu_custom_call" | custom-call | tf_op jit(solution)/shard_map/turn/pallas_call | solution.py:370
  102.6 1.5 %backward.7.sum_ref = f32[512,128]{1,0:T(8,128)S(1)} custom-call(s32[8,128]{1,0:T(8,128)S(1)} %copy-done.24, f32[256,128]{1,0:T(8,128)S(1)} %get-tuple-element.69.residual, s32[320,128]{1,0:T(8,128)S(1)} %get-tuple-element.64.refs_0_, f32[320,128]{1,0:T(8,128)S(1)} %get-tuple-element.65.refs_1_, f32[320,128]{1,0:T(8,128)S(1)} %get-tuple-element.66.refs_2_), custom_call_target="tpu_custom_call" | custom-call | tf_op jit(solution)/shard_map/backward/pallas_call | solution.py:370
  104.1 0.8 collective-permute-start.7
  105.0 2.2 %backward.6.sum_ref = f32[512,128]{1,0:T(8,128)S(1)} custom-call(s32[8,128]{1,0:T(8,128)S(1)} %copy-done.22, f32[256,128]{1,0:T(8,128)S(1)} %get-tuple-element.69.residual, s32[320,128]{1,0:T(8,128)S(1)} %get-tuple-element.60.refs_0_, f32[320,128]{1,0:T(8,128)S(1)} %get-tuple-element.61.refs_1_, f32[320,128]{1,0:T(8,128)S(1)} %get-tuple-element.62.refs_2_), custom_call_target="tpu_custom_call" | custom-call | tf_op jit(solution)/shard_map/backward/pallas_call | solution.py:370
  107.2 2.9 %collective-permute-done.7.y_ref = bf16[512,128]{1,0:T(8,128)(2,1)S(1)} collective-permute-done((bf16[512,128]{1,0:T(8,128)(2,1)S(1)}, bf16[512,128]{1,0:T(8,128)(2,1)S(1)}, u32[]{:S(2)}, u32[]{:S(2)}) %collective-permute-start.7) | collective-permute-done | bytes 131104 | tf_op jit(solution)/shard_map/ppermute | solution.py:382
  110.1 0.8 combine_z.3
  110.9 17.9 %reduce-scatter.5.cloned.1.call-done.refs_0_ = f32[128,128]{1,0:T(8,128)} async-done(((f32[512,128]{1,0:T(8,128)}), f32[128,128]{1,0:T(8,128)}) %reduce-scatter.5.cloned.1.call-update) | async-done | bytes 65552 | tf_op jit(solution)/shard_map/reduce_scatter | solution.py:489
  128.8 0.8 copy-done.28
  (95 shorter events, 7.2 us)
Async XLA Ops:
  6.5 65.5 %reduce-scatter.3.cloned.1.call-start = ((), (), s32[]{:S(2)}) async-start(), calls=%async_computation.2 | async-start | bytes 327680 | tf_op jit(solution)/shard_map/reduce_scatter | solution.py:489
  24.5 5.7 %collective-permute-start = (bf16[768,128]{1,0:T(8,128)(2,1)S(1)}, bf16[768,128]{1,0:T(8,128)(2,1)S(1)}, u32[]{:S(2)}, u32[]{:S(2)}) collective-permute-start(bf16[768,128]{1,0:T(8,128)(2,1)S(1)} %all_gather.6.payload_ref.values_ref.z_ref), channel_id=1, source_target_pairs={{0,2},{1,3},{2,0},{3,1},{4,6},{5,7},{6,4},{7,5},{8,10},{9,11},{10,... | collective-permute-start | bytes 589832 | tf_op jit(solution)/shard_map/ppermute | solution.py:382
  27.2 2.6 %copy-start = (f32[320,128]{1,0:T(8,128)}, f32[320,128]{1,0:T(8,128)S(1)}, u32[]{:S(2)}) copy-start(f32[320,128]{1,0:T(8,128)S(1)} %get-tuple-element.42.refs_3_) | copy-start | bytes 491524
  27.2 18.0 %copy-start.21 = (s32[8,128]{1,0:T(8,128)}, s32[8,128]{1,0:T(8,128)S(1)}, u32[]{:S(2)}) copy-start(s32[8,128]{1,0:T(8,128)S(1)} %get-tuple-element.38.list_ref) | copy-start | bytes 12292
  30.2 3.1 %collective-permute-start.1 = (bf16[1536,128]{1,0:T(8,128)(2,1)S(1)}, bf16[1536,128]{1,0:T(8,128)(2,1)S(1)}, u32[]{:S(2)}, u32[]{:S(2)}) collective-permute-start(bf16[1536,128]{1,0:T(8,128)(2,1)S(1)} %join.2), channel_id=1, source_target_pairs={{0,1},{1,0},{2,3},{3,2},{4,5},{5,4},{6,7},{7,6},{8,9},{9,8},{10,11... | collective-permute-start | bytes 1179656 | tf_op jit(solution)/shard_map/ppermute | solution.py:382
  31.4 1.8 %copy-start.2 = (s32[320,128]{1,0:T(8,128)}, s32[320,128]{1,0:T(8,128)S(1)}, u32[]{:S(2)}) copy-start(s32[320,128]{1,0:T(8,128)S(1)} %get-tuple-element.55.refs_0_) | copy-start | bytes 491524
  31.4 1.9 %copy-start.4 = (f32[320,128]{1,0:T(8,128)}, f32[320,128]{1,0:T(8,128)S(1)}, u32[]{:S(2)}) copy-start(f32[320,128]{1,0:T(8,128)S(1)} %get-tuple-element.56.refs_1_) | copy-start | bytes 491524
  31.5 1.9 %copy-start.6 = (f32[320,128]{1,0:T(8,128)}, f32[320,128]{1,0:T(8,128)S(1)}, u32[]{:S(2)}) copy-start(f32[320,128]{1,0:T(8,128)S(1)} %get-tuple-element.57.refs_2_) | copy-start | bytes 491524
  31.5 1.8 %copy-start.8 = (f32[320,128]{1,0:T(8,128)}, f32[320,128]{1,0:T(8,128)S(1)}, u32[]{:S(2)}) copy-start(f32[320,128]{1,0:T(8,128)S(1)} %get-tuple-element.58.refs_3_) | copy-start | bytes 491524
  31.5 3.1 %copy-start.17 = (f32[32,128]{1,0:T(8,128)}, f32[32,128]{1,0:T(8,128)S(1)}, u32[]{:S(2)}) copy-start(f32[32,128]{1,0:T(8,128)S(1)} %get-tuple-element.52.refs_9_) | copy-start | bytes 49156
  31.5 11.1 %copy-start.23 = (s32[8,128]{1,0:T(8,128)}, s32[8,128]{1,0:T(8,128)S(1)}, u32[]{:S(2)}) copy-start(s32[8,128]{1,0:T(8,128)S(1)} %get-tuple-element.54.list_ref) | copy-start | bytes 12292
  33.3 1.8 %copy-start.15 = (bf16[32,8,128]{2,1,0:T(8,128)(2,1)S(1)}, bf16[32,8,128]{2,1,0:T(8,128)(2,1)}, u32[]{:S(2)}) copy-start(bf16[32,8,128]{2,1,0:T(8,128)(2,1)} %param.7) | copy-start | bytes 196612
  34.6 8.0 %copy-start.19 = (f32[32,128]{1,0:T(8,128)}, f32[32,128]{1,0:T(8,128)S(1)}, u32[]{:S(2)}) copy-start(f32[32,128]{1,0:T(8,128)S(1)} %get-tuple-element.53.refs_10_) | copy-start | bytes 49156
  42.5 1.6 %collective-permute-start.2 = (bf16[1024,128]{1,0:T(8,128)(2,1)S(1)}, bf16[1024,128]{1,0:T(8,128)(2,1)S(1)}, u32[]{:S(2)}, u32[]{:S(2)}) collective-permute-start(bf16[1024,128]{1,0:T(8,128)(2,1)S(1)} %get-tuple-element.63), channel_id=1, source_target_pairs={{0,1},{1,0},{2,3},{3,2},{4,5},{5,4},{6,7},{7,6},{8,9},{9,8},{10,11... | collective-permute-start | bytes 786440 | tf_op jit(solution)/shard_map/ppermute | solution.py:382
  44.2 6.0 %collective-permute-start.3 = (bf16[512,128]{1,0:T(8,128)(2,1)S(1)}, bf16[512,128]{1,0:T(8,128)(2,1)S(1)}, u32[]{:S(2)}, u32[]{:S(2)}) collective-permute-start(bf16[512,128]{1,0:T(8,128)(2,1)S(1)} %combine_y.2), channel_id=1, source_target_pairs={{0,2},{1,3},{2,0},{3,1},{4,6},{5,7},{6,4},{7,5},{8,10},{9,11},{10,... | collective-permute-start | bytes 393224 | tf_op jit(solution)/shard_map/ppermute | solution.py:382
  50.9 77.8 %reduce-scatter.5.cloned.1.call-start = ((), (), s32[]{:S(2)}) async-start(), calls=%async_computation.3 | async-start | bytes 327680 | tf_op jit(solution)/shard_map/reduce_scatter | solution.py:489
  74.5 15.0 %copy-start.1 = (f32[320,128]{1,0:T(8,128)S(1)}, f32[320,128]{1,0:T(8,128)}, u32[]{:S(2)}) copy-start(f32[320,128]{1,0:T(8,128)} %copy-done) | copy-start | bytes 491524
  74.6 13.5 %copy-start.26 = (f32[128,128]{1,0:T(8,128)}, f32[128,128]{1,0:T(8,128)S(1)}, u32[]{:S(2)}) copy-start(f32[128,128]{1,0:T(8,128)S(1)} %get-tuple-element.67.volume_ref) | copy-start | bytes 196612
  74.6 15.0 %copy-start.22 = (s32[8,128]{1,0:T(8,128)S(1)}, s32[8,128]{1,0:T(8,128)}, u32[]{:S(2)}) copy-start(s32[8,128]{1,0:T(8,128)} %copy-done.21) | copy-start | bytes 12292
  88.1 5.0 %collective-permute-start.4 = (bf16[512,128]{1,0:T(8,128)(2,1)S(1)}, bf16[512,128]{1,0:T(8,128)(2,1)S(1)}, u32[]{:S(2)}, u32[]{:S(2)}) collective-permute-start(bf16[512,128]{1,0:T(8,128)(2,1)S(1)} %all_gather.7.values_ref.z_ref), channel_id=1, source_target_pairs={{0,2},{1,3},{2,0},{3,1},{4,6},{5,7},{6,4},{7,5},{8,10},{9,11},{10,... | collective-permute-start | bytes 393224 | tf_op jit(solution)/shard_map/ppermute | solution.py:382
  89.5 3.7 %copy-start.24 = (s32[8,128]{1,0:T(8,128)S(1)}, s32[8,128]{1,0:T(8,128)}, u32[]{:S(2)}) copy-start(s32[8,128]{1,0:T(8,128)} %copy-done.23) | copy-start | bytes 12292
  92.1 1.1 copy-start.3
  92.2 1.1 copy-start.9
  93.1 2.0 %copy-start.16 = (bf16[32,8,128]{2,1,0:T(8,128)(2,1)S(1)}, bf16[32,8,128]{2,1,0:T(8,128)(2,1)}, u32[]{:S(2)}) copy-start(bf16[32,8,128]{2,1,0:T(8,128)(2,1)} %param.7) | copy-start | bytes 196612
  93.1 2.0 %copy-start.18 = (f32[32,128]{1,0:T(8,128)S(1)}, f32[32,128]{1,0:T(8,128)}, u32[]{:S(2)}) copy-start(f32[32,128]{1,0:T(8,128)} %copy-done.17) | copy-start | bytes 49156
  93.1 2.0 %copy-start.20 = (f32[32,128]{1,0:T(8,128)S(1)}, f32[32,128]{1,0:T(8,128)}, u32[]{:S(2)}) copy-start(f32[32,128]{1,0:T(8,128)} %copy-done.19) | copy-start | bytes 49156
  93.1 2.0 %copy-start.30 = (s32[8,128]{1,0:T(8,128)S(1)}, s32[8,128]{1,0:T(8,128)}, u32[]{:S(2)}) copy-start(s32[8,128]{1,0:T(8,128)} %copy-done.29) | copy-start | bytes 12292
  93.1 2.0 %collective-permute-start.5 = (bf16[1024,128]{1,0:T(8,128)(2,1)S(1)}, bf16[1024,128]{1,0:T(8,128)(2,1)S(1)}, u32[]{:S(2)}, u32[]{:S(2)}) collective-permute-start(bf16[1024,128]{1,0:T(8,128)(2,1)S(1)} %join.3), channel_id=1, source_target_pairs={{0,1},{1,0},{2,3},{3,2},{4,5},{5,4},{6,7},{7,6},{8,9},{9,8},{10,11... | collective-permute-start | bytes 786440 | tf_op jit(solution)/shard_map/ppermute | solution.py:382
  102.5 1.6 %collective-permute-start.6 = (bf16[1024,128]{1,0:T(8,128)(2,1)S(1)}, bf16[1024,128]{1,0:T(8,128)(2,1)S(1)}, u32[]{:S(2)}, u32[]{:S(2)}) collective-permute-start(bf16[1024,128]{1,0:T(8,128)(2,1)S(1)} %get-tuple-element.70), channel_id=1, source_target_pairs={{0,1},{1,0},{2,3},{3,2},{4,5},{5,4},{6,7},{7,6},{8,9},{9,8},{10,11... | collective-permute-start | bytes 786440 | tf_op jit(solution)/shard_map/ppermute | solution.py:382
  104.1 6.0 %collective-permute-start.7 = (bf16[512,128]{1,0:T(8,128)(2,1)S(1)}, bf16[512,128]{1,0:T(8,128)(2,1)S(1)}, u32[]{:S(2)}, u32[]{:S(2)}) collective-permute-start(bf16[512,128]{1,0:T(8,128)(2,1)S(1)} %combine_y.3), channel_id=1, source_target_pairs={{0,2},{1,3},{2,0},{3,1},{4,6},{5,7},{6,4},{7,5},{8,10},{9,11},{10,... | collective-permute-start | bytes 393224 | tf_op jit(solution)/shard_map/ppermute | solution.py:382
  110.8 17.9 %copy-start.12 = (f32[128,128]{1,0:T(8,128)S(1)}, f32[128,128]{1,0:T(8,128)}, u32[]{:S(2)}) copy-start(f32[128,128]{1,0:T(8,128)} %copy-done.10) | copy-start | bytes 196612
  110.8 17.9 %copy-start.27 = (f32[128,128]{1,0:T(8,128)S(1)}, f32[128,128]{1,0:T(8,128)}, u32[]{:S(2)}) copy-start(f32[128,128]{1,0:T(8,128)} %copy-done.26) | copy-start | bytes 196612
  (18 other events, 13.8 us)
Sparse Core Ops, SparseCore 0:
  51.0 20.9 reduce-scatter.2
  111.0 17.7 reduce-scatter.4

commit v7 on v6

--- a/solution.py
+++ b/solution.py
@@ -31,7 +31,7 @@
     middle = jnp.floor((ray - offset) / slope + 0.5)
     middle = jnp.minimum(jnp.maximum(middle, 1.0), extent - 2.0)
     weights = [hat(ray, offset + slope * (middle + step)) for step in (-1.0, 0.0, 1.0)]
-    return middle.astype(I32), weights
+    return middle, weights
 
 
 def column_taps(offset, slope, extent):
@@ -203,7 +203,12 @@
 
 
 def pick(values, index):
-    return jnp.take_along_axis(values, index, axis=1, mode="promise_in_bounds")
+    numbers = lax.GatherDimensionNumbers(
+        offset_dims=(), collapsed_slice_dims=(1,), start_index_map=(1,),
+        operand_batching_dims=(0,), start_indices_batching_dims=(0,))
+    return lax.gather(
+        values, index[:, :, None], numbers, slice_sizes=(1, 1),
+        mode=lax.GatherScatterMode.PROMISE_IN_BOUNDS)
 
 
 def spread(ref, row, frames):
@@ -233,37 +238,43 @@
     lax.fori_loop(0, rows // step, some, 0)
 
 
-def project(sizes, stride, list_ref, values_ref, tables, projection, wides):
+def project(sizes, stride, list_ref, values_ref, tables, projection, taps_ref):
     capacity, depth, frames = sizes
     members = values_ref.shape[0] // stride
-    rows = wides[0].shape[0] // members
+    room = 4 * frames
+    tiles = taps_ref.shape[0] // (members * room)
     extent = values_ref.shape[1]
 
     def widen(member, carry):
-        values = values_ref[pl.ds(pl.multiple_of(member * stride, 16), rows), :].astype(F32)
-        at = pl.ds(pl.multiple_of(member * rows, rows), rows)
-        wides[0][at, :] = values
-        if len(wides) == 3:
-            wides[1][at, :] = pltpu.roll(values, 1, axis=1)
-            wides[2][at, :] = pltpu.roll(values, extent - 1, axis=1)
+        rows = pl.ds(pl.multiple_of(member * stride, 16), tiles * frames)
+        values = values_ref[rows, :].astype(F32)
+        before = pltpu.roll(values, 1, axis=1)
+        after = pltpu.roll(values, extent - 1, axis=1)
+        for tile in range(tiles):
+            at = slice(tile * frames, (tile + 1) * frames)
+            taps = jnp.concatenate([before[at], values[at], after[at], values[at]], axis=0)
+            to = pl.multiple_of((member * tiles + tile) * room, room)
+            taps_ref[pl.ds(to, room), :] = taps.astype(BF16)
         return carry
 
     lax.fori_loop(0, members, widen, 0)
+    step = 16
+    voxel = lax.broadcasted_iota(I32, (step, extent), 0)
+    voxels = [(voxel + start).astype(F32).astype(BF16) for start in range(0, extent, step)]
+    one_hot, zero = jnp.ones((step, extent), BF16), jnp.zeros((step, extent), BF16)
 
     def one(slot):
         line = list_ref[0, slot]
         total = None
         for level in range(depth):
-            at = tile_at(list_ref[2 + level, slot], frames)
             row = line + level * capacity
-            index = spread(tables[0], row, frames)
-            if len(wides) == 3:
-                taps = [pick(ref[at, :], index) for ref in (wides[1], wides[0], wides[2])]
-            else:
-                values = wides[0][at, :]
-                taps = [pick(values, index + shift) for shift in (-1, 0, 1)]
-            for ref, tap in zip(tables[1:], taps):
-                term = spread(ref, row, frames) * tap
+            at = pl.ds(pl.multiple_of(list_ref[2 + level, slot] * 4, room), room)
+            middle = spread(tables[0], row, step).astype(BF16)
+            choose = jnp.concatenate(
+                [jnp.where(voxel == middle, one_hot, zero) for voxel in voxels], axis=0)
+            taps = jnp.dot(taps_ref[at, :], choose, preferred_element_type=F32)
+            for place, ref in enumerate(tables[1:]):
+                term = spread(ref, row, frames) * taps[place * frames:(place + 1) * frames]
                 total = term if total is None else total + term
         projection[tile_at(list_ref[1, slot], frames), :] += total.astype(BF16).astype(F32)
 
@@ -282,11 +293,14 @@
     def one(slot):
         line = list_ref[0, slot]
         values = residual[tile_at(list_ref[1, slot], frames), :]
+        twice = jnp.concatenate([values, values], axis=0).astype(BF16)
         for level in range(depth):
             row = line + level * capacity
-            index = spread(tables[0], row, frames)
-            term = (spread(tables[1], row, frames) * pick(values, index)
-                    + spread(tables[2], row, frames) * pick(values, index + 1))
+            first = spread(tables[0], row, frames)
+            index = jnp.concatenate([first, first + 1], axis=0).astype(jnp.int16)
+            taps = pick(twice, index).astype(F32)
+            term = (spread(tables[1], row, frames) * taps[0:frames]
+                    + spread(tables[2], row, frames) * taps[frames:2 * frames])
             banks[level % len(banks)][tile_at(list_ref[2 + level, slot], frames), :] += term
 
     for_slots(list_ref, one)
@@ -296,9 +310,9 @@
     tables, refs = refs[:4], refs[4:]
     if not first:
         start_ref, refs = refs[0], refs[1:]
-    projection, wides = refs[0], refs[1:]
+    projection, taps_ref = refs
     projection[...] = jnp.zeros_like(projection) if first else start_ref[...]
-    project(sizes, stride, list_ref, values_ref, tables, projection, wides)
+    project(sizes, stride, list_ref, values_ref, tables, projection, taps_ref)
 
 
 def residual_of(sizes, projection, sinogram_ref, row_refs):
@@ -308,15 +322,15 @@
     return scaled.astype(BF16).astype(F32)
 
 
-def turn_kernel(sizes, stride, n_rows, n_wide, first, list_ref, values_ref, *refs):
+def turn_kernel(sizes, stride, n_rows, first, list_ref, values_ref, *refs):
     forward, backward, refs = refs[:4], refs[4:7], refs[7:]
     sinogram_ref, row_refs, refs = refs[0], refs[1:1 + n_rows], refs[1 + n_rows:]
     if not first:
         start_ref, refs = refs[0], refs[1:]
     out_ref, residual, projection = refs[:3]
-    wides, banks = refs[3:3 + n_wide], refs[3 + n_wide:]
+    taps_ref, banks = refs[3], refs[4:]
     projection[...] = jnp.zeros_like(projection) if first else start_ref[...]
-    project(sizes, stride, list_ref, values_ref, forward, projection, wides)
+    project(sizes, stride, list_ref, values_ref, forward, projection, taps_ref)
     residual[...] = residual_of(sizes, projection, sinogram_ref, row_refs)
     backproject(sizes, list_ref, residual, backward, banks)
 
@@ -342,11 +356,12 @@
     out_ref[...] = (sum_ref[...] + core_ref[rows:2 * rows, :].astype(F32)).astype(BF16)
 
 
-def combine_z_kernel(sum_ref, core_ref, y_ref, out_ref):
-    def add(at):
-        out_ref[at, :] = sum_ref[at, :] + core_ref[at, :].astype(F32) + y_ref[at, :].astype(F32)
-
-    for_rows(out_ref.shape[0], add)
+def combine_z_kernel(sum_ref, core_ref, y_ref, own_ref, *piece_refs):
+    rows = own_ref.shape[0]
+    for place, ref in enumerate((own_ref,) + piece_refs):
+        at = pl.ds(place * rows, rows)
+        total = sum_ref[at, :] + core_ref[at, :].astype(F32) + y_ref[at, :].astype(F32)
+        ref[...] = total.astype(ref.dtype)
 
 
 def join_kernel(z_ref, y_ref, after_ref, out_ref):
@@ -392,7 +407,7 @@
     rows = voxel_tiles * frames
     sizes = (capacity, depth, frames)
     paired = n_slab == 16
-    n_wide, n_bank = (3, 2) if paired else (1, 1)
+    n_bank = 2 if paired else 1
     shape = jax.ShapeDtypeStruct
     rays = shape((ray_tiles * frames, extent), F32)
     volume = start_volume.reshape(rows, extent)
@@ -403,7 +418,7 @@
     height = -(-(7 * depth + 2) // 16) * 16 * (n_slots // extent)
     operands = (volume, *slots_by_depth, slot_ray.reshape(1, n_slots), live)
     payload = call(
-        functools.partial(pack_kernel, capacity), "pack", 16, [ANY] * 6,
+        functools.partial(pack_kernel, capacity), "pack", 60, [ANY] * 6,
         shape((rows + height, extent), BF16), *operands,
         scratch=[pltpu.VMEM(operand.shape, operand.dtype) for operand in operands]
         + [pltpu.SemaphoreType.DMA((6,))])
@@ -412,7 +427,7 @@
         group = capacity * depth
         lines = (members + 1) * group
         lanes = -(-members * capacity // 128) * 128
-        table = [shape((lines, extent), I32)] + [shape((lines, extent), F32)] * 3
+        table = [shape((lines, extent), F32)] * 4
         table += [shape((lines, extent), I32)] + [shape((lines, extent), F32)] * 2
         out = [shape((8, lanes), I32), shape((ray_tiles, extent), F32)] + table
         stride = values.shape[0] // members
@@ -424,22 +439,25 @@
     def wide(members):
         return pltpu.VMEM((members * rows, extent), F32)
 
+    def taps(members):
+        return pltpu.VMEM((members * rows * 4, extent), BF16)
+
     def forward(values, group, start, members):
         operands = [values, *group[2]] + ([] if start is None else [start])
         return call(
             functools.partial(forward_kernel, sizes, values.shape[0] // members, start is None),
             "forward", 16, [SMEM] + [VMEM] * len(operands), rays,
-            group[0], *operands, scratch=[wide(members)] * n_wide)
+            group[0], *operands, scratch=[taps(members)])
 
     def turn(values, group, row_sums, start, members):
         operands = [values, *group[2], *group[3], sino, *row_sums] + ([] if start is None else [start])
         return call(
-            functools.partial(turn_kernel, sizes, values.shape[0] // members, len(row_sums), n_wide,
+            functools.partial(turn_kernel, sizes, values.shape[0] // members, len(row_sums),
                               start is None),
             "turn", 24 if paired else 40, [SMEM] + [VMEM] * len(operands),
             [shape((members * rows, extent), BF16), rays],
             group[0], *operands,
-            scratch=[pltpu.VMEM(rays.shape, F32)] + [wide(members)] * (n_wide + n_bank))
+            scratch=[pltpu.VMEM(rays.shape, F32), taps(members)] + [wide(members)] * n_bank)
 
     def backward(residual, group, members):
         return call(
@@ -461,9 +479,8 @@
     for sweep in range(ITERS):
         last = sweep + 1 == ITERS
         if paired:
-            columns = [list(range(place, n_slab, 4)) for place in range(4)]
-            along_z = lax.all_gather(
-                payload, "slab", axis=0, axis_index_groups=columns, tiled=True)
+            along_z = jnp.concatenate(
+                [payload] + [exchange(payload, n_slab, distance) for distance in (8, 12, 4)], axis=0)
             along_y = exchange(along_z, n_slab, 2)
             if sweep == 0:
                 groups = [setup(along_z, 4)]
@@ -483,11 +500,12 @@
                 call(combine_y_kernel, "combine_y", 16, [VMEM] * 2,
                      shape((4 * rows, extent), BF16), y_sum, core_part), n_slab, 2)
             z_sum = backward(residual, groups[0], 4)
-            total = call(
-                combine_z_kernel, "combine_z", 16, [VMEM] * 3, shape((4 * rows, extent), F32),
+            own, *pieces = call(
+                combine_z_kernel, "combine_z", 16, [VMEM] * 3,
+                [shape((rows, extent), F32)] + [shape((rows, extent), BF16)] * 3,
                 z_sum, core_part, y_part)
-            pieces = [lax.psum_scatter(
-                total, "slab", scatter_dimension=0, axis_index_groups=columns, tiled=True)]
+            pieces = [own] + [
+                exchange(piece, n_slab, distance) for piece, distance in zip(pieces, (8, 12, 4))]
         else:
             everyone = lax.all_gather(payload, "slab", axis=0, tiled=True)
             if groups is None:

time: 139 us -> 87.2 us (0.63)
  blocking collectives: 29 us -> 0 us
  starting transfers between devices: 5.13 us -> 28.6 us
  waiting for transfers between devices: 41.9 us -> 22.7 us
  between operations: 13.9 us -> 0.21 us
  local copies, waits for them, and re-layouts: 9.69 us -> 0.06 us
  Pallas kernels: 37.5 us -> 33.5 us
    reduce_scatter x2 -> x0, waiting for transfers between devices: 35 us -> none  [shards(): lax.psum_scatter(total, 'slab', scatter_dimension=0, axis_index_groups=co...]
    all_gather x2 -> x0, blocking collectives: 29 us -> none  [shards(): lax.all_gather(payload, 'slab', axis=0, axis_index_groups=columns, tiled=...]
    ppermute x8 -> x20, starting transfers between devices: 5.09 us -> 28.6 us  [exchange(): lax.ppermute(values, 'slab', [(device, device ^ distance) for device in r...]
    ppermute x8 -> x20, waiting for transfers between devices: 6.92 us -> 22.7 us  [exchange(): lax.ppermute(values, 'slab', [(device, device ^ distance) for device in r...]
    unnamed x80 -> x15, local copies, waits for them, and re-layouts: 9.69 us -> 0.05 us
    pallas_call x23, Pallas kernels: 37.5 us -> 33.5 us  [call(): pl.pallas_call(kernel, out_shape=out_shape, in_specs=in_specs, out_specs=...]
  transfers between devices with their start and end apart: 10 -> 20, of which waited for: 6 -> 11; matrix products, arithmetic and copies ran while one was open for 0% -> 0% of each run, Pallas kernels for 14% -> 24%
where the time goes in v7:
time: 87.2 us; the launch traced here: 85.9 us
  Pallas kernels  33.5 us (38%)
  starting transfers between devices  28.6 us (33%)
  waiting for transfers between devices  22.7 us (26%)
    pallas_call x23, Pallas kernels, call(): pl.pallas_call(kernel, out_shape=out_shape, in_specs=in_specs, out_specs=...  33.5 us
    ppermute x20, starting transfers between devices, exchange(): lax.ppermute(values, 'slab', [(device, device ^ distance) for device in r...  28.6 us
    ppermute x20, waiting for transfers between devices, exchange(): lax.ppermute(values, 'slab', [(device, device ^ distance) for device in r...  22.7 us
  transfers between devices with their start and end apart: 20, of which 11 were waited for; matrix products, arithmetic and copies ran while one was open for 0% of the time, Pallas kernels for 24%

profile of v7, /device:TPU:0, one launch (start us, length us, event | category | flops | bytes accessed | tf_op | source)
XLA Modules:
  0.0 85.9 jit_solution(2504054005738120378)
XLA Ops:
  0.0 1.7 %pack.1 = bf16[192,128]{1,0:T(8,128)(2,1)} custom-call(f32[128,128]{1,0:T(8,128)} %bitcast.9, f32[4,256]{1,0:T(4,128)} %bitcast.13, f32[4,256]{1,0:T(4,128)} %bitcast.15, s32[4,256]{1,0:T(4,128)} %bitcast.17, s32[1,256]{1,0:T(1,128)} %bitcast.21, s32[1,16]{1,0:T(1,128)} %bitcast.19), custom_call_target="tpu_custom_call" | custom-call | tf_op jit(solution)/shard_map/pack/pallas_call | solution.py:385
  1.7 4.1 %collective-permute-start = (bf16[192,128]{1,0:T(8,128)(2,1)}, bf16[192,128]{1,0:T(8,128)(2,1)S(1)}, u32[]{:S(2)}, u32[]{:S(2)}) collective-permute-start(bf16[192,128]{1,0:T(8,128)(2,1)} %pack.1), channel_id=1, source_target_pairs={{0,8},{1,9},{2,10},{3,11},{4,12},{5,13},{6,14},{7,15},{8,0},{9,1},... | collective-permute-start | bytes 147464 | tf_op jit(solution)/shard_map/ppermute | solution.py:397
  5.8 1.3 %collective-permute-start.1 = (bf16[192,128]{1,0:T(8,128)(2,1)}, bf16[192,128]{1,0:T(8,128)(2,1)S(1)}, u32[]{:S(2)}, u32[]{:S(2)}) collective-permute-start(bf16[192,128]{1,0:T(8,128)(2,1)} %pack.1), channel_id=1, source_target_pairs={{0,12},{1,13},{2,14},{3,15},{4,8},{5,9},{6,10},{7,11},{8,4},{9,5},... | collective-permute-start | bytes 147464 | tf_op jit(solution)/shard_map/ppermute | solution.py:397
  7.3 1.2 %collective-permute-done = bf16[192,128]{1,0:T(8,128)(2,1)S(1)} collective-permute-done((bf16[192,128]{1,0:T(8,128)(2,1)}, bf16[192,128]{1,0:T(8,128)(2,1)S(1)}, u32[]{:S(2)}, u32[]{:S(2)}) %collective-permute-start) | collective-permute-done | bytes 49184 | tf_op jit(solution)/shard_map/ppermute | solution.py:397
  8.6 3.4 %collective-permute-done.1 = bf16[192,128]{1,0:T(8,128)(2,1)S(1)} collective-permute-done((bf16[192,128]{1,0:T(8,128)(2,1)}, bf16[192,128]{1,0:T(8,128)(2,1)S(1)}, u32[]{:S(2)}, u32[]{:S(2)}) %collective-permute-start.1) | collective-permute-done | bytes 49184 | tf_op jit(solution)/shard_map/ppermute | solution.py:397
  12.8 1.6 %collective-permute-start.3 = (bf16[768,128]{1,0:T(8,128)(2,1)S(1)}, bf16[768,128]{1,0:T(8,128)(2,1)S(1)}, u32[]{:S(2)}, u32[]{:S(2)}) collective-permute-start(bf16[768,128]{1,0:T(8,128)(2,1)S(1)} %pad_maximum_fusion.payload_ref.values_ref.z_ref), channel_id=1, source_target_pairs={{0,2},{1,3},{2,0},{3,1},{4,6},{5,7},{6,4},{7,5},{8,10},{9,11},{10,... | collective-permute-start | bytes 589832 | tf_op jit(solution)/shard_map/ppermute | solution.py:397
  15.5 3.4 %forward.4.after_ref.refs_4_ = f32[256,128]{1,0:T(8,128)S(1)} custom-call(s32[8,128]{1,0:T(8,128)S(1)} %get-tuple-element.46.list_ref, bf16[768,128]{1,0:T(8,128)(2,1)S(1)} %pad_maximum_fusion.payload_ref.values_ref.z_ref, f32[320,128]{1,0:T(8,128)S(1)} %get-tuple-element.47.refs_0_, f32[320,128]{1,0:T(8,128)S(1)} %get-tuple-element.48.refs_1_, ...), custom_call_target="tpu_custom_call" | custom-call | tf_op jit(solution)/shard_map/forward/pallas_call | solution.py:385
  20.1 2.6 %forward.5.refs_11_ = f32[256,128]{1,0:T(8,128)S(1)} custom-call(s32[8,128]{1,0:T(8,128)S(1)} %get-tuple-element.62.list_ref, bf16[768,128]{1,0:T(8,128)(2,1)S(1)} %collective-permute-done.3.y_ref.payload_ref.values_ref, f32[320,128]{1,0:T(8,128)S(1)} %get-tuple-element.63.refs_0_, f32[320,128]{1,0:T(8,128)S(1)} %get-tuple-element.64.refs_1_, ...), custom_call_target="tpu_custom_call" | custom-call | tf_op jit(solution)/shard_map/forward/pallas_call | solution.py:385
  22.7 1.2 %setup.4 = (s32[8,128]{1,0:T(8,128)S(1)}, f32[32,128]{1,0:T(8,128)S(1)}, f32[576,128]{1,0:T(8,128)S(1)}, f32[576,128]{1,0:T(8,128)S(1)}, f32[576,128]{1,0:T(8,12...) custom-call(s32[1]{0:T(128)} %bitcast.5.me_ref, ...), custom_call_target="tpu_custom_call" | custom-call | tf_op jit(solution)/shard_map/setup/pallas_call | solution.py:385
  24.0 4.4 %turn.2 = (bf16[1024,128]{1,0:T(8,128)(2,1)S(1)}, f32[256,128]{1,0:T(8,128)S(1)}) custom-call(s32[8,128]{1,0:T(8,128)S(1)} %get-tuple-element.51.list_ref, bf16[1536,128]{1,0:T(8,128)(2,1)S(1)} %collective-permute-done.4.payload_ref.values_ref, f32[576,128]{1,0:T(8,128)S(1)} %get-tuple-element.52.refs_0_, f32[576,128]{1,0:T(8,128)S(1)} %get-tuple-element.53.refs_1_, ...), custom_call_target="tpu_custom_call" | custom-call | tf_op jit(solution)/shard_map/turn/pallas_call | solution.py:385
  28.4 3.0 %collective-permute-start.5 = (bf16[1024,128]{1,0:T(8,128)(2,1)S(1)}, bf16[1024,128]{1,0:T(8,128)(2,1)S(1)}, u32[]{:S(2)}, u32[]{:S(2)}) collective-permute-start(bf16[1024,128]{1,0:T(8,128)(2,1)S(1)} %get-tuple-element.71), channel_id=1, source_target_pairs={{0,1},{1,0},{2,3},{3,2},{4,5},{5,4},{6,7},{7,6},{8,9},{9,8},{10,11... | collective-permute-start | bytes 786440 | tf_op jit(solution)/shard_map/ppermute | solution.py:397
  31.4 1.4 %backward.5.sum_ref = f32[512,128]{1,0:T(8,128)S(1)} custom-call(s32[8,128]{1,0:T(8,128)S(1)} %get-tuple-element.62.list_ref, f32[256,128]{1,0:T(8,128)S(1)} %get-tuple-element.67.residual, s32[320,128]{1,0:T(8,128)S(1)} %get-tuple-element.72.refs_0_, f32[320,128]{1,0:T(8,128)S(1)} %get-tuple-element.73.refs_1_, f32[320,128]{1,0:T(8,128)S(1)} %get-tuple-element.74.refs_2_), custom_call_target="tpu_custom_call" | custom-call | tf_op jit(solution)/shard_map/backward/pallas_call | solution.py:385
  32.8 2.2 %collective-permute-start.6 = (bf16[512,128]{1,0:T(8,128)(2,1)S(1)}, bf16[512,128]{1,0:T(8,128)(2,1)S(1)}, u32[]{:S(2)}, u32[]{:S(2)}) collective-permute-start(bf16[512,128]{1,0:T(8,128)(2,1)S(1)} %combine_y.2), channel_id=1, source_target_pairs={{0,2},{1,3},{2,0},{3,1},{4,6},{5,7},{6,4},{7,5},{8,10},{9,11},{10,... | collective-permute-start | bytes 393224 | tf_op jit(solution)/shard_map/ppermute | solution.py:397
  35.0 1.7 %backward.4.sum_ref = f32[512,128]{1,0:T(8,128)S(1)} custom-call(s32[8,128]{1,0:T(8,128)S(1)} %get-tuple-element.46.list_ref, f32[256,128]{1,0:T(8,128)S(1)} %get-tuple-element.67.residual, s32[320,128]{1,0:T(8,128)S(1)} %get-tuple-element.68.refs_0_, f32[320,128]{1,0:T(8,128)S(1)} %get-tuple-element.69.refs_1_, f32[320,128]{1,0:T(8,128)S(1)} %get-tuple-element.70.refs_2_), custom_call_target="tpu_custom_call" | custom-call | tf_op jit(solution)/shard_map/backward/pallas_call | solution.py:385
  36.8 2.5 %collective-permute-done.6.y_ref = bf16[512,128]{1,0:T(8,128)(2,1)S(1)} collective-permute-done((bf16[512,128]{1,0:T(8,128)(2,1)S(1)}, bf16[512,128]{1,0:T(8,128)(2,1)S(1)}, u32[]{:S(2)}, u32[]{:S(2)}) %collective-permute-start.6) | collective-permute-done | bytes 131104 | tf_op jit(solution)/shard_map/ppermute | solution.py:397
  39.3 2.6 %collective-permute-start.7 = (bf16[128,128]{1,0:T(8,128)(2,1)S(1)}, bf16[128,128]{1,0:T(8,128)(2,1)S(1)}, u32[]{:S(2)}, u32[]{:S(2)}) collective-permute-start(bf16[128,128]{1,0:T(8,128)(2,1)S(1)} %get-tuple-element.76), channel_id=1, source_target_pairs={{0,8},{1,9},{2,10},{3,11},{4,12},{5,13},{6,14},{7,15},{8,0},{9,1},... | collective-permute-start | bytes 98312 | tf_op jit(solution)/shard_map/ppermute | solution.py:397
  44.5 3.1 %collective-permute-done.8.refs_2_ = bf16[128,128]{1,0:T(8,128)(2,1)S(1)} collective-permute-done((bf16[128,128]{1,0:T(8,128)(2,1)S(1)}, bf16[128,128]{1,0:T(8,128)(2,1)S(1)}, u32[]{:S(2)}, u32[]{:S(2)}) %collective-permute-start.8) | collective-permute-done | bytes 32800 | tf_op jit(solution)/shard_map/ppermute | solution.py:397
  48.6 1.2 %collective-permute-start.11 = (bf16[128,128]{1,0:T(8,128)(2,1)S(1)}, bf16[128,128]{1,0:T(8,128)(2,1)S(1)}, u32[]{:S(2)}, u32[]{:S(2)}) collective-permute-start(bf16[128,128]{1,0:T(8,128)(2,1)S(1)} %get-tuple-element.80), channel_id=1, source_target_pairs={{0,12},{1,13},{2,14},{3,15},{4,8},{5,9},{6,10},{7,11},{8,4},{9,5},... | collective-permute-start | bytes 98312 | tf_op jit(solution)/shard_map/ppermute | solution.py:397
  49.8 1.4 %collective-permute-start.12 = (bf16[128,128]{1,0:T(8,128)(2,1)S(1)}, bf16[128,128]{1,0:T(8,128)(2,1)S(1)}, u32[]{:S(2)}, u32[]{:S(2)}) collective-permute-start(bf16[128,128]{1,0:T(8,128)(2,1)S(1)} %get-tuple-element.80), channel_id=1, source_target_pairs={{0,4},{1,5},{2,6},{3,7},{4,0},{5,1},{6,2},{7,3},{8,12},{9,13},{10,... | collective-permute-start | bytes 98312 | tf_op jit(solution)/shard_map/ppermute | solution.py:397
  51.2 1.3 %collective-permute-done.10 = bf16[128,128]{1,0:T(8,128)(2,1)S(1)} collective-permute-done((bf16[128,128]{1,0:T(8,128)(2,1)S(1)}, bf16[128,128]{1,0:T(8,128)(2,1)S(1)}, u32[]{:S(2)}, u32[]{:S(2)}) %collective-permute-start.10) | collective-permute-done | bytes 32800 | tf_op jit(solution)/shard_map/ppermute | solution.py:397
  52.5 1.8 %collective-permute-done.11 = bf16[128,128]{1,0:T(8,128)(2,1)S(1)} collective-permute-done((bf16[128,128]{1,0:T(8,128)(2,1)S(1)}, bf16[128,128]{1,0:T(8,128)(2,1)S(1)}, u32[]{:S(2)}, u32[]{:S(2)}) %collective-permute-start.11) | collective-permute-done | bytes 32800 | tf_op jit(solution)/shard_map/ppermute | solution.py:397
  55.0 3.4 %forward.6.after_ref.refs_4_ = f32[256,128]{1,0:T(8,128)S(1)} custom-call(s32[8,128]{1,0:T(8,128)S(1)} %get-tuple-element.46.list_ref, bf16[512,128]{1,0:T(8,128)(2,1)S(1)} %constant_dynamic-update-slice_fusion.values_ref.z_ref, f32[320,128]{1,0:T(8,128)S(1)} %get-tuple-element.47.refs_0_, f32[320,128]{1,0:T(8,128)S(1)} %get-tuple-element.48.refs_1_, ...), custom_call_target="tpu_custom_call" | custom-call | tf_op jit(solution)/shard_map/forward/pallas_call | solution.py:385
  59.5 2.6 %forward.7.refs_11_ = f32[256,128]{1,0:T(8,128)S(1)} custom-call(s32[8,128]{1,0:T(8,128)S(1)} %get-tuple-element.62.list_ref, bf16[512,128]{1,0:T(8,128)(2,1)S(1)} %collective-permute-done.13.y_ref.values_ref, f32[320,128]{1,0:T(8,128)S(1)} %get-tuple-element.63.refs_0_, f32[320,128]{1,0:T(8,128)S(1)} %get-tuple-element.64.refs_1_, ...), custom_call_target="tpu_custom_call" | custom-call | tf_op jit(solution)/shard_map/forward/pallas_call | solution.py:385
  62.1 4.4 %turn.3 = (bf16[1024,128]{1,0:T(8,128)(2,1)S(1)}, f32[256,128]{1,0:T(8,128)S(1)}) custom-call(s32[8,128]{1,0:T(8,128)S(1)} %get-tuple-element.51.list_ref, bf16[1024,128]{1,0:T(8,128)(2,1)S(1)} %collective-permute-done.14.values_ref, f32[576,128]{1,0:T(8,128)S(1)} %get-tuple-element.52.refs_0_, f32[576,128]{1,0:T(8,128)S(1)} %get-tuple-element.53.refs_1_, ...), custom_call_target="tpu_custom_call" | custom-call | tf_op jit(solution)/shard_map/turn/pallas_call | solution.py:385
  66.5 3.0 %collective-permute-start.15 = (bf16[1024,128]{1,0:T(8,128)(2,1)S(1)}, bf16[1024,128]{1,0:T(8,128)(2,1)S(1)}, u32[]{:S(2)}, u32[]{:S(2)}) collective-permute-start(bf16[1024,128]{1,0:T(8,128)(2,1)S(1)} %get-tuple-element.82), channel_id=1, source_target_pairs={{0,1},{1,0},{2,3},{3,2},{4,5},{5,4},{6,7},{7,6},{8,9},{9,8},{10,11... | collective-permute-start | bytes 786440 | tf_op jit(solution)/shard_map/ppermute | solution.py:397
  69.5 1.4 %backward.7.sum_ref = f32[512,128]{1,0:T(8,128)S(1)} custom-call(s32[8,128]{1,0:T(8,128)S(1)} %get-tuple-element.62.list_ref, f32[256,128]{1,0:T(8,128)S(1)} %get-tuple-element.81.residual, s32[320,128]{1,0:T(8,128)S(1)} %get-tuple-element.72.refs_0_, f32[320,128]{1,0:T(8,128)S(1)} %get-tuple-element.73.refs_1_, f32[320,128]{1,0:T(8,128)S(1)} %get-tuple-element.74.refs_2_), custom_call_target="tpu_custom_call" | custom-call | tf_op jit(solution)/shard_map/backward/pallas_call | solution.py:385
  70.9 1.7 %collective-permute-start.16 = (bf16[512,128]{1,0:T(8,128)(2,1)S(1)}, bf16[512,128]{1,0:T(8,128)(2,1)S(1)}, u32[]{:S(2)}, u32[]{:S(2)}) collective-permute-start(bf16[512,128]{1,0:T(8,128)(2,1)S(1)} %combine_y.3), channel_id=1, source_target_pairs={{0,2},{1,3},{2,0},{3,1},{4,6},{5,7},{6,4},{7,5},{8,10},{9,11},{10,... | collective-permute-start | bytes 393224 | tf_op jit(solution)/shard_map/ppermute | solution.py:397
  72.6 1.7 %backward.6.sum_ref = f32[512,128]{1,0:T(8,128)S(1)} custom-call(s32[8,128]{1,0:T(8,128)S(1)} %get-tuple-element.46.list_ref, f32[256,128]{1,0:T(8,128)S(1)} %get-tuple-element.81.residual, s32[320,128]{1,0:T(8,128)S(1)} %get-tuple-element.68.refs_0_, f32[320,128]{1,0:T(8,128)S(1)} %get-tuple-element.69.refs_1_, f32[320,128]{1,0:T(8,128)S(1)} %get-tuple-element.70.refs_2_), custom_call_target="tpu_custom_call" | custom-call | tf_op jit(solution)/shard_map/backward/pallas_call | solution.py:385
  74.3 2.5 %collective-permute-done.16.y_ref = bf16[512,128]{1,0:T(8,128)(2,1)S(1)} collective-permute-done((bf16[512,128]{1,0:T(8,128)(2,1)S(1)}, bf16[512,128]{1,0:T(8,128)(2,1)S(1)}, u32[]{:S(2)}, u32[]{:S(2)}) %collective-permute-start.16) | collective-permute-done | bytes 131104 | tf_op jit(solution)/shard_map/ppermute | solution.py:397
  76.8 2.7 %collective-permute-start.17 = (bf16[128,128]{1,0:T(8,128)(2,1)S(1)}, bf16[128,128]{1,0:T(8,128)(2,1)S(1)}, u32[]{:S(2)}, u32[]{:S(2)}) collective-permute-start(bf16[128,128]{1,0:T(8,128)(2,1)S(1)} %get-tuple-element.84), channel_id=1, source_target_pairs={{0,8},{1,9},{2,10},{3,11},{4,12},{5,13},{6,14},{7,15},{8,0},{9,1},... | collective-permute-start | bytes 98312 | tf_op jit(solution)/shard_map/ppermute | solution.py:397
  80.4 1.3 %collective-permute-done.17.refs_1_ = bf16[128,128]{1,0:T(8,128)(2,1)S(1)} collective-permute-done((bf16[128,128]{1,0:T(8,128)(2,1)S(1)}, bf16[128,128]{1,0:T(8,128)(2,1)S(1)}, u32[]{:S(2)}, u32[]{:S(2)}) %collective-permute-start.17) | collective-permute-done | bytes 32800 | tf_op jit(solution)/shard_map/ppermute | solution.py:397
  81.7 3.5 %collective-permute-done.18.refs_2_ = bf16[128,128]{1,0:T(8,128)(2,1)S(1)} collective-permute-done((bf16[128,128]{1,0:T(8,128)(2,1)S(1)}, bf16[128,128]{1,0:T(8,128)(2,1)S(1)}, u32[]{:S(2)}, u32[]{:S(2)}) %collective-permute-start.18) | collective-permute-done | bytes 32800 | tf_op jit(solution)/shard_map/ppermute | solution.py:397
  (48 shorter events, 10.5 us)
Async XLA Ops:
  1.7 6.9 %collective-permute-start = (bf16[192,128]{1,0:T(8,128)(2,1)}, bf16[192,128]{1,0:T(8,128)(2,1)S(1)}, u32[]{:S(2)}, u32[]{:S(2)}) collective-permute-start(bf16[192,128]{1,0:T(8,128)(2,1)} %pack.1), channel_id=1, source_target_pairs={{0,8},{1,9},{2,10},{3,11},{4,12},{5,13},{6,14},{7,15},{8,0},{9,1},... | collective-permute-start | bytes 147464 | tf_op jit(solution)/shard_map/ppermute | solution.py:397
  5.8 6.2 %collective-permute-start.1 = (bf16[192,128]{1,0:T(8,128)(2,1)}, bf16[192,128]{1,0:T(8,128)(2,1)S(1)}, u32[]{:S(2)}, u32[]{:S(2)}) collective-permute-start(bf16[192,128]{1,0:T(8,128)(2,1)} %pack.1), channel_id=1, source_target_pairs={{0,12},{1,13},{2,14},{3,15},{4,8},{5,9},{6,10},{7,11},{8,4},{9,5},... | collective-permute-start | bytes 147464 | tf_op jit(solution)/shard_map/ppermute | solution.py:397
  7.1 4.8 %collective-permute-start.2 = (bf16[192,128]{1,0:T(8,128)(2,1)}, bf16[192,128]{1,0:T(8,128)(2,1)S(1)}, u32[]{:S(2)}, u32[]{:S(2)}) collective-permute-start(bf16[192,128]{1,0:T(8,128)(2,1)} %pack.1), channel_id=1, source_target_pairs={{0,4},{1,5},{2,6},{3,7},{4,0},{5,1},{6,2},{7,3},{8,12},{9,13},{10,... | collective-permute-start | bytes 147464 | tf_op jit(solution)/shard_map/ppermute | solution.py:397
  12.8 6.1 %collective-permute-start.3 = (bf16[768,128]{1,0:T(8,128)(2,1)S(1)}, bf16[768,128]{1,0:T(8,128)(2,1)S(1)}, u32[]{:S(2)}, u32[]{:S(2)}) collective-permute-start(bf16[768,128]{1,0:T(8,128)(2,1)S(1)} %pad_maximum_fusion.payload_ref.values_ref.z_ref), channel_id=1, source_target_pairs={{0,2},{1,3},{2,0},{3,1},{4,6},{5,7},{6,4},{7,5},{8,10},{9,11},{10,... | collective-permute-start | bytes 589832 | tf_op jit(solution)/shard_map/ppermute | solution.py:397
  18.9 3.8 %collective-permute-start.4 = (bf16[1536,128]{1,0:T(8,128)(2,1)S(1)}, bf16[1536,128]{1,0:T(8,128)(2,1)S(1)}, u32[]{:S(2)}, u32[]{:S(2)}) collective-permute-start(bf16[1536,128]{1,0:T(8,128)(2,1)S(1)} %join.2), channel_id=1, source_target_pairs={{0,1},{1,0},{2,3},{3,2},{4,5},{5,4},{6,7},{7,6},{8,9},{9,8},{10,11... | collective-permute-start | bytes 1179656 | tf_op jit(solution)/shard_map/ppermute | solution.py:397
  22.7 1.2 %copy-start.1 = (bf16[32,8,128]{2,1,0:T(8,128)(2,1)S(1)}, bf16[32,8,128]{2,1,0:T(8,128)(2,1)}, u32[]{:S(2)}) copy-start(bf16[32,8,128]{2,1,0:T(8,128)(2,1)} %param.7) | copy-start | bytes 196612
  28.4 4.4 %collective-permute-start.5 = (bf16[1024,128]{1,0:T(8,128)(2,1)S(1)}, bf16[1024,128]{1,0:T(8,128)(2,1)S(1)}, u32[]{:S(2)}, u32[]{:S(2)}) collective-permute-start(bf16[1024,128]{1,0:T(8,128)(2,1)S(1)} %get-tuple-element.71), channel_id=1, source_target_pairs={{0,1},{1,0},{2,3},{3,2},{4,5},{5,4},{6,7},{7,6},{8,9},{9,8},{10,11... | collective-permute-start | bytes 786440 | tf_op jit(solution)/shard_map/ppermute | solution.py:397
  32.8 6.5 %collective-permute-start.6 = (bf16[512,128]{1,0:T(8,128)(2,1)S(1)}, bf16[512,128]{1,0:T(8,128)(2,1)S(1)}, u32[]{:S(2)}, u32[]{:S(2)}) collective-permute-start(bf16[512,128]{1,0:T(8,128)(2,1)S(1)} %combine_y.2), channel_id=1, source_target_pairs={{0,2},{1,3},{2,0},{3,1},{4,6},{5,7},{6,4},{7,5},{8,10},{9,11},{10,... | collective-permute-start | bytes 393224 | tf_op jit(solution)/shard_map/ppermute | solution.py:397
  39.2 3.6 %copy-start.2 = (f32[256,4]{0,1:T(4,128)S(1)}, f32[256,4]{0,1:T(4,128)}, u32[]{:S(2)}) copy-start(f32[256,4]{0,1:T(4,128)} %param.13) | copy-start | bytes 12292
  39.2 3.6 %copy-start.3 = (f32[256,4]{0,1:T(4,128)S(1)}, f32[256,4]{0,1:T(4,128)}, u32[]{:S(2)}) copy-start(f32[256,4]{0,1:T(4,128)} %param.12) | copy-start | bytes 12292
  39.2 3.6 %copy-start.4 = (s32[256,4]{0,1:T(4,128)S(1)}, s32[256,4]{0,1:T(4,128)}, u32[]{:S(2)}) copy-start(s32[256,4]{0,1:T(4,128)} %param.9) | copy-start | bytes 12292
  39.2 3.6 %copy-start.5 = (s32[16]{0:T(128)S(1)}, s32[16]{0:T(128)}, u32[]{:S(2)}) copy-start(s32[16]{0:T(128)} %param.11) | copy-start | bytes 196
  39.3 8.3 %copy-start = (f32[16,8,128]{2,1,0:T(8,128)S(1)}, f32[16,8,128]{2,1,0:T(8,128)}, u32[]{:S(2)}) copy-start(f32[16,8,128]{2,1,0:T(8,128)} %param.8) | copy-start | bytes 196612
  39.3 5.2 %collective-permute-start.7 = (bf16[128,128]{1,0:T(8,128)(2,1)S(1)}, bf16[128,128]{1,0:T(8,128)(2,1)S(1)}, u32[]{:S(2)}, u32[]{:S(2)}) collective-permute-start(bf16[128,128]{1,0:T(8,128)(2,1)S(1)} %get-tuple-element.76), channel_id=1, source_target_pairs={{0,8},{1,9},{2,10},{3,11},{4,12},{5,13},{6,14},{7,15},{8,0},{9,1},... | collective-permute-start | bytes 98312 | tf_op jit(solution)/shard_map/ppermute | solution.py:397
  41.9 5.7 %collective-permute-start.8 = (bf16[128,128]{1,0:T(8,128)(2,1)S(1)}, bf16[128,128]{1,0:T(8,128)(2,1)S(1)}, u32[]{:S(2)}, u32[]{:S(2)}) collective-permute-start(bf16[128,128]{1,0:T(8,128)(2,1)S(1)} %get-tuple-element.77), channel_id=1, source_target_pairs={{0,12},{1,13},{2,14},{3,15},{4,8},{5,9},{6,10},{7,11},{8,4},{9,5},... | collective-permute-start | bytes 98312 | tf_op jit(solution)/shard_map/ppermute | solution.py:397
  42.2 5.4 %collective-permute-start.9 = (bf16[128,128]{1,0:T(8,128)(2,1)S(1)}, bf16[128,128]{1,0:T(8,128)(2,1)S(1)}, u32[]{:S(2)}, u32[]{:S(2)}) collective-permute-start(bf16[128,128]{1,0:T(8,128)(2,1)S(1)} %get-tuple-element.78), channel_id=1, source_target_pairs={{0,4},{1,5},{2,6},{3,7},{4,0},{5,1},{6,2},{7,3},{8,12},{9,13},{10,... | collective-permute-start | bytes 98312 | tf_op jit(solution)/shard_map/ppermute | solution.py:397
  47.7 4.9 %collective-permute-start.10 = (bf16[128,128]{1,0:T(8,128)(2,1)S(1)}, bf16[128,128]{1,0:T(8,128)(2,1)S(1)}, u32[]{:S(2)}, u32[]{:S(2)}) collective-permute-start(bf16[128,128]{1,0:T(8,128)(2,1)S(1)} %get-tuple-element.80), channel_id=1, source_target_pairs={{0,8},{1,9},{2,10},{3,11},{4,12},{5,13},{6,14},{7,15},{8,0},{9,1},... | collective-permute-start | bytes 98312 | tf_op jit(solution)/shard_map/ppermute | solution.py:397
  48.6 5.7 %collective-permute-start.11 = (bf16[128,128]{1,0:T(8,128)(2,1)S(1)}, bf16[128,128]{1,0:T(8,128)(2,1)S(1)}, u32[]{:S(2)}, u32[]{:S(2)}) collective-permute-start(bf16[128,128]{1,0:T(8,128)(2,1)S(1)} %get-tuple-element.80), channel_id=1, source_target_pairs={{0,12},{1,13},{2,14},{3,15},{4,8},{5,9},{6,10},{7,11},{8,4},{9,5},... | collective-permute-start | bytes 98312 | tf_op jit(solution)/shard_map/ppermute | solution.py:397
  49.8 4.5 %collective-permute-start.12 = (bf16[128,128]{1,0:T(8,128)(2,1)S(1)}, bf16[128,128]{1,0:T(8,128)(2,1)S(1)}, u32[]{:S(2)}, u32[]{:S(2)}) collective-permute-start(bf16[128,128]{1,0:T(8,128)(2,1)S(1)} %get-tuple-element.80), channel_id=1, source_target_pairs={{0,4},{1,5},{2,6},{3,7},{4,0},{5,1},{6,2},{7,3},{8,12},{9,13},{10,... | collective-permute-start | bytes 98312 | tf_op jit(solution)/shard_map/ppermute | solution.py:397
  54.4 5.0 %collective-permute-start.13 = (bf16[512,128]{1,0:T(8,128)(2,1)S(1)}, bf16[512,128]{1,0:T(8,128)(2,1)S(1)}, u32[]{:S(2)}, u32[]{:S(2)}) collective-permute-start(bf16[512,128]{1,0:T(8,128)(2,1)S(1)} %constant_dynamic-update-slice_fusion.values_ref.z_ref), channel_id=1, source_target_pairs={{0,2},{1,3},{2,0},{3,1},{4,6},{5,7},{6,4},{7,5},{8,10},{9,11},{10,... | collective-permute-start | bytes 393224 | tf_op jit(solution)/shard_map/ppermute | solution.py:397
  59.4 2.6 %collective-permute-start.14 = (bf16[1024,128]{1,0:T(8,128)(2,1)S(1)}, bf16[1024,128]{1,0:T(8,128)(2,1)S(1)}, u32[]{:S(2)}, u32[]{:S(2)}) collective-permute-start(bf16[1024,128]{1,0:T(8,128)(2,1)S(1)} %join.3), channel_id=1, source_target_pairs={{0,1},{1,0},{2,3},{3,2},{4,5},{5,4},{6,7},{7,6},{8,9},{9,8},{10,11... | collective-permute-start | bytes 786440 | tf_op jit(solution)/shard_map/ppermute | solution.py:397
  66.5 4.4 %collective-permute-start.15 = (bf16[1024,128]{1,0:T(8,128)(2,1)S(1)}, bf16[1024,128]{1,0:T(8,128)(2,1)S(1)}, u32[]{:S(2)}, u32[]{:S(2)}) collective-permute-start(bf16[1024,128]{1,0:T(8,128)(2,1)S(1)} %get-tuple-element.82), channel_id=1, source_target_pairs={{0,1},{1,0},{2,3},{3,2},{4,5},{5,4},{6,7},{7,6},{8,9},{9,8},{10,11... | collective-permute-start | bytes 786440 | tf_op jit(solution)/shard_map/ppermute | solution.py:397
  70.9 5.9 %collective-permute-start.16 = (bf16[512,128]{1,0:T(8,128)(2,1)S(1)}, bf16[512,128]{1,0:T(8,128)(2,1)S(1)}, u32[]{:S(2)}, u32[]{:S(2)}) collective-permute-start(bf16[512,128]{1,0:T(8,128)(2,1)S(1)} %combine_y.3), channel_id=1, source_target_pairs={{0,2},{1,3},{2,0},{3,1},{4,6},{5,7},{6,4},{7,5},{8,10},{9,11},{10,... | collective-permute-start | bytes 393224 | tf_op jit(solution)/shard_map/ppermute | solution.py:397
  76.8 4.9 %collective-permute-start.17 = (bf16[128,128]{1,0:T(8,128)(2,1)S(1)}, bf16[128,128]{1,0:T(8,128)(2,1)S(1)}, u32[]{:S(2)}, u32[]{:S(2)}) collective-permute-start(bf16[128,128]{1,0:T(8,128)(2,1)S(1)} %get-tuple-element.84), channel_id=1, source_target_pairs={{0,8},{1,9},{2,10},{3,11},{4,12},{5,13},{6,14},{7,15},{8,0},{9,1},... | collective-permute-start | bytes 98312 | tf_op jit(solution)/shard_map/ppermute | solution.py:397
  79.5 5.7 %collective-permute-start.18 = (bf16[128,128]{1,0:T(8,128)(2,1)S(1)}, bf16[128,128]{1,0:T(8,128)(2,1)S(1)}, u32[]{:S(2)}, u32[]{:S(2)}) collective-permute-start(bf16[128,128]{1,0:T(8,128)(2,1)S(1)} %get-tuple-element.85), channel_id=1, source_target_pairs={{0,12},{1,13},{2,14},{3,15},{4,8},{5,9},{6,10},{7,11},{8,4},{9,5},... | collective-permute-start | bytes 98312 | tf_op jit(solution)/shard_map/ppermute | solution.py:397
  80.1 5.1 %collective-permute-start.19 = (bf16[128,128]{1,0:T(8,128)(2,1)S(1)}, bf16[128,128]{1,0:T(8,128)(2,1)S(1)}, u32[]{:S(2)}, u32[]{:S(2)}) collective-permute-start(bf16[128,128]{1,0:T(8,128)(2,1)S(1)} %get-tuple-element.86), channel_id=1, source_target_pairs={{0,4},{1,5},{2,6},{3,7},{4,0},{5,1},{6,2},{7,3},{8,12},{9,13},{10,... | collective-permute-start | bytes 98312 | tf_op jit(solution)/shard_map/ppermute | solution.py:397

commit v8 on v7

--- a/solution.py
+++ b/solution.py
@@ -31,7 +31,7 @@
     middle = jnp.floor((ray - offset) / slope + 0.5)
     middle = jnp.minimum(jnp.maximum(middle, 1.0), extent - 2.0)
     weights = [hat(ray, offset + slope * (middle + step)) for step in (-1.0, 0.0, 1.0)]
-    return middle, weights
+    return middle.astype(I32), weights
 
 
 def column_taps(offset, slope, extent):
@@ -211,6 +211,11 @@
         mode=lax.GatherScatterMode.PROMISE_IN_BOUNDS)
 
 
+def pack_pair(first, second):
+    kind = jnp.int16 if first.dtype == I32 else BF16
+    return jnp.concatenate([first, second], axis=0).astype(kind)
+
+
 def spread(ref, row, frames):
     return jnp.broadcast_to(ref[pl.ds(row, 1), :], (frames, ref.shape[1]))
 
@@ -222,7 +227,7 @@
 def for_slots(list_ref, body):
     def some(step, carry):
         for place in range(CHUNK):
-            body(step * CHUNK + place)
+            body(step * CHUNK + place, place)
         return carry
 
     lax.fori_loop(0, lax.div(list_ref[7, 0] + (CHUNK - 1), CHUNK), some, 0)
@@ -238,44 +243,39 @@
     lax.fori_loop(0, rows // step, some, 0)
 
 
-def project(sizes, stride, list_ref, values_ref, tables, projection, taps_ref):
+def project(sizes, stride, list_ref, values_ref, tables, projections, wide):
     capacity, depth, frames = sizes
     members = values_ref.shape[0] // stride
-    room = 4 * frames
-    tiles = taps_ref.shape[0] // (members * room)
-    extent = values_ref.shape[1]
+    rows = wide.shape[0] // members
 
     def widen(member, carry):
-        rows = pl.ds(pl.multiple_of(member * stride, 16), tiles * frames)
-        values = values_ref[rows, :].astype(F32)
-        before = pltpu.roll(values, 1, axis=1)
-        after = pltpu.roll(values, extent - 1, axis=1)
-        for tile in range(tiles):
-            at = slice(tile * frames, (tile + 1) * frames)
-            taps = jnp.concatenate([before[at], values[at], after[at], values[at]], axis=0)
-            to = pl.multiple_of((member * tiles + tile) * room, room)
-            taps_ref[pl.ds(to, room), :] = taps.astype(BF16)
+        at = pl.ds(pl.multiple_of(member * rows, rows), rows)
+        wide[at, :] = values_ref[pl.ds(pl.multiple_of(member * stride, 16), rows), :].astype(F32)
         return carry
 
     lax.fori_loop(0, members, widen, 0)
-    step = 16
-    voxel = lax.broadcasted_iota(I32, (step, extent), 0)
-    voxels = [(voxel + start).astype(F32).astype(BF16) for start in range(0, extent, step)]
-    one_hot, zero = jnp.ones((step, extent), BF16), jnp.zeros((step, extent), BF16)
-
-    def one(slot):
+
+    def one(slot, place):
         line = list_ref[0, slot]
+        taps = []
+        for start in range(0, depth, 2):
+            levels = range(start, start + 2)
+            values = [wide[tile_at(list_ref[2 + level, slot], frames), :] for level in levels]
+            middles = [spread(tables[0], line + level * capacity, frames) for level in levels]
+            lower = [
+                pick(pack_pair(value, value), pack_pair(middle - 1, middle)).astype(F32)
+                for value, middle in zip(values, middles)]
+            upper = pick(
+                pack_pair(*values), pack_pair(*[middle + 1 for middle in middles])).astype(F32)
+            for which, pair in enumerate(lower):
+                taps.append((pair[0:frames], pair[frames:2 * frames],
+                             upper[which * frames:(which + 1) * frames]))
         total = None
-        for level in range(depth):
-            row = line + level * capacity
-            at = pl.ds(pl.multiple_of(list_ref[2 + level, slot] * 4, room), room)
-            middle = spread(tables[0], row, step).astype(BF16)
-            choose = jnp.concatenate(
-                [jnp.where(voxel == middle, one_hot, zero) for voxel in voxels], axis=0)
-            taps = jnp.dot(taps_ref[at, :], choose, preferred_element_type=F32)
-            for place, ref in enumerate(tables[1:]):
-                term = spread(ref, row, frames) * taps[place * frames:(place + 1) * frames]
+        for level, three in enumerate(taps):
+            for ref, tap in zip(tables[1:], three):
+                term = spread(ref, line + level * capacity, frames) * tap
                 total = term if total is None else total + term
+        projection = projections[place % len(projections)]
         projection[tile_at(list_ref[1, slot], frames), :] += total.astype(BF16).astype(F32)
 
     for_slots(list_ref, one)
@@ -290,15 +290,14 @@
 
     for_rows(banks[0].shape[0], clear)
 
-    def one(slot):
+    def one(slot, place):
         line = list_ref[0, slot]
         values = residual[tile_at(list_ref[1, slot], frames), :]
-        twice = jnp.concatenate([values, values], axis=0).astype(BF16)
+        twice = pack_pair(values, values)
         for level in range(depth):
             row = line + level * capacity
             first = spread(tables[0], row, frames)
-            index = jnp.concatenate([first, first + 1], axis=0).astype(jnp.int16)
-            taps = pick(twice, index).astype(F32)
+            taps = pick(twice, pack_pair(first, first + 1)).astype(F32)
             term = (spread(tables[1], row, frames) * taps[0:frames]
                     + spread(tables[2], row, frames) * taps[frames:2 * frames])
             banks[level % len(banks)][tile_at(list_ref[2 + level, slot], frames), :] += term
@@ -310,15 +309,17 @@
     tables, refs = refs[:4], refs[4:]
     if not first:
         start_ref, refs = refs[0], refs[1:]
-    projection, taps_ref = refs
+    out_ref, wide, projection = refs
     projection[...] = jnp.zeros_like(projection) if first else start_ref[...]
-    project(sizes, stride, list_ref, values_ref, tables, projection, taps_ref)
+    out_ref[...] = jnp.zeros_like(out_ref)
+    project(sizes, stride, list_ref, values_ref, tables, (projection, out_ref), wide)
+    out_ref[...] += projection[...]
 
 
 def residual_of(sizes, projection, sinogram_ref, row_refs):
     total = sum([ref[...] for ref in row_refs[1:]], row_refs[0][...])
     weight = repeat_rows(1.0 / jnp.maximum(total, 1.0), sizes[2])
-    scaled = (sinogram_ref[...].astype(F32) - projection[...]) * weight
+    scaled = (sinogram_ref[...].astype(F32) - projection) * weight
     return scaled.astype(BF16).astype(F32)
 
 
@@ -327,11 +328,12 @@
     sinogram_ref, row_refs, refs = refs[0], refs[1:1 + n_rows], refs[1 + n_rows:]
     if not first:
         start_ref, refs = refs[0], refs[1:]
-    out_ref, residual, projection = refs[:3]
-    taps_ref, banks = refs[3], refs[4:]
+    out_ref, residual, projection, other = refs[:4]
+    wide, banks = refs[4], refs[5:]
     projection[...] = jnp.zeros_like(projection) if first else start_ref[...]
-    project(sizes, stride, list_ref, values_ref, forward, projection, taps_ref)
-    residual[...] = residual_of(sizes, projection, sinogram_ref, row_refs)
+    other[...] = jnp.zeros_like(other)
+    project(sizes, stride, list_ref, values_ref, forward, (projection, other), wide)
+    residual[...] = residual_of(sizes, projection[...] + other[...], sinogram_ref, row_refs)
     backproject(sizes, list_ref, residual, backward, banks)
 
     def finish(at):
@@ -364,11 +366,12 @@
         ref[...] = total.astype(ref.dtype)
 
 
-def join_kernel(z_ref, y_ref, after_ref, out_ref):
-    del after_ref
-    rows = z_ref.shape[0]
-    out_ref[0:rows, :] = z_ref[...]
-    out_ref[rows:2 * rows, :] = y_ref[...]
+def join_kernel(*refs):
+    out_ref, at = refs[-1], 0
+    for ref in refs[:-1]:
+        if ref.dtype == out_ref.dtype:
+            out_ref[at:at + ref.shape[0], :] = ref[...]
+            at += ref.shape[0]
 
 
 def update_kernel(n_pieces, volume_ref, column_ref, *refs):
@@ -407,7 +410,7 @@
     rows = voxel_tiles * frames
     sizes = (capacity, depth, frames)
     paired = n_slab == 16
-    n_bank = 2 if paired else 1
+    n_bank = 4 if paired else 1
     shape = jax.ShapeDtypeStruct
     rays = shape((ray_tiles * frames, extent), F32)
     volume = start_volume.reshape(rows, extent)
@@ -427,7 +430,7 @@
         group = capacity * depth
         lines = (members + 1) * group
         lanes = -(-members * capacity // 128) * 128
-        table = [shape((lines, extent), F32)] * 4
+        table = [shape((lines, extent), I32)] + [shape((lines, extent), F32)] * 3
         table += [shape((lines, extent), I32)] + [shape((lines, extent), F32)] * 2
         out = [shape((8, lanes), I32), shape((ray_tiles, extent), F32)] + table
         stride = values.shape[0] // members
@@ -436,18 +439,22 @@
             [SMEM, VMEM], out, me, values)
         return found[0], found[1], found[2:6], found[6:9]
 
+    def join(*parts, after=None):
+        total = sum(part.shape[0] for part in parts)
+        waits = [] if after is None else [after]
+        return call(
+            join_kernel, "join", 16, [VMEM] * len(parts) + [ANY] * len(waits),
+            shape((total, extent), BF16), *parts, *waits)
+
     def wide(members):
         return pltpu.VMEM((members * rows, extent), F32)
-
-    def taps(members):
-        return pltpu.VMEM((members * rows * 4, extent), BF16)
 
     def forward(values, group, start, members):
         operands = [values, *group[2]] + ([] if start is None else [start])
         return call(
             functools.partial(forward_kernel, sizes, values.shape[0] // members, start is None),
             "forward", 16, [SMEM] + [VMEM] * len(operands), rays,
-            group[0], *operands, scratch=[taps(members)])
+            group[0], *operands, scratch=[wide(members), pltpu.VMEM(rays.shape, F32)])
 
     def turn(values, group, row_sums, start, members):
         operands = [values, *group[2], *group[3], sino, *row_sums] + ([] if start is None else [start])
@@ -457,7 +464,7 @@
             "turn", 24 if paired else 40, [SMEM] + [VMEM] * len(operands),
             [shape((members * rows, extent), BF16), rays],
             group[0], *operands,
-            scratch=[pltpu.VMEM(rays.shape, F32), taps(members)] + [wide(members)] * n_bank)
+            scratch=[pltpu.VMEM(rays.shape, F32)] * 2 + [wide(members)] * (1 + n_bank))
 
     def backward(residual, group, members):
         return call(
@@ -479,16 +486,13 @@
     for sweep in range(ITERS):
         last = sweep + 1 == ITERS
         if paired:
-            along_z = jnp.concatenate(
-                [payload] + [exchange(payload, n_slab, distance) for distance in (8, 12, 4)], axis=0)
+            along_z = join(
+                payload, *[exchange(payload, n_slab, distance) for distance in (8, 12, 4)])
             along_y = exchange(along_z, n_slab, 2)
             if sweep == 0:
                 groups = [setup(along_z, 4)]
             projection = forward(along_z, groups[0], None, 4)
-            stride = along_z.shape[0]
-            other = exchange(
-                call(join_kernel, "join", 16, [VMEM, VMEM, ANY],
-                     shape((2 * stride, extent), BF16), along_z, along_y, projection), n_slab, 1)
+            other = exchange(join(along_z, along_y, after=projection), n_slab, 1)
             if sweep == 0:
                 groups += [setup(along_y, 4), setup(other, 8)]
                 row_sums = [group[1] for group in groups]

time: 87.2 us -> 79.3 us (0.909)
  Pallas kernels: 33.5 us -> 28.2 us
  starting transfers between devices: 28.6 us -> 23.7 us
  waiting for transfers between devices: 22.7 us -> 25.8 us
    pallas_call x23 -> x25, Pallas kernels: 33.5 us -> 28.2 us  [call(): pl.pallas_call(kernel, out_shape=out_shape, in_specs=in_specs, out_specs=...]
    ppermute x20, starting transfers between devices: 28.6 us -> 23.7 us  [exchange(): lax.ppermute(values, 'slab', [(device, device ^ distance) for device in r...]
    ppermute x20, waiting for transfers between devices: 22.7 us -> 25.8 us  [exchange(): lax.ppermute(values, 'slab', [(device, device ^ distance) for device in r...]
  transfers between devices with their start and end apart: 20 -> 20, of which waited for: 11 -> 13; matrix products, arithmetic and copies ran while one was open for 0% -> 0% of each run, Pallas kernels for 24% -> 21%
where the time goes in v8:
time: 79.3 us; the launch traced here: 78.8 us
  Pallas kernels  28.2 us (36%)
  waiting for transfers between devices  25.8 us (33%)
  starting transfers between devices  23.7 us (30%)
  local copies, waits for them, and re-layouts  0.83 us (1%)
    pallas_call x25, Pallas kernels, call(): pl.pallas_call(kernel, out_shape=out_shape, in_specs=in_specs, out_specs=...  28.2 us
    ppermute x20, waiting for transfers between devices, exchange(): lax.ppermute(values, 'slab', [(device, device ^ distance) for device in r...  25.8 us
    ppermute x20, starting transfers between devices, exchange(): lax.ppermute(values, 'slab', [(device, device ^ distance) for device in r...  23.7 us
  transfers between devices with their start and end apart: 20, of which 13 were waited for; matrix products, arithmetic and copies ran while one was open for 0% of the time, Pallas kernels for 21%

profile of v8, /device:TPU:0, one launch (start us, length us, event | category | flops | bytes accessed | tf_op | source)
XLA Modules:
  0.0 78.8 jit_solution(17481410714172615635)
XLA Ops:
  0.0 1.7 %pack.1.refs_0_ = bf16[192,128]{1,0:T(8,128)(2,1)} custom-call(f32[128,128]{1,0:T(8,128)} %bitcast.9, f32[4,256]{1,0:T(4,128)} %bitcast.13, f32[4,256]{1,0:T(4,128)} %bitcast.15, s32[4,256]{1,0:T(4,128)} %bitcast.17, s32[1,256]{1,0:T(1,128)} %bitcast.21, s32[1,16]{1,0:T(1,128)} %bitcast.19), custom_call_target="tpu_custom_call" | custom-call | tf_op jit(solution)/shard_map/pack/pallas_call | solution.py:388
  1.7 4.1 %collective-permute-start = (bf16[192,128]{1,0:T(8,128)(2,1)}, bf16[192,128]{1,0:T(8,128)(2,1)S(1)}, u32[]{:S(2)}, u32[]{:S(2)}) collective-permute-start(bf16[192,128]{1,0:T(8,128)(2,1)} %pack.1.refs_0_), channel_id=1, source_target_pairs={{0,8},{1,9},{2,10},{3,11},{4,12},{5,13},{6,14},{7,15},{8,0},{9,1},... | collective-permute-start | bytes 147464 | tf_op jit(solution)/shard_map/ppermute | solution.py:400
  5.8 1.3 %collective-permute-start.1 = (bf16[192,128]{1,0:T(8,128)(2,1)}, bf16[192,128]{1,0:T(8,128)(2,1)S(1)}, u32[]{:S(2)}, u32[]{:S(2)}) collective-permute-start(bf16[192,128]{1,0:T(8,128)(2,1)} %pack.1.refs_0_), channel_id=1, source_target_pairs={{0,12},{1,13},{2,14},{3,15},{4,8},{5,9},{6,10},{7,11},{8,4},{9,5},... | collective-permute-start | bytes 147464 | tf_op jit(solution)/shard_map/ppermute | solution.py:400
  7.3 1.2 %collective-permute-done.refs_1_ = bf16[192,128]{1,0:T(8,128)(2,1)S(1)} collective-permute-done((bf16[192,128]{1,0:T(8,128)(2,1)}, bf16[192,128]{1,0:T(8,128)(2,1)S(1)}, u32[]{:S(2)}, u32[]{:S(2)}) %collective-permute-start) | collective-permute-done | bytes 49184 | tf_op jit(solution)/shard_map/ppermute | solution.py:400
  8.6 3.4 %collective-permute-done.1.refs_2_ = bf16[192,128]{1,0:T(8,128)(2,1)S(1)} collective-permute-done((bf16[192,128]{1,0:T(8,128)(2,1)}, bf16[192,128]{1,0:T(8,128)(2,1)S(1)}, u32[]{:S(2)}, u32[]{:S(2)}) %collective-permute-start.1) | collective-permute-done | bytes 49184 | tf_op jit(solution)/shard_map/ppermute | solution.py:400
  12.8 1.6 %collective-permute-start.3 = (bf16[768,128]{1,0:T(8,128)(2,1)S(1)}, bf16[768,128]{1,0:T(8,128)(2,1)S(1)}, u32[]{:S(2)}, u32[]{:S(2)}) collective-permute-start(bf16[768,128]{1,0:T(8,128)(2,1)S(1)} %join.4.payload_ref.values_ref.refs_0_), channel_id=1, source_target_pairs={{0,2},{1,3},{2,0},{3,1},{4,6},{5,7},{6,4},{7,5},{8,10},{9,11},{10,... | collective-permute-start | bytes 589832 | tf_op jit(solution)/shard_map/ppermute | solution.py:400
  15.5 1.8 %forward.4.refs_2_.refs_4_ = f32[256,128]{1,0:T(8,128)S(1)} custom-call(s32[8,128]{1,0:T(8,128)S(1)} %get-tuple-element.46.list_ref, bf16[768,128]{1,0:T(8,128)(2,1)S(1)} %join.4.payload_ref.values_ref.refs_0_, s32[320,128]{1,0:T(8,128)S(1)} %get-tuple-element.47.refs_0_, f32[320,128]{1,0:T(8,128)S(1)} %get-tuple-element.48.refs_1_, ...), custom_call_target="tpu_custom_call" | custom-call | tf_op jit(solution)/shard_map/forward/pallas_call | solution.py:388
  17.2 1.2 %collective-permute-done.3.refs_1_.payload_ref.values_ref = bf16[768,128]{1,0:T(8,128)(2,1)S(1)} collective-permute-done((bf16[768,128]{1,0:T(8,128)(2,1)S(1)}, bf16[768,128]{1,0:T(8,128)(2,1)S(1)}, u32[]{:S(2)}, u32[]{:S(2)}) %collective-permute-start.3) | collective-permute-done | bytes 196640 | tf_op jit(solution)/shard_map/ppermute | solution.py:400
  19.8 1.7 %forward.5.refs_11_ = f32[256,128]{1,0:T(8,128)S(1)} custom-call(s32[8,128]{1,0:T(8,128)S(1)} %get-tuple-element.62.list_ref, bf16[768,128]{1,0:T(8,128)(2,1)S(1)} %collective-permute-done.3.refs_1_.payload_ref.values_ref, s32[320,128]{1,0:T(8,128)S(1)} %get-tuple-element.63.refs_0_, f32[320,128]{1,0:T(8,128)S(1)} %get-tuple-element.64.refs_1_, ...), custom_call_target="tpu_custom_call" | custom-call | tf_op jit(solution)/shard_map/forward/pallas_call | solution.py:388
  21.5 1.2 %setup.4 = (s32[8,128]{1,0:T(8,128)S(1)}, f32[32,128]{1,0:T(8,128)S(1)}, s32[576,128]{1,0:T(8,128)S(1)}, f32[576,128]{1,0:T(8,128)S(1)}, f32[576,128]{1,0:T(8,12...) custom-call(s32[1]{0:T(128)} %bitcast.5.me_ref, ...), custom_call_target="tpu_custom_call" | custom-call | tf_op jit(solution)/shard_map/setup/pallas_call | solution.py:388
  22.8 4.1 %turn.2 = (bf16[1024,128]{1,0:T(8,128)(2,1)S(1)}, f32[256,128]{1,0:T(8,128)S(1)}) custom-call(s32[8,128]{1,0:T(8,128)S(1)} %get-tuple-element.51.list_ref, bf16[1536,128]{1,0:T(8,128)(2,1)S(1)} %collective-permute-done.4.payload_ref.values_ref, s32[576,128]{1,0:T(8,128)S(1)} %get-tuple-element.52.refs_0_, f32[576,128]{1,0:T(8,128)S(1)} %get-tuple-element.53.refs_1_, ...), custom_call_target="tpu_custom_call" | custom-call | tf_op jit(solution)/shard_map/turn/pallas_call | solution.py:388
  26.9 1.3 %collective-permute-start.5 = (bf16[1024,128]{1,0:T(8,128)(2,1)S(1)}, bf16[1024,128]{1,0:T(8,128)(2,1)S(1)}, u32[]{:S(2)}, u32[]{:S(2)}) collective-permute-start(bf16[1024,128]{1,0:T(8,128)(2,1)S(1)} %get-tuple-element.71), channel_id=1, source_target_pairs={{0,1},{1,0},{2,3},{3,2},{4,5},{5,4},{6,7},{7,6},{8,9},{9,8},{10,11... | collective-permute-start | bytes 786440 | tf_op jit(solution)/shard_map/ppermute | solution.py:400
  28.1 1.6 %backward.5.sum_ref = f32[512,128]{1,0:T(8,128)S(1)} custom-call(s32[8,128]{1,0:T(8,128)S(1)} %get-tuple-element.62.list_ref, f32[256,128]{1,0:T(8,128)S(1)} %get-tuple-element.67.residual, s32[320,128]{1,0:T(8,128)S(1)} %get-tuple-element.72.refs_0_, f32[320,128]{1,0:T(8,128)S(1)} %get-tuple-element.73.refs_1_, f32[320,128]{1,0:T(8,128)S(1)} %get-tuple-element.74.refs_2_), custom_call_target="tpu_custom_call" | custom-call | tf_op jit(solution)/shard_map/backward/pallas_call | solution.py:388
  29.8 1.5 %collective-permute-start.6 = (bf16[512,128]{1,0:T(8,128)(2,1)S(1)}, bf16[512,128]{1,0:T(8,128)(2,1)S(1)}, u32[]{:S(2)}, u32[]{:S(2)}) collective-permute-start(bf16[512,128]{1,0:T(8,128)(2,1)S(1)} %combine_y.2), channel_id=1, source_target_pairs={{0,2},{1,3},{2,0},{3,1},{4,6},{5,7},{6,4},{7,5},{8,10},{9,11},{10,... | collective-permute-start | bytes 393224 | tf_op jit(solution)/shard_map/ppermute | solution.py:400
  31.3 1.6 %backward.4.sum_ref = f32[512,128]{1,0:T(8,128)S(1)} custom-call(s32[8,128]{1,0:T(8,128)S(1)} %get-tuple-element.46.list_ref, f32[256,128]{1,0:T(8,128)S(1)} %get-tuple-element.67.residual, s32[320,128]{1,0:T(8,128)S(1)} %get-tuple-element.68.refs_0_, f32[320,128]{1,0:T(8,128)S(1)} %get-tuple-element.69.refs_1_, f32[320,128]{1,0:T(8,128)S(1)} %get-tuple-element.70.refs_2_), custom_call_target="tpu_custom_call" | custom-call | tf_op jit(solution)/shard_map/backward/pallas_call | solution.py:388
  32.9 2.6 %collective-permute-done.6.y_ref = bf16[512,128]{1,0:T(8,128)(2,1)S(1)} collective-permute-done((bf16[512,128]{1,0:T(8,128)(2,1)S(1)}, bf16[512,128]{1,0:T(8,128)(2,1)S(1)}, u32[]{:S(2)}, u32[]{:S(2)}) %collective-permute-start.6) | collective-permute-done | bytes 131104 | tf_op jit(solution)/shard_map/ppermute | solution.py:400
  35.6 2.7 %collective-permute-start.7 = (bf16[128,128]{1,0:T(8,128)(2,1)S(1)}, bf16[128,128]{1,0:T(8,128)(2,1)S(1)}, u32[]{:S(2)}, u32[]{:S(2)}) collective-permute-start(bf16[128,128]{1,0:T(8,128)(2,1)S(1)} %get-tuple-element.76), channel_id=1, source_target_pairs={{0,8},{1,9},{2,10},{3,11},{4,12},{5,13},{6,14},{7,15},{8,0},{9,1},... | collective-permute-start | bytes 98312 | tf_op jit(solution)/shard_map/ppermute | solution.py:400
  40.4 3.5 %collective-permute-done.8.refs_2_ = bf16[128,128]{1,0:T(8,128)(2,1)S(1)} collective-permute-done((bf16[128,128]{1,0:T(8,128)(2,1)S(1)}, bf16[128,128]{1,0:T(8,128)(2,1)S(1)}, u32[]{:S(2)}, u32[]{:S(2)}) %collective-permute-start.8) | collective-permute-done | bytes 32800 | tf_op jit(solution)/shard_map/ppermute | solution.py:400
  46.1 1.4 %collective-permute-start.12 = (bf16[128,128]{1,0:T(8,128)(2,1)S(1)}, bf16[128,128]{1,0:T(8,128)(2,1)S(1)}, u32[]{:S(2)}, u32[]{:S(2)}) collective-permute-start(bf16[128,128]{1,0:T(8,128)(2,1)S(1)} %get-tuple-element.80.refs_0_), channel_id=1, source_target_pairs={{0,4},{1,5},{2,6},{3,7},{4,0},{5,1},{6,2},{7,3},{8,12},{9,13},{10,... | collective-permute-start | bytes 98312 | tf_op jit(solution)/shard_map/ppermute | solution.py:400
  47.5 1.3 %collective-permute-done.10.refs_1_ = bf16[128,128]{1,0:T(8,128)(2,1)S(1)} collective-permute-done((bf16[128,128]{1,0:T(8,128)(2,1)S(1)}, bf16[128,128]{1,0:T(8,128)(2,1)S(1)}, u32[]{:S(2)}, u32[]{:S(2)}) %collective-permute-start.10) | collective-permute-done | bytes 32800 | tf_op jit(solution)/shard_map/ppermute | solution.py:400
  48.8 1.8 %collective-permute-done.11.refs_2_ = bf16[128,128]{1,0:T(8,128)(2,1)S(1)} collective-permute-done((bf16[128,128]{1,0:T(8,128)(2,1)S(1)}, bf16[128,128]{1,0:T(8,128)(2,1)S(1)}, u32[]{:S(2)}, u32[]{:S(2)}) %collective-permute-start.11) | collective-permute-done | bytes 32800 | tf_op jit(solution)/shard_map/ppermute | solution.py:400
  51.4 1.7 %forward.6.refs_2_.refs_4_ = f32[256,128]{1,0:T(8,128)S(1)} custom-call(s32[8,128]{1,0:T(8,128)S(1)} %get-tuple-element.46.list_ref, bf16[512,128]{1,0:T(8,128)(2,1)S(1)} %join.6.values_ref.refs_0_, s32[320,128]{1,0:T(8,128)S(1)} %get-tuple-element.47.refs_0_, f32[320,128]{1,0:T(8,128)S(1)} %get-tuple-element.48.refs_1_, ...), custom_call_target="tpu_custom_call" | custom-call | tf_op jit(solution)/shard_map/forward/pallas_call | solution.py:388
  53.1 2.6 %collective-permute-done.13.refs_1_.values_ref = bf16[512,128]{1,0:T(8,128)(2,1)S(1)} collective-permute-done((bf16[512,128]{1,0:T(8,128)(2,1)S(1)}, bf16[512,128]{1,0:T(8,128)(2,1)S(1)}, u32[]{:S(2)}, u32[]{:S(2)}) %collective-permute-start.13) | collective-permute-done | bytes 131104 | tf_op jit(solution)/shard_map/ppermute | solution.py:400
  55.8 1.7 %forward.7.refs_11_ = f32[256,128]{1,0:T(8,128)S(1)} custom-call(s32[8,128]{1,0:T(8,128)S(1)} %get-tuple-element.62.list_ref, bf16[512,128]{1,0:T(8,128)(2,1)S(1)} %collective-permute-done.13.refs_1_.values_ref, s32[320,128]{1,0:T(8,128)S(1)} %get-tuple-element.63.refs_0_, f32[320,128]{1,0:T(8,128)S(1)} %get-tuple-element.64.refs_1_, ...), custom_call_target="tpu_custom_call" | custom-call | tf_op jit(solution)/shard_map/forward/pallas_call | solution.py:388
  57.5 4.1 %turn.3 = (bf16[1024,128]{1,0:T(8,128)(2,1)S(1)}, f32[256,128]{1,0:T(8,128)S(1)}) custom-call(s32[8,128]{1,0:T(8,128)S(1)} %get-tuple-element.51.list_ref, bf16[1024,128]{1,0:T(8,128)(2,1)S(1)} %collective-permute-done.14.values_ref, s32[576,128]{1,0:T(8,128)S(1)} %get-tuple-element.52.refs_0_, f32[576,128]{1,0:T(8,128)S(1)} %get-tuple-element.53.refs_1_, ...), custom_call_target="tpu_custom_call" | custom-call | tf_op jit(solution)/shard_map/turn/pallas_call | solution.py:388
  61.6 1.3 %collective-permute-start.15 = (bf16[1024,128]{1,0:T(8,128)(2,1)S(1)}, bf16[1024,128]{1,0:T(8,128)(2,1)S(1)}, u32[]{:S(2)}, u32[]{:S(2)}) collective-permute-start(bf16[1024,128]{1,0:T(8,128)(2,1)S(1)} %get-tuple-element.82), channel_id=1, source_target_pairs={{0,1},{1,0},{2,3},{3,2},{4,5},{5,4},{6,7},{7,6},{8,9},{9,8},{10,11... | collective-permute-start | bytes 786440 | tf_op jit(solution)/shard_map/ppermute | solution.py:400
  62.9 1.6 %backward.7.sum_ref = f32[512,128]{1,0:T(8,128)S(1)} custom-call(s32[8,128]{1,0:T(8,128)S(1)} %get-tuple-element.62.list_ref, f32[256,128]{1,0:T(8,128)S(1)} %get-tuple-element.81.residual, s32[320,128]{1,0:T(8,128)S(1)} %get-tuple-element.72.refs_0_, f32[320,128]{1,0:T(8,128)S(1)} %get-tuple-element.73.refs_1_, f32[320,128]{1,0:T(8,128)S(1)} %get-tuple-element.74.refs_2_), custom_call_target="tpu_custom_call" | custom-call | tf_op jit(solution)/shard_map/backward/pallas_call | solution.py:388
  65.2 1.6 %backward.6.sum_ref = f32[512,128]{1,0:T(8,128)S(1)} custom-call(s32[8,128]{1,0:T(8,128)S(1)} %get-tuple-element.46.list_ref, f32[256,128]{1,0:T(8,128)S(1)} %get-tuple-element.81.residual, s32[320,128]{1,0:T(8,128)S(1)} %get-tuple-element.68.refs_0_, f32[320,128]{1,0:T(8,128)S(1)} %get-tuple-element.69.refs_1_, f32[320,128]{1,0:T(8,128)S(1)} %get-tuple-element.70.refs_2_), custom_call_target="tpu_custom_call" | custom-call | tf_op jit(solution)/shard_map/backward/pallas_call | solution.py:388
  66.8 3.2 %collective-permute-done.16.y_ref = bf16[512,128]{1,0:T(8,128)(2,1)S(1)} collective-permute-done((bf16[512,128]{1,0:T(8,128)(2,1)S(1)}, bf16[512,128]{1,0:T(8,128)(2,1)S(1)}, u32[]{:S(2)}, u32[]{:S(2)}) %collective-permute-start.16) | collective-permute-done | bytes 131104 | tf_op jit(solution)/shard_map/ppermute | solution.py:400
  70.0 2.1 %collective-permute-start.17 = (bf16[128,128]{1,0:T(8,128)(2,1)S(1)}, bf16[128,128]{1,0:T(8,128)(2,1)S(1)}, u32[]{:S(2)}, u32[]{:S(2)}) collective-permute-start(bf16[128,128]{1,0:T(8,128)(2,1)S(1)} %get-tuple-element.84), channel_id=1, source_target_pairs={{0,8},{1,9},{2,10},{3,11},{4,12},{5,13},{6,14},{7,15},{8,0},{9,1},... | collective-permute-start | bytes 98312 | tf_op jit(solution)/shard_map/ppermute | solution.py:400
  72.1 1.8 %collective-permute-start.18 = (bf16[128,128]{1,0:T(8,128)(2,1)S(1)}, bf16[128,128]{1,0:T(8,128)(2,1)S(1)}, u32[]{:S(2)}, u32[]{:S(2)}) collective-permute-start(bf16[128,128]{1,0:T(8,128)(2,1)S(1)} %get-tuple-element.85), channel_id=1, source_target_pairs={{0,12},{1,13},{2,14},{3,15},{4,8},{5,9},{6,10},{7,11},{8,4},{9,5},... | collective-permute-start | bytes 98312 | tf_op jit(solution)/shard_map/ppermute | solution.py:400
  75.0 3.0 %collective-permute-done.18.refs_2_ = bf16[128,128]{1,0:T(8,128)(2,1)S(1)} collective-permute-done((bf16[128,128]{1,0:T(8,128)(2,1)S(1)}, bf16[128,128]{1,0:T(8,128)(2,1)S(1)}, u32[]{:S(2)}, u32[]{:S(2)}) %collective-permute-start.18) | collective-permute-done | bytes 32800 | tf_op jit(solution)/shard_map/ppermute | solution.py:400
  (47 shorter events, 11.3 us)
Async XLA Ops:
  1.7 6.9 %collective-permute-start = (bf16[192,128]{1,0:T(8,128)(2,1)}, bf16[192,128]{1,0:T(8,128)(2,1)S(1)}, u32[]{:S(2)}, u32[]{:S(2)}) collective-permute-start(bf16[192,128]{1,0:T(8,128)(2,1)} %pack.1.refs_0_), channel_id=1, source_target_pairs={{0,8},{1,9},{2,10},{3,11},{4,12},{5,13},{6,14},{7,15},{8,0},{9,1},... | collective-permute-start | bytes 147464 | tf_op jit(solution)/shard_map/ppermute | solution.py:400
  5.8 6.2 %collective-permute-start.1 = (bf16[192,128]{1,0:T(8,128)(2,1)}, bf16[192,128]{1,0:T(8,128)(2,1)S(1)}, u32[]{:S(2)}, u32[]{:S(2)}) collective-permute-start(bf16[192,128]{1,0:T(8,128)(2,1)} %pack.1.refs_0_), channel_id=1, source_target_pairs={{0,12},{1,13},{2,14},{3,15},{4,8},{5,9},{6,10},{7,11},{8,4},{9,5},... | collective-permute-start | bytes 147464 | tf_op jit(solution)/shard_map/ppermute | solution.py:400
  7.1 4.8 %collective-permute-start.2 = (bf16[192,128]{1,0:T(8,128)(2,1)}, bf16[192,128]{1,0:T(8,128)(2,1)S(1)}, u32[]{:S(2)}, u32[]{:S(2)}) collective-permute-start(bf16[192,128]{1,0:T(8,128)(2,1)} %pack.1.refs_0_), channel_id=1, source_target_pairs={{0,4},{1,5},{2,6},{3,7},{4,0},{5,1},{6,2},{7,3},{8,12},{9,13},{10,... | collective-permute-start | bytes 147464 | tf_op jit(solution)/shard_map/ppermute | solution.py:400
  11.9 0.8 %copy-start.2 = (bf16[192,128]{1,0:T(8,128)(2,1)S(1)}, bf16[192,128]{1,0:T(8,128)(2,1)}, u32[]{:S(2)}) copy-start(bf16[192,128]{1,0:T(8,128)(2,1)} %pack.1.refs_0_) | copy-start | bytes 147460
  12.8 5.7 %collective-permute-start.3 = (bf16[768,128]{1,0:T(8,128)(2,1)S(1)}, bf16[768,128]{1,0:T(8,128)(2,1)S(1)}, u32[]{:S(2)}, u32[]{:S(2)}) collective-permute-start(bf16[768,128]{1,0:T(8,128)(2,1)S(1)} %join.4.payload_ref.values_ref.refs_0_), channel_id=1, source_target_pairs={{0,2},{1,3},{2,0},{3,1},{4,6},{5,7},{6,4},{7,5},{8,10},{9,11},{10,... | collective-permute-start | bytes 589832 | tf_op jit(solution)/shard_map/ppermute | solution.py:400
  18.5 3.0 %collective-permute-start.4 = (bf16[1536,128]{1,0:T(8,128)(2,1)S(1)}, bf16[1536,128]{1,0:T(8,128)(2,1)S(1)}, u32[]{:S(2)}, u32[]{:S(2)}) collective-permute-start(bf16[1536,128]{1,0:T(8,128)(2,1)S(1)} %join.5), channel_id=1, source_target_pairs={{0,1},{1,0},{2,3},{3,2},{4,5},{5,4},{6,7},{7,6},{8,9},{9,8},{10,11... | collective-permute-start | bytes 1179656 | tf_op jit(solution)/shard_map/ppermute | solution.py:400
  21.5 1.2 %copy-start.1 = (bf16[32,8,128]{2,1,0:T(8,128)(2,1)S(1)}, bf16[32,8,128]{2,1,0:T(8,128)(2,1)}, u32[]{:S(2)}) copy-start(bf16[32,8,128]{2,1,0:T(8,128)(2,1)} %param.7) | copy-start | bytes 196612
  26.9 2.9 %collective-permute-start.5 = (bf16[1024,128]{1,0:T(8,128)(2,1)S(1)}, bf16[1024,128]{1,0:T(8,128)(2,1)S(1)}, u32[]{:S(2)}, u32[]{:S(2)}) collective-permute-start(bf16[1024,128]{1,0:T(8,128)(2,1)S(1)} %get-tuple-element.71), channel_id=1, source_target_pairs={{0,1},{1,0},{2,3},{3,2},{4,5},{5,4},{6,7},{7,6},{8,9},{9,8},{10,11... | collective-permute-start | bytes 786440 | tf_op jit(solution)/shard_map/ppermute | solution.py:400
  29.8 5.7 %collective-permute-start.6 = (bf16[512,128]{1,0:T(8,128)(2,1)S(1)}, bf16[512,128]{1,0:T(8,128)(2,1)S(1)}, u32[]{:S(2)}, u32[]{:S(2)}) collective-permute-start(bf16[512,128]{1,0:T(8,128)(2,1)S(1)} %combine_y.2), channel_id=1, source_target_pairs={{0,2},{1,3},{2,0},{3,1},{4,6},{5,7},{6,4},{7,5},{8,10},{9,11},{10,... | collective-permute-start | bytes 393224 | tf_op jit(solution)/shard_map/ppermute | solution.py:400
  35.5 3.6 %copy-start.3 = (f32[256,4]{0,1:T(4,128)S(1)}, f32[256,4]{0,1:T(4,128)}, u32[]{:S(2)}) copy-start(f32[256,4]{0,1:T(4,128)} %param.13) | copy-start | bytes 12292
  35.5 3.6 %copy-start.4 = (f32[256,4]{0,1:T(4,128)S(1)}, f32[256,4]{0,1:T(4,128)}, u32[]{:S(2)}) copy-start(f32[256,4]{0,1:T(4,128)} %param.12) | copy-start | bytes 12292
  35.5 3.6 %copy-start.5 = (s32[256,4]{0,1:T(4,128)S(1)}, s32[256,4]{0,1:T(4,128)}, u32[]{:S(2)}) copy-start(s32[256,4]{0,1:T(4,128)} %param.9) | copy-start | bytes 12292
  35.5 3.6 %copy-start.6 = (s32[16]{0:T(128)S(1)}, s32[16]{0:T(128)}, u32[]{:S(2)}) copy-start(s32[16]{0:T(128)} %param.11) | copy-start | bytes 196
  35.5 8.4 %copy-start = (f32[16,8,128]{2,1,0:T(8,128)S(1)}, f32[16,8,128]{2,1,0:T(8,128)}, u32[]{:S(2)}) copy-start(f32[16,8,128]{2,1,0:T(8,128)} %param.8) | copy-start | bytes 196612
  35.6 4.9 %collective-permute-start.7 = (bf16[128,128]{1,0:T(8,128)(2,1)S(1)}, bf16[128,128]{1,0:T(8,128)(2,1)S(1)}, u32[]{:S(2)}, u32[]{:S(2)}) collective-permute-start(bf16[128,128]{1,0:T(8,128)(2,1)S(1)} %get-tuple-element.76), channel_id=1, source_target_pairs={{0,8},{1,9},{2,10},{3,11},{4,12},{5,13},{6,14},{7,15},{8,0},{9,1},... | collective-permute-start | bytes 98312 | tf_op jit(solution)/shard_map/ppermute | solution.py:400
  38.2 5.7 %collective-permute-start.8 = (bf16[128,128]{1,0:T(8,128)(2,1)S(1)}, bf16[128,128]{1,0:T(8,128)(2,1)S(1)}, u32[]{:S(2)}, u32[]{:S(2)}) collective-permute-start(bf16[128,128]{1,0:T(8,128)(2,1)S(1)} %get-tuple-element.77), channel_id=1, source_target_pairs={{0,12},{1,13},{2,14},{3,15},{4,8},{5,9},{6,10},{7,11},{8,4},{9,5},... | collective-permute-start | bytes 98312 | tf_op jit(solution)/shard_map/ppermute | solution.py:400
  39.0 4.9 %collective-permute-start.9 = (bf16[128,128]{1,0:T(8,128)(2,1)S(1)}, bf16[128,128]{1,0:T(8,128)(2,1)S(1)}, u32[]{:S(2)}, u32[]{:S(2)}) collective-permute-start(bf16[128,128]{1,0:T(8,128)(2,1)S(1)} %get-tuple-element.78), channel_id=1, source_target_pairs={{0,4},{1,5},{2,6},{3,7},{4,0},{5,1},{6,2},{7,3},{8,12},{9,13},{10,... | collective-permute-start | bytes 98312 | tf_op jit(solution)/shard_map/ppermute | solution.py:400
  44.0 4.9 %collective-permute-start.10 = (bf16[128,128]{1,0:T(8,128)(2,1)S(1)}, bf16[128,128]{1,0:T(8,128)(2,1)S(1)}, u32[]{:S(2)}, u32[]{:S(2)}) collective-permute-start(bf16[128,128]{1,0:T(8,128)(2,1)S(1)} %get-tuple-element.80.refs_0_), channel_id=1, source_target_pairs={{0,8},{1,9},{2,10},{3,11},{4,12},{5,13},{6,14},{7,15},{8,0},{9,1},... | collective-permute-start | bytes 98312 | tf_op jit(solution)/shard_map/ppermute | solution.py:400
  44.9 5.7 %collective-permute-start.11 = (bf16[128,128]{1,0:T(8,128)(2,1)S(1)}, bf16[128,128]{1,0:T(8,128)(2,1)S(1)}, u32[]{:S(2)}, u32[]{:S(2)}) collective-permute-start(bf16[128,128]{1,0:T(8,128)(2,1)S(1)} %get-tuple-element.80.refs_0_), channel_id=1, source_target_pairs={{0,12},{1,13},{2,14},{3,15},{4,8},{5,9},{6,10},{7,11},{8,4},{9,5},... | collective-permute-start | bytes 98312 | tf_op jit(solution)/shard_map/ppermute | solution.py:400
  46.1 4.5 %collective-permute-start.12 = (bf16[128,128]{1,0:T(8,128)(2,1)S(1)}, bf16[128,128]{1,0:T(8,128)(2,1)S(1)}, u32[]{:S(2)}, u32[]{:S(2)}) collective-permute-start(bf16[128,128]{1,0:T(8,128)(2,1)S(1)} %get-tuple-element.80.refs_0_), channel_id=1, source_target_pairs={{0,4},{1,5},{2,6},{3,7},{4,0},{5,1},{6,2},{7,3},{8,12},{9,13},{10,... | collective-permute-start | bytes 98312 | tf_op jit(solution)/shard_map/ppermute | solution.py:400
  50.7 5.0 %collective-permute-start.13 = (bf16[512,128]{1,0:T(8,128)(2,1)S(1)}, bf16[512,128]{1,0:T(8,128)(2,1)S(1)}, u32[]{:S(2)}, u32[]{:S(2)}) collective-permute-start(bf16[512,128]{1,0:T(8,128)(2,1)S(1)} %join.6.values_ref.refs_0_), channel_id=1, source_target_pairs={{0,2},{1,3},{2,0},{3,1},{4,6},{5,7},{6,4},{7,5},{8,10},{9,11},{10,... | collective-permute-start | bytes 393224 | tf_op jit(solution)/shard_map/ppermute | solution.py:400
  55.7 1.8 %collective-permute-start.14 = (bf16[1024,128]{1,0:T(8,128)(2,1)S(1)}, bf16[1024,128]{1,0:T(8,128)(2,1)S(1)}, u32[]{:S(2)}, u32[]{:S(2)}) collective-permute-start(bf16[1024,128]{1,0:T(8,128)(2,1)S(1)} %join.7), channel_id=1, source_target_pairs={{0,1},{1,0},{2,3},{3,2},{4,5},{5,4},{6,7},{7,6},{8,9},{9,8},{10,11... | collective-permute-start | bytes 786440 | tf_op jit(solution)/shard_map/ppermute | solution.py:400
  61.6 2.9 %collective-permute-start.15 = (bf16[1024,128]{1,0:T(8,128)(2,1)S(1)}, bf16[1024,128]{1,0:T(8,128)(2,1)S(1)}, u32[]{:S(2)}, u32[]{:S(2)}) collective-permute-start(bf16[1024,128]{1,0:T(8,128)(2,1)S(1)} %get-tuple-element.82), channel_id=1, source_target_pairs={{0,1},{1,0},{2,3},{3,2},{4,5},{5,4},{6,7},{7,6},{8,9},{9,8},{10,11... | collective-permute-start | bytes 786440 | tf_op jit(solution)/shard_map/ppermute | solution.py:400
  64.6 5.4 %collective-permute-start.16 = (bf16[512,128]{1,0:T(8,128)(2,1)S(1)}, bf16[512,128]{1,0:T(8,128)(2,1)S(1)}, u32[]{:S(2)}, u32[]{:S(2)}) collective-permute-start(bf16[512,128]{1,0:T(8,128)(2,1)S(1)} %combine_y.3), channel_id=1, source_target_pairs={{0,2},{1,3},{2,0},{3,1},{4,6},{5,7},{6,4},{7,5},{8,10},{9,11},{10,... | collective-permute-start | bytes 393224 | tf_op jit(solution)/shard_map/ppermute | solution.py:400
  70.0 5.0 %collective-permute-start.17 = (bf16[128,128]{1,0:T(8,128)(2,1)S(1)}, bf16[128,128]{1,0:T(8,128)(2,1)S(1)}, u32[]{:S(2)}, u32[]{:S(2)}) collective-permute-start(bf16[128,128]{1,0:T(8,128)(2,1)S(1)} %get-tuple-element.84), channel_id=1, source_target_pairs={{0,8},{1,9},{2,10},{3,11},{4,12},{5,13},{6,14},{7,15},{8,0},{9,1},... | collective-permute-start | bytes 98312 | tf_op jit(solution)/shard_map/ppermute | solution.py:400
  72.1 5.8 %collective-permute-start.18 = (bf16[128,128]{1,0:T(8,128)(2,1)S(1)}, bf16[128,128]{1,0:T(8,128)(2,1)S(1)}, u32[]{:S(2)}, u32[]{:S(2)}) collective-permute-start(bf16[128,128]{1,0:T(8,128)(2,1)S(1)} %get-tuple-element.85), channel_id=1, source_target_pairs={{0,12},{1,13},{2,14},{3,15},{4,8},{5,9},{6,10},{7,11},{8,4},{9,5},... | collective-permute-start | bytes 98312 | tf_op jit(solution)/shard_map/ppermute | solution.py:400
  73.9 4.3 %collective-permute-start.19 = (bf16[128,128]{1,0:T(8,128)(2,1)S(1)}, bf16[128,128]{1,0:T(8,128)(2,1)S(1)}, u32[]{:S(2)}, u32[]{:S(2)}) collective-permute-start(bf16[128,128]{1,0:T(8,128)(2,1)S(1)} %get-tuple-element.86), channel_id=1, source_target_pairs={{0,4},{1,5},{2,6},{3,7},{4,0},{5,1},{6,2},{7,3},{8,12},{9,13},{10,... | collective-permute-start | bytes 98312 | tf_op jit(solution)/shard_map/ppermute | solution.py:400

commit v9 on v8

v9 whole, which is shorter than its diff:
```python
import functools

import jax
import jax.numpy as jnp
from jax import lax
from jax.experimental import pallas as pl
from jax.experimental.pallas import tpu as pltpu
from jax.sharding import PartitionSpec as P

ITERS = 2
CHUNK = 8
F32 = jnp.float32
BF16 = jnp.bfloat16
I32 = jnp.int32
HIGHEST = lax.Precision.HIGHEST
VMEM = pl.BlockSpec(memory_space=pltpu.VMEM)
ANY = pl.BlockSpec(memory_space=pl.ANY)


def hat(ray, centre):
    return jnp.maximum(0.0, 1.0 - jnp.abs(ray - centre)).astype(BF16)


def row_taps(offset, slope, extent):
    shape = (offset.shape[0], extent)
    ray = lax.broadcasted_iota(I32, shape, 1).astype(F32)
    offset = jnp.broadcast_to(offset, shape)
    slope = jnp.broadcast_to(slope, shape)
    middle = jnp.floor((ray - offset) / slope + 0.5)
    middle = jnp.minimum(jnp.maximum(middle, 1.0), extent - 2.0)
    weights = [hat(ray, offset + slope * (middle + step)) for step in (-1.0, 0.0, 1.0)]
    return middle.astype(I32), weights


def column_taps(offset, slope, extent):
    shape = (offset.shape[0], extent)
    voxel = lax.broadcasted_iota(I32, shape, 1).astype(F32)
    centre = jnp.broadcast_to(offset, shape) + jnp.broadcast_to(slope, shape) * voxel
    first = jnp.minimum(jnp.maximum(jnp.floor(centre), 0.0), extent - 2.0)
    weights = [hat(first + step, centre) for step in (0.0, 1.0)]
    return first.astype(I32), weights


def repeat_rows(values, times):
    return jnp.concatenate(
        [jnp.broadcast_to(values[row:row + 1, :], (times, values.shape[1]))
         for row in range(values.shape[0])], axis=0)


def contract_lanes(left, right):
    return lax.dot_general(
        left.astype(BF16), right.astype(BF16), (((1,), (1,)), ((), ())), preferred_element_type=F32)


def per_slot(live_ref, slots, capacity):
    targets = live_ref.shape[1]
    slot = lax.broadcasted_iota(I32, (targets, slots), 1)
    owner = lax.broadcasted_iota(I32, (targets, slots), 0)
    expand = (lax.div(slot, capacity) == owner).astype(F32)
    return jnp.dot(live_ref[...].astype(F32), expand, precision=HIGHEST, preferred_element_type=F32)


def pack_kernel(capacity, *refs):
    sources, out_ref, loaded, arrived = refs[:6], refs[6], refs[7:13], refs[13]
    copies = [
        pltpu.make_async_copy(source, ref, arrived.at[place])
        for place, (source, ref) in enumerate(zip(sources, loaded))]
    for copy in copies:
        copy.start()
    for copy in copies:
        copy.wait()
    volume_ref, offset_ref, slope_ref, voxel_ref, ray_ref, live_ref = loaded
    rows, extent = volume_ref.shape
    out_ref[0:rows, :] = volume_ref[...].astype(BF16)
    slots = ray_ref.shape[1]
    fields = []
    for ref in (offset_ref, slope_ref):
        left = ref[...]
        for addend in range(3):
            part = left.astype(BF16).astype(F32)
            fields.append(part)
            left = left - part
    fields.append(voxel_ref[...].astype(F32))
    fields.append(ray_ref[...].astype(F32))
    fields.append(per_slot(live_ref, slots, capacity))
    used = sum(field.shape[0] for field in fields)
    fields.append(jnp.zeros((-used % 16, slots), F32))
    fields = jnp.concatenate(fields, axis=0)
    height = fields.shape[0]
    for part in range(slots // extent):
        at = pl.ds(rows + part * height, height)
        out_ref[at, :] = fields[:, part * extent:(part + 1) * extent].astype(BF16)


def setup_kernel(members, stride, span, sizes, tiles, wanted, payload_ref, *refs):
    refs = refs[-(len(wanted) + 8):]
    list_refs, row_ref, tables = refs[:len(wanted)], refs[len(wanted)], refs[len(wanted) + 1:]
    capacity, depth, frames = sizes
    width = span * capacity
    extent = row_ref.shape[1]
    ray_tiles = row_ref.shape[0] // span
    height = -(-(7 * depth + 2) // 16) * 16
    lanes = list_refs[0].shape[1]
    me = lax.axis_index("slab").astype(I32)
    parity = lax.rem(me, span)
    first_slot = (me - parity) * capacity
    part = lax.div(first_slot, extent)
    shift = lax.rem(extent - lax.rem(first_slot, extent), extent)

    def collect(member, lined):
        at = member * stride + tiles * frames + part * height
        raw = payload_ref[pl.ds(pl.multiple_of(at, 16), height), :].astype(F32)
        offset = (raw[0:depth] + raw[depth:2 * depth]) + raw[2 * depth:3 * depth]
        slope = (raw[3 * depth:4 * depth] + raw[4 * depth:5 * depth]) + raw[5 * depth:6 * depth]
        fields = jnp.concatenate(
            [offset, slope, raw[6 * depth:7 * depth + 2],
             jnp.zeros((16 - 3 * depth - 2, extent), F32)], axis=0)
        fields = pltpu.roll(fields, shift, axis=1)
        lane = lax.broadcasted_iota(I32, fields.shape, 1)
        fields = jnp.where(lane < width, fields, 0.0)
        if lanes > extent:
            fields = jnp.concatenate(
                [fields, jnp.zeros((fields.shape[0], lanes - extent), F32)], axis=1)
        return lined + pltpu.roll(fields, member * width, axis=1)

    lined = jnp.zeros((16, lanes), F32)
    if members <= 16:
        for member in range(members):
            lined = collect(member, lined)
    else:
        lined = lax.fori_loop(0, members, collect, lined)

    columns = lined.T
    summed = None
    for level in range(depth):
        offset = columns[:, level:level + 1]
        slope = columns[:, depth + level:depth + level + 1]
        middle, weights = row_taps(offset, slope, extent)
        first, pair = column_taps(offset, slope, extent)
        wide = [weight.astype(F32) for weight in weights]
        values = [middle] + wide + [first] + [weight.astype(F32) for weight in pair]
        at = level * (lanes + 8)
        for ref, value in zip(tables, values):
            ref[at:at + lanes, :] = value
            blank = jnp.ones if ref.dtype == I32 else jnp.zeros
            ref[at + lanes:at + lanes + 8, :] = blank((8, extent), ref.dtype)
        parts = (wide[0] + wide[1]) + wide[2]
        summed = parts if summed is None else summed + parts

    slot = lax.broadcasted_iota(I32, (1, lanes), 1)
    within = lax.rem(slot, width)
    target = lax.bitwise_xor(lax.div(within, capacity), parity)
    ray = lined[3 * depth:3 * depth + 1]
    count = lined[3 * depth + 1:3 * depth + 2]
    alive = jnp.logical_and(lax.rem(within, capacity).astype(F32) < count, slot < members * width)
    tile = lax.broadcasted_iota(I32, (span * ray_tiles, lanes), 0).astype(F32)
    place = ray + (target * ray_tiles).astype(F32)
    place = jnp.where(alive, place, -1.0)
    hot = (jnp.broadcast_to(place, tile.shape) == tile).astype(F32)
    row_ref[...] = jnp.dot(hot, summed, precision=HIGHEST, preferred_element_type=F32)

    table = jnp.concatenate(
        [slot.astype(F32), ray, target.astype(F32), lined[2 * depth:3 * depth],
         jnp.zeros((5 - depth, lanes), F32)], axis=0)
    order = lax.broadcasted_iota(I32, (lanes, lanes), 0)
    earlier = (lax.broadcasted_iota(I32, (lanes, lanes), 1) < order).astype(F32)
    for ref, kind in zip(list_refs, wanted):
        taken = alive if kind is None else jnp.logical_and(alive, target == kind)
        taken = taken.astype(F32)
        position = contract_lanes(jnp.broadcast_to(taken, (8, lanes)), earlier)[0:1]
        position = jnp.where(taken > 0.0, position, -1.0).astype(I32)
        choose = jnp.broadcast_to(position, (lanes, lanes)) == order
        packed = (contract_lanes(table, choose.astype(F32)) + 0.5).astype(I32)
        total = jnp.sum(taken, axis=1, keepdims=True).astype(I32)
        line = jnp.where(slot < total, packed[0:1], lanes)
        base = packed[1:2] if kind is not None else packed[1:2] + packed[2:3] * ray_tiles
        member = lax.div(packed[0:1], width) * tiles
        rows = [line, base * frames]
        rows += [(packed[3 + level:4 + level] + member) * frames for level in range(depth)]
        rows += [jnp.zeros((5 - depth, lanes), I32), jnp.broadcast_to(total, (1, lanes))]
        ref[...] = jnp.concatenate(rows, axis=0)


def column_kernel(sizes, offset_ref, slope_ref, voxel_ref, live_ref, out_ref):
    capacity, depth, frames = sizes
    tiles = out_ref.shape[0] // frames
    slots = offset_ref.shape[1]
    extent = out_ref.shape[1]
    offsets = offset_ref[...].T
    slopes = slope_ref[...].T
    within = lax.rem(lax.broadcasted_iota(I32, (1, slots), 1), capacity).astype(F32)
    alive = jnp.broadcast_to(within, (tiles, slots)) < per_slot(live_ref, slots, capacity)
    total = jnp.zeros((tiles, extent), F32)
    for level in range(depth):
        unused, pair = column_taps(
            offsets[:, level:level + 1], slopes[:, level:level + 1], extent)
        tile_of = jnp.broadcast_to(voxel_ref[level:level + 1, :], (tiles, slots))
        match = tile_of == lax.broadcasted_iota(I32, (tiles, slots), 0)
        hot = jnp.logical_and(match, alive).astype(F32).astype(BF16)
        for weight in pair:
            total += jnp.dot(hot, weight, preferred_element_type=F32)
    out_ref[...] = repeat_rows(1.0 / jnp.maximum(total, 1.0), frames)


def pick(values, index):
    numbers = lax.GatherDimensionNumbers(
        offset_dims=(), collapsed_slice_dims=(1,), start_index_map=(1,),
        operand_batching_dims=(0,), start_indices_batching_dims=(0,))
    return lax.gather(
        values, index[:, :, None], numbers, slice_sizes=(1, 1),
        mode=lax.GatherScatterMode.PROMISE_IN_BOUNDS)


def pack_pair(first, second):
    kind = jnp.int16 if first.dtype == I32 else BF16
    return jnp.concatenate([first, second], axis=0).astype(kind)


def spread(ref, row, frames):
    return jnp.broadcast_to(ref[pl.ds(row, 1), :], (frames, ref.shape[1]))


def tile_at(start, frames):
    return pl.ds(pl.multiple_of(start, frames), frames)


def for_slots(slots, body):
    def some(step, carry):
        for place in range(CHUNK):
            body(step * CHUNK + place, place)
        return carry

    lax.fori_loop(0, lax.div(slots[7, 0] + (CHUNK - 1), CHUNK), some, 0)


def for_rows(rows, body):
    step = 128

    def some(number, carry):
        body(pl.ds(pl.multiple_of(number * step, step), step))
        return carry

    lax.fori_loop(0, rows // step, some, 0)


def forward_kernel(sizes, stride, start_row, n_sums, list_ref, values_ref, *refs):
    capacity, depth, frames = sizes
    tables, refs = refs[:4], refs[4:]
    start_ref = None
    if start_row is not None:
        start_ref, refs = refs[0], refs[1:]
    sum_refs, (out_ref, slots, arrived, wide, second) = refs[:n_sums], refs[n_sums:]
    copy = pltpu.make_async_copy(list_ref, slots, arrived.at[0])
    copy.start()
    members = values_ref.shape[0] // stride
    rows = wide.shape[0] // members
    rays = second.shape[0]
    line_step = tables[0].shape[0] // depth

    def widen(member, carry):
        at = pl.ds(pl.multiple_of(member * rows, rows), rows)
        wide[at, :] = values_ref[pl.ds(pl.multiple_of(member * stride, 16), rows), :].astype(F32)
        return carry

    lax.fori_loop(0, members, widen, 0)
    second[...] = jnp.zeros_like(second)
    if start_ref is None:
        out_ref[...] = jnp.zeros_like(out_ref)
    else:
        out_ref[0:rays, :] = start_ref[start_row:start_row + rays, :]
    if n_sums:
        half = sum_refs[0].shape[0] // 2
        out_ref[rays:, :] = sum([ref[half:, :] for ref in sum_refs[1:]], sum_refs[0][half:, :])
    copy.wait()

    def one(slot, place):
        line = slots[0, slot]
        taps = []
        for start in range(0, depth, 2):
            levels = range(start, start + 2)
            values = [wide[tile_at(slots[2 + level, slot], frames), :] for level in levels]
            middles = [spread(tables[0], line + level * line_step, frames) for level in levels]
            lower = [
                pick(pack_pair(value, value), pack_pair(middle - 1, middle)).astype(F32)
                for value, middle in zip(values, middles)]
            upper = pick(
                pack_pair(*values), pack_pair(*[middle + 1 for middle in middles])).astype(F32)
            for which, pair in enumerate(lower):
                taps.append((pair[0:frames], pair[frames:2 * frames],
                             upper[which * frames:(which + 1) * frames]))
        total = None
        for level, three in enumerate(taps):
            for ref, tap in zip(tables[1:], three):
                term = spread(ref, line + level * line_step, frames) * tap
                total = term if total is None else total + term
        projection = (out_ref, second)[place % 2]
        projection[tile_at(slots[1, slot], frames), :] += total.astype(BF16).astype(F32)

    for_slots(slots, one)
    out_ref[0:rays, :] += second[...]


def residual_kernel(frames, n_own, projection_ref, sinogram_ref, *refs):
    own, refs, out_ref = refs[:n_own], refs[n_own:-1], refs[-1]
    rays = out_ref.shape[0]
    ray_tiles = rays // frames
    total = sum([ref[0:ray_tiles, :] for ref in own[1:]], own[0][0:ray_tiles, :])
    projection = projection_ref[...]
    if refs:
        projection = projection + refs[0][0:rays, :]
        total = total + refs[-1][rays:, :]
    weight = repeat_rows(1.0 / jnp.maximum(total, 1.0), frames)
    out_ref[...] = ((sinogram_ref[...].astype(F32) - projection) * weight).astype(BF16)


def backward_kernel(sizes, n_parts, has_start, list_ref, *refs):
    capacity, depth, frames = sizes
    part_refs, tables, refs = refs[:n_parts], refs[n_parts:n_parts + 3], refs[n_parts + 3:]
    start_ref = None
    if has_start:
        start_ref, refs = refs[0], refs[1:]
    out_ref, slots, arrived, residual, banks = refs[0], refs[1], refs[2], refs[3], refs[4:]
    copy = pltpu.make_async_copy(list_ref, slots, arrived.at[0])
    copy.start()
    rays = part_refs[0].shape[0]
    line_step = tables[0].shape[0] // depth
    for place, ref in enumerate(part_refs):
        residual[place * rays:(place + 1) * rays, :] = ref[...].astype(F32)

    def clear(at):
        for place, bank in enumerate(banks):
            if place == 0 and has_start:
                bank[at, :] = start_ref[at, :]
            else:
                bank[at, :] = jnp.zeros((at.size, bank.shape[1]), F32)

    for_rows(out_ref.shape[0], clear)
    copy.wait()

    def one(slot, place):
        line = slots[0, slot]
        values = residual[tile_at(slots[1, slot], frames), :]
        twice = pack_pair(values, values)
        for level in range(depth):
            row = line + level * line_step
            first = spread(tables[0], row, frames)
            taps = pick(twice, pack_pair(first, first + 1)).astype(F32)
            term = (spread(tables[1], row, frames) * taps[0:frames]
                    + spread(tables[2], row, frames) * taps[frames:2 * frames])
            banks[level % len(banks)][tile_at(slots[2 + level, slot], frames), :] += term

    for_slots(slots, one)

    def finish(at):
        total = sum([bank[at, :] for bank in banks[1:]], banks[0][at, :])
        out_ref[at, :] = total.astype(out_ref.dtype)

    for_rows(out_ref.shape[0], finish)


def join_kernel(*refs):
    out_ref, at = refs[-1], 0
    for ref in refs[:-1]:
        out_ref[at:at + ref.shape[0], :] = ref[...]
        at += ref.shape[0]


def combine_kernel(sum_ref, y_ref, own_ref, *piece_refs):
    rows = own_ref.shape[0]
    for place, ref in enumerate((own_ref,) + piece_refs):
        at = pl.ds(place * rows, rows)
        ref[...] = (sum_ref[at, :] + y_ref[at, :].astype(F32)).astype(ref.dtype)


def update_kernel(n_pieces, volume_ref, column_ref, *refs):
    back = refs[0][...]
    for ref in refs[1:n_pieces]:
        back = back + ref[...].astype(F32)
    volume = volume_ref[...] + column_ref[...] * back
    for ref in refs[n_pieces:]:
        ref[...] = volume.astype(ref.dtype)


def call(kernel, name, mib, in_specs, out_shape, *operands, scratch=()):
    one = not isinstance(out_shape, list)
    return pl.pallas_call(
        kernel,
        out_shape=out_shape,
        in_specs=in_specs,
        out_specs=VMEM if one else [VMEM] * len(out_shape),
        scratch_shapes=list(scratch),
        compiler_params=pltpu.CompilerParams(vmem_limit_bytes=mib * 1024 * 1024),
        name=name,
    )(*operands)


def exchange(values, n_slab, distance):
    return lax.ppermute(
        values, "slab", [(device, device ^ distance) for device in range(n_slab)])


def shards(sinogram, start_volume, slot_voxel, slot_ray, live_count, block_slope, block_offset):
    n_slab = lax.axis_size("slab")
    n_slots, depth = slot_voxel.shape
    capacity = n_slots // n_slab
    ray_tiles, frames, extent = sinogram.shape
    voxel_tiles = start_volume.shape[0]
    rows = voxel_tiles * frames
    sizes = (capacity, depth, frames)
    paired = n_slab == 16
    span = 2 if paired else 1
    n_bank = 2 if paired else 1
    shape = jax.ShapeDtypeStruct
    n_rays = ray_tiles * frames
    volume = start_volume.reshape(rows, extent)
    sino = sinogram.reshape(n_rays, extent)
    slots_by_depth = (block_offset.T, block_slope.T, slot_voxel.T)
    live = live_count.reshape(1, n_slab)
    height = -(-(7 * depth + 2) // 16) * 16 * (n_slots // extent)
    operands = (volume, *slots_by_depth, slot_ray.reshape(1, n_slots), live)
    payload = call(
        functools.partial(pack_kernel, capacity), "pack", 60, [ANY] * 6,
        shape((rows + height, extent), BF16), *operands,
        scratch=[pltpu.VMEM(operand.shape, operand.dtype) for operand in operands]
        + [pltpu.SemaphoreType.DMA((6,))])

    def setup(values, members, wanted, after=None):
        lanes = -(-members * span * capacity // 128) * 128
        lines = depth * (lanes + 8)
        table = [shape((lines, extent), I32)] + [shape((lines, extent), F32)] * 3
        table += [shape((lines, extent), I32)] + [shape((lines, extent), F32)] * 2
        out = [shape((8, lanes), I32)] * len(wanted) + [shape((span * ray_tiles, extent), F32)] + table
        waits = [] if after is None else [after]
        found = call(
            functools.partial(setup_kernel, members, values.shape[0] // members, span, sizes,
                              voxel_tiles, wanted),
            "setup", 24, [VMEM] + [ANY] * len(waits), out, values, *waits)
        n = len(wanted)
        return found[:n], found[n], found[n + 1:n + 5], found[n + 5:]

    def list_scratch(slots):
        return [pltpu.SMEM(slots.shape, I32), pltpu.SemaphoreType.DMA((1,))]

    def forward(slots, values, members, table, n_out, start=None, start_row=None, sums=()):
        operands = [slots, values, *table] + ([] if start is None else [start]) + list(sums)
        extra = ray_tiles if sums else 0
        return call(
            functools.partial(forward_kernel, sizes, values.shape[0] // members, start_row, len(sums)),
            "forward", 16 if paired else 32, [ANY] + [VMEM] * (len(operands) - 1),
            shape((n_out + extra, extent), F32), *operands,
            scratch=list_scratch(slots)
            + [pltpu.VMEM((members * rows, extent), F32), pltpu.VMEM((n_out, extent), F32)])

    def residual_of(projection, row_sums, *sibling):
        operands = [projection, sino, *row_sums, *sibling]
        return call(
            functools.partial(residual_kernel, frames, len(row_sums)), "residual", 16,
            [VMEM] * len(operands), shape((n_rays, extent), BF16), *operands)

    def backward(slots, parts, members, table, kind, start=None):
        operands = [slots, *parts, *table] + ([] if start is None else [start])
        return call(
            functools.partial(backward_kernel, sizes, len(parts), start is not None),
            "backward", 16 if paired else 32, [ANY] + [VMEM] * (len(operands) - 1),
            shape((members * rows, extent), kind), *operands,
            scratch=list_scratch(slots) + [pltpu.VMEM((len(parts) * n_rays, extent), F32)]
            + [pltpu.VMEM((members * rows, extent), F32)] * n_bank)

    def join(*parts):
        total = sum(part.shape[0] for part in parts)
        return call(join_kernel, "join", 16, [VMEM] * len(parts), shape((total, extent), BF16), *parts)

    def update(volume, pieces, last):
        out = [shape((rows, extent), F32)] + ([] if last else [shape((rows, extent), BF16)])
        return call(
            functools.partial(update_kernel, len(pieces)), "update", 16,
            [VMEM] * (2 + len(pieces)), out, volume, column_weight, *pieces)

    column_weight = call(
        functools.partial(column_kernel, sizes), "column_weight", 16, [VMEM] * 4,
        shape((rows, extent), F32), *slots_by_depth, live)

    for sweep in range(ITERS):
        last = sweep + 1 == ITERS
        if paired:
            along_z = join(
                payload, *[exchange(payload, n_slab, distance) for distance in (8, 12, 4)])
            along_y = exchange(along_z, n_slab, 2)
            if sweep == 0:
                (z_list,), z_rows, z_forward, z_backward = setup(along_z, 4, (None,))
            both = forward(z_list, along_z, 4, z_forward, 2 * n_rays)
            if sweep == 0:
                (own_list, other_list), y_rows, y_forward, y_backward = setup(
                    along_y, 4, (0, 1), after=both)
            other = exchange(
                forward(other_list, along_y, 4, y_forward, n_rays, both, n_rays,
                        (z_rows, y_rows) if sweep == 0 else ()), n_slab, 1)
            if sweep == 0:
                first_other = other
            own = forward(own_list, along_y, 4, y_forward, n_rays, both, 0)
            residual = residual_of(own, (z_rows, y_rows), other, first_other)
            other_residual = exchange(residual, n_slab, 1)
            y_sum = backward(own_list, [residual], 4, y_backward, F32)
            y_sum = backward(other_list, [other_residual], 4, y_backward, BF16, y_sum)
            y_part = exchange(y_sum, n_slab, 2)
            z_sum = backward(z_list, [residual, other_residual], 4, z_backward, F32)
            own_piece, *pieces = call(
                combine_kernel, "combine", 16, [VMEM] * 2,
                [shape((rows, extent), F32)] + [shape((rows, extent), BF16)] * 3, z_sum, y_part)
            pieces = [own_piece] + [
                exchange(piece, n_slab, distance) for piece, distance in zip(pieces, (8, 12, 4))]
        else:
            everyone = lax.all_gather(payload, "slab", axis=0, tiled=True)
            if sweep == 0:
                (slots,), row_sums, to_rays, to_voxels = setup(everyone, n_slab, (None,))
            projection = forward(slots, everyone, n_slab, to_rays, n_rays)
            residual = residual_of(projection, (row_sums,))
            sums = backward(slots, [residual], n_slab, to_voxels, BF16)
            parts = lax.all_to_all(
                sums.reshape(n_slab, rows, extent), "slab", split_axis=0, concat_axis=0, tiled=True)
            pieces = [jnp.sum(parts.astype(F32), axis=0)]
        volume, *rounded = update(volume, pieces, last)
        if not last:
            payload = rounded[0]
    return volume.reshape(start_volume.shape)


def solution(mesh):
    in_specs = (
        P(("scan", "slab"), None, None),
        P(("scan", "slab"), None, None),
        P(("scan", "slab"), None),
        P(("scan", "slab")),
        P(("scan", "slab")),
        P(("scan", "slab"), None),
        P(("scan", "slab"), None),
    )
    out_specs = P(("scan", "slab"), None, None)
    return jax.shard_map(shards, mesh=mesh, in_specs=in_specs, out_specs=out_specs, check_vma=False)
```

time: 79.3 us -> 73.2 us (0.923)
  waiting for transfers between devices: 25.8 us -> 21.9 us
  Pallas kernels: 28.2 us -> 26.9 us
  starting transfers between devices: 23.7 us -> 22.7 us
    ppermute x20, waiting for transfers between devices: 25.8 us -> 21.9 us  [exchange(): lax.ppermute(values, 'slab', [(device, device ^ distance) for device in r...]
    pallas_call x25 -> x24, Pallas kernels: 28.2 us -> 26.9 us  [call(): pl.pallas_call(kernel, out_shape=out_shape, in_specs=in_specs, out_specs=...]
    ppermute x20, starting transfers between devices: 23.7 us -> 22.7 us  [exchange(): lax.ppermute(values, 'slab', [(device, device ^ distance) for device in r...]
  transfers between devices with their start and end apart: 20 -> 20, of which waited for: 13 -> 13; matrix products, arithmetic and copies ran while one was open for 0% -> 0% of each run, Pallas kernels for 21% -> 25%
where the time goes in v9:
time: 73.2 us; the launch traced here: 72.6 us
  Pallas kernels  26.9 us (37%)
  starting transfers between devices  22.7 us (31%)
  waiting for transfers between devices  21.9 us (30%)
  local copies, waits for them, and re-layouts  0.83 us (1%)
    pallas_call x24, Pallas kernels, call(): pl.pallas_call(kernel, out_shape=out_shape, in_specs=in_specs, out_specs=...  26.9 us
    ppermute x20, starting transfers between devices, exchange(): lax.ppermute(values, 'slab', [(device, device ^ distance) for device in r...  22.7 us
    ppermute x20, waiting for transfers between devices, exchange(): lax.ppermute(values, 'slab', [(device, device ^ distance) for device in r...  21.9 us
  transfers between devices with their start and end apart: 20, of which 13 were waited for; matrix products, arithmetic and copies ran while one was open for 0% of the time, Pallas kernels for 25%

profile of v9, /device:TPU:0, one launch (start us, length us, event | category | flops | bytes accessed | tf_op | source)
XLA Modules:
  0.0 72.6 jit_solution(10516214152425905976)
XLA Ops:
  0.0 1.7 %pack.1.refs_0_ = bf16[192,128]{1,0:T(8,128)(2,1)} custom-call(f32[128,128]{1,0:T(8,128)} %bitcast.10, f32[4,256]{1,0:T(4,128)} %bitcast.12, f32[4,256]{1,0:T(4,128)} %bitcast.14, s32[4,256]{1,0:T(4,128)} %bitcast.16, s32[1,256]{1,0:T(1,128)} %bitcast.20, s32[1,16]{1,0:T(1,128)} %bitcast.18), custom_call_target="tpu_custom_call" | custom-call | tf_op jit(solution)/shard_map/pack/pallas_call | solution.py:386
  1.7 4.1 %collective-permute-start = (bf16[192,128]{1,0:T(8,128)(2,1)}, bf16[192,128]{1,0:T(8,128)(2,1)S(1)}, u32[]{:S(2)}, u32[]{:S(2)}) collective-permute-start(bf16[192,128]{1,0:T(8,128)(2,1)} %pack.1.refs_0_), channel_id=1, source_target_pairs={{0,8},{1,9},{2,10},{3,11},{4,12},{5,13},{6,14},{7,15},{8,0},{9,1},... | collective-permute-start | bytes 147464 | tf_op jit(solution)/shard_map/ppermute | solution.py:398
  5.8 1.3 %collective-permute-start.1 = (bf16[192,128]{1,0:T(8,128)(2,1)}, bf16[192,128]{1,0:T(8,128)(2,1)S(1)}, u32[]{:S(2)}, u32[]{:S(2)}) collective-permute-start(bf16[192,128]{1,0:T(8,128)(2,1)} %pack.1.refs_0_), channel_id=1, source_target_pairs={{0,12},{1,13},{2,14},{3,15},{4,8},{5,9},{6,10},{7,11},{8,4},{9,5},... | collective-permute-start | bytes 147464 | tf_op jit(solution)/shard_map/ppermute | solution.py:398
  7.3 1.2 %collective-permute-done.refs_1_ = bf16[192,128]{1,0:T(8,128)(2,1)S(1)} collective-permute-done((bf16[192,128]{1,0:T(8,128)(2,1)}, bf16[192,128]{1,0:T(8,128)(2,1)S(1)}, u32[]{:S(2)}, u32[]{:S(2)}) %collective-permute-start) | collective-permute-done | bytes 49184 | tf_op jit(solution)/shard_map/ppermute | solution.py:398
  8.6 3.4 %collective-permute-done.1.refs_2_ = bf16[192,128]{1,0:T(8,128)(2,1)S(1)} collective-permute-done((bf16[192,128]{1,0:T(8,128)(2,1)}, bf16[192,128]{1,0:T(8,128)(2,1)S(1)}, u32[]{:S(2)}, u32[]{:S(2)}) %collective-permute-start.1) | collective-permute-done | bytes 49184 | tf_op jit(solution)/shard_map/ppermute | solution.py:398
  12.8 1.6 %collective-permute-start.3 = (bf16[768,128]{1,0:T(8,128)(2,1)S(1)}, bf16[768,128]{1,0:T(8,128)(2,1)S(1)}, u32[]{:S(2)}, u32[]{:S(2)}) collective-permute-start(bf16[768,128]{1,0:T(8,128)(2,1)S(1)} %join.2.payload_ref.values_ref), channel_id=1, source_target_pairs={{0,2},{1,3},{2,0},{3,1},{4,6},{5,7},{6,4},{7,5},{8,10},{9,11},{10,... | collective-permute-start | bytes 589832 | tf_op jit(solution)/shard_map/ppermute | solution.py:398
  15.4 2.3 %forward.6.refs_0_.refs_4_ = f32[512,128]{1,0:T(8,128)S(1)} custom-call(s32[8,128]{1,0:T(8,128)S(1)} %get-tuple-element.34.list_ref, bf16[768,128]{1,0:T(8,128)(2,1)S(1)} %join.2.payload_ref.values_ref, s32[544,128]{1,0:T(8,128)S(1)} %get-tuple-element.35.refs_0_, f32[544,128]{1,0:T(8,128)S(1)} %get-tuple-element.36.refs_1_, ...), custom_call_target="tpu_custom_call" | custom-call | tf_op jit(solution)/shard_map/forward/pallas_call | solution.py:386
  18.5 1.3 %setup.3 = (s32[8,128]{1,0:T(8,128)S(1)}, s32[8,128]{1,0:T(8,128)S(1)}, f32[64,128]{1,0:T(8,128)S(1)}, s32[544,128]{1,0:T(8,128)S(1)}, f32[544,128]{1,0:T(8,128)...) custom-call(bf16[768,128]{1,0:T(8,128)(2,1)S(1)} %collective-permute, ...), custom_call_target="tpu_custom_call" | custom-call | tf_op jit(solution)/shard_map/setup/pallas_call | solution.py:386
  19.8 1.3 %forward.8 = f32[288,128]{1,0:T(8,128)S(1)} custom-call(s32[8,128]{1,0:T(8,128)S(1)} %get-tuple-element.46.list_ref, bf16[768,128]{1,0:T(8,128)(2,1)S(1)} %collective-permute-done.3.payload_ref.values_ref, s32[544,128]{1,0:T(8,128)S(1)} %get-tuple-element.40.refs_0_, f32[544,128]{1,0:T(8,128)S(1)} %get-tuple-element.41.refs_1_, ...), custom_call_target="tpu_custom_call" | custom-call | tf_op jit(solution)/shard_map/forward/pallas_call | solution.py:386
  21.2 2.1 %forward.7.projection_ref = f32[256,128]{1,0:T(8,128)S(1)} custom-call(s32[8,128]{1,0:T(8,128)S(1)} %get-tuple-element.39.list_ref, bf16[768,128]{1,0:T(8,128)(2,1)S(1)} %collective-permute-done.3.payload_ref.values_ref, s32[544,128]{1,0:T(8,128)S(1)} %get-tuple-element.40.refs_0_, f32[544,128]{1,0:T(8,128)S(1)} %get-tuple-element.41.refs_1_, ...), custom_call_target="tpu_custom_call" | custom-call | tf_op jit(solution)/shard_map/forward/pallas_call | solution.py:386
  23.7 1.8 %backward.7.refs_4_ = f32[512,128]{1,0:T(8,128)S(1)} custom-call(s32[8,128]{1,0:T(8,128)S(1)} %get-tuple-element.39.list_ref, bf16[256,128]{1,0:T(8,128)(2,1)S(1)} %residual.2.refs_0_, s32[544,128]{1,0:T(8,128)S(1)} %get-tuple-element.50.refs_1_, f32[544,128]{1,0:T(8,128)S(1)} %get-tuple-element.51.refs_2_, f32[544,128]{1,0:T(8,128)S(1)} %get-tuple-element.52.refs_3_), custom_call_target="tpu_custom_call" | custom-call | tf_op jit(solution)/shard_map/backward/pallas_call | solution.py:386
  26.7 1.5 %collective-permute-start.6 = (bf16[512,128]{1,0:T(8,128)(2,1)S(1)}, bf16[512,128]{1,0:T(8,128)(2,1)S(1)}, u32[]{:S(2)}, u32[]{:S(2)}) collective-permute-start(bf16[512,128]{1,0:T(8,128)(2,1)S(1)} %backward.8), channel_id=1, source_target_pairs={{0,2},{1,3},{2,0},{3,1},{4,6},{5,7},{6,4},{7,5},{8,10},{9,11},{10,... | collective-permute-start | bytes 393224 | tf_op jit(solution)/shard_map/ppermute | solution.py:398
  28.2 2.0 %backward.6.sum_ref = f32[512,128]{1,0:T(8,128)S(1)} custom-call(s32[8,128]{1,0:T(8,128)S(1)} %get-tuple-element.34.list_ref, bf16[256,128]{1,0:T(8,128)(2,1)S(1)} %residual.2.refs_0_, bf16[256,128]{1,0:T(8,128)(2,1)S(1)} %collective-permute-done.5.refs_1_.refs_0_, s32[544,128]{1,0:T(8,128)S(1)} %get-tuple-element.47.refs_2_, ...), custom_call_target="tpu_custom_call" | custom-call | tf_op jit(solution)/shard_map/backward/pallas_call | solution.py:386
  30.2 2.2 %collective-permute-done.6.y_ref = bf16[512,128]{1,0:T(8,128)(2,1)S(1)} collective-permute-done((bf16[512,128]{1,0:T(8,128)(2,1)S(1)}, bf16[512,128]{1,0:T(8,128)(2,1)S(1)}, u32[]{:S(2)}, u32[]{:S(2)}) %collective-permute-start.6) | collective-permute-done | bytes 131104 | tf_op jit(solution)/shard_map/ppermute | solution.py:398
  32.5 2.1 %collective-permute-start.7 = (bf16[128,128]{1,0:T(8,128)(2,1)S(1)}, bf16[128,128]{1,0:T(8,128)(2,1)S(1)}, u32[]{:S(2)}, u32[]{:S(2)}) collective-permute-start(bf16[128,128]{1,0:T(8,128)(2,1)S(1)} %get-tuple-element.54), channel_id=1, source_target_pairs={{0,8},{1,9},{2,10},{3,11},{4,12},{5,13},{6,14},{7,15},{8,0},{9,1},... | collective-permute-start | bytes 98312 | tf_op jit(solution)/shard_map/ppermute | solution.py:398
  36.7 1.4 %collective-permute-done.7.refs_1_ = bf16[128,128]{1,0:T(8,128)(2,1)S(1)} collective-permute-done((bf16[128,128]{1,0:T(8,128)(2,1)S(1)}, bf16[128,128]{1,0:T(8,128)(2,1)S(1)}, u32[]{:S(2)}, u32[]{:S(2)}) %collective-permute-start.7) | collective-permute-done | bytes 32800 | tf_op jit(solution)/shard_map/ppermute | solution.py:398
  38.1 2.2 %collective-permute-done.8.refs_2_ = bf16[128,128]{1,0:T(8,128)(2,1)S(1)} collective-permute-done((bf16[128,128]{1,0:T(8,128)(2,1)S(1)}, bf16[128,128]{1,0:T(8,128)(2,1)S(1)}, u32[]{:S(2)}, u32[]{:S(2)}) %collective-permute-start.8) | collective-permute-done | bytes 32800 | tf_op jit(solution)/shard_map/ppermute | solution.py:398
  42.5 1.4 %collective-permute-start.12 = (bf16[128,128]{1,0:T(8,128)(2,1)S(1)}, bf16[128,128]{1,0:T(8,128)(2,1)S(1)}, u32[]{:S(2)}, u32[]{:S(2)}) collective-permute-start(bf16[128,128]{1,0:T(8,128)(2,1)S(1)} %get-tuple-element.58.refs_0_), channel_id=1, source_target_pairs={{0,4},{1,5},{2,6},{3,7},{4,0},{5,1},{6,2},{7,3},{8,12},{9,13},{10,... | collective-permute-start | bytes 98312 | tf_op jit(solution)/shard_map/ppermute | solution.py:398
  43.9 1.3 %collective-permute-done.10.refs_1_ = bf16[128,128]{1,0:T(8,128)(2,1)S(1)} collective-permute-done((bf16[128,128]{1,0:T(8,128)(2,1)S(1)}, bf16[128,128]{1,0:T(8,128)(2,1)S(1)}, u32[]{:S(2)}, u32[]{:S(2)}) %collective-permute-start.10) | collective-permute-done | bytes 32800 | tf_op jit(solution)/shard_map/ppermute | solution.py:398
  45.2 1.8 %collective-permute-done.11.refs_2_ = bf16[128,128]{1,0:T(8,128)(2,1)S(1)} collective-permute-done((bf16[128,128]{1,0:T(8,128)(2,1)S(1)}, bf16[128,128]{1,0:T(8,128)(2,1)S(1)}, u32[]{:S(2)}, u32[]{:S(2)}) %collective-permute-start.11) | collective-permute-done | bytes 32800 | tf_op jit(solution)/shard_map/ppermute | solution.py:398
  47.0 1.3 %collective-permute-start.13 = (bf16[512,128]{1,0:T(8,128)(2,1)S(1)}, bf16[512,128]{1,0:T(8,128)(2,1)S(1)}, u32[]{:S(2)}, u32[]{:S(2)}) collective-permute-start(bf16[512,128]{1,0:T(8,128)(2,1)S(1)} %join.3.values_ref), channel_id=1, source_target_pairs={{0,2},{1,3},{2,0},{3,1},{4,6},{5,7},{6,4},{7,5},{8,10},{9,11},{10,... | collective-permute-start | bytes 393224 | tf_op jit(solution)/shard_map/ppermute | solution.py:398
  48.3 2.3 %forward.9.refs_4_ = f32[512,128]{1,0:T(8,128)S(1)} custom-call(s32[8,128]{1,0:T(8,128)S(1)} %get-tuple-element.34.list_ref, bf16[512,128]{1,0:T(8,128)(2,1)S(1)} %join.3.values_ref, s32[544,128]{1,0:T(8,128)S(1)} %get-tuple-element.35.refs_0_, f32[544,128]{1,0:T(8,128)S(1)} %get-tuple-element.36.refs_1_, f32[544,128]{1,0:T(8,128)S(1)} %get-tuple-element.37.refs_2_, ...), custom_call_target="tpu_custom_call" | custom-call | tf_op jit(solution)/shard_map/forward/pallas_call | solution.py:386
  50.7 1.4 %collective-permute-done.13.values_ref = bf16[512,128]{1,0:T(8,128)(2,1)S(1)} collective-permute-done((bf16[512,128]{1,0:T(8,128)(2,1)S(1)}, bf16[512,128]{1,0:T(8,128)(2,1)S(1)}, u32[]{:S(2)}, u32[]{:S(2)}) %collective-permute-start.13) | collective-permute-done | bytes 131104 | tf_op jit(solution)/shard_map/ppermute | solution.py:398
  52.1 1.3 %forward.11 = f32[256,128]{1,0:T(8,128)S(1)} custom-call(s32[8,128]{1,0:T(8,128)S(1)} %get-tuple-element.46.list_ref, bf16[512,128]{1,0:T(8,128)(2,1)S(1)} %collective-permute-done.13.values_ref, s32[544,128]{1,0:T(8,128)S(1)} %get-tuple-element.40.refs_0_, f32[544,128]{1,0:T(8,128)S(1)} %get-tuple-element.41.refs_1_, ...), custom_call_target="tpu_custom_call" | custom-call | tf_op jit(solution)/shard_map/forward/pallas_call | solution.py:386
  53.4 2.1 %forward.10.projection_ref = f32[256,128]{1,0:T(8,128)S(1)} custom-call(s32[8,128]{1,0:T(8,128)S(1)} %get-tuple-element.39.list_ref, bf16[512,128]{1,0:T(8,128)(2,1)S(1)} %collective-permute-done.13.values_ref, s32[544,128]{1,0:T(8,128)S(1)} %get-tuple-element.40.refs_0_, f32[544,128]{1,0:T(8,128)S(1)} %get-tuple-element.41.refs_1_, ...), custom_call_target="tpu_custom_call" | custom-call | tf_op jit(solution)/shard_map/forward/pallas_call | solution.py:386
  56.0 1.8 %backward.10.refs_4_ = f32[512,128]{1,0:T(8,128)S(1)} custom-call(s32[8,128]{1,0:T(8,128)S(1)} %get-tuple-element.39.list_ref, bf16[256,128]{1,0:T(8,128)(2,1)S(1)} %residual.3.refs_0_, s32[544,128]{1,0:T(8,128)S(1)} %get-tuple-element.50.refs_1_, f32[544,128]{1,0:T(8,128)S(1)} %get-tuple-element.51.refs_2_, f32[544,128]{1,0:T(8,128)S(1)} %get-tuple-element.52.refs_3_), custom_call_target="tpu_custom_call" | custom-call | tf_op jit(solution)/shard_map/backward/pallas_call | solution.py:386
  60.2 2.0 %backward.9.sum_ref = f32[512,128]{1,0:T(8,128)S(1)} custom-call(s32[8,128]{1,0:T(8,128)S(1)} %get-tuple-element.34.list_ref, bf16[256,128]{1,0:T(8,128)(2,1)S(1)} %residual.3.refs_0_, bf16[256,128]{1,0:T(8,128)(2,1)S(1)} %collective-permute-done.15.refs_1_.refs_0_, s32[544,128]{1,0:T(8,128)S(1)} %get-tuple-element.47.refs_2_, ...), custom_call_target="tpu_custom_call" | custom-call | tf_op jit(solution)/shard_map/backward/pallas_call | solution.py:386
  62.2 2.5 %collective-permute-done.16.y_ref = bf16[512,128]{1,0:T(8,128)(2,1)S(1)} collective-permute-done((bf16[512,128]{1,0:T(8,128)(2,1)S(1)}, bf16[512,128]{1,0:T(8,128)(2,1)S(1)}, u32[]{:S(2)}, u32[]{:S(2)}) %collective-permute-start.16) | collective-permute-done | bytes 131104 | tf_op jit(solution)/shard_map/ppermute | solution.py:398
  64.7 1.3 %collective-permute-start.17 = (bf16[128,128]{1,0:T(8,128)(2,1)S(1)}, bf16[128,128]{1,0:T(8,128)(2,1)S(1)}, u32[]{:S(2)}, u32[]{:S(2)}) collective-permute-start(bf16[128,128]{1,0:T(8,128)(2,1)S(1)} %get-tuple-element.60), channel_id=1, source_target_pairs={{0,8},{1,9},{2,10},{3,11},{4,12},{5,13},{6,14},{7,15},{8,0},{9,1},... | collective-permute-start | bytes 98312 | tf_op jit(solution)/shard_map/ppermute | solution.py:398
  66.0 1.6 %collective-permute-start.18 = (bf16[128,128]{1,0:T(8,128)(2,1)S(1)}, bf16[128,128]{1,0:T(8,128)(2,1)S(1)}, u32[]{:S(2)}, u32[]{:S(2)}) collective-permute-start(bf16[128,128]{1,0:T(8,128)(2,1)S(1)} %get-tuple-element.61), channel_id=1, source_target_pairs={{0,12},{1,13},{2,14},{3,15},{4,8},{5,9},{6,10},{7,11},{8,4},{9,5},... | collective-permute-start | bytes 98312 | tf_op jit(solution)/shard_map/ppermute | solution.py:398
  68.3 1.6 %collective-permute-done.17.refs_1_ = bf16[128,128]{1,0:T(8,128)(2,1)S(1)} collective-permute-done((bf16[128,128]{1,0:T(8,128)(2,1)S(1)}, bf16[128,128]{1,0:T(8,128)(2,1)S(1)}, u32[]{:S(2)}, u32[]{:S(2)}) %collective-permute-start.17) | collective-permute-done | bytes 32800 | tf_op jit(solution)/shard_map/ppermute | solution.py:398
  69.9 1.9 %collective-permute-done.18.refs_2_ = bf16[128,128]{1,0:T(8,128)(2,1)S(1)} collective-permute-done((bf16[128,128]{1,0:T(8,128)(2,1)S(1)}, bf16[128,128]{1,0:T(8,128)(2,1)S(1)}, u32[]{:S(2)}, u32[]{:S(2)}) %collective-permute-start.18) | collective-permute-done | bytes 32800 | tf_op jit(solution)/shard_map/ppermute | solution.py:398
  (46 shorter events, 13.0 us)
Async XLA Ops:
  1.7 6.9 %collective-permute-start = (bf16[192,128]{1,0:T(8,128)(2,1)}, bf16[192,128]{1,0:T(8,128)(2,1)S(1)}, u32[]{:S(2)}, u32[]{:S(2)}) collective-permute-start(bf16[192,128]{1,0:T(8,128)(2,1)} %pack.1.refs_0_), channel_id=1, source_target_pairs={{0,8},{1,9},{2,10},{3,11},{4,12},{5,13},{6,14},{7,15},{8,0},{9,1},... | collective-permute-start | bytes 147464 | tf_op jit(solution)/shard_map/ppermute | solution.py:398
  5.8 6.2 %collective-permute-start.1 = (bf16[192,128]{1,0:T(8,128)(2,1)}, bf16[192,128]{1,0:T(8,128)(2,1)S(1)}, u32[]{:S(2)}, u32[]{:S(2)}) collective-permute-start(bf16[192,128]{1,0:T(8,128)(2,1)} %pack.1.refs_0_), channel_id=1, source_target_pairs={{0,12},{1,13},{2,14},{3,15},{4,8},{5,9},{6,10},{7,11},{8,4},{9,5},... | collective-permute-start | bytes 147464 | tf_op jit(solution)/shard_map/ppermute | solution.py:398
  7.1 4.8 %collective-permute-start.2 = (bf16[192,128]{1,0:T(8,128)(2,1)}, bf16[192,128]{1,0:T(8,128)(2,1)S(1)}, u32[]{:S(2)}, u32[]{:S(2)}) collective-permute-start(bf16[192,128]{1,0:T(8,128)(2,1)} %pack.1.refs_0_), channel_id=1, source_target_pairs={{0,4},{1,5},{2,6},{3,7},{4,0},{5,1},{6,2},{7,3},{8,12},{9,13},{10,... | collective-permute-start | bytes 147464 | tf_op jit(solution)/shard_map/ppermute | solution.py:398
  11.9 0.8 %copy-start.2 = (bf16[192,128]{1,0:T(8,128)(2,1)S(1)}, bf16[192,128]{1,0:T(8,128)(2,1)}, u32[]{:S(2)}) copy-start(bf16[192,128]{1,0:T(8,128)(2,1)} %pack.1.refs_0_) | copy-start | bytes 147460
  12.8 5.7 %collective-permute-start.3 = (bf16[768,128]{1,0:T(8,128)(2,1)S(1)}, bf16[768,128]{1,0:T(8,128)(2,1)S(1)}, u32[]{:S(2)}, u32[]{:S(2)}) collective-permute-start(bf16[768,128]{1,0:T(8,128)(2,1)S(1)} %join.2.payload_ref.values_ref), channel_id=1, source_target_pairs={{0,2},{1,3},{2,0},{3,1},{4,6},{5,7},{6,4},{7,5},{8,10},{9,11},{10,... | collective-permute-start | bytes 589832 | tf_op jit(solution)/shard_map/ppermute | solution.py:398
  21.1 2.2 %collective-permute-start.4 = (f32[288,128]{1,0:T(8,128)S(1)}, f32[288,128]{1,0:T(8,128)S(1)}, u32[]{:S(2)}, u32[]{:S(2)}) collective-permute-start(f32[288,128]{1,0:T(8,128)S(1)} %forward.8), channel_id=1, source_target_pairs={{0,1},{1,0},{2,3},{3,2},{4,5},{5,4},{6,7},{7,6},{8,9},{9,8},{10,11... | collective-permute-start | bytes 442376 | tf_op jit(solution)/shard_map/ppermute | solution.py:398
  21.1 2.1 %copy-start = (bf16[32,8,128]{2,1,0:T(8,128)(2,1)S(1)}, bf16[32,8,128]{2,1,0:T(8,128)(2,1)}, u32[]{:S(2)}) copy-start(bf16[32,8,128]{2,1,0:T(8,128)(2,1)} %param.7) | copy-start | bytes 196612
  23.3 2.2 %collective-permute-start.5 = (bf16[256,128]{1,0:T(8,128)(2,1)S(1)}, bf16[256,128]{1,0:T(8,128)(2,1)S(1)}, u32[]{:S(2)}, u32[]{:S(2)}) collective-permute-start(bf16[256,128]{1,0:T(8,128)(2,1)S(1)} %residual.2.refs_0_), channel_id=1, source_target_pairs={{0,1},{1,0},{2,3},{3,2},{4,5},{5,4},{6,7},{7,6},{8,9},{9,8},{10,11... | collective-permute-start | bytes 196616 | tf_op jit(solution)/shard_map/ppermute | solution.py:398
  26.7 5.7 %collective-permute-start.6 = (bf16[512,128]{1,0:T(8,128)(2,1)S(1)}, bf16[512,128]{1,0:T(8,128)(2,1)S(1)}, u32[]{:S(2)}, u32[]{:S(2)}) collective-permute-start(bf16[512,128]{1,0:T(8,128)(2,1)S(1)} %backward.8), channel_id=1, source_target_pairs={{0,2},{1,3},{2,0},{3,1},{4,6},{5,7},{6,4},{7,5},{8,10},{9,11},{10,... | collective-permute-start | bytes 393224 | tf_op jit(solution)/shard_map/ppermute | solution.py:398
  32.4 3.6 %copy-start.3 = (f32[256,4]{0,1:T(4,128)S(1)}, f32[256,4]{0,1:T(4,128)}, u32[]{:S(2)}) copy-start(f32[256,4]{0,1:T(4,128)} %param.13) | copy-start | bytes 12292
  32.4 3.6 %copy-start.4 = (f32[256,4]{0,1:T(4,128)S(1)}, f32[256,4]{0,1:T(4,128)}, u32[]{:S(2)}) copy-start(f32[256,4]{0,1:T(4,128)} %param.12) | copy-start | bytes 12292
  32.4 3.6 %copy-start.5 = (s32[256,4]{0,1:T(4,128)S(1)}, s32[256,4]{0,1:T(4,128)}, u32[]{:S(2)}) copy-start(s32[256,4]{0,1:T(4,128)} %param.9) | copy-start | bytes 12292
  32.4 3.6 %copy-start.6 = (s32[16]{0:T(128)S(1)}, s32[16]{0:T(128)}, u32[]{:S(2)}) copy-start(s32[16]{0:T(128)} %param.11) | copy-start | bytes 196
  32.5 7.8 %copy-start.1 = (f32[16,8,128]{2,1,0:T(8,128)S(1)}, f32[16,8,128]{2,1,0:T(8,128)}, u32[]{:S(2)}) copy-start(f32[16,8,128]{2,1,0:T(8,128)} %param.8) | copy-start | bytes 196612
  32.5 5.6 %collective-permute-start.7 = (bf16[128,128]{1,0:T(8,128)(2,1)S(1)}, bf16[128,128]{1,0:T(8,128)(2,1)S(1)}, u32[]{:S(2)}, u32[]{:S(2)}) collective-permute-start(bf16[128,128]{1,0:T(8,128)(2,1)S(1)} %get-tuple-element.54), channel_id=1, source_target_pairs={{0,8},{1,9},{2,10},{3,11},{4,12},{5,13},{6,14},{7,15},{8,0},{9,1},... | collective-permute-start | bytes 98312 | tf_op jit(solution)/shard_map/ppermute | solution.py:398
  34.6 5.7 %collective-permute-start.8 = (bf16[128,128]{1,0:T(8,128)(2,1)S(1)}, bf16[128,128]{1,0:T(8,128)(2,1)S(1)}, u32[]{:S(2)}, u32[]{:S(2)}) collective-permute-start(bf16[128,128]{1,0:T(8,128)(2,1)S(1)} %get-tuple-element.55), channel_id=1, source_target_pairs={{0,12},{1,13},{2,14},{3,15},{4,8},{5,9},{6,10},{7,11},{8,4},{9,5},... | collective-permute-start | bytes 98312 | tf_op jit(solution)/shard_map/ppermute | solution.py:398
  35.5 4.8 %collective-permute-start.9 = (bf16[128,128]{1,0:T(8,128)(2,1)S(1)}, bf16[128,128]{1,0:T(8,128)(2,1)S(1)}, u32[]{:S(2)}, u32[]{:S(2)}) collective-permute-start(bf16[128,128]{1,0:T(8,128)(2,1)S(1)} %get-tuple-element.56), channel_id=1, source_target_pairs={{0,4},{1,5},{2,6},{3,7},{4,0},{5,1},{6,2},{7,3},{8,12},{9,13},{10,... | collective-permute-start | bytes 98312 | tf_op jit(solution)/shard_map/ppermute | solution.py:398
  40.3 4.9 %collective-permute-start.10 = (bf16[128,128]{1,0:T(8,128)(2,1)S(1)}, bf16[128,128]{1,0:T(8,128)(2,1)S(1)}, u32[]{:S(2)}, u32[]{:S(2)}) collective-permute-start(bf16[128,128]{1,0:T(8,128)(2,1)S(1)} %get-tuple-element.58.refs_0_), channel_id=1, source_target_pairs={{0,8},{1,9},{2,10},{3,11},{4,12},{5,13},{6,14},{7,15},{8,0},{9,1},... | collective-permute-start | bytes 98312 | tf_op jit(solution)/shard_map/ppermute | solution.py:398
  41.3 5.7 %collective-permute-start.11 = (bf16[128,128]{1,0:T(8,128)(2,1)S(1)}, bf16[128,128]{1,0:T(8,128)(2,1)S(1)}, u32[]{:S(2)}, u32[]{:S(2)}) collective-permute-start(bf16[128,128]{1,0:T(8,128)(2,1)S(1)} %get-tuple-element.58.refs_0_), channel_id=1, source_target_pairs={{0,12},{1,13},{2,14},{3,15},{4,8},{5,9},{6,10},{7,11},{8,4},{9,5},... | collective-permute-start | bytes 98312 | tf_op jit(solution)/shard_map/ppermute | solution.py:398
  42.5 4.5 %collective-permute-start.12 = (bf16[128,128]{1,0:T(8,128)(2,1)S(1)}, bf16[128,128]{1,0:T(8,128)(2,1)S(1)}, u32[]{:S(2)}, u32[]{:S(2)}) collective-permute-start(bf16[128,128]{1,0:T(8,128)(2,1)S(1)} %get-tuple-element.58.refs_0_), channel_id=1, source_target_pairs={{0,4},{1,5},{2,6},{3,7},{4,0},{5,1},{6,2},{7,3},{8,12},{9,13},{10,... | collective-permute-start | bytes 98312 | tf_op jit(solution)/shard_map/ppermute | solution.py:398
  47.0 5.0 %collective-permute-start.13 = (bf16[512,128]{1,0:T(8,128)(2,1)S(1)}, bf16[512,128]{1,0:T(8,128)(2,1)S(1)}, u32[]{:S(2)}, u32[]{:S(2)}) collective-permute-start(bf16[512,128]{1,0:T(8,128)(2,1)S(1)} %join.3.values_ref), channel_id=1, source_target_pairs={{0,2},{1,3},{2,0},{3,1},{4,6},{5,7},{6,4},{7,5},{8,10},{9,11},{10,... | collective-permute-start | bytes 393224 | tf_op jit(solution)/shard_map/ppermute | solution.py:398
  53.4 2.2 %collective-permute-start.14 = (f32[256,128]{1,0:T(8,128)S(1)}, f32[256,128]{1,0:T(8,128)S(1)}, u32[]{:S(2)}, u32[]{:S(2)}) collective-permute-start(f32[256,128]{1,0:T(8,128)S(1)} %forward.11), channel_id=1, source_target_pairs={{0,1},{1,0},{2,3},{3,2},{4,5},{5,4},{6,7},{7,6},{8,9},{9,8},{10,11... | collective-permute-start | bytes 393224 | tf_op jit(solution)/shard_map/ppermute | solution.py:398
  55.6 2.2 %collective-permute-start.15 = (bf16[256,128]{1,0:T(8,128)(2,1)S(1)}, bf16[256,128]{1,0:T(8,128)(2,1)S(1)}, u32[]{:S(2)}, u32[]{:S(2)}) collective-permute-start(bf16[256,128]{1,0:T(8,128)(2,1)S(1)} %residual.3.refs_0_), channel_id=1, source_target_pairs={{0,1},{1,0},{2,3},{3,2},{4,5},{5,4},{6,7},{7,6},{8,9},{9,8},{10,11... | collective-permute-start | bytes 196616 | tf_op jit(solution)/shard_map/ppermute | solution.py:398
  59.0 5.7 %collective-permute-start.16 = (bf16[512,128]{1,0:T(8,128)(2,1)S(1)}, bf16[512,128]{1,0:T(8,128)(2,1)S(1)}, u32[]{:S(2)}, u32[]{:S(2)}) collective-permute-start(bf16[512,128]{1,0:T(8,128)(2,1)S(1)} %backward.11), channel_id=1, source_target_pairs={{0,2},{1,3},{2,0},{3,1},{4,6},{5,7},{6,4},{7,5},{8,10},{9,11},{10,... | collective-permute-start | bytes 393224 | tf_op jit(solution)/shard_map/ppermute | solution.py:398
  64.7 5.2 %collective-permute-start.17 = (bf16[128,128]{1,0:T(8,128)(2,1)S(1)}, bf16[128,128]{1,0:T(8,128)(2,1)S(1)}, u32[]{:S(2)}, u32[]{:S(2)}) collective-permute-start(bf16[128,128]{1,0:T(8,128)(2,1)S(1)} %get-tuple-element.60), channel_id=1, source_target_pairs={{0,8},{1,9},{2,10},{3,11},{4,12},{5,13},{6,14},{7,15},{8,0},{9,1},... | collective-permute-start | bytes 98312 | tf_op jit(solution)/shard_map/ppermute | solution.py:398
  66.0 5.8 %collective-permute-start.18 = (bf16[128,128]{1,0:T(8,128)(2,1)S(1)}, bf16[128,128]{1,0:T(8,128)(2,1)S(1)}, u32[]{:S(2)}, u32[]{:S(2)}) collective-permute-start(bf16[128,128]{1,0:T(8,128)(2,1)S(1)} %get-tuple-element.61), channel_id=1, source_target_pairs={{0,12},{1,13},{2,14},{3,15},{4,8},{5,9},{6,10},{7,11},{8,4},{9,5},... | collective-permute-start | bytes 98312 | tf_op jit(solution)/shard_map/ppermute | solution.py:398
  67.6 4.3 %collective-permute-start.19 = (bf16[128,128]{1,0:T(8,128)(2,1)S(1)}, bf16[128,128]{1,0:T(8,128)(2,1)S(1)}, u32[]{:S(2)}, u32[]{:S(2)}) collective-permute-start(bf16[128,128]{1,0:T(8,128)(2,1)S(1)} %get-tuple-element.62), channel_id=1, source_target_pairs={{0,4},{1,5},{2,6},{3,7},{4,0},{5,1},{6,2},{7,3},{8,12},{9,13},{10,... | collective-permute-start | bytes 98312 | tf_op jit(solution)/shard_map/ppermute | solution.py:398

commit v10 on v9

--- a/solution.py
+++ b/solution.py
@@ -15,6 +15,8 @@
 HIGHEST = lax.Precision.HIGHEST
 VMEM = pl.BlockSpec(memory_space=pltpu.VMEM)
 ANY = pl.BlockSpec(memory_space=pl.ANY)
+SMEM = pl.BlockSpec(memory_space=pltpu.SMEM)
+HBM = pl.BlockSpec(memory_space=pltpu.HBM)
 
 
 def hat(ray, centre):
@@ -93,14 +95,18 @@
 
 
 def setup_kernel(members, stride, span, sizes, tiles, wanted, payload_ref, *refs):
-    refs = refs[-(len(wanted) + 8):]
-    list_refs, row_ref, tables = refs[:len(wanted)], refs[len(wanted)], refs[len(wanted) + 1:]
+    refs = refs[-(2 * len(wanted) + 9):]
+    list_refs, row_ref, tables = refs[:len(wanted)], refs[len(wanted)], refs[len(wanted) + 1:-len(wanted) - 1]
+    drafts, arrived = refs[-len(wanted) - 1:-1], refs[-1]
+    copies = [
+        pltpu.make_async_copy(draft, ref, arrived.at[place])
+        for place, (draft, ref) in enumerate(zip(drafts, list_refs))]
     capacity, depth, frames = sizes
     width = span * capacity
     extent = row_ref.shape[1]
     ray_tiles = row_ref.shape[0] // span
     height = -(-(7 * depth + 2) // 16) * 16
-    lanes = list_refs[0].shape[1]
+    lanes = drafts[0].shape[1]
     me = lax.axis_index("slab").astype(I32)
     parity = lax.rem(me, span)
     first_slot = (me - parity) * capacity
@@ -129,6 +135,35 @@
             lined = collect(member, lined)
     else:
         lined = lax.fori_loop(0, members, collect, lined)
+
+    slot = lax.broadcasted_iota(I32, (1, lanes), 1)
+    within = lax.rem(slot, width)
+    target = lax.bitwise_xor(lax.div(within, capacity), parity)
+    ray = lined[3 * depth:3 * depth + 1]
+    count = lined[3 * depth + 1:3 * depth + 2]
+    alive = jnp.logical_and(lax.rem(within, capacity).astype(F32) < count, slot < members * width)
+
+    table = jnp.concatenate(
+        [slot.astype(F32), ray, target.astype(F32), lined[2 * depth:3 * depth],
+         jnp.zeros((5 - depth, lanes), F32)], axis=0)
+    order = lax.broadcasted_iota(I32, (lanes, lanes), 0)
+    earlier = (lax.broadcasted_iota(I32, (lanes, lanes), 1) < order).astype(F32)
+    for ref, kind, copy in zip(drafts, wanted, copies):
+        taken = alive if kind is None else jnp.logical_and(alive, target == kind)
+        taken = taken.astype(F32)
+        position = contract_lanes(jnp.broadcast_to(taken, (8, lanes)), earlier)[0:1]
+        position = jnp.where(taken > 0.0, position, -1.0).astype(I32)
+        choose = jnp.broadcast_to(position, (lanes, lanes)) == order
+        packed = (contract_lanes(table, choose.astype(F32)) + 0.5).astype(I32)
+        total = jnp.sum(taken, axis=1, keepdims=True).astype(I32)
+        line = jnp.where(slot < total, packed[0:1], lanes)
+        base = packed[1:2] if kind is not None else packed[1:2] + packed[2:3] * ray_tiles
+        member = lax.div(packed[0:1], width) * tiles
+        rows = [line, base * frames]
+        rows += [(packed[3 + level:4 + level] + member) * frames for level in range(depth)]
+        rows += [jnp.zeros((5 - depth, lanes), I32), jnp.broadcast_to(total, (1, lanes))]
+        ref[...] = jnp.concatenate(rows, axis=0)
+        copy.start()
 
     columns = lined.T
     summed = None
@@ -147,38 +182,13 @@
         parts = (wide[0] + wide[1]) + wide[2]
         summed = parts if summed is None else summed + parts
 
-    slot = lax.broadcasted_iota(I32, (1, lanes), 1)
-    within = lax.rem(slot, width)
-    target = lax.bitwise_xor(lax.div(within, capacity), parity)
-    ray = lined[3 * depth:3 * depth + 1]
-    count = lined[3 * depth + 1:3 * depth + 2]
-    alive = jnp.logical_and(lax.rem(within, capacity).astype(F32) < count, slot < members * width)
     tile = lax.broadcasted_iota(I32, (span * ray_tiles, lanes), 0).astype(F32)
     place = ray + (target * ray_tiles).astype(F32)
     place = jnp.where(alive, place, -1.0)
     hot = (jnp.broadcast_to(place, tile.shape) == tile).astype(F32)
     row_ref[...] = jnp.dot(hot, summed, precision=HIGHEST, preferred_element_type=F32)
-
-    table = jnp.concatenate(
-        [slot.astype(F32), ray, target.astype(F32), lined[2 * depth:3 * depth],
-         jnp.zeros((5 - depth, lanes), F32)], axis=0)
-    order = lax.broadcasted_iota(I32, (lanes, lanes), 0)
-    earlier = (lax.broadcasted_iota(I32, (lanes, lanes), 1) < order).astype(F32)
-    for ref, kind in zip(list_refs, wanted):
-        taken = alive if kind is None else jnp.logical_and(alive, target == kind)
-        taken = taken.astype(F32)
-        position = contract_lanes(jnp.broadcast_to(taken, (8, lanes)), earlier)[0:1]
-        position = jnp.where(taken > 0.0, position, -1.0).astype(I32)
-        choose = jnp.broadcast_to(position, (lanes, lanes)) == order
-        packed = (contract_lanes(table, choose.astype(F32)) + 0.5).astype(I32)
-        total = jnp.sum(taken, axis=1, keepdims=True).astype(I32)
-        line = jnp.where(slot < total, packed[0:1], lanes)
-        base = packed[1:2] if kind is not None else packed[1:2] + packed[2:3] * ray_tiles
-        member = lax.div(packed[0:1], width) * tiles
-        rows = [line, base * frames]
-        rows += [(packed[3 + level:4 + level] + member) * frames for level in range(depth)]
-        rows += [jnp.zeros((5 - depth, lanes), I32), jnp.broadcast_to(total, (1, lanes))]
-        ref[...] = jnp.concatenate(rows, axis=0)
+    for copy in copies:
+        copy.wait()
 
 
 def column_kernel(sizes, offset_ref, slope_ref, voxel_ref, live_ref, out_ref):
@@ -243,15 +253,13 @@
     lax.fori_loop(0, rows // step, some, 0)
 
 
-def forward_kernel(sizes, stride, start_row, n_sums, list_ref, values_ref, *refs):
+def forward_kernel(sizes, stride, start_row, n_sums, slots, values_ref, *refs):
     capacity, depth, frames = sizes
     tables, refs = refs[:4], refs[4:]
     start_ref = None
     if start_row is not None:
         start_ref, refs = refs[0], refs[1:]
-    sum_refs, (out_ref, slots, arrived, wide, second) = refs[:n_sums], refs[n_sums:]
-    copy = pltpu.make_async_copy(list_ref, slots, arrived.at[0])
-    copy.start()
+    sum_refs, (out_ref, wide, second) = refs[:n_sums], refs[n_sums:]
     members = values_ref.shape[0] // stride
     rows = wide.shape[0] // members
     rays = second.shape[0]
@@ -271,7 +279,6 @@
     if n_sums:
         half = sum_refs[0].shape[0] // 2
         out_ref[rays:, :] = sum([ref[half:, :] for ref in sum_refs[1:]], sum_refs[0][half:, :])
-    copy.wait()
 
     def one(slot, place):
         line = slots[0, slot]
@@ -313,15 +320,13 @@
     out_ref[...] = ((sinogram_ref[...].astype(F32) - projection) * weight).astype(BF16)
 
 
-def backward_kernel(sizes, n_parts, has_start, list_ref, *refs):
+def backward_kernel(sizes, n_parts, has_start, slots, *refs):
     capacity, depth, frames = sizes
     part_refs, tables, refs = refs[:n_parts], refs[n_parts:n_parts + 3], refs[n_parts + 3:]
     start_ref = None
     if has_start:
         start_ref, refs = refs[0], refs[1:]
-    out_ref, slots, arrived, residual, banks = refs[0], refs[1], refs[2], refs[3], refs[4:]
-    copy = pltpu.make_async_copy(list_ref, slots, arrived.at[0])
-    copy.start()
+    out_ref, residual, banks = refs[0], refs[1], refs[2:]
     rays = part_refs[0].shape[0]
     line_step = tables[0].shape[0] // depth
     for place, ref in enumerate(part_refs):
@@ -335,7 +340,6 @@
                 bank[at, :] = jnp.zeros((at.size, bank.shape[1]), F32)
 
     for_rows(out_ref.shape[0], clear)
-    copy.wait()
 
     def one(slot, place):
         line = slots[0, slot]
@@ -387,7 +391,8 @@
         kernel,
         out_shape=out_shape,
         in_specs=in_specs,
-        out_specs=VMEM if one else [VMEM] * len(out_shape),
+        out_specs=VMEM if one else [
+            SMEM if getattr(out, "memory_space", None) == pltpu.SMEM else VMEM for out in out_shape],
         scratch_shapes=list(scratch),
         compiler_params=pltpu.CompilerParams(vmem_limit_bytes=mib * 1024 * 1024),
         name=name,
@@ -419,8 +424,9 @@
     height = -(-(7 * depth + 2) // 16) * 16 * (n_slots // extent)
     operands = (volume, *slots_by_depth, slot_ray.reshape(1, n_slots), live)
     payload = call(
-        functools.partial(pack_kernel, capacity), "pack", 60, [ANY] * 6,
-        shape((rows + height, extent), BF16), *operands,
+        functools.partial(pack_kernel, capacity), "pack", 16, [HBM] * 6,
+        shape((rows + height, extent), BF16),
+        *[pltpu.with_memory_space_constraint(operand, pltpu.HBM) for operand in operands],
         scratch=[pltpu.VMEM(operand.shape, operand.dtype) for operand in operands]
         + [pltpu.SemaphoreType.DMA((6,))])
 
@@ -429,27 +435,24 @@
         lines = depth * (lanes + 8)
         table = [shape((lines, extent), I32)] + [shape((lines, extent), F32)] * 3
         table += [shape((lines, extent), I32)] + [shape((lines, extent), F32)] * 2
-        out = [shape((8, lanes), I32)] * len(wanted) + [shape((span * ray_tiles, extent), F32)] + table
+        n = len(wanted)
+        out = [pltpu.SMEM((8, lanes), I32)] * n + [shape((span * ray_tiles, extent), F32)] + table
         waits = [] if after is None else [after]
         found = call(
             functools.partial(setup_kernel, members, values.shape[0] // members, span, sizes,
                               voxel_tiles, wanted),
-            "setup", 24, [VMEM] + [ANY] * len(waits), out, values, *waits)
-        n = len(wanted)
+            "setup", 24, [VMEM] + [ANY] * len(waits), out, values, *waits,
+            scratch=[pltpu.VMEM((8, lanes), I32)] * n + [pltpu.SemaphoreType.DMA((n,))])
         return found[:n], found[n], found[n + 1:n + 5], found[n + 5:]
 
-    def list_scratch(slots):
-        return [pltpu.SMEM(slots.shape, I32), pltpu.SemaphoreType.DMA((1,))]
-
     def forward(slots, values, members, table, n_out, start=None, start_row=None, sums=()):
-        operands = [slots, values, *table] + ([] if start is None else [start]) + list(sums)
+        operands = [pltpu.with_memory_space_constraint(slots, pltpu.SMEM), values, *table] + ([] if start is None else [start]) + list(sums)
         extra = ray_tiles if sums else 0
         return call(
             functools.partial(forward_kernel, sizes, values.shape[0] // members, start_row, len(sums)),
-            "forward", 16 if paired else 32, [ANY] + [VMEM] * (len(operands) - 1),
+            "forward", 16 if paired else 32, [SMEM] + [VMEM] * (len(operands) - 1),
             shape((n_out + extra, extent), F32), *operands,
-            scratch=list_scratch(slots)
-            + [pltpu.VMEM((members * rows, extent), F32), pltpu.VMEM((n_out, extent), F32)])
+            scratch=[pltpu.VMEM((members * rows, extent), F32), pltpu.VMEM((n_out, extent), F32)])
 
     def residual_of(projection, row_sums, *sibling):
         operands = [projection, sino, *row_sums, *sibling]
@@ -458,12 +461,12 @@
             [VMEM] * len(operands), shape((n_rays, extent), BF16), *operands)
 
     def backward(slots, parts, members, table, kind, start=None):
-        operands = [slots, *parts, *table] + ([] if start is None else [start])
+        operands = [pltpu.with_memory_space_constraint(slots, pltpu.SMEM), *parts, *table] + ([] if start is None else [start])
         return call(
             functools.partial(backward_kernel, sizes, len(parts), start is not None),
-            "backward", 16 if paired else 32, [ANY] + [VMEM] * (len(operands) - 1),
+            "backward", 16 if paired else 32, [SMEM] + [VMEM] * (len(operands) - 1),
             shape((members * rows, extent), kind), *operands,
-            scratch=list_scratch(slots) + [pltpu.VMEM((len(parts) * n_rays, extent), F32)]
+            scratch=[pltpu.VMEM((len(parts) * n_rays, extent), F32)]
             + [pltpu.VMEM((members * rows, extent), F32)] * n_bank)
 
     def join(*parts):

time: 73.2 us -> 67.3 us (0.919); the launches traced: 72.6 us -> 67.4 us
  Pallas kernels: 26.9 us -> 19.4 us
  waiting for transfers between devices: 21.9 us -> 24.1 us
  starting transfers between devices: 22.7 us -> 23.6 us
  local copies, waits for them, and re-layouts: 0.83 us -> 0.03 us
    pallas_call x24, Pallas kernels: 26.9 us -> 19.4 us  [call(): pl.pallas_call(kernel, out_shape=out_shape, in_specs=in_specs, out_specs=...]
    ppermute x20, waiting for transfers between devices: 21.9 us -> 24.1 us  [exchange(): lax.ppermute(values, 'slab', [(device, device ^ distance) for device in r...]
    ppermute x20, starting transfers between devices: 22.7 us -> 23.6 us  [exchange(): lax.ppermute(values, 'slab', [(device, device ^ distance) for device in r...]
    unnamed x14 -> x12, local copies, waits for them, and re-layouts: 0.83 us -> 0.03 us
  transfers between devices with their start and end apart: 20 -> 20, of which waited for: 13 -> 19; matrix products, arithmetic and copies ran while one was open for 0% -> 0% of each run, Pallas kernels for 25% -> 19%
where the time goes in v10:
time: 67.3 us; the launch traced here: 67.4 us
  waiting for transfers between devices  24.1 us (36%)
  starting transfers between devices  23.6 us (35%)
  Pallas kernels  19.4 us (29%)
    ppermute x20, waiting for transfers between devices, exchange(): lax.ppermute(values, 'slab', [(device, device ^ distance) for device in r...  24.1 us
    ppermute x20, starting transfers between devices, exchange(): lax.ppermute(values, 'slab', [(device, device ^ distance) for device in r...  23.6 us
    pallas_call x24, Pallas kernels, call(): pl.pallas_call(kernel, out_shape=out_shape, in_specs=in_specs, out_specs=...  19.4 us
  transfers between devices with their start and end apart: 20, of which 19 were waited for; matrix products, arithmetic and copies ran while one was open for 0% of the time, Pallas kernels for 19%

profile of v10, /device:TPU:0, one launch (start us, length us, event | category | flops | bytes accessed | tf_op | source)
XLA Modules:
  0.0 67.4 jit_solution(2928879105492265834)
XLA Ops:
  0.0 1.0 %pack.1.refs_0_ = bf16[192,128]{1,0:T(8,128)(2,1)S(1)} custom-call(f32[128,128]{1,0:T(8,128)} %bitcast.10, f32[4,256]{1,0:T(4,128)} %bitcast.12, f32[4,256]{1,0:T(4,128)} %bitcast.14, s32[4,256]{1,0:T(4,128)} %bitcast.16, s32[1,256]{1,0:T(1,128)} %bitcast.20, s32[1,16]{1,0:T(1,128)} %bitcast.18), custom_call_target="tpu_custom_call" | custom-call | tf_op jit(solution)/shard_map/pack/pallas_call | solution.py:390
  1.0 4.1 %collective-permute-start = (bf16[192,128]{1,0:T(8,128)(2,1)S(1)}, bf16[192,128]{1,0:T(8,128)(2,1)S(1)}, u32[]{:S(2)}, u32[]{:S(2)}) collective-permute-start(bf16[192,128]{1,0:T(8,128)(2,1)S(1)} %pack.1.refs_0_), channel_id=1, source_target_pairs={{0,8},{1,9},{2,10},{3,11},{4,12},{5,13},{6,14},{7,15},{8,0},{9,1},... | collective-permute-start | bytes 147464 | tf_op jit(solution)/shard_map/ppermute | solution.py:403
  5.2 1.3 %collective-permute-start.1 = (bf16[192,128]{1,0:T(8,128)(2,1)S(1)}, bf16[192,128]{1,0:T(8,128)(2,1)S(1)}, u32[]{:S(2)}, u32[]{:S(2)}) collective-permute-start(bf16[192,128]{1,0:T(8,128)(2,1)S(1)} %pack.1.refs_0_), channel_id=1, source_target_pairs={{0,12},{1,13},{2,14},{3,15},{4,8},{5,9},{6,10},{7,11},{8,4},{9,5},... | collective-permute-start | bytes 147464 | tf_op jit(solution)/shard_map/ppermute | solution.py:403
  6.7 1.0 %collective-permute-done.refs_1_ = bf16[192,128]{1,0:T(8,128)(2,1)S(1)} collective-permute-done((bf16[192,128]{1,0:T(8,128)(2,1)S(1)}, bf16[192,128]{1,0:T(8,128)(2,1)S(1)}, u32[]{:S(2)}, u32[]{:S(2)}) %collective-permute-start) | collective-permute-done | bytes 49184 | tf_op jit(solution)/shard_map/ppermute | solution.py:403
  7.7 3.4 %collective-permute-done.1.refs_2_ = bf16[192,128]{1,0:T(8,128)(2,1)S(1)} collective-permute-done((bf16[192,128]{1,0:T(8,128)(2,1)S(1)}, bf16[192,128]{1,0:T(8,128)(2,1)S(1)}, u32[]{:S(2)}, u32[]{:S(2)}) %collective-permute-start.1) | collective-permute-done | bytes 49184 | tf_op jit(solution)/shard_map/ppermute | solution.py:403
  11.1 1.6 %collective-permute-start.3 = (bf16[768,128]{1,0:T(8,128)(2,1)S(1)}, bf16[768,128]{1,0:T(8,128)(2,1)S(1)}, u32[]{:S(2)}, u32[]{:S(2)}) collective-permute-start(bf16[768,128]{1,0:T(8,128)(2,1)S(1)} %join.2.payload_ref.values_ref), channel_id=1, source_target_pairs={{0,2},{1,3},{2,0},{3,1},{4,6},{5,7},{6,4},{7,5},{8,10},{9,11},{10,... | collective-permute-start | bytes 589832 | tf_op jit(solution)/shard_map/ppermute | solution.py:403
  12.7 1.5 %setup.2 = (s32[8,128]{1,0:T(8,128)S(4)}, f32[64,128]{1,0:T(8,128)S(1)}, s32[544,128]{1,0:T(8,128)S(1)}, f32[544,128]{1,0:T(8,128)S(1)}, f32[544,128]{1,0:T(8,12...) custom-call(bf16[768,128]{1,0:T(8,128)(2,1)S(1)} %join.2.payload_ref., ...), custom_call_target="tpu_custom_call" | custom-call | tf_op jit(solution)/shard_map/setup/pallas_call | solution.py:390
  14.2 2.2 %forward.6.refs_0_.refs_4_ = f32[512,128]{1,0:T(8,128)S(1)} custom-call(s32[8,128]{1,0:T(8,128)S(4)} %get-tuple-element.34.slots, bf16[768,128]{1,0:T(8,128)(2,1)S(1)} %join.2.payload_ref.values_ref, s32[544,128]{1,0:T(8,128)S(1)} %get-tuple-element.35.refs_0_, f32[544,128]{1,0:T(8,128)S(1)} %get-tuple-element.36.refs_1_, ...), custom_call_target="tpu_custom_call" | custom-call | tf_op jit(solution)/shard_map/forward/pallas_call | solution.py:390
  16.9 1.6 %setup.3 = (s32[8,128]{1,0:T(8,128)S(4)}, s32[8,128]{1,0:T(8,128)S(4)}, f32[64,128]{1,0:T(8,128)S(1)}, s32[544,128]{1,0:T(8,128)S(1)}, f32[544,128]{1,0:T(8,128)...) custom-call(bf16[768,128]{1,0:T(8,128)(2,1)S(1)} %collective-permute, ...), custom_call_target="tpu_custom_call" | custom-call | tf_op jit(solution)/shard_map/setup/pallas_call | solution.py:390
  18.5 0.9 %forward.8 = f32[288,128]{1,0:T(8,128)S(1)} custom-call(s32[8,128]{1,0:T(8,128)S(4)} %get-tuple-element.46.slots, bf16[768,128]{1,0:T(8,128)(2,1)S(1)} %collective-permute-done.3.payload_ref.values_ref, s32[544,128]{1,0:T(8,128)S(1)} %get-tuple-element.40.refs_0_, f32[544,128]{1,0:T(8,128)S(1)} %get-tuple-element.41.refs_1_, ...), custom_call_target="tpu_custom_call" | custom-call | tf_op jit(solution)/shard_map/forward/pallas_call | solution.py:390
  23.0 2.0 %collective-permute-start.6 = (bf16[512,128]{1,0:T(8,128)(2,1)S(1)}, bf16[512,128]{1,0:T(8,128)(2,1)S(1)}, u32[]{:S(2)}, u32[]{:S(2)}) collective-permute-start(bf16[512,128]{1,0:T(8,128)(2,1)S(1)} %backward.8), channel_id=1, source_target_pairs={{0,2},{1,3},{2,0},{3,1},{4,6},{5,7},{6,4},{7,5},{8,10},{9,11},{10,... | collective-permute-start | bytes 393224 | tf_op jit(solution)/shard_map/ppermute | solution.py:403
  24.9 1.8 %backward.6.sum_ref = f32[512,128]{1,0:T(8,128)S(1)} custom-call(s32[8,128]{1,0:T(8,128)S(4)} %get-tuple-element.34.slots, bf16[256,128]{1,0:T(8,128)(2,1)S(1)} %residual.2.refs_0_, bf16[256,128]{1,0:T(8,128)(2,1)S(1)} %collective-permute-done.5.refs_1_.refs_0_, s32[544,128]{1,0:T(8,128)S(1)} %get-tuple-element.47.refs_2_, ...), custom_call_target="tpu_custom_call" | custom-call | tf_op jit(solution)/shard_map/backward/pallas_call | solution.py:390
  26.7 2.2 %collective-permute-done.6.y_ref = bf16[512,128]{1,0:T(8,128)(2,1)S(1)} collective-permute-done((bf16[512,128]{1,0:T(8,128)(2,1)S(1)}, bf16[512,128]{1,0:T(8,128)(2,1)S(1)}, u32[]{:S(2)}, u32[]{:S(2)}) %collective-permute-start.6) | collective-permute-done | bytes 131104 | tf_op jit(solution)/shard_map/ppermute | solution.py:403
  29.0 2.0 %collective-permute-start.7 = (bf16[128,128]{1,0:T(8,128)(2,1)S(1)}, bf16[128,128]{1,0:T(8,128)(2,1)S(1)}, u32[]{:S(2)}, u32[]{:S(2)}) collective-permute-start(bf16[128,128]{1,0:T(8,128)(2,1)S(1)} %get-tuple-element.54), channel_id=1, source_target_pairs={{0,8},{1,9},{2,10},{3,11},{4,12},{5,13},{6,14},{7,15},{8,0},{9,1},... | collective-permute-start | bytes 98312 | tf_op jit(solution)/shard_map/ppermute | solution.py:403
  31.0 1.6 %collective-permute-start.8 = (bf16[128,128]{1,0:T(8,128)(2,1)S(1)}, bf16[128,128]{1,0:T(8,128)(2,1)S(1)}, u32[]{:S(2)}, u32[]{:S(2)}) collective-permute-start(bf16[128,128]{1,0:T(8,128)(2,1)S(1)} %get-tuple-element.55), channel_id=1, source_target_pairs={{0,12},{1,13},{2,14},{3,15},{4,8},{5,9},{6,10},{7,11},{8,4},{9,5},... | collective-permute-start | bytes 98312 | tf_op jit(solution)/shard_map/ppermute | solution.py:403
  34.1 2.7 %collective-permute-done.8.refs_2_ = bf16[128,128]{1,0:T(8,128)(2,1)S(1)} collective-permute-done((bf16[128,128]{1,0:T(8,128)(2,1)S(1)}, bf16[128,128]{1,0:T(8,128)(2,1)S(1)}, u32[]{:S(2)}, u32[]{:S(2)}) %collective-permute-start.8) | collective-permute-done | bytes 32800 | tf_op jit(solution)/shard_map/ppermute | solution.py:403
  37.7 1.6 %collective-permute-start.11 = (bf16[128,128]{1,0:T(8,128)(2,1)S(1)}, bf16[128,128]{1,0:T(8,128)(2,1)S(1)}, u32[]{:S(2)}, u32[]{:S(2)}) collective-permute-start(bf16[128,128]{1,0:T(8,128)(2,1)S(1)} %get-tuple-element.58.refs_0_), channel_id=1, source_target_pairs={{0,12},{1,13},{2,14},{3,15},{4,8},{5,9},{6,10},{7,11},{8,4},{9,5},... | collective-permute-start | bytes 98312 | tf_op jit(solution)/shard_map/ppermute | solution.py:403
  39.3 1.1 %collective-permute-start.12 = (bf16[128,128]{1,0:T(8,128)(2,1)S(1)}, bf16[128,128]{1,0:T(8,128)(2,1)S(1)}, u32[]{:S(2)}, u32[]{:S(2)}) collective-permute-start(bf16[128,128]{1,0:T(8,128)(2,1)S(1)} %get-tuple-element.58.refs_0_), channel_id=1, source_target_pairs={{0,4},{1,5},{2,6},{3,7},{4,0},{5,1},{6,2},{7,3},{8,12},{9,13},{10,... | collective-permute-start | bytes 98312 | tf_op jit(solution)/shard_map/ppermute | solution.py:403
  40.4 1.3 %collective-permute-done.10.refs_1_ = bf16[128,128]{1,0:T(8,128)(2,1)S(1)} collective-permute-done((bf16[128,128]{1,0:T(8,128)(2,1)S(1)}, bf16[128,128]{1,0:T(8,128)(2,1)S(1)}, u32[]{:S(2)}, u32[]{:S(2)}) %collective-permute-start.10) | collective-permute-done | bytes 32800 | tf_op jit(solution)/shard_map/ppermute | solution.py:403
  41.8 1.7 %collective-permute-done.11.refs_2_ = bf16[128,128]{1,0:T(8,128)(2,1)S(1)} collective-permute-done((bf16[128,128]{1,0:T(8,128)(2,1)S(1)}, bf16[128,128]{1,0:T(8,128)(2,1)S(1)}, u32[]{:S(2)}, u32[]{:S(2)}) %collective-permute-start.11) | collective-permute-done | bytes 32800 | tf_op jit(solution)/shard_map/ppermute | solution.py:403
  43.6 1.3 %collective-permute-start.13 = (bf16[512,128]{1,0:T(8,128)(2,1)S(1)}, bf16[512,128]{1,0:T(8,128)(2,1)S(1)}, u32[]{:S(2)}, u32[]{:S(2)}) collective-permute-start(bf16[512,128]{1,0:T(8,128)(2,1)S(1)} %join.3.values_ref), channel_id=1, source_target_pairs={{0,2},{1,3},{2,0},{3,1},{4,6},{5,7},{6,4},{7,5},{8,10},{9,11},{10,... | collective-permute-start | bytes 393224 | tf_op jit(solution)/shard_map/ppermute | solution.py:403
  44.8 2.2 %forward.9.refs_4_ = f32[512,128]{1,0:T(8,128)S(1)} custom-call(s32[8,128]{1,0:T(8,128)S(4)} %get-tuple-element.34.slots, bf16[512,128]{1,0:T(8,128)(2,1)S(1)} %join.3.values_ref, s32[544,128]{1,0:T(8,128)S(1)} %get-tuple-element.35.refs_0_, f32[544,128]{1,0:T(8,128)S(1)} %get-tuple-element.36.refs_1_, f32[544,128]{1,0:T(8,128)S(1)} %get-tuple-element.37.refs_2_, ...), custom_call_target="tpu_custom_call" | custom-call | tf_op jit(solution)/shard_map/forward/pallas_call | solution.py:390
  47.0 1.6 %collective-permute-done.13.values_ref = bf16[512,128]{1,0:T(8,128)(2,1)S(1)} collective-permute-done((bf16[512,128]{1,0:T(8,128)(2,1)S(1)}, bf16[512,128]{1,0:T(8,128)(2,1)S(1)}, u32[]{:S(2)}, u32[]{:S(2)}) %collective-permute-start.13) | collective-permute-done | bytes 131104 | tf_op jit(solution)/shard_map/ppermute | solution.py:403
  48.6 0.9 %forward.11 = f32[256,128]{1,0:T(8,128)S(1)} custom-call(s32[8,128]{1,0:T(8,128)S(4)} %get-tuple-element.46.slots, bf16[512,128]{1,0:T(8,128)(2,1)S(1)} %collective-permute-done.13.values_ref, s32[544,128]{1,0:T(8,128)S(1)} %get-tuple-element.40.refs_0_, f32[544,128]{1,0:T(8,128)S(1)} %get-tuple-element.41.refs_1_, ...), custom_call_target="tpu_custom_call" | custom-call | tf_op jit(solution)/shard_map/forward/pallas_call | solution.py:390
  53.1 1.6 %collective-permute-start.16 = (bf16[512,128]{1,0:T(8,128)(2,1)S(1)}, bf16[512,128]{1,0:T(8,128)(2,1)S(1)}, u32[]{:S(2)}, u32[]{:S(2)}) collective-permute-start(bf16[512,128]{1,0:T(8,128)(2,1)S(1)} %backward.11), channel_id=1, source_target_pairs={{0,2},{1,3},{2,0},{3,1},{4,6},{5,7},{6,4},{7,5},{8,10},{9,11},{10,... | collective-permute-start | bytes 393224 | tf_op jit(solution)/shard_map/ppermute | solution.py:403
  54.7 1.8 %backward.9.sum_ref = f32[512,128]{1,0:T(8,128)S(1)} custom-call(s32[8,128]{1,0:T(8,128)S(4)} %get-tuple-element.34.slots, bf16[256,128]{1,0:T(8,128)(2,1)S(1)} %residual.3.refs_0_, bf16[256,128]{1,0:T(8,128)(2,1)S(1)} %collective-permute-done.15.refs_1_.refs_0_, s32[544,128]{1,0:T(8,128)S(1)} %get-tuple-element.47.refs_2_, ...), custom_call_target="tpu_custom_call" | custom-call | tf_op jit(solution)/shard_map/backward/pallas_call | solution.py:390
  56.5 2.5 %collective-permute-done.16.y_ref = bf16[512,128]{1,0:T(8,128)(2,1)S(1)} collective-permute-done((bf16[512,128]{1,0:T(8,128)(2,1)S(1)}, bf16[512,128]{1,0:T(8,128)(2,1)S(1)}, u32[]{:S(2)}, u32[]{:S(2)}) %collective-permute-start.16) | collective-permute-done | bytes 131104 | tf_op jit(solution)/shard_map/ppermute | solution.py:403
  59.1 1.0 %collective-permute-start.17 = (bf16[128,128]{1,0:T(8,128)(2,1)S(1)}, bf16[128,128]{1,0:T(8,128)(2,1)S(1)}, u32[]{:S(2)}, u32[]{:S(2)}) collective-permute-start(bf16[128,128]{1,0:T(8,128)(2,1)S(1)} %get-tuple-element.60), channel_id=1, source_target_pairs={{0,8},{1,9},{2,10},{3,11},{4,12},{5,13},{6,14},{7,15},{8,0},{9,1},... | collective-permute-start | bytes 98312 | tf_op jit(solution)/shard_map/ppermute | solution.py:403
  60.1 2.8 %collective-permute-start.18 = (bf16[128,128]{1,0:T(8,128)(2,1)S(1)}, bf16[128,128]{1,0:T(8,128)(2,1)S(1)}, u32[]{:S(2)}, u32[]{:S(2)}) collective-permute-start(bf16[128,128]{1,0:T(8,128)(2,1)S(1)} %get-tuple-element.61), channel_id=1, source_target_pairs={{0,12},{1,13},{2,14},{3,15},{4,8},{5,9},{6,10},{7,11},{8,4},{9,5},... | collective-permute-start | bytes 98312 | tf_op jit(solution)/shard_map/ppermute | solution.py:403
  62.9 1.1 %collective-permute-done.17.refs_1_ = bf16[128,128]{1,0:T(8,128)(2,1)S(1)} collective-permute-done((bf16[128,128]{1,0:T(8,128)(2,1)S(1)}, bf16[128,128]{1,0:T(8,128)(2,1)S(1)}, u32[]{:S(2)}, u32[]{:S(2)}) %collective-permute-start.17) | collective-permute-done | bytes 32800 | tf_op jit(solution)/shard_map/ppermute | solution.py:403
  64.0 1.9 %collective-permute-done.18.refs_2_ = bf16[128,128]{1,0:T(8,128)(2,1)S(1)} collective-permute-done((bf16[128,128]{1,0:T(8,128)(2,1)S(1)}, bf16[128,128]{1,0:T(8,128)(2,1)S(1)}, u32[]{:S(2)}, u32[]{:S(2)}) %collective-permute-start.18) | collective-permute-done | bytes 32800 | tf_op jit(solution)/shard_map/ppermute | solution.py:403
  65.8 1.0 %collective-permute-done.19.refs_3_ = bf16[128,128]{1,0:T(8,128)(2,1)S(1)} collective-permute-done((bf16[128,128]{1,0:T(8,128)(2,1)S(1)}, bf16[128,128]{1,0:T(8,128)(2,1)S(1)}, u32[]{:S(2)}, u32[]{:S(2)}) %collective-permute-start.19) | collective-permute-done | bytes 32800 | tf_op jit(solution)/shard_map/ppermute | solution.py:403
  (44 shorter events, 11.0 us)
Async XLA Ops:
  1.0 6.7 %collective-permute-start = (bf16[192,128]{1,0:T(8,128)(2,1)S(1)}, bf16[192,128]{1,0:T(8,128)(2,1)S(1)}, u32[]{:S(2)}, u32[]{:S(2)}) collective-permute-start(bf16[192,128]{1,0:T(8,128)(2,1)S(1)} %pack.1.refs_0_), channel_id=1, source_target_pairs={{0,8},{1,9},{2,10},{3,11},{4,12},{5,13},{6,14},{7,15},{8,0},{9,1},... | collective-permute-start | bytes 147464 | tf_op jit(solution)/shard_map/ppermute | solution.py:403
  5.2 6.0 %collective-permute-start.1 = (bf16[192,128]{1,0:T(8,128)(2,1)S(1)}, bf16[192,128]{1,0:T(8,128)(2,1)S(1)}, u32[]{:S(2)}, u32[]{:S(2)}) collective-permute-start(bf16[192,128]{1,0:T(8,128)(2,1)S(1)} %pack.1.refs_0_), channel_id=1, source_target_pairs={{0,12},{1,13},{2,14},{3,15},{4,8},{5,9},{6,10},{7,11},{8,4},{9,5},... | collective-permute-start | bytes 147464 | tf_op jit(solution)/shard_map/ppermute | solution.py:403
  6.5 4.6 %collective-permute-start.2 = (bf16[192,128]{1,0:T(8,128)(2,1)S(1)}, bf16[192,128]{1,0:T(8,128)(2,1)S(1)}, u32[]{:S(2)}, u32[]{:S(2)}) collective-permute-start(bf16[192,128]{1,0:T(8,128)(2,1)S(1)} %pack.1.refs_0_), channel_id=1, source_target_pairs={{0,4},{1,5},{2,6},{3,7},{4,0},{5,1},{6,2},{7,3},{8,12},{9,13},{10,... | collective-permute-start | bytes 147464 | tf_op jit(solution)/shard_map/ppermute | solution.py:403
  11.1 5.7 %collective-permute-start.3 = (bf16[768,128]{1,0:T(8,128)(2,1)S(1)}, bf16[768,128]{1,0:T(8,128)(2,1)S(1)}, u32[]{:S(2)}, u32[]{:S(2)}) collective-permute-start(bf16[768,128]{1,0:T(8,128)(2,1)S(1)} %join.2.payload_ref.values_ref), channel_id=1, source_target_pairs={{0,2},{1,3},{2,0},{3,1},{4,6},{5,7},{6,4},{7,5},{8,10},{9,11},{10,... | collective-permute-start | bytes 589832 | tf_op jit(solution)/shard_map/ppermute | solution.py:403
  19.4 1.4 %collective-permute-start.4 = (f32[288,128]{1,0:T(8,128)S(1)}, f32[288,128]{1,0:T(8,128)S(1)}, u32[]{:S(2)}, u32[]{:S(2)}) collective-permute-start(f32[288,128]{1,0:T(8,128)S(1)} %forward.8), channel_id=1, source_target_pairs={{0,1},{1,0},{2,3},{3,2},{4,5},{5,4},{6,7},{7,6},{8,9},{9,8},{10,11... | collective-permute-start | bytes 442376 | tf_op jit(solution)/shard_map/ppermute | solution.py:403
  19.5 1.4 %copy-start = (bf16[32,8,128]{2,1,0:T(8,128)(2,1)S(1)}, bf16[32,8,128]{2,1,0:T(8,128)(2,1)}, u32[]{:S(2)}) copy-start(bf16[32,8,128]{2,1,0:T(8,128)(2,1)} %param.7) | copy-start | bytes 196612
  20.9 1.3 %collective-permute-start.5 = (bf16[256,128]{1,0:T(8,128)(2,1)S(1)}, bf16[256,128]{1,0:T(8,128)(2,1)S(1)}, u32[]{:S(2)}, u32[]{:S(2)}) collective-permute-start(bf16[256,128]{1,0:T(8,128)(2,1)S(1)} %residual.2.refs_0_), channel_id=1, source_target_pairs={{0,1},{1,0},{2,3},{3,2},{4,5},{5,4},{6,7},{7,6},{8,9},{9,8},{10,11... | collective-permute-start | bytes 196616 | tf_op jit(solution)/shard_map/ppermute | solution.py:403
  23.0 6.0 %collective-permute-start.6 = (bf16[512,128]{1,0:T(8,128)(2,1)S(1)}, bf16[512,128]{1,0:T(8,128)(2,1)S(1)}, u32[]{:S(2)}, u32[]{:S(2)}) collective-permute-start(bf16[512,128]{1,0:T(8,128)(2,1)S(1)} %backward.8), channel_id=1, source_target_pairs={{0,2},{1,3},{2,0},{3,1},{4,6},{5,7},{6,4},{7,5},{8,10},{9,11},{10,... | collective-permute-start | bytes 393224 | tf_op jit(solution)/shard_map/ppermute | solution.py:403
  28.9 3.7 %copy-start.2 = (f32[256,4]{0,1:T(4,128)S(1)}, f32[256,4]{0,1:T(4,128)}, u32[]{:S(2)}) copy-start(f32[256,4]{0,1:T(4,128)} %param.13) | copy-start | bytes 12292
  28.9 3.7 %copy-start.3 = (f32[256,4]{0,1:T(4,128)S(1)}, f32[256,4]{0,1:T(4,128)}, u32[]{:S(2)}) copy-start(f32[256,4]{0,1:T(4,128)} %param.12) | copy-start | bytes 12292
  28.9 3.7 %copy-start.4 = (s32[256,4]{0,1:T(4,128)S(1)}, s32[256,4]{0,1:T(4,128)}, u32[]{:S(2)}) copy-start(s32[256,4]{0,1:T(4,128)} %param.9) | copy-start | bytes 12292
  28.9 3.7 %copy-start.5 = (s32[16]{0:T(128)S(1)}, s32[16]{0:T(128)}, u32[]{:S(2)}) copy-start(s32[16]{0:T(128)} %param.11) | copy-start | bytes 196
  29.0 7.9 %copy-start.1 = (f32[16,8,128]{2,1,0:T(8,128)S(1)}, f32[16,8,128]{2,1,0:T(8,128)}, u32[]{:S(2)}) copy-start(f32[16,8,128]{2,1,0:T(8,128)} %param.8) | copy-start | bytes 196612
  29.0 5.1 %collective-permute-start.7 = (bf16[128,128]{1,0:T(8,128)(2,1)S(1)}, bf16[128,128]{1,0:T(8,128)(2,1)S(1)}, u32[]{:S(2)}, u32[]{:S(2)}) collective-permute-start(bf16[128,128]{1,0:T(8,128)(2,1)S(1)} %get-tuple-element.54), channel_id=1, source_target_pairs={{0,8},{1,9},{2,10},{3,11},{4,12},{5,13},{6,14},{7,15},{8,0},{9,1},... | collective-permute-start | bytes 98312 | tf_op jit(solution)/shard_map/ppermute | solution.py:403
  31.0 5.8 %collective-permute-start.8 = (bf16[128,128]{1,0:T(8,128)(2,1)S(1)}, bf16[128,128]{1,0:T(8,128)(2,1)S(1)}, u32[]{:S(2)}, u32[]{:S(2)}) collective-permute-start(bf16[128,128]{1,0:T(8,128)(2,1)S(1)} %get-tuple-element.55), channel_id=1, source_target_pairs={{0,12},{1,13},{2,14},{3,15},{4,8},{5,9},{6,10},{7,11},{8,4},{9,5},... | collective-permute-start | bytes 98312 | tf_op jit(solution)/shard_map/ppermute | solution.py:403
  32.6 4.3 %collective-permute-start.9 = (bf16[128,128]{1,0:T(8,128)(2,1)S(1)}, bf16[128,128]{1,0:T(8,128)(2,1)S(1)}, u32[]{:S(2)}, u32[]{:S(2)}) collective-permute-start(bf16[128,128]{1,0:T(8,128)(2,1)S(1)} %get-tuple-element.56), channel_id=1, source_target_pairs={{0,4},{1,5},{2,6},{3,7},{4,0},{5,1},{6,2},{7,3},{8,12},{9,13},{10,... | collective-permute-start | bytes 98312 | tf_op jit(solution)/shard_map/ppermute | solution.py:403
  36.9 4.9 %collective-permute-start.10 = (bf16[128,128]{1,0:T(8,128)(2,1)S(1)}, bf16[128,128]{1,0:T(8,128)(2,1)S(1)}, u32[]{:S(2)}, u32[]{:S(2)}) collective-permute-start(bf16[128,128]{1,0:T(8,128)(2,1)S(1)} %get-tuple-element.58.refs_0_), channel_id=1, source_target_pairs={{0,8},{1,9},{2,10},{3,11},{4,12},{5,13},{6,14},{7,15},{8,0},{9,1},... | collective-permute-start | bytes 98312 | tf_op jit(solution)/shard_map/ppermute | solution.py:403
  37.7 5.8 %collective-permute-start.11 = (bf16[128,128]{1,0:T(8,128)(2,1)S(1)}, bf16[128,128]{1,0:T(8,128)(2,1)S(1)}, u32[]{:S(2)}, u32[]{:S(2)}) collective-permute-start(bf16[128,128]{1,0:T(8,128)(2,1)S(1)} %get-tuple-element.58.refs_0_), channel_id=1, source_target_pairs={{0,12},{1,13},{2,14},{3,15},{4,8},{5,9},{6,10},{7,11},{8,4},{9,5},... | collective-permute-start | bytes 98312 | tf_op jit(solution)/shard_map/ppermute | solution.py:403
  39.3 4.3 %collective-permute-start.12 = (bf16[128,128]{1,0:T(8,128)(2,1)S(1)}, bf16[128,128]{1,0:T(8,128)(2,1)S(1)}, u32[]{:S(2)}, u32[]{:S(2)}) collective-permute-start(bf16[128,128]{1,0:T(8,128)(2,1)S(1)} %get-tuple-element.58.refs_0_), channel_id=1, source_target_pairs={{0,4},{1,5},{2,6},{3,7},{4,0},{5,1},{6,2},{7,3},{8,12},{9,13},{10,... | collective-permute-start | bytes 98312 | tf_op jit(solution)/shard_map/ppermute | solution.py:403
  43.6 5.0 %collective-permute-start.13 = (bf16[512,128]{1,0:T(8,128)(2,1)S(1)}, bf16[512,128]{1,0:T(8,128)(2,1)S(1)}, u32[]{:S(2)}, u32[]{:S(2)}) collective-permute-start(bf16[512,128]{1,0:T(8,128)(2,1)S(1)} %join.3.values_ref), channel_id=1, source_target_pairs={{0,2},{1,3},{2,0},{3,1},{4,6},{5,7},{6,4},{7,5},{8,10},{9,11},{10,... | collective-permute-start | bytes 393224 | tf_op jit(solution)/shard_map/ppermute | solution.py:403
  49.5 1.4 %collective-permute-start.14 = (f32[256,128]{1,0:T(8,128)S(1)}, f32[256,128]{1,0:T(8,128)S(1)}, u32[]{:S(2)}, u32[]{:S(2)}) collective-permute-start(f32[256,128]{1,0:T(8,128)S(1)} %forward.11), channel_id=1, source_target_pairs={{0,1},{1,0},{2,3},{3,2},{4,5},{5,4},{6,7},{7,6},{8,9},{9,8},{10,11... | collective-permute-start | bytes 393224 | tf_op jit(solution)/shard_map/ppermute | solution.py:403
  51.0 1.3 %collective-permute-start.15 = (bf16[256,128]{1,0:T(8,128)(2,1)S(1)}, bf16[256,128]{1,0:T(8,128)(2,1)S(1)}, u32[]{:S(2)}, u32[]{:S(2)}) collective-permute-start(bf16[256,128]{1,0:T(8,128)(2,1)S(1)} %residual.3.refs_0_), channel_id=1, source_target_pairs={{0,1},{1,0},{2,3},{3,2},{4,5},{5,4},{6,7},{7,6},{8,9},{9,8},{10,11... | collective-permute-start | bytes 196616 | tf_op jit(solution)/shard_map/ppermute | solution.py:403
  53.1 6.0 %collective-permute-start.16 = (bf16[512,128]{1,0:T(8,128)(2,1)S(1)}, bf16[512,128]{1,0:T(8,128)(2,1)S(1)}, u32[]{:S(2)}, u32[]{:S(2)}) collective-permute-start(bf16[512,128]{1,0:T(8,128)(2,1)S(1)} %backward.11), channel_id=1, source_target_pairs={{0,2},{1,3},{2,0},{3,1},{4,6},{5,7},{6,4},{7,5},{8,10},{9,11},{10,... | collective-permute-start | bytes 393224 | tf_op jit(solution)/shard_map/ppermute | solution.py:403
  59.1 4.9 %collective-permute-start.17 = (bf16[128,128]{1,0:T(8,128)(2,1)S(1)}, bf16[128,128]{1,0:T(8,128)(2,1)S(1)}, u32[]{:S(2)}, u32[]{:S(2)}) collective-permute-start(bf16[128,128]{1,0:T(8,128)(2,1)S(1)} %get-tuple-element.60), channel_id=1, source_target_pairs={{0,8},{1,9},{2,10},{3,11},{4,12},{5,13},{6,14},{7,15},{8,0},{9,1},... | collective-permute-start | bytes 98312 | tf_op jit(solution)/shard_map/ppermute | solution.py:403
  60.1 5.7 %collective-permute-start.18 = (bf16[128,128]{1,0:T(8,128)(2,1)S(1)}, bf16[128,128]{1,0:T(8,128)(2,1)S(1)}, u32[]{:S(2)}, u32[]{:S(2)}) collective-permute-start(bf16[128,128]{1,0:T(8,128)(2,1)S(1)} %get-tuple-element.61), channel_id=1, source_target_pairs={{0,12},{1,13},{2,14},{3,15},{4,8},{5,9},{6,10},{7,11},{8,4},{9,5},... | collective-permute-start | bytes 98312 | tf_op jit(solution)/shard_map/ppermute | solution.py:403
  62.9 3.9 %collective-permute-start.19 = (bf16[128,128]{1,0:T(8,128)(2,1)S(1)}, bf16[128,128]{1,0:T(8,128)(2,1)S(1)}, u32[]{:S(2)}, u32[]{:S(2)}) collective-permute-start(bf16[128,128]{1,0:T(8,128)(2,1)S(1)} %get-tuple-element.62), channel_id=1, source_target_pairs={{0,4},{1,5},{2,6},{3,7},{4,0},{5,1},{6,2},{7,3},{8,12},{9,13},{10,... | collective-permute-start | bytes 98312 | tf_op jit(solution)/shard_map/ppermute | solution.py:403

commit v11 on v10

--- a/solution.py
+++ b/solution.py
@@ -94,8 +94,9 @@
         out_ref[at, :] = fields[:, part * extent:(part + 1) * extent].astype(BF16)
 
 
-def setup_kernel(members, stride, span, sizes, tiles, wanted, payload_ref, *refs):
-    refs = refs[-(2 * len(wanted) + 9):]
+def setup_kernel(n_payloads, members, stride, span, sizes, tiles, wanted, *refs):
+    payload_refs, refs = refs[:n_payloads], refs[-(2 * len(wanted) + 9):]
+    each = members // n_payloads
     list_refs, row_ref, tables = refs[:len(wanted)], refs[len(wanted)], refs[len(wanted) + 1:-len(wanted) - 1]
     drafts, arrived = refs[-len(wanted) - 1:-1], refs[-1]
     copies = [
@@ -113,8 +114,8 @@
     part = lax.div(first_slot, extent)
     shift = lax.rem(extent - lax.rem(first_slot, extent), extent)
 
-    def collect(member, lined):
-        at = member * stride + tiles * frames + part * height
+    def collect(member, lined, payload_ref, within):
+        at = within * stride + tiles * frames + part * height
         raw = payload_ref[pl.ds(pl.multiple_of(at, 16), height), :].astype(F32)
         offset = (raw[0:depth] + raw[depth:2 * depth]) + raw[2 * depth:3 * depth]
         slope = (raw[3 * depth:4 * depth] + raw[4 * depth:5 * depth]) + raw[5 * depth:6 * depth]
@@ -132,9 +133,10 @@
     lined = jnp.zeros((16, lanes), F32)
     if members <= 16:
         for member in range(members):
-            lined = collect(member, lined)
+            lined = collect(member, lined, payload_refs[member // each], member % each)
     else:
-        lined = lax.fori_loop(0, members, collect, lined)
+        lined = lax.fori_loop(
+            0, members, lambda member, lined: collect(member, lined, payload_refs[0], member), lined)
 
     slot = lax.broadcasted_iota(I32, (1, lanes), 1)
     within = lax.rem(slot, width)
@@ -253,24 +255,26 @@
     lax.fori_loop(0, rows // step, some, 0)
 
 
-def forward_kernel(sizes, stride, start_row, n_sums, slots, values_ref, *refs):
+def forward_kernel(sizes, n_values, members, start_row, n_sums, slots, *refs):
     capacity, depth, frames = sizes
-    tables, refs = refs[:4], refs[4:]
+    value_refs, tables, refs = refs[:n_values], refs[n_values:n_values + 4], refs[n_values + 4:]
     start_ref = None
     if start_row is not None:
         start_ref, refs = refs[0], refs[1:]
     sum_refs, (out_ref, wide, second) = refs[:n_sums], refs[n_sums:]
-    members = values_ref.shape[0] // stride
     rows = wide.shape[0] // members
+    each = members // n_values
+    stride = value_refs[0].shape[0] // each
     rays = second.shape[0]
     line_step = tables[0].shape[0] // depth
 
     def widen(member, carry):
-        at = pl.ds(pl.multiple_of(member * rows, rows), rows)
-        wide[at, :] = values_ref[pl.ds(pl.multiple_of(member * stride, 16), rows), :].astype(F32)
+        for place, ref in enumerate(value_refs):
+            at = pl.ds(pl.multiple_of((place * each + member) * rows, rows), rows)
+            wide[at, :] = ref[pl.ds(pl.multiple_of(member * stride, 16), rows), :].astype(F32)
         return carry
 
-    lax.fori_loop(0, members, widen, 0)
+    lax.fori_loop(0, each, widen, 0)
     second[...] = jnp.zeros_like(second)
     if start_ref is None:
         out_ref[...] = jnp.zeros_like(out_ref)
@@ -320,13 +324,14 @@
     out_ref[...] = ((sinogram_ref[...].astype(F32) - projection) * weight).astype(BF16)
 
 
-def backward_kernel(sizes, n_parts, has_start, slots, *refs):
+def backward_kernel(sizes, n_parts, has_start, split, slots, *refs):
     capacity, depth, frames = sizes
     part_refs, tables, refs = refs[:n_parts], refs[n_parts:n_parts + 3], refs[n_parts + 3:]
     start_ref = None
     if has_start:
         start_ref, refs = refs[0], refs[1:]
-    out_ref, residual, banks = refs[0], refs[1], refs[2:]
+    outs = refs[:len(split)] if split else refs[:1]
+    residual, banks = refs[len(outs)], refs[len(outs) + 1:]
     rays = part_refs[0].shape[0]
     line_step = tables[0].shape[0] // depth
     for place, ref in enumerate(part_refs):
@@ -339,7 +344,7 @@
             else:
                 bank[at, :] = jnp.zeros((at.size, bank.shape[1]), F32)
 
-    for_rows(out_ref.shape[0], clear)
+    for_rows(banks[0].shape[0], clear)
 
     def one(slot, place):
         line = slots[0, slot]
@@ -355,11 +360,19 @@
 
     for_slots(slots, one)
 
-    def finish(at):
-        total = sum([bank[at, :] for bank in banks[1:]], banks[0][at, :])
-        out_ref[at, :] = total.astype(out_ref.dtype)
-
-    for_rows(out_ref.shape[0], finish)
+    def total(at):
+        return sum([bank[at, :] for bank in banks[1:]], banks[0][at, :]).astype(outs[0].dtype)
+
+    if split:
+        for ref, members in zip(outs, split):
+            rows = ref.shape[0] // len(members)
+            for place, member in enumerate(members):
+                ref[place * rows:(place + 1) * rows, :] = total(pl.ds(member * rows, rows))
+    else:
+        def finish(at):
+            outs[0][at, :] = total(at)
+
+        for_rows(outs[0].shape[0], finish)
 
 
 def join_kernel(*refs):
@@ -369,11 +382,11 @@
         at += ref.shape[0]
 
 
-def combine_kernel(sum_ref, y_ref, own_ref, *piece_refs):
-    rows = own_ref.shape[0]
-    for place, ref in enumerate((own_ref,) + piece_refs):
-        at = pl.ds(place * rows, rows)
-        ref[...] = (sum_ref[at, :] + y_ref[at, :].astype(F32)).astype(ref.dtype)
+def combine_kernel(members, sum_ref, y_ref, *piece_refs):
+    rows = piece_refs[0].shape[0]
+    for place, (member, ref) in enumerate(zip(members, piece_refs)):
+        mine = sum_ref[member * rows:(member + 1) * rows, :]
+        ref[...] = (mine + y_ref[place * rows:(place + 1) * rows, :].astype(F32)).astype(ref.dtype)
 
 
 def update_kernel(n_pieces, volume_ref, column_ref, *refs):
@@ -430,7 +443,7 @@
         scratch=[pltpu.VMEM(operand.shape, operand.dtype) for operand in operands]
         + [pltpu.SemaphoreType.DMA((6,))])
 
-    def setup(values, members, wanted, after=None):
+    def setup(payloads, members, wanted, after=None):
         lanes = -(-members * span * capacity // 128) * 128
         lines = depth * (lanes + 8)
         table = [shape((lines, extent), I32)] + [shape((lines, extent), F32)] * 3
@@ -439,17 +452,18 @@
         out = [pltpu.SMEM((8, lanes), I32)] * n + [shape((span * ray_tiles, extent), F32)] + table
         waits = [] if after is None else [after]
         found = call(
-            functools.partial(setup_kernel, members, values.shape[0] // members, span, sizes,
+            functools.partial(setup_kernel, len(payloads), members,
+                              payloads[0].shape[0] * len(payloads) // members, span, sizes,
                               voxel_tiles, wanted),
-            "setup", 24, [VMEM] + [ANY] * len(waits), out, values, *waits,
+            "setup", 24, [VMEM] * len(payloads) + [ANY] * len(waits), out, *payloads, *waits,
             scratch=[pltpu.VMEM((8, lanes), I32)] * n + [pltpu.SemaphoreType.DMA((n,))])
         return found[:n], found[n], found[n + 1:n + 5], found[n + 5:]
 
     def forward(slots, values, members, table, n_out, start=None, start_row=None, sums=()):
-        operands = [pltpu.with_memory_space_constraint(slots, pltpu.SMEM), values, *table] + ([] if start is None else [start]) + list(sums)
+        operands = [pltpu.with_memory_space_constraint(slots, pltpu.SMEM), *values, *table] + ([] if start is None else [start]) + list(sums)
         extra = ray_tiles if sums else 0
         return call(
-            functools.partial(forward_kernel, sizes, values.shape[0] // members, start_row, len(sums)),
+            functools.partial(forward_kernel, sizes, len(values), members, start_row, len(sums)),
             "forward", 16 if paired else 32, [SMEM] + [VMEM] * (len(operands) - 1),
             shape((n_out + extra, extent), F32), *operands,
             scratch=[pltpu.VMEM((members * rows, extent), F32), pltpu.VMEM((n_out, extent), F32)])
@@ -460,12 +474,13 @@
             functools.partial(residual_kernel, frames, len(row_sums)), "residual", 16,
             [VMEM] * len(operands), shape((n_rays, extent), BF16), *operands)
 
-    def backward(slots, parts, members, table, kind, start=None):
+    def backward(slots, parts, members, table, kind, start=None, split=()):
         operands = [pltpu.with_memory_space_constraint(slots, pltpu.SMEM), *parts, *table] + ([] if start is None else [start])
         return call(
-            functools.partial(backward_kernel, sizes, len(parts), start is not None),
+            functools.partial(backward_kernel, sizes, len(parts), start is not None, split),
             "backward", 16 if paired else 32, [SMEM] + [VMEM] * (len(operands) - 1),
-            shape((members * rows, extent), kind), *operands,
+            [shape((len(some) * rows, extent), kind) for some in split]
+            if split else shape((members * rows, extent), kind), *operands,
             scratch=[pltpu.VMEM((len(parts) * n_rays, extent), F32)]
             + [pltpu.VMEM((members * rows, extent), F32)] * n_bank)
 
@@ -486,9 +501,13 @@
     for sweep in range(ITERS):
         last = sweep + 1 == ITERS
         if paired:
-            along_z = join(
-                payload, *[exchange(payload, n_slab, distance) for distance in (8, 12, 4)])
-            along_y = exchange(along_z, n_slab, 2)
+            over_2, over_3, over_1 = [
+                exchange(payload, n_slab, distance) for distance in (8, 12, 4)]
+            z_half = join(payload, over_2)
+            y_half = exchange(z_half, n_slab, 2)
+            z_rest = join(over_3, over_1)
+            y_rest = exchange(z_rest, n_slab, 2)
+            along_z, along_y = (z_half, z_rest), (y_half, y_rest)
             if sweep == 0:
                 (z_list,), z_rows, z_forward, z_backward = setup(along_z, 4, (None,))
             both = forward(z_list, along_z, 4, z_forward, 2 * n_rays)
@@ -504,19 +523,24 @@
             residual = residual_of(own, (z_rows, y_rows), other, first_other)
             other_residual = exchange(residual, n_slab, 1)
             y_sum = backward(own_list, [residual], 4, y_backward, F32)
-            y_sum = backward(other_list, [other_residual], 4, y_backward, BF16, y_sum)
-            y_part = exchange(y_sum, n_slab, 2)
+            far_sum, near_sum = backward(
+                other_list, [other_residual], 4, y_backward, BF16, y_sum, ((1, 2), (0, 3)))
+            far_part, near_part = exchange(far_sum, n_slab, 2), exchange(near_sum, n_slab, 2)
             z_sum = backward(z_list, [residual, other_residual], 4, z_backward, F32)
-            own_piece, *pieces = call(
-                combine_kernel, "combine", 16, [VMEM] * 2,
-                [shape((rows, extent), F32)] + [shape((rows, extent), BF16)] * 3, z_sum, y_part)
-            pieces = [own_piece] + [
-                exchange(piece, n_slab, distance) for piece, distance in zip(pieces, (8, 12, 4))]
+            piece = shape((rows, extent), BF16)
+            piece_2, piece_3 = call(
+                functools.partial(combine_kernel, (1, 2)), "combine", 16, [VMEM] * 2,
+                [piece, piece], z_sum, far_part)
+            got = [exchange(piece_2, n_slab, 8), exchange(piece_3, n_slab, 12)]
+            own_piece, piece_1 = call(
+                functools.partial(combine_kernel, (0, 3)), "combine", 16, [VMEM] * 2,
+                [shape((rows, extent), F32), piece], z_sum, near_part)
+            pieces = [own_piece, *got, exchange(piece_1, n_slab, 4)]
         else:
             everyone = lax.all_gather(payload, "slab", axis=0, tiled=True)
             if sweep == 0:
-                (slots,), row_sums, to_rays, to_voxels = setup(everyone, n_slab, (None,))
-            projection = forward(slots, everyone, n_slab, to_rays, n_rays)
+                (slots,), row_sums, to_rays, to_voxels = setup((everyone,), n_slab, (None,))
+            projection = forward(slots, (everyone,), n_slab, to_rays, n_rays)
             residual = residual_of(projection, (row_sums,))
             sums = backward(slots, [residual], n_slab, to_voxels, BF16)
             parts = lax.all_to_all(

time: 67.3 us -> 66.1 us (0.982)
  waiting for transfers between devices: 24.1 us -> 14 us
  starting transfers between devices: 23.6 us -> 28.8 us
  Pallas kernels: 19.4 us -> 23.1 us
    ppermute x20 -> x24, waiting for transfers between devices: 24.1 us -> 14 us  [exchange(): lax.ppermute(values, 'slab', [(device, device ^ distance) for device in r...]
    ppermute x20 -> x24, starting transfers between devices: 23.6 us -> 28.8 us  [exchange(): lax.ppermute(values, 'slab', [(device, device ^ distance) for device in r...]
    pallas_call x24 -> x28, Pallas kernels: 19.4 us -> 23.1 us  [call(): pl.pallas_call(kernel, out_shape=out_shape, in_specs=in_specs, out_specs=...]
  transfers between devices with their start and end apart: 20 -> 24, of which waited for: 19 -> 14; matrix products, arithmetic and copies ran while one was open for 0% -> 0% of each run, Pallas kernels for 19% -> 23%
where the time goes in v11:
time: 66.1 us; the launch traced here: 66.3 us
  starting transfers between devices  28.8 us (44%)
  Pallas kernels  23.1 us (35%)
  waiting for transfers between devices  14 us (21%)
    ppermute x24, starting transfers between devices, exchange(): lax.ppermute(values, 'slab', [(device, device ^ distance) for device in r...  28.8 us
    pallas_call x28, Pallas kernels, call(): pl.pallas_call(kernel, out_shape=out_shape, in_specs=in_specs, out_specs=...  23.1 us
    ppermute x24, waiting for transfers between devices, exchange(): lax.ppermute(values, 'slab', [(device, device ^ distance) for device in r...  14 us
  transfers between devices with their start and end apart: 24, of which 14 were waited for; matrix products, arithmetic and copies ran while one was open for 0% of the time, Pallas kernels for 23%

profile of v11, /device:TPU:0, one launch (start us, length us, event | category | flops | bytes accessed | tf_op | source)
XLA Modules:
  0.0 66.3 jit_solution(11475238208474338881)
XLA Ops:
  0.0 1.0 %pack.1.refs_0_ = bf16[192,128]{1,0:T(8,128)(2,1)S(1)} custom-call(f32[128,128]{1,0:T(8,128)} %bitcast.10, f32[4,256]{1,0:T(4,128)} %bitcast.12, f32[4,256]{1,0:T(4,128)} %bitcast.14, s32[4,256]{1,0:T(4,128)} %bitcast.16, s32[1,256]{1,0:T(1,128)} %bitcast.20, s32[1,16]{1,0:T(1,128)} %bitcast.18), custom_call_target="tpu_custom_call" | custom-call | tf_op jit(solution)/shard_map/pack/pallas_call | solution.py:403
  1.0 5.1 %collective-permute-start.1 = (bf16[192,128]{1,0:T(8,128)(2,1)S(1)}, bf16[192,128]{1,0:T(8,128)(2,1)S(1)}, u32[]{:S(2)}, u32[]{:S(2)}) collective-permute-start(bf16[192,128]{1,0:T(8,128)(2,1)S(1)} %pack.1.refs_0_), channel_id=1, source_target_pairs={{0,12},{1,13},{2,14},{3,15},{4,8},{5,9},{6,10},{7,11},{8,4},{9,5},... | collective-permute-start | bytes 147464 | tf_op jit(solution)/shard_map/ppermute | solution.py:416
  6.8 1.6 %collective-permute-done.1.refs_0_ = bf16[192,128]{1,0:T(8,128)(2,1)S(1)} collective-permute-done((bf16[192,128]{1,0:T(8,128)(2,1)S(1)}, bf16[192,128]{1,0:T(8,128)(2,1)S(1)}, u32[]{:S(2)}, u32[]{:S(2)}) %collective-permute-start.1) | collective-permute-done | bytes 49184 | tf_op jit(solution)/shard_map/ppermute | solution.py:416
  8.4 1.8 %collective-permute-done.2.refs_1_ = bf16[192,128]{1,0:T(8,128)(2,1)S(1)} collective-permute-done((bf16[192,128]{1,0:T(8,128)(2,1)S(1)}, bf16[192,128]{1,0:T(8,128)(2,1)S(1)}, u32[]{:S(2)}, u32[]{:S(2)}) %collective-permute-start.2) | collective-permute-done | bytes 49184 | tf_op jit(solution)/shard_map/ppermute | solution.py:416
  10.3 1.6 %collective-permute-start.4 = (bf16[384,128]{1,0:T(8,128)(2,1)S(1)}, bf16[384,128]{1,0:T(8,128)(2,1)S(1)}, u32[]{:S(2)}, u32[]{:S(2)}) collective-permute-start(bf16[384,128]{1,0:T(8,128)(2,1)S(1)} %join.5.refs_1_), channel_id=1, source_target_pairs={{0,2},{1,3},{2,0},{3,1},{4,6},{5,7},{6,4},{7,5},{8,10},{9,11},{10,... | collective-permute-start | bytes 294920 | tf_op jit(solution)/shard_map/ppermute | solution.py:416
  11.9 1.2 %collective-permute-start.3 = (bf16[384,128]{1,0:T(8,128)(2,1)S(1)}, bf16[384,128]{1,0:T(8,128)(2,1)S(1)}, u32[]{:S(2)}, u32[]{:S(2)}) collective-permute-start(bf16[384,128]{1,0:T(8,128)(2,1)S(1)} %join.4.refs_0_), channel_id=1, source_target_pairs={{0,2},{1,3},{2,0},{3,1},{4,6},{5,7},{6,4},{7,5},{8,10},{9,11},{10,... | collective-permute-start | bytes 294920 | tf_op jit(solution)/shard_map/ppermute | solution.py:416
  13.0 1.5 %setup.2 = (s32[8,128]{1,0:T(8,128)S(4)}, f32[64,128]{1,0:T(8,128)S(1)}, s32[544,128]{1,0:T(8,128)S(1)}, f32[544,128]{1,0:T(8,128)S(1)}, f32[544,128]{1,0:T(8,12...) custom-call(bf16[384,128]{1,0:T(8,128)(2,1)S(1)} %join.4.refs_0_, ...), custom_call_target="tpu_custom_call" | custom-call | tf_op jit(solution)/shard_map/setup/pallas_call | solution.py:403
  14.5 2.4 %forward.6.refs_2_.refs_6_ = f32[512,128]{1,0:T(8,128)S(1)} custom-call(s32[8,128]{1,0:T(8,128)S(4)} %get-tuple-element.38.slots, bf16[384,128]{1,0:T(8,128)(2,1)S(1)} %join.4.refs_0_, bf16[384,128]{1,0:T(8,128)(2,1)S(1)} %join.5.refs_1_, s32[544,128]{1,0:T(8,128)S(1)} %get-tuple-element.39.refs_2_, f32[544,128]{1,0:T(8,128)S(1)} %get-tuple-element.40.refs_3_, ...), custom_call_target="tpu_custom_call" | custom-call | tf_op jit(solution)/shard_map/forward/pallas_call | solution.py:403
  16.9 1.6 %setup.3 = (s32[8,128]{1,0:T(8,128)S(4)}, s32[8,128]{1,0:T(8,128)S(4)}, f32[64,128]{1,0:T(8,128)S(1)}, s32[544,128]{1,0:T(8,128)S(1)}, f32[544,128]{1,0:T(8,128)...) custom-call(bf16[384,128]{1,0:T(8,128)(2,1)S(1)} %collective-permute, ...), custom_call_target="tpu_custom_call" | custom-call | tf_op jit(solution)/shard_map/setup/pallas_call | solution.py:403
  18.5 1.3 %forward.8 = f32[288,128]{1,0:T(8,128)S(1)} custom-call(s32[8,128]{1,0:T(8,128)S(4)} %get-tuple-element.50.slots, bf16[384,128]{1,0:T(8,128)(2,1)S(1)} %collective-permute-done.3.refs_0_, bf16[384,128]{1,0:T(8,128)(2,1)S(1)} %collective-permute-done.4.refs_1_, s32[544,128]{1,0:T(8,128)S(1)} %get-tuple-element.44.refs_2_, ...), custom_call_target="tpu_custom_call" | custom-call | tf_op jit(solution)/shard_map/forward/pallas_call | solution.py:403
  20.0 1.1 %forward.7.projection_ref = f32[256,128]{1,0:T(8,128)S(1)} custom-call(s32[8,128]{1,0:T(8,128)S(4)} %get-tuple-element.43.slots, bf16[384,128]{1,0:T(8,128)(2,1)S(1)} %collective-permute-done.3.refs_0_, bf16[384,128]{1,0:T(8,128)(2,1)S(1)} %collective-permute-done.4.refs_1_, s32[544,128]{1,0:T(8,128)S(1)} %get-tuple-element.44.refs_2_, ...), custom_call_target="tpu_custom_call" | custom-call | tf_op jit(solution)/shard_map/forward/pallas_call | solution.py:403
  22.7 1.1 %backward.8 = (bf16[256,128]{1,0:T(8,128)(2,1)S(1)}, bf16[256,128]{1,0:T(8,128)(2,1)S(1)}) custom-call(s32[8,128]{1,0:T(8,128)S(4)} %get-tuple-element.50.slots, bf16[256,128]{1,0:T(8,128)(2,1)S(1)} %collective-permute-done.6.refs_1_.refs_0_, s32[544,128]{1,0:T(8,128)S(1)} %get-tuple-element.54.refs_1_, f32[544,128]{1,0:T(8,128)S(1)} %get-tuple-element.55.refs_2_, ...), custom_call_target="tpu_custom_call" | custom-call | tf_op jit(solution)/shard_map/backward/pallas_call | solution.py:403
  24.4 1.5 %collective-permute-start.7 = (bf16[256,128]{1,0:T(8,128)(2,1)S(1)}, bf16[256,128]{1,0:T(8,128)(2,1)S(1)}, u32[]{:S(2)}, u32[]{:S(2)}) collective-permute-start(bf16[256,128]{1,0:T(8,128)(2,1)S(1)} %get-tuple-element.57), channel_id=1, source_target_pairs={{0,2},{1,3},{2,0},{3,1},{4,6},{5,7},{6,4},{7,5},{8,10},{9,11},{10,... | collective-permute-start | bytes 196616 | tf_op jit(solution)/shard_map/ppermute | solution.py:416
  25.9 2.0 %backward.6.sum_ref = f32[512,128]{1,0:T(8,128)S(1)} custom-call(s32[8,128]{1,0:T(8,128)S(4)} %get-tuple-element.38.slots, bf16[256,128]{1,0:T(8,128)(2,1)S(1)} %residual.2.refs_0_, bf16[256,128]{1,0:T(8,128)(2,1)S(1)} %collective-permute-done.6.refs_1_.refs_0_, s32[544,128]{1,0:T(8,128)S(1)} %get-tuple-element.51.refs_2_, ...), custom_call_target="tpu_custom_call" | custom-call | tf_op jit(solution)/shard_map/backward/pallas_call | solution.py:403
  28.5 1.9 %collective-permute-start.10 = (bf16[128,128]{1,0:T(8,128)(2,1)S(1)}, bf16[128,128]{1,0:T(8,128)(2,1)S(1)}, u32[]{:S(2)}, u32[]{:S(2)}) collective-permute-start(bf16[128,128]{1,0:T(8,128)(2,1)S(1)} %get-tuple-element.61), channel_id=1, source_target_pairs={{0,12},{1,13},{2,14},{3,15},{4,8},{5,9},{6,10},{7,11},{8,4},{9,5},... | collective-permute-start | bytes 98312 | tf_op jit(solution)/shard_map/ppermute | solution.py:416
  30.4 1.2 %collective-permute-start.9 = (bf16[128,128]{1,0:T(8,128)(2,1)S(1)}, bf16[128,128]{1,0:T(8,128)(2,1)S(1)}, u32[]{:S(2)}, u32[]{:S(2)}) collective-permute-start(bf16[128,128]{1,0:T(8,128)(2,1)S(1)} %get-tuple-element.60), channel_id=1, source_target_pairs={{0,8},{1,9},{2,10},{3,11},{4,12},{5,13},{6,14},{7,15},{8,0},{9,1},... | collective-permute-start | bytes 98312 | tf_op jit(solution)/shard_map/ppermute | solution.py:416
  31.7 1.3 %collective-permute-start.11 = (bf16[128,128]{1,0:T(8,128)(2,1)S(1)}, bf16[128,128]{1,0:T(8,128)(2,1)S(1)}, u32[]{:S(2)}, u32[]{:S(2)}) collective-permute-start(bf16[128,128]{1,0:T(8,128)(2,1)S(1)} %get-tuple-element.62), channel_id=1, source_target_pairs={{0,4},{1,5},{2,6},{3,7},{4,0},{5,1},{6,2},{7,3},{8,12},{9,13},{10,... | collective-permute-start | bytes 98312 | tf_op jit(solution)/shard_map/ppermute | solution.py:416
  35.7 1.9 %collective-permute-start.14 = (bf16[128,128]{1,0:T(8,128)(2,1)S(1)}, bf16[128,128]{1,0:T(8,128)(2,1)S(1)}, u32[]{:S(2)}, u32[]{:S(2)}) collective-permute-start(bf16[128,128]{1,0:T(8,128)(2,1)S(1)} %get-tuple-element.64.refs_0_), channel_id=1, source_target_pairs={{0,12},{1,13},{2,14},{3,15},{4,8},{5,9},{6,10},{7,11},{8,4},{9,5},... | collective-permute-start | bytes 98312 | tf_op jit(solution)/shard_map/ppermute | solution.py:416
  38.1 2.1 %collective-permute-start.12 = (bf16[128,128]{1,0:T(8,128)(2,1)S(1)}, bf16[128,128]{1,0:T(8,128)(2,1)S(1)}, u32[]{:S(2)}, u32[]{:S(2)}) collective-permute-start(bf16[128,128]{1,0:T(8,128)(2,1)S(1)} %get-tuple-element.64.refs_0_), channel_id=1, source_target_pairs={{0,8},{1,9},{2,10},{3,11},{4,12},{5,13},{6,14},{7,15},{8,0},{9,1},... | collective-permute-start | bytes 98312 | tf_op jit(solution)/shard_map/ppermute | solution.py:416
  40.2 1.4 %collective-permute-done.14.refs_0_ = bf16[128,128]{1,0:T(8,128)(2,1)S(1)} collective-permute-done((bf16[128,128]{1,0:T(8,128)(2,1)S(1)}, bf16[128,128]{1,0:T(8,128)(2,1)S(1)}, u32[]{:S(2)}, u32[]{:S(2)}) %collective-permute-start.14) | collective-permute-done | bytes 32800 | tf_op jit(solution)/shard_map/ppermute | solution.py:416
  41.9 1.1 %collective-permute-start.16 = (bf16[256,128]{1,0:T(8,128)(2,1)S(1)}, bf16[256,128]{1,0:T(8,128)(2,1)S(1)}, u32[]{:S(2)}, u32[]{:S(2)}) collective-permute-start(bf16[256,128]{1,0:T(8,128)(2,1)S(1)} %join.7.refs_1_), channel_id=1, source_target_pairs={{0,2},{1,3},{2,0},{3,1},{4,6},{5,7},{6,4},{7,5},{8,10},{9,11},{10,... | collective-permute-start | bytes 196616 | tf_op jit(solution)/shard_map/ppermute | solution.py:416
  42.9 1.4 %collective-permute-start.13 = (bf16[256,128]{1,0:T(8,128)(2,1)S(1)}, bf16[256,128]{1,0:T(8,128)(2,1)S(1)}, u32[]{:S(2)}, u32[]{:S(2)}) collective-permute-start(bf16[256,128]{1,0:T(8,128)(2,1)S(1)} %join.6.refs_0_), channel_id=1, source_target_pairs={{0,2},{1,3},{2,0},{3,1},{4,6},{5,7},{6,4},{7,5},{8,10},{9,11},{10,... | collective-permute-start | bytes 196616 | tf_op jit(solution)/shard_map/ppermute | solution.py:416
  44.4 2.4 %forward.9.refs_6_ = f32[512,128]{1,0:T(8,128)S(1)} custom-call(s32[8,128]{1,0:T(8,128)S(4)} %get-tuple-element.38.slots, bf16[256,128]{1,0:T(8,128)(2,1)S(1)} %join.6.refs_0_, bf16[256,128]{1,0:T(8,128)(2,1)S(1)} %join.7.refs_1_, s32[544,128]{1,0:T(8,128)S(1)} %get-tuple-element.39.refs_2_, f32[544,128]{1,0:T(8,128)S(1)} %get-tuple-element.40.refs_3_, ...), custom_call_target="tpu_custom_call" | custom-call | tf_op jit(solution)/shard_map/forward/pallas_call | solution.py:403
  47.3 1.3 %forward.11 = f32[256,128]{1,0:T(8,128)S(1)} custom-call(s32[8,128]{1,0:T(8,128)S(4)} %get-tuple-element.50.slots, bf16[256,128]{1,0:T(8,128)(2,1)S(1)} %collective-permute-done.13.refs_0_, bf16[256,128]{1,0:T(8,128)(2,1)S(1)} %collective-permute-done.16.refs_1_, s32[544,128]{1,0:T(8,128)S(1)} %get-tuple-element.44.refs_2_, ...), custom_call_target="tpu_custom_call" | custom-call | tf_op jit(solution)/shard_map/forward/pallas_call | solution.py:403
  48.7 1.1 %forward.10.projection_ref = f32[256,128]{1,0:T(8,128)S(1)} custom-call(s32[8,128]{1,0:T(8,128)S(4)} %get-tuple-element.43.slots, bf16[256,128]{1,0:T(8,128)(2,1)S(1)} %collective-permute-done.13.refs_0_, bf16[256,128]{1,0:T(8,128)(2,1)S(1)} %collective-permute-done.16.refs_1_, s32[544,128]{1,0:T(8,128)S(1)} %get-tuple-element.44.refs_2_, ...), custom_call_target="tpu_custom_call" | custom-call | tf_op jit(solution)/shard_map/forward/pallas_call | solution.py:403
  51.4 1.1 %backward.11 = (bf16[256,128]{1,0:T(8,128)(2,1)S(1)}, bf16[256,128]{1,0:T(8,128)(2,1)S(1)}) custom-call(s32[8,128]{1,0:T(8,128)S(4)} %get-tuple-element.50.slots, bf16[256,128]{1,0:T(8,128)(2,1)S(1)} %collective-permute-done.18.refs_1_.refs_0_, s32[544,128]{1,0:T(8,128)S(1)} %get-tuple-element.54.refs_1_, f32[544,128]{1,0:T(8,128)S(1)} %get-tuple-element.55.refs_2_, ...), custom_call_target="tpu_custom_call" | custom-call | tf_op jit(solution)/shard_map/backward/pallas_call | solution.py:403
  52.5 1.2 %collective-permute-start.20 = (bf16[256,128]{1,0:T(8,128)(2,1)S(1)}, bf16[256,128]{1,0:T(8,128)(2,1)S(1)}, u32[]{:S(2)}, u32[]{:S(2)}) collective-permute-start(bf16[256,128]{1,0:T(8,128)(2,1)S(1)} %get-tuple-element.67), channel_id=1, source_target_pairs={{0,2},{1,3},{2,0},{3,1},{4,6},{5,7},{6,4},{7,5},{8,10},{9,11},{10,... | collective-permute-start | bytes 196616 | tf_op jit(solution)/shard_map/ppermute | solution.py:416
  54.6 2.0 %backward.9.sum_ref = f32[512,128]{1,0:T(8,128)S(1)} custom-call(s32[8,128]{1,0:T(8,128)S(4)} %get-tuple-element.38.slots, bf16[256,128]{1,0:T(8,128)(2,1)S(1)} %residual.3.refs_0_, bf16[256,128]{1,0:T(8,128)(2,1)S(1)} %collective-permute-done.18.refs_1_.refs_0_, s32[544,128]{1,0:T(8,128)S(1)} %get-tuple-element.51.refs_2_, ...), custom_call_target="tpu_custom_call" | custom-call | tf_op jit(solution)/shard_map/backward/pallas_call | solution.py:403
  57.3 2.6 %collective-permute-start.21 = (bf16[128,128]{1,0:T(8,128)(2,1)S(1)}, bf16[128,128]{1,0:T(8,128)(2,1)S(1)}, u32[]{:S(2)}, u32[]{:S(2)}) collective-permute-start(bf16[128,128]{1,0:T(8,128)(2,1)S(1)} %get-tuple-element.68), channel_id=1, source_target_pairs={{0,8},{1,9},{2,10},{3,11},{4,12},{5,13},{6,14},{7,15},{8,0},{9,1},... | collective-permute-start | bytes 98312 | tf_op jit(solution)/shard_map/ppermute | solution.py:416
  59.9 1.2 %collective-permute-start.22 = (bf16[128,128]{1,0:T(8,128)(2,1)S(1)}, bf16[128,128]{1,0:T(8,128)(2,1)S(1)}, u32[]{:S(2)}, u32[]{:S(2)}) collective-permute-start(bf16[128,128]{1,0:T(8,128)(2,1)S(1)} %get-tuple-element.69), channel_id=1, source_target_pairs={{0,12},{1,13},{2,14},{3,15},{4,8},{5,9},{6,10},{7,11},{8,4},{9,5},... | collective-permute-start | bytes 98312 | tf_op jit(solution)/shard_map/ppermute | solution.py:416
  61.2 1.1 %collective-permute-done.21.refs_1_ = bf16[128,128]{1,0:T(8,128)(2,1)S(1)} collective-permute-done((bf16[128,128]{1,0:T(8,128)(2,1)S(1)}, bf16[128,128]{1,0:T(8,128)(2,1)S(1)}, u32[]{:S(2)}, u32[]{:S(2)}) %collective-permute-start.21) | collective-permute-done | bytes 32800 | tf_op jit(solution)/shard_map/ppermute | solution.py:416
  62.2 3.4 %collective-permute-done.22.refs_2_ = bf16[128,128]{1,0:T(8,128)(2,1)S(1)} collective-permute-done((bf16[128,128]{1,0:T(8,128)(2,1)S(1)}, bf16[128,128]{1,0:T(8,128)(2,1)S(1)}, u32[]{:S(2)}, u32[]{:S(2)}) %collective-permute-start.22) | collective-permute-done | bytes 32800 | tf_op jit(solution)/shard_map/ppermute | solution.py:416
  (56 shorter events, 11.5 us)
Async XLA Ops:
  1.0 7.4 %collective-permute-start.1 = (bf16[192,128]{1,0:T(8,128)(2,1)S(1)}, bf16[192,128]{1,0:T(8,128)(2,1)S(1)}, u32[]{:S(2)}, u32[]{:S(2)}) collective-permute-start(bf16[192,128]{1,0:T(8,128)(2,1)S(1)} %pack.1.refs_0_), channel_id=1, source_target_pairs={{0,12},{1,13},{2,14},{3,15},{4,8},{5,9},{6,10},{7,11},{8,4},{9,5},... | collective-permute-start | bytes 147464 | tf_op jit(solution)/shard_map/ppermute | solution.py:416
  6.2 4.1 %collective-permute-start.2 = (bf16[192,128]{1,0:T(8,128)(2,1)S(1)}, bf16[192,128]{1,0:T(8,128)(2,1)S(1)}, u32[]{:S(2)}, u32[]{:S(2)}) collective-permute-start(bf16[192,128]{1,0:T(8,128)(2,1)S(1)} %pack.1.refs_0_), channel_id=1, source_target_pairs={{0,4},{1,5},{2,6},{3,7},{4,0},{5,1},{6,2},{7,3},{8,12},{9,13},{10,... | collective-permute-start | bytes 147464 | tf_op jit(solution)/shard_map/ppermute | solution.py:416
  6.2 5.7 %collective-permute-start = (bf16[192,128]{1,0:T(8,128)(2,1)S(1)}, bf16[192,128]{1,0:T(8,128)(2,1)S(1)}, u32[]{:S(2)}, u32[]{:S(2)}) collective-permute-start(bf16[192,128]{1,0:T(8,128)(2,1)S(1)} %pack.1.refs_0_), channel_id=1, source_target_pairs={{0,8},{1,9},{2,10},{3,11},{4,12},{5,13},{6,14},{7,15},{8,0},{9,1},... | collective-permute-start | bytes 147464 | tf_op jit(solution)/shard_map/ppermute | solution.py:416
  10.3 6.7 %collective-permute-start.4 = (bf16[384,128]{1,0:T(8,128)(2,1)S(1)}, bf16[384,128]{1,0:T(8,128)(2,1)S(1)}, u32[]{:S(2)}, u32[]{:S(2)}) collective-permute-start(bf16[384,128]{1,0:T(8,128)(2,1)S(1)} %join.5.refs_1_), channel_id=1, source_target_pairs={{0,2},{1,3},{2,0},{3,1},{4,6},{5,7},{6,4},{7,5},{8,10},{9,11},{10,... | collective-permute-start | bytes 294920 | tf_op jit(solution)/shard_map/ppermute | solution.py:416
  11.9 5.1 %collective-permute-start.3 = (bf16[384,128]{1,0:T(8,128)(2,1)S(1)}, bf16[384,128]{1,0:T(8,128)(2,1)S(1)}, u32[]{:S(2)}, u32[]{:S(2)}) collective-permute-start(bf16[384,128]{1,0:T(8,128)(2,1)S(1)} %join.4.refs_0_), channel_id=1, source_target_pairs={{0,2},{1,3},{2,0},{3,1},{4,6},{5,7},{6,4},{7,5},{8,10},{9,11},{10,... | collective-permute-start | bytes 294920 | tf_op jit(solution)/shard_map/ppermute | solution.py:416
  19.9 1.4 %collective-permute-start.5 = (f32[288,128]{1,0:T(8,128)S(1)}, f32[288,128]{1,0:T(8,128)S(1)}, u32[]{:S(2)}, u32[]{:S(2)}) collective-permute-start(f32[288,128]{1,0:T(8,128)S(1)} %forward.8), channel_id=1, source_target_pairs={{0,1},{1,0},{2,3},{3,2},{4,5},{5,4},{6,7},{7,6},{8,9},{9,8},{10,11... | collective-permute-start | bytes 442376 | tf_op jit(solution)/shard_map/ppermute | solution.py:416
  20.0 1.4 %copy-start = (bf16[32,8,128]{2,1,0:T(8,128)(2,1)S(1)}, bf16[32,8,128]{2,1,0:T(8,128)(2,1)}, u32[]{:S(2)}) copy-start(bf16[32,8,128]{2,1,0:T(8,128)(2,1)} %param.7) | copy-start | bytes 196612
  21.3 1.3 %collective-permute-start.6 = (bf16[256,128]{1,0:T(8,128)(2,1)S(1)}, bf16[256,128]{1,0:T(8,128)(2,1)S(1)}, u32[]{:S(2)}, u32[]{:S(2)}) collective-permute-start(bf16[256,128]{1,0:T(8,128)(2,1)S(1)} %residual.2.refs_0_), channel_id=1, source_target_pairs={{0,1},{1,0},{2,3},{3,2},{4,5},{5,4},{6,7},{7,6},{8,9},{9,8},{10,11... | collective-permute-start | bytes 196616 | tf_op jit(solution)/shard_map/ppermute | solution.py:416
  23.8 4.7 %collective-permute-start.8 = (bf16[256,128]{1,0:T(8,128)(2,1)S(1)}, bf16[256,128]{1,0:T(8,128)(2,1)S(1)}, u32[]{:S(2)}, u32[]{:S(2)}) collective-permute-start(bf16[256,128]{1,0:T(8,128)(2,1)S(1)} %get-tuple-element.59), channel_id=1, source_target_pairs={{0,2},{1,3},{2,0},{3,1},{4,6},{5,7},{6,4},{7,5},{8,10},{9,11},{10,... | collective-permute-start | bytes 196616 | tf_op jit(solution)/shard_map/ppermute | solution.py:416
  24.4 7.3 %collective-permute-start.7 = (bf16[256,128]{1,0:T(8,128)(2,1)S(1)}, bf16[256,128]{1,0:T(8,128)(2,1)S(1)}, u32[]{:S(2)}, u32[]{:S(2)}) collective-permute-start(bf16[256,128]{1,0:T(8,128)(2,1)S(1)} %get-tuple-element.57), channel_id=1, source_target_pairs={{0,2},{1,3},{2,0},{3,1},{4,6},{5,7},{6,4},{7,5},{8,10},{9,11},{10,... | collective-permute-start | bytes 196616 | tf_op jit(solution)/shard_map/ppermute | solution.py:416
  28.5 5.8 %collective-permute-start.10 = (bf16[128,128]{1,0:T(8,128)(2,1)S(1)}, bf16[128,128]{1,0:T(8,128)(2,1)S(1)}, u32[]{:S(2)}, u32[]{:S(2)}) collective-permute-start(bf16[128,128]{1,0:T(8,128)(2,1)S(1)} %get-tuple-element.61), channel_id=1, source_target_pairs={{0,12},{1,13},{2,14},{3,15},{4,8},{5,9},{6,10},{7,11},{8,4},{9,5},... | collective-permute-start | bytes 98312 | tf_op jit(solution)/shard_map/ppermute | solution.py:416
  30.4 4.8 %collective-permute-start.9 = (bf16[128,128]{1,0:T(8,128)(2,1)S(1)}, bf16[128,128]{1,0:T(8,128)(2,1)S(1)}, u32[]{:S(2)}, u32[]{:S(2)}) collective-permute-start(bf16[128,128]{1,0:T(8,128)(2,1)S(1)} %get-tuple-element.60), channel_id=1, source_target_pairs={{0,8},{1,9},{2,10},{3,11},{4,12},{5,13},{6,14},{7,15},{8,0},{9,1},... | collective-permute-start | bytes 98312 | tf_op jit(solution)/shard_map/ppermute | solution.py:416
  31.7 1.4 %copy-start.2 = (f32[256,4]{0,1:T(4,128)S(1)}, f32[256,4]{0,1:T(4,128)}, u32[]{:S(2)}) copy-start(f32[256,4]{0,1:T(4,128)} %param.13) | copy-start | bytes 12292
  31.7 1.4 %copy-start.3 = (f32[256,4]{0,1:T(4,128)S(1)}, f32[256,4]{0,1:T(4,128)}, u32[]{:S(2)}) copy-start(f32[256,4]{0,1:T(4,128)} %param.12) | copy-start | bytes 12292
  31.7 1.4 %copy-start.4 = (s32[256,4]{0,1:T(4,128)S(1)}, s32[256,4]{0,1:T(4,128)}, u32[]{:S(2)}) copy-start(s32[256,4]{0,1:T(4,128)} %param.9) | copy-start | bytes 12292
  31.7 1.4 %copy-start.5 = (s32[16]{0:T(128)S(1)}, s32[16]{0:T(128)}, u32[]{:S(2)}) copy-start(s32[16]{0:T(128)} %param.11) | copy-start | bytes 196
  31.7 4.0 %copy-start.1 = (f32[16,8,128]{2,1,0:T(8,128)S(1)}, f32[16,8,128]{2,1,0:T(8,128)}, u32[]{:S(2)}) copy-start(f32[16,8,128]{2,1,0:T(8,128)} %param.8) | copy-start | bytes 196612
  31.7 4.0 %collective-permute-start.11 = (bf16[128,128]{1,0:T(8,128)(2,1)S(1)}, bf16[128,128]{1,0:T(8,128)(2,1)S(1)}, u32[]{:S(2)}, u32[]{:S(2)}) collective-permute-start(bf16[128,128]{1,0:T(8,128)(2,1)S(1)} %get-tuple-element.62), channel_id=1, source_target_pairs={{0,4},{1,5},{2,6},{3,7},{4,0},{5,1},{6,2},{7,3},{8,12},{9,13},{10,... | collective-permute-start | bytes 98312 | tf_op jit(solution)/shard_map/ppermute | solution.py:416
  35.7 5.8 %collective-permute-start.14 = (bf16[128,128]{1,0:T(8,128)(2,1)S(1)}, bf16[128,128]{1,0:T(8,128)(2,1)S(1)}, u32[]{:S(2)}, u32[]{:S(2)}) collective-permute-start(bf16[128,128]{1,0:T(8,128)(2,1)S(1)} %get-tuple-element.64.refs_0_), channel_id=1, source_target_pairs={{0,12},{1,13},{2,14},{3,15},{4,8},{5,9},{6,10},{7,11},{8,4},{9,5},... | collective-permute-start | bytes 98312 | tf_op jit(solution)/shard_map/ppermute | solution.py:416
  37.6 4.2 %collective-permute-start.15 = (bf16[128,128]{1,0:T(8,128)(2,1)S(1)}, bf16[128,128]{1,0:T(8,128)(2,1)S(1)}, u32[]{:S(2)}, u32[]{:S(2)}) collective-permute-start(bf16[128,128]{1,0:T(8,128)(2,1)S(1)} %get-tuple-element.64.refs_0_), channel_id=1, source_target_pairs={{0,4},{1,5},{2,6},{3,7},{4,0},{5,1},{6,2},{7,3},{8,12},{9,13},{10,... | collective-permute-start | bytes 98312 | tf_op jit(solution)/shard_map/ppermute | solution.py:416
  38.1 4.9 %collective-permute-start.12 = (bf16[128,128]{1,0:T(8,128)(2,1)S(1)}, bf16[128,128]{1,0:T(8,128)(2,1)S(1)}, u32[]{:S(2)}, u32[]{:S(2)}) collective-permute-start(bf16[128,128]{1,0:T(8,128)(2,1)S(1)} %get-tuple-element.64.refs_0_), channel_id=1, source_target_pairs={{0,8},{1,9},{2,10},{3,11},{4,12},{5,13},{6,14},{7,15},{8,0},{9,1},... | collective-permute-start | bytes 98312 | tf_op jit(solution)/shard_map/ppermute | solution.py:416
  41.9 4.9 %collective-permute-start.16 = (bf16[256,128]{1,0:T(8,128)(2,1)S(1)}, bf16[256,128]{1,0:T(8,128)(2,1)S(1)}, u32[]{:S(2)}, u32[]{:S(2)}) collective-permute-start(bf16[256,128]{1,0:T(8,128)(2,1)S(1)} %join.7.refs_1_), channel_id=1, source_target_pairs={{0,2},{1,3},{2,0},{3,1},{4,6},{5,7},{6,4},{7,5},{8,10},{9,11},{10,... | collective-permute-start | bytes 196616 | tf_op jit(solution)/shard_map/ppermute | solution.py:416
  42.9 4.3 %collective-permute-start.13 = (bf16[256,128]{1,0:T(8,128)(2,1)S(1)}, bf16[256,128]{1,0:T(8,128)(2,1)S(1)}, u32[]{:S(2)}, u32[]{:S(2)}) collective-permute-start(bf16[256,128]{1,0:T(8,128)(2,1)S(1)} %join.6.refs_0_), channel_id=1, source_target_pairs={{0,2},{1,3},{2,0},{3,1},{4,6},{5,7},{6,4},{7,5},{8,10},{9,11},{10,... | collective-permute-start | bytes 196616 | tf_op jit(solution)/shard_map/ppermute | solution.py:416
  48.6 1.4 %collective-permute-start.17 = (f32[256,128]{1,0:T(8,128)S(1)}, f32[256,128]{1,0:T(8,128)S(1)}, u32[]{:S(2)}, u32[]{:S(2)}) collective-permute-start(f32[256,128]{1,0:T(8,128)S(1)} %forward.11), channel_id=1, source_target_pairs={{0,1},{1,0},{2,3},{3,2},{4,5},{5,4},{6,7},{7,6},{8,9},{9,8},{10,11... | collective-permute-start | bytes 393224 | tf_op jit(solution)/shard_map/ppermute | solution.py:416
  50.0 1.3 %collective-permute-start.18 = (bf16[256,128]{1,0:T(8,128)(2,1)S(1)}, bf16[256,128]{1,0:T(8,128)(2,1)S(1)}, u32[]{:S(2)}, u32[]{:S(2)}) collective-permute-start(bf16[256,128]{1,0:T(8,128)(2,1)S(1)} %residual.3.refs_0_), channel_id=1, source_target_pairs={{0,1},{1,0},{2,3},{3,2},{4,5},{5,4},{6,7},{7,6},{8,9},{9,8},{10,11... | collective-permute-start | bytes 196616 | tf_op jit(solution)/shard_map/ppermute | solution.py:416
  52.5 4.8 %collective-permute-start.20 = (bf16[256,128]{1,0:T(8,128)(2,1)S(1)}, bf16[256,128]{1,0:T(8,128)(2,1)S(1)}, u32[]{:S(2)}, u32[]{:S(2)}) collective-permute-start(bf16[256,128]{1,0:T(8,128)(2,1)S(1)} %get-tuple-element.67), channel_id=1, source_target_pairs={{0,2},{1,3},{2,0},{3,1},{4,6},{5,7},{6,4},{7,5},{8,10},{9,11},{10,... | collective-permute-start | bytes 196616 | tf_op jit(solution)/shard_map/ppermute | solution.py:416
  53.7 7.4 %collective-permute-start.19 = (bf16[256,128]{1,0:T(8,128)(2,1)S(1)}, bf16[256,128]{1,0:T(8,128)(2,1)S(1)}, u32[]{:S(2)}, u32[]{:S(2)}) collective-permute-start(bf16[256,128]{1,0:T(8,128)(2,1)S(1)} %get-tuple-element.65), channel_id=1, source_target_pairs={{0,2},{1,3},{2,0},{3,1},{4,6},{5,7},{6,4},{7,5},{8,10},{9,11},{10,... | collective-permute-start | bytes 196616 | tf_op jit(solution)/shard_map/ppermute | solution.py:416
  57.3 4.9 %collective-permute-start.21 = (bf16[128,128]{1,0:T(8,128)(2,1)S(1)}, bf16[128,128]{1,0:T(8,128)(2,1)S(1)}, u32[]{:S(2)}, u32[]{:S(2)}) collective-permute-start(bf16[128,128]{1,0:T(8,128)(2,1)S(1)} %get-tuple-element.68), channel_id=1, source_target_pairs={{0,8},{1,9},{2,10},{3,11},{4,12},{5,13},{6,14},{7,15},{8,0},{9,1},... | collective-permute-start | bytes 98312 | tf_op jit(solution)/shard_map/ppermute | solution.py:416
  59.9 5.7 %collective-permute-start.22 = (bf16[128,128]{1,0:T(8,128)(2,1)S(1)}, bf16[128,128]{1,0:T(8,128)(2,1)S(1)}, u32[]{:S(2)}, u32[]{:S(2)}) collective-permute-start(bf16[128,128]{1,0:T(8,128)(2,1)S(1)} %get-tuple-element.69), channel_id=1, source_target_pairs={{0,12},{1,13},{2,14},{3,15},{4,8},{5,9},{6,10},{7,11},{8,4},{9,5},... | collective-permute-start | bytes 98312 | tf_op jit(solution)/shard_map/ppermute | solution.py:416
  61.1 4.5 %collective-permute-start.23 = (bf16[128,128]{1,0:T(8,128)(2,1)S(1)}, bf16[128,128]{1,0:T(8,128)(2,1)S(1)}, u32[]{:S(2)}, u32[]{:S(2)}) collective-permute-start(bf16[128,128]{1,0:T(8,128)(2,1)S(1)} %get-tuple-element.70), channel_id=1, source_target_pairs={{0,4},{1,5},{2,6},{3,7},{4,0},{5,1},{6,2},{7,3},{8,12},{9,13},{10,... | collective-permute-start | bytes 98312 | tf_op jit(solution)/shard_map/ppermute | solution.py:416

commit v12 on v11

--- a/solution.py
+++ b/solution.py
@@ -501,11 +501,12 @@
     for sweep in range(ITERS):
         last = sweep + 1 == ITERS
         if paired:
-            over_2, over_3, over_1 = [
-                exchange(payload, n_slab, distance) for distance in (8, 12, 4)]
-            z_half = join(payload, over_2)
+            over_2 = exchange(payload, n_slab, 8)
+            over_1 = exchange(payload, n_slab, 4)
+            over_3 = exchange(over_2, n_slab, 4)
+            z_half = join(payload, over_1)
             y_half = exchange(z_half, n_slab, 2)
-            z_rest = join(over_3, over_1)
+            z_rest = join(over_2, over_3)
             y_rest = exchange(z_rest, n_slab, 2)
             along_z, along_y = (z_half, z_rest), (y_half, y_rest)
             if sweep == 0:
@@ -524,18 +525,20 @@
             other_residual = exchange(residual, n_slab, 1)
             y_sum = backward(own_list, [residual], 4, y_backward, F32)
             far_sum, near_sum = backward(
-                other_list, [other_residual], 4, y_backward, BF16, y_sum, ((1, 2), (0, 3)))
+                other_list, [other_residual], 4, y_backward, BF16, y_sum, ((2, 3), (0, 1)))
             far_part, near_part = exchange(far_sum, n_slab, 2), exchange(near_sum, n_slab, 2)
             z_sum = backward(z_list, [residual, other_residual], 4, z_backward, F32)
-            piece = shape((rows, extent), BF16)
-            piece_2, piece_3 = call(
-                functools.partial(combine_kernel, (1, 2)), "combine", 16, [VMEM] * 2,
-                [piece, piece], z_sum, far_part)
-            got = [exchange(piece_2, n_slab, 8), exchange(piece_3, n_slab, 12)]
+            whole, piece = shape((rows, extent), F32), shape((rows, extent), BF16)
+            sum_2, piece_3 = call(
+                functools.partial(combine_kernel, (2, 3)), "combine", 16, [VMEM] * 2,
+                [whole, piece], z_sum, far_part)
+            piece_2 = call(
+                functools.partial(combine_kernel, (0,)), "combine", 16, [VMEM] * 2,
+                [piece], sum_2, exchange(piece_3, n_slab, 4))[0]
             own_piece, piece_1 = call(
-                functools.partial(combine_kernel, (0, 3)), "combine", 16, [VMEM] * 2,
-                [shape((rows, extent), F32), piece], z_sum, near_part)
-            pieces = [own_piece, *got, exchange(piece_1, n_slab, 4)]
+                functools.partial(combine_kernel, (0, 1)), "combine", 16, [VMEM] * 2,
+                [whole, piece], z_sum, near_part)
+            pieces = [own_piece, exchange(piece_2, n_slab, 8), exchange(piece_1, n_slab, 4)]
         else:
             everyone = lax.all_gather(payload, "slab", axis=0, tiled=True)
             if sweep == 0:

time: 66.1 us -> 70.3 us (1.064)
  starting transfers between devices: 28.8 us -> 38.9 us
  Pallas kernels: 23.1 us -> 19.5 us
  waiting for transfers between devices: 14 us -> 11.6 us
    ppermute x24, starting transfers between devices: 28.8 us -> 38.9 us  [exchange(): lax.ppermute(values, 'slab', [(device, device ^ distance) for device in r...]
    pallas_call x28 -> x30, Pallas kernels: 23.1 us -> 19.5 us  [call(): pl.pallas_call(kernel, out_shape=out_shape, in_specs=in_specs, out_specs=...]
    ppermute x24, waiting for transfers between devices: 14 us -> 11.6 us  [exchange(): lax.ppermute(values, 'slab', [(device, device ^ distance) for device in r...]
  transfers between devices with their start and end apart: 24 -> 24, of which waited for: 14 -> 11; matrix products, arithmetic and copies ran while one was open for 0% -> 0% of each run, Pallas kernels for 23% -> 19%
where the time goes in v12:
time: 70.3 us
  starting transfers between devices  38.9 us (55%)
  Pallas kernels  19.5 us (28%)
  waiting for transfers between devices  11.6 us (17%)
    ppermute x24, starting transfers between devices, exchange(): lax.ppermute(values, 'slab', [(device, device ^ distance) for device in r...  38.9 us
    pallas_call x30, Pallas kernels, call(): pl.pallas_call(kernel, out_shape=out_shape, in_specs=in_specs, out_specs=...  19.5 us
    ppermute x24, waiting for transfers between devices, exchange(): lax.ppermute(values, 'slab', [(device, device ^ distance) for device in r...  11.6 us
  transfers between devices with their start and end apart: 24, of which 11 were waited for; matrix products, arithmetic and copies ran while one was open for 0% of the time, Pallas kernels for 19%

profile of v12, /device:TPU:0, one launch (start us, length us, event | category | flops | bytes accessed | tf_op | source)
XLA Modules:
  0.0 70.3 jit_solution(18338521600424412435)
XLA Ops:
  0.0 1.0 %pack.1.refs_0_ = bf16[192,128]{1,0:T(8,128)(2,1)S(1)} custom-call(f32[128,128]{1,0:T(8,128)} %bitcast.10, f32[4,256]{1,0:T(4,128)} %bitcast.12, f32[4,256]{1,0:T(4,128)} %bitcast.14, s32[4,256]{1,0:T(4,128)} %bitcast.16, s32[1,256]{1,0:T(1,128)} %bitcast.20, s32[1,16]{1,0:T(1,128)} %bitcast.18), custom_call_target="tpu_custom_call" | custom-call | tf_op jit(solution)/shard_map/pack/pallas_call | solution.py:403
  1.0 4.1 %collective-permute-start.1 = (bf16[192,128]{1,0:T(8,128)(2,1)S(1)}, bf16[192,128]{1,0:T(8,128)(2,1)S(1)}, u32[]{:S(2)}, u32[]{:S(2)}) collective-permute-start(bf16[192,128]{1,0:T(8,128)(2,1)S(1)} %pack.1.refs_0_), channel_id=1, source_target_pairs={{0,8},{1,9},{2,10},{3,11},{4,12},{5,13},{6,14},{7,15},{8,0},{9,1},... | collective-permute-start | bytes 147464 | tf_op jit(solution)/shard_map/ppermute | solution.py:416
  5.2 1.6 %collective-permute-start = (bf16[192,128]{1,0:T(8,128)(2,1)S(1)}, bf16[192,128]{1,0:T(8,128)(2,1)S(1)}, u32[]{:S(2)}, u32[]{:S(2)}) collective-permute-start(bf16[192,128]{1,0:T(8,128)(2,1)S(1)} %pack.1.refs_0_), channel_id=1, source_target_pairs={{0,4},{1,5},{2,6},{3,7},{4,0},{5,1},{6,2},{7,3},{8,12},{9,13},{10,... | collective-permute-start | bytes 147464 | tf_op jit(solution)/shard_map/ppermute | solution.py:416
  6.7 1.1 %collective-permute-done.1.refs_0_ = bf16[192,128]{1,0:T(8,128)(2,1)S(1)} collective-permute-done((bf16[192,128]{1,0:T(8,128)(2,1)S(1)}, bf16[192,128]{1,0:T(8,128)(2,1)S(1)}, u32[]{:S(2)}, u32[]{:S(2)}) %collective-permute-start.1) | collective-permute-done | bytes 49184 | tf_op jit(solution)/shard_map/ppermute | solution.py:416
  7.9 1.3 %collective-permute-start.2 = (bf16[192,128]{1,0:T(8,128)(2,1)S(1)}, bf16[192,128]{1,0:T(8,128)(2,1)S(1)}, u32[]{:S(2)}, u32[]{:S(2)}) collective-permute-start(bf16[192,128]{1,0:T(8,128)(2,1)S(1)} %collective-permute-done.1.refs_0_), channel_id=1, source_target_pairs={{0,4},{1,5},{2,6},{3,7},{4,0},{5,1},{6,2},{7,3},{8,12},{9,13},{10,... | collective-permute-start | bytes 147464 | tf_op jit(solution)/shard_map/ppermute | solution.py:416
  9.7 1.5 %collective-permute-start.3 = (bf16[384,128]{1,0:T(8,128)(2,1)S(1)}, bf16[384,128]{1,0:T(8,128)(2,1)S(1)}, u32[]{:S(2)}, u32[]{:S(2)}) collective-permute-start(bf16[384,128]{1,0:T(8,128)(2,1)S(1)} %join.4.refs_0_), channel_id=1, source_target_pairs={{0,2},{1,3},{2,0},{3,1},{4,6},{5,7},{6,4},{7,5},{8,10},{9,11},{10,... | collective-permute-start | bytes 294920 | tf_op jit(solution)/shard_map/ppermute | solution.py:416
  12.0 1.8 %collective-permute-start.4 = (bf16[384,128]{1,0:T(8,128)(2,1)S(1)}, bf16[384,128]{1,0:T(8,128)(2,1)S(1)}, u32[]{:S(2)}, u32[]{:S(2)}) collective-permute-start(bf16[384,128]{1,0:T(8,128)(2,1)S(1)} %join.5.refs_1_), channel_id=1, source_target_pairs={{0,2},{1,3},{2,0},{3,1},{4,6},{5,7},{6,4},{7,5},{8,10},{9,11},{10,... | collective-permute-start | bytes 294920 | tf_op jit(solution)/shard_map/ppermute | solution.py:416
  13.7 1.5 %setup.2 = (s32[8,128]{1,0:T(8,128)S(4)}, f32[64,128]{1,0:T(8,128)S(1)}, s32[544,128]{1,0:T(8,128)S(1)}, f32[544,128]{1,0:T(8,128)S(1)}, f32[544,128]{1,0:T(8,12...) custom-call(bf16[384,128]{1,0:T(8,128)(2,1)S(1)} %join.4.refs_0_, ...), custom_call_target="tpu_custom_call" | custom-call | tf_op jit(solution)/shard_map/setup/pallas_call | solution.py:403
  15.2 1.8 %forward.6.refs_2_.refs_6_ = f32[512,128]{1,0:T(8,128)S(1)} custom-call(s32[8,128]{1,0:T(8,128)S(4)} %get-tuple-element.38.slots, bf16[384,128]{1,0:T(8,128)(2,1)S(1)} %join.4.refs_0_, bf16[384,128]{1,0:T(8,128)(2,1)S(1)} %join.5.refs_1_, s32[544,128]{1,0:T(8,128)S(1)} %get-tuple-element.39.refs_2_, f32[544,128]{1,0:T(8,128)S(1)} %get-tuple-element.40.refs_3_, ...), custom_call_target="tpu_custom_call" | custom-call | tf_op jit(solution)/shard_map/forward/pallas_call | solution.py:403
  17.0 1.6 %setup.3 = (s32[8,128]{1,0:T(8,128)S(4)}, s32[8,128]{1,0:T(8,128)S(4)}, f32[64,128]{1,0:T(8,128)S(1)}, s32[544,128]{1,0:T(8,128)S(1)}, f32[544,128]{1,0:T(8,128)...) custom-call(bf16[384,128]{1,0:T(8,128)(2,1)S(1)} %collective-permute, ...), custom_call_target="tpu_custom_call" | custom-call | tf_op jit(solution)/shard_map/setup/pallas_call | solution.py:403
  19.4 1.3 %forward.7.projection_ref = f32[256,128]{1,0:T(8,128)S(1)} custom-call(s32[8,128]{1,0:T(8,128)S(4)} %get-tuple-element.43.slots, bf16[384,128]{1,0:T(8,128)(2,1)S(1)} %collective-permute-done.3.refs_0_, bf16[384,128]{1,0:T(8,128)(2,1)S(1)} %collective-permute-done.4.refs_1_, s32[544,128]{1,0:T(8,128)S(1)} %get-tuple-element.44.refs_2_, ...), custom_call_target="tpu_custom_call" | custom-call | tf_op jit(solution)/shard_map/forward/pallas_call | solution.py:403
  21.3 1.1 %backward.7.refs_4_ = f32[512,128]{1,0:T(8,128)S(1)} custom-call(s32[8,128]{1,0:T(8,128)S(4)} %get-tuple-element.43.slots, bf16[256,128]{1,0:T(8,128)(2,1)S(1)} %residual.2.refs_0_, s32[544,128]{1,0:T(8,128)S(1)} %get-tuple-element.54.refs_1_, f32[544,128]{1,0:T(8,128)S(1)} %get-tuple-element.55.refs_2_, f32[544,128]{1,0:T(8,128)S(1)} %get-tuple-element.56.refs_3_), custom_call_target="tpu_custom_call" | custom-call | tf_op jit(solution)/shard_map/backward/pallas_call | solution.py:403
  23.1 2.3 %collective-permute-start.8 = (bf16[256,128]{1,0:T(8,128)(2,1)S(1)}, bf16[256,128]{1,0:T(8,128)(2,1)S(1)}, u32[]{:S(2)}, u32[]{:S(2)}) collective-permute-start(bf16[256,128]{1,0:T(8,128)(2,1)S(1)} %get-tuple-element.59), channel_id=1, source_target_pairs={{0,2},{1,3},{2,0},{3,1},{4,6},{5,7},{6,4},{7,5},{8,10},{9,11},{10,... | collective-permute-start | bytes 196616 | tf_op jit(solution)/shard_map/ppermute | solution.py:416
  25.5 1.5 %backward.6.sum_ref = f32[512,128]{1,0:T(8,128)S(1)} custom-call(s32[8,128]{1,0:T(8,128)S(4)} %get-tuple-element.38.slots, bf16[256,128]{1,0:T(8,128)(2,1)S(1)} %residual.2.refs_0_, bf16[256,128]{1,0:T(8,128)(2,1)S(1)} %collective-permute-done.6.refs_1_.refs_0_, s32[544,128]{1,0:T(8,128)S(1)} %get-tuple-element.51.refs_2_, ...), custom_call_target="tpu_custom_call" | custom-call | tf_op jit(solution)/shard_map/backward/pallas_call | solution.py:403
  27.7 2.0 %collective-permute-start.9 = (bf16[128,128]{1,0:T(8,128)(2,1)S(1)}, bf16[128,128]{1,0:T(8,128)(2,1)S(1)}, u32[]{:S(2)}, u32[]{:S(2)}) collective-permute-start(bf16[128,128]{1,0:T(8,128)(2,1)S(1)} %get-tuple-element.61), channel_id=1, source_target_pairs={{0,4},{1,5},{2,6},{3,7},{4,0},{5,1},{6,2},{7,3},{8,12},{9,13},{10,... | collective-permute-start | bytes 98312 | tf_op jit(solution)/shard_map/ppermute | solution.py:416
  31.8 3.8 %collective-permute-start.10 = (bf16[128,128]{1,0:T(8,128)(2,1)S(1)}, bf16[128,128]{1,0:T(8,128)(2,1)S(1)}, u32[]{:S(2)}, u32[]{:S(2)}) collective-permute-start(bf16[128,128]{1,0:T(8,128)(2,1)S(1)} %combine.8), channel_id=1, source_target_pairs={{0,8},{1,9},{2,10},{3,11},{4,12},{5,13},{6,14},{7,15},{8,0},{9,1},... | collective-permute-start | bytes 98312 | tf_op jit(solution)/shard_map/ppermute | solution.py:416
  36.2 1.3 %collective-permute-done.10.refs_1_ = bf16[128,128]{1,0:T(8,128)(2,1)S(1)} collective-permute-done((bf16[128,128]{1,0:T(8,128)(2,1)S(1)}, bf16[128,128]{1,0:T(8,128)(2,1)S(1)}, u32[]{:S(2)}, u32[]{:S(2)}) %collective-permute-start.10) | collective-permute-done | bytes 32800 | tf_op jit(solution)/shard_map/ppermute | solution.py:416
  37.5 3.0 %collective-permute-start.14 = (bf16[128,128]{1,0:T(8,128)(2,1)S(1)}, bf16[128,128]{1,0:T(8,128)(2,1)S(1)}, u32[]{:S(2)}, u32[]{:S(2)}) collective-permute-start(bf16[128,128]{1,0:T(8,128)(2,1)S(1)} %get-tuple-element.64.refs_0_), channel_id=1, source_target_pairs={{0,8},{1,9},{2,10},{3,11},{4,12},{5,13},{6,14},{7,15},{8,0},{9,1},... | collective-permute-start | bytes 98312 | tf_op jit(solution)/shard_map/ppermute | solution.py:416
  40.5 2.1 %collective-permute-start.12 = (bf16[128,128]{1,0:T(8,128)(2,1)S(1)}, bf16[128,128]{1,0:T(8,128)(2,1)S(1)}, u32[]{:S(2)}, u32[]{:S(2)}) collective-permute-start(bf16[128,128]{1,0:T(8,128)(2,1)S(1)} %get-tuple-element.64.refs_0_), channel_id=1, source_target_pairs={{0,4},{1,5},{2,6},{3,7},{4,0},{5,1},{6,2},{7,3},{8,12},{9,13},{10,... | collective-permute-start | bytes 98312 | tf_op jit(solution)/shard_map/ppermute | solution.py:416
  42.6 1.9 %collective-permute-start.15 = (bf16[128,128]{1,0:T(8,128)(2,1)S(1)}, bf16[128,128]{1,0:T(8,128)(2,1)S(1)}, u32[]{:S(2)}, u32[]{:S(2)}) collective-permute-start(bf16[128,128]{1,0:T(8,128)(2,1)S(1)} %collective-permute-done.14.refs_0_), channel_id=1, source_target_pairs={{0,4},{1,5},{2,6},{3,7},{4,0},{5,1},{6,2},{7,3},{8,12},{9,13},{10,... | collective-permute-start | bytes 98312 | tf_op jit(solution)/shard_map/ppermute | solution.py:416
  44.5 1.1 %collective-permute-start.13 = (bf16[256,128]{1,0:T(8,128)(2,1)S(1)}, bf16[256,128]{1,0:T(8,128)(2,1)S(1)}, u32[]{:S(2)}, u32[]{:S(2)}) collective-permute-start(bf16[256,128]{1,0:T(8,128)(2,1)S(1)} %join.6.refs_0_), channel_id=1, source_target_pairs={{0,2},{1,3},{2,0},{3,1},{4,6},{5,7},{6,4},{7,5},{8,10},{9,11},{10,... | collective-permute-start | bytes 196616 | tf_op jit(solution)/shard_map/ppermute | solution.py:416
  46.5 1.3 %collective-permute-start.16 = (bf16[256,128]{1,0:T(8,128)(2,1)S(1)}, bf16[256,128]{1,0:T(8,128)(2,1)S(1)}, u32[]{:S(2)}, u32[]{:S(2)}) collective-permute-start(bf16[256,128]{1,0:T(8,128)(2,1)S(1)} %join.7.refs_1_), channel_id=1, source_target_pairs={{0,2},{1,3},{2,0},{3,1},{4,6},{5,7},{6,4},{7,5},{8,10},{9,11},{10,... | collective-permute-start | bytes 196616 | tf_op jit(solution)/shard_map/ppermute | solution.py:416
  47.8 1.8 %forward.9.refs_6_ = f32[512,128]{1,0:T(8,128)S(1)} custom-call(s32[8,128]{1,0:T(8,128)S(4)} %get-tuple-element.38.slots, bf16[256,128]{1,0:T(8,128)(2,1)S(1)} %join.6.refs_0_, bf16[256,128]{1,0:T(8,128)(2,1)S(1)} %join.7.refs_1_, s32[544,128]{1,0:T(8,128)S(1)} %get-tuple-element.39.refs_2_, f32[544,128]{1,0:T(8,128)S(1)} %get-tuple-element.40.refs_3_, ...), custom_call_target="tpu_custom_call" | custom-call | tf_op jit(solution)/shard_map/forward/pallas_call | solution.py:403
  49.6 1.2 %collective-permute-done.16.refs_1_ = bf16[256,128]{1,0:T(8,128)(2,1)S(1)} collective-permute-done((bf16[256,128]{1,0:T(8,128)(2,1)S(1)}, bf16[256,128]{1,0:T(8,128)(2,1)S(1)}, u32[]{:S(2)}, u32[]{:S(2)}) %collective-permute-start.16) | collective-permute-done | bytes 65568 | tf_op jit(solution)/shard_map/ppermute | solution.py:416
  51.5 1.3 %forward.10.projection_ref = f32[256,128]{1,0:T(8,128)S(1)} custom-call(s32[8,128]{1,0:T(8,128)S(4)} %get-tuple-element.43.slots, bf16[256,128]{1,0:T(8,128)(2,1)S(1)} %collective-permute-done.13.refs_0_, bf16[256,128]{1,0:T(8,128)(2,1)S(1)} %collective-permute-done.16.refs_1_, s32[544,128]{1,0:T(8,128)S(1)} %get-tuple-element.44.refs_2_, ...), custom_call_target="tpu_custom_call" | custom-call | tf_op jit(solution)/shard_map/forward/pallas_call | solution.py:403
  53.5 1.1 %backward.10.refs_4_ = f32[512,128]{1,0:T(8,128)S(1)} custom-call(s32[8,128]{1,0:T(8,128)S(4)} %get-tuple-element.43.slots, bf16[256,128]{1,0:T(8,128)(2,1)S(1)} %residual.3.refs_0_, s32[544,128]{1,0:T(8,128)S(1)} %get-tuple-element.54.refs_1_, f32[544,128]{1,0:T(8,128)S(1)} %get-tuple-element.55.refs_2_, f32[544,128]{1,0:T(8,128)S(1)} %get-tuple-element.56.refs_3_), custom_call_target="tpu_custom_call" | custom-call | tf_op jit(solution)/shard_map/backward/pallas_call | solution.py:403
  55.2 2.3 %collective-permute-start.20 = (bf16[256,128]{1,0:T(8,128)(2,1)S(1)}, bf16[256,128]{1,0:T(8,128)(2,1)S(1)}, u32[]{:S(2)}, u32[]{:S(2)}) collective-permute-start(bf16[256,128]{1,0:T(8,128)(2,1)S(1)} %get-tuple-element.67), channel_id=1, source_target_pairs={{0,2},{1,3},{2,0},{3,1},{4,6},{5,7},{6,4},{7,5},{8,10},{9,11},{10,... | collective-permute-start | bytes 196616 | tf_op jit(solution)/shard_map/ppermute | solution.py:416
  57.6 1.5 %backward.9.sum_ref = f32[512,128]{1,0:T(8,128)S(1)} custom-call(s32[8,128]{1,0:T(8,128)S(4)} %get-tuple-element.38.slots, bf16[256,128]{1,0:T(8,128)(2,1)S(1)} %residual.3.refs_0_, bf16[256,128]{1,0:T(8,128)(2,1)S(1)} %collective-permute-done.18.refs_1_.refs_0_, s32[544,128]{1,0:T(8,128)S(1)} %get-tuple-element.51.refs_2_, ...), custom_call_target="tpu_custom_call" | custom-call | tf_op jit(solution)/shard_map/backward/pallas_call | solution.py:403
  59.8 3.1 %collective-permute-start.21 = (bf16[128,128]{1,0:T(8,128)(2,1)S(1)}, bf16[128,128]{1,0:T(8,128)(2,1)S(1)}, u32[]{:S(2)}, u32[]{:S(2)}) collective-permute-start(bf16[128,128]{1,0:T(8,128)(2,1)S(1)} %get-tuple-element.69), channel_id=1, source_target_pairs={{0,4},{1,5},{2,6},{3,7},{4,0},{5,1},{6,2},{7,3},{8,12},{9,13},{10,... | collective-permute-start | bytes 98312 | tf_op jit(solution)/shard_map/ppermute | solution.py:416
  63.7 1.1 %collective-permute-done.21.y_ref = bf16[128,128]{1,0:T(8,128)(2,1)S(1)} collective-permute-done((bf16[128,128]{1,0:T(8,128)(2,1)S(1)}, bf16[128,128]{1,0:T(8,128)(2,1)S(1)}, u32[]{:S(2)}, u32[]{:S(2)}) %collective-permute-start.21) | collective-permute-done | bytes 32800 | tf_op jit(solution)/shard_map/ppermute | solution.py:416
  64.8 2.6 %collective-permute-start.22 = (bf16[128,128]{1,0:T(8,128)(2,1)S(1)}, bf16[128,128]{1,0:T(8,128)(2,1)S(1)}, u32[]{:S(2)}, u32[]{:S(2)}) collective-permute-start(bf16[128,128]{1,0:T(8,128)(2,1)S(1)} %combine.11), channel_id=1, source_target_pairs={{0,8},{1,9},{2,10},{3,11},{4,12},{5,13},{6,14},{7,15},{8,0},{9,1},... | collective-permute-start | bytes 98312 | tf_op jit(solution)/shard_map/ppermute | solution.py:416
  67.4 2.3 %collective-permute-done.22.refs_1_ = bf16[128,128]{1,0:T(8,128)(2,1)S(1)} collective-permute-done((bf16[128,128]{1,0:T(8,128)(2,1)S(1)}, bf16[128,128]{1,0:T(8,128)(2,1)S(1)}, u32[]{:S(2)}, u32[]{:S(2)}) %collective-permute-start.22) | collective-permute-done | bytes 32800 | tf_op jit(solution)/shard_map/ppermute | solution.py:416
  (58 shorter events, 11.9 us)
Async XLA Ops:
  1.0 6.8 %collective-permute-start.1 = (bf16[192,128]{1,0:T(8,128)(2,1)S(1)}, bf16[192,128]{1,0:T(8,128)(2,1)S(1)}, u32[]{:S(2)}, u32[]{:S(2)}) collective-permute-start(bf16[192,128]{1,0:T(8,128)(2,1)S(1)} %pack.1.refs_0_), channel_id=1, source_target_pairs={{0,8},{1,9},{2,10},{3,11},{4,12},{5,13},{6,14},{7,15},{8,0},{9,1},... | collective-permute-start | bytes 147464 | tf_op jit(solution)/shard_map/ppermute | solution.py:416
  5.2 4.6 %collective-permute-start = (bf16[192,128]{1,0:T(8,128)(2,1)S(1)}, bf16[192,128]{1,0:T(8,128)(2,1)S(1)}, u32[]{:S(2)}, u32[]{:S(2)}) collective-permute-start(bf16[192,128]{1,0:T(8,128)(2,1)S(1)} %pack.1.refs_0_), channel_id=1, source_target_pairs={{0,4},{1,5},{2,6},{3,7},{4,0},{5,1},{6,2},{7,3},{8,12},{9,13},{10,... | collective-permute-start | bytes 147464 | tf_op jit(solution)/shard_map/ppermute | solution.py:416
  7.9 4.1 %collective-permute-start.2 = (bf16[192,128]{1,0:T(8,128)(2,1)S(1)}, bf16[192,128]{1,0:T(8,128)(2,1)S(1)}, u32[]{:S(2)}, u32[]{:S(2)}) collective-permute-start(bf16[192,128]{1,0:T(8,128)(2,1)S(1)} %collective-permute-done.1.refs_0_), channel_id=1, source_target_pairs={{0,4},{1,5},{2,6},{3,7},{4,0},{5,1},{6,2},{7,3},{8,12},{9,13},{10,... | collective-permute-start | bytes 147464 | tf_op jit(solution)/shard_map/ppermute | solution.py:416
  9.7 7.3 %collective-permute-start.3 = (bf16[384,128]{1,0:T(8,128)(2,1)S(1)}, bf16[384,128]{1,0:T(8,128)(2,1)S(1)}, u32[]{:S(2)}, u32[]{:S(2)}) collective-permute-start(bf16[384,128]{1,0:T(8,128)(2,1)S(1)} %join.4.refs_0_), channel_id=1, source_target_pairs={{0,2},{1,3},{2,0},{3,1},{4,6},{5,7},{6,4},{7,5},{8,10},{9,11},{10,... | collective-permute-start | bytes 294920 | tf_op jit(solution)/shard_map/ppermute | solution.py:416
  12.0 5.1 %collective-permute-start.4 = (bf16[384,128]{1,0:T(8,128)(2,1)S(1)}, bf16[384,128]{1,0:T(8,128)(2,1)S(1)}, u32[]{:S(2)}, u32[]{:S(2)}) collective-permute-start(bf16[384,128]{1,0:T(8,128)(2,1)S(1)} %join.5.refs_1_), channel_id=1, source_target_pairs={{0,2},{1,3},{2,0},{3,1},{4,6},{5,7},{6,4},{7,5},{8,10},{9,11},{10,... | collective-permute-start | bytes 294920 | tf_op jit(solution)/shard_map/ppermute | solution.py:416
  19.3 1.4 %collective-permute-start.5 = (f32[288,128]{1,0:T(8,128)S(1)}, f32[288,128]{1,0:T(8,128)S(1)}, u32[]{:S(2)}, u32[]{:S(2)}) collective-permute-start(f32[288,128]{1,0:T(8,128)S(1)} %forward.8), channel_id=1, source_target_pairs={{0,1},{1,0},{2,3},{3,2},{4,5},{5,4},{6,7},{7,6},{8,9},{9,8},{10,11... | collective-permute-start | bytes 442376 | tf_op jit(solution)/shard_map/ppermute | solution.py:416
  19.4 1.4 %copy-start = (bf16[32,8,128]{2,1,0:T(8,128)(2,1)S(1)}, bf16[32,8,128]{2,1,0:T(8,128)(2,1)}, u32[]{:S(2)}) copy-start(bf16[32,8,128]{2,1,0:T(8,128)(2,1)} %param.7) | copy-start | bytes 196612
  20.8 1.7 %collective-permute-start.6 = (bf16[256,128]{1,0:T(8,128)(2,1)S(1)}, bf16[256,128]{1,0:T(8,128)(2,1)S(1)}, u32[]{:S(2)}, u32[]{:S(2)}) collective-permute-start(bf16[256,128]{1,0:T(8,128)(2,1)S(1)} %residual.2.refs_0_), channel_id=1, source_target_pairs={{0,1},{1,0},{2,3},{3,2},{4,5},{5,4},{6,7},{7,6},{8,9},{9,8},{10,11... | collective-permute-start | bytes 196616 | tf_op jit(solution)/shard_map/ppermute | solution.py:416
  23.1 4.6 %collective-permute-start.8 = (bf16[256,128]{1,0:T(8,128)(2,1)S(1)}, bf16[256,128]{1,0:T(8,128)(2,1)S(1)}, u32[]{:S(2)}, u32[]{:S(2)}) collective-permute-start(bf16[256,128]{1,0:T(8,128)(2,1)S(1)} %get-tuple-element.59), channel_id=1, source_target_pairs={{0,2},{1,3},{2,0},{3,1},{4,6},{5,7},{6,4},{7,5},{8,10},{9,11},{10,... | collective-permute-start | bytes 196616 | tf_op jit(solution)/shard_map/ppermute | solution.py:416
  25.4 4.3 %collective-permute-start.7 = (bf16[256,128]{1,0:T(8,128)(2,1)S(1)}, bf16[256,128]{1,0:T(8,128)(2,1)S(1)}, u32[]{:S(2)}, u32[]{:S(2)}) collective-permute-start(bf16[256,128]{1,0:T(8,128)(2,1)S(1)} %get-tuple-element.57), channel_id=1, source_target_pairs={{0,2},{1,3},{2,0},{3,1},{4,6},{5,7},{6,4},{7,5},{8,10},{9,11},{10,... | collective-permute-start | bytes 196616 | tf_op jit(solution)/shard_map/ppermute | solution.py:416
  27.7 4.1 %collective-permute-start.9 = (bf16[128,128]{1,0:T(8,128)(2,1)S(1)}, bf16[128,128]{1,0:T(8,128)(2,1)S(1)}, u32[]{:S(2)}, u32[]{:S(2)}) collective-permute-start(bf16[128,128]{1,0:T(8,128)(2,1)S(1)} %get-tuple-element.61), channel_id=1, source_target_pairs={{0,4},{1,5},{2,6},{3,7},{4,0},{5,1},{6,2},{7,3},{8,12},{9,13},{10,... | collective-permute-start | bytes 98312 | tf_op jit(solution)/shard_map/ppermute | solution.py:416
  29.7 6.5 %collective-permute-start.11 = (bf16[128,128]{1,0:T(8,128)(2,1)S(1)}, bf16[128,128]{1,0:T(8,128)(2,1)S(1)}, u32[]{:S(2)}, u32[]{:S(2)}) collective-permute-start(bf16[128,128]{1,0:T(8,128)(2,1)S(1)} %get-tuple-element.62), channel_id=1, source_target_pairs={{0,4},{1,5},{2,6},{3,7},{4,0},{5,1},{6,2},{7,3},{8,12},{9,13},{10,... | collective-permute-start | bytes 98312 | tf_op jit(solution)/shard_map/ppermute | solution.py:416
  31.7 3.8 %copy-start.2 = (f32[256,4]{0,1:T(4,128)S(1)}, f32[256,4]{0,1:T(4,128)}, u32[]{:S(2)}) copy-start(f32[256,4]{0,1:T(4,128)} %param.13) | copy-start | bytes 12292
  31.7 3.8 %copy-start.3 = (f32[256,4]{0,1:T(4,128)S(1)}, f32[256,4]{0,1:T(4,128)}, u32[]{:S(2)}) copy-start(f32[256,4]{0,1:T(4,128)} %param.12) | copy-start | bytes 12292
  31.7 3.8 %copy-start.4 = (s32[256,4]{0,1:T(4,128)S(1)}, s32[256,4]{0,1:T(4,128)}, u32[]{:S(2)}) copy-start(s32[256,4]{0,1:T(4,128)} %param.9) | copy-start | bytes 12292
  31.7 3.8 %copy-start.5 = (s32[16]{0:T(128)S(1)}, s32[16]{0:T(128)}, u32[]{:S(2)}) copy-start(s32[16]{0:T(128)} %param.11) | copy-start | bytes 196
  31.8 5.7 %copy-start.1 = (f32[16,8,128]{2,1,0:T(8,128)S(1)}, f32[16,8,128]{2,1,0:T(8,128)}, u32[]{:S(2)}) copy-start(f32[16,8,128]{2,1,0:T(8,128)} %param.8) | copy-start | bytes 196612
  31.8 5.7 %collective-permute-start.10 = (bf16[128,128]{1,0:T(8,128)(2,1)S(1)}, bf16[128,128]{1,0:T(8,128)(2,1)S(1)}, u32[]{:S(2)}, u32[]{:S(2)}) collective-permute-start(bf16[128,128]{1,0:T(8,128)(2,1)S(1)} %combine.8), channel_id=1, source_target_pairs={{0,8},{1,9},{2,10},{3,11},{4,12},{5,13},{6,14},{7,15},{8,0},{9,1},... | collective-permute-start | bytes 98312 | tf_op jit(solution)/shard_map/ppermute | solution.py:416
  37.5 5.1 %collective-permute-start.14 = (bf16[128,128]{1,0:T(8,128)(2,1)S(1)}, bf16[128,128]{1,0:T(8,128)(2,1)S(1)}, u32[]{:S(2)}, u32[]{:S(2)}) collective-permute-start(bf16[128,128]{1,0:T(8,128)(2,1)S(1)} %get-tuple-element.64.refs_0_), channel_id=1, source_target_pairs={{0,8},{1,9},{2,10},{3,11},{4,12},{5,13},{6,14},{7,15},{8,0},{9,1},... | collective-permute-start | bytes 98312 | tf_op jit(solution)/shard_map/ppermute | solution.py:416
  40.5 4.0 %collective-permute-start.12 = (bf16[128,128]{1,0:T(8,128)(2,1)S(1)}, bf16[128,128]{1,0:T(8,128)(2,1)S(1)}, u32[]{:S(2)}, u32[]{:S(2)}) collective-permute-start(bf16[128,128]{1,0:T(8,128)(2,1)S(1)} %get-tuple-element.64.refs_0_), channel_id=1, source_target_pairs={{0,4},{1,5},{2,6},{3,7},{4,0},{5,1},{6,2},{7,3},{8,12},{9,13},{10,... | collective-permute-start | bytes 98312 | tf_op jit(solution)/shard_map/ppermute | solution.py:416
  42.6 3.9 %collective-permute-start.15 = (bf16[128,128]{1,0:T(8,128)(2,1)S(1)}, bf16[128,128]{1,0:T(8,128)(2,1)S(1)}, u32[]{:S(2)}, u32[]{:S(2)}) collective-permute-start(bf16[128,128]{1,0:T(8,128)(2,1)S(1)} %collective-permute-done.14.refs_0_), channel_id=1, source_target_pairs={{0,4},{1,5},{2,6},{3,7},{4,0},{5,1},{6,2},{7,3},{8,12},{9,13},{10,... | collective-permute-start | bytes 98312 | tf_op jit(solution)/shard_map/ppermute | solution.py:416
  44.5 5.1 %collective-permute-start.13 = (bf16[256,128]{1,0:T(8,128)(2,1)S(1)}, bf16[256,128]{1,0:T(8,128)(2,1)S(1)}, u32[]{:S(2)}, u32[]{:S(2)}) collective-permute-start(bf16[256,128]{1,0:T(8,128)(2,1)S(1)} %join.6.refs_0_), channel_id=1, source_target_pairs={{0,2},{1,3},{2,0},{3,1},{4,6},{5,7},{6,4},{7,5},{8,10},{9,11},{10,... | collective-permute-start | bytes 196616 | tf_op jit(solution)/shard_map/ppermute | solution.py:416
  46.5 4.3 %collective-permute-start.16 = (bf16[256,128]{1,0:T(8,128)(2,1)S(1)}, bf16[256,128]{1,0:T(8,128)(2,1)S(1)}, u32[]{:S(2)}, u32[]{:S(2)}) collective-permute-start(bf16[256,128]{1,0:T(8,128)(2,1)S(1)} %join.7.refs_1_), channel_id=1, source_target_pairs={{0,2},{1,3},{2,0},{3,1},{4,6},{5,7},{6,4},{7,5},{8,10},{9,11},{10,... | collective-permute-start | bytes 196616 | tf_op jit(solution)/shard_map/ppermute | solution.py:416
  51.5 1.4 %collective-permute-start.17 = (f32[256,128]{1,0:T(8,128)S(1)}, f32[256,128]{1,0:T(8,128)S(1)}, u32[]{:S(2)}, u32[]{:S(2)}) collective-permute-start(f32[256,128]{1,0:T(8,128)S(1)} %forward.11), channel_id=1, source_target_pairs={{0,1},{1,0},{2,3},{3,2},{4,5},{5,4},{6,7},{7,6},{8,9},{9,8},{10,11... | collective-permute-start | bytes 393224 | tf_op jit(solution)/shard_map/ppermute | solution.py:416
  52.9 1.7 %collective-permute-start.18 = (bf16[256,128]{1,0:T(8,128)(2,1)S(1)}, bf16[256,128]{1,0:T(8,128)(2,1)S(1)}, u32[]{:S(2)}, u32[]{:S(2)}) collective-permute-start(bf16[256,128]{1,0:T(8,128)(2,1)S(1)} %residual.3.refs_0_), channel_id=1, source_target_pairs={{0,1},{1,0},{2,3},{3,2},{4,5},{5,4},{6,7},{7,6},{8,9},{9,8},{10,11... | collective-permute-start | bytes 196616 | tf_op jit(solution)/shard_map/ppermute | solution.py:416
  55.2 4.6 %collective-permute-start.20 = (bf16[256,128]{1,0:T(8,128)(2,1)S(1)}, bf16[256,128]{1,0:T(8,128)(2,1)S(1)}, u32[]{:S(2)}, u32[]{:S(2)}) collective-permute-start(bf16[256,128]{1,0:T(8,128)(2,1)S(1)} %get-tuple-element.67), channel_id=1, source_target_pairs={{0,2},{1,3},{2,0},{3,1},{4,6},{5,7},{6,4},{7,5},{8,10},{9,11},{10,... | collective-permute-start | bytes 196616 | tf_op jit(solution)/shard_map/ppermute | solution.py:416
  57.5 5.3 %collective-permute-start.19 = (bf16[256,128]{1,0:T(8,128)(2,1)S(1)}, bf16[256,128]{1,0:T(8,128)(2,1)S(1)}, u32[]{:S(2)}, u32[]{:S(2)}) collective-permute-start(bf16[256,128]{1,0:T(8,128)(2,1)S(1)} %get-tuple-element.65), channel_id=1, source_target_pairs={{0,2},{1,3},{2,0},{3,1},{4,6},{5,7},{6,4},{7,5},{8,10},{9,11},{10,... | collective-permute-start | bytes 196616 | tf_op jit(solution)/shard_map/ppermute | solution.py:416
  59.8 5.0 %collective-permute-start.21 = (bf16[128,128]{1,0:T(8,128)(2,1)S(1)}, bf16[128,128]{1,0:T(8,128)(2,1)S(1)}, u32[]{:S(2)}, u32[]{:S(2)}) collective-permute-start(bf16[128,128]{1,0:T(8,128)(2,1)S(1)} %get-tuple-element.69), channel_id=1, source_target_pairs={{0,4},{1,5},{2,6},{3,7},{4,0},{5,1},{6,2},{7,3},{8,12},{9,13},{10,... | collective-permute-start | bytes 98312 | tf_op jit(solution)/shard_map/ppermute | solution.py:416
  62.9 4.5 %collective-permute-start.23 = (bf16[128,128]{1,0:T(8,128)(2,1)S(1)}, bf16[128,128]{1,0:T(8,128)(2,1)S(1)}, u32[]{:S(2)}, u32[]{:S(2)}) collective-permute-start(bf16[128,128]{1,0:T(8,128)(2,1)S(1)} %get-tuple-element.70), channel_id=1, source_target_pairs={{0,4},{1,5},{2,6},{3,7},{4,0},{5,1},{6,2},{7,3},{8,12},{9,13},{10,... | collective-permute-start | bytes 98312 | tf_op jit(solution)/shard_map/ppermute | solution.py:416
  64.8 4.9 %collective-permute-start.22 = (bf16[128,128]{1,0:T(8,128)(2,1)S(1)}, bf16[128,128]{1,0:T(8,128)(2,1)S(1)}, u32[]{:S(2)}, u32[]{:S(2)}) collective-permute-start(bf16[128,128]{1,0:T(8,128)(2,1)S(1)} %combine.11), channel_id=1, source_target_pairs={{0,8},{1,9},{2,10},{3,11},{4,12},{5,13},{6,14},{7,15},{8,0},{9,1},... | collective-permute-start | bytes 98312 | tf_op jit(solution)/shard_map/ppermute | solution.py:416

commit v13 on v11

--- a/solution.py
+++ b/solution.py
@@ -412,9 +412,10 @@
     )(*operands)
 
 
-def exchange(values, n_slab, distance):
+def exchange(values, n_slab, distance, odd_distance=None):
+    far = (distance, distance if odd_distance is None else odd_distance)
     return lax.ppermute(
-        values, "slab", [(device, device ^ distance) for device in range(n_slab)])
+        values, "slab", [(device, device ^ far[device % 2]) for device in range(n_slab)])
 
 
 def shards(sinogram, start_volume, slot_voxel, slot_ray, live_count, block_slope, block_offset):
@@ -501,11 +502,11 @@
     for sweep in range(ITERS):
         last = sweep + 1 == ITERS
         if paired:
-            over_2, over_3, over_1 = [
-                exchange(payload, n_slab, distance) for distance in (8, 12, 4)]
-            z_half = join(payload, over_2)
+            place_1, place_2, place_3 = [
+                exchange(payload, n_slab, *pair) for pair in ((8, 12), (12, 4), (4, 8))]
+            z_half = join(payload, place_1)
             y_half = exchange(z_half, n_slab, 2)
-            z_rest = join(over_3, over_1)
+            z_rest = join(place_2, place_3)
             y_rest = exchange(z_rest, n_slab, 2)
             along_z, along_y = (z_half, z_rest), (y_half, y_rest)
             if sweep == 0:
@@ -528,14 +529,14 @@
             far_part, near_part = exchange(far_sum, n_slab, 2), exchange(near_sum, n_slab, 2)
             z_sum = backward(z_list, [residual, other_residual], 4, z_backward, F32)
             piece = shape((rows, extent), BF16)
-            piece_2, piece_3 = call(
+            piece_1, piece_2 = call(
                 functools.partial(combine_kernel, (1, 2)), "combine", 16, [VMEM] * 2,
                 [piece, piece], z_sum, far_part)
-            got = [exchange(piece_2, n_slab, 8), exchange(piece_3, n_slab, 12)]
-            own_piece, piece_1 = call(
+            got = [exchange(piece_1, n_slab, 8, 12), exchange(piece_2, n_slab, 12, 4)]
+            own_piece, piece_3 = call(
                 functools.partial(combine_kernel, (0, 3)), "combine", 16, [VMEM] * 2,
                 [shape((rows, extent), F32), piece], z_sum, near_part)
-            pieces = [own_piece, *got, exchange(piece_1, n_slab, 4)]
+            pieces = [own_piece, *got, exchange(piece_3, n_slab, 4, 8)]
         else:
             everyone = lax.all_gather(payload, "slab", axis=0, tiled=True)
             if sweep == 0:

time: 66.1 us -> 65.4 us (0.989)
  starting transfers between devices: 28.8 us -> 29.8 us
  Pallas kernels: 23.1 us -> 22.4 us
  waiting for transfers between devices: 14 us -> 13.3 us
    ppermute x24, starting transfers between devices: 28.8 us -> 29.8 us  [exchange(): lax.ppermute(values, 'slab', [(device, device ^ far[device % 2]) for devi...]
    ppermute x24, waiting for transfers between devices: 14 us -> 13.3 us  [exchange(): lax.ppermute(values, 'slab', [(device, device ^ far[device % 2]) for devi...]
    pallas_call x28, Pallas kernels: 23.1 us -> 22.4 us  [call(): pl.pallas_call(kernel, out_shape=out_shape, in_specs=in_specs, out_specs=...]
  transfers between devices with their start and end apart: 24 -> 24, of which waited for: 14 -> 12; matrix products, arithmetic and copies ran while one was open for 0% -> 0% of each run, Pallas kernels for 23% -> 24%
where the time goes in v13:
time: 65.4 us; the launch traced here: 65.8 us
  starting transfers between devices  29.8 us (46%)
  Pallas kernels  22.4 us (34%)
  waiting for transfers between devices  13.3 us (20%)
    ppermute x24, starting transfers between devices, exchange(): lax.ppermute(values, 'slab', [(device, device ^ far[device % 2]) for devi...  29.8 us
    pallas_call x28, Pallas kernels, call(): pl.pallas_call(kernel, out_shape=out_shape, in_specs=in_specs, out_specs=...  22.4 us
    ppermute x24, waiting for transfers between devices, exchange(): lax.ppermute(values, 'slab', [(device, device ^ far[device % 2]) for devi...  13.3 us
  transfers between devices with their start and end apart: 24, of which 12 were waited for; matrix products, arithmetic and copies ran while one was open for 0% of the time, Pallas kernels for 24%

profile of v13, /device:TPU:0, one launch (start us, length us, event | category | flops | bytes accessed | tf_op | source)
XLA Modules:
  0.0 65.8 jit_solution(918783925640965324)
XLA Ops:
  0.0 1.0 %pack.1.refs_0_ = bf16[192,128]{1,0:T(8,128)(2,1)S(1)} custom-call(f32[128,128]{1,0:T(8,128)} %bitcast.10, f32[4,256]{1,0:T(4,128)} %bitcast.12, f32[4,256]{1,0:T(4,128)} %bitcast.14, s32[4,256]{1,0:T(4,128)} %bitcast.16, s32[1,256]{1,0:T(1,128)} %bitcast.20, s32[1,16]{1,0:T(1,128)} %bitcast.18), custom_call_target="tpu_custom_call" | custom-call | tf_op jit(solution)/shard_map/pack/pallas_call | solution.py:403
  1.0 5.1 %collective-permute-start.1 = (bf16[192,128]{1,0:T(8,128)(2,1)S(1)}, bf16[192,128]{1,0:T(8,128)(2,1)S(1)}, u32[]{:S(2)}, u32[]{:S(2)}) collective-permute-start(bf16[192,128]{1,0:T(8,128)(2,1)S(1)} %pack.1.refs_0_), channel_id=1, source_target_pairs={{0,12},{1,5},{2,14},{3,7},{4,8},{5,1},{6,10},{7,3},{8,4},{9,13},{1... | collective-permute-start | bytes 147464 | tf_op jit(solution)/shard_map/ppermute | solution.py:417
  6.8 1.9 %collective-permute-done.1.refs_0_ = bf16[192,128]{1,0:T(8,128)(2,1)S(1)} collective-permute-done((bf16[192,128]{1,0:T(8,128)(2,1)S(1)}, bf16[192,128]{1,0:T(8,128)(2,1)S(1)}, u32[]{:S(2)}, u32[]{:S(2)}) %collective-permute-start.1) | collective-permute-done | bytes 49184 | tf_op jit(solution)/shard_map/ppermute | solution.py:417
  8.7 1.6 %collective-permute-done.2.refs_1_ = bf16[192,128]{1,0:T(8,128)(2,1)S(1)} collective-permute-done((bf16[192,128]{1,0:T(8,128)(2,1)S(1)}, bf16[192,128]{1,0:T(8,128)(2,1)S(1)}, u32[]{:S(2)}, u32[]{:S(2)}) %collective-permute-start.2) | collective-permute-done | bytes 49184 | tf_op jit(solution)/shard_map/ppermute | solution.py:417
  10.3 1.6 %collective-permute-start.4 = (bf16[384,128]{1,0:T(8,128)(2,1)S(1)}, bf16[384,128]{1,0:T(8,128)(2,1)S(1)}, u32[]{:S(2)}, u32[]{:S(2)}) collective-permute-start(bf16[384,128]{1,0:T(8,128)(2,1)S(1)} %join.5.refs_1_), channel_id=1, source_target_pairs={{0,2},{1,3},{2,0},{3,1},{4,6},{5,7},{6,4},{7,5},{8,10},{9,11},{10,... | collective-permute-start | bytes 294920 | tf_op jit(solution)/shard_map/ppermute | solution.py:417
  11.9 1.2 %collective-permute-start.3 = (bf16[384,128]{1,0:T(8,128)(2,1)S(1)}, bf16[384,128]{1,0:T(8,128)(2,1)S(1)}, u32[]{:S(2)}, u32[]{:S(2)}) collective-permute-start(bf16[384,128]{1,0:T(8,128)(2,1)S(1)} %join.4.refs_0_), channel_id=1, source_target_pairs={{0,2},{1,3},{2,0},{3,1},{4,6},{5,7},{6,4},{7,5},{8,10},{9,11},{10,... | collective-permute-start | bytes 294920 | tf_op jit(solution)/shard_map/ppermute | solution.py:417
  13.0 1.5 %setup.2 = (s32[8,128]{1,0:T(8,128)S(4)}, f32[64,128]{1,0:T(8,128)S(1)}, s32[544,128]{1,0:T(8,128)S(1)}, f32[544,128]{1,0:T(8,128)S(1)}, f32[544,128]{1,0:T(8,12...) custom-call(bf16[384,128]{1,0:T(8,128)(2,1)S(1)} %join.4.refs_0_, ...), custom_call_target="tpu_custom_call" | custom-call | tf_op jit(solution)/shard_map/setup/pallas_call | solution.py:403
  14.5 2.4 %forward.6.refs_2_.refs_6_ = f32[512,128]{1,0:T(8,128)S(1)} custom-call(s32[8,128]{1,0:T(8,128)S(4)} %get-tuple-element.38.slots, bf16[384,128]{1,0:T(8,128)(2,1)S(1)} %join.4.refs_0_, bf16[384,128]{1,0:T(8,128)(2,1)S(1)} %join.5.refs_1_, s32[544,128]{1,0:T(8,128)S(1)} %get-tuple-element.39.refs_2_, f32[544,128]{1,0:T(8,128)S(1)} %get-tuple-element.40.refs_3_, ...), custom_call_target="tpu_custom_call" | custom-call | tf_op jit(solution)/shard_map/forward/pallas_call | solution.py:403
  16.9 1.6 %setup.3 = (s32[8,128]{1,0:T(8,128)S(4)}, s32[8,128]{1,0:T(8,128)S(4)}, f32[64,128]{1,0:T(8,128)S(1)}, s32[544,128]{1,0:T(8,128)S(1)}, f32[544,128]{1,0:T(8,128)...) custom-call(bf16[384,128]{1,0:T(8,128)(2,1)S(1)} %collective-permute, ...), custom_call_target="tpu_custom_call" | custom-call | tf_op jit(solution)/shard_map/setup/pallas_call | solution.py:403
  18.5 0.9 %forward.8 = f32[288,128]{1,0:T(8,128)S(1)} custom-call(s32[8,128]{1,0:T(8,128)S(4)} %get-tuple-element.50.slots, bf16[384,128]{1,0:T(8,128)(2,1)S(1)} %collective-permute-done.3.refs_0_, bf16[384,128]{1,0:T(8,128)(2,1)S(1)} %collective-permute-done.4.refs_1_, s32[544,128]{1,0:T(8,128)S(1)} %get-tuple-element.44.refs_2_, ...), custom_call_target="tpu_custom_call" | custom-call | tf_op jit(solution)/shard_map/forward/pallas_call | solution.py:403
  19.5 1.3 %forward.7.projection_ref = f32[256,128]{1,0:T(8,128)S(1)} custom-call(s32[8,128]{1,0:T(8,128)S(4)} %get-tuple-element.43.slots, bf16[384,128]{1,0:T(8,128)(2,1)S(1)} %collective-permute-done.3.refs_0_, bf16[384,128]{1,0:T(8,128)(2,1)S(1)} %collective-permute-done.4.refs_1_, s32[544,128]{1,0:T(8,128)S(1)} %get-tuple-element.44.refs_2_, ...), custom_call_target="tpu_custom_call" | custom-call | tf_op jit(solution)/shard_map/forward/pallas_call | solution.py:403
  21.5 1.1 %backward.7.refs_4_ = f32[512,128]{1,0:T(8,128)S(1)} custom-call(s32[8,128]{1,0:T(8,128)S(4)} %get-tuple-element.43.slots, bf16[256,128]{1,0:T(8,128)(2,1)S(1)} %residual.2.refs_0_, s32[544,128]{1,0:T(8,128)S(1)} %get-tuple-element.54.refs_1_, f32[544,128]{1,0:T(8,128)S(1)} %get-tuple-element.55.refs_2_, f32[544,128]{1,0:T(8,128)S(1)} %get-tuple-element.56.refs_3_), custom_call_target="tpu_custom_call" | custom-call | tf_op jit(solution)/shard_map/backward/pallas_call | solution.py:403
  23.4 1.2 %collective-permute-start.8 = (bf16[256,128]{1,0:T(8,128)(2,1)S(1)}, bf16[256,128]{1,0:T(8,128)(2,1)S(1)}, u32[]{:S(2)}, u32[]{:S(2)}) collective-permute-start(bf16[256,128]{1,0:T(8,128)(2,1)S(1)} %get-tuple-element.59), channel_id=1, source_target_pairs={{0,2},{1,3},{2,0},{3,1},{4,6},{5,7},{6,4},{7,5},{8,10},{9,11},{10,... | collective-permute-start | bytes 196616 | tf_op jit(solution)/shard_map/ppermute | solution.py:417
  25.5 1.9 %backward.6.sum_ref = f32[512,128]{1,0:T(8,128)S(1)} custom-call(s32[8,128]{1,0:T(8,128)S(4)} %get-tuple-element.38.slots, bf16[256,128]{1,0:T(8,128)(2,1)S(1)} %residual.2.refs_0_, bf16[256,128]{1,0:T(8,128)(2,1)S(1)} %collective-permute-done.6.refs_1_.refs_0_, s32[544,128]{1,0:T(8,128)S(1)} %get-tuple-element.51.refs_2_, ...), custom_call_target="tpu_custom_call" | custom-call | tf_op jit(solution)/shard_map/backward/pallas_call | solution.py:403
  27.4 0.9 %collective-permute-done.8.y_ref = bf16[256,128]{1,0:T(8,128)(2,1)S(1)} collective-permute-done((bf16[256,128]{1,0:T(8,128)(2,1)S(1)}, bf16[256,128]{1,0:T(8,128)(2,1)S(1)}, u32[]{:S(2)}, u32[]{:S(2)}) %collective-permute-start.8) | collective-permute-done | bytes 65568 | tf_op jit(solution)/shard_map/ppermute | solution.py:417
  28.3 1.3 %collective-permute-start.10 = (bf16[128,128]{1,0:T(8,128)(2,1)S(1)}, bf16[128,128]{1,0:T(8,128)(2,1)S(1)}, u32[]{:S(2)}, u32[]{:S(2)}) collective-permute-start(bf16[128,128]{1,0:T(8,128)(2,1)S(1)} %get-tuple-element.61), channel_id=1, source_target_pairs={{0,12},{1,5},{2,14},{3,7},{4,8},{5,1},{6,10},{7,3},{8,4},{9,13},{1... | collective-permute-start | bytes 98312 | tf_op jit(solution)/shard_map/ppermute | solution.py:417
  29.7 2.1 %collective-permute-start.9 = (bf16[128,128]{1,0:T(8,128)(2,1)S(1)}, bf16[128,128]{1,0:T(8,128)(2,1)S(1)}, u32[]{:S(2)}, u32[]{:S(2)}) collective-permute-start(bf16[128,128]{1,0:T(8,128)(2,1)S(1)} %get-tuple-element.60), channel_id=1, source_target_pairs={{0,8},{1,13},{2,10},{3,15},{4,12},{5,9},{6,14},{7,11},{8,0},{9,5},... | collective-permute-start | bytes 98312 | tf_op jit(solution)/shard_map/ppermute | solution.py:417
  31.8 1.1 %collective-permute-start.11 = (bf16[128,128]{1,0:T(8,128)(2,1)S(1)}, bf16[128,128]{1,0:T(8,128)(2,1)S(1)}, u32[]{:S(2)}, u32[]{:S(2)}) collective-permute-start(bf16[128,128]{1,0:T(8,128)(2,1)S(1)} %get-tuple-element.62), channel_id=1, source_target_pairs={{0,4},{1,9},{2,6},{3,11},{4,0},{5,13},{6,2},{7,15},{8,12},{9,1},{1... | collective-permute-start | bytes 98312 | tf_op jit(solution)/shard_map/ppermute | solution.py:417
  35.0 1.0 %collective-permute-done.11.refs_3_ = bf16[128,128]{1,0:T(8,128)(2,1)S(1)} collective-permute-done((bf16[128,128]{1,0:T(8,128)(2,1)S(1)}, bf16[128,128]{1,0:T(8,128)(2,1)S(1)}, u32[]{:S(2)}, u32[]{:S(2)}) %collective-permute-start.11) | collective-permute-done | bytes 32800 | tf_op jit(solution)/shard_map/ppermute | solution.py:417
  36.0 1.3 %collective-permute-start.14 = (bf16[128,128]{1,0:T(8,128)(2,1)S(1)}, bf16[128,128]{1,0:T(8,128)(2,1)S(1)}, u32[]{:S(2)}, u32[]{:S(2)}) collective-permute-start(bf16[128,128]{1,0:T(8,128)(2,1)S(1)} %get-tuple-element.64.refs_0_), channel_id=1, source_target_pairs={{0,12},{1,5},{2,14},{3,7},{4,8},{5,1},{6,10},{7,3},{8,4},{9,13},{1... | collective-permute-start | bytes 98312 | tf_op jit(solution)/shard_map/ppermute | solution.py:417
  37.3 3.1 %collective-permute-start.12 = (bf16[128,128]{1,0:T(8,128)(2,1)S(1)}, bf16[128,128]{1,0:T(8,128)(2,1)S(1)}, u32[]{:S(2)}, u32[]{:S(2)}) collective-permute-start(bf16[128,128]{1,0:T(8,128)(2,1)S(1)} %get-tuple-element.64.refs_0_), channel_id=1, source_target_pairs={{0,8},{1,13},{2,10},{3,15},{4,12},{5,9},{6,14},{7,11},{8,0},{9,5},... | collective-permute-start | bytes 98312 | tf_op jit(solution)/shard_map/ppermute | solution.py:417
  40.4 1.3 %collective-permute-done.14.refs_0_ = bf16[128,128]{1,0:T(8,128)(2,1)S(1)} collective-permute-done((bf16[128,128]{1,0:T(8,128)(2,1)S(1)}, bf16[128,128]{1,0:T(8,128)(2,1)S(1)}, u32[]{:S(2)}, u32[]{:S(2)}) %collective-permute-start.14) | collective-permute-done | bytes 32800 | tf_op jit(solution)/shard_map/ppermute | solution.py:417
  42.4 1.6 %collective-permute-start.13 = (bf16[256,128]{1,0:T(8,128)(2,1)S(1)}, bf16[256,128]{1,0:T(8,128)(2,1)S(1)}, u32[]{:S(2)}, u32[]{:S(2)}) collective-permute-start(bf16[256,128]{1,0:T(8,128)(2,1)S(1)} %join.6.refs_0_), channel_id=1, source_target_pairs={{0,2},{1,3},{2,0},{3,1},{4,6},{5,7},{6,4},{7,5},{8,10},{9,11},{10,... | collective-permute-start | bytes 196616 | tf_op jit(solution)/shard_map/ppermute | solution.py:417
  43.9 2.4 %forward.9.refs_6_ = f32[512,128]{1,0:T(8,128)S(1)} custom-call(s32[8,128]{1,0:T(8,128)S(4)} %get-tuple-element.38.slots, bf16[256,128]{1,0:T(8,128)(2,1)S(1)} %join.6.refs_0_, bf16[256,128]{1,0:T(8,128)(2,1)S(1)} %join.7.refs_1_, s32[544,128]{1,0:T(8,128)S(1)} %get-tuple-element.39.refs_2_, f32[544,128]{1,0:T(8,128)S(1)} %get-tuple-element.40.refs_3_, ...), custom_call_target="tpu_custom_call" | custom-call | tf_op jit(solution)/shard_map/forward/pallas_call | solution.py:403
  46.8 0.9 %forward.11 = f32[256,128]{1,0:T(8,128)S(1)} custom-call(s32[8,128]{1,0:T(8,128)S(4)} %get-tuple-element.50.slots, bf16[256,128]{1,0:T(8,128)(2,1)S(1)} %collective-permute-done.13.refs_0_, bf16[256,128]{1,0:T(8,128)(2,1)S(1)} %collective-permute-done.16.refs_1_, s32[544,128]{1,0:T(8,128)S(1)} %get-tuple-element.44.refs_2_, ...), custom_call_target="tpu_custom_call" | custom-call | tf_op jit(solution)/shard_map/forward/pallas_call | solution.py:403
  47.8 1.3 %forward.10.projection_ref = f32[256,128]{1,0:T(8,128)S(1)} custom-call(s32[8,128]{1,0:T(8,128)S(4)} %get-tuple-element.43.slots, bf16[256,128]{1,0:T(8,128)(2,1)S(1)} %collective-permute-done.13.refs_0_, bf16[256,128]{1,0:T(8,128)(2,1)S(1)} %collective-permute-done.16.refs_1_, s32[544,128]{1,0:T(8,128)S(1)} %get-tuple-element.44.refs_2_, ...), custom_call_target="tpu_custom_call" | custom-call | tf_op jit(solution)/shard_map/forward/pallas_call | solution.py:403
  49.7 1.1 %backward.10.refs_4_ = f32[512,128]{1,0:T(8,128)S(1)} custom-call(s32[8,128]{1,0:T(8,128)S(4)} %get-tuple-element.43.slots, bf16[256,128]{1,0:T(8,128)(2,1)S(1)} %residual.3.refs_0_, s32[544,128]{1,0:T(8,128)S(1)} %get-tuple-element.54.refs_1_, f32[544,128]{1,0:T(8,128)S(1)} %get-tuple-element.55.refs_2_, f32[544,128]{1,0:T(8,128)S(1)} %get-tuple-element.56.refs_3_), custom_call_target="tpu_custom_call" | custom-call | tf_op jit(solution)/shard_map/backward/pallas_call | solution.py:403
  51.6 1.4 %collective-permute-start.20 = (bf16[256,128]{1,0:T(8,128)(2,1)S(1)}, bf16[256,128]{1,0:T(8,128)(2,1)S(1)}, u32[]{:S(2)}, u32[]{:S(2)}) collective-permute-start(bf16[256,128]{1,0:T(8,128)(2,1)S(1)} %get-tuple-element.67), channel_id=1, source_target_pairs={{0,2},{1,3},{2,0},{3,1},{4,6},{5,7},{6,4},{7,5},{8,10},{9,11},{10,... | collective-permute-start | bytes 196616 | tf_op jit(solution)/shard_map/ppermute | solution.py:417
  53.7 1.9 %backward.9.sum_ref = f32[512,128]{1,0:T(8,128)S(1)} custom-call(s32[8,128]{1,0:T(8,128)S(4)} %get-tuple-element.38.slots, bf16[256,128]{1,0:T(8,128)(2,1)S(1)} %residual.3.refs_0_, bf16[256,128]{1,0:T(8,128)(2,1)S(1)} %collective-permute-done.18.refs_1_.refs_0_, s32[544,128]{1,0:T(8,128)S(1)} %get-tuple-element.51.refs_2_, ...), custom_call_target="tpu_custom_call" | custom-call | tf_op jit(solution)/shard_map/backward/pallas_call | solution.py:403
  56.5 2.1 %collective-permute-start.21 = (bf16[128,128]{1,0:T(8,128)(2,1)S(1)}, bf16[128,128]{1,0:T(8,128)(2,1)S(1)}, u32[]{:S(2)}, u32[]{:S(2)}) collective-permute-start(bf16[128,128]{1,0:T(8,128)(2,1)S(1)} %get-tuple-element.68), channel_id=1, source_target_pairs={{0,8},{1,13},{2,10},{3,15},{4,12},{5,9},{6,14},{7,11},{8,0},{9,5},... | collective-permute-start | bytes 98312 | tf_op jit(solution)/shard_map/ppermute | solution.py:417
  58.6 2.5 %collective-permute-start.22 = (bf16[128,128]{1,0:T(8,128)(2,1)S(1)}, bf16[128,128]{1,0:T(8,128)(2,1)S(1)}, u32[]{:S(2)}, u32[]{:S(2)}) collective-permute-start(bf16[128,128]{1,0:T(8,128)(2,1)S(1)} %get-tuple-element.69), channel_id=1, source_target_pairs={{0,12},{1,5},{2,14},{3,7},{4,8},{5,1},{6,10},{7,3},{8,4},{9,13},{1... | collective-permute-start | bytes 98312 | tf_op jit(solution)/shard_map/ppermute | solution.py:417
  61.7 2.7 %collective-permute-done.22.refs_2_ = bf16[128,128]{1,0:T(8,128)(2,1)S(1)} collective-permute-done((bf16[128,128]{1,0:T(8,128)(2,1)S(1)}, bf16[128,128]{1,0:T(8,128)(2,1)S(1)}, u32[]{:S(2)}, u32[]{:S(2)}) %collective-permute-start.22) | collective-permute-done | bytes 32800 | tf_op jit(solution)/shard_map/ppermute | solution.py:417
  (56 shorter events, 11.1 us)
Async XLA Ops:
  1.0 7.6 %collective-permute-start.1 = (bf16[192,128]{1,0:T(8,128)(2,1)S(1)}, bf16[192,128]{1,0:T(8,128)(2,1)S(1)}, u32[]{:S(2)}, u32[]{:S(2)}) collective-permute-start(bf16[192,128]{1,0:T(8,128)(2,1)S(1)} %pack.1.refs_0_), channel_id=1, source_target_pairs={{0,12},{1,5},{2,14},{3,7},{4,8},{5,1},{6,10},{7,3},{8,4},{9,13},{1... | collective-permute-start | bytes 147464 | tf_op jit(solution)/shard_map/ppermute | solution.py:417
  6.2 4.1 %collective-permute-start.2 = (bf16[192,128]{1,0:T(8,128)(2,1)S(1)}, bf16[192,128]{1,0:T(8,128)(2,1)S(1)}, u32[]{:S(2)}, u32[]{:S(2)}) collective-permute-start(bf16[192,128]{1,0:T(8,128)(2,1)S(1)} %pack.1.refs_0_), channel_id=1, source_target_pairs={{0,4},{1,9},{2,6},{3,11},{4,0},{5,13},{6,2},{7,15},{8,12},{9,1},{1... | collective-permute-start | bytes 147464 | tf_op jit(solution)/shard_map/ppermute | solution.py:417
  6.2 5.7 %collective-permute-start = (bf16[192,128]{1,0:T(8,128)(2,1)S(1)}, bf16[192,128]{1,0:T(8,128)(2,1)S(1)}, u32[]{:S(2)}, u32[]{:S(2)}) collective-permute-start(bf16[192,128]{1,0:T(8,128)(2,1)S(1)} %pack.1.refs_0_), channel_id=1, source_target_pairs={{0,8},{1,13},{2,10},{3,15},{4,12},{5,9},{6,14},{7,11},{8,0},{9,5},... | collective-permute-start | bytes 147464 | tf_op jit(solution)/shard_map/ppermute | solution.py:417
  10.3 6.7 %collective-permute-start.4 = (bf16[384,128]{1,0:T(8,128)(2,1)S(1)}, bf16[384,128]{1,0:T(8,128)(2,1)S(1)}, u32[]{:S(2)}, u32[]{:S(2)}) collective-permute-start(bf16[384,128]{1,0:T(8,128)(2,1)S(1)} %join.5.refs_1_), channel_id=1, source_target_pairs={{0,2},{1,3},{2,0},{3,1},{4,6},{5,7},{6,4},{7,5},{8,10},{9,11},{10,... | collective-permute-start | bytes 294920 | tf_op jit(solution)/shard_map/ppermute | solution.py:417
  11.9 5.1 %collective-permute-start.3 = (bf16[384,128]{1,0:T(8,128)(2,1)S(1)}, bf16[384,128]{1,0:T(8,128)(2,1)S(1)}, u32[]{:S(2)}, u32[]{:S(2)}) collective-permute-start(bf16[384,128]{1,0:T(8,128)(2,1)S(1)} %join.4.refs_0_), channel_id=1, source_target_pairs={{0,2},{1,3},{2,0},{3,1},{4,6},{5,7},{6,4},{7,5},{8,10},{9,11},{10,... | collective-permute-start | bytes 294920 | tf_op jit(solution)/shard_map/ppermute | solution.py:417
  19.5 1.4 %collective-permute-start.5 = (f32[288,128]{1,0:T(8,128)S(1)}, f32[288,128]{1,0:T(8,128)S(1)}, u32[]{:S(2)}, u32[]{:S(2)}) collective-permute-start(f32[288,128]{1,0:T(8,128)S(1)} %forward.8), channel_id=1, source_target_pairs={{0,1},{1,0},{2,3},{3,2},{4,5},{5,4},{6,7},{7,6},{8,9},{9,8},{10,11... | collective-permute-start | bytes 442376 | tf_op jit(solution)/shard_map/ppermute | solution.py:417
  19.5 1.4 %copy-start = (bf16[32,8,128]{2,1,0:T(8,128)(2,1)S(1)}, bf16[32,8,128]{2,1,0:T(8,128)(2,1)}, u32[]{:S(2)}) copy-start(bf16[32,8,128]{2,1,0:T(8,128)(2,1)} %param.7) | copy-start | bytes 196612
  20.9 1.7 %collective-permute-start.6 = (bf16[256,128]{1,0:T(8,128)(2,1)S(1)}, bf16[256,128]{1,0:T(8,128)(2,1)S(1)}, u32[]{:S(2)}, u32[]{:S(2)}) collective-permute-start(bf16[256,128]{1,0:T(8,128)(2,1)S(1)} %residual.2.refs_0_), channel_id=1, source_target_pairs={{0,1},{1,0},{2,3},{3,2},{4,5},{5,4},{6,7},{7,6},{8,9},{9,8},{10,11... | collective-permute-start | bytes 196616 | tf_op jit(solution)/shard_map/ppermute | solution.py:417
  23.4 4.9 %collective-permute-start.8 = (bf16[256,128]{1,0:T(8,128)(2,1)S(1)}, bf16[256,128]{1,0:T(8,128)(2,1)S(1)}, u32[]{:S(2)}, u32[]{:S(2)}) collective-permute-start(bf16[256,128]{1,0:T(8,128)(2,1)S(1)} %get-tuple-element.59), channel_id=1, source_target_pairs={{0,2},{1,3},{2,0},{3,1},{4,6},{5,7},{6,4},{7,5},{8,10},{9,11},{10,... | collective-permute-start | bytes 196616 | tf_op jit(solution)/shard_map/ppermute | solution.py:417
  24.6 7.2 %collective-permute-start.7 = (bf16[256,128]{1,0:T(8,128)(2,1)S(1)}, bf16[256,128]{1,0:T(8,128)(2,1)S(1)}, u32[]{:S(2)}, u32[]{:S(2)}) collective-permute-start(bf16[256,128]{1,0:T(8,128)(2,1)S(1)} %get-tuple-element.57), channel_id=1, source_target_pairs={{0,2},{1,3},{2,0},{3,1},{4,6},{5,7},{6,4},{7,5},{8,10},{9,11},{10,... | collective-permute-start | bytes 196616 | tf_op jit(solution)/shard_map/ppermute | solution.py:417
  28.3 5.8 %collective-permute-start.10 = (bf16[128,128]{1,0:T(8,128)(2,1)S(1)}, bf16[128,128]{1,0:T(8,128)(2,1)S(1)}, u32[]{:S(2)}, u32[]{:S(2)}) collective-permute-start(bf16[128,128]{1,0:T(8,128)(2,1)S(1)} %get-tuple-element.61), channel_id=1, source_target_pairs={{0,12},{1,5},{2,14},{3,7},{4,8},{5,1},{6,10},{7,3},{8,4},{9,13},{1... | collective-permute-start | bytes 98312 | tf_op jit(solution)/shard_map/ppermute | solution.py:417
  29.7 5.3 %collective-permute-start.9 = (bf16[128,128]{1,0:T(8,128)(2,1)S(1)}, bf16[128,128]{1,0:T(8,128)(2,1)S(1)}, u32[]{:S(2)}, u32[]{:S(2)}) collective-permute-start(bf16[128,128]{1,0:T(8,128)(2,1)S(1)} %get-tuple-element.60), channel_id=1, source_target_pairs={{0,8},{1,13},{2,10},{3,15},{4,12},{5,9},{6,14},{7,11},{8,0},{9,5},... | collective-permute-start | bytes 98312 | tf_op jit(solution)/shard_map/ppermute | solution.py:417
  31.8 1.1 %copy-start.2 = (f32[256,4]{0,1:T(4,128)S(1)}, f32[256,4]{0,1:T(4,128)}, u32[]{:S(2)}) copy-start(f32[256,4]{0,1:T(4,128)} %param.13) | copy-start | bytes 12292
  31.8 1.1 %copy-start.3 = (f32[256,4]{0,1:T(4,128)S(1)}, f32[256,4]{0,1:T(4,128)}, u32[]{:S(2)}) copy-start(f32[256,4]{0,1:T(4,128)} %param.12) | copy-start | bytes 12292
  31.8 1.1 %copy-start.4 = (s32[256,4]{0,1:T(4,128)S(1)}, s32[256,4]{0,1:T(4,128)}, u32[]{:S(2)}) copy-start(s32[256,4]{0,1:T(4,128)} %param.9) | copy-start | bytes 12292
  31.8 1.1 %copy-start.5 = (s32[16]{0:T(128)S(1)}, s32[16]{0:T(128)}, u32[]{:S(2)}) copy-start(s32[16]{0:T(128)} %param.11) | copy-start | bytes 196
  31.8 4.1 %copy-start.1 = (f32[16,8,128]{2,1,0:T(8,128)S(1)}, f32[16,8,128]{2,1,0:T(8,128)}, u32[]{:S(2)}) copy-start(f32[16,8,128]{2,1,0:T(8,128)} %param.8) | copy-start | bytes 196612
  31.8 4.1 %collective-permute-start.11 = (bf16[128,128]{1,0:T(8,128)(2,1)S(1)}, bf16[128,128]{1,0:T(8,128)(2,1)S(1)}, u32[]{:S(2)}, u32[]{:S(2)}) collective-permute-start(bf16[128,128]{1,0:T(8,128)(2,1)S(1)} %get-tuple-element.62), channel_id=1, source_target_pairs={{0,4},{1,9},{2,6},{3,11},{4,0},{5,13},{6,2},{7,15},{8,12},{9,1},{1... | collective-permute-start | bytes 98312 | tf_op jit(solution)/shard_map/ppermute | solution.py:417
  36.0 5.8 %collective-permute-start.14 = (bf16[128,128]{1,0:T(8,128)(2,1)S(1)}, bf16[128,128]{1,0:T(8,128)(2,1)S(1)}, u32[]{:S(2)}, u32[]{:S(2)}) collective-permute-start(bf16[128,128]{1,0:T(8,128)(2,1)S(1)} %get-tuple-element.64.refs_0_), channel_id=1, source_target_pairs={{0,12},{1,5},{2,14},{3,7},{4,8},{5,1},{6,10},{7,3},{8,4},{9,13},{1... | collective-permute-start | bytes 98312 | tf_op jit(solution)/shard_map/ppermute | solution.py:417
  37.2 4.5 %collective-permute-start.15 = (bf16[128,128]{1,0:T(8,128)(2,1)S(1)}, bf16[128,128]{1,0:T(8,128)(2,1)S(1)}, u32[]{:S(2)}, u32[]{:S(2)}) collective-permute-start(bf16[128,128]{1,0:T(8,128)(2,1)S(1)} %get-tuple-element.64.refs_0_), channel_id=1, source_target_pairs={{0,4},{1,9},{2,6},{3,11},{4,0},{5,13},{6,2},{7,15},{8,12},{9,1},{1... | collective-permute-start | bytes 98312 | tf_op jit(solution)/shard_map/ppermute | solution.py:417
  37.3 5.0 %collective-permute-start.12 = (bf16[128,128]{1,0:T(8,128)(2,1)S(1)}, bf16[128,128]{1,0:T(8,128)(2,1)S(1)}, u32[]{:S(2)}, u32[]{:S(2)}) collective-permute-start(bf16[128,128]{1,0:T(8,128)(2,1)S(1)} %get-tuple-element.64.refs_0_), channel_id=1, source_target_pairs={{0,8},{1,13},{2,10},{3,15},{4,12},{5,9},{6,14},{7,11},{8,0},{9,5},... | collective-permute-start | bytes 98312 | tf_op jit(solution)/shard_map/ppermute | solution.py:417
  41.8 4.6 %collective-permute-start.16 = (bf16[256,128]{1,0:T(8,128)(2,1)S(1)}, bf16[256,128]{1,0:T(8,128)(2,1)S(1)}, u32[]{:S(2)}, u32[]{:S(2)}) collective-permute-start(bf16[256,128]{1,0:T(8,128)(2,1)S(1)} %join.7.refs_1_), channel_id=1, source_target_pairs={{0,2},{1,3},{2,0},{3,1},{4,6},{5,7},{6,4},{7,5},{8,10},{9,11},{10,... | collective-permute-start | bytes 196616 | tf_op jit(solution)/shard_map/ppermute | solution.py:417
  42.4 4.4 %collective-permute-start.13 = (bf16[256,128]{1,0:T(8,128)(2,1)S(1)}, bf16[256,128]{1,0:T(8,128)(2,1)S(1)}, u32[]{:S(2)}, u32[]{:S(2)}) collective-permute-start(bf16[256,128]{1,0:T(8,128)(2,1)S(1)} %join.6.refs_0_), channel_id=1, source_target_pairs={{0,2},{1,3},{2,0},{3,1},{4,6},{5,7},{6,4},{7,5},{8,10},{9,11},{10,... | collective-permute-start | bytes 196616 | tf_op jit(solution)/shard_map/ppermute | solution.py:417
  47.7 1.4 %collective-permute-start.17 = (f32[256,128]{1,0:T(8,128)S(1)}, f32[256,128]{1,0:T(8,128)S(1)}, u32[]{:S(2)}, u32[]{:S(2)}) collective-permute-start(f32[256,128]{1,0:T(8,128)S(1)} %forward.11), channel_id=1, source_target_pairs={{0,1},{1,0},{2,3},{3,2},{4,5},{5,4},{6,7},{7,6},{8,9},{9,8},{10,11... | collective-permute-start | bytes 393224 | tf_op jit(solution)/shard_map/ppermute | solution.py:417
  49.1 1.7 %collective-permute-start.18 = (bf16[256,128]{1,0:T(8,128)(2,1)S(1)}, bf16[256,128]{1,0:T(8,128)(2,1)S(1)}, u32[]{:S(2)}, u32[]{:S(2)}) collective-permute-start(bf16[256,128]{1,0:T(8,128)(2,1)S(1)} %residual.3.refs_0_), channel_id=1, source_target_pairs={{0,1},{1,0},{2,3},{3,2},{4,5},{5,4},{6,7},{7,6},{8,9},{9,8},{10,11... | collective-permute-start | bytes 196616 | tf_op jit(solution)/shard_map/ppermute | solution.py:417
  51.6 4.9 %collective-permute-start.20 = (bf16[256,128]{1,0:T(8,128)(2,1)S(1)}, bf16[256,128]{1,0:T(8,128)(2,1)S(1)}, u32[]{:S(2)}, u32[]{:S(2)}) collective-permute-start(bf16[256,128]{1,0:T(8,128)(2,1)S(1)} %get-tuple-element.67), channel_id=1, source_target_pairs={{0,2},{1,3},{2,0},{3,1},{4,6},{5,7},{6,4},{7,5},{8,10},{9,11},{10,... | collective-permute-start | bytes 196616 | tf_op jit(solution)/shard_map/ppermute | solution.py:417
  53.1 8.1 %collective-permute-start.19 = (bf16[256,128]{1,0:T(8,128)(2,1)S(1)}, bf16[256,128]{1,0:T(8,128)(2,1)S(1)}, u32[]{:S(2)}, u32[]{:S(2)}) collective-permute-start(bf16[256,128]{1,0:T(8,128)(2,1)S(1)} %get-tuple-element.65), channel_id=1, source_target_pairs={{0,2},{1,3},{2,0},{3,1},{4,6},{5,7},{6,4},{7,5},{8,10},{9,11},{10,... | collective-permute-start | bytes 196616 | tf_op jit(solution)/shard_map/ppermute | solution.py:417
  56.5 5.1 %collective-permute-start.21 = (bf16[128,128]{1,0:T(8,128)(2,1)S(1)}, bf16[128,128]{1,0:T(8,128)(2,1)S(1)}, u32[]{:S(2)}, u32[]{:S(2)}) collective-permute-start(bf16[128,128]{1,0:T(8,128)(2,1)S(1)} %get-tuple-element.68), channel_id=1, source_target_pairs={{0,8},{1,13},{2,10},{3,15},{4,12},{5,9},{6,14},{7,11},{8,0},{9,5},... | collective-permute-start | bytes 98312 | tf_op jit(solution)/shard_map/ppermute | solution.py:417
  58.6 5.7 %collective-permute-start.22 = (bf16[128,128]{1,0:T(8,128)(2,1)S(1)}, bf16[128,128]{1,0:T(8,128)(2,1)S(1)}, u32[]{:S(2)}, u32[]{:S(2)}) collective-permute-start(bf16[128,128]{1,0:T(8,128)(2,1)S(1)} %get-tuple-element.69), channel_id=1, source_target_pairs={{0,12},{1,5},{2,14},{3,7},{4,8},{5,1},{6,10},{7,3},{8,4},{9,13},{1... | collective-permute-start | bytes 98312 | tf_op jit(solution)/shard_map/ppermute | solution.py:417
  61.2 4.0 %collective-permute-start.23 = (bf16[128,128]{1,0:T(8,128)(2,1)S(1)}, bf16[128,128]{1,0:T(8,128)(2,1)S(1)}, u32[]{:S(2)}, u32[]{:S(2)}) collective-permute-start(bf16[128,128]{1,0:T(8,128)(2,1)S(1)} %get-tuple-element.70), channel_id=1, source_target_pairs={{0,4},{1,9},{2,6},{3,11},{4,0},{5,13},{6,2},{7,15},{8,12},{9,1},{1... | collective-permute-start | bytes 98312 | tf_op jit(solution)/shard_map/ppermute | solution.py:417

commit v14 on v11

--- a/solution.py
+++ b/solution.py
@@ -92,6 +92,20 @@
     for part in range(slots // extent):
         at = pl.ds(rows + part * height, height)
         out_ref[at, :] = fields[:, part * extent:(part + 1) * extent].astype(BF16)
+    below = rows + height * (slots // extent)
+    if below < out_ref.shape[0]:
+        left = volume_ref[...] - volume_ref[...].astype(BF16).astype(F32)
+        out_ref[below:below + rows, :] = left.astype(BF16)
+
+
+def read_fields(payload_ref, at, depth):
+    height = -(-(7 * depth + 2) // 16) * 16
+    raw = payload_ref[pl.ds(at, height), :].astype(F32)
+    offset = (raw[0:depth] + raw[depth:2 * depth]) + raw[2 * depth:3 * depth]
+    slope = (raw[3 * depth:4 * depth] + raw[4 * depth:5 * depth]) + raw[5 * depth:6 * depth]
+    return jnp.concatenate(
+        [offset, slope, raw[6 * depth:7 * depth + 2],
+         jnp.zeros((16 - 3 * depth - 2, raw.shape[1]), F32)], axis=0)
 
 
 def setup_kernel(n_payloads, members, stride, span, sizes, tiles, wanted, *refs):
@@ -116,12 +130,7 @@
 
     def collect(member, lined, payload_ref, within):
         at = within * stride + tiles * frames + part * height
-        raw = payload_ref[pl.ds(pl.multiple_of(at, 16), height), :].astype(F32)
-        offset = (raw[0:depth] + raw[depth:2 * depth]) + raw[2 * depth:3 * depth]
-        slope = (raw[3 * depth:4 * depth] + raw[4 * depth:5 * depth]) + raw[5 * depth:6 * depth]
-        fields = jnp.concatenate(
-            [offset, slope, raw[6 * depth:7 * depth + 2],
-             jnp.zeros((16 - 3 * depth - 2, extent), F32)], axis=0)
+        fields = read_fields(payload_ref, pl.multiple_of(at, 16), depth)
         fields = pltpu.roll(fields, shift, axis=1)
         lane = lax.broadcasted_iota(I32, fields.shape, 1)
         fields = jnp.where(lane < width, fields, 0.0)
@@ -150,8 +159,9 @@
          jnp.zeros((5 - depth, lanes), F32)], axis=0)
     order = lax.broadcasted_iota(I32, (lanes, lanes), 0)
     earlier = (lax.broadcasted_iota(I32, (lanes, lanes), 1) < order).astype(F32)
-    for ref, kind, copy in zip(drafts, wanted, copies):
+    for ref, (low, high, kind), copy in zip(drafts, wanted, copies):
         taken = alive if kind is None else jnp.logical_and(alive, target == kind)
+        taken = jnp.logical_and(taken, jnp.logical_and(slot >= low * width, slot < high * width))
         taken = taken.astype(F32)
         position = contract_lanes(jnp.broadcast_to(taken, (8, lanes)), earlier)[0:1]
         position = jnp.where(taken > 0.0, position, -1.0).astype(I32)
@@ -160,7 +170,7 @@
         total = jnp.sum(taken, axis=1, keepdims=True).astype(I32)
         line = jnp.where(slot < total, packed[0:1], lanes)
         base = packed[1:2] if kind is not None else packed[1:2] + packed[2:3] * ray_tiles
-        member = lax.div(packed[0:1], width) * tiles
+        member = jnp.maximum(lax.div(packed[0:1], width) - low, 0) * tiles
         rows = [line, base * frames]
         rows += [(packed[3 + level:4 + level] + member) * frames for level in range(depth)]
         rows += [jnp.zeros((5 - depth, lanes), I32), jnp.broadcast_to(total, (1, lanes))]
@@ -193,25 +203,29 @@
         copy.wait()
 
 
-def column_kernel(sizes, offset_ref, slope_ref, voxel_ref, live_ref, out_ref):
+def column_kernel(sizes, stride, tiles, slots, payload_ref, out_ref):
     capacity, depth, frames = sizes
-    tiles = out_ref.shape[0] // frames
-    slots = offset_ref.shape[1]
     extent = out_ref.shape[1]
-    offsets = offset_ref[...].T
-    slopes = slope_ref[...].T
-    within = lax.rem(lax.broadcasted_iota(I32, (1, slots), 1), capacity).astype(F32)
-    alive = jnp.broadcast_to(within, (tiles, slots)) < per_slot(live_ref, slots, capacity)
-    total = jnp.zeros((tiles, extent), F32)
-    for level in range(depth):
-        unused, pair = column_taps(
-            offsets[:, level:level + 1], slopes[:, level:level + 1], extent)
-        tile_of = jnp.broadcast_to(voxel_ref[level:level + 1, :], (tiles, slots))
-        match = tile_of == lax.broadcasted_iota(I32, (tiles, slots), 0)
-        hot = jnp.logical_and(match, alive).astype(F32).astype(BF16)
-        for weight in pair:
-            total += jnp.dot(hot, weight, preferred_element_type=F32)
-    out_ref[...] = repeat_rows(1.0 / jnp.maximum(total, 1.0), frames)
+    height = -(-(7 * depth + 2) // 16) * 16
+    rows = tiles * frames
+    within = lax.rem(lax.broadcasted_iota(I32, (1, extent), 1), capacity).astype(F32)
+    tile = lax.broadcasted_iota(I32, (tiles, extent), 0).astype(F32)
+    for member in range(out_ref.shape[0] // rows):
+        total = jnp.zeros((tiles, extent), F32)
+        for part in range(slots // extent):
+            at = member * stride + rows + part * height
+            fields = read_fields(payload_ref, at, depth)
+            columns = fields.T
+            alive = within < fields[3 * depth + 1:3 * depth + 2]
+            for level in range(depth):
+                unused, pair = column_taps(
+                    columns[:, level:level + 1], columns[:, depth + level:depth + level + 1], extent)
+                voxel = jnp.where(alive, fields[2 * depth + level:2 * depth + level + 1], -1.0)
+                hot = (jnp.broadcast_to(voxel, tile.shape) == tile).astype(F32).astype(BF16)
+                for weight in pair:
+                    total += jnp.dot(hot, weight, preferred_element_type=F32)
+        out_ref[member * rows:(member + 1) * rows, :] = repeat_rows(
+            1.0 / jnp.maximum(total, 1.0), frames)
 
 
 def pick(values, index):
@@ -324,14 +338,13 @@
     out_ref[...] = ((sinogram_ref[...].astype(F32) - projection) * weight).astype(BF16)
 
 
-def backward_kernel(sizes, n_parts, has_start, split, slots, *refs):
+def backward_kernel(sizes, n_parts, has_start, slots, *refs):
     capacity, depth, frames = sizes
     part_refs, tables, refs = refs[:n_parts], refs[n_parts:n_parts + 3], refs[n_parts + 3:]
     start_ref = None
     if has_start:
         start_ref, refs = refs[0], refs[1:]
-    outs = refs[:len(split)] if split else refs[:1]
-    residual, banks = refs[len(outs)], refs[len(outs) + 1:]
+    out_ref, residual, banks = refs[0], refs[1], refs[2:]
     rays = part_refs[0].shape[0]
     line_step = tables[0].shape[0] // depth
     for place, ref in enumerate(part_refs):
@@ -360,41 +373,53 @@
 
     for_slots(slots, one)
 
-    def total(at):
-        return sum([bank[at, :] for bank in banks[1:]], banks[0][at, :]).astype(outs[0].dtype)
-
-    if split:
-        for ref, members in zip(outs, split):
-            rows = ref.shape[0] // len(members)
-            for place, member in enumerate(members):
-                ref[place * rows:(place + 1) * rows, :] = total(pl.ds(member * rows, rows))
+    def finish(at):
+        total = sum([bank[at, :] for bank in banks[1:]], banks[0][at, :])
+        out_ref[at, :] = total.astype(out_ref.dtype)
+
+    for_rows(out_ref.shape[0], finish)
+
+
+def join_kernel(rows, *refs):
+    for place, ref in enumerate(refs[:-1]):
+        refs[-1][place * rows:(place + 1) * rows, :] = ref[0:rows, :]
+
+
+def combine_kernel(sum_ref, *refs):
+    total = sum_ref[...]
+    for ref in refs[:-2]:
+        total = total + ref[...].astype(F32)
+    out_ref, send_ref = refs[-2:]
+    out_ref[...] = total
+    send_ref[...] = total[total.shape[0] - send_ref.shape[0]:].astype(BF16)
+
+
+def update_pair_kernel(last, volume_ref, column_ref, sum_ref, got_ref, *refs):
+    rows = volume_ref.shape[0]
+    if last:
+        back = sum_ref[0:rows, :] + got_ref[...].astype(F32)
+        refs[0][...] = volume_ref[...] + column_ref[0:rows, :] * back
+        return
+    other_ref, out_ref, other_out, payload_ref = refs
+    if other_ref.dtype == BF16:
+        left = other_ref.shape[0] - rows
+        other = other_ref[0:rows, :].astype(F32) + other_ref[left:, :].astype(F32)
     else:
-        def finish(at):
-            outs[0][at, :] = total(at)
-
-        for_rows(outs[0].shape[0], finish)
-
-
-def join_kernel(*refs):
-    out_ref, at = refs[-1], 0
-    for ref in refs[:-1]:
-        out_ref[at:at + ref.shape[0], :] = ref[...]
-        at += ref.shape[0]
-
-
-def combine_kernel(members, sum_ref, y_ref, *piece_refs):
-    rows = piece_refs[0].shape[0]
-    for place, (member, ref) in enumerate(zip(members, piece_refs)):
-        mine = sum_ref[member * rows:(member + 1) * rows, :]
-        ref[...] = (mine + y_ref[place * rows:(place + 1) * rows, :].astype(F32)).astype(ref.dtype)
-
-
-def update_kernel(n_pieces, volume_ref, column_ref, *refs):
-    back = refs[0][...]
-    for ref in refs[1:n_pieces]:
-        back = back + ref[...].astype(F32)
-    volume = volume_ref[...] + column_ref[...] * back
-    for ref in refs[n_pieces:]:
+        other = other_ref[...]
+    mine = sum_ref[...].astype(BF16).astype(F32)
+    back = mine[0:rows] + got_ref[rows:, :].astype(F32)
+    other_back = mine[rows:] + got_ref[0:rows, :].astype(F32)
+    volume = volume_ref[...] + column_ref[0:rows, :] * back
+    other = other + column_ref[rows:, :] * other_back
+    out_ref[...] = volume
+    other_out[...] = other
+    payload_ref[0:rows, :] = volume.astype(BF16)
+    payload_ref[rows:, :] = other.astype(BF16)
+
+
+def update_kernel(volume_ref, column_ref, back_ref, *refs):
+    volume = volume_ref[...] + column_ref[...] * back_ref[...]
+    for ref in refs:
         ref[...] = volume.astype(ref.dtype)
 
 
@@ -438,7 +463,7 @@
     operands = (volume, *slots_by_depth, slot_ray.reshape(1, n_slots), live)
     payload = call(
         functools.partial(pack_kernel, capacity), "pack", 16, [HBM] * 6,
-        shape((rows + height, extent), BF16),
+        shape((rows + height + (rows if paired else 0), extent), BF16),
         *[pltpu.with_memory_space_constraint(operand, pltpu.HBM) for operand in operands],
         scratch=[pltpu.VMEM(operand.shape, operand.dtype) for operand in operands]
         + [pltpu.SemaphoreType.DMA((6,))])
@@ -474,81 +499,86 @@
             functools.partial(residual_kernel, frames, len(row_sums)), "residual", 16,
             [VMEM] * len(operands), shape((n_rays, extent), BF16), *operands)
 
-    def backward(slots, parts, members, table, kind, start=None, split=()):
-        operands = [pltpu.with_memory_space_constraint(slots, pltpu.SMEM), *parts, *table] + ([] if start is None else [start])
+    def backward(slots, parts, members, table, kind, start=None):
+        operands = [pltpu.with_memory_space_constraint(slots, pltpu.SMEM), *parts, *table]
+        operands += [] if start is None else [start]
         return call(
-            functools.partial(backward_kernel, sizes, len(parts), start is not None, split),
+            functools.partial(backward_kernel, sizes, len(parts), start is not None),
             "backward", 16 if paired else 32, [SMEM] + [VMEM] * (len(operands) - 1),
-            [shape((len(some) * rows, extent), kind) for some in split]
-            if split else shape((members * rows, extent), kind), *operands,
+            shape((members * rows, extent), kind), *operands,
             scratch=[pltpu.VMEM((len(parts) * n_rays, extent), F32)]
             + [pltpu.VMEM((members * rows, extent), F32)] * n_bank)
 
-    def join(*parts):
-        total = sum(part.shape[0] for part in parts)
-        return call(join_kernel, "join", 16, [VMEM] * len(parts), shape((total, extent), BF16), *parts)
-
-    def update(volume, pieces, last):
-        out = [shape((rows, extent), F32)] + ([] if last else [shape((rows, extent), BF16)])
+    def column_weights(payload, members):
         return call(
-            functools.partial(update_kernel, len(pieces)), "update", 16,
-            [VMEM] * (2 + len(pieces)), out, volume, column_weight, *pieces)
-
-    column_weight = call(
-        functools.partial(column_kernel, sizes), "column_weight", 16, [VMEM] * 4,
-        shape((rows, extent), F32), *slots_by_depth, live)
-
+            functools.partial(column_kernel, sizes, payload.shape[0] // members, voxel_tiles, n_slots),
+            "column_weight", 16, [VMEM], shape((members * rows, extent), F32), payload)
+
+    whole, rounded = shape((rows, extent), F32), shape((rows, extent), BF16)
+    if not paired:
+        column_weight = column_weights(payload, 1)
     for sweep in range(ITERS):
         last = sweep + 1 == ITERS
         if paired:
-            over_2, over_3, over_1 = [
-                exchange(payload, n_slab, distance) for distance in (8, 12, 4)]
-            z_half = join(payload, over_2)
-            y_half = exchange(z_half, n_slab, 2)
-            z_rest = join(over_3, over_1)
-            y_rest = exchange(z_rest, n_slab, 2)
-            along_z, along_y = (z_half, z_rest), (y_half, y_rest)
             if sweep == 0:
-                (z_list,), z_rows, z_forward, z_backward = setup(along_z, 4, (None,))
-            both = forward(z_list, along_z, 4, z_forward, 2 * n_rays)
+                beside = exchange(payload, n_slab, 2)
+                group_0 = call(
+                    functools.partial(join_kernel, rows + height), "join", 16, [VMEM] * 2,
+                    shape((2 * (rows + height), extent), BF16), payload, beside)
+            group_1, group_2, group_3 = [
+                exchange(group_0, n_slab, distance) for distance in (8, 12, 4)]
             if sweep == 0:
-                (own_list, other_list), y_rows, y_forward, y_backward = setup(
-                    along_y, 4, (0, 1), after=both)
+                (list_0, list_1), rows_a, forward_a, backward_a = setup(
+                    (group_0, group_1), 4, ((0, 2, None), (2, 4, None)))
+            both = forward(list_0, (group_0,), 2, forward_a, 2 * n_rays)
+            both = forward(list_1, (group_1,), 2, forward_a, 2 * n_rays, both, 0)
+            if sweep == 0:
+                (list_3, list_own, list_other), rows_b, forward_b, backward_b = setup(
+                    (group_3, group_2), 4, ((0, 2, None), (2, 4, 0), (2, 4, 1)), after=both)
+                row_sums = (rows_a, rows_b)
+            both = forward(list_3, (group_3,), 2, forward_b, 2 * n_rays, both, 0)
             other = exchange(
-                forward(other_list, along_y, 4, y_forward, n_rays, both, n_rays,
-                        (z_rows, y_rows) if sweep == 0 else ()), n_slab, 1)
+                forward(list_other, (group_2,), 2, forward_b, n_rays, both, n_rays,
+                        row_sums if sweep == 0 else ()), n_slab, 1)
             if sweep == 0:
                 first_other = other
-            own = forward(own_list, along_y, 4, y_forward, n_rays, both, 0)
-            residual = residual_of(own, (z_rows, y_rows), other, first_other)
+                column_weight = column_weights(group_0, 2)
+            own = forward(list_own, (group_2,), 2, forward_b, n_rays, both, 0)
+            residual = residual_of(own, row_sums, other, first_other)
             other_residual = exchange(residual, n_slab, 1)
-            y_sum = backward(own_list, [residual], 4, y_backward, F32)
-            far_sum, near_sum = backward(
-                other_list, [other_residual], 4, y_backward, BF16, y_sum, ((1, 2), (0, 3)))
-            far_part, near_part = exchange(far_sum, n_slab, 2), exchange(near_sum, n_slab, 2)
-            z_sum = backward(z_list, [residual, other_residual], 4, z_backward, F32)
-            piece = shape((rows, extent), BF16)
-            piece_2, piece_3 = call(
-                functools.partial(combine_kernel, (1, 2)), "combine", 16, [VMEM] * 2,
-                [piece, piece], z_sum, far_part)
-            got = [exchange(piece_2, n_slab, 8), exchange(piece_3, n_slab, 12)]
-            own_piece, piece_1 = call(
-                functools.partial(combine_kernel, (0, 3)), "combine", 16, [VMEM] * 2,
-                [shape((rows, extent), F32), piece], z_sum, near_part)
-            pieces = [own_piece, *got, exchange(piece_1, n_slab, 4)]
+            residuals = [residual, other_residual]
+            sum_2 = backward(list_own, [residual], 2, backward_b, F32)
+            sum_2 = backward(list_other, [other_residual], 2, backward_b, BF16, sum_2)
+            got_2 = exchange(sum_2, n_slab, 12)
+            got_1 = exchange(backward(list_1, residuals, 2, backward_a, BF16), n_slab, 8)
+            got_3 = exchange(backward(list_3, residuals, 2, backward_b, BF16), n_slab, 4)
+            sum_0 = backward(list_0, residuals, 2, backward_a, F32)
+            total, send = call(
+                combine_kernel, "combine", 16, [VMEM] * 4,
+                [shape((2 * rows, extent), F32), shape(((1 if last else 2) * rows, extent), BF16)],
+                sum_0, got_1, got_2, got_3)
+            operands = [volume, column_weight, total, exchange(send, n_slab, 2)]
+            operands += [] if last else [beside]
+            volume, *rest = call(
+                functools.partial(update_pair_kernel, last), "update", 16, [VMEM] * len(operands),
+                [whole] if last else [whole, whole, shape((2 * rows, extent), BF16)], *operands)
+            if not last:
+                beside, group_0 = rest
         else:
             everyone = lax.all_gather(payload, "slab", axis=0, tiled=True)
             if sweep == 0:
-                (slots,), row_sums, to_rays, to_voxels = setup((everyone,), n_slab, (None,))
+                (slots,), row_sums, to_rays, to_voxels = setup(
+                    (everyone,), n_slab, ((0, n_slab, None),))
             projection = forward(slots, (everyone,), n_slab, to_rays, n_rays)
             residual = residual_of(projection, (row_sums,))
             sums = backward(slots, [residual], n_slab, to_voxels, BF16)
             parts = lax.all_to_all(
                 sums.reshape(n_slab, rows, extent), "slab", split_axis=0, concat_axis=0, tiled=True)
-            pieces = [jnp.sum(parts.astype(F32), axis=0)]
-        volume, *rounded = update(volume, pieces, last)
-        if not last:
-            payload = rounded[0]
+            volume, *rest = call(
+                update_kernel, "update", 16, [VMEM] * 3, [whole] if last else [whole, rounded],
+                volume, column_weight, jnp.sum(parts.astype(F32), axis=0))
+            if not last:
+                payload = rest[0]
     return volume.reshape(start_volume.shape)
 
 

time: 66.1 us -> 71.2 us (1.077)
  waiting for transfers between devices: 14 us -> 23.4 us
  starting transfers between devices: 28.8 us -> 24.7 us
    ppermute x24 -> x19, waiting for transfers between devices: 14 us -> 23.4 us  [exchange(): lax.ppermute(values, 'slab', [(device, device ^ distance) for device in r...]
    ppermute x24 -> x19, starting transfers between devices: 28.8 us -> 24.7 us  [exchange(): lax.ppermute(values, 'slab', [(device, device ^ distance) for device in r...]
    pallas_call x28 -> x31, Pallas kernels: 23.1 us -> 23.1 us  [call(): pl.pallas_call(kernel, out_shape=out_shape, in_specs=in_specs, out_specs=...]
  transfers between devices with their start and end apart: 24 -> 19, of which waited for: 14 -> 14; matrix products, arithmetic and copies ran while one was open for 0% -> 0% of each run, Pallas kernels for 23% -> 22%
where the time goes in v14:
time: 71.2 us; the launch traced here: 71.6 us
  starting transfers between devices  24.7 us (35%)
  waiting for transfers between devices  23.4 us (33%)
  Pallas kernels  23.1 us (32%)
    ppermute x19, starting transfers between devices, exchange(): lax.ppermute(values, 'slab', [(device, device ^ distance) for device in r...  24.7 us
    ppermute x19, waiting for transfers between devices, exchange(): lax.ppermute(values, 'slab', [(device, device ^ distance) for device in r...  23.4 us
    pallas_call x31, Pallas kernels, call(): pl.pallas_call(kernel, out_shape=out_shape, in_specs=in_specs, out_specs=...  23.1 us
  transfers between devices with their start and end apart: 19, of which 14 were waited for; matrix products, arithmetic and copies ran while one was open for 0% of the time, Pallas kernels for 22%

profile of v14, /device:TPU:0, one launch (start us, length us, event | category | flops | bytes accessed | tf_op | source)
XLA Modules:
  0.0 71.6 jit_solution(15755278814760480706)
XLA Ops:
  0.0 1.0 %pack.1.refs_0_ = bf16[320,128]{1,0:T(8,128)(2,1)S(1)} custom-call(f32[128,128]{1,0:T(8,128)} %bitcast.10, f32[4,256]{1,0:T(4,128)} %bitcast.12, f32[4,256]{1,0:T(4,128)} %bitcast.13, s32[4,256]{1,0:T(4,128)} %bitcast.14, s32[1,256]{1,0:T(1,128)} %bitcast.15, s32[1,16]{1,0:T(1,128)} %bitcast.16), custom_call_target="tpu_custom_call" | custom-call | tf_op jit(solution)/shard_map/pack/pallas_call | solution.py:428
  1.1 3.0 %collective-permute-start = (bf16[320,128]{1,0:T(8,128)(2,1)S(1)}, bf16[320,128]{1,0:T(8,128)(2,1)S(1)}, u32[]{:S(2)}, u32[]{:S(2)}) collective-permute-start(bf16[320,128]{1,0:T(8,128)(2,1)S(1)} %pack.1.refs_0_), channel_id=1, source_target_pairs={{0,2},{1,3},{2,0},{3,1},{4,6},{5,7},{6,4},{7,5},{8,10},{9,11},{10,... | collective-permute-start | bytes 245768 | tf_op jit(solution)/shard_map/ppermute | solution.py:441
  4.1 2.4 %collective-permute-done.refs_1_.refs_0_ = bf16[320,128]{1,0:T(8,128)(2,1)S(1)} collective-permute-done((bf16[320,128]{1,0:T(8,128)(2,1)S(1)}, bf16[320,128]{1,0:T(8,128)(2,1)S(1)}, u32[]{:S(2)}, u32[]{:S(2)}) %collective-permute-start) | collective-permute-done | bytes 81952 | tf_op jit(solution)/shard_map/ppermute | solution.py:441
  6.5 3.1 %collective-permute-start.1 = (bf16[384,128]{1,0:T(8,128)(2,1)S(1)}, bf16[384,128]{1,0:T(8,128)(2,1)S(1)}, u32[]{:S(2)}, u32[]{:S(2)}) collective-permute-start(bf16[384,128]{1,0:T(8,128)(2,1)S(1)} %join.1.payload_ref.refs_0_), channel_id=1, source_target_pairs={{0,8},{1,9},{2,10},{3,11},{4,12},{5,13},{6,14},{7,15},{8,0},{9,1},... | collective-permute-start | bytes 294920 | tf_op jit(solution)/shard_map/ppermute | solution.py:441
  9.7 1.3 %collective-permute-start.3 = (bf16[384,128]{1,0:T(8,128)(2,1)S(1)}, bf16[384,128]{1,0:T(8,128)(2,1)S(1)}, u32[]{:S(2)}, u32[]{:S(2)}) collective-permute-start(bf16[384,128]{1,0:T(8,128)(2,1)S(1)} %join.1.payload_ref.refs_0_), channel_id=1, source_target_pairs={{0,12},{1,13},{2,14},{3,15},{4,8},{5,9},{6,10},{7,11},{8,4},{9,5},... | collective-permute-start | bytes 294920 | tf_op jit(solution)/shard_map/ppermute | solution.py:441
  11.3 4.6 %collective-permute-done.1.refs_1_.refs_0_ = bf16[384,128]{1,0:T(8,128)(2,1)S(1)} collective-permute-done((bf16[384,128]{1,0:T(8,128)(2,1)S(1)}, bf16[384,128]{1,0:T(8,128)(2,1)S(1)}, u32[]{:S(2)}, u32[]{:S(2)}) %collective-permute-start.1) | collective-permute-done | bytes 98336 | tf_op jit(solution)/shard_map/ppermute | solution.py:441
  15.9 1.6 %setup.2 = (s32[8,128]{1,0:T(8,128)S(4)}, s32[8,128]{1,0:T(8,128)S(4)}, f32[64,128]{1,0:T(8,128)S(1)}, s32[544,128]{1,0:T(8,128)S(1)}, f32[544,128]{1,0:T(8,128)...) custom-call(bf16[384,128]{1,0:T(8,128)(2,1)S(1)} %join.1.payload_ref, ...), custom_call_target="tpu_custom_call" | custom-call | tf_op jit(solution)/shard_map/setup/pallas_call | solution.py:428
  17.5 1.3 %forward.10.refs_5_ = f32[512,128]{1,0:T(8,128)S(1)} custom-call(s32[8,128]{1,0:T(8,128)S(4)} %get-tuple-element.32.slots, bf16[384,128]{1,0:T(8,128)(2,1)S(1)} %join.1.payload_ref.refs_0_, s32[544,128]{1,0:T(8,128)S(1)} %get-tuple-element.34.refs_1_, f32[544,128]{1,0:T(8,128)S(1)} %get-tuple-element.35.refs_2_, f32[544,128]{1,0:T(8,128)S(1)} %get-tuple-element.36.refs_3_, ...), custom_call_target="tpu_custom_call" | custom-call | tf_op jit(solution)/shard_map/forward/pallas_call | solution.py:428
  18.8 1.1 %forward.11.refs_2_.refs_5_ = f32[512,128]{1,0:T(8,128)S(1)} custom-call(s32[8,128]{1,0:T(8,128)S(4)} %get-tuple-element.33.slots, bf16[384,128]{1,0:T(8,128)(2,1)S(1)} %collective-permute-done.1.refs_1_.refs_0_, s32[544,128]{1,0:T(8,128)S(1)} %get-tuple-element.34.refs_1_, f32[544,128]{1,0:T(8,128)S(1)} %get-tuple-element.35.refs_2_, ...), custom_call_target="tpu_custom_call" | custom-call | tf_op jit(solution)/shard_map/forward/pallas_call | solution.py:428
  20.0 1.7 %setup.3 = (s32[8,128]{1,0:T(8,128)S(4)}, s32[8,128]{1,0:T(8,128)S(4)}, s32[8,128]{1,0:T(8,128)S(4)}, f32[64,128]{1,0:T(8,128)S(1)}, s32[544,128]{1,0:T(8,128)S(...) custom-call(bf16[384,128]{1,0:T(8,128)(2,1)S(1)} %collective-permute, ...), custom_call_target="tpu_custom_call" | custom-call | tf_op jit(solution)/shard_map/setup/pallas_call | solution.py:428
  21.6 0.7 forward.12.refs_5_
  27.6 3.1 %collective-permute-start.7 = (bf16[256,128]{1,0:T(8,128)(2,1)S(1)}, bf16[256,128]{1,0:T(8,128)(2,1)S(1)}, u32[]{:S(2)}, u32[]{:S(2)}) collective-permute-start(bf16[256,128]{1,0:T(8,128)(2,1)S(1)} %backward.13), channel_id=1, source_target_pairs={{0,12},{1,13},{2,14},{3,15},{4,8},{5,9},{6,10},{7,11},{8,4},{9,5},... | collective-permute-start | bytes 196616 | tf_op jit(solution)/shard_map/ppermute | solution.py:441
  30.7 0.9 %backward.11 = bf16[256,128]{1,0:T(8,128)(2,1)S(1)} custom-call(s32[8,128]{1,0:T(8,128)S(4)} %get-tuple-element.33.slots, bf16[256,128]{1,0:T(8,128)(2,1)S(1)} %residual.2.refs_0_, bf16[256,128]{1,0:T(8,128)(2,1)S(1)} %collective-permute-done.5.refs_1_.refs_0_, s32[544,128]{1,0:T(8,128)S(1)} %get-tuple-element.47.refs_2_, ...), custom_call_target="tpu_custom_call" | custom-call | tf_op jit(solution)/shard_map/backward/pallas_call | solution.py:428
  32.3 1.1 %backward.10.sum_ref = f32[256,128]{1,0:T(8,128)S(1)} custom-call(s32[8,128]{1,0:T(8,128)S(4)} %get-tuple-element.32.slots, bf16[256,128]{1,0:T(8,128)(2,1)S(1)} %residual.2.refs_0_, bf16[256,128]{1,0:T(8,128)(2,1)S(1)} %collective-permute-done.5.refs_1_.refs_0_, s32[544,128]{1,0:T(8,128)S(1)} %get-tuple-element.47.refs_2_, ...), custom_call_target="tpu_custom_call" | custom-call | tf_op jit(solution)/shard_map/backward/pallas_call | solution.py:428
  33.4 0.8 %collective-permute-done.7.refs_1_ = bf16[256,128]{1,0:T(8,128)(2,1)S(1)} collective-permute-done((bf16[256,128]{1,0:T(8,128)(2,1)S(1)}, bf16[256,128]{1,0:T(8,128)(2,1)S(1)}, u32[]{:S(2)}, u32[]{:S(2)}) %collective-permute-start.7) | collective-permute-done | bytes 65568 | tf_op jit(solution)/shard_map/ppermute | solution.py:441
  34.2 4.3 %collective-permute-done.6.refs_0_ = bf16[256,128]{1,0:T(8,128)(2,1)S(1)} collective-permute-done((bf16[256,128]{1,0:T(8,128)(2,1)S(1)}, bf16[256,128]{1,0:T(8,128)(2,1)S(1)}, u32[]{:S(2)}, u32[]{:S(2)}) %collective-permute-start.6) | collective-permute-done | bytes 65568 | tf_op jit(solution)/shard_map/ppermute | solution.py:441
  38.6 1.7 %collective-permute-start.9 = (bf16[256,128]{1,0:T(8,128)(2,1)S(1)}, bf16[256,128]{1,0:T(8,128)(2,1)S(1)}, u32[]{:S(2)}, u32[]{:S(2)}) collective-permute-start(bf16[256,128]{1,0:T(8,128)(2,1)S(1)} %get-tuple-element.54), channel_id=1, source_target_pairs={{0,2},{1,3},{2,0},{3,1},{4,6},{5,7},{6,4},{7,5},{8,10},{9,11},{10,... | collective-permute-start | bytes 196616 | tf_op jit(solution)/shard_map/ppermute | solution.py:441
  40.2 1.0 %column_weight.1.column_ref = f32[256,128]{1,0:T(8,128)S(1)} custom-call(bf16[384,128]{1,0:T(8,128)(2,1)S(1)} %join.1.payload_ref.refs_0_), custom_call_target="tpu_custom_call" | custom-call | tf_op jit(solution)/shard_map/column_weight/pallas_call | solution.py:428
  41.2 1.7 %collective-permute-done.9.got_ref = bf16[256,128]{1,0:T(8,128)(2,1)S(1)} collective-permute-done((bf16[256,128]{1,0:T(8,128)(2,1)S(1)}, bf16[256,128]{1,0:T(8,128)(2,1)S(1)}, u32[]{:S(2)}, u32[]{:S(2)}) %collective-permute-start.9) | collective-permute-done | bytes 65568 | tf_op jit(solution)/shard_map/ppermute | solution.py:441
  44.0 2.4 %collective-permute-start.11 = (bf16[256,128]{1,0:T(8,128)(2,1)S(1)}, bf16[256,128]{1,0:T(8,128)(2,1)S(1)}, u32[]{:S(2)}, u32[]{:S(2)}) collective-permute-start(bf16[256,128]{1,0:T(8,128)(2,1)S(1)} %get-tuple-element.56.refs_0_), channel_id=1, source_target_pairs={{0,4},{1,5},{2,6},{3,7},{4,0},{5,1},{6,2},{7,3},{8,12},{9,13},{10,... | collective-permute-start | bytes 196616 | tf_op jit(solution)/shard_map/ppermute | solution.py:441
  46.4 1.6 %collective-permute-start.10 = (bf16[256,128]{1,0:T(8,128)(2,1)S(1)}, bf16[256,128]{1,0:T(8,128)(2,1)S(1)}, u32[]{:S(2)}, u32[]{:S(2)}) collective-permute-start(bf16[256,128]{1,0:T(8,128)(2,1)S(1)} %get-tuple-element.56.refs_0_), channel_id=1, source_target_pairs={{0,12},{1,13},{2,14},{3,15},{4,8},{5,9},{6,10},{7,11},{8,4},{9,5},... | collective-permute-start | bytes 196616 | tf_op jit(solution)/shard_map/ppermute | solution.py:441
  47.9 1.3 %forward.15.refs_5_ = f32[512,128]{1,0:T(8,128)S(1)} custom-call(s32[8,128]{1,0:T(8,128)S(4)} %get-tuple-element.32.slots, bf16[256,128]{1,0:T(8,128)(2,1)S(1)} %get-tuple-element.56.refs_0_, s32[544,128]{1,0:T(8,128)S(1)} %get-tuple-element.34.refs_1_, f32[544,128]{1,0:T(8,128)S(1)} %get-tuple-element.35.refs_2_, f32[544,128]{1,0:T(8,128)S(1)} %get-tuple-element.36.refs_3_, ...), custom_call_target="tpu_custom_call" | custom-call | tf_op jit(solution)/shard_map/forward/pallas_call | solution.py:428
  49.8 1.1 %forward.16.refs_5_ = f32[512,128]{1,0:T(8,128)S(1)} custom-call(s32[8,128]{1,0:T(8,128)S(4)} %get-tuple-element.33.slots, bf16[256,128]{1,0:T(8,128)(2,1)S(1)} %collective-permute-done.12.refs_0_, s32[544,128]{1,0:T(8,128)S(1)} %get-tuple-element.34.refs_1_, f32[544,128]{1,0:T(8,128)S(1)} %get-tuple-element.35.refs_2_, ...), custom_call_target="tpu_custom_call" | custom-call | tf_op jit(solution)/shard_map/forward/pallas_call | solution.py:428
  50.9 0.7 forward.17.refs_5_
  51.6 0.8 %collective-permute-done.10.refs_0_ = bf16[256,128]{1,0:T(8,128)(2,1)S(1)} collective-permute-done((bf16[256,128]{1,0:T(8,128)(2,1)S(1)}, bf16[256,128]{1,0:T(8,128)(2,1)S(1)}, u32[]{:S(2)}, u32[]{:S(2)}) %collective-permute-start.10) | collective-permute-done | bytes 65568 | tf_op jit(solution)/shard_map/ppermute | solution.py:441
  57.1 1.8 %collective-permute-start.16 = (bf16[256,128]{1,0:T(8,128)(2,1)S(1)}, bf16[256,128]{1,0:T(8,128)(2,1)S(1)}, u32[]{:S(2)}, u32[]{:S(2)}) collective-permute-start(bf16[256,128]{1,0:T(8,128)(2,1)S(1)} %backward.18), channel_id=1, source_target_pairs={{0,12},{1,13},{2,14},{3,15},{4,8},{5,9},{6,10},{7,11},{8,4},{9,5},... | collective-permute-start | bytes 196616 | tf_op jit(solution)/shard_map/ppermute | solution.py:441
  58.9 0.9 %backward.16 = bf16[256,128]{1,0:T(8,128)(2,1)S(1)} custom-call(s32[8,128]{1,0:T(8,128)S(4)} %get-tuple-element.33.slots, bf16[256,128]{1,0:T(8,128)(2,1)S(1)} %residual.3.refs_0_, bf16[256,128]{1,0:T(8,128)(2,1)S(1)} %collective-permute-done.14.refs_1_.refs_0_, s32[544,128]{1,0:T(8,128)S(1)} %get-tuple-element.47.refs_2_, ...), custom_call_target="tpu_custom_call" | custom-call | tf_op jit(solution)/shard_map/backward/pallas_call | solution.py:428
  59.8 2.0 %collective-permute-start.15 = (bf16[256,128]{1,0:T(8,128)(2,1)S(1)}, bf16[256,128]{1,0:T(8,128)(2,1)S(1)}, u32[]{:S(2)}, u32[]{:S(2)}) collective-permute-start(bf16[256,128]{1,0:T(8,128)(2,1)S(1)} %backward.16), channel_id=1, source_target_pairs={{0,8},{1,9},{2,10},{3,11},{4,12},{5,13},{6,14},{7,15},{8,0},{9,1},... | collective-permute-start | bytes 196616 | tf_op jit(solution)/shard_map/ppermute | solution.py:441
  61.8 1.1 %backward.15.sum_ref = f32[256,128]{1,0:T(8,128)S(1)} custom-call(s32[8,128]{1,0:T(8,128)S(4)} %get-tuple-element.32.slots, bf16[256,128]{1,0:T(8,128)(2,1)S(1)} %residual.3.refs_0_, bf16[256,128]{1,0:T(8,128)(2,1)S(1)} %collective-permute-done.14.refs_1_.refs_0_, s32[544,128]{1,0:T(8,128)S(1)} %get-tuple-element.47.refs_2_, ...), custom_call_target="tpu_custom_call" | custom-call | tf_op jit(solution)/shard_map/backward/pallas_call | solution.py:428
  63.4 3.5 %collective-permute-done.15.refs_0_ = bf16[256,128]{1,0:T(8,128)(2,1)S(1)} collective-permute-done((bf16[256,128]{1,0:T(8,128)(2,1)S(1)}, bf16[256,128]{1,0:T(8,128)(2,1)S(1)}, u32[]{:S(2)}, u32[]{:S(2)}) %collective-permute-start.15) | collective-permute-done | bytes 65568 | tf_op jit(solution)/shard_map/ppermute | solution.py:441
  66.9 2.1 %collective-permute-start.18 = (bf16[128,128]{1,0:T(8,128)(2,1)S(1)}, bf16[128,128]{1,0:T(8,128)(2,1)S(1)}, u32[]{:S(2)}, u32[]{:S(2)}) collective-permute-start(bf16[128,128]{1,0:T(8,128)(2,1)S(1)} %get-tuple-element.58), channel_id=1, source_target_pairs={{0,2},{1,3},{2,0},{3,1},{4,6},{5,7},{6,4},{7,5},{8,10},{9,11},{10,... | collective-permute-start | bytes 98312 | tf_op jit(solution)/shard_map/ppermute | solution.py:441
  69.0 1.9 %collective-permute-done.18.got_ref = bf16[128,128]{1,0:T(8,128)(2,1)S(1)} collective-permute-done((bf16[128,128]{1,0:T(8,128)(2,1)S(1)}, bf16[128,128]{1,0:T(8,128)(2,1)S(1)}, u32[]{:S(2)}, u32[]{:S(2)}) %collective-permute-start.18) | collective-permute-done | bytes 32800 | tf_op jit(solution)/shard_map/ppermute | solution.py:441
  (41 shorter events, 13.6 us)
Async XLA Ops:
  1.1 5.5 %collective-permute-start = (bf16[320,128]{1,0:T(8,128)(2,1)S(1)}, bf16[320,128]{1,0:T(8,128)(2,1)S(1)}, u32[]{:S(2)}, u32[]{:S(2)}) collective-permute-start(bf16[320,128]{1,0:T(8,128)(2,1)S(1)} %pack.1.refs_0_), channel_id=1, source_target_pairs={{0,2},{1,3},{2,0},{3,1},{4,6},{5,7},{6,4},{7,5},{8,10},{9,11},{10,... | collective-permute-start | bytes 245768 | tf_op jit(solution)/shard_map/ppermute | solution.py:441
  6.5 9.4 %collective-permute-start.1 = (bf16[384,128]{1,0:T(8,128)(2,1)S(1)}, bf16[384,128]{1,0:T(8,128)(2,1)S(1)}, u32[]{:S(2)}, u32[]{:S(2)}) collective-permute-start(bf16[384,128]{1,0:T(8,128)(2,1)S(1)} %join.1.payload_ref.refs_0_), channel_id=1, source_target_pairs={{0,8},{1,9},{2,10},{3,11},{4,12},{5,13},{6,14},{7,15},{8,0},{9,1},... | collective-permute-start | bytes 294920 | tf_op jit(solution)/shard_map/ppermute | solution.py:441
  9.7 10.3 %collective-permute-start.3 = (bf16[384,128]{1,0:T(8,128)(2,1)S(1)}, bf16[384,128]{1,0:T(8,128)(2,1)S(1)}, u32[]{:S(2)}, u32[]{:S(2)}) collective-permute-start(bf16[384,128]{1,0:T(8,128)(2,1)S(1)} %join.1.payload_ref.refs_0_), channel_id=1, source_target_pairs={{0,12},{1,13},{2,14},{3,15},{4,8},{5,9},{6,10},{7,11},{8,4},{9,5},... | collective-permute-start | bytes 294920 | tf_op jit(solution)/shard_map/ppermute | solution.py:441
  11.0 8.9 %collective-permute-start.2 = (bf16[384,128]{1,0:T(8,128)(2,1)S(1)}, bf16[384,128]{1,0:T(8,128)(2,1)S(1)}, u32[]{:S(2)}, u32[]{:S(2)}) collective-permute-start(bf16[384,128]{1,0:T(8,128)(2,1)S(1)} %join.1.payload_ref.refs_0_), channel_id=1, source_target_pairs={{0,4},{1,5},{2,6},{3,7},{4,0},{5,1},{6,2},{7,3},{8,12},{9,13},{10,... | collective-permute-start | bytes 294920 | tf_op jit(solution)/shard_map/ppermute | solution.py:441
  23.1 1.4 %collective-permute-start.4 = (f32[288,128]{1,0:T(8,128)S(1)}, f32[288,128]{1,0:T(8,128)S(1)}, u32[]{:S(2)}, u32[]{:S(2)}) collective-permute-start(f32[288,128]{1,0:T(8,128)S(1)} %forward.14), channel_id=1, source_target_pairs={{0,1},{1,0},{2,3},{3,2},{4,5},{5,4},{6,7},{7,6},{8,9},{9,8},{10,11... | collective-permute-start | bytes 442376 | tf_op jit(solution)/shard_map/ppermute | solution.py:441
  23.1 1.4 %copy-start = (bf16[32,8,128]{2,1,0:T(8,128)(2,1)S(1)}, bf16[32,8,128]{2,1,0:T(8,128)(2,1)}, u32[]{:S(2)}) copy-start(bf16[32,8,128]{2,1,0:T(8,128)(2,1)} %param.7) | copy-start | bytes 196612
  24.5 1.3 %collective-permute-start.5 = (bf16[256,128]{1,0:T(8,128)(2,1)S(1)}, bf16[256,128]{1,0:T(8,128)(2,1)S(1)}, u32[]{:S(2)}, u32[]{:S(2)}) collective-permute-start(bf16[256,128]{1,0:T(8,128)(2,1)S(1)} %residual.2.refs_0_), channel_id=1, source_target_pairs={{0,1},{1,0},{2,3},{3,2},{4,5},{5,4},{6,7},{7,6},{8,9},{9,8},{10,11... | collective-permute-start | bytes 196616 | tf_op jit(solution)/shard_map/ppermute | solution.py:441
  26.4 7.0 %collective-permute-start.8 = (bf16[256,128]{1,0:T(8,128)(2,1)S(1)}, bf16[256,128]{1,0:T(8,128)(2,1)S(1)}, u32[]{:S(2)}, u32[]{:S(2)}) collective-permute-start(bf16[256,128]{1,0:T(8,128)(2,1)S(1)} %backward.14), channel_id=1, source_target_pairs={{0,4},{1,5},{2,6},{3,7},{4,0},{5,1},{6,2},{7,3},{8,12},{9,13},{10,... | collective-permute-start | bytes 196616 | tf_op jit(solution)/shard_map/ppermute | solution.py:441
  27.6 6.5 %collective-permute-start.7 = (bf16[256,128]{1,0:T(8,128)(2,1)S(1)}, bf16[256,128]{1,0:T(8,128)(2,1)S(1)}, u32[]{:S(2)}, u32[]{:S(2)}) collective-permute-start(bf16[256,128]{1,0:T(8,128)(2,1)S(1)} %backward.13), channel_id=1, source_target_pairs={{0,12},{1,13},{2,14},{3,15},{4,8},{5,9},{6,10},{7,11},{8,4},{9,5},... | collective-permute-start | bytes 196616 | tf_op jit(solution)/shard_map/ppermute | solution.py:441
  31.7 6.8 %collective-permute-start.6 = (bf16[256,128]{1,0:T(8,128)(2,1)S(1)}, bf16[256,128]{1,0:T(8,128)(2,1)S(1)}, u32[]{:S(2)}, u32[]{:S(2)}) collective-permute-start(bf16[256,128]{1,0:T(8,128)(2,1)S(1)} %backward.11), channel_id=1, source_target_pairs={{0,8},{1,9},{2,10},{3,11},{4,12},{5,13},{6,14},{7,15},{8,0},{9,1},... | collective-permute-start | bytes 196616 | tf_op jit(solution)/shard_map/ppermute | solution.py:441
  38.5 4.3 %copy-start.1 = (f32[16,8,128]{2,1,0:T(8,128)S(1)}, f32[16,8,128]{2,1,0:T(8,128)}, u32[]{:S(2)}) copy-start(f32[16,8,128]{2,1,0:T(8,128)} %param.8) | copy-start | bytes 196612
  38.6 4.3 %collective-permute-start.9 = (bf16[256,128]{1,0:T(8,128)(2,1)S(1)}, bf16[256,128]{1,0:T(8,128)(2,1)S(1)}, u32[]{:S(2)}, u32[]{:S(2)}) collective-permute-start(bf16[256,128]{1,0:T(8,128)(2,1)S(1)} %get-tuple-element.54), channel_id=1, source_target_pairs={{0,2},{1,3},{2,0},{3,1},{4,6},{5,7},{6,4},{7,5},{8,10},{9,11},{10,... | collective-permute-start | bytes 196616 | tf_op jit(solution)/shard_map/ppermute | solution.py:441
  43.5 6.2 %collective-permute-start.12 = (bf16[256,128]{1,0:T(8,128)(2,1)S(1)}, bf16[256,128]{1,0:T(8,128)(2,1)S(1)}, u32[]{:S(2)}, u32[]{:S(2)}) collective-permute-start(bf16[256,128]{1,0:T(8,128)(2,1)S(1)} %get-tuple-element.56.refs_0_), channel_id=1, source_target_pairs={{0,8},{1,9},{2,10},{3,11},{4,12},{5,13},{6,14},{7,15},{8,0},{9,1},... | collective-permute-start | bytes 196616 | tf_op jit(solution)/shard_map/ppermute | solution.py:441
  44.0 6.9 %collective-permute-start.11 = (bf16[256,128]{1,0:T(8,128)(2,1)S(1)}, bf16[256,128]{1,0:T(8,128)(2,1)S(1)}, u32[]{:S(2)}, u32[]{:S(2)}) collective-permute-start(bf16[256,128]{1,0:T(8,128)(2,1)S(1)} %get-tuple-element.56.refs_0_), channel_id=1, source_target_pairs={{0,4},{1,5},{2,6},{3,7},{4,0},{5,1},{6,2},{7,3},{8,12},{9,13},{10,... | collective-permute-start | bytes 196616 | tf_op jit(solution)/shard_map/ppermute | solution.py:441
  46.4 6.1 %collective-permute-start.10 = (bf16[256,128]{1,0:T(8,128)(2,1)S(1)}, bf16[256,128]{1,0:T(8,128)(2,1)S(1)}, u32[]{:S(2)}, u32[]{:S(2)}) collective-permute-start(bf16[256,128]{1,0:T(8,128)(2,1)S(1)} %get-tuple-element.56.refs_0_), channel_id=1, source_target_pairs={{0,12},{1,13},{2,14},{3,15},{4,8},{5,9},{6,10},{7,11},{8,4},{9,5},... | collective-permute-start | bytes 196616 | tf_op jit(solution)/shard_map/ppermute | solution.py:441
  53.1 1.4 %collective-permute-start.13 = (f32[256,128]{1,0:T(8,128)S(1)}, f32[256,128]{1,0:T(8,128)S(1)}, u32[]{:S(2)}, u32[]{:S(2)}) collective-permute-start(f32[256,128]{1,0:T(8,128)S(1)} %forward.19), channel_id=1, source_target_pairs={{0,1},{1,0},{2,3},{3,2},{4,5},{5,4},{6,7},{7,6},{8,9},{9,8},{10,11... | collective-permute-start | bytes 393224 | tf_op jit(solution)/shard_map/ppermute | solution.py:441
  54.6 1.3 %collective-permute-start.14 = (bf16[256,128]{1,0:T(8,128)(2,1)S(1)}, bf16[256,128]{1,0:T(8,128)(2,1)S(1)}, u32[]{:S(2)}, u32[]{:S(2)}) collective-permute-start(bf16[256,128]{1,0:T(8,128)(2,1)S(1)} %residual.3.refs_0_), channel_id=1, source_target_pairs={{0,1},{1,0},{2,3},{3,2},{4,5},{5,4},{6,7},{7,6},{8,9},{9,8},{10,11... | collective-permute-start | bytes 196616 | tf_op jit(solution)/shard_map/ppermute | solution.py:441
  56.4 6.4 %collective-permute-start.17 = (bf16[256,128]{1,0:T(8,128)(2,1)S(1)}, bf16[256,128]{1,0:T(8,128)(2,1)S(1)}, u32[]{:S(2)}, u32[]{:S(2)}) collective-permute-start(bf16[256,128]{1,0:T(8,128)(2,1)S(1)} %backward.19), channel_id=1, source_target_pairs={{0,4},{1,5},{2,6},{3,7},{4,0},{5,1},{6,2},{7,3},{8,12},{9,13},{10,... | collective-permute-start | bytes 196616 | tf_op jit(solution)/shard_map/ppermute | solution.py:441
  57.1 6.3 %collective-permute-start.16 = (bf16[256,128]{1,0:T(8,128)(2,1)S(1)}, bf16[256,128]{1,0:T(8,128)(2,1)S(1)}, u32[]{:S(2)}, u32[]{:S(2)}) collective-permute-start(bf16[256,128]{1,0:T(8,128)(2,1)S(1)} %backward.18), channel_id=1, source_target_pairs={{0,12},{1,13},{2,14},{3,15},{4,8},{5,9},{6,10},{7,11},{8,4},{9,5},... | collective-permute-start | bytes 196616 | tf_op jit(solution)/shard_map/ppermute | solution.py:441
  59.8 7.0 %collective-permute-start.15 = (bf16[256,128]{1,0:T(8,128)(2,1)S(1)}, bf16[256,128]{1,0:T(8,128)(2,1)S(1)}, u32[]{:S(2)}, u32[]{:S(2)}) collective-permute-start(bf16[256,128]{1,0:T(8,128)(2,1)S(1)} %backward.16), channel_id=1, source_target_pairs={{0,8},{1,9},{2,10},{3,11},{4,12},{5,13},{6,14},{7,15},{8,0},{9,1},... | collective-permute-start | bytes 196616 | tf_op jit(solution)/shard_map/ppermute | solution.py:441
  66.9 4.0 %collective-permute-start.18 = (bf16[128,128]{1,0:T(8,128)(2,1)S(1)}, bf16[128,128]{1,0:T(8,128)(2,1)S(1)}, u32[]{:S(2)}, u32[]{:S(2)}) collective-permute-start(bf16[128,128]{1,0:T(8,128)(2,1)S(1)} %get-tuple-element.58), channel_id=1, source_target_pairs={{0,2},{1,3},{2,0},{3,1},{4,6},{5,7},{6,4},{7,5},{8,10},{9,11},{10,... | collective-permute-start | bytes 98312 | tf_op jit(solution)/shard_map/ppermute | solution.py:441

commit v15 on v13

--- a/solution.py
+++ b/solution.py
@@ -8,7 +8,7 @@
 from jax.sharding import PartitionSpec as P
 
 ITERS = 2
-CHUNK = 8
+CHUNK = 16
 F32 = jnp.float32
 BF16 = jnp.bfloat16
 I32 = jnp.int32

time: 65.4 us -> 65.3 us (level); the launches traced: 65.8 us -> 64.9 us
  waiting for transfers between devices: 13.3 us -> 15.9 us
  Pallas kernels: 22.4 us -> 20.3 us
  starting transfers between devices: 29.8 us -> 28.4 us
    ppermute x24, waiting for transfers between devices: 13.3 us -> 15.9 us  [exchange(): lax.ppermute(values, 'slab', [(device, device ^ far[device % 2]) for devi...]
    pallas_call x28, Pallas kernels: 22.4 us -> 20.3 us  [call(): pl.pallas_call(kernel, out_shape=out_shape, in_specs=in_specs, out_specs=...]
    ppermute x24, starting transfers between devices: 29.8 us -> 28.4 us  [exchange(): lax.ppermute(values, 'slab', [(device, device ^ far[device % 2]) for devi...]
  transfers between devices with their start and end apart: 24 -> 24, of which waited for: 12 -> 17; matrix products, arithmetic and copies ran while one was open for 0% -> 0% of each run, Pallas kernels for 24% -> 20%
where the time goes in v15:
time: 65.3 us; the launch traced here: 64.9 us
  starting transfers between devices  28.4 us (43%)
  Pallas kernels  20.3 us (31%)
  waiting for transfers between devices  15.9 us (24%)
    ppermute x24, starting transfers between devices, exchange(): lax.ppermute(values, 'slab', [(device, device ^ far[device % 2]) for devi...  28.4 us
    pallas_call x28, Pallas kernels, call(): pl.pallas_call(kernel, out_shape=out_shape, in_specs=in_specs, out_specs=...  20.3 us
    ppermute x24, waiting for transfers between devices, exchange(): lax.ppermute(values, 'slab', [(device, device ^ far[device % 2]) for devi...  15.9 us
  transfers between devices with their start and end apart: 24, of which 17 were waited for; matrix products, arithmetic and copies ran while one was open for 0% of the time, Pallas kernels for 20%

profile of v15, /device:TPU:0, one launch (start us, length us, event | category | flops | bytes accessed | tf_op | source)
XLA Modules:
  0.0 64.9 jit_solution(8650227268169948547)
XLA Ops:
  0.0 1.0 %pack.1.refs_0_ = bf16[192,128]{1,0:T(8,128)(2,1)S(1)} custom-call(f32[128,128]{1,0:T(8,128)} %bitcast.10, f32[4,256]{1,0:T(4,128)} %bitcast.12, f32[4,256]{1,0:T(4,128)} %bitcast.14, s32[4,256]{1,0:T(4,128)} %bitcast.16, s32[1,256]{1,0:T(1,128)} %bitcast.20, s32[1,16]{1,0:T(1,128)} %bitcast.18), custom_call_target="tpu_custom_call" | custom-call | tf_op jit(solution)/shard_map/pack/pallas_call | solution.py:403
  1.0 5.1 %collective-permute-start.1 = (bf16[192,128]{1,0:T(8,128)(2,1)S(1)}, bf16[192,128]{1,0:T(8,128)(2,1)S(1)}, u32[]{:S(2)}, u32[]{:S(2)}) collective-permute-start(bf16[192,128]{1,0:T(8,128)(2,1)S(1)} %pack.1.refs_0_), channel_id=1, source_target_pairs={{0,12},{1,5},{2,14},{3,7},{4,8},{5,1},{6,10},{7,3},{8,4},{9,13},{1... | collective-permute-start | bytes 147464 | tf_op jit(solution)/shard_map/ppermute | solution.py:417
  6.8 1.9 %collective-permute-done.1.refs_0_ = bf16[192,128]{1,0:T(8,128)(2,1)S(1)} collective-permute-done((bf16[192,128]{1,0:T(8,128)(2,1)S(1)}, bf16[192,128]{1,0:T(8,128)(2,1)S(1)}, u32[]{:S(2)}, u32[]{:S(2)}) %collective-permute-start.1) | collective-permute-done | bytes 49184 | tf_op jit(solution)/shard_map/ppermute | solution.py:417
  8.7 1.6 %collective-permute-done.2.refs_1_ = bf16[192,128]{1,0:T(8,128)(2,1)S(1)} collective-permute-done((bf16[192,128]{1,0:T(8,128)(2,1)S(1)}, bf16[192,128]{1,0:T(8,128)(2,1)S(1)}, u32[]{:S(2)}, u32[]{:S(2)}) %collective-permute-start.2) | collective-permute-done | bytes 49184 | tf_op jit(solution)/shard_map/ppermute | solution.py:417
  10.3 1.6 %collective-permute-start.4 = (bf16[384,128]{1,0:T(8,128)(2,1)S(1)}, bf16[384,128]{1,0:T(8,128)(2,1)S(1)}, u32[]{:S(2)}, u32[]{:S(2)}) collective-permute-start(bf16[384,128]{1,0:T(8,128)(2,1)S(1)} %join.5.refs_1_), channel_id=1, source_target_pairs={{0,2},{1,3},{2,0},{3,1},{4,6},{5,7},{6,4},{7,5},{8,10},{9,11},{10,... | collective-permute-start | bytes 294920 | tf_op jit(solution)/shard_map/ppermute | solution.py:417
  11.9 1.2 %collective-permute-start.3 = (bf16[384,128]{1,0:T(8,128)(2,1)S(1)}, bf16[384,128]{1,0:T(8,128)(2,1)S(1)}, u32[]{:S(2)}, u32[]{:S(2)}) collective-permute-start(bf16[384,128]{1,0:T(8,128)(2,1)S(1)} %join.4.refs_0_), channel_id=1, source_target_pairs={{0,2},{1,3},{2,0},{3,1},{4,6},{5,7},{6,4},{7,5},{8,10},{9,11},{10,... | collective-permute-start | bytes 294920 | tf_op jit(solution)/shard_map/ppermute | solution.py:417
  13.0 1.5 %setup.2 = (s32[8,128]{1,0:T(8,128)S(4)}, f32[64,128]{1,0:T(8,128)S(1)}, s32[544,128]{1,0:T(8,128)S(1)}, f32[544,128]{1,0:T(8,128)S(1)}, f32[544,128]{1,0:T(8,12...) custom-call(bf16[384,128]{1,0:T(8,128)(2,1)S(1)} %join.4.refs_0_, ...), custom_call_target="tpu_custom_call" | custom-call | tf_op jit(solution)/shard_map/setup/pallas_call | solution.py:403
  14.5 1.8 %forward.6.refs_2_.refs_6_ = f32[512,128]{1,0:T(8,128)S(1)} custom-call(s32[8,128]{1,0:T(8,128)S(4)} %get-tuple-element.38.slots, bf16[384,128]{1,0:T(8,128)(2,1)S(1)} %join.4.refs_0_, bf16[384,128]{1,0:T(8,128)(2,1)S(1)} %join.5.refs_1_, s32[544,128]{1,0:T(8,128)S(1)} %get-tuple-element.39.refs_2_, f32[544,128]{1,0:T(8,128)S(1)} %get-tuple-element.40.refs_3_, ...), custom_call_target="tpu_custom_call" | custom-call | tf_op jit(solution)/shard_map/forward/pallas_call | solution.py:403
  16.6 1.6 %setup.3 = (s32[8,128]{1,0:T(8,128)S(4)}, s32[8,128]{1,0:T(8,128)S(4)}, f32[64,128]{1,0:T(8,128)S(1)}, s32[544,128]{1,0:T(8,128)S(1)}, f32[544,128]{1,0:T(8,128)...) custom-call(bf16[384,128]{1,0:T(8,128)(2,1)S(1)} %collective-permute, ...), custom_call_target="tpu_custom_call" | custom-call | tf_op jit(solution)/shard_map/setup/pallas_call | solution.py:403
  18.2 1.1 %forward.8 = f32[288,128]{1,0:T(8,128)S(1)} custom-call(s32[8,128]{1,0:T(8,128)S(4)} %get-tuple-element.50.slots, bf16[384,128]{1,0:T(8,128)(2,1)S(1)} %collective-permute-done.3.refs_0_, bf16[384,128]{1,0:T(8,128)(2,1)S(1)} %collective-permute-done.4.refs_1_, s32[544,128]{1,0:T(8,128)S(1)} %get-tuple-element.44.refs_2_, ...), custom_call_target="tpu_custom_call" | custom-call | tf_op jit(solution)/shard_map/forward/pallas_call | solution.py:403
  19.4 1.1 %forward.7.projection_ref = f32[256,128]{1,0:T(8,128)S(1)} custom-call(s32[8,128]{1,0:T(8,128)S(4)} %get-tuple-element.43.slots, bf16[384,128]{1,0:T(8,128)(2,1)S(1)} %collective-permute-done.3.refs_0_, bf16[384,128]{1,0:T(8,128)(2,1)S(1)} %collective-permute-done.4.refs_1_, s32[544,128]{1,0:T(8,128)S(1)} %get-tuple-element.44.refs_2_, ...), custom_call_target="tpu_custom_call" | custom-call | tf_op jit(solution)/shard_map/forward/pallas_call | solution.py:403
  23.0 1.6 %collective-permute-start.8 = (bf16[256,128]{1,0:T(8,128)(2,1)S(1)}, bf16[256,128]{1,0:T(8,128)(2,1)S(1)}, u32[]{:S(2)}, u32[]{:S(2)}) collective-permute-start(bf16[256,128]{1,0:T(8,128)(2,1)S(1)} %get-tuple-element.59), channel_id=1, source_target_pairs={{0,2},{1,3},{2,0},{3,1},{4,6},{5,7},{6,4},{7,5},{8,10},{9,11},{10,... | collective-permute-start | bytes 196616 | tf_op jit(solution)/shard_map/ppermute | solution.py:417
  25.1 1.5 %backward.6.sum_ref = f32[512,128]{1,0:T(8,128)S(1)} custom-call(s32[8,128]{1,0:T(8,128)S(4)} %get-tuple-element.38.slots, bf16[256,128]{1,0:T(8,128)(2,1)S(1)} %residual.2.refs_0_, bf16[256,128]{1,0:T(8,128)(2,1)S(1)} %collective-permute-done.6.refs_1_.refs_0_, s32[544,128]{1,0:T(8,128)S(1)} %get-tuple-element.51.refs_2_, ...), custom_call_target="tpu_custom_call" | custom-call | tf_op jit(solution)/shard_map/backward/pallas_call | solution.py:403
  26.6 1.1 %collective-permute-done.8.y_ref = bf16[256,128]{1,0:T(8,128)(2,1)S(1)} collective-permute-done((bf16[256,128]{1,0:T(8,128)(2,1)S(1)}, bf16[256,128]{1,0:T(8,128)(2,1)S(1)}, u32[]{:S(2)}, u32[]{:S(2)}) %collective-permute-start.8) | collective-permute-done | bytes 65568 | tf_op jit(solution)/shard_map/ppermute | solution.py:417
  27.8 2.2 %collective-permute-start.10 = (bf16[128,128]{1,0:T(8,128)(2,1)S(1)}, bf16[128,128]{1,0:T(8,128)(2,1)S(1)}, u32[]{:S(2)}, u32[]{:S(2)}) collective-permute-start(bf16[128,128]{1,0:T(8,128)(2,1)S(1)} %get-tuple-element.61), channel_id=1, source_target_pairs={{0,12},{1,5},{2,14},{3,7},{4,8},{5,1},{6,10},{7,3},{8,4},{9,13},{1... | collective-permute-start | bytes 98312 | tf_op jit(solution)/shard_map/ppermute | solution.py:417
  30.3 2.0 %collective-permute-start.11 = (bf16[128,128]{1,0:T(8,128)(2,1)S(1)}, bf16[128,128]{1,0:T(8,128)(2,1)S(1)}, u32[]{:S(2)}, u32[]{:S(2)}) collective-permute-start(bf16[128,128]{1,0:T(8,128)(2,1)S(1)} %get-tuple-element.62), channel_id=1, source_target_pairs={{0,4},{1,9},{2,6},{3,11},{4,0},{5,13},{6,2},{7,15},{8,12},{9,1},{1... | collective-permute-start | bytes 98312 | tf_op jit(solution)/shard_map/ppermute | solution.py:417
  33.9 1.0 %collective-permute-done.9.refs_1_ = bf16[128,128]{1,0:T(8,128)(2,1)S(1)} collective-permute-done((bf16[128,128]{1,0:T(8,128)(2,1)S(1)}, bf16[128,128]{1,0:T(8,128)(2,1)S(1)}, u32[]{:S(2)}, u32[]{:S(2)}) %collective-permute-start.9) | collective-permute-done | bytes 32800 | tf_op jit(solution)/shard_map/ppermute | solution.py:417
  34.9 2.2 %collective-permute-start.14 = (bf16[128,128]{1,0:T(8,128)(2,1)S(1)}, bf16[128,128]{1,0:T(8,128)(2,1)S(1)}, u32[]{:S(2)}, u32[]{:S(2)}) collective-permute-start(bf16[128,128]{1,0:T(8,128)(2,1)S(1)} %get-tuple-element.64.refs_0_), channel_id=1, source_target_pairs={{0,12},{1,5},{2,14},{3,7},{4,8},{5,1},{6,10},{7,3},{8,4},{9,13},{1... | collective-permute-start | bytes 98312 | tf_op jit(solution)/shard_map/ppermute | solution.py:417
  37.6 1.7 %collective-permute-start.12 = (bf16[128,128]{1,0:T(8,128)(2,1)S(1)}, bf16[128,128]{1,0:T(8,128)(2,1)S(1)}, u32[]{:S(2)}, u32[]{:S(2)}) collective-permute-start(bf16[128,128]{1,0:T(8,128)(2,1)S(1)} %get-tuple-element.64.refs_0_), channel_id=1, source_target_pairs={{0,8},{1,13},{2,10},{3,15},{4,12},{5,9},{6,14},{7,11},{8,0},{9,5},... | collective-permute-start | bytes 98312 | tf_op jit(solution)/shard_map/ppermute | solution.py:417
  39.4 1.3 %collective-permute-done.14.refs_0_ = bf16[128,128]{1,0:T(8,128)(2,1)S(1)} collective-permute-done((bf16[128,128]{1,0:T(8,128)(2,1)S(1)}, bf16[128,128]{1,0:T(8,128)(2,1)S(1)}, u32[]{:S(2)}, u32[]{:S(2)}) %collective-permute-start.14) | collective-permute-done | bytes 32800 | tf_op jit(solution)/shard_map/ppermute | solution.py:417
  41.1 1.7 %collective-permute-start.16 = (bf16[256,128]{1,0:T(8,128)(2,1)S(1)}, bf16[256,128]{1,0:T(8,128)(2,1)S(1)}, u32[]{:S(2)}, u32[]{:S(2)}) collective-permute-start(bf16[256,128]{1,0:T(8,128)(2,1)S(1)} %join.7.refs_1_), channel_id=1, source_target_pairs={{0,2},{1,3},{2,0},{3,1},{4,6},{5,7},{6,4},{7,5},{8,10},{9,11},{10,... | collective-permute-start | bytes 196616 | tf_op jit(solution)/shard_map/ppermute | solution.py:417
  43.4 1.8 %forward.9.refs_6_ = f32[512,128]{1,0:T(8,128)S(1)} custom-call(s32[8,128]{1,0:T(8,128)S(4)} %get-tuple-element.38.slots, bf16[256,128]{1,0:T(8,128)(2,1)S(1)} %join.6.refs_0_, bf16[256,128]{1,0:T(8,128)(2,1)S(1)} %join.7.refs_1_, s32[544,128]{1,0:T(8,128)S(1)} %get-tuple-element.39.refs_2_, f32[544,128]{1,0:T(8,128)S(1)} %get-tuple-element.40.refs_3_, ...), custom_call_target="tpu_custom_call" | custom-call | tf_op jit(solution)/shard_map/forward/pallas_call | solution.py:403
  45.5 1.7 %collective-permute-done.13.refs_0_ = bf16[256,128]{1,0:T(8,128)(2,1)S(1)} collective-permute-done((bf16[256,128]{1,0:T(8,128)(2,1)S(1)}, bf16[256,128]{1,0:T(8,128)(2,1)S(1)}, u32[]{:S(2)}, u32[]{:S(2)}) %collective-permute-start.13) | collective-permute-done | bytes 65568 | tf_op jit(solution)/shard_map/ppermute | solution.py:417
  47.2 1.1 %forward.11 = f32[256,128]{1,0:T(8,128)S(1)} custom-call(s32[8,128]{1,0:T(8,128)S(4)} %get-tuple-element.50.slots, bf16[256,128]{1,0:T(8,128)(2,1)S(1)} %collective-permute-done.13.refs_0_, bf16[256,128]{1,0:T(8,128)(2,1)S(1)} %collective-permute-done.16.refs_1_, s32[544,128]{1,0:T(8,128)S(1)} %get-tuple-element.44.refs_2_, ...), custom_call_target="tpu_custom_call" | custom-call | tf_op jit(solution)/shard_map/forward/pallas_call | solution.py:403
  48.3 1.1 %forward.10.projection_ref = f32[256,128]{1,0:T(8,128)S(1)} custom-call(s32[8,128]{1,0:T(8,128)S(4)} %get-tuple-element.43.slots, bf16[256,128]{1,0:T(8,128)(2,1)S(1)} %collective-permute-done.13.refs_0_, bf16[256,128]{1,0:T(8,128)(2,1)S(1)} %collective-permute-done.16.refs_1_, s32[544,128]{1,0:T(8,128)S(1)} %get-tuple-element.44.refs_2_, ...), custom_call_target="tpu_custom_call" | custom-call | tf_op jit(solution)/shard_map/forward/pallas_call | solution.py:403
  52.6 1.4 %collective-permute-start.19 = (bf16[256,128]{1,0:T(8,128)(2,1)S(1)}, bf16[256,128]{1,0:T(8,128)(2,1)S(1)}, u32[]{:S(2)}, u32[]{:S(2)}) collective-permute-start(bf16[256,128]{1,0:T(8,128)(2,1)S(1)} %get-tuple-element.65), channel_id=1, source_target_pairs={{0,2},{1,3},{2,0},{3,1},{4,6},{5,7},{6,4},{7,5},{8,10},{9,11},{10,... | collective-permute-start | bytes 196616 | tf_op jit(solution)/shard_map/ppermute | solution.py:417
  54.0 1.5 %backward.9.sum_ref = f32[512,128]{1,0:T(8,128)S(1)} custom-call(s32[8,128]{1,0:T(8,128)S(4)} %get-tuple-element.38.slots, bf16[256,128]{1,0:T(8,128)(2,1)S(1)} %residual.3.refs_0_, bf16[256,128]{1,0:T(8,128)(2,1)S(1)} %collective-permute-done.18.refs_1_.refs_0_, s32[544,128]{1,0:T(8,128)S(1)} %get-tuple-element.51.refs_2_, ...), custom_call_target="tpu_custom_call" | custom-call | tf_op jit(solution)/shard_map/backward/pallas_call | solution.py:403
  55.6 1.2 %collective-permute-done.20.y_ref = bf16[256,128]{1,0:T(8,128)(2,1)S(1)} collective-permute-done((bf16[256,128]{1,0:T(8,128)(2,1)S(1)}, bf16[256,128]{1,0:T(8,128)(2,1)S(1)}, u32[]{:S(2)}, u32[]{:S(2)}) %collective-permute-start.20) | collective-permute-done | bytes 65568 | tf_op jit(solution)/shard_map/ppermute | solution.py:417
  56.8 1.5 %collective-permute-start.21 = (bf16[128,128]{1,0:T(8,128)(2,1)S(1)}, bf16[128,128]{1,0:T(8,128)(2,1)S(1)}, u32[]{:S(2)}, u32[]{:S(2)}) collective-permute-start(bf16[128,128]{1,0:T(8,128)(2,1)S(1)} %get-tuple-element.68), channel_id=1, source_target_pairs={{0,8},{1,13},{2,10},{3,15},{4,12},{5,9},{6,14},{7,11},{8,0},{9,5},... | collective-permute-start | bytes 98312 | tf_op jit(solution)/shard_map/ppermute | solution.py:417
  58.2 1.7 %collective-permute-start.22 = (bf16[128,128]{1,0:T(8,128)(2,1)S(1)}, bf16[128,128]{1,0:T(8,128)(2,1)S(1)}, u32[]{:S(2)}, u32[]{:S(2)}) collective-permute-start(bf16[128,128]{1,0:T(8,128)(2,1)S(1)} %get-tuple-element.69), channel_id=1, source_target_pairs={{0,12},{1,5},{2,14},{3,7},{4,8},{5,1},{6,10},{7,3},{8,4},{9,13},{1... | collective-permute-start | bytes 98312 | tf_op jit(solution)/shard_map/ppermute | solution.py:417
  60.4 1.9 %collective-permute-done.21.refs_1_ = bf16[128,128]{1,0:T(8,128)(2,1)S(1)} collective-permute-done((bf16[128,128]{1,0:T(8,128)(2,1)S(1)}, bf16[128,128]{1,0:T(8,128)(2,1)S(1)}, u32[]{:S(2)}, u32[]{:S(2)}) %collective-permute-start.21) | collective-permute-done | bytes 32800 | tf_op jit(solution)/shard_map/ppermute | solution.py:417
  62.3 1.7 %collective-permute-done.22.refs_2_ = bf16[128,128]{1,0:T(8,128)(2,1)S(1)} collective-permute-done((bf16[128,128]{1,0:T(8,128)(2,1)S(1)}, bf16[128,128]{1,0:T(8,128)(2,1)S(1)}, u32[]{:S(2)}, u32[]{:S(2)}) %collective-permute-start.22) | collective-permute-done | bytes 32800 | tf_op jit(solution)/shard_map/ppermute | solution.py:417
  (56 shorter events, 12.1 us)
Async XLA Ops:
  1.0 7.6 %collective-permute-start.1 = (bf16[192,128]{1,0:T(8,128)(2,1)S(1)}, bf16[192,128]{1,0:T(8,128)(2,1)S(1)}, u32[]{:S(2)}, u32[]{:S(2)}) collective-permute-start(bf16[192,128]{1,0:T(8,128)(2,1)S(1)} %pack.1.refs_0_), channel_id=1, source_target_pairs={{0,12},{1,5},{2,14},{3,7},{4,8},{5,1},{6,10},{7,3},{8,4},{9,13},{1... | collective-permute-start | bytes 147464 | tf_op jit(solution)/shard_map/ppermute | solution.py:417
  6.2 4.1 %collective-permute-start.2 = (bf16[192,128]{1,0:T(8,128)(2,1)S(1)}, bf16[192,128]{1,0:T(8,128)(2,1)S(1)}, u32[]{:S(2)}, u32[]{:S(2)}) collective-permute-start(bf16[192,128]{1,0:T(8,128)(2,1)S(1)} %pack.1.refs_0_), channel_id=1, source_target_pairs={{0,4},{1,9},{2,6},{3,11},{4,0},{5,13},{6,2},{7,15},{8,12},{9,1},{1... | collective-permute-start | bytes 147464 | tf_op jit(solution)/shard_map/ppermute | solution.py:417
  6.2 5.7 %collective-permute-start = (bf16[192,128]{1,0:T(8,128)(2,1)S(1)}, bf16[192,128]{1,0:T(8,128)(2,1)S(1)}, u32[]{:S(2)}, u32[]{:S(2)}) collective-permute-start(bf16[192,128]{1,0:T(8,128)(2,1)S(1)} %pack.1.refs_0_), channel_id=1, source_target_pairs={{0,8},{1,13},{2,10},{3,15},{4,12},{5,9},{6,14},{7,11},{8,0},{9,5},... | collective-permute-start | bytes 147464 | tf_op jit(solution)/shard_map/ppermute | solution.py:417
  10.3 6.1 %collective-permute-start.4 = (bf16[384,128]{1,0:T(8,128)(2,1)S(1)}, bf16[384,128]{1,0:T(8,128)(2,1)S(1)}, u32[]{:S(2)}, u32[]{:S(2)}) collective-permute-start(bf16[384,128]{1,0:T(8,128)(2,1)S(1)} %join.5.refs_1_), channel_id=1, source_target_pairs={{0,2},{1,3},{2,0},{3,1},{4,6},{5,7},{6,4},{7,5},{8,10},{9,11},{10,... | collective-permute-start | bytes 294920 | tf_op jit(solution)/shard_map/ppermute | solution.py:417
  11.9 4.7 %collective-permute-start.3 = (bf16[384,128]{1,0:T(8,128)(2,1)S(1)}, bf16[384,128]{1,0:T(8,128)(2,1)S(1)}, u32[]{:S(2)}, u32[]{:S(2)}) collective-permute-start(bf16[384,128]{1,0:T(8,128)(2,1)S(1)} %join.4.refs_0_), channel_id=1, source_target_pairs={{0,2},{1,3},{2,0},{3,1},{4,6},{5,7},{6,4},{7,5},{8,10},{9,11},{10,... | collective-permute-start | bytes 294920 | tf_op jit(solution)/shard_map/ppermute | solution.py:417
  19.3 1.4 %collective-permute-start.5 = (f32[288,128]{1,0:T(8,128)S(1)}, f32[288,128]{1,0:T(8,128)S(1)}, u32[]{:S(2)}, u32[]{:S(2)}) collective-permute-start(f32[288,128]{1,0:T(8,128)S(1)} %forward.8), channel_id=1, source_target_pairs={{0,1},{1,0},{2,3},{3,2},{4,5},{5,4},{6,7},{7,6},{8,9},{9,8},{10,11... | collective-permute-start | bytes 442376 | tf_op jit(solution)/shard_map/ppermute | solution.py:417
  19.4 1.4 %copy-start = (bf16[32,8,128]{2,1,0:T(8,128)(2,1)S(1)}, bf16[32,8,128]{2,1,0:T(8,128)(2,1)}, u32[]{:S(2)}) copy-start(bf16[32,8,128]{2,1,0:T(8,128)(2,1)} %param.7) | copy-start | bytes 196612
  20.8 1.3 %collective-permute-start.6 = (bf16[256,128]{1,0:T(8,128)(2,1)S(1)}, bf16[256,128]{1,0:T(8,128)(2,1)S(1)}, u32[]{:S(2)}, u32[]{:S(2)}) collective-permute-start(bf16[256,128]{1,0:T(8,128)(2,1)S(1)} %residual.2.refs_0_), channel_id=1, source_target_pairs={{0,1},{1,0},{2,3},{3,2},{4,5},{5,4},{6,7},{7,6},{8,9},{9,8},{10,11... | collective-permute-start | bytes 196616 | tf_op jit(solution)/shard_map/ppermute | solution.py:417
  23.0 4.7 %collective-permute-start.8 = (bf16[256,128]{1,0:T(8,128)(2,1)S(1)}, bf16[256,128]{1,0:T(8,128)(2,1)S(1)}, u32[]{:S(2)}, u32[]{:S(2)}) collective-permute-start(bf16[256,128]{1,0:T(8,128)(2,1)S(1)} %get-tuple-element.59), channel_id=1, source_target_pairs={{0,2},{1,3},{2,0},{3,1},{4,6},{5,7},{6,4},{7,5},{8,10},{9,11},{10,... | collective-permute-start | bytes 196616 | tf_op jit(solution)/shard_map/ppermute | solution.py:417
  24.6 5.7 %collective-permute-start.7 = (bf16[256,128]{1,0:T(8,128)(2,1)S(1)}, bf16[256,128]{1,0:T(8,128)(2,1)S(1)}, u32[]{:S(2)}, u32[]{:S(2)}) collective-permute-start(bf16[256,128]{1,0:T(8,128)(2,1)S(1)} %get-tuple-element.57), channel_id=1, source_target_pairs={{0,2},{1,3},{2,0},{3,1},{4,6},{5,7},{6,4},{7,5},{8,10},{9,11},{10,... | collective-permute-start | bytes 196616 | tf_op jit(solution)/shard_map/ppermute | solution.py:417
  27.8 6.1 %collective-permute-start.10 = (bf16[128,128]{1,0:T(8,128)(2,1)S(1)}, bf16[128,128]{1,0:T(8,128)(2,1)S(1)}, u32[]{:S(2)}, u32[]{:S(2)}) collective-permute-start(bf16[128,128]{1,0:T(8,128)(2,1)S(1)} %get-tuple-element.61), channel_id=1, source_target_pairs={{0,12},{1,5},{2,14},{3,7},{4,8},{5,1},{6,10},{7,3},{8,4},{9,13},{1... | collective-permute-start | bytes 98312 | tf_op jit(solution)/shard_map/ppermute | solution.py:417
  30.0 4.9 %collective-permute-start.9 = (bf16[128,128]{1,0:T(8,128)(2,1)S(1)}, bf16[128,128]{1,0:T(8,128)(2,1)S(1)}, u32[]{:S(2)}, u32[]{:S(2)}) collective-permute-start(bf16[128,128]{1,0:T(8,128)(2,1)S(1)} %get-tuple-element.60), channel_id=1, source_target_pairs={{0,8},{1,13},{2,10},{3,15},{4,12},{5,9},{6,14},{7,11},{8,0},{9,5},... | collective-permute-start | bytes 98312 | tf_op jit(solution)/shard_map/ppermute | solution.py:417
  30.3 2.1 %copy-start.2 = (f32[256,4]{0,1:T(4,128)S(1)}, f32[256,4]{0,1:T(4,128)}, u32[]{:S(2)}) copy-start(f32[256,4]{0,1:T(4,128)} %param.13) | copy-start | bytes 12292
  30.3 2.1 %copy-start.3 = (f32[256,4]{0,1:T(4,128)S(1)}, f32[256,4]{0,1:T(4,128)}, u32[]{:S(2)}) copy-start(f32[256,4]{0,1:T(4,128)} %param.12) | copy-start | bytes 12292
  30.3 2.1 %copy-start.4 = (s32[256,4]{0,1:T(4,128)S(1)}, s32[256,4]{0,1:T(4,128)}, u32[]{:S(2)}) copy-start(s32[256,4]{0,1:T(4,128)} %param.9) | copy-start | bytes 12292
  30.3 2.1 %copy-start.5 = (s32[16]{0:T(128)S(1)}, s32[16]{0:T(128)}, u32[]{:S(2)}) copy-start(s32[16]{0:T(128)} %param.11) | copy-start | bytes 196
  30.3 4.6 %copy-start.1 = (f32[16,8,128]{2,1,0:T(8,128)S(1)}, f32[16,8,128]{2,1,0:T(8,128)}, u32[]{:S(2)}) copy-start(f32[16,8,128]{2,1,0:T(8,128)} %param.8) | copy-start | bytes 196612
  30.3 4.5 %collective-permute-start.11 = (bf16[128,128]{1,0:T(8,128)(2,1)S(1)}, bf16[128,128]{1,0:T(8,128)(2,1)S(1)}, u32[]{:S(2)}, u32[]{:S(2)}) collective-permute-start(bf16[128,128]{1,0:T(8,128)(2,1)S(1)} %get-tuple-element.62), channel_id=1, source_target_pairs={{0,4},{1,9},{2,6},{3,11},{4,0},{5,13},{6,2},{7,15},{8,12},{9,1},{1... | collective-permute-start | bytes 98312 | tf_op jit(solution)/shard_map/ppermute | solution.py:417
  34.9 5.8 %collective-permute-start.14 = (bf16[128,128]{1,0:T(8,128)(2,1)S(1)}, bf16[128,128]{1,0:T(8,128)(2,1)S(1)}, u32[]{:S(2)}, u32[]{:S(2)}) collective-permute-start(bf16[128,128]{1,0:T(8,128)(2,1)S(1)} %get-tuple-element.64.refs_0_), channel_id=1, source_target_pairs={{0,12},{1,5},{2,14},{3,7},{4,8},{5,1},{6,10},{7,3},{8,4},{9,13},{1... | collective-permute-start | bytes 98312 | tf_op jit(solution)/shard_map/ppermute | solution.py:417
  37.2 3.9 %collective-permute-start.15 = (bf16[128,128]{1,0:T(8,128)(2,1)S(1)}, bf16[128,128]{1,0:T(8,128)(2,1)S(1)}, u32[]{:S(2)}, u32[]{:S(2)}) collective-permute-start(bf16[128,128]{1,0:T(8,128)(2,1)S(1)} %get-tuple-element.64.refs_0_), channel_id=1, source_target_pairs={{0,4},{1,9},{2,6},{3,11},{4,0},{5,13},{6,2},{7,15},{8,12},{9,1},{1... | collective-permute-start | bytes 98312 | tf_op jit(solution)/shard_map/ppermute | solution.py:417
  37.6 5.2 %collective-permute-start.12 = (bf16[128,128]{1,0:T(8,128)(2,1)S(1)}, bf16[128,128]{1,0:T(8,128)(2,1)S(1)}, u32[]{:S(2)}, u32[]{:S(2)}) collective-permute-start(bf16[128,128]{1,0:T(8,128)(2,1)S(1)} %get-tuple-element.64.refs_0_), channel_id=1, source_target_pairs={{0,8},{1,13},{2,10},{3,15},{4,12},{5,9},{6,14},{7,11},{8,0},{9,5},... | collective-permute-start | bytes 98312 | tf_op jit(solution)/shard_map/ppermute | solution.py:417
  41.1 4.4 %collective-permute-start.16 = (bf16[256,128]{1,0:T(8,128)(2,1)S(1)}, bf16[256,128]{1,0:T(8,128)(2,1)S(1)}, u32[]{:S(2)}, u32[]{:S(2)}) collective-permute-start(bf16[256,128]{1,0:T(8,128)(2,1)S(1)} %join.7.refs_1_), channel_id=1, source_target_pairs={{0,2},{1,3},{2,0},{3,1},{4,6},{5,7},{6,4},{7,5},{8,10},{9,11},{10,... | collective-permute-start | bytes 196616 | tf_op jit(solution)/shard_map/ppermute | solution.py:417
  42.8 4.3 %collective-permute-start.13 = (bf16[256,128]{1,0:T(8,128)(2,1)S(1)}, bf16[256,128]{1,0:T(8,128)(2,1)S(1)}, u32[]{:S(2)}, u32[]{:S(2)}) collective-permute-start(bf16[256,128]{1,0:T(8,128)(2,1)S(1)} %join.6.refs_0_), channel_id=1, source_target_pairs={{0,2},{1,3},{2,0},{3,1},{4,6},{5,7},{6,4},{7,5},{8,10},{9,11},{10,... | collective-permute-start | bytes 196616 | tf_op jit(solution)/shard_map/ppermute | solution.py:417
  48.3 1.4 %collective-permute-start.17 = (f32[256,128]{1,0:T(8,128)S(1)}, f32[256,128]{1,0:T(8,128)S(1)}, u32[]{:S(2)}, u32[]{:S(2)}) collective-permute-start(f32[256,128]{1,0:T(8,128)S(1)} %forward.11), channel_id=1, source_target_pairs={{0,1},{1,0},{2,3},{3,2},{4,5},{5,4},{6,7},{7,6},{8,9},{9,8},{10,11... | collective-permute-start | bytes 393224 | tf_op jit(solution)/shard_map/ppermute | solution.py:417
  49.7 1.3 %collective-permute-start.18 = (bf16[256,128]{1,0:T(8,128)(2,1)S(1)}, bf16[256,128]{1,0:T(8,128)(2,1)S(1)}, u32[]{:S(2)}, u32[]{:S(2)}) collective-permute-start(bf16[256,128]{1,0:T(8,128)(2,1)S(1)} %residual.3.refs_0_), channel_id=1, source_target_pairs={{0,1},{1,0},{2,3},{3,2},{4,5},{5,4},{6,7},{7,6},{8,9},{9,8},{10,11... | collective-permute-start | bytes 196616 | tf_op jit(solution)/shard_map/ppermute | solution.py:417
  52.0 4.8 %collective-permute-start.20 = (bf16[256,128]{1,0:T(8,128)(2,1)S(1)}, bf16[256,128]{1,0:T(8,128)(2,1)S(1)}, u32[]{:S(2)}, u32[]{:S(2)}) collective-permute-start(bf16[256,128]{1,0:T(8,128)(2,1)S(1)} %get-tuple-element.67), channel_id=1, source_target_pairs={{0,2},{1,3},{2,0},{3,1},{4,6},{5,7},{6,4},{7,5},{8,10},{9,11},{10,... | collective-permute-start | bytes 196616 | tf_op jit(solution)/shard_map/ppermute | solution.py:417
  52.6 7.2 %collective-permute-start.19 = (bf16[256,128]{1,0:T(8,128)(2,1)S(1)}, bf16[256,128]{1,0:T(8,128)(2,1)S(1)}, u32[]{:S(2)}, u32[]{:S(2)}) collective-permute-start(bf16[256,128]{1,0:T(8,128)(2,1)S(1)} %get-tuple-element.65), channel_id=1, source_target_pairs={{0,2},{1,3},{2,0},{3,1},{4,6},{5,7},{6,4},{7,5},{8,10},{9,11},{10,... | collective-permute-start | bytes 196616 | tf_op jit(solution)/shard_map/ppermute | solution.py:417
  56.8 5.6 %collective-permute-start.21 = (bf16[128,128]{1,0:T(8,128)(2,1)S(1)}, bf16[128,128]{1,0:T(8,128)(2,1)S(1)}, u32[]{:S(2)}, u32[]{:S(2)}) collective-permute-start(bf16[128,128]{1,0:T(8,128)(2,1)S(1)} %get-tuple-element.68), channel_id=1, source_target_pairs={{0,8},{1,13},{2,10},{3,15},{4,12},{5,9},{6,14},{7,11},{8,0},{9,5},... | collective-permute-start | bytes 98312 | tf_op jit(solution)/shard_map/ppermute | solution.py:417
  58.2 5.8 %collective-permute-start.22 = (bf16[128,128]{1,0:T(8,128)(2,1)S(1)}, bf16[128,128]{1,0:T(8,128)(2,1)S(1)}, u32[]{:S(2)}, u32[]{:S(2)}) collective-permute-start(bf16[128,128]{1,0:T(8,128)(2,1)S(1)} %get-tuple-element.69), channel_id=1, source_target_pairs={{0,12},{1,5},{2,14},{3,7},{4,8},{5,1},{6,10},{7,3},{8,4},{9,13},{1... | collective-permute-start | bytes 98312 | tf_op jit(solution)/shard_map/ppermute | solution.py:417
  59.9 4.3 %collective-permute-start.23 = (bf16[128,128]{1,0:T(8,128)(2,1)S(1)}, bf16[128,128]{1,0:T(8,128)(2,1)S(1)}, u32[]{:S(2)}, u32[]{:S(2)}) collective-permute-start(bf16[128,128]{1,0:T(8,128)(2,1)S(1)} %get-tuple-element.70), channel_id=1, source_target_pairs={{0,4},{1,9},{2,6},{3,11},{4,0},{5,13},{6,2},{7,15},{8,12},{9,1},{1... | collective-permute-start | bytes 98312 | tf_op jit(solution)/shard_map/ppermute | solution.py:417

commit v16 on v15

--- a/solution.py
+++ b/solution.py
@@ -375,6 +375,10 @@
         for_rows(outs[0].shape[0], finish)
 
 
+def widen_kernel(values_ref, out_ref):
+    out_ref[...] = values_ref[...].astype(F32)
+
+
 def join_kernel(*refs):
     out_ref, at = refs[-1], 0
     for ref in refs[:-1]:
@@ -508,13 +512,14 @@
             y_half = exchange(z_half, n_slab, 2)
             z_rest = join(place_2, place_3)
             y_rest = exchange(z_rest, n_slab, 2)
-            along_z, along_y = (z_half, z_rest), (y_half, y_rest)
+            along_z = (z_half, z_rest)
+            along_y = (call(widen_kernel, "widen", 16, [VMEM], shape(y_half.shape, F32), y_half), y_rest)
             if sweep == 0:
                 (z_list,), z_rows, z_forward, z_backward = setup(along_z, 4, (None,))
             both = forward(z_list, along_z, 4, z_forward, 2 * n_rays)
             if sweep == 0:
                 (own_list, other_list), y_rows, y_forward, y_backward = setup(
-                    along_y, 4, (0, 1), after=both)
+                    (y_half, y_rest), 4, (0, 1), after=both)
             other = exchange(
                 forward(other_list, along_y, 4, y_forward, n_rays, both, n_rays,
                         (z_rows, y_rows) if sweep == 0 else ()), n_slab, 1)

time: 65.3 us -> 65.7 us (level)
  waiting for transfers between devices: 15.9 us -> 21.4 us
  Pallas kernels: 20.3 us -> 17.9 us
  starting transfers between devices: 28.4 us -> 26.1 us
    ppermute x24, waiting for transfers between devices: 15.9 us -> 21.4 us  [exchange(): lax.ppermute(values, 'slab', [(device, device ^ far[device % 2]) for devi...]
    pallas_call x28 -> x30, Pallas kernels: 20.3 us -> 17.9 us  [call(): pl.pallas_call(kernel, out_shape=out_shape, in_specs=in_specs, out_specs=...]
    ppermute x24, starting transfers between devices: 28.4 us -> 26.1 us  [exchange(): lax.ppermute(values, 'slab', [(device, device ^ far[device % 2]) for devi...]
  transfers between devices with their start and end apart: 24 -> 24, of which waited for: 17 -> 16; matrix products, arithmetic and copies ran while one was open for 0% -> 0% of each run, Pallas kernels for 20% -> 16%
where the time goes in v16:
time: 65.7 us
  starting transfers between devices  26.1 us (40%)
  waiting for transfers between devices  21.4 us (33%)
  Pallas kernels  17.9 us (27%)
    ppermute x24, starting transfers between devices, exchange(): lax.ppermute(values, 'slab', [(device, device ^ far[device % 2]) for devi...  26.1 us
    ppermute x24, waiting for transfers between devices, exchange(): lax.ppermute(values, 'slab', [(device, device ^ far[device % 2]) for devi...  21.4 us
    pallas_call x30, Pallas kernels, call(): pl.pallas_call(kernel, out_shape=out_shape, in_specs=in_specs, out_specs=...  17.9 us
  transfers between devices with their start and end apart: 24, of which 16 were waited for; matrix products, arithmetic and copies ran while one was open for 0% of the time, Pallas kernels for 16%

profile of v16, /device:TPU:0, one launch (start us, length us, event | category | flops | bytes accessed | tf_op | source)
XLA Modules:
  0.0 65.7 jit_solution(17735322387758453817)
XLA Ops:
  0.0 1.0 %pack.1.refs_0_ = bf16[192,128]{1,0:T(8,128)(2,1)S(1)} custom-call(f32[128,128]{1,0:T(8,128)} %bitcast.10, f32[4,256]{1,0:T(4,128)} %bitcast.12, f32[4,256]{1,0:T(4,128)} %bitcast.14, s32[4,256]{1,0:T(4,128)} %bitcast.16, s32[1,256]{1,0:T(1,128)} %bitcast.20, s32[1,16]{1,0:T(1,128)} %bitcast.18), custom_call_target="tpu_custom_call" | custom-call | tf_op jit(solution)/shard_map/pack/pallas_call | solution.py:407
  1.0 4.1 %collective-permute-start = (bf16[192,128]{1,0:T(8,128)(2,1)S(1)}, bf16[192,128]{1,0:T(8,128)(2,1)S(1)}, u32[]{:S(2)}, u32[]{:S(2)}) collective-permute-start(bf16[192,128]{1,0:T(8,128)(2,1)S(1)} %pack.1.refs_0_), channel_id=1, source_target_pairs={{0,8},{1,13},{2,10},{3,15},{4,12},{5,9},{6,14},{7,11},{8,0},{9,5},... | collective-permute-start | bytes 147464 | tf_op jit(solution)/shard_map/ppermute | solution.py:421
  5.2 1.3 %collective-permute-start.1 = (bf16[192,128]{1,0:T(8,128)(2,1)S(1)}, bf16[192,128]{1,0:T(8,128)(2,1)S(1)}, u32[]{:S(2)}, u32[]{:S(2)}) collective-permute-start(bf16[192,128]{1,0:T(8,128)(2,1)S(1)} %pack.1.refs_0_), channel_id=1, source_target_pairs={{0,12},{1,5},{2,14},{3,7},{4,8},{5,1},{6,10},{7,3},{8,4},{9,13},{1... | collective-permute-start | bytes 147464 | tf_op jit(solution)/shard_map/ppermute | solution.py:421
  6.7 1.0 %collective-permute-done.refs_1_ = bf16[192,128]{1,0:T(8,128)(2,1)S(1)} collective-permute-done((bf16[192,128]{1,0:T(8,128)(2,1)S(1)}, bf16[192,128]{1,0:T(8,128)(2,1)S(1)}, u32[]{:S(2)}, u32[]{:S(2)}) %collective-permute-start) | collective-permute-done | bytes 49184 | tf_op jit(solution)/shard_map/ppermute | solution.py:421
  7.8 1.7 %collective-permute-start.3 = (bf16[384,128]{1,0:T(8,128)(2,1)S(1)}, bf16[384,128]{1,0:T(8,128)(2,1)S(1)}, u32[]{:S(2)}, u32[]{:S(2)}) collective-permute-start(bf16[384,128]{1,0:T(8,128)(2,1)S(1)} %join.4.refs_0_), channel_id=1, source_target_pairs={{0,2},{1,3},{2,0},{3,1},{4,6},{5,7},{6,4},{7,5},{8,10},{9,11},{10,... | collective-permute-start | bytes 294920 | tf_op jit(solution)/shard_map/ppermute | solution.py:421
  9.5 1.9 %collective-permute-done.1.refs_0_ = bf16[192,128]{1,0:T(8,128)(2,1)S(1)} collective-permute-done((bf16[192,128]{1,0:T(8,128)(2,1)S(1)}, bf16[192,128]{1,0:T(8,128)(2,1)S(1)}, u32[]{:S(2)}, u32[]{:S(2)}) %collective-permute-start.1) | collective-permute-done | bytes 49184 | tf_op jit(solution)/shard_map/ppermute | solution.py:421
  11.5 1.6 %collective-permute-start.4 = (bf16[384,128]{1,0:T(8,128)(2,1)S(1)}, bf16[384,128]{1,0:T(8,128)(2,1)S(1)}, u32[]{:S(2)}, u32[]{:S(2)}) collective-permute-start(bf16[384,128]{1,0:T(8,128)(2,1)S(1)} %join.5.refs_1_), channel_id=1, source_target_pairs={{0,2},{1,3},{2,0},{3,1},{4,6},{5,7},{6,4},{7,5},{8,10},{9,11},{10,... | collective-permute-start | bytes 294920 | tf_op jit(solution)/shard_map/ppermute | solution.py:421
  13.0 1.5 %setup.2 = (s32[8,128]{1,0:T(8,128)S(4)}, f32[64,128]{1,0:T(8,128)S(1)}, s32[544,128]{1,0:T(8,128)S(1)}, f32[544,128]{1,0:T(8,128)S(1)}, f32[544,128]{1,0:T(8,12...) custom-call(bf16[384,128]{1,0:T(8,128)(2,1)S(1)} %join.4.refs_0_, ...), custom_call_target="tpu_custom_call" | custom-call | tf_op jit(solution)/shard_map/setup/pallas_call | solution.py:407
  14.5 1.1 %forward.6.refs_2_.refs_6_ = f32[512,128]{1,0:T(8,128)S(1)} custom-call(s32[8,128]{1,0:T(8,128)S(4)} %get-tuple-element.38.slots, bf16[384,128]{1,0:T(8,128)(2,1)S(1)} %join.4.refs_0_, bf16[384,128]{1,0:T(8,128)(2,1)S(1)} %join.5.refs_1_, s32[544,128]{1,0:T(8,128)S(1)} %get-tuple-element.39.refs_2_, f32[544,128]{1,0:T(8,128)S(1)} %get-tuple-element.40.refs_3_, ...), custom_call_target="tpu_custom_call" | custom-call | tf_op jit(solution)/shard_map/forward/pallas_call | solution.py:407
  16.1 1.6 %setup.3 = (s32[8,128]{1,0:T(8,128)S(4)}, s32[8,128]{1,0:T(8,128)S(4)}, f32[64,128]{1,0:T(8,128)S(1)}, s32[544,128]{1,0:T(8,128)S(1)}, f32[544,128]{1,0:T(8,128)...) custom-call(bf16[384,128]{1,0:T(8,128)(2,1)S(1)} %collective-permute, ...), custom_call_target="tpu_custom_call" | custom-call | tf_op jit(solution)/shard_map/setup/pallas_call | solution.py:407
  17.7 1.1 %forward.8 = f32[288,128]{1,0:T(8,128)S(1)} custom-call(s32[8,128]{1,0:T(8,128)S(4)} %get-tuple-element.50.slots, f32[384,128]{1,0:T(8,128)S(1)} %widen.2.refs_0_, bf16[384,128]{1,0:T(8,128)(2,1)S(1)} %collective-permute-done.4.refs_1_, s32[544,128]{1,0:T(8,128)S(1)} %get-tuple-element.44.refs_2_, f32[544,128]{1,0:T(8,128)S(1)} %get-tuple-element.45.refs_3_, ...), custom_call_target="tpu_custom_call" | custom-call | tf_op jit(solution)/shard_map/forward/pallas_call | solution.py:407
  18.9 1.1 %forward.7.projection_ref = f32[256,128]{1,0:T(8,128)S(1)} custom-call(s32[8,128]{1,0:T(8,128)S(4)} %get-tuple-element.43.slots, f32[384,128]{1,0:T(8,128)S(1)} %widen.2.refs_0_, bf16[384,128]{1,0:T(8,128)(2,1)S(1)} %collective-permute-done.4.refs_1_, s32[544,128]{1,0:T(8,128)S(1)} %get-tuple-element.44.refs_2_, f32[544,128]{1,0:T(8,128)S(1)} %get-tuple-element.45.refs_3_, ...), custom_call_target="tpu_custom_call" | custom-call | tf_op jit(solution)/shard_map/forward/pallas_call | solution.py:407
  20.5 0.9 %backward.7.refs_4_ = f32[512,128]{1,0:T(8,128)S(1)} custom-call(s32[8,128]{1,0:T(8,128)S(4)} %get-tuple-element.43.slots, bf16[256,128]{1,0:T(8,128)(2,1)S(1)} %residual.2.refs_0_, s32[544,128]{1,0:T(8,128)S(1)} %get-tuple-element.54.refs_1_, f32[544,128]{1,0:T(8,128)S(1)} %get-tuple-element.55.refs_2_, f32[544,128]{1,0:T(8,128)S(1)} %get-tuple-element.56.refs_3_), custom_call_target="tpu_custom_call" | custom-call | tf_op jit(solution)/shard_map/backward/pallas_call | solution.py:407
  22.6 1.9 %collective-permute-start.8 = (bf16[256,128]{1,0:T(8,128)(2,1)S(1)}, bf16[256,128]{1,0:T(8,128)(2,1)S(1)}, u32[]{:S(2)}, u32[]{:S(2)}) collective-permute-start(bf16[256,128]{1,0:T(8,128)(2,1)S(1)} %get-tuple-element.59), channel_id=1, source_target_pairs={{0,2},{1,3},{2,0},{3,1},{4,6},{5,7},{6,4},{7,5},{8,10},{9,11},{10,... | collective-permute-start | bytes 196616 | tf_op jit(solution)/shard_map/ppermute | solution.py:421
  25.6 1.5 %collective-permute-done.8.y_ref = bf16[256,128]{1,0:T(8,128)(2,1)S(1)} collective-permute-done((bf16[256,128]{1,0:T(8,128)(2,1)S(1)}, bf16[256,128]{1,0:T(8,128)(2,1)S(1)}, u32[]{:S(2)}, u32[]{:S(2)}) %collective-permute-start.8) | collective-permute-done | bytes 65568 | tf_op jit(solution)/shard_map/ppermute | solution.py:421
  27.1 4.4 %collective-permute-start.10 = (bf16[128,128]{1,0:T(8,128)(2,1)S(1)}, bf16[128,128]{1,0:T(8,128)(2,1)S(1)}, u32[]{:S(2)}, u32[]{:S(2)}) collective-permute-start(bf16[128,128]{1,0:T(8,128)(2,1)S(1)} %get-tuple-element.61), channel_id=1, source_target_pairs={{0,12},{1,5},{2,14},{3,7},{4,8},{5,1},{6,10},{7,3},{8,4},{9,13},{1... | collective-permute-start | bytes 98312 | tf_op jit(solution)/shard_map/ppermute | solution.py:421
  33.5 2.9 %collective-permute-done.9.refs_1_ = bf16[128,128]{1,0:T(8,128)(2,1)S(1)} collective-permute-done((bf16[128,128]{1,0:T(8,128)(2,1)S(1)}, bf16[128,128]{1,0:T(8,128)(2,1)S(1)}, u32[]{:S(2)}, u32[]{:S(2)}) %collective-permute-start.9) | collective-permute-done | bytes 32800 | tf_op jit(solution)/shard_map/ppermute | solution.py:421
  36.4 2.2 %collective-permute-start.12 = (bf16[128,128]{1,0:T(8,128)(2,1)S(1)}, bf16[128,128]{1,0:T(8,128)(2,1)S(1)}, u32[]{:S(2)}, u32[]{:S(2)}) collective-permute-start(bf16[128,128]{1,0:T(8,128)(2,1)S(1)} %get-tuple-element.64.refs_0_), channel_id=1, source_target_pairs={{0,8},{1,13},{2,10},{3,15},{4,12},{5,9},{6,14},{7,11},{8,0},{9,5},... | collective-permute-start | bytes 98312 | tf_op jit(solution)/shard_map/ppermute | solution.py:421
  38.7 1.3 %collective-permute-start.15 = (bf16[128,128]{1,0:T(8,128)(2,1)S(1)}, bf16[128,128]{1,0:T(8,128)(2,1)S(1)}, u32[]{:S(2)}, u32[]{:S(2)}) collective-permute-start(bf16[128,128]{1,0:T(8,128)(2,1)S(1)} %get-tuple-element.64.refs_0_), channel_id=1, source_target_pairs={{0,4},{1,9},{2,6},{3,11},{4,0},{5,13},{6,2},{7,15},{8,12},{9,1},{1... | collective-permute-start | bytes 98312 | tf_op jit(solution)/shard_map/ppermute | solution.py:421
  40.0 1.3 %collective-permute-done.12.refs_1_ = bf16[128,128]{1,0:T(8,128)(2,1)S(1)} collective-permute-done((bf16[128,128]{1,0:T(8,128)(2,1)S(1)}, bf16[128,128]{1,0:T(8,128)(2,1)S(1)}, u32[]{:S(2)}, u32[]{:S(2)}) %collective-permute-start.12) | collective-permute-done | bytes 32800 | tf_op jit(solution)/shard_map/ppermute | solution.py:421
  41.3 3.0 %collective-permute-done.14.refs_0_ = bf16[128,128]{1,0:T(8,128)(2,1)S(1)} collective-permute-done((bf16[128,128]{1,0:T(8,128)(2,1)S(1)}, bf16[128,128]{1,0:T(8,128)(2,1)S(1)}, u32[]{:S(2)}, u32[]{:S(2)}) %collective-permute-start.14) | collective-permute-done | bytes 32800 | tf_op jit(solution)/shard_map/ppermute | solution.py:421
  44.4 1.1 %forward.9.refs_6_ = f32[512,128]{1,0:T(8,128)S(1)} custom-call(s32[8,128]{1,0:T(8,128)S(4)} %get-tuple-element.38.slots, bf16[256,128]{1,0:T(8,128)(2,1)S(1)} %join.6.refs_0_, bf16[256,128]{1,0:T(8,128)(2,1)S(1)} %join.7.refs_1_, s32[544,128]{1,0:T(8,128)S(1)} %get-tuple-element.39.refs_2_, f32[544,128]{1,0:T(8,128)S(1)} %get-tuple-element.40.refs_3_, ...), custom_call_target="tpu_custom_call" | custom-call | tf_op jit(solution)/shard_map/forward/pallas_call | solution.py:407
  45.6 3.1 %collective-permute-done.16.refs_1_ = bf16[256,128]{1,0:T(8,128)(2,1)S(1)} collective-permute-done((bf16[256,128]{1,0:T(8,128)(2,1)S(1)}, bf16[256,128]{1,0:T(8,128)(2,1)S(1)}, u32[]{:S(2)}, u32[]{:S(2)}) %collective-permute-start.16) | collective-permute-done | bytes 65568 | tf_op jit(solution)/shard_map/ppermute | solution.py:421
  48.7 1.1 %forward.11 = f32[256,128]{1,0:T(8,128)S(1)} custom-call(s32[8,128]{1,0:T(8,128)S(4)} %get-tuple-element.50.slots, f32[256,128]{1,0:T(8,128)S(1)} %widen.3.refs_0_, bf16[256,128]{1,0:T(8,128)(2,1)S(1)} %collective-permute-done.16.refs_1_, s32[544,128]{1,0:T(8,128)S(1)} %get-tuple-element.44.refs_2_, f32[544,128]{1,0:T(8,128)S(1)} %get-tuple-element.45.refs_3_, ...), custom_call_target="tpu_custom_call" | custom-call | tf_op jit(solution)/shard_map/forward/pallas_call | solution.py:407
  49.9 1.1 %forward.10.projection_ref = f32[256,128]{1,0:T(8,128)S(1)} custom-call(s32[8,128]{1,0:T(8,128)S(4)} %get-tuple-element.43.slots, f32[256,128]{1,0:T(8,128)S(1)} %widen.3.refs_0_, bf16[256,128]{1,0:T(8,128)(2,1)S(1)} %collective-permute-done.16.refs_1_, s32[544,128]{1,0:T(8,128)S(1)} %get-tuple-element.44.refs_2_, f32[544,128]{1,0:T(8,128)S(1)} %get-tuple-element.45.refs_3_, ...), custom_call_target="tpu_custom_call" | custom-call | tf_op jit(solution)/shard_map/forward/pallas_call | solution.py:407
  53.9 1.7 %collective-permute-start.19 = (bf16[256,128]{1,0:T(8,128)(2,1)S(1)}, bf16[256,128]{1,0:T(8,128)(2,1)S(1)}, u32[]{:S(2)}, u32[]{:S(2)}) collective-permute-start(bf16[256,128]{1,0:T(8,128)(2,1)S(1)} %get-tuple-element.65), channel_id=1, source_target_pairs={{0,2},{1,3},{2,0},{3,1},{4,6},{5,7},{6,4},{7,5},{8,10},{9,11},{10,... | collective-permute-start | bytes 196616 | tf_op jit(solution)/shard_map/ppermute | solution.py:421
  56.5 1.6 %collective-permute-done.20.y_ref = bf16[256,128]{1,0:T(8,128)(2,1)S(1)} collective-permute-done((bf16[256,128]{1,0:T(8,128)(2,1)S(1)}, bf16[256,128]{1,0:T(8,128)(2,1)S(1)}, u32[]{:S(2)}, u32[]{:S(2)}) %collective-permute-start.20) | collective-permute-done | bytes 65568 | tf_op jit(solution)/shard_map/ppermute | solution.py:421
  58.2 1.2 %collective-permute-start.21 = (bf16[128,128]{1,0:T(8,128)(2,1)S(1)}, bf16[128,128]{1,0:T(8,128)(2,1)S(1)}, u32[]{:S(2)}, u32[]{:S(2)}) collective-permute-start(bf16[128,128]{1,0:T(8,128)(2,1)S(1)} %get-tuple-element.68), channel_id=1, source_target_pairs={{0,8},{1,13},{2,10},{3,15},{4,12},{5,9},{6,14},{7,11},{8,0},{9,5},... | collective-permute-start | bytes 98312 | tf_op jit(solution)/shard_map/ppermute | solution.py:421
  59.3 1.4 %collective-permute-start.22 = (bf16[128,128]{1,0:T(8,128)(2,1)S(1)}, bf16[128,128]{1,0:T(8,128)(2,1)S(1)}, u32[]{:S(2)}, u32[]{:S(2)}) collective-permute-start(bf16[128,128]{1,0:T(8,128)(2,1)S(1)} %get-tuple-element.69), channel_id=1, source_target_pairs={{0,12},{1,5},{2,14},{3,7},{4,8},{5,1},{6,10},{7,3},{8,4},{9,13},{1... | collective-permute-start | bytes 98312 | tf_op jit(solution)/shard_map/ppermute | solution.py:421
  60.8 1.0 %collective-permute-start.23 = (bf16[128,128]{1,0:T(8,128)(2,1)S(1)}, bf16[128,128]{1,0:T(8,128)(2,1)S(1)}, u32[]{:S(2)}, u32[]{:S(2)}) collective-permute-start(bf16[128,128]{1,0:T(8,128)(2,1)S(1)} %get-tuple-element.70), channel_id=1, source_target_pairs={{0,4},{1,9},{2,6},{3,11},{4,0},{5,13},{6,2},{7,15},{8,12},{9,1},{1... | collective-permute-start | bytes 98312 | tf_op jit(solution)/shard_map/ppermute | solution.py:421
  61.8 1.4 %collective-permute-done.21.refs_1_ = bf16[128,128]{1,0:T(8,128)(2,1)S(1)} collective-permute-done((bf16[128,128]{1,0:T(8,128)(2,1)S(1)}, bf16[128,128]{1,0:T(8,128)(2,1)S(1)}, u32[]{:S(2)}, u32[]{:S(2)}) %collective-permute-start.21) | collective-permute-done | bytes 32800 | tf_op jit(solution)/shard_map/ppermute | solution.py:421
  63.2 1.8 %collective-permute-done.22.refs_2_ = bf16[128,128]{1,0:T(8,128)(2,1)S(1)} collective-permute-done((bf16[128,128]{1,0:T(8,128)(2,1)S(1)}, bf16[128,128]{1,0:T(8,128)(2,1)S(1)}, u32[]{:S(2)}, u32[]{:S(2)}) %collective-permute-start.22) | collective-permute-done | bytes 32800 | tf_op jit(solution)/shard_map/ppermute | solution.py:421
  (58 shorter events, 10.1 us)
Async XLA Ops:
  1.0 6.7 %collective-permute-start = (bf16[192,128]{1,0:T(8,128)(2,1)S(1)}, bf16[192,128]{1,0:T(8,128)(2,1)S(1)}, u32[]{:S(2)}, u32[]{:S(2)}) collective-permute-start(bf16[192,128]{1,0:T(8,128)(2,1)S(1)} %pack.1.refs_0_), channel_id=1, source_target_pairs={{0,8},{1,13},{2,10},{3,15},{4,12},{5,9},{6,14},{7,11},{8,0},{9,5},... | collective-permute-start | bytes 147464 | tf_op jit(solution)/shard_map/ppermute | solution.py:421
  5.2 6.3 %collective-permute-start.1 = (bf16[192,128]{1,0:T(8,128)(2,1)S(1)}, bf16[192,128]{1,0:T(8,128)(2,1)S(1)}, u32[]{:S(2)}, u32[]{:S(2)}) collective-permute-start(bf16[192,128]{1,0:T(8,128)(2,1)S(1)} %pack.1.refs_0_), channel_id=1, source_target_pairs={{0,12},{1,5},{2,14},{3,7},{4,8},{5,1},{6,10},{7,3},{8,4},{9,13},{1... | collective-permute-start | bytes 147464 | tf_op jit(solution)/shard_map/ppermute | solution.py:421
  6.5 5.0 %collective-permute-start.2 = (bf16[192,128]{1,0:T(8,128)(2,1)S(1)}, bf16[192,128]{1,0:T(8,128)(2,1)S(1)}, u32[]{:S(2)}, u32[]{:S(2)}) collective-permute-start(bf16[192,128]{1,0:T(8,128)(2,1)S(1)} %pack.1.refs_0_), channel_id=1, source_target_pairs={{0,4},{1,9},{2,6},{3,11},{4,0},{5,13},{6,2},{7,15},{8,12},{9,1},{1... | collective-permute-start | bytes 147464 | tf_op jit(solution)/shard_map/ppermute | solution.py:421
  7.8 7.9 %collective-permute-start.3 = (bf16[384,128]{1,0:T(8,128)(2,1)S(1)}, bf16[384,128]{1,0:T(8,128)(2,1)S(1)}, u32[]{:S(2)}, u32[]{:S(2)}) collective-permute-start(bf16[384,128]{1,0:T(8,128)(2,1)S(1)} %join.4.refs_0_), channel_id=1, source_target_pairs={{0,2},{1,3},{2,0},{3,1},{4,6},{5,7},{6,4},{7,5},{8,10},{9,11},{10,... | collective-permute-start | bytes 294920 | tf_op jit(solution)/shard_map/ppermute | solution.py:421
  11.5 4.7 %collective-permute-start.4 = (bf16[384,128]{1,0:T(8,128)(2,1)S(1)}, bf16[384,128]{1,0:T(8,128)(2,1)S(1)}, u32[]{:S(2)}, u32[]{:S(2)}) collective-permute-start(bf16[384,128]{1,0:T(8,128)(2,1)S(1)} %join.5.refs_1_), channel_id=1, source_target_pairs={{0,2},{1,3},{2,0},{3,1},{4,6},{5,7},{6,4},{7,5},{8,10},{9,11},{10,... | collective-permute-start | bytes 294920 | tf_op jit(solution)/shard_map/ppermute | solution.py:421
  18.8 1.4 %collective-permute-start.5 = (f32[288,128]{1,0:T(8,128)S(1)}, f32[288,128]{1,0:T(8,128)S(1)}, u32[]{:S(2)}, u32[]{:S(2)}) collective-permute-start(f32[288,128]{1,0:T(8,128)S(1)} %forward.8), channel_id=1, source_target_pairs={{0,1},{1,0},{2,3},{3,2},{4,5},{5,4},{6,7},{7,6},{8,9},{9,8},{10,11... | collective-permute-start | bytes 442376 | tf_op jit(solution)/shard_map/ppermute | solution.py:421
  18.9 1.4 %copy-start = (bf16[32,8,128]{2,1,0:T(8,128)(2,1)S(1)}, bf16[32,8,128]{2,1,0:T(8,128)(2,1)}, u32[]{:S(2)}) copy-start(bf16[32,8,128]{2,1,0:T(8,128)(2,1)} %param.7) | copy-start | bytes 196612
  20.3 1.3 %collective-permute-start.6 = (bf16[256,128]{1,0:T(8,128)(2,1)S(1)}, bf16[256,128]{1,0:T(8,128)(2,1)S(1)}, u32[]{:S(2)}, u32[]{:S(2)}) collective-permute-start(bf16[256,128]{1,0:T(8,128)(2,1)S(1)} %residual.2.refs_0_), channel_id=1, source_target_pairs={{0,1},{1,0},{2,3},{3,2},{4,5},{5,4},{6,7},{7,6},{8,9},{9,8},{10,11... | collective-permute-start | bytes 196616 | tf_op jit(solution)/shard_map/ppermute | solution.py:421
  22.6 4.5 %collective-permute-start.8 = (bf16[256,128]{1,0:T(8,128)(2,1)S(1)}, bf16[256,128]{1,0:T(8,128)(2,1)S(1)}, u32[]{:S(2)}, u32[]{:S(2)}) collective-permute-start(bf16[256,128]{1,0:T(8,128)(2,1)S(1)} %get-tuple-element.59), channel_id=1, source_target_pairs={{0,2},{1,3},{2,0},{3,1},{4,6},{5,7},{6,4},{7,5},{8,10},{9,11},{10,... | collective-permute-start | bytes 196616 | tf_op jit(solution)/shard_map/ppermute | solution.py:421
  24.5 7.1 %collective-permute-start.7 = (bf16[256,128]{1,0:T(8,128)(2,1)S(1)}, bf16[256,128]{1,0:T(8,128)(2,1)S(1)}, u32[]{:S(2)}, u32[]{:S(2)}) collective-permute-start(bf16[256,128]{1,0:T(8,128)(2,1)S(1)} %get-tuple-element.57), channel_id=1, source_target_pairs={{0,2},{1,3},{2,0},{3,1},{4,6},{5,7},{6,4},{7,5},{8,10},{9,11},{10,... | collective-permute-start | bytes 196616 | tf_op jit(solution)/shard_map/ppermute | solution.py:421
  27.1 6.3 %collective-permute-start.10 = (bf16[128,128]{1,0:T(8,128)(2,1)S(1)}, bf16[128,128]{1,0:T(8,128)(2,1)S(1)}, u32[]{:S(2)}, u32[]{:S(2)}) collective-permute-start(bf16[128,128]{1,0:T(8,128)(2,1)S(1)} %get-tuple-element.61), channel_id=1, source_target_pairs={{0,12},{1,5},{2,14},{3,7},{4,8},{5,1},{6,10},{7,3},{8,4},{9,13},{1... | collective-permute-start | bytes 98312 | tf_op jit(solution)/shard_map/ppermute | solution.py:421
  31.6 4.8 %collective-permute-start.9 = (bf16[128,128]{1,0:T(8,128)(2,1)S(1)}, bf16[128,128]{1,0:T(8,128)(2,1)S(1)}, u32[]{:S(2)}, u32[]{:S(2)}) collective-permute-start(bf16[128,128]{1,0:T(8,128)(2,1)S(1)} %get-tuple-element.60), channel_id=1, source_target_pairs={{0,8},{1,13},{2,10},{3,15},{4,12},{5,9},{6,14},{7,11},{8,0},{9,5},... | collective-permute-start | bytes 98312 | tf_op jit(solution)/shard_map/ppermute | solution.py:421
  31.6 0.8 %copy-start.2 = (f32[256,4]{0,1:T(4,128)S(1)}, f32[256,4]{0,1:T(4,128)}, u32[]{:S(2)}) copy-start(f32[256,4]{0,1:T(4,128)} %param.13) | copy-start | bytes 12292
  31.6 0.8 %copy-start.3 = (f32[256,4]{0,1:T(4,128)S(1)}, f32[256,4]{0,1:T(4,128)}, u32[]{:S(2)}) copy-start(f32[256,4]{0,1:T(4,128)} %param.12) | copy-start | bytes 12292
  31.6 0.8 %copy-start.4 = (s32[256,4]{0,1:T(4,128)S(1)}, s32[256,4]{0,1:T(4,128)}, u32[]{:S(2)}) copy-start(s32[256,4]{0,1:T(4,128)} %param.9) | copy-start | bytes 12292
  31.6 0.7 %copy-start.5 = (s32[16]{0:T(128)S(1)}, s32[16]{0:T(128)}, u32[]{:S(2)}) copy-start(s32[16]{0:T(128)} %param.11) | copy-start | bytes 196
  31.6 4.7 %copy-start.1 = (f32[16,8,128]{2,1,0:T(8,128)S(1)}, f32[16,8,128]{2,1,0:T(8,128)}, u32[]{:S(2)}) copy-start(f32[16,8,128]{2,1,0:T(8,128)} %param.8) | copy-start | bytes 196612
  31.6 4.7 %collective-permute-start.11 = (bf16[128,128]{1,0:T(8,128)(2,1)S(1)}, bf16[128,128]{1,0:T(8,128)(2,1)S(1)}, u32[]{:S(2)}, u32[]{:S(2)}) collective-permute-start(bf16[128,128]{1,0:T(8,128)(2,1)S(1)} %get-tuple-element.62), channel_id=1, source_target_pairs={{0,4},{1,9},{2,6},{3,11},{4,0},{5,13},{6,2},{7,15},{8,12},{9,1},{1... | collective-permute-start | bytes 98312 | tf_op jit(solution)/shard_map/ppermute | solution.py:421
  36.4 4.9 %collective-permute-start.12 = (bf16[128,128]{1,0:T(8,128)(2,1)S(1)}, bf16[128,128]{1,0:T(8,128)(2,1)S(1)}, u32[]{:S(2)}, u32[]{:S(2)}) collective-permute-start(bf16[128,128]{1,0:T(8,128)(2,1)S(1)} %get-tuple-element.64.refs_0_), channel_id=1, source_target_pairs={{0,8},{1,13},{2,10},{3,15},{4,12},{5,9},{6,14},{7,11},{8,0},{9,5},... | collective-permute-start | bytes 98312 | tf_op jit(solution)/shard_map/ppermute | solution.py:421
  38.6 5.7 %collective-permute-start.14 = (bf16[128,128]{1,0:T(8,128)(2,1)S(1)}, bf16[128,128]{1,0:T(8,128)(2,1)S(1)}, u32[]{:S(2)}, u32[]{:S(2)}) collective-permute-start(bf16[128,128]{1,0:T(8,128)(2,1)S(1)} %get-tuple-element.64.refs_0_), channel_id=1, source_target_pairs={{0,12},{1,5},{2,14},{3,7},{4,8},{5,1},{6,10},{7,3},{8,4},{9,13},{1... | collective-permute-start | bytes 98312 | tf_op jit(solution)/shard_map/ppermute | solution.py:421
  38.7 5.6 %collective-permute-start.15 = (bf16[128,128]{1,0:T(8,128)(2,1)S(1)}, bf16[128,128]{1,0:T(8,128)(2,1)S(1)}, u32[]{:S(2)}, u32[]{:S(2)}) collective-permute-start(bf16[128,128]{1,0:T(8,128)(2,1)S(1)} %get-tuple-element.64.refs_0_), channel_id=1, source_target_pairs={{0,4},{1,9},{2,6},{3,11},{4,0},{5,13},{6,2},{7,15},{8,12},{9,1},{1... | collective-permute-start | bytes 98312 | tf_op jit(solution)/shard_map/ppermute | solution.py:421
  41.3 4.3 %collective-permute-start.13 = (bf16[256,128]{1,0:T(8,128)(2,1)S(1)}, bf16[256,128]{1,0:T(8,128)(2,1)S(1)}, u32[]{:S(2)}, u32[]{:S(2)}) collective-permute-start(bf16[256,128]{1,0:T(8,128)(2,1)S(1)} %join.6.refs_0_), channel_id=1, source_target_pairs={{0,2},{1,3},{2,0},{3,1},{4,6},{5,7},{6,4},{7,5},{8,10},{9,11},{10,... | collective-permute-start | bytes 196616 | tf_op jit(solution)/shard_map/ppermute | solution.py:421
  44.4 4.3 %collective-permute-start.16 = (bf16[256,128]{1,0:T(8,128)(2,1)S(1)}, bf16[256,128]{1,0:T(8,128)(2,1)S(1)}, u32[]{:S(2)}, u32[]{:S(2)}) collective-permute-start(bf16[256,128]{1,0:T(8,128)(2,1)S(1)} %join.7.refs_1_), channel_id=1, source_target_pairs={{0,2},{1,3},{2,0},{3,1},{4,6},{5,7},{6,4},{7,5},{8,10},{9,11},{10,... | collective-permute-start | bytes 196616 | tf_op jit(solution)/shard_map/ppermute | solution.py:421
  49.8 1.4 %collective-permute-start.17 = (f32[256,128]{1,0:T(8,128)S(1)}, f32[256,128]{1,0:T(8,128)S(1)}, u32[]{:S(2)}, u32[]{:S(2)}) collective-permute-start(f32[256,128]{1,0:T(8,128)S(1)} %forward.11), channel_id=1, source_target_pairs={{0,1},{1,0},{2,3},{3,2},{4,5},{5,4},{6,7},{7,6},{8,9},{9,8},{10,11... | collective-permute-start | bytes 393224 | tf_op jit(solution)/shard_map/ppermute | solution.py:421
  51.2 1.3 %collective-permute-start.18 = (bf16[256,128]{1,0:T(8,128)(2,1)S(1)}, bf16[256,128]{1,0:T(8,128)(2,1)S(1)}, u32[]{:S(2)}, u32[]{:S(2)}) collective-permute-start(bf16[256,128]{1,0:T(8,128)(2,1)S(1)} %residual.3.refs_0_), channel_id=1, source_target_pairs={{0,1},{1,0},{2,3},{3,2},{4,5},{5,4},{6,7},{7,6},{8,9},{9,8},{10,11... | collective-permute-start | bytes 196616 | tf_op jit(solution)/shard_map/ppermute | solution.py:421
  53.5 4.6 %collective-permute-start.20 = (bf16[256,128]{1,0:T(8,128)(2,1)S(1)}, bf16[256,128]{1,0:T(8,128)(2,1)S(1)}, u32[]{:S(2)}, u32[]{:S(2)}) collective-permute-start(bf16[256,128]{1,0:T(8,128)(2,1)S(1)} %get-tuple-element.67), channel_id=1, source_target_pairs={{0,2},{1,3},{2,0},{3,1},{4,6},{5,7},{6,4},{7,5},{8,10},{9,11},{10,... | collective-permute-start | bytes 196616 | tf_op jit(solution)/shard_map/ppermute | solution.py:421
  53.9 6.8 %collective-permute-start.19 = (bf16[256,128]{1,0:T(8,128)(2,1)S(1)}, bf16[256,128]{1,0:T(8,128)(2,1)S(1)}, u32[]{:S(2)}, u32[]{:S(2)}) collective-permute-start(bf16[256,128]{1,0:T(8,128)(2,1)S(1)} %get-tuple-element.65), channel_id=1, source_target_pairs={{0,2},{1,3},{2,0},{3,1},{4,6},{5,7},{6,4},{7,5},{8,10},{9,11},{10,... | collective-permute-start | bytes 196616 | tf_op jit(solution)/shard_map/ppermute | solution.py:421
  58.2 5.1 %collective-permute-start.21 = (bf16[128,128]{1,0:T(8,128)(2,1)S(1)}, bf16[128,128]{1,0:T(8,128)(2,1)S(1)}, u32[]{:S(2)}, u32[]{:S(2)}) collective-permute-start(bf16[128,128]{1,0:T(8,128)(2,1)S(1)} %get-tuple-element.68), channel_id=1, source_target_pairs={{0,8},{1,13},{2,10},{3,15},{4,12},{5,9},{6,14},{7,11},{8,0},{9,5},... | collective-permute-start | bytes 98312 | tf_op jit(solution)/shard_map/ppermute | solution.py:421
  59.3 5.8 %collective-permute-start.22 = (bf16[128,128]{1,0:T(8,128)(2,1)S(1)}, bf16[128,128]{1,0:T(8,128)(2,1)S(1)}, u32[]{:S(2)}, u32[]{:S(2)}) collective-permute-start(bf16[128,128]{1,0:T(8,128)(2,1)S(1)} %get-tuple-element.69), channel_id=1, source_target_pairs={{0,12},{1,5},{2,14},{3,7},{4,8},{5,1},{6,10},{7,3},{8,4},{9,13},{1... | collective-permute-start | bytes 98312 | tf_op jit(solution)/shard_map/ppermute | solution.py:421
  60.8 4.3 %collective-permute-start.23 = (bf16[128,128]{1,0:T(8,128)(2,1)S(1)}, bf16[128,128]{1,0:T(8,128)(2,1)S(1)}, u32[]{:S(2)}, u32[]{:S(2)}) collective-permute-start(bf16[128,128]{1,0:T(8,128)(2,1)S(1)} %get-tuple-element.70), channel_id=1, source_target_pairs={{0,4},{1,9},{2,6},{3,11},{4,0},{5,13},{6,2},{7,15},{8,12},{9,1},{1... | collective-permute-start | bytes 98312 | tf_op jit(solution)/shard_map/ppermute | solution.py:421

commit v17 on v11

--- a/solution.py
+++ b/solution.py
@@ -8,7 +8,7 @@
 from jax.sharding import PartitionSpec as P
 
 ITERS = 2
-CHUNK = 8
+CHUNK = 16
 F32 = jnp.float32
 BF16 = jnp.bfloat16
 I32 = jnp.int32
@@ -96,7 +96,7 @@
 
 def setup_kernel(n_payloads, members, stride, span, sizes, tiles, wanted, *refs):
     payload_refs, refs = refs[:n_payloads], refs[-(2 * len(wanted) + 9):]
-    each = members // n_payloads
+    where = [(ref, index) for ref in payload_refs for index in range(ref.shape[0] // stride)]
     list_refs, row_ref, tables = refs[:len(wanted)], refs[len(wanted)], refs[len(wanted) + 1:-len(wanted) - 1]
     drafts, arrived = refs[-len(wanted) - 1:-1], refs[-1]
     copies = [
@@ -133,7 +133,7 @@
     lined = jnp.zeros((16, lanes), F32)
     if members <= 16:
         for member in range(members):
-            lined = collect(member, lined, payload_refs[member // each], member % each)
+            lined = collect(member, lined, *where[member])
     else:
         lined = lax.fori_loop(
             0, members, lambda member, lined: collect(member, lined, payload_refs[0], member), lined)
@@ -263,18 +263,19 @@
         start_ref, refs = refs[0], refs[1:]
     sum_refs, (out_ref, wide, second) = refs[:n_sums], refs[n_sums:]
     rows = wide.shape[0] // members
-    each = members // n_values
-    stride = value_refs[0].shape[0] // each
+    stride = sum(ref.shape[0] for ref in value_refs) // members
     rays = second.shape[0]
     line_step = tables[0].shape[0] // depth
 
-    def widen(member, carry):
-        for place, ref in enumerate(value_refs):
-            at = pl.ds(pl.multiple_of((place * each + member) * rows, rows), rows)
+    base = 0
+    for ref in value_refs:
+        def widen(member, carry, ref=ref, base=base):
+            at = pl.ds(pl.multiple_of((base + member) * rows, rows), rows)
             wide[at, :] = ref[pl.ds(pl.multiple_of(member * stride, 16), rows), :].astype(F32)
-        return carry
-
-    lax.fori_loop(0, each, widen, 0)
+            return carry
+
+        lax.fori_loop(0, ref.shape[0] // stride, widen, 0)
+        base += ref.shape[0] // stride
     second[...] = jnp.zeros_like(second)
     if start_ref is None:
         out_ref[...] = jnp.zeros_like(out_ref)
@@ -361,16 +362,16 @@
     for_slots(slots, one)
 
     def total(at):
-        return sum([bank[at, :] for bank in banks[1:]], banks[0][at, :]).astype(outs[0].dtype)
+        return sum([bank[at, :] for bank in banks[1:]], banks[0][at, :])
 
     if split:
         for ref, members in zip(outs, split):
             rows = ref.shape[0] // len(members)
             for place, member in enumerate(members):
-                ref[place * rows:(place + 1) * rows, :] = total(pl.ds(member * rows, rows))
+                ref[place * rows:(place + 1) * rows, :] = total(pl.ds(member * rows, rows)).astype(ref.dtype)
     else:
         def finish(at):
-            outs[0][at, :] = total(at)
+            outs[0][at, :] = total(at).astype(outs[0].dtype)
 
         for_rows(outs[0].shape[0], finish)
 
@@ -409,6 +410,7 @@
         scratch_shapes=list(scratch),
         compiler_params=pltpu.CompilerParams(vmem_limit_bytes=mib * 1024 * 1024),
         name=name,
+        cost_estimate=pl.CostEstimate(flops=4 * 10**9, bytes_accessed=8 * 10**6, transcendentals=0),
     )(*operands)
 
 
@@ -453,7 +455,7 @@
         waits = [] if after is None else [after]
         found = call(
             functools.partial(setup_kernel, len(payloads), members,
-                              payloads[0].shape[0] * len(payloads) // members, span, sizes,
+                              sum(one.shape[0] for one in payloads) // members, span, sizes,
                               voxel_tiles, wanted),
             "setup", 24, [VMEM] * len(payloads) + [ANY] * len(waits), out, *payloads, *waits,
             scratch=[pltpu.VMEM((8, lanes), I32)] * n + [pltpu.SemaphoreType.DMA((n,))])
@@ -479,7 +481,7 @@
         return call(
             functools.partial(backward_kernel, sizes, len(parts), start is not None, split),
             "backward", 16 if paired else 32, [SMEM] + [VMEM] * (len(operands) - 1),
-            [shape((len(some) * rows, extent), kind) for some in split]
+            [shape((len(some) * rows, extent), each) for some, each in zip(split, kind)]
             if split else shape((members * rows, extent), kind), *operands,
             scratch=[pltpu.VMEM((len(parts) * n_rays, extent), F32)]
             + [pltpu.VMEM((members * rows, extent), F32)] * n_bank)
@@ -501,13 +503,11 @@
     for sweep in range(ITERS):
         last = sweep + 1 == ITERS
         if paired:
-            over_2, over_3, over_1 = [
-                exchange(payload, n_slab, distance) for distance in (8, 12, 4)]
-            z_half = join(payload, over_2)
-            y_half = exchange(z_half, n_slab, 2)
-            z_rest = join(over_3, over_1)
-            y_rest = exchange(z_rest, n_slab, 2)
-            along_z, along_y = (z_half, z_rest), (y_half, y_rest)
+            over_2, over_1, over_3, across = [
+                exchange(payload, n_slab, distance) for distance in (8, 4, 12, 14)]
+            z_part = join(payload, over_2, over_1)
+            y_part = exchange(z_part, n_slab, 2)
+            along_z, along_y = (z_part, over_3), (y_part, across)
             if sweep == 0:
                 (z_list,), z_rows, z_forward, z_backward = setup(along_z, 4, (None,))
             both = forward(z_list, along_z, 4, z_forward, 2 * n_rays)
@@ -523,19 +523,18 @@
             residual = residual_of(own, (z_rows, y_rows), other, first_other)
             other_residual = exchange(residual, n_slab, 1)
             y_sum = backward(own_list, [residual], 4, y_backward, F32)
-            far_sum, near_sum = backward(
-                other_list, [other_residual], 4, y_backward, BF16, y_sum, ((1, 2), (0, 3)))
-            far_part, near_part = exchange(far_sum, n_slab, 2), exchange(near_sum, n_slab, 2)
-            z_sum = backward(z_list, [residual, other_residual], 4, z_backward, F32)
+            y_sum, across_sum = backward(
+                other_list, [other_residual], 4, y_backward, (BF16, BF16), y_sum, ((0, 1, 2), (3,)))
+            y_got, across_got = exchange(y_sum, n_slab, 2), exchange(across_sum, n_slab, 14)
+            z_sum, sum_3 = backward(
+                z_list, [residual, other_residual], 4, z_backward, (F32, BF16), None, ((0, 1, 2), (3,)))
+            got_3 = exchange(sum_3, n_slab, 12)
             piece = shape((rows, extent), BF16)
-            piece_2, piece_3 = call(
-                functools.partial(combine_kernel, (1, 2)), "combine", 16, [VMEM] * 2,
-                [piece, piece], z_sum, far_part)
-            got = [exchange(piece_2, n_slab, 8), exchange(piece_3, n_slab, 12)]
-            own_piece, piece_1 = call(
-                functools.partial(combine_kernel, (0, 3)), "combine", 16, [VMEM] * 2,
-                [shape((rows, extent), F32), piece], z_sum, near_part)
-            pieces = [own_piece, *got, exchange(piece_1, n_slab, 4)]
+            own_piece, piece_2, piece_1 = call(
+                functools.partial(combine_kernel, (0, 1, 2)), "combine", 16, [VMEM] * 2,
+                [shape((rows, extent), F32), piece, piece], z_sum, y_got)
+            pieces = [own_piece, exchange(piece_2, n_slab, 8), exchange(piece_1, n_slab, 4),
+                      got_3, across_got]
         else:
             everyone = lax.all_gather(payload, "slab", axis=0, tiled=True)
             if sweep == 0:

time: 66.1 us -> 64.3 us (0.973); the launches traced: 66.3 us -> 63.4 us
  starting transfers between devices: 28.8 us -> 33.1 us
  Pallas kernels: 23.1 us -> 19 us
  waiting for transfers between devices: 14 us -> 11 us
    ppermute x24, starting transfers between devices: 28.8 us -> 33.1 us  [exchange(): lax.ppermute(values, 'slab', [(device, device ^ distance) for device in r...]
    pallas_call x28 -> x24, Pallas kernels: 23.1 us -> 19 us  [call(): pl.pallas_call(kernel, out_shape=out_shape, in_specs=in_specs, out_specs=...]
    ppermute x24, waiting for transfers between devices: 14 us -> 11 us  [exchange(): lax.ppermute(values, 'slab', [(device, device ^ distance) for device in r...]
  transfers between devices with their start and end apart: 24 -> 24, of which waited for: 14 -> 13; matrix products, arithmetic and copies ran while one was open for 0% -> 0% of each run, Pallas kernels for 23% -> 18%
where the time goes in v17:
time: 64.3 us; the launch traced here: 63.4 us
  starting transfers between devices  33.1 us (51%)
  Pallas kernels  19 us (30%)
  waiting for transfers between devices  11 us (17%)
    ppermute x24, starting transfers between devices, exchange(): lax.ppermute(values, 'slab', [(device, device ^ distance) for device in r...  33.1 us
    pallas_call x24, Pallas kernels, call(): pl.pallas_call(kernel, out_shape=out_shape, in_specs=in_specs, out_specs=...  19 us
    ppermute x24, waiting for transfers between devices, exchange(): lax.ppermute(values, 'slab', [(device, device ^ distance) for device in r...  11 us
  transfers between devices with their start and end apart: 24, of which 13 were waited for; matrix products, arithmetic and copies ran while one was open for 0% of the time, Pallas kernels for 18%

profile of v17, /device:TPU:0, one launch (start us, length us, event | category | flops | bytes accessed | tf_op | source)
XLA Modules:
  0.0 63.4 jit_solution(17028779776446920107)
XLA Ops:
  0.0 1.0 %pack.1.refs_0_ = bf16[192,128]{1,0:T(8,128)(2,1)S(1)} custom-call(f32[128,128]{1,0:T(8,128)} %bitcast.8, f32[4,256]{1,0:T(4,128)} %bitcast.12, f32[4,256]{1,0:T(4,128)} %bitcast.14, s32[4,256]{1,0:T(4,128)} %bitcast.16, s32[1,256]{1,0:T(1,128)} %bitcast.20, s32[1,16]{1,0:T(1,128)} %bitcast.18), custom_call_target="tpu_custom_call" | custom-call | flops 4000000000 | bytes 8000000 | tf_op jit(solution)/shard_map/pack/pallas_call | solution.py:404
  1.0 4.1 %collective-permute-start = (bf16[192,128]{1,0:T(8,128)(2,1)S(1)}, bf16[192,128]{1,0:T(8,128)(2,1)S(1)}, u32[]{:S(2)}, u32[]{:S(2)}) collective-permute-start(bf16[192,128]{1,0:T(8,128)(2,1)S(1)} %pack.1.refs_0_), channel_id=1, source_target_pairs={{0,8},{1,9},{2,10},{3,11},{4,12},{5,13},{6,14},{7,15},{8,0},{9,1},... | collective-permute-start | bytes 147464 | tf_op jit(solution)/shard_map/ppermute | solution.py:418
  5.2 1.6 %collective-permute-start.1 = (bf16[192,128]{1,0:T(8,128)(2,1)S(1)}, bf16[192,128]{1,0:T(8,128)(2,1)S(1)}, u32[]{:S(2)}, u32[]{:S(2)}) collective-permute-start(bf16[192,128]{1,0:T(8,128)(2,1)S(1)} %pack.1.refs_0_), channel_id=1, source_target_pairs={{0,4},{1,5},{2,6},{3,7},{4,0},{5,1},{6,2},{7,3},{8,12},{9,13},{10,... | collective-permute-start | bytes 147464 | tf_op jit(solution)/shard_map/ppermute | solution.py:418
  6.7 4.8 %collective-permute-start.4 = (bf16[192,128]{1,0:T(8,128)(2,1)S(1)}, bf16[192,128]{1,0:T(8,128)(2,1)S(1)}, u32[]{:S(2)}, u32[]{:S(2)}) collective-permute-start(bf16[192,128]{1,0:T(8,128)(2,1)S(1)} %pack.1.refs_0_), channel_id=1, source_target_pairs={{0,14},{1,15},{2,12},{3,13},{4,10},{5,11},{6,8},{7,9},{8,6},{9,7},... | collective-permute-start | bytes 147464 | tf_op jit(solution)/shard_map/ppermute | solution.py:418
  12.6 1.5 %setup.2 = (s32[8,128]{1,0:T(8,128)S(4)}, f32[64,128]{1,0:T(8,128)S(1)}, s32[544,128]{1,0:T(8,128)S(1)}, f32[544,128]{1,0:T(8,128)S(1)}, f32[544,128]{1,0:T(8,12...) custom-call(bf16[576,128]{1,0:T(8,128)(2,1)S(1)} %join.2.refs_0_, ...), custom_call_target="tpu_custom_call" | custom-call | flops 4000000000 | bytes 8000000 | tf_op jit(solution)/shard_map/setup/pallas_call | solution.py:404
  14.1 2.2 %forward.6.refs_2_.refs_6_ = f32[512,128]{1,0:T(8,128)S(1)} custom-call(s32[8,128]{1,0:T(8,128)S(4)} %get-tuple-element.40.slots, bf16[576,128]{1,0:T(8,128)(2,1)S(1)} %join.2.refs_0_, bf16[192,128]{1,0:T(8,128)(2,1)S(1)} %collective-permute-done.2.refs_1_, s32[544,128]{1,0:T(8,128)S(1)} %get-tuple-element.41.refs_2_, ...), custom_call_target="tpu_custom_call" | custom-call | flops 4000000000 | bytes 8000000 | tf_op jit(solution)/shard_map/forward/pallas_call | solution.py:404
  16.7 1.6 %setup.3 = (s32[8,128]{1,0:T(8,128)S(4)}, s32[8,128]{1,0:T(8,128)S(4)}, f32[64,128]{1,0:T(8,128)S(1)}, s32[544,128]{1,0:T(8,128)S(1)}, f32[544,128]{1,0:T(8,128)...) custom-call(bf16[576,128]{1,0:T(8,128)(2,1)S(1)} %collective-permute, ...), custom_call_target="tpu_custom_call" | custom-call | flops 4000000000 | bytes 8000000 | tf_op jit(solution)/shard_map/setup/pallas_call | solution.py:404
  18.3 1.1 %forward.8 = f32[288,128]{1,0:T(8,128)S(1)} custom-call(s32[8,128]{1,0:T(8,128)S(4)} %get-tuple-element.52.slots, bf16[576,128]{1,0:T(8,128)(2,1)S(1)} %collective-permute-done.3.refs_0_, bf16[192,128]{1,0:T(8,128)(2,1)S(1)} %collective-permute-done.4.refs_1_, s32[544,128]{1,0:T(8,128)S(1)} %get-tuple-element.46.refs_2_, ...), custom_call_target="tpu_custom_call" | custom-call | flops 4000000000 | bytes 8000000 | tf_op jit(solution)/shard_map/forward/pallas_call | solution.py:404
  20.0 0.9 %collective-permute-done.5.refs_2_.refs_3_ = f32[288,128]{1,0:T(8,128)S(1)} collective-permute-done((f32[288,128]{1,0:T(8,128)S(1)}, f32[288,128]{1,0:T(8,128)S(1)}, u32[]{:S(2)}, u32[]{:S(2)}) %collective-permute-start.5) | collective-permute-done | bytes 147488 | tf_op jit(solution)/shard_map/ppermute | solution.py:418
  21.5 0.7 %collective-permute-done.6.refs_1_.refs_0_ = bf16[256,128]{1,0:T(8,128)(2,1)S(1)} collective-permute-done((bf16[256,128]{1,0:T(8,128)(2,1)S(1)}, bf16[256,128]{1,0:T(8,128)(2,1)S(1)}, u32[]{:S(2)}, u32[]{:S(2)}) %collective-permute-start.6) | collective-permute-done | bytes 65568 | tf_op jit(solution)/shard_map/ppermute | solution.py:418
  22.2 0.9 %backward.8 = (bf16[384,128]{1,0:T(8,128)(2,1)S(1)}, bf16[128,128]{1,0:T(8,128)(2,1)S(1)}) custom-call(s32[8,128]{1,0:T(8,128)S(4)} %get-tuple-element.52.slots, bf16[256,128]{1,0:T(8,128)(2,1)S(1)} %collective-permute-done.6.refs_1_.refs_0_, s32[544,128]{1,0:T(8,128)S(1)} %get-tuple-element.57.refs_1_, f32[544,128]{1,0:T(8,128)S(1)} %get-tuple-element.58.refs_2_, ...), custom_call_target="tpu_custom_call" | custom-call | flops 4000000000 | bytes 8000000 | tf_op jit(solution)/shard_map/backward/pallas_call | solution.py:404
  23.7 1.9 %collective-permute-start.11 = (bf16[128,128]{1,0:T(8,128)(2,1)S(1)}, bf16[128,128]{1,0:T(8,128)(2,1)S(1)}, u32[]{:S(2)}, u32[]{:S(2)}) collective-permute-start(bf16[128,128]{1,0:T(8,128)(2,1)S(1)} %get-tuple-element.65), channel_id=1, source_target_pairs={{0,14},{1,15},{2,12},{3,13},{4,10},{5,11},{6,8},{7,9},{8,6},{9,7},... | collective-permute-start | bytes 98312 | tf_op jit(solution)/shard_map/ppermute | solution.py:418
  25.6 1.7 %backward.6 = (f32[384,128]{1,0:T(8,128)S(1)}, bf16[128,128]{1,0:T(8,128)(2,1)S(1)}) custom-call(s32[8,128]{1,0:T(8,128)S(4)} %get-tuple-element.40.slots, bf16[256,128]{1,0:T(8,128)(2,1)S(1)} %residual.2.refs_0_, bf16[256,128]{1,0:T(8,128)(2,1)S(1)} %collective-permute-done.6.refs_1_.refs_0_, s32[544,128]{1,0:T(8,128)S(1)} %get-tuple-element.53.refs_2_, ...), custom_call_target="tpu_custom_call" | custom-call | flops 4000000000 | bytes 8000000 | tf_op jit(solution)/shard_map/backward/pallas_call | solution.py:404
  27.4 2.4 %collective-permute-start.10 = (bf16[128,128]{1,0:T(8,128)(2,1)S(1)}, bf16[128,128]{1,0:T(8,128)(2,1)S(1)}, u32[]{:S(2)}, u32[]{:S(2)}) collective-permute-start(bf16[128,128]{1,0:T(8,128)(2,1)S(1)} %get-tuple-element.64), channel_id=1, source_target_pairs={{0,12},{1,13},{2,14},{3,15},{4,8},{5,9},{6,10},{7,11},{8,4},{9,5},... | collective-permute-start | bytes 98312 | tf_op jit(solution)/shard_map/ppermute | solution.py:418
  29.9 2.0 %collective-permute-start.9 = (bf16[128,128]{1,0:T(8,128)(2,1)S(1)}, bf16[128,128]{1,0:T(8,128)(2,1)S(1)}, u32[]{:S(2)}, u32[]{:S(2)}) collective-permute-start(bf16[128,128]{1,0:T(8,128)(2,1)S(1)} %get-tuple-element.63), channel_id=1, source_target_pairs={{0,4},{1,5},{2,6},{3,7},{4,0},{5,1},{6,2},{7,3},{8,12},{9,13},{10,... | collective-permute-start | bytes 98312 | tf_op jit(solution)/shard_map/ppermute | solution.py:418
  33.2 1.6 %collective-permute-done.8.refs_1_ = bf16[128,128]{1,0:T(8,128)(2,1)S(1)} collective-permute-done((bf16[128,128]{1,0:T(8,128)(2,1)S(1)}, bf16[128,128]{1,0:T(8,128)(2,1)S(1)}, u32[]{:S(2)}, u32[]{:S(2)}) %collective-permute-start.8) | collective-permute-done | bytes 32800 | tf_op jit(solution)/shard_map/ppermute | solution.py:418
  34.8 2.1 %collective-permute-start.12 = (bf16[128,128]{1,0:T(8,128)(2,1)S(1)}, bf16[128,128]{1,0:T(8,128)(2,1)S(1)}, u32[]{:S(2)}, u32[]{:S(2)}) collective-permute-start(bf16[128,128]{1,0:T(8,128)(2,1)S(1)} %get-tuple-element.67.refs_0_), channel_id=1, source_target_pairs={{0,8},{1,9},{2,10},{3,11},{4,12},{5,13},{6,14},{7,15},{8,0},{9,1},... | collective-permute-start | bytes 98312 | tf_op jit(solution)/shard_map/ppermute | solution.py:418
  37.2 2.0 %collective-permute-start.16 = (bf16[128,128]{1,0:T(8,128)(2,1)S(1)}, bf16[128,128]{1,0:T(8,128)(2,1)S(1)}, u32[]{:S(2)}, u32[]{:S(2)}) collective-permute-start(bf16[128,128]{1,0:T(8,128)(2,1)S(1)} %get-tuple-element.67.refs_0_), channel_id=1, source_target_pairs={{0,12},{1,13},{2,14},{3,15},{4,8},{5,9},{6,10},{7,11},{8,4},{9,5},... | collective-permute-start | bytes 98312 | tf_op jit(solution)/shard_map/ppermute | solution.py:418
  39.2 2.1 %collective-permute-start.15 = (bf16[128,128]{1,0:T(8,128)(2,1)S(1)}, bf16[128,128]{1,0:T(8,128)(2,1)S(1)}, u32[]{:S(2)}, u32[]{:S(2)}) collective-permute-start(bf16[128,128]{1,0:T(8,128)(2,1)S(1)} %get-tuple-element.67.refs_0_), channel_id=1, source_target_pairs={{0,14},{1,15},{2,12},{3,13},{4,10},{5,11},{6,8},{7,9},{8,6},{9,7},... | collective-permute-start | bytes 98312 | tf_op jit(solution)/shard_map/ppermute | solution.py:418
  41.3 1.2 %collective-permute-start.14 = (bf16[384,128]{1,0:T(8,128)(2,1)S(1)}, bf16[384,128]{1,0:T(8,128)(2,1)S(1)}, u32[]{:S(2)}, u32[]{:S(2)}) collective-permute-start(bf16[384,128]{1,0:T(8,128)(2,1)S(1)} %join.3.refs_0_), channel_id=1, source_target_pairs={{0,2},{1,3},{2,0},{3,1},{4,6},{5,7},{6,4},{7,5},{8,10},{9,11},{10,... | collective-permute-start | bytes 294920 | tf_op jit(solution)/shard_map/ppermute | solution.py:418
  42.9 2.2 %forward.9.refs_6_ = f32[512,128]{1,0:T(8,128)S(1)} custom-call(s32[8,128]{1,0:T(8,128)S(4)} %get-tuple-element.40.slots, bf16[384,128]{1,0:T(8,128)(2,1)S(1)} %join.3.refs_0_, bf16[128,128]{1,0:T(8,128)(2,1)S(1)} %collective-permute-done.16.refs_1_, s32[544,128]{1,0:T(8,128)S(1)} %get-tuple-element.41.refs_2_, f32[544,128]{1,0:T(8,128)S(1)} %get-tuple-element.42.refs_3_, ...), custom_call_target="tpu_custom_call" | custom-call | flops 4000000000 | bytes 8000000 | tf_op jit(solution)/shard_map/forward/pallas_call | solution.py:404
  45.1 0.8 %collective-permute-done.15.refs_1_ = bf16[128,128]{1,0:T(8,128)(2,1)S(1)} collective-permute-done((bf16[128,128]{1,0:T(8,128)(2,1)S(1)}, bf16[128,128]{1,0:T(8,128)(2,1)S(1)}, u32[]{:S(2)}, u32[]{:S(2)}) %collective-permute-start.15) | collective-permute-done | bytes 32800 | tf_op jit(solution)/shard_map/ppermute | solution.py:418
  46.4 1.1 %forward.11 = f32[256,128]{1,0:T(8,128)S(1)} custom-call(s32[8,128]{1,0:T(8,128)S(4)} %get-tuple-element.52.slots, bf16[384,128]{1,0:T(8,128)(2,1)S(1)} %collective-permute-done.14.refs_0_, bf16[128,128]{1,0:T(8,128)(2,1)S(1)} %collective-permute-done.15.refs_1_, s32[544,128]{1,0:T(8,128)S(1)} %get-tuple-element.46.refs_2_, ...), custom_call_target="tpu_custom_call" | custom-call | flops 4000000000 | bytes 8000000 | tf_op jit(solution)/shard_map/forward/pallas_call | solution.py:404
  48.0 0.9 %collective-permute-done.17.refs_2_ = f32[256,128]{1,0:T(8,128)S(1)} collective-permute-done((f32[256,128]{1,0:T(8,128)S(1)}, f32[256,128]{1,0:T(8,128)S(1)}, u32[]{:S(2)}, u32[]{:S(2)}) %collective-permute-start.17) | collective-permute-done | bytes 131104 | tf_op jit(solution)/shard_map/ppermute | solution.py:418
  50.2 0.9 %backward.11 = (bf16[384,128]{1,0:T(8,128)(2,1)S(1)}, bf16[128,128]{1,0:T(8,128)(2,1)S(1)}) custom-call(s32[8,128]{1,0:T(8,128)S(4)} %get-tuple-element.52.slots, bf16[256,128]{1,0:T(8,128)(2,1)S(1)} %collective-permute-done.18.refs_1_.refs_0_, s32[544,128]{1,0:T(8,128)S(1)} %get-tuple-element.57.refs_1_, f32[544,128]{1,0:T(8,128)S(1)} %get-tuple-element.58.refs_2_, ...), custom_call_target="tpu_custom_call" | custom-call | flops 4000000000 | bytes 8000000 | tf_op jit(solution)/shard_map/backward/pallas_call | solution.py:404
  51.2 1.2 %collective-permute-start.19 = (bf16[384,128]{1,0:T(8,128)(2,1)S(1)}, bf16[384,128]{1,0:T(8,128)(2,1)S(1)}, u32[]{:S(2)}, u32[]{:S(2)}) collective-permute-start(bf16[384,128]{1,0:T(8,128)(2,1)S(1)} %get-tuple-element.69), channel_id=1, source_target_pairs={{0,2},{1,3},{2,0},{3,1},{4,6},{5,7},{6,4},{7,5},{8,10},{9,11},{10,... | collective-permute-start | bytes 294920 | tf_op jit(solution)/shard_map/ppermute | solution.py:418
  52.4 1.0 %collective-permute-start.23 = (bf16[128,128]{1,0:T(8,128)(2,1)S(1)}, bf16[128,128]{1,0:T(8,128)(2,1)S(1)}, u32[]{:S(2)}, u32[]{:S(2)}) collective-permute-start(bf16[128,128]{1,0:T(8,128)(2,1)S(1)} %get-tuple-element.74), channel_id=1, source_target_pairs={{0,14},{1,15},{2,12},{3,13},{4,10},{5,11},{6,8},{7,9},{8,6},{9,7},... | collective-permute-start | bytes 98312 | tf_op jit(solution)/shard_map/ppermute | solution.py:418
  53.4 1.7 %backward.9 = (f32[384,128]{1,0:T(8,128)S(1)}, bf16[128,128]{1,0:T(8,128)(2,1)S(1)}) custom-call(s32[8,128]{1,0:T(8,128)S(4)} %get-tuple-element.40.slots, bf16[256,128]{1,0:T(8,128)(2,1)S(1)} %residual.3.refs_0_, bf16[256,128]{1,0:T(8,128)(2,1)S(1)} %collective-permute-done.18.refs_1_.refs_0_, s32[544,128]{1,0:T(8,128)S(1)} %get-tuple-element.53.refs_2_, ...), custom_call_target="tpu_custom_call" | custom-call | flops 4000000000 | bytes 8000000 | tf_op jit(solution)/shard_map/backward/pallas_call | solution.py:404
  55.2 2.6 %collective-permute-start.22 = (bf16[128,128]{1,0:T(8,128)(2,1)S(1)}, bf16[128,128]{1,0:T(8,128)(2,1)S(1)}, u32[]{:S(2)}, u32[]{:S(2)}) collective-permute-start(bf16[128,128]{1,0:T(8,128)(2,1)S(1)} %get-tuple-element.73), channel_id=1, source_target_pairs={{0,12},{1,13},{2,14},{3,15},{4,8},{5,9},{6,10},{7,11},{8,4},{9,5},... | collective-permute-start | bytes 98312 | tf_op jit(solution)/shard_map/ppermute | solution.py:418
  57.9 1.8 %collective-permute-start.21 = (bf16[128,128]{1,0:T(8,128)(2,1)S(1)}, bf16[128,128]{1,0:T(8,128)(2,1)S(1)}, u32[]{:S(2)}, u32[]{:S(2)}) collective-permute-start(bf16[128,128]{1,0:T(8,128)(2,1)S(1)} %get-tuple-element.72), channel_id=1, source_target_pairs={{0,4},{1,5},{2,6},{3,7},{4,0},{5,1},{6,2},{7,3},{8,12},{9,13},{10,... | collective-permute-start | bytes 98312 | tf_op jit(solution)/shard_map/ppermute | solution.py:418
  59.7 1.2 %collective-permute-done.22.refs_3_ = bf16[128,128]{1,0:T(8,128)(2,1)S(1)} collective-permute-done((bf16[128,128]{1,0:T(8,128)(2,1)S(1)}, bf16[128,128]{1,0:T(8,128)(2,1)S(1)}, u32[]{:S(2)}, u32[]{:S(2)}) %collective-permute-start.22) | collective-permute-done | bytes 32800 | tf_op jit(solution)/shard_map/ppermute | solution.py:418
  60.9 1.8 %collective-permute-done.20.refs_1_ = bf16[128,128]{1,0:T(8,128)(2,1)S(1)} collective-permute-done((bf16[128,128]{1,0:T(8,128)(2,1)S(1)}, bf16[128,128]{1,0:T(8,128)(2,1)S(1)}, u32[]{:S(2)}, u32[]{:S(2)}) %collective-permute-start.20) | collective-permute-done | bytes 32800 | tf_op jit(solution)/shard_map/ppermute | solution.py:418
  (52 shorter events, 8.3 us)
Async XLA Ops:
  1.0 10.5 %collective-permute-start = (bf16[192,128]{1,0:T(8,128)(2,1)S(1)}, bf16[192,128]{1,0:T(8,128)(2,1)S(1)}, u32[]{:S(2)}, u32[]{:S(2)}) collective-permute-start(bf16[192,128]{1,0:T(8,128)(2,1)S(1)} %pack.1.refs_0_), channel_id=1, source_target_pairs={{0,8},{1,9},{2,10},{3,11},{4,12},{5,13},{6,14},{7,15},{8,0},{9,1},... | collective-permute-start | bytes 147464 | tf_op jit(solution)/shard_map/ppermute | solution.py:418
  5.2 6.4 %collective-permute-start.1 = (bf16[192,128]{1,0:T(8,128)(2,1)S(1)}, bf16[192,128]{1,0:T(8,128)(2,1)S(1)}, u32[]{:S(2)}, u32[]{:S(2)}) collective-permute-start(bf16[192,128]{1,0:T(8,128)(2,1)S(1)} %pack.1.refs_0_), channel_id=1, source_target_pairs={{0,4},{1,5},{2,6},{3,7},{4,0},{5,1},{6,2},{7,3},{8,12},{9,13},{10,... | collective-permute-start | bytes 147464 | tf_op jit(solution)/shard_map/ppermute | solution.py:418
  6.7 5.9 %collective-permute-start.2 = (bf16[192,128]{1,0:T(8,128)(2,1)S(1)}, bf16[192,128]{1,0:T(8,128)(2,1)S(1)}, u32[]{:S(2)}, u32[]{:S(2)}) collective-permute-start(bf16[192,128]{1,0:T(8,128)(2,1)S(1)} %pack.1.refs_0_), channel_id=1, source_target_pairs={{0,12},{1,13},{2,14},{3,15},{4,8},{5,9},{6,10},{7,11},{8,4},{9,5},... | collective-permute-start | bytes 147464 | tf_op jit(solution)/shard_map/ppermute | solution.py:418
  6.7 9.6 %collective-permute-start.4 = (bf16[192,128]{1,0:T(8,128)(2,1)S(1)}, bf16[192,128]{1,0:T(8,128)(2,1)S(1)}, u32[]{:S(2)}, u32[]{:S(2)}) collective-permute-start(bf16[192,128]{1,0:T(8,128)(2,1)S(1)} %pack.1.refs_0_), channel_id=1, source_target_pairs={{0,14},{1,15},{2,12},{3,13},{4,10},{5,11},{6,8},{7,9},{8,6},{9,7},... | collective-permute-start | bytes 147464 | tf_op jit(solution)/shard_map/ppermute | solution.py:418
  11.5 5.2 %collective-permute-start.3 = (bf16[576,128]{1,0:T(8,128)(2,1)S(1)}, bf16[576,128]{1,0:T(8,128)(2,1)S(1)}, u32[]{:S(2)}, u32[]{:S(2)}) collective-permute-start(bf16[576,128]{1,0:T(8,128)(2,1)S(1)} %join.2.refs_0_), channel_id=1, source_target_pairs={{0,2},{1,3},{2,0},{3,1},{4,6},{5,7},{6,4},{7,5},{8,10},{9,11},{10,... | collective-permute-start | bytes 442376 | tf_op jit(solution)/shard_map/ppermute | solution.py:418
  19.4 1.4 %collective-permute-start.5 = (f32[288,128]{1,0:T(8,128)S(1)}, f32[288,128]{1,0:T(8,128)S(1)}, u32[]{:S(2)}, u32[]{:S(2)}) collective-permute-start(f32[288,128]{1,0:T(8,128)S(1)} %forward.8), channel_id=1, source_target_pairs={{0,1},{1,0},{2,3},{3,2},{4,5},{5,4},{6,7},{7,6},{8,9},{9,8},{10,11... | collective-permute-start | bytes 442376 | tf_op jit(solution)/shard_map/ppermute | solution.py:418
  19.5 1.4 %copy-start.1 = (bf16[32,8,128]{2,1,0:T(8,128)(2,1)S(1)}, bf16[32,8,128]{2,1,0:T(8,128)(2,1)}, u32[]{:S(2)}) copy-start(bf16[32,8,128]{2,1,0:T(8,128)(2,1)} %param.7) | copy-start | bytes 196612
  20.9 1.3 %collective-permute-start.6 = (bf16[256,128]{1,0:T(8,128)(2,1)S(1)}, bf16[256,128]{1,0:T(8,128)(2,1)S(1)}, u32[]{:S(2)}, u32[]{:S(2)}) collective-permute-start(bf16[256,128]{1,0:T(8,128)(2,1)S(1)} %residual.2.refs_0_), channel_id=1, source_target_pairs={{0,1},{1,0},{2,3},{3,2},{4,5},{5,4},{6,7},{7,6},{8,9},{9,8},{10,11... | collective-permute-start | bytes 196616 | tf_op jit(solution)/shard_map/ppermute | solution.py:418
  23.2 6.6 %collective-permute-start.7 = (bf16[384,128]{1,0:T(8,128)(2,1)S(1)}, bf16[384,128]{1,0:T(8,128)(2,1)S(1)}, u32[]{:S(2)}, u32[]{:S(2)}) collective-permute-start(bf16[384,128]{1,0:T(8,128)(2,1)S(1)} %get-tuple-element.60), channel_id=1, source_target_pairs={{0,2},{1,3},{2,0},{3,1},{4,6},{5,7},{6,4},{7,5},{8,10},{9,11},{10,... | collective-permute-start | bytes 294920 | tf_op jit(solution)/shard_map/ppermute | solution.py:418
  23.7 8.8 %collective-permute-start.11 = (bf16[128,128]{1,0:T(8,128)(2,1)S(1)}, bf16[128,128]{1,0:T(8,128)(2,1)S(1)}, u32[]{:S(2)}, u32[]{:S(2)}) collective-permute-start(bf16[128,128]{1,0:T(8,128)(2,1)S(1)} %get-tuple-element.65), channel_id=1, source_target_pairs={{0,14},{1,15},{2,12},{3,13},{4,10},{5,11},{6,8},{7,9},{8,6},{9,7},... | collective-permute-start | bytes 98312 | tf_op jit(solution)/shard_map/ppermute | solution.py:418
  27.4 5.8 %collective-permute-start.10 = (bf16[128,128]{1,0:T(8,128)(2,1)S(1)}, bf16[128,128]{1,0:T(8,128)(2,1)S(1)}, u32[]{:S(2)}, u32[]{:S(2)}) collective-permute-start(bf16[128,128]{1,0:T(8,128)(2,1)S(1)} %get-tuple-element.64), channel_id=1, source_target_pairs={{0,12},{1,13},{2,14},{3,15},{4,8},{5,9},{6,10},{7,11},{8,4},{9,5},... | collective-permute-start | bytes 98312 | tf_op jit(solution)/shard_map/ppermute | solution.py:418
  29.8 2.1 %copy-start.2 = (f32[256,4]{0,1:T(4,128)S(1)}, f32[256,4]{0,1:T(4,128)}, u32[]{:S(2)}) copy-start(f32[256,4]{0,1:T(4,128)} %param.13) | copy-start | bytes 12292
  29.8 2.1 %copy-start.3 = (f32[256,4]{0,1:T(4,128)S(1)}, f32[256,4]{0,1:T(4,128)}, u32[]{:S(2)}) copy-start(f32[256,4]{0,1:T(4,128)} %param.12) | copy-start | bytes 12292
  29.8 2.1 %copy-start.4 = (s32[256,4]{0,1:T(4,128)S(1)}, s32[256,4]{0,1:T(4,128)}, u32[]{:S(2)}) copy-start(s32[256,4]{0,1:T(4,128)} %param.9) | copy-start | bytes 12292
  29.8 2.1 %copy-start.5 = (s32[16]{0:T(128)S(1)}, s32[16]{0:T(128)}, u32[]{:S(2)}) copy-start(s32[16]{0:T(128)} %param.11) | copy-start | bytes 196
  29.8 4.9 %collective-permute-start.8 = (bf16[128,128]{1,0:T(8,128)(2,1)S(1)}, bf16[128,128]{1,0:T(8,128)(2,1)S(1)}, u32[]{:S(2)}, u32[]{:S(2)}) collective-permute-start(bf16[128,128]{1,0:T(8,128)(2,1)S(1)} %get-tuple-element.62), channel_id=1, source_target_pairs={{0,8},{1,9},{2,10},{3,11},{4,12},{5,13},{6,14},{7,15},{8,0},{9,1},... | collective-permute-start | bytes 98312 | tf_op jit(solution)/shard_map/ppermute | solution.py:418
  29.9 4.8 %copy-start = (f32[16,8,128]{2,1,0:T(8,128)S(1)}, f32[16,8,128]{2,1,0:T(8,128)}, u32[]{:S(2)}) copy-start(f32[16,8,128]{2,1,0:T(8,128)} %param.8) | copy-start | bytes 196612
  29.9 4.8 %collective-permute-start.9 = (bf16[128,128]{1,0:T(8,128)(2,1)S(1)}, bf16[128,128]{1,0:T(8,128)(2,1)S(1)}, u32[]{:S(2)}, u32[]{:S(2)}) collective-permute-start(bf16[128,128]{1,0:T(8,128)(2,1)S(1)} %get-tuple-element.63), channel_id=1, source_target_pairs={{0,4},{1,5},{2,6},{3,7},{4,0},{5,1},{6,2},{7,3},{8,12},{9,13},{10,... | collective-permute-start | bytes 98312 | tf_op jit(solution)/shard_map/ppermute | solution.py:418
  34.8 6.5 %collective-permute-start.12 = (bf16[128,128]{1,0:T(8,128)(2,1)S(1)}, bf16[128,128]{1,0:T(8,128)(2,1)S(1)}, u32[]{:S(2)}, u32[]{:S(2)}) collective-permute-start(bf16[128,128]{1,0:T(8,128)(2,1)S(1)} %get-tuple-element.67.refs_0_), channel_id=1, source_target_pairs={{0,8},{1,9},{2,10},{3,11},{4,12},{5,13},{6,14},{7,15},{8,0},{9,1},... | collective-permute-start | bytes 98312 | tf_op jit(solution)/shard_map/ppermute | solution.py:418
  36.9 4.5 %collective-permute-start.13 = (bf16[128,128]{1,0:T(8,128)(2,1)S(1)}, bf16[128,128]{1,0:T(8,128)(2,1)S(1)}, u32[]{:S(2)}, u32[]{:S(2)}) collective-permute-start(bf16[128,128]{1,0:T(8,128)(2,1)S(1)} %get-tuple-element.67.refs_0_), channel_id=1, source_target_pairs={{0,4},{1,5},{2,6},{3,7},{4,0},{5,1},{6,2},{7,3},{8,12},{9,13},{10,... | collective-permute-start | bytes 98312 | tf_op jit(solution)/shard_map/ppermute | solution.py:418
  37.2 5.7 %collective-permute-start.16 = (bf16[128,128]{1,0:T(8,128)(2,1)S(1)}, bf16[128,128]{1,0:T(8,128)(2,1)S(1)}, u32[]{:S(2)}, u32[]{:S(2)}) collective-permute-start(bf16[128,128]{1,0:T(8,128)(2,1)S(1)} %get-tuple-element.67.refs_0_), channel_id=1, source_target_pairs={{0,12},{1,13},{2,14},{3,15},{4,8},{5,9},{6,10},{7,11},{8,4},{9,5},... | collective-permute-start | bytes 98312 | tf_op jit(solution)/shard_map/ppermute | solution.py:418
  39.2 6.7 %collective-permute-start.15 = (bf16[128,128]{1,0:T(8,128)(2,1)S(1)}, bf16[128,128]{1,0:T(8,128)(2,1)S(1)}, u32[]{:S(2)}, u32[]{:S(2)}) collective-permute-start(bf16[128,128]{1,0:T(8,128)(2,1)S(1)} %get-tuple-element.67.refs_0_), channel_id=1, source_target_pairs={{0,14},{1,15},{2,12},{3,13},{4,10},{5,11},{6,8},{7,9},{8,6},{9,7},... | collective-permute-start | bytes 98312 | tf_op jit(solution)/shard_map/ppermute | solution.py:418
  41.3 5.0 %collective-permute-start.14 = (bf16[384,128]{1,0:T(8,128)(2,1)S(1)}, bf16[384,128]{1,0:T(8,128)(2,1)S(1)}, u32[]{:S(2)}, u32[]{:S(2)}) collective-permute-start(bf16[384,128]{1,0:T(8,128)(2,1)S(1)} %join.3.refs_0_), channel_id=1, source_target_pairs={{0,2},{1,3},{2,0},{3,1},{4,6},{5,7},{6,4},{7,5},{8,10},{9,11},{10,... | collective-permute-start | bytes 294920 | tf_op jit(solution)/shard_map/ppermute | solution.py:418
  47.5 1.4 %collective-permute-start.17 = (f32[256,128]{1,0:T(8,128)S(1)}, f32[256,128]{1,0:T(8,128)S(1)}, u32[]{:S(2)}, u32[]{:S(2)}) collective-permute-start(f32[256,128]{1,0:T(8,128)S(1)} %forward.11), channel_id=1, source_target_pairs={{0,1},{1,0},{2,3},{3,2},{4,5},{5,4},{6,7},{7,6},{8,9},{9,8},{10,11... | collective-permute-start | bytes 393224 | tf_op jit(solution)/shard_map/ppermute | solution.py:418
  48.9 1.3 %collective-permute-start.18 = (bf16[256,128]{1,0:T(8,128)(2,1)S(1)}, bf16[256,128]{1,0:T(8,128)(2,1)S(1)}, u32[]{:S(2)}, u32[]{:S(2)}) collective-permute-start(bf16[256,128]{1,0:T(8,128)(2,1)S(1)} %residual.3.refs_0_), channel_id=1, source_target_pairs={{0,1},{1,0},{2,3},{3,2},{4,5},{5,4},{6,7},{7,6},{8,9},{9,8},{10,11... | collective-permute-start | bytes 196616 | tf_op jit(solution)/shard_map/ppermute | solution.py:418
  51.2 6.6 %collective-permute-start.19 = (bf16[384,128]{1,0:T(8,128)(2,1)S(1)}, bf16[384,128]{1,0:T(8,128)(2,1)S(1)}, u32[]{:S(2)}, u32[]{:S(2)}) collective-permute-start(bf16[384,128]{1,0:T(8,128)(2,1)S(1)} %get-tuple-element.69), channel_id=1, source_target_pairs={{0,2},{1,3},{2,0},{3,1},{4,6},{5,7},{6,4},{7,5},{8,10},{9,11},{10,... | collective-permute-start | bytes 294920 | tf_op jit(solution)/shard_map/ppermute | solution.py:418
  52.4 7.3 %collective-permute-start.23 = (bf16[128,128]{1,0:T(8,128)(2,1)S(1)}, bf16[128,128]{1,0:T(8,128)(2,1)S(1)}, u32[]{:S(2)}, u32[]{:S(2)}) collective-permute-start(bf16[128,128]{1,0:T(8,128)(2,1)S(1)} %get-tuple-element.74), channel_id=1, source_target_pairs={{0,14},{1,15},{2,12},{3,13},{4,10},{5,11},{6,8},{7,9},{8,6},{9,7},... | collective-permute-start | bytes 98312 | tf_op jit(solution)/shard_map/ppermute | solution.py:418
  55.2 5.8 %collective-permute-start.22 = (bf16[128,128]{1,0:T(8,128)(2,1)S(1)}, bf16[128,128]{1,0:T(8,128)(2,1)S(1)}, u32[]{:S(2)}, u32[]{:S(2)}) collective-permute-start(bf16[128,128]{1,0:T(8,128)(2,1)S(1)} %get-tuple-element.73), channel_id=1, source_target_pairs={{0,12},{1,13},{2,14},{3,15},{4,8},{5,9},{6,10},{7,11},{8,4},{9,5},... | collective-permute-start | bytes 98312 | tf_op jit(solution)/shard_map/ppermute | solution.py:418
  57.8 4.9 %collective-permute-start.20 = (bf16[128,128]{1,0:T(8,128)(2,1)S(1)}, bf16[128,128]{1,0:T(8,128)(2,1)S(1)}, u32[]{:S(2)}, u32[]{:S(2)}) collective-permute-start(bf16[128,128]{1,0:T(8,128)(2,1)S(1)} %get-tuple-element.71), channel_id=1, source_target_pairs={{0,8},{1,9},{2,10},{3,11},{4,12},{5,13},{6,14},{7,15},{8,0},{9,1},... | collective-permute-start | bytes 98312 | tf_op jit(solution)/shard_map/ppermute | solution.py:418
  57.9 4.8 %collective-permute-start.21 = (bf16[128,128]{1,0:T(8,128)(2,1)S(1)}, bf16[128,128]{1,0:T(8,128)(2,1)S(1)}, u32[]{:S(2)}, u32[]{:S(2)}) collective-permute-start(bf16[128,128]{1,0:T(8,128)(2,1)S(1)} %get-tuple-element.72), channel_id=1, source_target_pairs={{0,4},{1,5},{2,6},{3,7},{4,0},{5,1},{6,2},{7,3},{8,12},{9,13},{10,... | collective-permute-start | bytes 98312 | tf_op jit(solution)/shard_map/ppermute | solution.py:418

commit v18 on v17

--- a/solution.py
+++ b/solution.py
@@ -229,7 +229,7 @@
 
 
 def spread(ref, row, frames):
-    return jnp.broadcast_to(ref[pl.ds(row, 1), :], (frames, ref.shape[1]))
+    return ref[pl.ds(row, frames, stride=0), :]
 
 
 def tile_at(start, frames):
@@ -523,18 +523,19 @@
             residual = residual_of(own, (z_rows, y_rows), other, first_other)
             other_residual = exchange(residual, n_slab, 1)
             y_sum = backward(own_list, [residual], 4, y_backward, F32)
-            y_sum, across_sum = backward(
-                other_list, [other_residual], 4, y_backward, (BF16, BF16), y_sum, ((0, 1, 2), (3,)))
-            y_got, across_got = exchange(y_sum, n_slab, 2), exchange(across_sum, n_slab, 14)
-            z_sum, sum_3 = backward(
-                z_list, [residual, other_residual], 4, z_backward, (F32, BF16), None, ((0, 1, 2), (3,)))
-            got_3 = exchange(sum_3, n_slab, 12)
+            far_sum, near_sum = backward(
+                other_list, [other_residual], 4, y_backward, (BF16, BF16), y_sum, ((1, 3), (0, 2)))
+            far_part, near_part = exchange(far_sum, n_slab, 2), exchange(near_sum, n_slab, 2)
+            z_sum = backward(z_list, [residual, other_residual], 4, z_backward, F32)
             piece = shape((rows, extent), BF16)
-            own_piece, piece_2, piece_1 = call(
-                functools.partial(combine_kernel, (0, 1, 2)), "combine", 16, [VMEM] * 2,
-                [shape((rows, extent), F32), piece, piece], z_sum, y_got)
-            pieces = [own_piece, exchange(piece_2, n_slab, 8), exchange(piece_1, n_slab, 4),
-                      got_3, across_got]
+            piece_2, piece_3 = call(
+                functools.partial(combine_kernel, (1, 3)), "combine", 16, [VMEM] * 2,
+                [piece, piece], z_sum, far_part)
+            got = [exchange(piece_2, n_slab, 8), exchange(piece_3, n_slab, 12)]
+            own_piece, piece_1 = call(
+                functools.partial(combine_kernel, (0, 2)), "combine", 16, [VMEM] * 2,
+                [shape((rows, extent), F32), piece], z_sum, near_part)
+            pieces = [own_piece, *got, exchange(piece_1, n_slab, 4)]
         else:
             everyone = lax.all_gather(payload, "slab", axis=0, tiled=True)
             if sweep == 0:

time: 64.3 us -> 63.8 us (level)
  waiting for transfers between devices: 11 us -> 14.5 us
  Pallas kernels: 19 us -> 16.4 us
  starting transfers between devices: 33.1 us -> 31.9 us
    ppermute x24, waiting for transfers between devices: 11 us -> 14.5 us  [exchange(): lax.ppermute(values, 'slab', [(device, device ^ distance) for device in r...]
    pallas_call x24 -> x26, Pallas kernels: 19 us -> 16.4 us  [call(): pl.pallas_call(kernel, out_shape=out_shape, in_specs=in_specs, out_specs=...]
    ppermute x24, starting transfers between devices: 33.1 us -> 31.9 us  [exchange(): lax.ppermute(values, 'slab', [(device, device ^ distance) for device in r...]
  transfers between devices with their start and end apart: 24 -> 24, of which waited for: 13 -> 17; matrix products, arithmetic and copies ran while one was open for 0% -> 0% of each run, Pallas kernels for 18% -> 16%
where the time goes in v18:
time: 63.8 us; the launch traced here: 63.2 us
  starting transfers between devices  31.9 us (50%)
  Pallas kernels  16.4 us (26%)
  waiting for transfers between devices  14.5 us (23%)
    ppermute x24, starting transfers between devices, exchange(): lax.ppermute(values, 'slab', [(device, device ^ distance) for device in r...  31.9 us
    pallas_call x26, Pallas kernels, call(): pl.pallas_call(kernel, out_shape=out_shape, in_specs=in_specs, out_specs=...  16.4 us
    ppermute x24, waiting for transfers between devices, exchange(): lax.ppermute(values, 'slab', [(device, device ^ distance) for device in r...  14.5 us
  transfers between devices with their start and end apart: 24, of which 17 were waited for; matrix products, arithmetic and copies ran while one was open for 0% of the time, Pallas kernels for 16%

profile of v18, /device:TPU:0, one launch (start us, length us, event | category | flops | bytes accessed | tf_op | source)
XLA Modules:
  0.0 63.2 jit_solution(7052971004691055153)
XLA Ops:
  0.0 1.0 %pack.1.refs_0_ = bf16[192,128]{1,0:T(8,128)(2,1)S(1)} custom-call(f32[128,128]{1,0:T(8,128)} %bitcast.8, f32[4,256]{1,0:T(4,128)} %bitcast.12, f32[4,256]{1,0:T(4,128)} %bitcast.14, s32[4,256]{1,0:T(4,128)} %bitcast.16, s32[1,256]{1,0:T(1,128)} %bitcast.20, s32[1,16]{1,0:T(1,128)} %bitcast.18), custom_call_target="tpu_custom_call" | custom-call | flops 4000000000 | bytes 8000000 | tf_op jit(solution)/shard_map/pack/pallas_call | solution.py:404
  1.0 4.1 %collective-permute-start = (bf16[192,128]{1,0:T(8,128)(2,1)S(1)}, bf16[192,128]{1,0:T(8,128)(2,1)S(1)}, u32[]{:S(2)}, u32[]{:S(2)}) collective-permute-start(bf16[192,128]{1,0:T(8,128)(2,1)S(1)} %pack.1.refs_0_), channel_id=1, source_target_pairs={{0,8},{1,9},{2,10},{3,11},{4,12},{5,13},{6,14},{7,15},{8,0},{9,1},... | collective-permute-start | bytes 147464 | tf_op jit(solution)/shard_map/ppermute | solution.py:418
  5.2 1.6 %collective-permute-start.1 = (bf16[192,128]{1,0:T(8,128)(2,1)S(1)}, bf16[192,128]{1,0:T(8,128)(2,1)S(1)}, u32[]{:S(2)}, u32[]{:S(2)}) collective-permute-start(bf16[192,128]{1,0:T(8,128)(2,1)S(1)} %pack.1.refs_0_), channel_id=1, source_target_pairs={{0,4},{1,5},{2,6},{3,7},{4,0},{5,1},{6,2},{7,3},{8,12},{9,13},{10,... | collective-permute-start | bytes 147464 | tf_op jit(solution)/shard_map/ppermute | solution.py:418
  6.7 4.8 %collective-permute-start.4 = (bf16[192,128]{1,0:T(8,128)(2,1)S(1)}, bf16[192,128]{1,0:T(8,128)(2,1)S(1)}, u32[]{:S(2)}, u32[]{:S(2)}) collective-permute-start(bf16[192,128]{1,0:T(8,128)(2,1)S(1)} %pack.1.refs_0_), channel_id=1, source_target_pairs={{0,14},{1,15},{2,12},{3,13},{4,10},{5,11},{6,8},{7,9},{8,6},{9,7},... | collective-permute-start | bytes 147464 | tf_op jit(solution)/shard_map/ppermute | solution.py:418
  12.6 1.5 %setup.2 = (s32[8,128]{1,0:T(8,128)S(4)}, f32[64,128]{1,0:T(8,128)S(1)}, s32[544,128]{1,0:T(8,128)S(1)}, f32[544,128]{1,0:T(8,128)S(1)}, f32[544,128]{1,0:T(8,12...) custom-call(bf16[576,128]{1,0:T(8,128)(2,1)S(1)} %join.2.refs_0_, ...), custom_call_target="tpu_custom_call" | custom-call | flops 4000000000 | bytes 8000000 | tf_op jit(solution)/shard_map/setup/pallas_call | solution.py:404
  14.1 1.5 %forward.6.refs_2_.refs_6_ = f32[512,128]{1,0:T(8,128)S(1)} custom-call(s32[8,128]{1,0:T(8,128)S(4)} %get-tuple-element.38.slots, bf16[576,128]{1,0:T(8,128)(2,1)S(1)} %join.2.refs_0_, bf16[192,128]{1,0:T(8,128)(2,1)S(1)} %collective-permute-done.2.refs_1_, s32[544,128]{1,0:T(8,128)S(1)} %get-tuple-element.39.refs_2_, ...), custom_call_target="tpu_custom_call" | custom-call | flops 4000000000 | bytes 8000000 | tf_op jit(solution)/shard_map/forward/pallas_call | solution.py:404
  15.6 1.1 %collective-permute-done.3.refs_0_ = bf16[576,128]{1,0:T(8,128)(2,1)S(1)} collective-permute-done((bf16[576,128]{1,0:T(8,128)(2,1)S(1)}, bf16[576,128]{1,0:T(8,128)(2,1)S(1)}, u32[]{:S(2)}, u32[]{:S(2)}) %collective-permute-start.3) | collective-permute-done | bytes 147488 | tf_op jit(solution)/shard_map/ppermute | solution.py:418
  16.7 1.6 %setup.3 = (s32[8,128]{1,0:T(8,128)S(4)}, s32[8,128]{1,0:T(8,128)S(4)}, f32[64,128]{1,0:T(8,128)S(1)}, s32[544,128]{1,0:T(8,128)S(1)}, f32[544,128]{1,0:T(8,128)...) custom-call(bf16[576,128]{1,0:T(8,128)(2,1)S(1)} %collective-permute, ...), custom_call_target="tpu_custom_call" | custom-call | flops 4000000000 | bytes 8000000 | tf_op jit(solution)/shard_map/setup/pallas_call | solution.py:404
  18.3 0.8 %forward.8 = f32[288,128]{1,0:T(8,128)S(1)} custom-call(s32[8,128]{1,0:T(8,128)S(4)} %get-tuple-element.50.slots, bf16[576,128]{1,0:T(8,128)(2,1)S(1)} %collective-permute-done.3.refs_0_, bf16[192,128]{1,0:T(8,128)(2,1)S(1)} %collective-permute-done.4.refs_1_, s32[544,128]{1,0:T(8,128)S(1)} %get-tuple-element.44.refs_2_, ...), custom_call_target="tpu_custom_call" | custom-call | flops 4000000000 | bytes 8000000 | tf_op jit(solution)/shard_map/forward/pallas_call | solution.py:404
  19.2 0.8 %forward.7.projection_ref = f32[256,128]{1,0:T(8,128)S(1)} custom-call(s32[8,128]{1,0:T(8,128)S(4)} %get-tuple-element.43.slots, bf16[576,128]{1,0:T(8,128)(2,1)S(1)} %collective-permute-done.3.refs_0_, bf16[192,128]{1,0:T(8,128)(2,1)S(1)} %collective-permute-done.4.refs_1_, s32[544,128]{1,0:T(8,128)S(1)} %get-tuple-element.44.refs_2_, ...), custom_call_target="tpu_custom_call" | custom-call | flops 4000000000 | bytes 8000000 | tf_op jit(solution)/shard_map/forward/pallas_call | solution.py:404
  22.5 1.2 %collective-permute-start.8 = (bf16[256,128]{1,0:T(8,128)(2,1)S(1)}, bf16[256,128]{1,0:T(8,128)(2,1)S(1)}, u32[]{:S(2)}, u32[]{:S(2)}) collective-permute-start(bf16[256,128]{1,0:T(8,128)(2,1)S(1)} %get-tuple-element.59), channel_id=1, source_target_pairs={{0,2},{1,3},{2,0},{3,1},{4,6},{5,7},{6,4},{7,5},{8,10},{9,11},{10,... | collective-permute-start | bytes 196616 | tf_op jit(solution)/shard_map/ppermute | solution.py:418
  23.7 0.9 %collective-permute-start.7 = (bf16[256,128]{1,0:T(8,128)(2,1)S(1)}, bf16[256,128]{1,0:T(8,128)(2,1)S(1)}, u32[]{:S(2)}, u32[]{:S(2)}) collective-permute-start(bf16[256,128]{1,0:T(8,128)(2,1)S(1)} %get-tuple-element.57), channel_id=1, source_target_pairs={{0,2},{1,3},{2,0},{3,1},{4,6},{5,7},{6,4},{7,5},{8,10},{9,11},{10,... | collective-permute-start | bytes 196616 | tf_op jit(solution)/shard_map/ppermute | solution.py:418
  24.6 1.2 %backward.6.sum_ref = f32[512,128]{1,0:T(8,128)S(1)} custom-call(s32[8,128]{1,0:T(8,128)S(4)} %get-tuple-element.38.slots, bf16[256,128]{1,0:T(8,128)(2,1)S(1)} %residual.2.refs_0_, bf16[256,128]{1,0:T(8,128)(2,1)S(1)} %collective-permute-done.6.refs_1_.refs_0_, s32[544,128]{1,0:T(8,128)S(1)} %get-tuple-element.51.refs_2_, ...), custom_call_target="tpu_custom_call" | custom-call | flops 4000000000 | bytes 8000000 | tf_op jit(solution)/shard_map/backward/pallas_call | solution.py:404
  25.8 1.6 %collective-permute-done.8.y_ref = bf16[256,128]{1,0:T(8,128)(2,1)S(1)} collective-permute-done((bf16[256,128]{1,0:T(8,128)(2,1)S(1)}, bf16[256,128]{1,0:T(8,128)(2,1)S(1)}, u32[]{:S(2)}, u32[]{:S(2)}) %collective-permute-start.8) | collective-permute-done | bytes 65568 | tf_op jit(solution)/shard_map/ppermute | solution.py:418
  27.4 1.7 %collective-permute-start.10 = (bf16[128,128]{1,0:T(8,128)(2,1)S(1)}, bf16[128,128]{1,0:T(8,128)(2,1)S(1)}, u32[]{:S(2)}, u32[]{:S(2)}) collective-permute-start(bf16[128,128]{1,0:T(8,128)(2,1)S(1)} %get-tuple-element.61), channel_id=1, source_target_pairs={{0,12},{1,13},{2,14},{3,15},{4,8},{5,9},{6,10},{7,11},{8,4},{9,5},... | collective-permute-start | bytes 98312 | tf_op jit(solution)/shard_map/ppermute | solution.py:418
  29.2 2.8 %collective-permute-start.11 = (bf16[128,128]{1,0:T(8,128)(2,1)S(1)}, bf16[128,128]{1,0:T(8,128)(2,1)S(1)}, u32[]{:S(2)}, u32[]{:S(2)}) collective-permute-start(bf16[128,128]{1,0:T(8,128)(2,1)S(1)} %get-tuple-element.62), channel_id=1, source_target_pairs={{0,4},{1,5},{2,6},{3,7},{4,0},{5,1},{6,2},{7,3},{8,12},{9,13},{10,... | collective-permute-start | bytes 98312 | tf_op jit(solution)/shard_map/ppermute | solution.py:418
  33.4 0.8 %collective-permute-done.9.refs_1_ = bf16[128,128]{1,0:T(8,128)(2,1)S(1)} collective-permute-done((bf16[128,128]{1,0:T(8,128)(2,1)S(1)}, bf16[128,128]{1,0:T(8,128)(2,1)S(1)}, u32[]{:S(2)}, u32[]{:S(2)}) %collective-permute-start.9) | collective-permute-done | bytes 32800 | tf_op jit(solution)/shard_map/ppermute | solution.py:418
  34.3 1.9 %collective-permute-start.12 = (bf16[128,128]{1,0:T(8,128)(2,1)S(1)}, bf16[128,128]{1,0:T(8,128)(2,1)S(1)}, u32[]{:S(2)}, u32[]{:S(2)}) collective-permute-start(bf16[128,128]{1,0:T(8,128)(2,1)S(1)} %get-tuple-element.64.refs_0_), channel_id=1, source_target_pairs={{0,8},{1,9},{2,10},{3,11},{4,12},{5,13},{6,14},{7,15},{8,0},{9,1},... | collective-permute-start | bytes 98312 | tf_op jit(solution)/shard_map/ppermute | solution.py:418
  36.8 1.9 %collective-permute-start.16 = (bf16[128,128]{1,0:T(8,128)(2,1)S(1)}, bf16[128,128]{1,0:T(8,128)(2,1)S(1)}, u32[]{:S(2)}, u32[]{:S(2)}) collective-permute-start(bf16[128,128]{1,0:T(8,128)(2,1)S(1)} %get-tuple-element.64.refs_0_), channel_id=1, source_target_pairs={{0,12},{1,13},{2,14},{3,15},{4,8},{5,9},{6,10},{7,11},{8,4},{9,5},... | collective-permute-start | bytes 98312 | tf_op jit(solution)/shard_map/ppermute | solution.py:418
  38.7 3.2 %collective-permute-start.15 = (bf16[128,128]{1,0:T(8,128)(2,1)S(1)}, bf16[128,128]{1,0:T(8,128)(2,1)S(1)}, u32[]{:S(2)}, u32[]{:S(2)}) collective-permute-start(bf16[128,128]{1,0:T(8,128)(2,1)S(1)} %get-tuple-element.64.refs_0_), channel_id=1, source_target_pairs={{0,14},{1,15},{2,12},{3,13},{4,10},{5,11},{6,8},{7,9},{8,6},{9,7},... | collective-permute-start | bytes 98312 | tf_op jit(solution)/shard_map/ppermute | solution.py:418
  42.5 1.5 %forward.9.refs_6_ = f32[512,128]{1,0:T(8,128)S(1)} custom-call(s32[8,128]{1,0:T(8,128)S(4)} %get-tuple-element.38.slots, bf16[384,128]{1,0:T(8,128)(2,1)S(1)} %join.3.refs_0_, bf16[128,128]{1,0:T(8,128)(2,1)S(1)} %collective-permute-done.16.refs_1_, s32[544,128]{1,0:T(8,128)S(1)} %get-tuple-element.39.refs_2_, f32[544,128]{1,0:T(8,128)S(1)} %get-tuple-element.40.refs_3_, ...), custom_call_target="tpu_custom_call" | custom-call | flops 4000000000 | bytes 8000000 | tf_op jit(solution)/shard_map/forward/pallas_call | solution.py:404
  44.0 1.4 %collective-permute-done.15.refs_1_ = bf16[128,128]{1,0:T(8,128)(2,1)S(1)} collective-permute-done((bf16[128,128]{1,0:T(8,128)(2,1)S(1)}, bf16[128,128]{1,0:T(8,128)(2,1)S(1)}, u32[]{:S(2)}, u32[]{:S(2)}) %collective-permute-start.15) | collective-permute-done | bytes 32800 | tf_op jit(solution)/shard_map/ppermute | solution.py:418
  45.4 1.3 %collective-permute-done.14.refs_0_ = bf16[384,128]{1,0:T(8,128)(2,1)S(1)} collective-permute-done((bf16[384,128]{1,0:T(8,128)(2,1)S(1)}, bf16[384,128]{1,0:T(8,128)(2,1)S(1)}, u32[]{:S(2)}, u32[]{:S(2)}) %collective-permute-start.14) | collective-permute-done | bytes 98336 | tf_op jit(solution)/shard_map/ppermute | solution.py:418
  46.6 0.7 %forward.11 = f32[256,128]{1,0:T(8,128)S(1)} custom-call(s32[8,128]{1,0:T(8,128)S(4)} %get-tuple-element.50.slots, bf16[384,128]{1,0:T(8,128)(2,1)S(1)} %collective-permute-done.14.refs_0_, bf16[128,128]{1,0:T(8,128)(2,1)S(1)} %collective-permute-done.15.refs_1_, s32[544,128]{1,0:T(8,128)S(1)} %get-tuple-element.44.refs_2_, ...), custom_call_target="tpu_custom_call" | custom-call | flops 4000000000 | bytes 8000000 | tf_op jit(solution)/shard_map/forward/pallas_call | solution.py:404
  47.5 0.8 %forward.10.projection_ref = f32[256,128]{1,0:T(8,128)S(1)} custom-call(s32[8,128]{1,0:T(8,128)S(4)} %get-tuple-element.43.slots, bf16[384,128]{1,0:T(8,128)(2,1)S(1)} %collective-permute-done.14.refs_0_, bf16[128,128]{1,0:T(8,128)(2,1)S(1)} %collective-permute-done.15.refs_1_, s32[544,128]{1,0:T(8,128)S(1)} %get-tuple-element.44.refs_2_, ...), custom_call_target="tpu_custom_call" | custom-call | flops 4000000000 | bytes 8000000 | tf_op jit(solution)/shard_map/forward/pallas_call | solution.py:404
  50.8 1.4 %collective-permute-start.20 = (bf16[256,128]{1,0:T(8,128)(2,1)S(1)}, bf16[256,128]{1,0:T(8,128)(2,1)S(1)}, u32[]{:S(2)}, u32[]{:S(2)}) collective-permute-start(bf16[256,128]{1,0:T(8,128)(2,1)S(1)} %get-tuple-element.67), channel_id=1, source_target_pairs={{0,2},{1,3},{2,0},{3,1},{4,6},{5,7},{6,4},{7,5},{8,10},{9,11},{10,... | collective-permute-start | bytes 196616 | tf_op jit(solution)/shard_map/ppermute | solution.py:418
  52.1 0.7 %collective-permute-start.19 = (bf16[256,128]{1,0:T(8,128)(2,1)S(1)}, bf16[256,128]{1,0:T(8,128)(2,1)S(1)}, u32[]{:S(2)}, u32[]{:S(2)}) collective-permute-start(bf16[256,128]{1,0:T(8,128)(2,1)S(1)} %get-tuple-element.65), channel_id=1, source_target_pairs={{0,2},{1,3},{2,0},{3,1},{4,6},{5,7},{6,4},{7,5},{8,10},{9,11},{10,... | collective-permute-start | bytes 196616 | tf_op jit(solution)/shard_map/ppermute | solution.py:418
  52.9 1.2 %backward.9.sum_ref = f32[512,128]{1,0:T(8,128)S(1)} custom-call(s32[8,128]{1,0:T(8,128)S(4)} %get-tuple-element.38.slots, bf16[256,128]{1,0:T(8,128)(2,1)S(1)} %residual.3.refs_0_, bf16[256,128]{1,0:T(8,128)(2,1)S(1)} %collective-permute-done.18.refs_1_.refs_0_, s32[544,128]{1,0:T(8,128)S(1)} %get-tuple-element.51.refs_2_, ...), custom_call_target="tpu_custom_call" | custom-call | flops 4000000000 | bytes 8000000 | tf_op jit(solution)/shard_map/backward/pallas_call | solution.py:404
  54.1 1.4 %collective-permute-done.20.y_ref = bf16[256,128]{1,0:T(8,128)(2,1)S(1)} collective-permute-done((bf16[256,128]{1,0:T(8,128)(2,1)S(1)}, bf16[256,128]{1,0:T(8,128)(2,1)S(1)}, u32[]{:S(2)}, u32[]{:S(2)}) %collective-permute-start.20) | collective-permute-done | bytes 65568 | tf_op jit(solution)/shard_map/ppermute | solution.py:418
  55.6 2.9 %collective-permute-start.22 = (bf16[128,128]{1,0:T(8,128)(2,1)S(1)}, bf16[128,128]{1,0:T(8,128)(2,1)S(1)}, u32[]{:S(2)}, u32[]{:S(2)}) collective-permute-start(bf16[128,128]{1,0:T(8,128)(2,1)S(1)} %get-tuple-element.69), channel_id=1, source_target_pairs={{0,12},{1,13},{2,14},{3,15},{4,8},{5,9},{6,10},{7,11},{8,4},{9,5},... | collective-permute-start | bytes 98312 | tf_op jit(solution)/shard_map/ppermute | solution.py:418
  59.2 1.6 %collective-permute-done.21.refs_1_ = bf16[128,128]{1,0:T(8,128)(2,1)S(1)} collective-permute-done((bf16[128,128]{1,0:T(8,128)(2,1)S(1)}, bf16[128,128]{1,0:T(8,128)(2,1)S(1)}, u32[]{:S(2)}, u32[]{:S(2)}) %collective-permute-start.21) | collective-permute-done | bytes 32800 | tf_op jit(solution)/shard_map/ppermute | solution.py:418
  61.4 1.1 %collective-permute-done.23.refs_3_ = bf16[128,128]{1,0:T(8,128)(2,1)S(1)} collective-permute-done((bf16[128,128]{1,0:T(8,128)(2,1)S(1)}, bf16[128,128]{1,0:T(8,128)(2,1)S(1)}, u32[]{:S(2)}, u32[]{:S(2)}) %collective-permute-start.23) | collective-permute-done | bytes 32800 | tf_op jit(solution)/shard_map/ppermute | solution.py:418
  (54 shorter events, 11.2 us)
Async XLA Ops:
  1.0 10.5 %collective-permute-start = (bf16[192,128]{1,0:T(8,128)(2,1)S(1)}, bf16[192,128]{1,0:T(8,128)(2,1)S(1)}, u32[]{:S(2)}, u32[]{:S(2)}) collective-permute-start(bf16[192,128]{1,0:T(8,128)(2,1)S(1)} %pack.1.refs_0_), channel_id=1, source_target_pairs={{0,8},{1,9},{2,10},{3,11},{4,12},{5,13},{6,14},{7,15},{8,0},{9,1},... | collective-permute-start | bytes 147464 | tf_op jit(solution)/shard_map/ppermute | solution.py:418
  5.2 6.4 %collective-permute-start.1 = (bf16[192,128]{1,0:T(8,128)(2,1)S(1)}, bf16[192,128]{1,0:T(8,128)(2,1)S(1)}, u32[]{:S(2)}, u32[]{:S(2)}) collective-permute-start(bf16[192,128]{1,0:T(8,128)(2,1)S(1)} %pack.1.refs_0_), channel_id=1, source_target_pairs={{0,4},{1,5},{2,6},{3,7},{4,0},{5,1},{6,2},{7,3},{8,12},{9,13},{10,... | collective-permute-start | bytes 147464 | tf_op jit(solution)/shard_map/ppermute | solution.py:418
  6.7 5.9 %collective-permute-start.2 = (bf16[192,128]{1,0:T(8,128)(2,1)S(1)}, bf16[192,128]{1,0:T(8,128)(2,1)S(1)}, u32[]{:S(2)}, u32[]{:S(2)}) collective-permute-start(bf16[192,128]{1,0:T(8,128)(2,1)S(1)} %pack.1.refs_0_), channel_id=1, source_target_pairs={{0,12},{1,13},{2,14},{3,15},{4,8},{5,9},{6,10},{7,11},{8,4},{9,5},... | collective-permute-start | bytes 147464 | tf_op jit(solution)/shard_map/ppermute | solution.py:418
  6.7 8.9 %collective-permute-start.4 = (bf16[192,128]{1,0:T(8,128)(2,1)S(1)}, bf16[192,128]{1,0:T(8,128)(2,1)S(1)}, u32[]{:S(2)}, u32[]{:S(2)}) collective-permute-start(bf16[192,128]{1,0:T(8,128)(2,1)S(1)} %pack.1.refs_0_), channel_id=1, source_target_pairs={{0,14},{1,15},{2,12},{3,13},{4,10},{5,11},{6,8},{7,9},{8,6},{9,7},... | collective-permute-start | bytes 147464 | tf_op jit(solution)/shard_map/ppermute | solution.py:418
  11.5 5.2 %collective-permute-start.3 = (bf16[576,128]{1,0:T(8,128)(2,1)S(1)}, bf16[576,128]{1,0:T(8,128)(2,1)S(1)}, u32[]{:S(2)}, u32[]{:S(2)}) collective-permute-start(bf16[576,128]{1,0:T(8,128)(2,1)S(1)} %join.2.refs_0_), channel_id=1, source_target_pairs={{0,2},{1,3},{2,0},{3,1},{4,6},{5,7},{6,4},{7,5},{8,10},{9,11},{10,... | collective-permute-start | bytes 442376 | tf_op jit(solution)/shard_map/ppermute | solution.py:418
  19.1 1.4 %collective-permute-start.5 = (f32[288,128]{1,0:T(8,128)S(1)}, f32[288,128]{1,0:T(8,128)S(1)}, u32[]{:S(2)}, u32[]{:S(2)}) collective-permute-start(f32[288,128]{1,0:T(8,128)S(1)} %forward.8), channel_id=1, source_target_pairs={{0,1},{1,0},{2,3},{3,2},{4,5},{5,4},{6,7},{7,6},{8,9},{9,8},{10,11... | collective-permute-start | bytes 442376 | tf_op jit(solution)/shard_map/ppermute | solution.py:418
  19.2 1.4 %copy-start.1 = (bf16[32,8,128]{2,1,0:T(8,128)(2,1)S(1)}, bf16[32,8,128]{2,1,0:T(8,128)(2,1)}, u32[]{:S(2)}) copy-start(bf16[32,8,128]{2,1,0:T(8,128)(2,1)} %param.7) | copy-start | bytes 196612
  20.6 1.3 %collective-permute-start.6 = (bf16[256,128]{1,0:T(8,128)(2,1)S(1)}, bf16[256,128]{1,0:T(8,128)(2,1)S(1)}, u32[]{:S(2)}, u32[]{:S(2)}) collective-permute-start(bf16[256,128]{1,0:T(8,128)(2,1)S(1)} %residual.2.refs_0_), channel_id=1, source_target_pairs={{0,1},{1,0},{2,3},{3,2},{4,5},{5,4},{6,7},{7,6},{8,9},{9,8},{10,11... | collective-permute-start | bytes 196616 | tf_op jit(solution)/shard_map/ppermute | solution.py:418
  22.5 4.9 %collective-permute-start.8 = (bf16[256,128]{1,0:T(8,128)(2,1)S(1)}, bf16[256,128]{1,0:T(8,128)(2,1)S(1)}, u32[]{:S(2)}, u32[]{:S(2)}) collective-permute-start(bf16[256,128]{1,0:T(8,128)(2,1)S(1)} %get-tuple-element.59), channel_id=1, source_target_pairs={{0,2},{1,3},{2,0},{3,1},{4,6},{5,7},{6,4},{7,5},{8,10},{9,11},{10,... | collective-permute-start | bytes 196616 | tf_op jit(solution)/shard_map/ppermute | solution.py:418
  23.7 5.4 %collective-permute-start.7 = (bf16[256,128]{1,0:T(8,128)(2,1)S(1)}, bf16[256,128]{1,0:T(8,128)(2,1)S(1)}, u32[]{:S(2)}, u32[]{:S(2)}) collective-permute-start(bf16[256,128]{1,0:T(8,128)(2,1)S(1)} %get-tuple-element.57), channel_id=1, source_target_pairs={{0,2},{1,3},{2,0},{3,1},{4,6},{5,7},{6,4},{7,5},{8,10},{9,11},{10,... | collective-permute-start | bytes 196616 | tf_op jit(solution)/shard_map/ppermute | solution.py:418
  27.4 5.9 %collective-permute-start.10 = (bf16[128,128]{1,0:T(8,128)(2,1)S(1)}, bf16[128,128]{1,0:T(8,128)(2,1)S(1)}, u32[]{:S(2)}, u32[]{:S(2)}) collective-permute-start(bf16[128,128]{1,0:T(8,128)(2,1)S(1)} %get-tuple-element.61), channel_id=1, source_target_pairs={{0,12},{1,13},{2,14},{3,15},{4,8},{5,9},{6,10},{7,11},{8,4},{9,5},... | collective-permute-start | bytes 98312 | tf_op jit(solution)/shard_map/ppermute | solution.py:418
  29.1 2.9 %copy-start.2 = (f32[256,4]{0,1:T(4,128)S(1)}, f32[256,4]{0,1:T(4,128)}, u32[]{:S(2)}) copy-start(f32[256,4]{0,1:T(4,128)} %param.13) | copy-start | bytes 12292
  29.1 2.9 %copy-start.3 = (f32[256,4]{0,1:T(4,128)S(1)}, f32[256,4]{0,1:T(4,128)}, u32[]{:S(2)}) copy-start(f32[256,4]{0,1:T(4,128)} %param.12) | copy-start | bytes 12292
  29.1 2.9 %copy-start.4 = (s32[256,4]{0,1:T(4,128)S(1)}, s32[256,4]{0,1:T(4,128)}, u32[]{:S(2)}) copy-start(s32[256,4]{0,1:T(4,128)} %param.9) | copy-start | bytes 12292
  29.1 5.1 %collective-permute-start.9 = (bf16[128,128]{1,0:T(8,128)(2,1)S(1)}, bf16[128,128]{1,0:T(8,128)(2,1)S(1)}, u32[]{:S(2)}, u32[]{:S(2)}) collective-permute-start(bf16[128,128]{1,0:T(8,128)(2,1)S(1)} %get-tuple-element.60), channel_id=1, source_target_pairs={{0,8},{1,9},{2,10},{3,11},{4,12},{5,13},{6,14},{7,15},{8,0},{9,1},... | collective-permute-start | bytes 98312 | tf_op jit(solution)/shard_map/ppermute | solution.py:418
  29.2 2.9 %copy-start.5 = (s32[16]{0:T(128)S(1)}, s32[16]{0:T(128)}, u32[]{:S(2)}) copy-start(s32[16]{0:T(128)} %param.11) | copy-start | bytes 196
  29.2 5.1 %copy-start = (f32[16,8,128]{2,1,0:T(8,128)S(1)}, f32[16,8,128]{2,1,0:T(8,128)}, u32[]{:S(2)}) copy-start(f32[16,8,128]{2,1,0:T(8,128)} %param.8) | copy-start | bytes 196612
  29.2 5.1 %collective-permute-start.11 = (bf16[128,128]{1,0:T(8,128)(2,1)S(1)}, bf16[128,128]{1,0:T(8,128)(2,1)S(1)}, u32[]{:S(2)}, u32[]{:S(2)}) collective-permute-start(bf16[128,128]{1,0:T(8,128)(2,1)S(1)} %get-tuple-element.62), channel_id=1, source_target_pairs={{0,4},{1,5},{2,6},{3,7},{4,0},{5,1},{6,2},{7,3},{8,12},{9,13},{10,... | collective-permute-start | bytes 98312 | tf_op jit(solution)/shard_map/ppermute | solution.py:418
  34.3 7.6 %collective-permute-start.12 = (bf16[128,128]{1,0:T(8,128)(2,1)S(1)}, bf16[128,128]{1,0:T(8,128)(2,1)S(1)}, u32[]{:S(2)}, u32[]{:S(2)}) collective-permute-start(bf16[128,128]{1,0:T(8,128)(2,1)S(1)} %get-tuple-element.64.refs_0_), channel_id=1, source_target_pairs={{0,8},{1,9},{2,10},{3,11},{4,12},{5,13},{6,14},{7,15},{8,0},{9,1},... | collective-permute-start | bytes 98312 | tf_op jit(solution)/shard_map/ppermute | solution.py:418
  36.2 5.8 %collective-permute-start.13 = (bf16[128,128]{1,0:T(8,128)(2,1)S(1)}, bf16[128,128]{1,0:T(8,128)(2,1)S(1)}, u32[]{:S(2)}, u32[]{:S(2)}) collective-permute-start(bf16[128,128]{1,0:T(8,128)(2,1)S(1)} %get-tuple-element.64.refs_0_), channel_id=1, source_target_pairs={{0,4},{1,5},{2,6},{3,7},{4,0},{5,1},{6,2},{7,3},{8,12},{9,13},{10,... | collective-permute-start | bytes 98312 | tf_op jit(solution)/shard_map/ppermute | solution.py:418
  36.8 5.7 %collective-permute-start.16 = (bf16[128,128]{1,0:T(8,128)(2,1)S(1)}, bf16[128,128]{1,0:T(8,128)(2,1)S(1)}, u32[]{:S(2)}, u32[]{:S(2)}) collective-permute-start(bf16[128,128]{1,0:T(8,128)(2,1)S(1)} %get-tuple-element.64.refs_0_), channel_id=1, source_target_pairs={{0,12},{1,13},{2,14},{3,15},{4,8},{5,9},{6,10},{7,11},{8,4},{9,5},... | collective-permute-start | bytes 98312 | tf_op jit(solution)/shard_map/ppermute | solution.py:418
  38.7 6.6 %collective-permute-start.15 = (bf16[128,128]{1,0:T(8,128)(2,1)S(1)}, bf16[128,128]{1,0:T(8,128)(2,1)S(1)}, u32[]{:S(2)}, u32[]{:S(2)}) collective-permute-start(bf16[128,128]{1,0:T(8,128)(2,1)S(1)} %get-tuple-element.64.refs_0_), channel_id=1, source_target_pairs={{0,14},{1,15},{2,12},{3,13},{4,10},{5,11},{6,8},{7,9},{8,6},{9,7},... | collective-permute-start | bytes 98312 | tf_op jit(solution)/shard_map/ppermute | solution.py:418
  41.9 4.7 %collective-permute-start.14 = (bf16[384,128]{1,0:T(8,128)(2,1)S(1)}, bf16[384,128]{1,0:T(8,128)(2,1)S(1)}, u32[]{:S(2)}, u32[]{:S(2)}) collective-permute-start(bf16[384,128]{1,0:T(8,128)(2,1)S(1)} %join.3.refs_0_), channel_id=1, source_target_pairs={{0,2},{1,3},{2,0},{3,1},{4,6},{5,7},{6,4},{7,5},{8,10},{9,11},{10,... | collective-permute-start | bytes 294920 | tf_op jit(solution)/shard_map/ppermute | solution.py:418
  47.4 1.4 %collective-permute-start.17 = (f32[256,128]{1,0:T(8,128)S(1)}, f32[256,128]{1,0:T(8,128)S(1)}, u32[]{:S(2)}, u32[]{:S(2)}) collective-permute-start(f32[256,128]{1,0:T(8,128)S(1)} %forward.11), channel_id=1, source_target_pairs={{0,1},{1,0},{2,3},{3,2},{4,5},{5,4},{6,7},{7,6},{8,9},{9,8},{10,11... | collective-permute-start | bytes 393224 | tf_op jit(solution)/shard_map/ppermute | solution.py:418
  48.8 1.3 %collective-permute-start.18 = (bf16[256,128]{1,0:T(8,128)(2,1)S(1)}, bf16[256,128]{1,0:T(8,128)(2,1)S(1)}, u32[]{:S(2)}, u32[]{:S(2)}) collective-permute-start(bf16[256,128]{1,0:T(8,128)(2,1)S(1)} %residual.3.refs_0_), channel_id=1, source_target_pairs={{0,1},{1,0},{2,3},{3,2},{4,5},{5,4},{6,7},{7,6},{8,9},{9,8},{10,11... | collective-permute-start | bytes 196616 | tf_op jit(solution)/shard_map/ppermute | solution.py:418
  50.8 4.7 %collective-permute-start.20 = (bf16[256,128]{1,0:T(8,128)(2,1)S(1)}, bf16[256,128]{1,0:T(8,128)(2,1)S(1)}, u32[]{:S(2)}, u32[]{:S(2)}) collective-permute-start(bf16[256,128]{1,0:T(8,128)(2,1)S(1)} %get-tuple-element.67), channel_id=1, source_target_pairs={{0,2},{1,3},{2,0},{3,1},{4,6},{5,7},{6,4},{7,5},{8,10},{9,11},{10,... | collective-permute-start | bytes 196616 | tf_op jit(solution)/shard_map/ppermute | solution.py:418
  52.1 6.4 %collective-permute-start.19 = (bf16[256,128]{1,0:T(8,128)(2,1)S(1)}, bf16[256,128]{1,0:T(8,128)(2,1)S(1)}, u32[]{:S(2)}, u32[]{:S(2)}) collective-permute-start(bf16[256,128]{1,0:T(8,128)(2,1)S(1)} %get-tuple-element.65), channel_id=1, source_target_pairs={{0,2},{1,3},{2,0},{3,1},{4,6},{5,7},{6,4},{7,5},{8,10},{9,11},{10,... | collective-permute-start | bytes 196616 | tf_op jit(solution)/shard_map/ppermute | solution.py:418
  55.5 5.2 %collective-permute-start.21 = (bf16[128,128]{1,0:T(8,128)(2,1)S(1)}, bf16[128,128]{1,0:T(8,128)(2,1)S(1)}, u32[]{:S(2)}, u32[]{:S(2)}) collective-permute-start(bf16[128,128]{1,0:T(8,128)(2,1)S(1)} %get-tuple-element.68), channel_id=1, source_target_pairs={{0,8},{1,9},{2,10},{3,11},{4,12},{5,13},{6,14},{7,15},{8,0},{9,1},... | collective-permute-start | bytes 98312 | tf_op jit(solution)/shard_map/ppermute | solution.py:418
  55.6 5.8 %collective-permute-start.22 = (bf16[128,128]{1,0:T(8,128)(2,1)S(1)}, bf16[128,128]{1,0:T(8,128)(2,1)S(1)}, u32[]{:S(2)}, u32[]{:S(2)}) collective-permute-start(bf16[128,128]{1,0:T(8,128)(2,1)S(1)} %get-tuple-element.69), channel_id=1, source_target_pairs={{0,12},{1,13},{2,14},{3,15},{4,8},{5,9},{6,10},{7,11},{8,4},{9,5},... | collective-permute-start | bytes 98312 | tf_op jit(solution)/shard_map/ppermute | solution.py:418
  58.5 4.0 %collective-permute-start.23 = (bf16[128,128]{1,0:T(8,128)(2,1)S(1)}, bf16[128,128]{1,0:T(8,128)(2,1)S(1)}, u32[]{:S(2)}, u32[]{:S(2)}) collective-permute-start(bf16[128,128]{1,0:T(8,128)(2,1)S(1)} %get-tuple-element.70), channel_id=1, source_target_pairs={{0,4},{1,5},{2,6},{3,7},{4,0},{5,1},{6,2},{7,3},{8,12},{9,13},{10,... | collective-permute-start | bytes 98312 | tf_op jit(solution)/shard_map/ppermute | solution.py:418

commit v19 on v18

--- a/solution.py
+++ b/solution.py
@@ -26,9 +26,10 @@
 def row_taps(offset, slope, extent):
     shape = (offset.shape[0], extent)
     ray = lax.broadcasted_iota(I32, shape, 1).astype(F32)
+    inverse = jnp.broadcast_to(1.0 / slope, shape)
     offset = jnp.broadcast_to(offset, shape)
     slope = jnp.broadcast_to(slope, shape)
-    middle = jnp.floor((ray - offset) / slope + 0.5)
+    middle = jnp.floor((ray - offset) * inverse + 0.5)
     middle = jnp.minimum(jnp.maximum(middle, 1.0), extent - 2.0)
     weights = [hat(ray, offset + slope * (middle + step)) for step in (-1.0, 0.0, 1.0)]
     return middle.astype(I32), weights
@@ -95,10 +96,10 @@
 
 
 def setup_kernel(n_payloads, members, stride, span, sizes, tiles, wanted, *refs):
-    payload_refs, refs = refs[:n_payloads], refs[-(2 * len(wanted) + 9):]
+    payload_refs, refs = refs[:n_payloads], refs[-(2 * len(wanted) + 10):]
     where = [(ref, index) for ref in payload_refs for index in range(ref.shape[0] // stride)]
-    list_refs, row_ref, tables = refs[:len(wanted)], refs[len(wanted)], refs[len(wanted) + 1:-len(wanted) - 1]
-    drafts, arrived = refs[-len(wanted) - 1:-1], refs[-1]
+    list_refs, row_ref, tables = refs[:len(wanted)], refs[len(wanted)], refs[len(wanted) + 1:-len(wanted) - 2]
+    drafts, arrived, summed = refs[-len(wanted) - 2:-2], refs[-2], refs[-1]
     copies = [
         pltpu.make_async_copy(draft, ref, arrived.at[place])
         for place, (draft, ref) in enumerate(zip(drafts, list_refs))]
@@ -168,27 +169,33 @@
         copy.start()
 
     columns = lined.T
-    summed = None
-    for level in range(depth):
-        offset = columns[:, level:level + 1]
-        slope = columns[:, depth + level:depth + level + 1]
-        middle, weights = row_taps(offset, slope, extent)
-        first, pair = column_taps(offset, slope, extent)
-        wide = [weight.astype(F32) for weight in weights]
-        values = [middle] + wide + [first] + [weight.astype(F32) for weight in pair]
-        at = level * (lanes + 8)
-        for ref, value in zip(tables, values):
-            ref[at:at + lanes, :] = value
-            blank = jnp.ones if ref.dtype == I32 else jnp.zeros
-            ref[at + lanes:at + lanes + 8, :] = blank((8, extent), ref.dtype)
-        parts = (wide[0] + wide[1]) + wide[2]
-        summed = parts if summed is None else summed + parts
+    step = 32
+    for row in range(0, lanes, step):
+        total = None
+        for level in range(depth):
+            offset = columns[row:row + step, level:level + 1]
+            slope = columns[row:row + step, depth + level:depth + level + 1]
+            middle, weights = row_taps(offset, slope, extent)
+            first, pair = column_taps(offset, slope, extent)
+            wide = [weight.astype(F32) for weight in weights]
+            values = [middle] + wide + [first] + [weight.astype(F32) for weight in pair]
+            at = level * (lanes + 8) + row
+            for ref, value in zip(tables, values):
+                ref[at:at + step, :] = value
+            parts = (wide[0] + wide[1]) + wide[2]
+            total = parts if total is None else total + parts
+        summed[row:row + step, :] = total
+    for ref in tables:
+        blank = jnp.ones if ref.dtype == I32 else jnp.zeros
+        for level in range(depth):
+            at = level * (lanes + 8) + lanes
+            ref[at:at + 8, :] = blank((8, extent), ref.dtype)
 
     tile = lax.broadcasted_iota(I32, (span * ray_tiles, lanes), 0).astype(F32)
     place = ray + (target * ray_tiles).astype(F32)
     place = jnp.where(alive, place, -1.0)
     hot = (jnp.broadcast_to(place, tile.shape) == tile).astype(F32)
-    row_ref[...] = jnp.dot(hot, summed, precision=HIGHEST, preferred_element_type=F32)
+    row_ref[...] = jnp.dot(hot, summed[...], precision=HIGHEST, preferred_element_type=F32)
     for copy in copies:
         copy.wait()
 
@@ -458,7 +465,8 @@
                               sum(one.shape[0] for one in payloads) // members, span, sizes,
                               voxel_tiles, wanted),
             "setup", 24, [VMEM] * len(payloads) + [ANY] * len(waits), out, *payloads, *waits,
-            scratch=[pltpu.VMEM((8, lanes), I32)] * n + [pltpu.SemaphoreType.DMA((n,))])
+            scratch=[pltpu.VMEM((8, lanes), I32)] * n
+            + [pltpu.SemaphoreType.DMA((n,)), pltpu.VMEM((lanes, extent), F32)])
         return found[:n], found[n], found[n + 1:n + 5], found[n + 5:]
 
     def forward(slots, values, members, table, n_out, start=None, start_row=None, sums=()):

time: 63.8 us -> 64.2 us (level)
  Pallas kernels: 16.4 us -> 17.7 us
  waiting for transfers between devices: 14.5 us -> 13.6 us
    pallas_call x26, Pallas kernels: 16.4 us -> 17.7 us  [call(): pl.pallas_call(kernel, out_shape=out_shape, in_specs=in_specs, out_specs=...]
    ppermute x24, waiting for transfers between devices: 14.5 us -> 13.6 us  [exchange(): lax.ppermute(values, 'slab', [(device, device ^ distance) for device in r...]
  transfers between devices with their start and end apart: 24 -> 24, of which waited for: 17 -> 16; matrix products, arithmetic and copies ran while one was open for 0% -> 0% of each run, Pallas kernels for 16% -> 16%
where the time goes in v19:
time: 64.2 us; the launch traced here: 63.5 us
  starting transfers between devices  31.8 us (50%)
  Pallas kernels  17.7 us (28%)
  waiting for transfers between devices  13.6 us (21%)
    ppermute x24, starting transfers between devices, exchange(): lax.ppermute(values, 'slab', [(device, device ^ distance) for device in r...  31.8 us
    pallas_call x26, Pallas kernels, call(): pl.pallas_call(kernel, out_shape=out_shape, in_specs=in_specs, out_specs=...  17.7 us
    ppermute x24, waiting for transfers between devices, exchange(): lax.ppermute(values, 'slab', [(device, device ^ distance) for device in r...  13.6 us
  transfers between devices with their start and end apart: 24, of which 16 were waited for; matrix products, arithmetic and copies ran while one was open for 0% of the time, Pallas kernels for 16%

profile of v19, /device:TPU:0, one launch (start us, length us, event | category | flops | bytes accessed | tf_op | source)
XLA Modules:
  0.0 63.5 jit_solution(4557587572981382596)
XLA Ops:
  0.0 1.0 %pack.1.refs_0_ = bf16[192,128]{1,0:T(8,128)(2,1)S(1)} custom-call(f32[128,128]{1,0:T(8,128)} %bitcast.8, f32[4,256]{1,0:T(4,128)} %bitcast.12, f32[4,256]{1,0:T(4,128)} %bitcast.14, s32[4,256]{1,0:T(4,128)} %bitcast.16, s32[1,256]{1,0:T(1,128)} %bitcast.20, s32[1,16]{1,0:T(1,128)} %bitcast.18), custom_call_target="tpu_custom_call" | custom-call | flops 4000000000 | bytes 8000000 | tf_op jit(solution)/shard_map/pack/pallas_call | solution.py:411
  1.0 4.1 %collective-permute-start = (bf16[192,128]{1,0:T(8,128)(2,1)S(1)}, bf16[192,128]{1,0:T(8,128)(2,1)S(1)}, u32[]{:S(2)}, u32[]{:S(2)}) collective-permute-start(bf16[192,128]{1,0:T(8,128)(2,1)S(1)} %pack.1.refs_0_), channel_id=1, source_target_pairs={{0,8},{1,9},{2,10},{3,11},{4,12},{5,13},{6,14},{7,15},{8,0},{9,1},... | collective-permute-start | bytes 147464 | tf_op jit(solution)/shard_map/ppermute | solution.py:425
  5.2 1.6 %collective-permute-start.1 = (bf16[192,128]{1,0:T(8,128)(2,1)S(1)}, bf16[192,128]{1,0:T(8,128)(2,1)S(1)}, u32[]{:S(2)}, u32[]{:S(2)}) collective-permute-start(bf16[192,128]{1,0:T(8,128)(2,1)S(1)} %pack.1.refs_0_), channel_id=1, source_target_pairs={{0,4},{1,5},{2,6},{3,7},{4,0},{5,1},{6,2},{7,3},{8,12},{9,13},{10,... | collective-permute-start | bytes 147464 | tf_op jit(solution)/shard_map/ppermute | solution.py:425
  6.7 4.8 %collective-permute-start.4 = (bf16[192,128]{1,0:T(8,128)(2,1)S(1)}, bf16[192,128]{1,0:T(8,128)(2,1)S(1)}, u32[]{:S(2)}, u32[]{:S(2)}) collective-permute-start(bf16[192,128]{1,0:T(8,128)(2,1)S(1)} %pack.1.refs_0_), channel_id=1, source_target_pairs={{0,14},{1,15},{2,12},{3,13},{4,10},{5,11},{6,8},{7,9},{8,6},{9,7},... | collective-permute-start | bytes 147464 | tf_op jit(solution)/shard_map/ppermute | solution.py:425
  12.6 1.5 %setup.2 = (s32[8,128]{1,0:T(8,128)S(4)}, f32[64,128]{1,0:T(8,128)S(1)}, s32[544,128]{1,0:T(8,128)S(1)}, f32[544,128]{1,0:T(8,128)S(1)}, f32[544,128]{1,0:T(8,12...) custom-call(bf16[576,128]{1,0:T(8,128)(2,1)S(1)} %join.2.refs_0_, ...), custom_call_target="tpu_custom_call" | custom-call | flops 4000000000 | bytes 8000000 | tf_op jit(solution)/shard_map/setup/pallas_call | solution.py:411
  14.1 1.8 %forward.6.refs_2_.refs_6_ = f32[512,128]{1,0:T(8,128)S(1)} custom-call(s32[8,128]{1,0:T(8,128)S(4)} %get-tuple-element.38.slots, bf16[576,128]{1,0:T(8,128)(2,1)S(1)} %join.2.refs_0_, bf16[192,128]{1,0:T(8,128)(2,1)S(1)} %collective-permute-done.2.refs_1_, s32[544,128]{1,0:T(8,128)S(1)} %get-tuple-element.39.refs_2_, ...), custom_call_target="tpu_custom_call" | custom-call | flops 4000000000 | bytes 8000000 | tf_op jit(solution)/shard_map/forward/pallas_call | solution.py:411
  16.7 1.6 %setup.3 = (s32[8,128]{1,0:T(8,128)S(4)}, s32[8,128]{1,0:T(8,128)S(4)}, f32[64,128]{1,0:T(8,128)S(1)}, s32[544,128]{1,0:T(8,128)S(1)}, f32[544,128]{1,0:T(8,128)...) custom-call(bf16[576,128]{1,0:T(8,128)(2,1)S(1)} %collective-permute, ...), custom_call_target="tpu_custom_call" | custom-call | flops 4000000000 | bytes 8000000 | tf_op jit(solution)/shard_map/setup/pallas_call | solution.py:411
  18.3 1.1 %forward.8 = f32[288,128]{1,0:T(8,128)S(1)} custom-call(s32[8,128]{1,0:T(8,128)S(4)} %get-tuple-element.50.slots, bf16[576,128]{1,0:T(8,128)(2,1)S(1)} %collective-permute-done.3.refs_0_, bf16[192,128]{1,0:T(8,128)(2,1)S(1)} %collective-permute-done.4.refs_1_, s32[544,128]{1,0:T(8,128)S(1)} %get-tuple-element.44.refs_2_, ...), custom_call_target="tpu_custom_call" | custom-call | flops 4000000000 | bytes 8000000 | tf_op jit(solution)/shard_map/forward/pallas_call | solution.py:411
  20.0 0.9 %collective-permute-done.5.refs_2_.refs_3_ = f32[288,128]{1,0:T(8,128)S(1)} collective-permute-done((f32[288,128]{1,0:T(8,128)S(1)}, f32[288,128]{1,0:T(8,128)S(1)}, u32[]{:S(2)}, u32[]{:S(2)}) %collective-permute-start.5) | collective-permute-done | bytes 147488 | tf_op jit(solution)/shard_map/ppermute | solution.py:425
  22.2 0.9 %backward.8 = (bf16[256,128]{1,0:T(8,128)(2,1)S(1)}, bf16[256,128]{1,0:T(8,128)(2,1)S(1)}) custom-call(s32[8,128]{1,0:T(8,128)S(4)} %get-tuple-element.50.slots, bf16[256,128]{1,0:T(8,128)(2,1)S(1)} %collective-permute-done.6.refs_1_.refs_0_, s32[544,128]{1,0:T(8,128)S(1)} %get-tuple-element.54.refs_1_, f32[544,128]{1,0:T(8,128)S(1)} %get-tuple-element.55.refs_2_, ...), custom_call_target="tpu_custom_call" | custom-call | flops 4000000000 | bytes 8000000 | tf_op jit(solution)/shard_map/backward/pallas_call | solution.py:411
  23.2 1.2 %collective-permute-start.8 = (bf16[256,128]{1,0:T(8,128)(2,1)S(1)}, bf16[256,128]{1,0:T(8,128)(2,1)S(1)}, u32[]{:S(2)}, u32[]{:S(2)}) collective-permute-start(bf16[256,128]{1,0:T(8,128)(2,1)S(1)} %get-tuple-element.59), channel_id=1, source_target_pairs={{0,2},{1,3},{2,0},{3,1},{4,6},{5,7},{6,4},{7,5},{8,10},{9,11},{10,... | collective-permute-start | bytes 196616 | tf_op jit(solution)/shard_map/ppermute | solution.py:425
  25.3 1.5 %backward.6.sum_ref = f32[512,128]{1,0:T(8,128)S(1)} custom-call(s32[8,128]{1,0:T(8,128)S(4)} %get-tuple-element.38.slots, bf16[256,128]{1,0:T(8,128)(2,1)S(1)} %residual.2.refs_0_, bf16[256,128]{1,0:T(8,128)(2,1)S(1)} %collective-permute-done.6.refs_1_.refs_0_, s32[544,128]{1,0:T(8,128)S(1)} %get-tuple-element.51.refs_2_, ...), custom_call_target="tpu_custom_call" | custom-call | flops 4000000000 | bytes 8000000 | tf_op jit(solution)/shard_map/backward/pallas_call | solution.py:411
  26.8 1.4 %collective-permute-done.8.y_ref = bf16[256,128]{1,0:T(8,128)(2,1)S(1)} collective-permute-done((bf16[256,128]{1,0:T(8,128)(2,1)S(1)}, bf16[256,128]{1,0:T(8,128)(2,1)S(1)}, u32[]{:S(2)}, u32[]{:S(2)}) %collective-permute-start.8) | collective-permute-done | bytes 65568 | tf_op jit(solution)/shard_map/ppermute | solution.py:425
  28.1 2.1 %collective-permute-start.10 = (bf16[128,128]{1,0:T(8,128)(2,1)S(1)}, bf16[128,128]{1,0:T(8,128)(2,1)S(1)}, u32[]{:S(2)}, u32[]{:S(2)}) collective-permute-start(bf16[128,128]{1,0:T(8,128)(2,1)S(1)} %get-tuple-element.61), channel_id=1, source_target_pairs={{0,12},{1,13},{2,14},{3,15},{4,8},{5,9},{6,10},{7,11},{8,4},{9,5},... | collective-permute-start | bytes 98312 | tf_op jit(solution)/shard_map/ppermute | solution.py:425
  30.3 2.4 %collective-permute-start.11 = (bf16[128,128]{1,0:T(8,128)(2,1)S(1)}, bf16[128,128]{1,0:T(8,128)(2,1)S(1)}, u32[]{:S(2)}, u32[]{:S(2)}) collective-permute-start(bf16[128,128]{1,0:T(8,128)(2,1)S(1)} %get-tuple-element.62), channel_id=1, source_target_pairs={{0,4},{1,5},{2,6},{3,7},{4,0},{5,1},{6,2},{7,3},{8,12},{9,13},{10,... | collective-permute-start | bytes 98312 | tf_op jit(solution)/shard_map/ppermute | solution.py:425
  33.9 1.1 %collective-permute-done.9.refs_1_ = bf16[128,128]{1,0:T(8,128)(2,1)S(1)} collective-permute-done((bf16[128,128]{1,0:T(8,128)(2,1)S(1)}, bf16[128,128]{1,0:T(8,128)(2,1)S(1)}, u32[]{:S(2)}, u32[]{:S(2)}) %collective-permute-start.9) | collective-permute-done | bytes 32800 | tf_op jit(solution)/shard_map/ppermute | solution.py:425
  35.1 2.4 %collective-permute-start.12 = (bf16[128,128]{1,0:T(8,128)(2,1)S(1)}, bf16[128,128]{1,0:T(8,128)(2,1)S(1)}, u32[]{:S(2)}, u32[]{:S(2)}) collective-permute-start(bf16[128,128]{1,0:T(8,128)(2,1)S(1)} %get-tuple-element.64.refs_0_), channel_id=1, source_target_pairs={{0,8},{1,9},{2,10},{3,11},{4,12},{5,13},{6,14},{7,15},{8,0},{9,1},... | collective-permute-start | bytes 98312 | tf_op jit(solution)/shard_map/ppermute | solution.py:425
  37.6 1.9 %collective-permute-start.16 = (bf16[128,128]{1,0:T(8,128)(2,1)S(1)}, bf16[128,128]{1,0:T(8,128)(2,1)S(1)}, u32[]{:S(2)}, u32[]{:S(2)}) collective-permute-start(bf16[128,128]{1,0:T(8,128)(2,1)S(1)} %get-tuple-element.64.refs_0_), channel_id=1, source_target_pairs={{0,12},{1,13},{2,14},{3,15},{4,8},{5,9},{6,10},{7,11},{8,4},{9,5},... | collective-permute-start | bytes 98312 | tf_op jit(solution)/shard_map/ppermute | solution.py:425
  39.5 2.2 %collective-permute-start.15 = (bf16[128,128]{1,0:T(8,128)(2,1)S(1)}, bf16[128,128]{1,0:T(8,128)(2,1)S(1)}, u32[]{:S(2)}, u32[]{:S(2)}) collective-permute-start(bf16[128,128]{1,0:T(8,128)(2,1)S(1)} %get-tuple-element.64.refs_0_), channel_id=1, source_target_pairs={{0,14},{1,15},{2,12},{3,13},{4,10},{5,11},{6,8},{7,9},{8,6},{9,7},... | collective-permute-start | bytes 98312 | tf_op jit(solution)/shard_map/ppermute | solution.py:425
  41.8 1.2 %collective-permute-start.14 = (bf16[384,128]{1,0:T(8,128)(2,1)S(1)}, bf16[384,128]{1,0:T(8,128)(2,1)S(1)}, u32[]{:S(2)}, u32[]{:S(2)}) collective-permute-start(bf16[384,128]{1,0:T(8,128)(2,1)S(1)} %join.3.refs_0_), channel_id=1, source_target_pairs={{0,2},{1,3},{2,0},{3,1},{4,6},{5,7},{6,4},{7,5},{8,10},{9,11},{10,... | collective-permute-start | bytes 294920 | tf_op jit(solution)/shard_map/ppermute | solution.py:425
  43.3 1.8 %forward.9.refs_6_ = f32[512,128]{1,0:T(8,128)S(1)} custom-call(s32[8,128]{1,0:T(8,128)S(4)} %get-tuple-element.38.slots, bf16[384,128]{1,0:T(8,128)(2,1)S(1)} %join.3.refs_0_, bf16[128,128]{1,0:T(8,128)(2,1)S(1)} %collective-permute-done.16.refs_1_, s32[544,128]{1,0:T(8,128)S(1)} %get-tuple-element.39.refs_2_, f32[544,128]{1,0:T(8,128)S(1)} %get-tuple-element.40.refs_3_, ...), custom_call_target="tpu_custom_call" | custom-call | flops 4000000000 | bytes 8000000 | tf_op jit(solution)/shard_map/forward/pallas_call | solution.py:411
  45.1 1.1 %collective-permute-done.15.refs_1_ = bf16[128,128]{1,0:T(8,128)(2,1)S(1)} collective-permute-done((bf16[128,128]{1,0:T(8,128)(2,1)S(1)}, bf16[128,128]{1,0:T(8,128)(2,1)S(1)}, u32[]{:S(2)}, u32[]{:S(2)}) %collective-permute-start.15) | collective-permute-done | bytes 32800 | tf_op jit(solution)/shard_map/ppermute | solution.py:425
  46.8 1.1 %forward.11 = f32[256,128]{1,0:T(8,128)S(1)} custom-call(s32[8,128]{1,0:T(8,128)S(4)} %get-tuple-element.50.slots, bf16[384,128]{1,0:T(8,128)(2,1)S(1)} %collective-permute-done.14.refs_0_, bf16[128,128]{1,0:T(8,128)(2,1)S(1)} %collective-permute-done.15.refs_1_, s32[544,128]{1,0:T(8,128)S(1)} %get-tuple-element.44.refs_2_, ...), custom_call_target="tpu_custom_call" | custom-call | flops 4000000000 | bytes 8000000 | tf_op jit(solution)/shard_map/forward/pallas_call | solution.py:411
  48.4 0.9 %collective-permute-done.17.refs_2_ = f32[256,128]{1,0:T(8,128)S(1)} collective-permute-done((f32[256,128]{1,0:T(8,128)S(1)}, f32[256,128]{1,0:T(8,128)S(1)}, u32[]{:S(2)}, u32[]{:S(2)}) %collective-permute-start.17) | collective-permute-done | bytes 131104 | tf_op jit(solution)/shard_map/ppermute | solution.py:425
  50.7 0.9 %backward.11 = (bf16[256,128]{1,0:T(8,128)(2,1)S(1)}, bf16[256,128]{1,0:T(8,128)(2,1)S(1)}) custom-call(s32[8,128]{1,0:T(8,128)S(4)} %get-tuple-element.50.slots, bf16[256,128]{1,0:T(8,128)(2,1)S(1)} %collective-permute-done.18.refs_1_.refs_0_, s32[544,128]{1,0:T(8,128)S(1)} %get-tuple-element.54.refs_1_, f32[544,128]{1,0:T(8,128)S(1)} %get-tuple-element.55.refs_2_, ...), custom_call_target="tpu_custom_call" | custom-call | flops 4000000000 | bytes 8000000 | tf_op jit(solution)/shard_map/backward/pallas_call | solution.py:411
  51.6 1.2 %collective-permute-start.20 = (bf16[256,128]{1,0:T(8,128)(2,1)S(1)}, bf16[256,128]{1,0:T(8,128)(2,1)S(1)}, u32[]{:S(2)}, u32[]{:S(2)}) collective-permute-start(bf16[256,128]{1,0:T(8,128)(2,1)S(1)} %get-tuple-element.67), channel_id=1, source_target_pairs={{0,2},{1,3},{2,0},{3,1},{4,6},{5,7},{6,4},{7,5},{8,10},{9,11},{10,... | collective-permute-start | bytes 196616 | tf_op jit(solution)/shard_map/ppermute | solution.py:425
  53.7 1.5 %backward.9.sum_ref = f32[512,128]{1,0:T(8,128)S(1)} custom-call(s32[8,128]{1,0:T(8,128)S(4)} %get-tuple-element.38.slots, bf16[256,128]{1,0:T(8,128)(2,1)S(1)} %residual.3.refs_0_, bf16[256,128]{1,0:T(8,128)(2,1)S(1)} %collective-permute-done.18.refs_1_.refs_0_, s32[544,128]{1,0:T(8,128)S(1)} %get-tuple-element.51.refs_2_, ...), custom_call_target="tpu_custom_call" | custom-call | flops 4000000000 | bytes 8000000 | tf_op jit(solution)/shard_map/backward/pallas_call | solution.py:411
  55.2 1.3 %collective-permute-done.20.y_ref = bf16[256,128]{1,0:T(8,128)(2,1)S(1)} collective-permute-done((bf16[256,128]{1,0:T(8,128)(2,1)S(1)}, bf16[256,128]{1,0:T(8,128)(2,1)S(1)}, u32[]{:S(2)}, u32[]{:S(2)}) %collective-permute-start.20) | collective-permute-done | bytes 65568 | tf_op jit(solution)/shard_map/ppermute | solution.py:425
  56.6 2.0 %collective-permute-start.22 = (bf16[128,128]{1,0:T(8,128)(2,1)S(1)}, bf16[128,128]{1,0:T(8,128)(2,1)S(1)}, u32[]{:S(2)}, u32[]{:S(2)}) collective-permute-start(bf16[128,128]{1,0:T(8,128)(2,1)S(1)} %get-tuple-element.69), channel_id=1, source_target_pairs={{0,12},{1,13},{2,14},{3,15},{4,8},{5,9},{6,10},{7,11},{8,4},{9,5},... | collective-permute-start | bytes 98312 | tf_op jit(solution)/shard_map/ppermute | solution.py:425
  58.6 1.6 %collective-permute-start.23 = (bf16[128,128]{1,0:T(8,128)(2,1)S(1)}, bf16[128,128]{1,0:T(8,128)(2,1)S(1)}, u32[]{:S(2)}, u32[]{:S(2)}) collective-permute-start(bf16[128,128]{1,0:T(8,128)(2,1)S(1)} %get-tuple-element.70), channel_id=1, source_target_pairs={{0,4},{1,5},{2,6},{3,7},{4,0},{5,1},{6,2},{7,3},{8,12},{9,13},{10,... | collective-permute-start | bytes 98312 | tf_op jit(solution)/shard_map/ppermute | solution.py:425
  60.2 1.2 %collective-permute-done.21.refs_1_ = bf16[128,128]{1,0:T(8,128)(2,1)S(1)} collective-permute-done((bf16[128,128]{1,0:T(8,128)(2,1)S(1)}, bf16[128,128]{1,0:T(8,128)(2,1)S(1)}, u32[]{:S(2)}, u32[]{:S(2)}) %collective-permute-start.21) | collective-permute-done | bytes 32800 | tf_op jit(solution)/shard_map/ppermute | solution.py:425
  61.4 1.1 %collective-permute-done.22.refs_2_ = bf16[128,128]{1,0:T(8,128)(2,1)S(1)} collective-permute-done((bf16[128,128]{1,0:T(8,128)(2,1)S(1)}, bf16[128,128]{1,0:T(8,128)(2,1)S(1)}, u32[]{:S(2)}, u32[]{:S(2)}) %collective-permute-start.22) | collective-permute-done | bytes 32800 | tf_op jit(solution)/shard_map/ppermute | solution.py:425
  (54 shorter events, 10.8 us)
Async XLA Ops:
  1.0 10.5 %collective-permute-start = (bf16[192,128]{1,0:T(8,128)(2,1)S(1)}, bf16[192,128]{1,0:T(8,128)(2,1)S(1)}, u32[]{:S(2)}, u32[]{:S(2)}) collective-permute-start(bf16[192,128]{1,0:T(8,128)(2,1)S(1)} %pack.1.refs_0_), channel_id=1, source_target_pairs={{0,8},{1,9},{2,10},{3,11},{4,12},{5,13},{6,14},{7,15},{8,0},{9,1},... | collective-permute-start | bytes 147464 | tf_op jit(solution)/shard_map/ppermute | solution.py:425
  5.2 6.4 %collective-permute-start.1 = (bf16[192,128]{1,0:T(8,128)(2,1)S(1)}, bf16[192,128]{1,0:T(8,128)(2,1)S(1)}, u32[]{:S(2)}, u32[]{:S(2)}) collective-permute-start(bf16[192,128]{1,0:T(8,128)(2,1)S(1)} %pack.1.refs_0_), channel_id=1, source_target_pairs={{0,4},{1,5},{2,6},{3,7},{4,0},{5,1},{6,2},{7,3},{8,12},{9,13},{10,... | collective-permute-start | bytes 147464 | tf_op jit(solution)/shard_map/ppermute | solution.py:425
  6.7 5.9 %collective-permute-start.2 = (bf16[192,128]{1,0:T(8,128)(2,1)S(1)}, bf16[192,128]{1,0:T(8,128)(2,1)S(1)}, u32[]{:S(2)}, u32[]{:S(2)}) collective-permute-start(bf16[192,128]{1,0:T(8,128)(2,1)S(1)} %pack.1.refs_0_), channel_id=1, source_target_pairs={{0,12},{1,13},{2,14},{3,15},{4,8},{5,9},{6,10},{7,11},{8,4},{9,5},... | collective-permute-start | bytes 147464 | tf_op jit(solution)/shard_map/ppermute | solution.py:425
  6.7 9.2 %collective-permute-start.4 = (bf16[192,128]{1,0:T(8,128)(2,1)S(1)}, bf16[192,128]{1,0:T(8,128)(2,1)S(1)}, u32[]{:S(2)}, u32[]{:S(2)}) collective-permute-start(bf16[192,128]{1,0:T(8,128)(2,1)S(1)} %pack.1.refs_0_), channel_id=1, source_target_pairs={{0,14},{1,15},{2,12},{3,13},{4,10},{5,11},{6,8},{7,9},{8,6},{9,7},... | collective-permute-start | bytes 147464 | tf_op jit(solution)/shard_map/ppermute | solution.py:425
  11.5 5.2 %collective-permute-start.3 = (bf16[576,128]{1,0:T(8,128)(2,1)S(1)}, bf16[576,128]{1,0:T(8,128)(2,1)S(1)}, u32[]{:S(2)}, u32[]{:S(2)}) collective-permute-start(bf16[576,128]{1,0:T(8,128)(2,1)S(1)} %join.2.refs_0_), channel_id=1, source_target_pairs={{0,2},{1,3},{2,0},{3,1},{4,6},{5,7},{6,4},{7,5},{8,10},{9,11},{10,... | collective-permute-start | bytes 442376 | tf_op jit(solution)/shard_map/ppermute | solution.py:425
  19.5 1.4 %collective-permute-start.5 = (f32[288,128]{1,0:T(8,128)S(1)}, f32[288,128]{1,0:T(8,128)S(1)}, u32[]{:S(2)}, u32[]{:S(2)}) collective-permute-start(f32[288,128]{1,0:T(8,128)S(1)} %forward.8), channel_id=1, source_target_pairs={{0,1},{1,0},{2,3},{3,2},{4,5},{5,4},{6,7},{7,6},{8,9},{9,8},{10,11... | collective-permute-start | bytes 442376 | tf_op jit(solution)/shard_map/ppermute | solution.py:425
  19.5 1.4 %copy-start.1 = (bf16[32,8,128]{2,1,0:T(8,128)(2,1)S(1)}, bf16[32,8,128]{2,1,0:T(8,128)(2,1)}, u32[]{:S(2)}) copy-start(bf16[32,8,128]{2,1,0:T(8,128)(2,1)} %param.7) | copy-start | bytes 196612
  20.9 1.3 %collective-permute-start.6 = (bf16[256,128]{1,0:T(8,128)(2,1)S(1)}, bf16[256,128]{1,0:T(8,128)(2,1)S(1)}, u32[]{:S(2)}, u32[]{:S(2)}) collective-permute-start(bf16[256,128]{1,0:T(8,128)(2,1)S(1)} %residual.2.refs_0_), channel_id=1, source_target_pairs={{0,1},{1,0},{2,3},{3,2},{4,5},{5,4},{6,7},{7,6},{8,9},{9,8},{10,11... | collective-permute-start | bytes 196616 | tf_op jit(solution)/shard_map/ppermute | solution.py:425
  23.2 4.9 %collective-permute-start.8 = (bf16[256,128]{1,0:T(8,128)(2,1)S(1)}, bf16[256,128]{1,0:T(8,128)(2,1)S(1)}, u32[]{:S(2)}, u32[]{:S(2)}) collective-permute-start(bf16[256,128]{1,0:T(8,128)(2,1)S(1)} %get-tuple-element.59), channel_id=1, source_target_pairs={{0,2},{1,3},{2,0},{3,1},{4,6},{5,7},{6,4},{7,5},{8,10},{9,11},{10,... | collective-permute-start | bytes 196616 | tf_op jit(solution)/shard_map/ppermute | solution.py:425
  24.4 5.8 %collective-permute-start.7 = (bf16[256,128]{1,0:T(8,128)(2,1)S(1)}, bf16[256,128]{1,0:T(8,128)(2,1)S(1)}, u32[]{:S(2)}, u32[]{:S(2)}) collective-permute-start(bf16[256,128]{1,0:T(8,128)(2,1)S(1)} %get-tuple-element.57), channel_id=1, source_target_pairs={{0,2},{1,3},{2,0},{3,1},{4,6},{5,7},{6,4},{7,5},{8,10},{9,11},{10,... | collective-permute-start | bytes 196616 | tf_op jit(solution)/shard_map/ppermute | solution.py:425
  28.1 5.8 %collective-permute-start.10 = (bf16[128,128]{1,0:T(8,128)(2,1)S(1)}, bf16[128,128]{1,0:T(8,128)(2,1)S(1)}, u32[]{:S(2)}, u32[]{:S(2)}) collective-permute-start(bf16[128,128]{1,0:T(8,128)(2,1)S(1)} %get-tuple-element.61), channel_id=1, source_target_pairs={{0,12},{1,13},{2,14},{3,15},{4,8},{5,9},{6,10},{7,11},{8,4},{9,5},... | collective-permute-start | bytes 98312 | tf_op jit(solution)/shard_map/ppermute | solution.py:425
  30.2 2.5 %copy-start.2 = (f32[256,4]{0,1:T(4,128)S(1)}, f32[256,4]{0,1:T(4,128)}, u32[]{:S(2)}) copy-start(f32[256,4]{0,1:T(4,128)} %param.13) | copy-start | bytes 12292
  30.2 2.5 %copy-start.3 = (f32[256,4]{0,1:T(4,128)S(1)}, f32[256,4]{0,1:T(4,128)}, u32[]{:S(2)}) copy-start(f32[256,4]{0,1:T(4,128)} %param.12) | copy-start | bytes 12292
  30.2 2.5 %copy-start.4 = (s32[256,4]{0,1:T(4,128)S(1)}, s32[256,4]{0,1:T(4,128)}, u32[]{:S(2)}) copy-start(s32[256,4]{0,1:T(4,128)} %param.9) | copy-start | bytes 12292
  30.2 4.8 %collective-permute-start.9 = (bf16[128,128]{1,0:T(8,128)(2,1)S(1)}, bf16[128,128]{1,0:T(8,128)(2,1)S(1)}, u32[]{:S(2)}, u32[]{:S(2)}) collective-permute-start(bf16[128,128]{1,0:T(8,128)(2,1)S(1)} %get-tuple-element.60), channel_id=1, source_target_pairs={{0,8},{1,9},{2,10},{3,11},{4,12},{5,13},{6,14},{7,15},{8,0},{9,1},... | collective-permute-start | bytes 98312 | tf_op jit(solution)/shard_map/ppermute | solution.py:425
  30.3 2.5 %copy-start.5 = (s32[16]{0:T(128)S(1)}, s32[16]{0:T(128)}, u32[]{:S(2)}) copy-start(s32[16]{0:T(128)} %param.11) | copy-start | bytes 196
  30.3 4.8 %copy-start = (f32[16,8,128]{2,1,0:T(8,128)S(1)}, f32[16,8,128]{2,1,0:T(8,128)}, u32[]{:S(2)}) copy-start(f32[16,8,128]{2,1,0:T(8,128)} %param.8) | copy-start | bytes 196612
  30.3 4.7 %collective-permute-start.11 = (bf16[128,128]{1,0:T(8,128)(2,1)S(1)}, bf16[128,128]{1,0:T(8,128)(2,1)S(1)}, u32[]{:S(2)}, u32[]{:S(2)}) collective-permute-start(bf16[128,128]{1,0:T(8,128)(2,1)S(1)} %get-tuple-element.62), channel_id=1, source_target_pairs={{0,4},{1,5},{2,6},{3,7},{4,0},{5,1},{6,2},{7,3},{8,12},{9,13},{10,... | collective-permute-start | bytes 98312 | tf_op jit(solution)/shard_map/ppermute | solution.py:425
  35.1 6.7 %collective-permute-start.12 = (bf16[128,128]{1,0:T(8,128)(2,1)S(1)}, bf16[128,128]{1,0:T(8,128)(2,1)S(1)}, u32[]{:S(2)}, u32[]{:S(2)}) collective-permute-start(bf16[128,128]{1,0:T(8,128)(2,1)S(1)} %get-tuple-element.64.refs_0_), channel_id=1, source_target_pairs={{0,8},{1,9},{2,10},{3,11},{4,12},{5,13},{6,14},{7,15},{8,0},{9,1},... | collective-permute-start | bytes 98312 | tf_op jit(solution)/shard_map/ppermute | solution.py:425
  37.4 4.3 %collective-permute-start.13 = (bf16[128,128]{1,0:T(8,128)(2,1)S(1)}, bf16[128,128]{1,0:T(8,128)(2,1)S(1)}, u32[]{:S(2)}, u32[]{:S(2)}) collective-permute-start(bf16[128,128]{1,0:T(8,128)(2,1)S(1)} %get-tuple-element.64.refs_0_), channel_id=1, source_target_pairs={{0,4},{1,5},{2,6},{3,7},{4,0},{5,1},{6,2},{7,3},{8,12},{9,13},{10,... | collective-permute-start | bytes 98312 | tf_op jit(solution)/shard_map/ppermute | solution.py:425
  37.6 5.7 %collective-permute-start.16 = (bf16[128,128]{1,0:T(8,128)(2,1)S(1)}, bf16[128,128]{1,0:T(8,128)(2,1)S(1)}, u32[]{:S(2)}, u32[]{:S(2)}) collective-permute-start(bf16[128,128]{1,0:T(8,128)(2,1)S(1)} %get-tuple-element.64.refs_0_), channel_id=1, source_target_pairs={{0,12},{1,13},{2,14},{3,15},{4,8},{5,9},{6,10},{7,11},{8,4},{9,5},... | collective-permute-start | bytes 98312 | tf_op jit(solution)/shard_map/ppermute | solution.py:425
  39.5 6.7 %collective-permute-start.15 = (bf16[128,128]{1,0:T(8,128)(2,1)S(1)}, bf16[128,128]{1,0:T(8,128)(2,1)S(1)}, u32[]{:S(2)}, u32[]{:S(2)}) collective-permute-start(bf16[128,128]{1,0:T(8,128)(2,1)S(1)} %get-tuple-element.64.refs_0_), channel_id=1, source_target_pairs={{0,14},{1,15},{2,12},{3,13},{4,10},{5,11},{6,8},{7,9},{8,6},{9,7},... | collective-permute-start | bytes 98312 | tf_op jit(solution)/shard_map/ppermute | solution.py:425
  41.8 5.0 %collective-permute-start.14 = (bf16[384,128]{1,0:T(8,128)(2,1)S(1)}, bf16[384,128]{1,0:T(8,128)(2,1)S(1)}, u32[]{:S(2)}, u32[]{:S(2)}) collective-permute-start(bf16[384,128]{1,0:T(8,128)(2,1)S(1)} %join.3.refs_0_), channel_id=1, source_target_pairs={{0,2},{1,3},{2,0},{3,1},{4,6},{5,7},{6,4},{7,5},{8,10},{9,11},{10,... | collective-permute-start | bytes 294920 | tf_op jit(solution)/shard_map/ppermute | solution.py:425
  47.9 1.4 %collective-permute-start.17 = (f32[256,128]{1,0:T(8,128)S(1)}, f32[256,128]{1,0:T(8,128)S(1)}, u32[]{:S(2)}, u32[]{:S(2)}) collective-permute-start(f32[256,128]{1,0:T(8,128)S(1)} %forward.11), channel_id=1, source_target_pairs={{0,1},{1,0},{2,3},{3,2},{4,5},{5,4},{6,7},{7,6},{8,9},{9,8},{10,11... | collective-permute-start | bytes 393224 | tf_op jit(solution)/shard_map/ppermute | solution.py:425
  49.3 1.3 %collective-permute-start.18 = (bf16[256,128]{1,0:T(8,128)(2,1)S(1)}, bf16[256,128]{1,0:T(8,128)(2,1)S(1)}, u32[]{:S(2)}, u32[]{:S(2)}) collective-permute-start(bf16[256,128]{1,0:T(8,128)(2,1)S(1)} %residual.3.refs_0_), channel_id=1, source_target_pairs={{0,1},{1,0},{2,3},{3,2},{4,5},{5,4},{6,7},{7,6},{8,9},{9,8},{10,11... | collective-permute-start | bytes 196616 | tf_op jit(solution)/shard_map/ppermute | solution.py:425
  51.6 4.9 %collective-permute-start.20 = (bf16[256,128]{1,0:T(8,128)(2,1)S(1)}, bf16[256,128]{1,0:T(8,128)(2,1)S(1)}, u32[]{:S(2)}, u32[]{:S(2)}) collective-permute-start(bf16[256,128]{1,0:T(8,128)(2,1)S(1)} %get-tuple-element.67), channel_id=1, source_target_pairs={{0,2},{1,3},{2,0},{3,1},{4,6},{5,7},{6,4},{7,5},{8,10},{9,11},{10,... | collective-permute-start | bytes 196616 | tf_op jit(solution)/shard_map/ppermute | solution.py:425
  52.8 5.8 %collective-permute-start.19 = (bf16[256,128]{1,0:T(8,128)(2,1)S(1)}, bf16[256,128]{1,0:T(8,128)(2,1)S(1)}, u32[]{:S(2)}, u32[]{:S(2)}) collective-permute-start(bf16[256,128]{1,0:T(8,128)(2,1)S(1)} %get-tuple-element.65), channel_id=1, source_target_pairs={{0,2},{1,3},{2,0},{3,1},{4,6},{5,7},{6,4},{7,5},{8,10},{9,11},{10,... | collective-permute-start | bytes 196616 | tf_op jit(solution)/shard_map/ppermute | solution.py:425
  56.5 4.9 %collective-permute-start.21 = (bf16[128,128]{1,0:T(8,128)(2,1)S(1)}, bf16[128,128]{1,0:T(8,128)(2,1)S(1)}, u32[]{:S(2)}, u32[]{:S(2)}) collective-permute-start(bf16[128,128]{1,0:T(8,128)(2,1)S(1)} %get-tuple-element.68), channel_id=1, source_target_pairs={{0,8},{1,9},{2,10},{3,11},{4,12},{5,13},{6,14},{7,15},{8,0},{9,1},... | collective-permute-start | bytes 98312 | tf_op jit(solution)/shard_map/ppermute | solution.py:425
  56.6 5.9 %collective-permute-start.22 = (bf16[128,128]{1,0:T(8,128)(2,1)S(1)}, bf16[128,128]{1,0:T(8,128)(2,1)S(1)}, u32[]{:S(2)}, u32[]{:S(2)}) collective-permute-start(bf16[128,128]{1,0:T(8,128)(2,1)S(1)} %get-tuple-element.69), channel_id=1, source_target_pairs={{0,12},{1,13},{2,14},{3,15},{4,8},{5,9},{6,10},{7,11},{8,4},{9,5},... | collective-permute-start | bytes 98312 | tf_op jit(solution)/shard_map/ppermute | solution.py:425
  58.6 4.2 %collective-permute-start.23 = (bf16[128,128]{1,0:T(8,128)(2,1)S(1)}, bf16[128,128]{1,0:T(8,128)(2,1)S(1)}, u32[]{:S(2)}, u32[]{:S(2)}) collective-permute-start(bf16[128,128]{1,0:T(8,128)(2,1)S(1)} %get-tuple-element.70), channel_id=1, source_target_pairs={{0,4},{1,5},{2,6},{3,7},{4,0},{5,1},{6,2},{7,3},{8,12},{9,13},{10,... | collective-permute-start | bytes 98312 | tf_op jit(solution)/shard_map/ppermute | solution.py:425

commit v20 on v19

--- a/solution.py
+++ b/solution.py
@@ -421,9 +421,10 @@
     )(*operands)
 
 
-def exchange(values, n_slab, distance):
+def exchange(values, n_slab, distance, odd_distance=None):
+    far = (distance, distance if odd_distance is None else odd_distance)
     return lax.ppermute(
-        values, "slab", [(device, device ^ distance) for device in range(n_slab)])
+        values, "slab", [(device, device ^ far[device % 2]) for device in range(n_slab)])
 
 
 def shards(sinogram, start_volume, slot_voxel, slot_ray, live_count, block_slope, block_offset):
@@ -511,11 +512,11 @@
     for sweep in range(ITERS):
         last = sweep + 1 == ITERS
         if paired:
-            over_2, over_1, over_3, across = [
-                exchange(payload, n_slab, distance) for distance in (8, 4, 12, 14)]
-            z_part = join(payload, over_2, over_1)
+            place_1, place_2, place_3, across = [
+                exchange(payload, n_slab, *pair) for pair in ((8, 12), (4, 8), (12, 4), (14, 6))]
+            z_part = join(payload, place_1, place_2)
             y_part = exchange(z_part, n_slab, 2)
-            along_z, along_y = (z_part, over_3), (y_part, across)
+            along_z, along_y = (z_part, place_3), (y_part, across)
             if sweep == 0:
                 (z_list,), z_rows, z_forward, z_backward = setup(along_z, 4, (None,))
             both = forward(z_list, along_z, 4, z_forward, 2 * n_rays)
@@ -536,14 +537,14 @@
             far_part, near_part = exchange(far_sum, n_slab, 2), exchange(near_sum, n_slab, 2)
             z_sum = backward(z_list, [residual, other_residual], 4, z_backward, F32)
             piece = shape((rows, extent), BF16)
-            piece_2, piece_3 = call(
+            piece_1, piece_3 = call(
                 functools.partial(combine_kernel, (1, 3)), "combine", 16, [VMEM] * 2,
                 [piece, piece], z_sum, far_part)
-            got = [exchange(piece_2, n_slab, 8), exchange(piece_3, n_slab, 12)]
-            own_piece, piece_1 = call(
+            got = [exchange(piece_1, n_slab, 8, 12), exchange(piece_3, n_slab, 12, 4)]
+            own_piece, piece_2 = call(
                 functools.partial(combine_kernel, (0, 2)), "combine", 16, [VMEM] * 2,
                 [shape((rows, extent), F32), piece], z_sum, near_part)
-            pieces = [own_piece, *got, exchange(piece_1, n_slab, 4)]
+            pieces = [own_piece, *got, exchange(piece_2, n_slab, 4, 8)]
         else:
             everyone = lax.all_gather(payload, "slab", axis=0, tiled=True)
             if sweep == 0:

time: 64.2 us -> 63.2 us (0.984); the launches traced: 63.5 us -> 63.2 us
  Pallas kernels: 17.7 us -> 16.5 us
  waiting for transfers between devices: 13.6 us -> 14.4 us
    pallas_call x26, Pallas kernels: 17.7 us -> 16.5 us  [call(): pl.pallas_call(kernel, out_shape=out_shape, in_specs=in_specs, out_specs=...]
    ppermute x24, waiting for transfers between devices: 13.6 us -> 14.4 us  [exchange(): lax.ppermute(values, 'slab', [(device, device ^ far[device % 2]) for devi...]
where the time goes in v20:
time: 63.2 us
  starting transfers between devices  32 us (51%)
  Pallas kernels  16.5 us (26%)
  waiting for transfers between devices  14.4 us (23%)
    ppermute x24, starting transfers between devices, exchange(): lax.ppermute(values, 'slab', [(device, device ^ far[device % 2]) for devi...  32 us
    pallas_call x26, Pallas kernels, call(): pl.pallas_call(kernel, out_shape=out_shape, in_specs=in_specs, out_specs=...  16.5 us
    ppermute x24, waiting for transfers between devices, exchange(): lax.ppermute(values, 'slab', [(device, device ^ far[device % 2]) for devi...  14.4 us
  transfers between devices with their start and end apart: 24, of which 16 were waited for; matrix products, arithmetic and copies ran while one was open for 0% of the time, Pallas kernels for 16%

profile of v20, /device:TPU:0, one launch (start us, length us, event | category | flops | bytes accessed | tf_op | source)
XLA Modules:
  0.0 63.2 jit_solution(1824730509811789380)
XLA Ops:
  0.0 1.0 %pack.1.refs_0_ = bf16[192,128]{1,0:T(8,128)(2,1)S(1)} custom-call(f32[128,128]{1,0:T(8,128)} %bitcast.8, f32[4,256]{1,0:T(4,128)} %bitcast.12, f32[4,256]{1,0:T(4,128)} %bitcast.14, s32[4,256]{1,0:T(4,128)} %bitcast.16, s32[1,256]{1,0:T(1,128)} %bitcast.20, s32[1,16]{1,0:T(1,128)} %bitcast.18), custom_call_target="tpu_custom_call" | custom-call | flops 4000000000 | bytes 8000000 | tf_op jit(solution)/shard_map/pack/pallas_call | solution.py:411
  1.0 4.1 %collective-permute-start = (bf16[192,128]{1,0:T(8,128)(2,1)S(1)}, bf16[192,128]{1,0:T(8,128)(2,1)S(1)}, u32[]{:S(2)}, u32[]{:S(2)}) collective-permute-start(bf16[192,128]{1,0:T(8,128)(2,1)S(1)} %pack.1.refs_0_), channel_id=1, source_target_pairs={{0,8},{1,13},{2,10},{3,15},{4,12},{5,9},{6,14},{7,11},{8,0},{9,5},... | collective-permute-start | bytes 147464 | tf_op jit(solution)/shard_map/ppermute | solution.py:426
  5.2 1.6 %collective-permute-start.1 = (bf16[192,128]{1,0:T(8,128)(2,1)S(1)}, bf16[192,128]{1,0:T(8,128)(2,1)S(1)}, u32[]{:S(2)}, u32[]{:S(2)}) collective-permute-start(bf16[192,128]{1,0:T(8,128)(2,1)S(1)} %pack.1.refs_0_), channel_id=1, source_target_pairs={{0,4},{1,9},{2,6},{3,11},{4,0},{5,13},{6,2},{7,15},{8,12},{9,1},{1... | collective-permute-start | bytes 147464 | tf_op jit(solution)/shard_map/ppermute | solution.py:426
  6.7 4.8 %collective-permute-start.4 = (bf16[192,128]{1,0:T(8,128)(2,1)S(1)}, bf16[192,128]{1,0:T(8,128)(2,1)S(1)}, u32[]{:S(2)}, u32[]{:S(2)}) collective-permute-start(bf16[192,128]{1,0:T(8,128)(2,1)S(1)} %pack.1.refs_0_), channel_id=1, source_target_pairs={{0,14},{1,7},{2,12},{3,5},{4,10},{5,3},{6,8},{7,1},{8,6},{9,15},{1... | collective-permute-start | bytes 147464 | tf_op jit(solution)/shard_map/ppermute | solution.py:426
  12.6 1.5 %setup.2 = (s32[8,128]{1,0:T(8,128)S(4)}, f32[64,128]{1,0:T(8,128)S(1)}, s32[544,128]{1,0:T(8,128)S(1)}, f32[544,128]{1,0:T(8,128)S(1)}, f32[544,128]{1,0:T(8,12...) custom-call(bf16[576,128]{1,0:T(8,128)(2,1)S(1)} %join.2.refs_0_, ...), custom_call_target="tpu_custom_call" | custom-call | flops 4000000000 | bytes 8000000 | tf_op jit(solution)/shard_map/setup/pallas_call | solution.py:411
  14.1 1.5 %forward.6.refs_2_.refs_6_ = f32[512,128]{1,0:T(8,128)S(1)} custom-call(s32[8,128]{1,0:T(8,128)S(4)} %get-tuple-element.38.slots, bf16[576,128]{1,0:T(8,128)(2,1)S(1)} %join.2.refs_0_, bf16[192,128]{1,0:T(8,128)(2,1)S(1)} %collective-permute-done.2.refs_1_, s32[544,128]{1,0:T(8,128)S(1)} %get-tuple-element.39.refs_2_, ...), custom_call_target="tpu_custom_call" | custom-call | flops 4000000000 | bytes 8000000 | tf_op jit(solution)/shard_map/forward/pallas_call | solution.py:411
  15.6 1.1 %collective-permute-done.3.refs_0_ = bf16[576,128]{1,0:T(8,128)(2,1)S(1)} collective-permute-done((bf16[576,128]{1,0:T(8,128)(2,1)S(1)}, bf16[576,128]{1,0:T(8,128)(2,1)S(1)}, u32[]{:S(2)}, u32[]{:S(2)}) %collective-permute-start.3) | collective-permute-done | bytes 147488 | tf_op jit(solution)/shard_map/ppermute | solution.py:426
  16.7 1.6 %setup.3 = (s32[8,128]{1,0:T(8,128)S(4)}, s32[8,128]{1,0:T(8,128)S(4)}, f32[64,128]{1,0:T(8,128)S(1)}, s32[544,128]{1,0:T(8,128)S(1)}, f32[544,128]{1,0:T(8,128)...) custom-call(bf16[576,128]{1,0:T(8,128)(2,1)S(1)} %collective-permute, ...), custom_call_target="tpu_custom_call" | custom-call | flops 4000000000 | bytes 8000000 | tf_op jit(solution)/shard_map/setup/pallas_call | solution.py:411
  18.3 0.8 %forward.8 = f32[288,128]{1,0:T(8,128)S(1)} custom-call(s32[8,128]{1,0:T(8,128)S(4)} %get-tuple-element.50.slots, bf16[576,128]{1,0:T(8,128)(2,1)S(1)} %collective-permute-done.3.refs_0_, bf16[192,128]{1,0:T(8,128)(2,1)S(1)} %collective-permute-done.4.refs_1_, s32[544,128]{1,0:T(8,128)S(1)} %get-tuple-element.44.refs_2_, ...), custom_call_target="tpu_custom_call" | custom-call | flops 4000000000 | bytes 8000000 | tf_op jit(solution)/shard_map/forward/pallas_call | solution.py:411
  19.2 0.8 %forward.7.projection_ref = f32[256,128]{1,0:T(8,128)S(1)} custom-call(s32[8,128]{1,0:T(8,128)S(4)} %get-tuple-element.43.slots, bf16[576,128]{1,0:T(8,128)(2,1)S(1)} %collective-permute-done.3.refs_0_, bf16[192,128]{1,0:T(8,128)(2,1)S(1)} %collective-permute-done.4.refs_1_, s32[544,128]{1,0:T(8,128)S(1)} %get-tuple-element.44.refs_2_, ...), custom_call_target="tpu_custom_call" | custom-call | flops 4000000000 | bytes 8000000 | tf_op jit(solution)/shard_map/forward/pallas_call | solution.py:411
  22.5 1.5 %collective-permute-start.8 = (bf16[256,128]{1,0:T(8,128)(2,1)S(1)}, bf16[256,128]{1,0:T(8,128)(2,1)S(1)}, u32[]{:S(2)}, u32[]{:S(2)}) collective-permute-start(bf16[256,128]{1,0:T(8,128)(2,1)S(1)} %get-tuple-element.59), channel_id=1, source_target_pairs={{0,2},{1,3},{2,0},{3,1},{4,6},{5,7},{6,4},{7,5},{8,10},{9,11},{10,... | collective-permute-start | bytes 196616 | tf_op jit(solution)/shard_map/ppermute | solution.py:426
  24.6 1.2 %backward.6.sum_ref = f32[512,128]{1,0:T(8,128)S(1)} custom-call(s32[8,128]{1,0:T(8,128)S(4)} %get-tuple-element.38.slots, bf16[256,128]{1,0:T(8,128)(2,1)S(1)} %residual.2.refs_0_, bf16[256,128]{1,0:T(8,128)(2,1)S(1)} %collective-permute-done.6.refs_1_.refs_0_, s32[544,128]{1,0:T(8,128)S(1)} %get-tuple-element.51.refs_2_, ...), custom_call_target="tpu_custom_call" | custom-call | flops 4000000000 | bytes 8000000 | tf_op jit(solution)/shard_map/backward/pallas_call | solution.py:411
  25.9 1.6 %collective-permute-done.8.y_ref = bf16[256,128]{1,0:T(8,128)(2,1)S(1)} collective-permute-done((bf16[256,128]{1,0:T(8,128)(2,1)S(1)}, bf16[256,128]{1,0:T(8,128)(2,1)S(1)}, u32[]{:S(2)}, u32[]{:S(2)}) %collective-permute-start.8) | collective-permute-done | bytes 65568 | tf_op jit(solution)/shard_map/ppermute | solution.py:426
  27.5 2.2 %collective-permute-start.10 = (bf16[128,128]{1,0:T(8,128)(2,1)S(1)}, bf16[128,128]{1,0:T(8,128)(2,1)S(1)}, u32[]{:S(2)}, u32[]{:S(2)}) collective-permute-start(bf16[128,128]{1,0:T(8,128)(2,1)S(1)} %get-tuple-element.61), channel_id=1, source_target_pairs={{0,12},{1,5},{2,14},{3,7},{4,8},{5,1},{6,10},{7,3},{8,4},{9,13},{1... | collective-permute-start | bytes 98312 | tf_op jit(solution)/shard_map/ppermute | solution.py:426
  29.8 2.3 %collective-permute-start.11 = (bf16[128,128]{1,0:T(8,128)(2,1)S(1)}, bf16[128,128]{1,0:T(8,128)(2,1)S(1)}, u32[]{:S(2)}, u32[]{:S(2)}) collective-permute-start(bf16[128,128]{1,0:T(8,128)(2,1)S(1)} %get-tuple-element.62), channel_id=1, source_target_pairs={{0,4},{1,9},{2,6},{3,11},{4,0},{5,13},{6,2},{7,15},{8,12},{9,1},{1... | collective-permute-start | bytes 98312 | tf_op jit(solution)/shard_map/ppermute | solution.py:426
  33.3 1.3 %collective-permute-done.9.refs_1_ = bf16[128,128]{1,0:T(8,128)(2,1)S(1)} collective-permute-done((bf16[128,128]{1,0:T(8,128)(2,1)S(1)}, bf16[128,128]{1,0:T(8,128)(2,1)S(1)}, u32[]{:S(2)}, u32[]{:S(2)}) %collective-permute-start.9) | collective-permute-done | bytes 32800 | tf_op jit(solution)/shard_map/ppermute | solution.py:426
  34.6 2.2 %collective-permute-start.12 = (bf16[128,128]{1,0:T(8,128)(2,1)S(1)}, bf16[128,128]{1,0:T(8,128)(2,1)S(1)}, u32[]{:S(2)}, u32[]{:S(2)}) collective-permute-start(bf16[128,128]{1,0:T(8,128)(2,1)S(1)} %get-tuple-element.64.refs_0_), channel_id=1, source_target_pairs={{0,8},{1,13},{2,10},{3,15},{4,12},{5,9},{6,14},{7,11},{8,0},{9,5},... | collective-permute-start | bytes 98312 | tf_op jit(solution)/shard_map/ppermute | solution.py:426
  37.2 1.9 %collective-permute-start.16 = (bf16[128,128]{1,0:T(8,128)(2,1)S(1)}, bf16[128,128]{1,0:T(8,128)(2,1)S(1)}, u32[]{:S(2)}, u32[]{:S(2)}) collective-permute-start(bf16[128,128]{1,0:T(8,128)(2,1)S(1)} %get-tuple-element.64.refs_0_), channel_id=1, source_target_pairs={{0,12},{1,5},{2,14},{3,7},{4,8},{5,1},{6,10},{7,3},{8,4},{9,13},{1... | collective-permute-start | bytes 98312 | tf_op jit(solution)/shard_map/ppermute | solution.py:426
  39.0 2.6 %collective-permute-start.15 = (bf16[128,128]{1,0:T(8,128)(2,1)S(1)}, bf16[128,128]{1,0:T(8,128)(2,1)S(1)}, u32[]{:S(2)}, u32[]{:S(2)}) collective-permute-start(bf16[128,128]{1,0:T(8,128)(2,1)S(1)} %get-tuple-element.64.refs_0_), channel_id=1, source_target_pairs={{0,14},{1,7},{2,12},{3,5},{4,10},{5,3},{6,8},{7,1},{8,6},{9,15},{1... | collective-permute-start | bytes 98312 | tf_op jit(solution)/shard_map/ppermute | solution.py:426
  41.6 0.9 %collective-permute-start.14 = (bf16[384,128]{1,0:T(8,128)(2,1)S(1)}, bf16[384,128]{1,0:T(8,128)(2,1)S(1)}, u32[]{:S(2)}, u32[]{:S(2)}) collective-permute-start(bf16[384,128]{1,0:T(8,128)(2,1)S(1)} %join.3.refs_0_), channel_id=1, source_target_pairs={{0,2},{1,3},{2,0},{3,1},{4,6},{5,7},{6,4},{7,5},{8,10},{9,11},{10,... | collective-permute-start | bytes 294920 | tf_op jit(solution)/shard_map/ppermute | solution.py:426
  42.9 1.5 %forward.9.refs_6_ = f32[512,128]{1,0:T(8,128)S(1)} custom-call(s32[8,128]{1,0:T(8,128)S(4)} %get-tuple-element.38.slots, bf16[384,128]{1,0:T(8,128)(2,1)S(1)} %join.3.refs_0_, bf16[128,128]{1,0:T(8,128)(2,1)S(1)} %collective-permute-done.16.refs_1_, s32[544,128]{1,0:T(8,128)S(1)} %get-tuple-element.39.refs_2_, f32[544,128]{1,0:T(8,128)S(1)} %get-tuple-element.40.refs_3_, ...), custom_call_target="tpu_custom_call" | custom-call | flops 4000000000 | bytes 8000000 | tf_op jit(solution)/shard_map/forward/pallas_call | solution.py:411
  44.3 1.4 %collective-permute-done.15.refs_1_ = bf16[128,128]{1,0:T(8,128)(2,1)S(1)} collective-permute-done((bf16[128,128]{1,0:T(8,128)(2,1)S(1)}, bf16[128,128]{1,0:T(8,128)(2,1)S(1)}, u32[]{:S(2)}, u32[]{:S(2)}) %collective-permute-start.15) | collective-permute-done | bytes 32800 | tf_op jit(solution)/shard_map/ppermute | solution.py:426
  45.8 0.9 %collective-permute-done.14.refs_0_ = bf16[384,128]{1,0:T(8,128)(2,1)S(1)} collective-permute-done((bf16[384,128]{1,0:T(8,128)(2,1)S(1)}, bf16[384,128]{1,0:T(8,128)(2,1)S(1)}, u32[]{:S(2)}, u32[]{:S(2)}) %collective-permute-start.14) | collective-permute-done | bytes 98336 | tf_op jit(solution)/shard_map/ppermute | solution.py:426
  46.7 0.7 %forward.11 = f32[256,128]{1,0:T(8,128)S(1)} custom-call(s32[8,128]{1,0:T(8,128)S(4)} %get-tuple-element.50.slots, bf16[384,128]{1,0:T(8,128)(2,1)S(1)} %collective-permute-done.14.refs_0_, bf16[128,128]{1,0:T(8,128)(2,1)S(1)} %collective-permute-done.15.refs_1_, s32[544,128]{1,0:T(8,128)S(1)} %get-tuple-element.44.refs_2_, ...), custom_call_target="tpu_custom_call" | custom-call | flops 4000000000 | bytes 8000000 | tf_op jit(solution)/shard_map/forward/pallas_call | solution.py:411
  47.5 0.8 %forward.10.projection_ref = f32[256,128]{1,0:T(8,128)S(1)} custom-call(s32[8,128]{1,0:T(8,128)S(4)} %get-tuple-element.43.slots, bf16[384,128]{1,0:T(8,128)(2,1)S(1)} %collective-permute-done.14.refs_0_, bf16[128,128]{1,0:T(8,128)(2,1)S(1)} %collective-permute-done.15.refs_1_, s32[544,128]{1,0:T(8,128)S(1)} %get-tuple-element.44.refs_2_, ...), custom_call_target="tpu_custom_call" | custom-call | flops 4000000000 | bytes 8000000 | tf_op jit(solution)/shard_map/forward/pallas_call | solution.py:411
  50.8 1.5 %collective-permute-start.20 = (bf16[256,128]{1,0:T(8,128)(2,1)S(1)}, bf16[256,128]{1,0:T(8,128)(2,1)S(1)}, u32[]{:S(2)}, u32[]{:S(2)}) collective-permute-start(bf16[256,128]{1,0:T(8,128)(2,1)S(1)} %get-tuple-element.67), channel_id=1, source_target_pairs={{0,2},{1,3},{2,0},{3,1},{4,6},{5,7},{6,4},{7,5},{8,10},{9,11},{10,... | collective-permute-start | bytes 196616 | tf_op jit(solution)/shard_map/ppermute | solution.py:426
  52.9 1.2 %backward.9.sum_ref = f32[512,128]{1,0:T(8,128)S(1)} custom-call(s32[8,128]{1,0:T(8,128)S(4)} %get-tuple-element.38.slots, bf16[256,128]{1,0:T(8,128)(2,1)S(1)} %residual.3.refs_0_, bf16[256,128]{1,0:T(8,128)(2,1)S(1)} %collective-permute-done.18.refs_1_.refs_0_, s32[544,128]{1,0:T(8,128)S(1)} %get-tuple-element.51.refs_2_, ...), custom_call_target="tpu_custom_call" | custom-call | flops 4000000000 | bytes 8000000 | tf_op jit(solution)/shard_map/backward/pallas_call | solution.py:411
  54.1 1.6 %collective-permute-done.20.y_ref = bf16[256,128]{1,0:T(8,128)(2,1)S(1)} collective-permute-done((bf16[256,128]{1,0:T(8,128)(2,1)S(1)}, bf16[256,128]{1,0:T(8,128)(2,1)S(1)}, u32[]{:S(2)}, u32[]{:S(2)}) %collective-permute-start.20) | collective-permute-done | bytes 65568 | tf_op jit(solution)/shard_map/ppermute | solution.py:426
  56.5 2.0 %collective-permute-start.22 = (bf16[128,128]{1,0:T(8,128)(2,1)S(1)}, bf16[128,128]{1,0:T(8,128)(2,1)S(1)}, u32[]{:S(2)}, u32[]{:S(2)}) collective-permute-start(bf16[128,128]{1,0:T(8,128)(2,1)S(1)} %get-tuple-element.69), channel_id=1, source_target_pairs={{0,12},{1,5},{2,14},{3,7},{4,8},{5,1},{6,10},{7,3},{8,4},{9,13},{1... | collective-permute-start | bytes 98312 | tf_op jit(solution)/shard_map/ppermute | solution.py:426
  58.5 0.9 %collective-permute-start.23 = (bf16[128,128]{1,0:T(8,128)(2,1)S(1)}, bf16[128,128]{1,0:T(8,128)(2,1)S(1)}, u32[]{:S(2)}, u32[]{:S(2)}) collective-permute-start(bf16[128,128]{1,0:T(8,128)(2,1)S(1)} %get-tuple-element.70), channel_id=1, source_target_pairs={{0,4},{1,9},{2,6},{3,11},{4,0},{5,13},{6,2},{7,15},{8,12},{9,1},{1... | collective-permute-start | bytes 98312 | tf_op jit(solution)/shard_map/ppermute | solution.py:426
  59.4 1.7 %collective-permute-done.21.refs_1_ = bf16[128,128]{1,0:T(8,128)(2,1)S(1)} collective-permute-done((bf16[128,128]{1,0:T(8,128)(2,1)S(1)}, bf16[128,128]{1,0:T(8,128)(2,1)S(1)}, u32[]{:S(2)}, u32[]{:S(2)}) %collective-permute-start.21) | collective-permute-done | bytes 32800 | tf_op jit(solution)/shard_map/ppermute | solution.py:426
  61.1 1.2 %collective-permute-done.22.refs_2_ = bf16[128,128]{1,0:T(8,128)(2,1)S(1)} collective-permute-done((bf16[128,128]{1,0:T(8,128)(2,1)S(1)}, bf16[128,128]{1,0:T(8,128)(2,1)S(1)}, u32[]{:S(2)}, u32[]{:S(2)}) %collective-permute-start.22) | collective-permute-done | bytes 32800 | tf_op jit(solution)/shard_map/ppermute | solution.py:426
  (54 shorter events, 11.1 us)
Async XLA Ops:
  1.0 10.5 %collective-permute-start = (bf16[192,128]{1,0:T(8,128)(2,1)S(1)}, bf16[192,128]{1,0:T(8,128)(2,1)S(1)}, u32[]{:S(2)}, u32[]{:S(2)}) collective-permute-start(bf16[192,128]{1,0:T(8,128)(2,1)S(1)} %pack.1.refs_0_), channel_id=1, source_target_pairs={{0,8},{1,13},{2,10},{3,15},{4,12},{5,9},{6,14},{7,11},{8,0},{9,5},... | collective-permute-start | bytes 147464 | tf_op jit(solution)/shard_map/ppermute | solution.py:426
  5.2 6.4 %collective-permute-start.1 = (bf16[192,128]{1,0:T(8,128)(2,1)S(1)}, bf16[192,128]{1,0:T(8,128)(2,1)S(1)}, u32[]{:S(2)}, u32[]{:S(2)}) collective-permute-start(bf16[192,128]{1,0:T(8,128)(2,1)S(1)} %pack.1.refs_0_), channel_id=1, source_target_pairs={{0,4},{1,9},{2,6},{3,11},{4,0},{5,13},{6,2},{7,15},{8,12},{9,1},{1... | collective-permute-start | bytes 147464 | tf_op jit(solution)/shard_map/ppermute | solution.py:426
  6.7 5.9 %collective-permute-start.2 = (bf16[192,128]{1,0:T(8,128)(2,1)S(1)}, bf16[192,128]{1,0:T(8,128)(2,1)S(1)}, u32[]{:S(2)}, u32[]{:S(2)}) collective-permute-start(bf16[192,128]{1,0:T(8,128)(2,1)S(1)} %pack.1.refs_0_), channel_id=1, source_target_pairs={{0,12},{1,5},{2,14},{3,7},{4,8},{5,1},{6,10},{7,3},{8,4},{9,13},{1... | collective-permute-start | bytes 147464 | tf_op jit(solution)/shard_map/ppermute | solution.py:426
  6.7 8.9 %collective-permute-start.4 = (bf16[192,128]{1,0:T(8,128)(2,1)S(1)}, bf16[192,128]{1,0:T(8,128)(2,1)S(1)}, u32[]{:S(2)}, u32[]{:S(2)}) collective-permute-start(bf16[192,128]{1,0:T(8,128)(2,1)S(1)} %pack.1.refs_0_), channel_id=1, source_target_pairs={{0,14},{1,7},{2,12},{3,5},{4,10},{5,3},{6,8},{7,1},{8,6},{9,15},{1... | collective-permute-start | bytes 147464 | tf_op jit(solution)/shard_map/ppermute | solution.py:426
  11.5 5.2 %collective-permute-start.3 = (bf16[576,128]{1,0:T(8,128)(2,1)S(1)}, bf16[576,128]{1,0:T(8,128)(2,1)S(1)}, u32[]{:S(2)}, u32[]{:S(2)}) collective-permute-start(bf16[576,128]{1,0:T(8,128)(2,1)S(1)} %join.2.refs_0_), channel_id=1, source_target_pairs={{0,2},{1,3},{2,0},{3,1},{4,6},{5,7},{6,4},{7,5},{8,10},{9,11},{10,... | collective-permute-start | bytes 442376 | tf_op jit(solution)/shard_map/ppermute | solution.py:426
  19.1 1.4 %collective-permute-start.5 = (f32[288,128]{1,0:T(8,128)S(1)}, f32[288,128]{1,0:T(8,128)S(1)}, u32[]{:S(2)}, u32[]{:S(2)}) collective-permute-start(f32[288,128]{1,0:T(8,128)S(1)} %forward.8), channel_id=1, source_target_pairs={{0,1},{1,0},{2,3},{3,2},{4,5},{5,4},{6,7},{7,6},{8,9},{9,8},{10,11... | collective-permute-start | bytes 442376 | tf_op jit(solution)/shard_map/ppermute | solution.py:426
  19.2 1.4 %copy-start.1 = (bf16[32,8,128]{2,1,0:T(8,128)(2,1)S(1)}, bf16[32,8,128]{2,1,0:T(8,128)(2,1)}, u32[]{:S(2)}) copy-start(bf16[32,8,128]{2,1,0:T(8,128)(2,1)} %param.7) | copy-start | bytes 196612
  20.6 1.3 %collective-permute-start.6 = (bf16[256,128]{1,0:T(8,128)(2,1)S(1)}, bf16[256,128]{1,0:T(8,128)(2,1)S(1)}, u32[]{:S(2)}, u32[]{:S(2)}) collective-permute-start(bf16[256,128]{1,0:T(8,128)(2,1)S(1)} %residual.2.refs_0_), channel_id=1, source_target_pairs={{0,1},{1,0},{2,3},{3,2},{4,5},{5,4},{6,7},{7,6},{8,9},{9,8},{10,11... | collective-permute-start | bytes 196616 | tf_op jit(solution)/shard_map/ppermute | solution.py:426
  22.5 4.9 %collective-permute-start.8 = (bf16[256,128]{1,0:T(8,128)(2,1)S(1)}, bf16[256,128]{1,0:T(8,128)(2,1)S(1)}, u32[]{:S(2)}, u32[]{:S(2)}) collective-permute-start(bf16[256,128]{1,0:T(8,128)(2,1)S(1)} %get-tuple-element.59), channel_id=1, source_target_pairs={{0,2},{1,3},{2,0},{3,1},{4,6},{5,7},{6,4},{7,5},{8,10},{9,11},{10,... | collective-permute-start | bytes 196616 | tf_op jit(solution)/shard_map/ppermute | solution.py:426
  24.1 5.7 %collective-permute-start.7 = (bf16[256,128]{1,0:T(8,128)(2,1)S(1)}, bf16[256,128]{1,0:T(8,128)(2,1)S(1)}, u32[]{:S(2)}, u32[]{:S(2)}) collective-permute-start(bf16[256,128]{1,0:T(8,128)(2,1)S(1)} %get-tuple-element.57), channel_id=1, source_target_pairs={{0,2},{1,3},{2,0},{3,1},{4,6},{5,7},{6,4},{7,5},{8,10},{9,11},{10,... | collective-permute-start | bytes 196616 | tf_op jit(solution)/shard_map/ppermute | solution.py:426
  27.5 5.8 %collective-permute-start.10 = (bf16[128,128]{1,0:T(8,128)(2,1)S(1)}, bf16[128,128]{1,0:T(8,128)(2,1)S(1)}, u32[]{:S(2)}, u32[]{:S(2)}) collective-permute-start(bf16[128,128]{1,0:T(8,128)(2,1)S(1)} %get-tuple-element.61), channel_id=1, source_target_pairs={{0,12},{1,5},{2,14},{3,7},{4,8},{5,1},{6,10},{7,3},{8,4},{9,13},{1... | collective-permute-start | bytes 98312 | tf_op jit(solution)/shard_map/ppermute | solution.py:426
  29.7 2.3 %copy-start.2 = (f32[256,4]{0,1:T(4,128)S(1)}, f32[256,4]{0,1:T(4,128)}, u32[]{:S(2)}) copy-start(f32[256,4]{0,1:T(4,128)} %param.13) | copy-start | bytes 12292
  29.7 2.3 %copy-start.3 = (f32[256,4]{0,1:T(4,128)S(1)}, f32[256,4]{0,1:T(4,128)}, u32[]{:S(2)}) copy-start(f32[256,4]{0,1:T(4,128)} %param.12) | copy-start | bytes 12292
  29.7 2.3 %copy-start.4 = (s32[256,4]{0,1:T(4,128)S(1)}, s32[256,4]{0,1:T(4,128)}, u32[]{:S(2)}) copy-start(s32[256,4]{0,1:T(4,128)} %param.9) | copy-start | bytes 12292
  29.7 4.8 %collective-permute-start.9 = (bf16[128,128]{1,0:T(8,128)(2,1)S(1)}, bf16[128,128]{1,0:T(8,128)(2,1)S(1)}, u32[]{:S(2)}, u32[]{:S(2)}) collective-permute-start(bf16[128,128]{1,0:T(8,128)(2,1)S(1)} %get-tuple-element.60), channel_id=1, source_target_pairs={{0,8},{1,13},{2,10},{3,15},{4,12},{5,9},{6,14},{7,11},{8,0},{9,5},... | collective-permute-start | bytes 98312 | tf_op jit(solution)/shard_map/ppermute | solution.py:426
  29.8 2.3 %copy-start.5 = (s32[16]{0:T(128)S(1)}, s32[16]{0:T(128)}, u32[]{:S(2)}) copy-start(s32[16]{0:T(128)} %param.11) | copy-start | bytes 196
  29.8 4.8 %copy-start = (f32[16,8,128]{2,1,0:T(8,128)S(1)}, f32[16,8,128]{2,1,0:T(8,128)}, u32[]{:S(2)}) copy-start(f32[16,8,128]{2,1,0:T(8,128)} %param.8) | copy-start | bytes 196612
  29.8 4.7 %collective-permute-start.11 = (bf16[128,128]{1,0:T(8,128)(2,1)S(1)}, bf16[128,128]{1,0:T(8,128)(2,1)S(1)}, u32[]{:S(2)}, u32[]{:S(2)}) collective-permute-start(bf16[128,128]{1,0:T(8,128)(2,1)S(1)} %get-tuple-element.62), channel_id=1, source_target_pairs={{0,4},{1,9},{2,6},{3,11},{4,0},{5,13},{6,2},{7,15},{8,12},{9,1},{1... | collective-permute-start | bytes 98312 | tf_op jit(solution)/shard_map/ppermute | solution.py:426
  34.6 7.0 %collective-permute-start.12 = (bf16[128,128]{1,0:T(8,128)(2,1)S(1)}, bf16[128,128]{1,0:T(8,128)(2,1)S(1)}, u32[]{:S(2)}, u32[]{:S(2)}) collective-permute-start(bf16[128,128]{1,0:T(8,128)(2,1)S(1)} %get-tuple-element.64.refs_0_), channel_id=1, source_target_pairs={{0,8},{1,13},{2,10},{3,15},{4,12},{5,9},{6,14},{7,11},{8,0},{9,5},... | collective-permute-start | bytes 98312 | tf_op jit(solution)/shard_map/ppermute | solution.py:426
  36.8 4.8 %collective-permute-start.13 = (bf16[128,128]{1,0:T(8,128)(2,1)S(1)}, bf16[128,128]{1,0:T(8,128)(2,1)S(1)}, u32[]{:S(2)}, u32[]{:S(2)}) collective-permute-start(bf16[128,128]{1,0:T(8,128)(2,1)S(1)} %get-tuple-element.64.refs_0_), channel_id=1, source_target_pairs={{0,4},{1,9},{2,6},{3,11},{4,0},{5,13},{6,2},{7,15},{8,12},{9,1},{1... | collective-permute-start | bytes 98312 | tf_op jit(solution)/shard_map/ppermute | solution.py:426
  37.2 5.7 %collective-permute-start.16 = (bf16[128,128]{1,0:T(8,128)(2,1)S(1)}, bf16[128,128]{1,0:T(8,128)(2,1)S(1)}, u32[]{:S(2)}, u32[]{:S(2)}) collective-permute-start(bf16[128,128]{1,0:T(8,128)(2,1)S(1)} %get-tuple-element.64.refs_0_), channel_id=1, source_target_pairs={{0,12},{1,5},{2,14},{3,7},{4,8},{5,1},{6,10},{7,3},{8,4},{9,13},{1... | collective-permute-start | bytes 98312 | tf_op jit(solution)/shard_map/ppermute | solution.py:426
  39.0 6.7 %collective-permute-start.15 = (bf16[128,128]{1,0:T(8,128)(2,1)S(1)}, bf16[128,128]{1,0:T(8,128)(2,1)S(1)}, u32[]{:S(2)}, u32[]{:S(2)}) collective-permute-start(bf16[128,128]{1,0:T(8,128)(2,1)S(1)} %get-tuple-element.64.refs_0_), channel_id=1, source_target_pairs={{0,14},{1,7},{2,12},{3,5},{4,10},{5,3},{6,8},{7,1},{8,6},{9,15},{1... | collective-permute-start | bytes 98312 | tf_op jit(solution)/shard_map/ppermute | solution.py:426
  41.6 5.0 %collective-permute-start.14 = (bf16[384,128]{1,0:T(8,128)(2,1)S(1)}, bf16[384,128]{1,0:T(8,128)(2,1)S(1)}, u32[]{:S(2)}, u32[]{:S(2)}) collective-permute-start(bf16[384,128]{1,0:T(8,128)(2,1)S(1)} %join.3.refs_0_), channel_id=1, source_target_pairs={{0,2},{1,3},{2,0},{3,1},{4,6},{5,7},{6,4},{7,5},{8,10},{9,11},{10,... | collective-permute-start | bytes 294920 | tf_op jit(solution)/shard_map/ppermute | solution.py:426
  47.4 1.4 %collective-permute-start.17 = (f32[256,128]{1,0:T(8,128)S(1)}, f32[256,128]{1,0:T(8,128)S(1)}, u32[]{:S(2)}, u32[]{:S(2)}) collective-permute-start(f32[256,128]{1,0:T(8,128)S(1)} %forward.11), channel_id=1, source_target_pairs={{0,1},{1,0},{2,3},{3,2},{4,5},{5,4},{6,7},{7,6},{8,9},{9,8},{10,11... | collective-permute-start | bytes 393224 | tf_op jit(solution)/shard_map/ppermute | solution.py:426
  48.9 1.3 %collective-permute-start.18 = (bf16[256,128]{1,0:T(8,128)(2,1)S(1)}, bf16[256,128]{1,0:T(8,128)(2,1)S(1)}, u32[]{:S(2)}, u32[]{:S(2)}) collective-permute-start(bf16[256,128]{1,0:T(8,128)(2,1)S(1)} %residual.3.refs_0_), channel_id=1, source_target_pairs={{0,1},{1,0},{2,3},{3,2},{4,5},{5,4},{6,7},{7,6},{8,9},{9,8},{10,11... | collective-permute-start | bytes 196616 | tf_op jit(solution)/shard_map/ppermute | solution.py:426
  50.8 4.9 %collective-permute-start.20 = (bf16[256,128]{1,0:T(8,128)(2,1)S(1)}, bf16[256,128]{1,0:T(8,128)(2,1)S(1)}, u32[]{:S(2)}, u32[]{:S(2)}) collective-permute-start(bf16[256,128]{1,0:T(8,128)(2,1)S(1)} %get-tuple-element.67), channel_id=1, source_target_pairs={{0,2},{1,3},{2,0},{3,1},{4,6},{5,7},{6,4},{7,5},{8,10},{9,11},{10,... | collective-permute-start | bytes 196616 | tf_op jit(solution)/shard_map/ppermute | solution.py:426
  52.3 6.2 %collective-permute-start.19 = (bf16[256,128]{1,0:T(8,128)(2,1)S(1)}, bf16[256,128]{1,0:T(8,128)(2,1)S(1)}, u32[]{:S(2)}, u32[]{:S(2)}) collective-permute-start(bf16[256,128]{1,0:T(8,128)(2,1)S(1)} %get-tuple-element.65), channel_id=1, source_target_pairs={{0,2},{1,3},{2,0},{3,1},{4,6},{5,7},{6,4},{7,5},{8,10},{9,11},{10,... | collective-permute-start | bytes 196616 | tf_op jit(solution)/shard_map/ppermute | solution.py:426
  55.8 5.3 %collective-permute-start.21 = (bf16[128,128]{1,0:T(8,128)(2,1)S(1)}, bf16[128,128]{1,0:T(8,128)(2,1)S(1)}, u32[]{:S(2)}, u32[]{:S(2)}) collective-permute-start(bf16[128,128]{1,0:T(8,128)(2,1)S(1)} %get-tuple-element.68), channel_id=1, source_target_pairs={{0,8},{1,13},{2,10},{3,15},{4,12},{5,9},{6,14},{7,11},{8,0},{9,5},... | collective-permute-start | bytes 98312 | tf_op jit(solution)/shard_map/ppermute | solution.py:426
  56.5 5.8 %collective-permute-start.22 = (bf16[128,128]{1,0:T(8,128)(2,1)S(1)}, bf16[128,128]{1,0:T(8,128)(2,1)S(1)}, u32[]{:S(2)}, u32[]{:S(2)}) collective-permute-start(bf16[128,128]{1,0:T(8,128)(2,1)S(1)} %get-tuple-element.69), channel_id=1, source_target_pairs={{0,12},{1,5},{2,14},{3,7},{4,8},{5,1},{6,10},{7,3},{8,4},{9,13},{1... | collective-permute-start | bytes 98312 | tf_op jit(solution)/shard_map/ppermute | solution.py:426
  58.5 4.1 %collective-permute-start.23 = (bf16[128,128]{1,0:T(8,128)(2,1)S(1)}, bf16[128,128]{1,0:T(8,128)(2,1)S(1)}, u32[]{:S(2)}, u32[]{:S(2)}) collective-permute-start(bf16[128,128]{1,0:T(8,128)(2,1)S(1)} %get-tuple-element.70), channel_id=1, source_target_pairs={{0,4},{1,9},{2,6},{3,11},{4,0},{5,13},{6,2},{7,15},{8,12},{9,1},{1... | collective-permute-start | bytes 98312 | tf_op jit(solution)/shard_map/ppermute | solution.py:426

commit v21 on v19

--- a/solution.py
+++ b/solution.py
@@ -512,9 +512,9 @@
         last = sweep + 1 == ITERS
         if paired:
             over_2, over_1, over_3, across = [
-                exchange(payload, n_slab, distance) for distance in (8, 4, 12, 14)]
+                exchange(payload, n_slab, distance) for distance in (9, 5, 12, 15)]
             z_part = join(payload, over_2, over_1)
-            y_part = exchange(z_part, n_slab, 2)
+            y_part = exchange(z_part, n_slab, 3)
             along_z, along_y = (z_part, over_3), (y_part, across)
             if sweep == 0:
                 (z_list,), z_rows, z_forward, z_backward = setup(along_z, 4, (None,))
@@ -533,17 +533,17 @@
             y_sum = backward(own_list, [residual], 4, y_backward, F32)
             far_sum, near_sum = backward(
                 other_list, [other_residual], 4, y_backward, (BF16, BF16), y_sum, ((1, 3), (0, 2)))
-            far_part, near_part = exchange(far_sum, n_slab, 2), exchange(near_sum, n_slab, 2)
+            far_part, near_part = exchange(far_sum, n_slab, 3), exchange(near_sum, n_slab, 3)
             z_sum = backward(z_list, [residual, other_residual], 4, z_backward, F32)
             piece = shape((rows, extent), BF16)
             piece_2, piece_3 = call(
                 functools.partial(combine_kernel, (1, 3)), "combine", 16, [VMEM] * 2,
                 [piece, piece], z_sum, far_part)
-            got = [exchange(piece_2, n_slab, 8), exchange(piece_3, n_slab, 12)]
+            got = [exchange(piece_2, n_slab, 9), exchange(piece_3, n_slab, 12)]
             own_piece, piece_1 = call(
                 functools.partial(combine_kernel, (0, 2)), "combine", 16, [VMEM] * 2,
                 [shape((rows, extent), F32), piece], z_sum, near_part)
-            pieces = [own_piece, *got, exchange(piece_1, n_slab, 4)]
+            pieces = [own_piece, *got, exchange(piece_1, n_slab, 5)]
         else:
             everyone = lax.all_gather(payload, "slab", axis=0, tiled=True)
             if sweep == 0:

time: 64.2 us -> 63.1 us (0.983)
  no operation moved by 1% of the time
where the time goes in v21:
time: 63.1 us; the launch traced here: 62.9 us
  starting transfers between devices  31.4 us (50%)
  Pallas kernels  17.7 us (28%)
  waiting for transfers between devices  13.5 us (21%)
    ppermute x24, starting transfers between devices, exchange(): lax.ppermute(values, 'slab', [(device, device ^ distance) for device in r...  31.4 us
    pallas_call x26, Pallas kernels, call(): pl.pallas_call(kernel, out_shape=out_shape, in_specs=in_specs, out_specs=...  17.7 us
    ppermute x24, waiting for transfers between devices, exchange(): lax.ppermute(values, 'slab', [(device, device ^ distance) for device in r...  13.5 us
  transfers between devices with their start and end apart: 24, of which 16 were waited for; matrix products, arithmetic and copies ran while one was open for 0% of the time, Pallas kernels for 16%

profile of v21, /device:TPU:0, one launch (start us, length us, event | category | flops | bytes accessed | tf_op | source)
XLA Modules:
  0.0 62.9 jit_solution(5088118504729162197)
XLA Ops:
  0.0 1.0 %pack.1.refs_0_ = bf16[192,128]{1,0:T(8,128)(2,1)S(1)} custom-call(f32[128,128]{1,0:T(8,128)} %bitcast.8, f32[4,256]{1,0:T(4,128)} %bitcast.12, f32[4,256]{1,0:T(4,128)} %bitcast.14, s32[4,256]{1,0:T(4,128)} %bitcast.16, s32[1,256]{1,0:T(1,128)} %bitcast.20, s32[1,16]{1,0:T(1,128)} %bitcast.18), custom_call_target="tpu_custom_call" | custom-call | flops 4000000000 | bytes 8000000 | tf_op jit(solution)/shard_map/pack/pallas_call | solution.py:411
  1.0 3.5 %collective-permute-start = (bf16[192,128]{1,0:T(8,128)(2,1)S(1)}, bf16[192,128]{1,0:T(8,128)(2,1)S(1)}, u32[]{:S(2)}, u32[]{:S(2)}) collective-permute-start(bf16[192,128]{1,0:T(8,128)(2,1)S(1)} %pack.1.refs_0_), channel_id=1, source_target_pairs={{0,9},{1,8},{2,11},{3,10},{4,13},{5,12},{6,15},{7,14},{8,1},{9,0},... | collective-permute-start | bytes 147464 | tf_op jit(solution)/shard_map/ppermute | solution.py:425
  4.6 1.9 %collective-permute-start.1 = (bf16[192,128]{1,0:T(8,128)(2,1)S(1)}, bf16[192,128]{1,0:T(8,128)(2,1)S(1)}, u32[]{:S(2)}, u32[]{:S(2)}) collective-permute-start(bf16[192,128]{1,0:T(8,128)(2,1)S(1)} %pack.1.refs_0_), channel_id=1, source_target_pairs={{0,5},{1,4},{2,7},{3,6},{4,1},{5,0},{6,3},{7,2},{8,13},{9,12},{10,... | collective-permute-start | bytes 147464 | tf_op jit(solution)/shard_map/ppermute | solution.py:425
  6.5 3.9 %collective-permute-start.4 = (bf16[192,128]{1,0:T(8,128)(2,1)S(1)}, bf16[192,128]{1,0:T(8,128)(2,1)S(1)}, u32[]{:S(2)}, u32[]{:S(2)}) collective-permute-start(bf16[192,128]{1,0:T(8,128)(2,1)S(1)} %pack.1.refs_0_), channel_id=1, source_target_pairs={{0,15},{1,14},{2,13},{3,12},{4,11},{5,10},{6,9},{7,8},{8,7},{9,6},... | collective-permute-start | bytes 147464 | tf_op jit(solution)/shard_map/ppermute | solution.py:425
  10.4 1.1 %collective-permute-start.3 = (bf16[576,128]{1,0:T(8,128)(2,1)S(1)}, bf16[576,128]{1,0:T(8,128)(2,1)S(1)}, u32[]{:S(2)}, u32[]{:S(2)}) collective-permute-start(bf16[576,128]{1,0:T(8,128)(2,1)S(1)} %join.2.refs_0_), channel_id=1, source_target_pairs={{0,3},{1,2},{2,1},{3,0},{4,7},{5,6},{6,5},{7,4},{8,11},{9,10},{10,... | collective-permute-start | bytes 442376 | tf_op jit(solution)/shard_map/ppermute | solution.py:425
  11.5 0.9 %collective-permute-done.2.refs_1_ = bf16[192,128]{1,0:T(8,128)(2,1)S(1)} collective-permute-done((bf16[192,128]{1,0:T(8,128)(2,1)S(1)}, bf16[192,128]{1,0:T(8,128)(2,1)S(1)}, u32[]{:S(2)}, u32[]{:S(2)}) %collective-permute-start.2) | collective-permute-done | bytes 49184 | tf_op jit(solution)/shard_map/ppermute | solution.py:425
  12.4 1.5 %setup.2 = (s32[8,128]{1,0:T(8,128)S(4)}, f32[64,128]{1,0:T(8,128)S(1)}, s32[544,128]{1,0:T(8,128)S(1)}, f32[544,128]{1,0:T(8,128)S(1)}, f32[544,128]{1,0:T(8,12...) custom-call(bf16[576,128]{1,0:T(8,128)(2,1)S(1)} %join.2.refs_0_, ...), custom_call_target="tpu_custom_call" | custom-call | flops 4000000000 | bytes 8000000 | tf_op jit(solution)/shard_map/setup/pallas_call | solution.py:411
  13.9 1.5 %forward.6.refs_2_.refs_6_ = f32[512,128]{1,0:T(8,128)S(1)} custom-call(s32[8,128]{1,0:T(8,128)S(4)} %get-tuple-element.38.slots, bf16[576,128]{1,0:T(8,128)(2,1)S(1)} %join.2.refs_0_, bf16[192,128]{1,0:T(8,128)(2,1)S(1)} %collective-permute-done.2.refs_1_, s32[544,128]{1,0:T(8,128)S(1)} %get-tuple-element.39.refs_2_, ...), custom_call_target="tpu_custom_call" | custom-call | flops 4000000000 | bytes 8000000 | tf_op jit(solution)/shard_map/forward/pallas_call | solution.py:411
  16.2 1.6 %setup.3 = (s32[8,128]{1,0:T(8,128)S(4)}, s32[8,128]{1,0:T(8,128)S(4)}, f32[64,128]{1,0:T(8,128)S(1)}, s32[544,128]{1,0:T(8,128)S(1)}, f32[544,128]{1,0:T(8,128)...) custom-call(bf16[576,128]{1,0:T(8,128)(2,1)S(1)} %collective-permute, ...), custom_call_target="tpu_custom_call" | custom-call | flops 4000000000 | bytes 8000000 | tf_op jit(solution)/shard_map/setup/pallas_call | solution.py:411
  17.8 1.1 %forward.8 = f32[288,128]{1,0:T(8,128)S(1)} custom-call(s32[8,128]{1,0:T(8,128)S(4)} %get-tuple-element.50.slots, bf16[576,128]{1,0:T(8,128)(2,1)S(1)} %collective-permute-done.3.refs_0_, bf16[192,128]{1,0:T(8,128)(2,1)S(1)} %collective-permute-done.4.refs_1_, s32[544,128]{1,0:T(8,128)S(1)} %get-tuple-element.44.refs_2_, ...), custom_call_target="tpu_custom_call" | custom-call | flops 4000000000 | bytes 8000000 | tf_op jit(solution)/shard_map/forward/pallas_call | solution.py:411
  22.0 0.9 %backward.8 = (bf16[256,128]{1,0:T(8,128)(2,1)S(1)}, bf16[256,128]{1,0:T(8,128)(2,1)S(1)}) custom-call(s32[8,128]{1,0:T(8,128)S(4)} %get-tuple-element.50.slots, bf16[256,128]{1,0:T(8,128)(2,1)S(1)} %collective-permute-done.6.refs_1_.refs_0_, s32[544,128]{1,0:T(8,128)S(1)} %get-tuple-element.54.refs_1_, f32[544,128]{1,0:T(8,128)S(1)} %get-tuple-element.55.refs_2_, ...), custom_call_target="tpu_custom_call" | custom-call | flops 4000000000 | bytes 8000000 | tf_op jit(solution)/shard_map/backward/pallas_call | solution.py:411
  23.7 1.0 %collective-permute-start.7 = (bf16[256,128]{1,0:T(8,128)(2,1)S(1)}, bf16[256,128]{1,0:T(8,128)(2,1)S(1)}, u32[]{:S(2)}, u32[]{:S(2)}) collective-permute-start(bf16[256,128]{1,0:T(8,128)(2,1)S(1)} %get-tuple-element.57), channel_id=1, source_target_pairs={{0,3},{1,2},{2,1},{3,0},{4,7},{5,6},{6,5},{7,4},{8,11},{9,10},{10,... | collective-permute-start | bytes 196616 | tf_op jit(solution)/shard_map/ppermute | solution.py:425
  24.7 1.2 %backward.6.sum_ref = f32[512,128]{1,0:T(8,128)S(1)} custom-call(s32[8,128]{1,0:T(8,128)S(4)} %get-tuple-element.38.slots, bf16[256,128]{1,0:T(8,128)(2,1)S(1)} %residual.2.refs_0_, bf16[256,128]{1,0:T(8,128)(2,1)S(1)} %collective-permute-done.6.refs_1_.refs_0_, s32[544,128]{1,0:T(8,128)S(1)} %get-tuple-element.51.refs_2_, ...), custom_call_target="tpu_custom_call" | custom-call | flops 4000000000 | bytes 8000000 | tf_op jit(solution)/shard_map/backward/pallas_call | solution.py:411
  25.9 1.0 %collective-permute-done.8.y_ref = bf16[256,128]{1,0:T(8,128)(2,1)S(1)} collective-permute-done((bf16[256,128]{1,0:T(8,128)(2,1)S(1)}, bf16[256,128]{1,0:T(8,128)(2,1)S(1)}, u32[]{:S(2)}, u32[]{:S(2)}) %collective-permute-start.8) | collective-permute-done | bytes 65568 | tf_op jit(solution)/shard_map/ppermute | solution.py:425
  26.9 2.9 %collective-permute-start.10 = (bf16[128,128]{1,0:T(8,128)(2,1)S(1)}, bf16[128,128]{1,0:T(8,128)(2,1)S(1)}, u32[]{:S(2)}, u32[]{:S(2)}) collective-permute-start(bf16[128,128]{1,0:T(8,128)(2,1)S(1)} %get-tuple-element.61), channel_id=1, source_target_pairs={{0,12},{1,13},{2,14},{3,15},{4,8},{5,9},{6,10},{7,11},{8,4},{9,5},... | collective-permute-start | bytes 98312 | tf_op jit(solution)/shard_map/ppermute | solution.py:425
  29.9 1.4 %collective-permute-start.11 = (bf16[128,128]{1,0:T(8,128)(2,1)S(1)}, bf16[128,128]{1,0:T(8,128)(2,1)S(1)}, u32[]{:S(2)}, u32[]{:S(2)}) collective-permute-start(bf16[128,128]{1,0:T(8,128)(2,1)S(1)} %get-tuple-element.62), channel_id=1, source_target_pairs={{0,5},{1,4},{2,7},{3,6},{4,1},{5,0},{6,3},{7,2},{8,13},{9,12},{10,... | collective-permute-start | bytes 98312 | tf_op jit(solution)/shard_map/ppermute | solution.py:425
  31.9 1.2 %collective-permute-done.10.refs_2_ = bf16[128,128]{1,0:T(8,128)(2,1)S(1)} collective-permute-done((bf16[128,128]{1,0:T(8,128)(2,1)S(1)}, bf16[128,128]{1,0:T(8,128)(2,1)S(1)}, u32[]{:S(2)}, u32[]{:S(2)}) %collective-permute-start.10) | collective-permute-done | bytes 32800 | tf_op jit(solution)/shard_map/ppermute | solution.py:425
  33.0 1.3 %collective-permute-done.9.refs_1_ = bf16[128,128]{1,0:T(8,128)(2,1)S(1)} collective-permute-done((bf16[128,128]{1,0:T(8,128)(2,1)S(1)}, bf16[128,128]{1,0:T(8,128)(2,1)S(1)}, u32[]{:S(2)}, u32[]{:S(2)}) %collective-permute-start.9) | collective-permute-done | bytes 32800 | tf_op jit(solution)/shard_map/ppermute | solution.py:425
  34.4 1.6 %collective-permute-start.12 = (bf16[128,128]{1,0:T(8,128)(2,1)S(1)}, bf16[128,128]{1,0:T(8,128)(2,1)S(1)}, u32[]{:S(2)}, u32[]{:S(2)}) collective-permute-start(bf16[128,128]{1,0:T(8,128)(2,1)S(1)} %get-tuple-element.64.refs_0_), channel_id=1, source_target_pairs={{0,9},{1,8},{2,11},{3,10},{4,13},{5,12},{6,15},{7,14},{8,1},{9,0},... | collective-permute-start | bytes 98312 | tf_op jit(solution)/shard_map/ppermute | solution.py:425
  36.0 1.2 %collective-permute-start.13 = (bf16[128,128]{1,0:T(8,128)(2,1)S(1)}, bf16[128,128]{1,0:T(8,128)(2,1)S(1)}, u32[]{:S(2)}, u32[]{:S(2)}) collective-permute-start(bf16[128,128]{1,0:T(8,128)(2,1)S(1)} %get-tuple-element.64.refs_0_), channel_id=1, source_target_pairs={{0,5},{1,4},{2,7},{3,6},{4,1},{5,0},{6,3},{7,2},{8,13},{9,12},{10,... | collective-permute-start | bytes 98312 | tf_op jit(solution)/shard_map/ppermute | solution.py:425
  37.2 1.4 %collective-permute-start.16 = (bf16[128,128]{1,0:T(8,128)(2,1)S(1)}, bf16[128,128]{1,0:T(8,128)(2,1)S(1)}, u32[]{:S(2)}, u32[]{:S(2)}) collective-permute-start(bf16[128,128]{1,0:T(8,128)(2,1)S(1)} %get-tuple-element.64.refs_0_), channel_id=1, source_target_pairs={{0,12},{1,13},{2,14},{3,15},{4,8},{5,9},{6,10},{7,11},{8,4},{9,5},... | collective-permute-start | bytes 98312 | tf_op jit(solution)/shard_map/ppermute | solution.py:425
  38.6 3.2 %collective-permute-start.15 = (bf16[128,128]{1,0:T(8,128)(2,1)S(1)}, bf16[128,128]{1,0:T(8,128)(2,1)S(1)}, u32[]{:S(2)}, u32[]{:S(2)}) collective-permute-start(bf16[128,128]{1,0:T(8,128)(2,1)S(1)} %get-tuple-element.64.refs_0_), channel_id=1, source_target_pairs={{0,15},{1,14},{2,13},{3,12},{4,11},{5,10},{6,9},{7,8},{8,7},{9,6},... | collective-permute-start | bytes 98312 | tf_op jit(solution)/shard_map/ppermute | solution.py:425
  43.0 1.5 %forward.9.refs_6_ = f32[512,128]{1,0:T(8,128)S(1)} custom-call(s32[8,128]{1,0:T(8,128)S(4)} %get-tuple-element.38.slots, bf16[384,128]{1,0:T(8,128)(2,1)S(1)} %join.3.refs_0_, bf16[128,128]{1,0:T(8,128)(2,1)S(1)} %collective-permute-done.16.refs_1_, s32[544,128]{1,0:T(8,128)S(1)} %get-tuple-element.39.refs_2_, f32[544,128]{1,0:T(8,128)S(1)} %get-tuple-element.40.refs_3_, ...), custom_call_target="tpu_custom_call" | custom-call | flops 4000000000 | bytes 8000000 | tf_op jit(solution)/shard_map/forward/pallas_call | solution.py:411
  45.0 1.3 %collective-permute-done.14.refs_0_ = bf16[384,128]{1,0:T(8,128)(2,1)S(1)} collective-permute-done((bf16[384,128]{1,0:T(8,128)(2,1)S(1)}, bf16[384,128]{1,0:T(8,128)(2,1)S(1)}, u32[]{:S(2)}, u32[]{:S(2)}) %collective-permute-start.14) | collective-permute-done | bytes 98336 | tf_op jit(solution)/shard_map/ppermute | solution.py:425
  46.3 1.1 %forward.11 = f32[256,128]{1,0:T(8,128)S(1)} custom-call(s32[8,128]{1,0:T(8,128)S(4)} %get-tuple-element.50.slots, bf16[384,128]{1,0:T(8,128)(2,1)S(1)} %collective-permute-done.14.refs_0_, bf16[128,128]{1,0:T(8,128)(2,1)S(1)} %collective-permute-done.15.refs_1_, s32[544,128]{1,0:T(8,128)S(1)} %get-tuple-element.44.refs_2_, ...), custom_call_target="tpu_custom_call" | custom-call | flops 4000000000 | bytes 8000000 | tf_op jit(solution)/shard_map/forward/pallas_call | solution.py:411
  50.4 0.9 %backward.11 = (bf16[256,128]{1,0:T(8,128)(2,1)S(1)}, bf16[256,128]{1,0:T(8,128)(2,1)S(1)}) custom-call(s32[8,128]{1,0:T(8,128)S(4)} %get-tuple-element.50.slots, bf16[256,128]{1,0:T(8,128)(2,1)S(1)} %collective-permute-done.18.refs_1_.refs_0_, s32[544,128]{1,0:T(8,128)S(1)} %get-tuple-element.54.refs_1_, f32[544,128]{1,0:T(8,128)S(1)} %get-tuple-element.55.refs_2_, ...), custom_call_target="tpu_custom_call" | custom-call | flops 4000000000 | bytes 8000000 | tf_op jit(solution)/shard_map/backward/pallas_call | solution.py:411
  52.0 1.1 %collective-permute-start.19 = (bf16[256,128]{1,0:T(8,128)(2,1)S(1)}, bf16[256,128]{1,0:T(8,128)(2,1)S(1)}, u32[]{:S(2)}, u32[]{:S(2)}) collective-permute-start(bf16[256,128]{1,0:T(8,128)(2,1)S(1)} %get-tuple-element.65), channel_id=1, source_target_pairs={{0,3},{1,2},{2,1},{3,0},{4,7},{5,6},{6,5},{7,4},{8,11},{9,10},{10,... | collective-permute-start | bytes 196616 | tf_op jit(solution)/shard_map/ppermute | solution.py:425
  53.1 1.2 %backward.9.sum_ref = f32[512,128]{1,0:T(8,128)S(1)} custom-call(s32[8,128]{1,0:T(8,128)S(4)} %get-tuple-element.38.slots, bf16[256,128]{1,0:T(8,128)(2,1)S(1)} %residual.3.refs_0_, bf16[256,128]{1,0:T(8,128)(2,1)S(1)} %collective-permute-done.18.refs_1_.refs_0_, s32[544,128]{1,0:T(8,128)S(1)} %get-tuple-element.51.refs_2_, ...), custom_call_target="tpu_custom_call" | custom-call | flops 4000000000 | bytes 8000000 | tf_op jit(solution)/shard_map/backward/pallas_call | solution.py:411
  54.3 1.0 %collective-permute-done.20.y_ref = bf16[256,128]{1,0:T(8,128)(2,1)S(1)} collective-permute-done((bf16[256,128]{1,0:T(8,128)(2,1)S(1)}, bf16[256,128]{1,0:T(8,128)(2,1)S(1)}, u32[]{:S(2)}, u32[]{:S(2)}) %collective-permute-start.20) | collective-permute-done | bytes 65568 | tf_op jit(solution)/shard_map/ppermute | solution.py:425
  56.0 2.0 %collective-permute-start.22 = (bf16[128,128]{1,0:T(8,128)(2,1)S(1)}, bf16[128,128]{1,0:T(8,128)(2,1)S(1)}, u32[]{:S(2)}, u32[]{:S(2)}) collective-permute-start(bf16[128,128]{1,0:T(8,128)(2,1)S(1)} %get-tuple-element.69), channel_id=1, source_target_pairs={{0,12},{1,13},{2,14},{3,15},{4,8},{5,9},{6,10},{7,11},{8,4},{9,5},... | collective-permute-start | bytes 98312 | tf_op jit(solution)/shard_map/ppermute | solution.py:425
  58.4 1.2 %collective-permute-done.21.refs_1_ = bf16[128,128]{1,0:T(8,128)(2,1)S(1)} collective-permute-done((bf16[128,128]{1,0:T(8,128)(2,1)S(1)}, bf16[128,128]{1,0:T(8,128)(2,1)S(1)}, u32[]{:S(2)}, u32[]{:S(2)}) %collective-permute-start.21) | collective-permute-done | bytes 32800 | tf_op jit(solution)/shard_map/ppermute | solution.py:425
  59.6 2.1 %collective-permute-done.22.refs_2_ = bf16[128,128]{1,0:T(8,128)(2,1)S(1)} collective-permute-done((bf16[128,128]{1,0:T(8,128)(2,1)S(1)}, bf16[128,128]{1,0:T(8,128)(2,1)S(1)}, u32[]{:S(2)}, u32[]{:S(2)}) %collective-permute-start.22) | collective-permute-done | bytes 32800 | tf_op jit(solution)/shard_map/ppermute | solution.py:425
  (54 shorter events, 13.0 us)
Async XLA Ops:
  1.0 9.3 %collective-permute-start = (bf16[192,128]{1,0:T(8,128)(2,1)S(1)}, bf16[192,128]{1,0:T(8,128)(2,1)S(1)}, u32[]{:S(2)}, u32[]{:S(2)}) collective-permute-start(bf16[192,128]{1,0:T(8,128)(2,1)S(1)} %pack.1.refs_0_), channel_id=1, source_target_pairs={{0,9},{1,8},{2,11},{3,10},{4,13},{5,12},{6,15},{7,14},{8,1},{9,0},... | collective-permute-start | bytes 147464 | tf_op jit(solution)/shard_map/ppermute | solution.py:425
  4.6 5.8 %collective-permute-start.1 = (bf16[192,128]{1,0:T(8,128)(2,1)S(1)}, bf16[192,128]{1,0:T(8,128)(2,1)S(1)}, u32[]{:S(2)}, u32[]{:S(2)}) collective-permute-start(bf16[192,128]{1,0:T(8,128)(2,1)S(1)} %pack.1.refs_0_), channel_id=1, source_target_pairs={{0,5},{1,4},{2,7},{3,6},{4,1},{5,0},{6,3},{7,2},{8,13},{9,12},{10,... | collective-permute-start | bytes 147464 | tf_op jit(solution)/shard_map/ppermute | solution.py:425
  6.4 6.0 %collective-permute-start.2 = (bf16[192,128]{1,0:T(8,128)(2,1)S(1)}, bf16[192,128]{1,0:T(8,128)(2,1)S(1)}, u32[]{:S(2)}, u32[]{:S(2)}) collective-permute-start(bf16[192,128]{1,0:T(8,128)(2,1)S(1)} %pack.1.refs_0_), channel_id=1, source_target_pairs={{0,12},{1,13},{2,14},{3,15},{4,8},{5,9},{6,10},{7,11},{8,4},{9,5},... | collective-permute-start | bytes 147464 | tf_op jit(solution)/shard_map/ppermute | solution.py:425
  6.5 9.0 %collective-permute-start.4 = (bf16[192,128]{1,0:T(8,128)(2,1)S(1)}, bf16[192,128]{1,0:T(8,128)(2,1)S(1)}, u32[]{:S(2)}, u32[]{:S(2)}) collective-permute-start(bf16[192,128]{1,0:T(8,128)(2,1)S(1)} %pack.1.refs_0_), channel_id=1, source_target_pairs={{0,15},{1,14},{2,13},{3,12},{4,11},{5,10},{6,9},{7,8},{8,7},{9,6},... | collective-permute-start | bytes 147464 | tf_op jit(solution)/shard_map/ppermute | solution.py:425
  10.4 5.8 %collective-permute-start.3 = (bf16[576,128]{1,0:T(8,128)(2,1)S(1)}, bf16[576,128]{1,0:T(8,128)(2,1)S(1)}, u32[]{:S(2)}, u32[]{:S(2)}) collective-permute-start(bf16[576,128]{1,0:T(8,128)(2,1)S(1)} %join.2.refs_0_), channel_id=1, source_target_pairs={{0,3},{1,2},{2,1},{3,0},{4,7},{5,6},{6,5},{7,4},{8,11},{9,10},{10,... | collective-permute-start | bytes 442376 | tf_op jit(solution)/shard_map/ppermute | solution.py:425
  18.9 1.7 %collective-permute-start.5 = (f32[288,128]{1,0:T(8,128)S(1)}, f32[288,128]{1,0:T(8,128)S(1)}, u32[]{:S(2)}, u32[]{:S(2)}) collective-permute-start(f32[288,128]{1,0:T(8,128)S(1)} %forward.8), channel_id=1, source_target_pairs={{0,1},{1,0},{2,3},{3,2},{4,5},{5,4},{6,7},{7,6},{8,9},{9,8},{10,11... | collective-permute-start | bytes 442376 | tf_op jit(solution)/shard_map/ppermute | solution.py:425
  19.6 1.0 %copy-start.1 = (bf16[32,8,128]{2,1,0:T(8,128)(2,1)S(1)}, bf16[32,8,128]{2,1,0:T(8,128)(2,1)}, u32[]{:S(2)}) copy-start(bf16[32,8,128]{2,1,0:T(8,128)(2,1)} %param.7) | copy-start | bytes 196612
  20.6 1.3 %collective-permute-start.6 = (bf16[256,128]{1,0:T(8,128)(2,1)S(1)}, bf16[256,128]{1,0:T(8,128)(2,1)S(1)}, u32[]{:S(2)}, u32[]{:S(2)}) collective-permute-start(bf16[256,128]{1,0:T(8,128)(2,1)S(1)} %residual.2.refs_0_), channel_id=1, source_target_pairs={{0,1},{1,0},{2,3},{3,2},{4,5},{5,4},{6,7},{7,6},{8,9},{9,8},{10,11... | collective-permute-start | bytes 196616 | tf_op jit(solution)/shard_map/ppermute | solution.py:425
  22.9 4.0 %collective-permute-start.8 = (bf16[256,128]{1,0:T(8,128)(2,1)S(1)}, bf16[256,128]{1,0:T(8,128)(2,1)S(1)}, u32[]{:S(2)}, u32[]{:S(2)}) collective-permute-start(bf16[256,128]{1,0:T(8,128)(2,1)S(1)} %get-tuple-element.59), channel_id=1, source_target_pairs={{0,3},{1,2},{2,1},{3,0},{4,7},{5,6},{6,5},{7,4},{8,11},{9,10},{10,... | collective-permute-start | bytes 196616 | tf_op jit(solution)/shard_map/ppermute | solution.py:425
  23.7 6.1 %collective-permute-start.7 = (bf16[256,128]{1,0:T(8,128)(2,1)S(1)}, bf16[256,128]{1,0:T(8,128)(2,1)S(1)}, u32[]{:S(2)}, u32[]{:S(2)}) collective-permute-start(bf16[256,128]{1,0:T(8,128)(2,1)S(1)} %get-tuple-element.57), channel_id=1, source_target_pairs={{0,3},{1,2},{2,1},{3,0},{4,7},{5,6},{6,5},{7,4},{8,11},{9,10},{10,... | collective-permute-start | bytes 196616 | tf_op jit(solution)/shard_map/ppermute | solution.py:425
  26.9 6.1 %collective-permute-start.10 = (bf16[128,128]{1,0:T(8,128)(2,1)S(1)}, bf16[128,128]{1,0:T(8,128)(2,1)S(1)}, u32[]{:S(2)}, u32[]{:S(2)}) collective-permute-start(bf16[128,128]{1,0:T(8,128)(2,1)S(1)} %get-tuple-element.61), channel_id=1, source_target_pairs={{0,12},{1,13},{2,14},{3,15},{4,8},{5,9},{6,10},{7,11},{8,4},{9,5},... | collective-permute-start | bytes 98312 | tf_op jit(solution)/shard_map/ppermute | solution.py:425
  29.8 1.4 %copy-start.2 = (f32[256,4]{0,1:T(4,128)S(1)}, f32[256,4]{0,1:T(4,128)}, u32[]{:S(2)}) copy-start(f32[256,4]{0,1:T(4,128)} %param.13) | copy-start | bytes 12292
  29.8 1.4 %copy-start.3 = (f32[256,4]{0,1:T(4,128)S(1)}, f32[256,4]{0,1:T(4,128)}, u32[]{:S(2)}) copy-start(f32[256,4]{0,1:T(4,128)} %param.12) | copy-start | bytes 12292
  29.8 1.4 %copy-start.4 = (s32[256,4]{0,1:T(4,128)S(1)}, s32[256,4]{0,1:T(4,128)}, u32[]{:S(2)}) copy-start(s32[256,4]{0,1:T(4,128)} %param.9) | copy-start | bytes 12292
  29.8 4.5 %collective-permute-start.9 = (bf16[128,128]{1,0:T(8,128)(2,1)S(1)}, bf16[128,128]{1,0:T(8,128)(2,1)S(1)}, u32[]{:S(2)}, u32[]{:S(2)}) collective-permute-start(bf16[128,128]{1,0:T(8,128)(2,1)S(1)} %get-tuple-element.60), channel_id=1, source_target_pairs={{0,9},{1,8},{2,11},{3,10},{4,13},{5,12},{6,15},{7,14},{8,1},{9,0},... | collective-permute-start | bytes 98312 | tf_op jit(solution)/shard_map/ppermute | solution.py:425
  29.8 1.4 %copy-start.5 = (s32[16]{0:T(128)S(1)}, s32[16]{0:T(128)}, u32[]{:S(2)}) copy-start(s32[16]{0:T(128)} %param.11) | copy-start | bytes 196
  29.8 4.5 %copy-start = (f32[16,8,128]{2,1,0:T(8,128)S(1)}, f32[16,8,128]{2,1,0:T(8,128)}, u32[]{:S(2)}) copy-start(f32[16,8,128]{2,1,0:T(8,128)} %param.8) | copy-start | bytes 196612
  29.9 4.5 %collective-permute-start.11 = (bf16[128,128]{1,0:T(8,128)(2,1)S(1)}, bf16[128,128]{1,0:T(8,128)(2,1)S(1)}, u32[]{:S(2)}, u32[]{:S(2)}) collective-permute-start(bf16[128,128]{1,0:T(8,128)(2,1)S(1)} %get-tuple-element.62), channel_id=1, source_target_pairs={{0,5},{1,4},{2,7},{3,6},{4,1},{5,0},{6,3},{7,2},{8,13},{9,12},{10,... | collective-permute-start | bytes 98312 | tf_op jit(solution)/shard_map/ppermute | solution.py:425
  34.4 7.4 %collective-permute-start.12 = (bf16[128,128]{1,0:T(8,128)(2,1)S(1)}, bf16[128,128]{1,0:T(8,128)(2,1)S(1)}, u32[]{:S(2)}, u32[]{:S(2)}) collective-permute-start(bf16[128,128]{1,0:T(8,128)(2,1)S(1)} %get-tuple-element.64.refs_0_), channel_id=1, source_target_pairs={{0,9},{1,8},{2,11},{3,10},{4,13},{5,12},{6,15},{7,14},{8,1},{9,0},... | collective-permute-start | bytes 98312 | tf_op jit(solution)/shard_map/ppermute | solution.py:425
  36.0 5.8 %collective-permute-start.13 = (bf16[128,128]{1,0:T(8,128)(2,1)S(1)}, bf16[128,128]{1,0:T(8,128)(2,1)S(1)}, u32[]{:S(2)}, u32[]{:S(2)}) collective-permute-start(bf16[128,128]{1,0:T(8,128)(2,1)S(1)} %get-tuple-element.64.refs_0_), channel_id=1, source_target_pairs={{0,5},{1,4},{2,7},{3,6},{4,1},{5,0},{6,3},{7,2},{8,13},{9,12},{10,... | collective-permute-start | bytes 98312 | tf_op jit(solution)/shard_map/ppermute | solution.py:425
  37.2 5.8 %collective-permute-start.16 = (bf16[128,128]{1,0:T(8,128)(2,1)S(1)}, bf16[128,128]{1,0:T(8,128)(2,1)S(1)}, u32[]{:S(2)}, u32[]{:S(2)}) collective-permute-start(bf16[128,128]{1,0:T(8,128)(2,1)S(1)} %get-tuple-element.64.refs_0_), channel_id=1, source_target_pairs={{0,12},{1,13},{2,14},{3,15},{4,8},{5,9},{6,10},{7,11},{8,4},{9,5},... | collective-permute-start | bytes 98312 | tf_op jit(solution)/shard_map/ppermute | solution.py:425
  38.6 6.4 %collective-permute-start.15 = (bf16[128,128]{1,0:T(8,128)(2,1)S(1)}, bf16[128,128]{1,0:T(8,128)(2,1)S(1)}, u32[]{:S(2)}, u32[]{:S(2)}) collective-permute-start(bf16[128,128]{1,0:T(8,128)(2,1)S(1)} %get-tuple-element.64.refs_0_), channel_id=1, source_target_pairs={{0,15},{1,14},{2,13},{3,12},{4,11},{5,10},{6,9},{7,8},{8,7},{9,6},... | collective-permute-start | bytes 98312 | tf_op jit(solution)/shard_map/ppermute | solution.py:425
  41.8 4.5 %collective-permute-start.14 = (bf16[384,128]{1,0:T(8,128)(2,1)S(1)}, bf16[384,128]{1,0:T(8,128)(2,1)S(1)}, u32[]{:S(2)}, u32[]{:S(2)}) collective-permute-start(bf16[384,128]{1,0:T(8,128)(2,1)S(1)} %join.3.refs_0_), channel_id=1, source_target_pairs={{0,3},{1,2},{2,1},{3,0},{4,7},{5,6},{6,5},{7,4},{8,11},{9,10},{10,... | collective-permute-start | bytes 294920 | tf_op jit(solution)/shard_map/ppermute | solution.py:425
  47.4 1.6 %collective-permute-start.17 = (f32[256,128]{1,0:T(8,128)S(1)}, f32[256,128]{1,0:T(8,128)S(1)}, u32[]{:S(2)}, u32[]{:S(2)}) collective-permute-start(f32[256,128]{1,0:T(8,128)S(1)} %forward.11), channel_id=1, source_target_pairs={{0,1},{1,0},{2,3},{3,2},{4,5},{5,4},{6,7},{7,6},{8,9},{9,8},{10,11... | collective-permute-start | bytes 393224 | tf_op jit(solution)/shard_map/ppermute | solution.py:425
  49.1 1.3 %collective-permute-start.18 = (bf16[256,128]{1,0:T(8,128)(2,1)S(1)}, bf16[256,128]{1,0:T(8,128)(2,1)S(1)}, u32[]{:S(2)}, u32[]{:S(2)}) collective-permute-start(bf16[256,128]{1,0:T(8,128)(2,1)S(1)} %residual.3.refs_0_), channel_id=1, source_target_pairs={{0,1},{1,0},{2,3},{3,2},{4,5},{5,4},{6,7},{7,6},{8,9},{9,8},{10,11... | collective-permute-start | bytes 196616 | tf_op jit(solution)/shard_map/ppermute | solution.py:425
  51.3 4.0 %collective-permute-start.20 = (bf16[256,128]{1,0:T(8,128)(2,1)S(1)}, bf16[256,128]{1,0:T(8,128)(2,1)S(1)}, u32[]{:S(2)}, u32[]{:S(2)}) collective-permute-start(bf16[256,128]{1,0:T(8,128)(2,1)S(1)} %get-tuple-element.67), channel_id=1, source_target_pairs={{0,3},{1,2},{2,1},{3,0},{4,7},{5,6},{6,5},{7,4},{8,11},{9,10},{10,... | collective-permute-start | bytes 196616 | tf_op jit(solution)/shard_map/ppermute | solution.py:425
  52.0 6.0 %collective-permute-start.19 = (bf16[256,128]{1,0:T(8,128)(2,1)S(1)}, bf16[256,128]{1,0:T(8,128)(2,1)S(1)}, u32[]{:S(2)}, u32[]{:S(2)}) collective-permute-start(bf16[256,128]{1,0:T(8,128)(2,1)S(1)} %get-tuple-element.65), channel_id=1, source_target_pairs={{0,3},{1,2},{2,1},{3,0},{4,7},{5,6},{6,5},{7,4},{8,11},{9,10},{10,... | collective-permute-start | bytes 196616 | tf_op jit(solution)/shard_map/ppermute | solution.py:425
  55.3 4.3 %collective-permute-start.21 = (bf16[128,128]{1,0:T(8,128)(2,1)S(1)}, bf16[128,128]{1,0:T(8,128)(2,1)S(1)}, u32[]{:S(2)}, u32[]{:S(2)}) collective-permute-start(bf16[128,128]{1,0:T(8,128)(2,1)S(1)} %get-tuple-element.68), channel_id=1, source_target_pairs={{0,9},{1,8},{2,11},{3,10},{4,13},{5,12},{6,15},{7,14},{8,1},{9,0},... | collective-permute-start | bytes 98312 | tf_op jit(solution)/shard_map/ppermute | solution.py:425
  56.0 5.8 %collective-permute-start.22 = (bf16[128,128]{1,0:T(8,128)(2,1)S(1)}, bf16[128,128]{1,0:T(8,128)(2,1)S(1)}, u32[]{:S(2)}, u32[]{:S(2)}) collective-permute-start(bf16[128,128]{1,0:T(8,128)(2,1)S(1)} %get-tuple-element.69), channel_id=1, source_target_pairs={{0,12},{1,13},{2,14},{3,15},{4,8},{5,9},{6,10},{7,11},{8,4},{9,5},... | collective-permute-start | bytes 98312 | tf_op jit(solution)/shard_map/ppermute | solution.py:425
  58.0 4.3 %collective-permute-start.23 = (bf16[128,128]{1,0:T(8,128)(2,1)S(1)}, bf16[128,128]{1,0:T(8,128)(2,1)S(1)}, u32[]{:S(2)}, u32[]{:S(2)}) collective-permute-start(bf16[128,128]{1,0:T(8,128)(2,1)S(1)} %get-tuple-element.70), channel_id=1, source_target_pairs={{0,5},{1,4},{2,7},{3,6},{4,1},{5,0},{6,3},{7,2},{8,13},{9,12},{10,... | collective-permute-start | bytes 98312 | tf_op jit(solution)/shard_map/ppermute | solution.py:425

commit v22 on v20

--- a/solution.py
+++ b/solution.py
@@ -421,10 +421,11 @@
     )(*operands)
 
 
-def exchange(values, n_slab, distance, odd_distance=None):
-    far = (distance, distance if odd_distance is None else odd_distance)
+def exchange(values, n_slab, distance, other_distance=None):
+    far = (distance, distance if other_distance is None else other_distance)
     return lax.ppermute(
-        values, "slab", [(device, device ^ far[device % 2]) for device in range(n_slab)])
+        values, "slab",
+        [(device, device ^ far[device.bit_count() % 2]) for device in range(n_slab)])
 
 
 def shards(sinogram, start_volume, slot_voxel, slot_ray, live_count, block_slope, block_offset):
@@ -513,9 +514,9 @@
         last = sweep + 1 == ITERS
         if paired:
             place_1, place_2, place_3, across = [
-                exchange(payload, n_slab, *pair) for pair in ((8, 12), (4, 8), (12, 4), (14, 6))]
+                exchange(payload, n_slab, *pair) for pair in ((9, 5), (5, 9), (12, 12), (15, 15))]
             z_part = join(payload, place_1, place_2)
-            y_part = exchange(z_part, n_slab, 2)
+            y_part = exchange(z_part, n_slab, 3)
             along_z, along_y = (z_part, place_3), (y_part, across)
             if sweep == 0:
                 (z_list,), z_rows, z_forward, z_backward = setup(along_z, 4, (None,))
@@ -534,17 +535,17 @@
             y_sum = backward(own_list, [residual], 4, y_backward, F32)
             far_sum, near_sum = backward(
                 other_list, [other_residual], 4, y_backward, (BF16, BF16), y_sum, ((1, 3), (0, 2)))
-            far_part, near_part = exchange(far_sum, n_slab, 2), exchange(near_sum, n_slab, 2)
+            far_part, near_part = exchange(far_sum, n_slab, 3), exchange(near_sum, n_slab, 3)
             z_sum = backward(z_list, [residual, other_residual], 4, z_backward, F32)
             piece = shape((rows, extent), BF16)
             piece_1, piece_3 = call(
                 functools.partial(combine_kernel, (1, 3)), "combine", 16, [VMEM] * 2,
                 [piece, piece], z_sum, far_part)
-            got = [exchange(piece_1, n_slab, 8, 12), exchange(piece_3, n_slab, 12, 4)]
+            got = [exchange(piece_1, n_slab, 9, 5), exchange(piece_3, n_slab, 12)]
             own_piece, piece_2 = call(
                 functools.partial(combine_kernel, (0, 2)), "combine", 16, [VMEM] * 2,
                 [shape((rows, extent), F32), piece], z_sum, near_part)
-            pieces = [own_piece, *got, exchange(piece_2, n_slab, 4, 8)]
+            pieces = [own_piece, *got, exchange(piece_2, n_slab, 5, 9)]
         else:
             everyone = lax.all_gather(payload, "slab", axis=0, tiled=True)
             if sweep == 0:

time: 63.2 us -> 62.5 us (0.989)
  waiting for transfers between devices: 14.4 us -> 10.3 us
  Pallas kernels: 16.5 us -> 18.9 us
  starting transfers between devices: 32 us -> 32.9 us
    ppermute x24, waiting for transfers between devices: 14.4 us -> 10.3 us  [exchange(): lax.ppermute(values, 'slab', [(device, device ^ far[device.bit_count() %...]
    pallas_call x26, Pallas kernels: 16.5 us -> 18.9 us  [call(): pl.pallas_call(kernel, out_shape=out_shape, in_specs=in_specs, out_specs=...]
    ppermute x24, starting transfers between devices: 32 us -> 32.9 us  [exchange(): lax.ppermute(values, 'slab', [(device, device ^ far[device.bit_count() %...]
  transfers between devices with their start and end apart: 24 -> 24, of which waited for: 16 -> 13; matrix products, arithmetic and copies ran while one was open for 0% -> 0% of each run, Pallas kernels for 16% -> 20%
where the time goes in v22:
time: 62.5 us; the launch traced here: 62.4 us
  starting transfers between devices  32.9 us (53%)
  Pallas kernels  18.9 us (30%)
  waiting for transfers between devices  10.3 us (16%)
    ppermute x24, starting transfers between devices, exchange(): lax.ppermute(values, 'slab', [(device, device ^ far[device.bit_count() %...  32.9 us
    pallas_call x26, Pallas kernels, call(): pl.pallas_call(kernel, out_shape=out_shape, in_specs=in_specs, out_specs=...  18.9 us
    ppermute x24, waiting for transfers between devices, exchange(): lax.ppermute(values, 'slab', [(device, device ^ far[device.bit_count() %...  10.3 us
  transfers between devices with their start and end apart: 24, of which 13 were waited for; matrix products, arithmetic and copies ran while one was open for 0% of the time, Pallas kernels for 20%

profile of v22, /device:TPU:0, one launch (start us, length us, event | category | flops | bytes accessed | tf_op | source)
XLA Modules:
  0.0 62.4 jit_solution(2421032560308464310)
XLA Ops:
  0.0 1.0 %pack.1.refs_0_ = bf16[192,128]{1,0:T(8,128)(2,1)S(1)} custom-call(f32[128,128]{1,0:T(8,128)} %bitcast.8, f32[4,256]{1,0:T(4,128)} %bitcast.12, f32[4,256]{1,0:T(4,128)} %bitcast.14, s32[4,256]{1,0:T(4,128)} %bitcast.16, s32[1,256]{1,0:T(1,128)} %bitcast.20, s32[1,16]{1,0:T(1,128)} %bitcast.18), custom_call_target="tpu_custom_call" | custom-call | flops 4000000000 | bytes 8000000 | tf_op jit(solution)/shard_map/pack/pallas_call | solution.py:411
  1.0 3.5 %collective-permute-start = (bf16[192,128]{1,0:T(8,128)(2,1)S(1)}, bf16[192,128]{1,0:T(8,128)(2,1)S(1)}, u32[]{:S(2)}, u32[]{:S(2)}) collective-permute-start(bf16[192,128]{1,0:T(8,128)(2,1)S(1)} %pack.1.refs_0_), channel_id=1, source_target_pairs={{0,9},{1,4},{2,7},{3,10},{4,1},{5,12},{6,15},{7,2},{8,13},{9,0},{1... | collective-permute-start | bytes 147464 | tf_op jit(solution)/shard_map/ppermute | solution.py:426
  4.6 1.9 %collective-permute-start.1 = (bf16[192,128]{1,0:T(8,128)(2,1)S(1)}, bf16[192,128]{1,0:T(8,128)(2,1)S(1)}, u32[]{:S(2)}, u32[]{:S(2)}) collective-permute-start(bf16[192,128]{1,0:T(8,128)(2,1)S(1)} %pack.1.refs_0_), channel_id=1, source_target_pairs={{0,5},{1,8},{2,11},{3,6},{4,13},{5,0},{6,3},{7,14},{8,1},{9,12},{1... | collective-permute-start | bytes 147464 | tf_op jit(solution)/shard_map/ppermute | solution.py:426
  6.5 3.9 %collective-permute-start.4 = (bf16[192,128]{1,0:T(8,128)(2,1)S(1)}, bf16[192,128]{1,0:T(8,128)(2,1)S(1)}, u32[]{:S(2)}, u32[]{:S(2)}) collective-permute-start(bf16[192,128]{1,0:T(8,128)(2,1)S(1)} %pack.1.refs_0_), channel_id=1, source_target_pairs={{0,15},{1,14},{2,13},{3,12},{4,11},{5,10},{6,9},{7,8},{8,7},{9,6},... | collective-permute-start | bytes 147464 | tf_op jit(solution)/shard_map/ppermute | solution.py:426
  10.4 1.1 %collective-permute-start.3 = (bf16[576,128]{1,0:T(8,128)(2,1)S(1)}, bf16[576,128]{1,0:T(8,128)(2,1)S(1)}, u32[]{:S(2)}, u32[]{:S(2)}) collective-permute-start(bf16[576,128]{1,0:T(8,128)(2,1)S(1)} %join.2.refs_0_), channel_id=1, source_target_pairs={{0,3},{1,2},{2,1},{3,0},{4,7},{5,6},{6,5},{7,4},{8,11},{9,10},{10,... | collective-permute-start | bytes 442376 | tf_op jit(solution)/shard_map/ppermute | solution.py:426
  11.5 0.9 %collective-permute-done.2.refs_1_ = bf16[192,128]{1,0:T(8,128)(2,1)S(1)} collective-permute-done((bf16[192,128]{1,0:T(8,128)(2,1)S(1)}, bf16[192,128]{1,0:T(8,128)(2,1)S(1)}, u32[]{:S(2)}, u32[]{:S(2)}) %collective-permute-start.2) | collective-permute-done | bytes 49184 | tf_op jit(solution)/shard_map/ppermute | solution.py:426
  12.4 1.5 %setup.2 = (s32[8,128]{1,0:T(8,128)S(4)}, f32[64,128]{1,0:T(8,128)S(1)}, s32[544,128]{1,0:T(8,128)S(1)}, f32[544,128]{1,0:T(8,128)S(1)}, f32[544,128]{1,0:T(8,12...) custom-call(bf16[576,128]{1,0:T(8,128)(2,1)S(1)} %join.2.refs_0_, ...), custom_call_target="tpu_custom_call" | custom-call | flops 4000000000 | bytes 8000000 | tf_op jit(solution)/shard_map/setup/pallas_call | solution.py:411
  13.9 1.8 %forward.6.refs_2_.refs_6_ = f32[512,128]{1,0:T(8,128)S(1)} custom-call(s32[8,128]{1,0:T(8,128)S(4)} %get-tuple-element.38.slots, bf16[576,128]{1,0:T(8,128)(2,1)S(1)} %join.2.refs_0_, bf16[192,128]{1,0:T(8,128)(2,1)S(1)} %collective-permute-done.2.refs_1_, s32[544,128]{1,0:T(8,128)S(1)} %get-tuple-element.39.refs_2_, ...), custom_call_target="tpu_custom_call" | custom-call | flops 4000000000 | bytes 8000000 | tf_op jit(solution)/shard_map/forward/pallas_call | solution.py:411
  16.2 1.6 %setup.3 = (s32[8,128]{1,0:T(8,128)S(4)}, s32[8,128]{1,0:T(8,128)S(4)}, f32[64,128]{1,0:T(8,128)S(1)}, s32[544,128]{1,0:T(8,128)S(1)}, f32[544,128]{1,0:T(8,128)...) custom-call(bf16[576,128]{1,0:T(8,128)(2,1)S(1)} %collective-permute, ...), custom_call_target="tpu_custom_call" | custom-call | flops 4000000000 | bytes 8000000 | tf_op jit(solution)/shard_map/setup/pallas_call | solution.py:411
  18.6 1.0 %collective-permute-start.5 = (f32[288,128]{1,0:T(8,128)S(1)}, f32[288,128]{1,0:T(8,128)S(1)}, u32[]{:S(2)}, u32[]{:S(2)}) collective-permute-start(f32[288,128]{1,0:T(8,128)S(1)} %forward.8), channel_id=1, source_target_pairs={{0,1},{1,0},{2,3},{3,2},{4,5},{5,4},{6,7},{7,6},{8,9},{9,8},{10,11... | collective-permute-start | bytes 442376 | tf_op jit(solution)/shard_map/ppermute | solution.py:426
  19.6 1.1 %forward.7.projection_ref = f32[256,128]{1,0:T(8,128)S(1)} custom-call(s32[8,128]{1,0:T(8,128)S(4)} %get-tuple-element.43.slots, bf16[576,128]{1,0:T(8,128)(2,1)S(1)} %collective-permute-done.3.refs_0_, bf16[192,128]{1,0:T(8,128)(2,1)S(1)} %collective-permute-done.4.refs_1_, s32[544,128]{1,0:T(8,128)S(1)} %get-tuple-element.44.refs_2_, ...), custom_call_target="tpu_custom_call" | custom-call | flops 4000000000 | bytes 8000000 | tf_op jit(solution)/shard_map/forward/pallas_call | solution.py:411
  21.1 0.9 %backward.7.refs_4_ = f32[512,128]{1,0:T(8,128)S(1)} custom-call(s32[8,128]{1,0:T(8,128)S(4)} %get-tuple-element.43.slots, bf16[256,128]{1,0:T(8,128)(2,1)S(1)} %residual.2.refs_0_, s32[544,128]{1,0:T(8,128)S(1)} %get-tuple-element.54.refs_1_, f32[544,128]{1,0:T(8,128)S(1)} %get-tuple-element.55.refs_2_, f32[544,128]{1,0:T(8,128)S(1)} %get-tuple-element.56.refs_3_), custom_call_target="tpu_custom_call" | custom-call | flops 4000000000 | bytes 8000000 | tf_op jit(solution)/shard_map/backward/pallas_call | solution.py:411
  22.7 1.0 %collective-permute-start.8 = (bf16[256,128]{1,0:T(8,128)(2,1)S(1)}, bf16[256,128]{1,0:T(8,128)(2,1)S(1)}, u32[]{:S(2)}, u32[]{:S(2)}) collective-permute-start(bf16[256,128]{1,0:T(8,128)(2,1)S(1)} %get-tuple-element.59), channel_id=1, source_target_pairs={{0,3},{1,2},{2,1},{3,0},{4,7},{5,6},{6,5},{7,4},{8,11},{9,10},{10,... | collective-permute-start | bytes 196616 | tf_op jit(solution)/shard_map/ppermute | solution.py:426
  23.7 0.8 %collective-permute-start.7 = (bf16[256,128]{1,0:T(8,128)(2,1)S(1)}, bf16[256,128]{1,0:T(8,128)(2,1)S(1)}, u32[]{:S(2)}, u32[]{:S(2)}) collective-permute-start(bf16[256,128]{1,0:T(8,128)(2,1)S(1)} %get-tuple-element.57), channel_id=1, source_target_pairs={{0,3},{1,2},{2,1},{3,0},{4,7},{5,6},{6,5},{7,4},{8,11},{9,10},{10,... | collective-permute-start | bytes 196616 | tf_op jit(solution)/shard_map/ppermute | solution.py:426
  24.5 1.4 %backward.6.sum_ref = f32[512,128]{1,0:T(8,128)S(1)} custom-call(s32[8,128]{1,0:T(8,128)S(4)} %get-tuple-element.38.slots, bf16[256,128]{1,0:T(8,128)(2,1)S(1)} %residual.2.refs_0_, bf16[256,128]{1,0:T(8,128)(2,1)S(1)} %collective-permute-done.6.refs_1_.refs_0_, s32[544,128]{1,0:T(8,128)S(1)} %get-tuple-element.51.refs_2_, ...), custom_call_target="tpu_custom_call" | custom-call | flops 4000000000 | bytes 8000000 | tf_op jit(solution)/shard_map/backward/pallas_call | solution.py:411
  26.5 3.3 %collective-permute-start.10 = (bf16[128,128]{1,0:T(8,128)(2,1)S(1)}, bf16[128,128]{1,0:T(8,128)(2,1)S(1)}, u32[]{:S(2)}, u32[]{:S(2)}) collective-permute-start(bf16[128,128]{1,0:T(8,128)(2,1)S(1)} %get-tuple-element.61), channel_id=1, source_target_pairs={{0,12},{1,13},{2,14},{3,15},{4,8},{5,9},{6,10},{7,11},{8,4},{9,5},... | collective-permute-start | bytes 98312 | tf_op jit(solution)/shard_map/ppermute | solution.py:426
  29.9 0.9 %collective-permute-start.11 = (bf16[128,128]{1,0:T(8,128)(2,1)S(1)}, bf16[128,128]{1,0:T(8,128)(2,1)S(1)}, u32[]{:S(2)}, u32[]{:S(2)}) collective-permute-start(bf16[128,128]{1,0:T(8,128)(2,1)S(1)} %get-tuple-element.62), channel_id=1, source_target_pairs={{0,5},{1,8},{2,11},{3,6},{4,13},{5,0},{6,3},{7,14},{8,1},{9,12},{1... | collective-permute-start | bytes 98312 | tf_op jit(solution)/shard_map/ppermute | solution.py:426
  31.4 0.8 %collective-permute-done.10.refs_2_ = bf16[128,128]{1,0:T(8,128)(2,1)S(1)} collective-permute-done((bf16[128,128]{1,0:T(8,128)(2,1)S(1)}, bf16[128,128]{1,0:T(8,128)(2,1)S(1)}, u32[]{:S(2)}, u32[]{:S(2)}) %collective-permute-start.10) | collective-permute-done | bytes 32800 | tf_op jit(solution)/shard_map/ppermute | solution.py:426
  32.3 1.9 %collective-permute-done.9.refs_1_ = bf16[128,128]{1,0:T(8,128)(2,1)S(1)} collective-permute-done((bf16[128,128]{1,0:T(8,128)(2,1)S(1)}, bf16[128,128]{1,0:T(8,128)(2,1)S(1)}, u32[]{:S(2)}, u32[]{:S(2)}) %collective-permute-start.9) | collective-permute-done | bytes 32800 | tf_op jit(solution)/shard_map/ppermute | solution.py:426
  34.2 1.9 %collective-permute-start.12 = (bf16[128,128]{1,0:T(8,128)(2,1)S(1)}, bf16[128,128]{1,0:T(8,128)(2,1)S(1)}, u32[]{:S(2)}, u32[]{:S(2)}) collective-permute-start(bf16[128,128]{1,0:T(8,128)(2,1)S(1)} %get-tuple-element.64.refs_0_), channel_id=1, source_target_pairs={{0,9},{1,4},{2,7},{3,10},{4,1},{5,12},{6,15},{7,2},{8,13},{9,0},{1... | collective-permute-start | bytes 98312 | tf_op jit(solution)/shard_map/ppermute | solution.py:426
  36.6 1.7 %collective-permute-start.16 = (bf16[128,128]{1,0:T(8,128)(2,1)S(1)}, bf16[128,128]{1,0:T(8,128)(2,1)S(1)}, u32[]{:S(2)}, u32[]{:S(2)}) collective-permute-start(bf16[128,128]{1,0:T(8,128)(2,1)S(1)} %get-tuple-element.64.refs_0_), channel_id=1, source_target_pairs={{0,12},{1,13},{2,14},{3,15},{4,8},{5,9},{6,10},{7,11},{8,4},{9,5},... | collective-permute-start | bytes 98312 | tf_op jit(solution)/shard_map/ppermute | solution.py:426
  38.4 1.2 %collective-permute-start.15 = (bf16[128,128]{1,0:T(8,128)(2,1)S(1)}, bf16[128,128]{1,0:T(8,128)(2,1)S(1)}, u32[]{:S(2)}, u32[]{:S(2)}) collective-permute-start(bf16[128,128]{1,0:T(8,128)(2,1)S(1)} %get-tuple-element.64.refs_0_), channel_id=1, source_target_pairs={{0,15},{1,14},{2,13},{3,12},{4,11},{5,10},{6,9},{7,8},{8,7},{9,6},... | collective-permute-start | bytes 98312 | tf_op jit(solution)/shard_map/ppermute | solution.py:426
  39.5 2.2 %collective-permute-start.14 = (bf16[384,128]{1,0:T(8,128)(2,1)S(1)}, bf16[384,128]{1,0:T(8,128)(2,1)S(1)}, u32[]{:S(2)}, u32[]{:S(2)}) collective-permute-start(bf16[384,128]{1,0:T(8,128)(2,1)S(1)} %join.3.refs_0_), channel_id=1, source_target_pairs={{0,3},{1,2},{2,1},{3,0},{4,7},{5,6},{6,5},{7,4},{8,11},{9,10},{10,... | collective-permute-start | bytes 294920 | tf_op jit(solution)/shard_map/ppermute | solution.py:426
  42.3 1.8 %forward.9.refs_6_ = f32[512,128]{1,0:T(8,128)S(1)} custom-call(s32[8,128]{1,0:T(8,128)S(4)} %get-tuple-element.38.slots, bf16[384,128]{1,0:T(8,128)(2,1)S(1)} %join.3.refs_0_, bf16[128,128]{1,0:T(8,128)(2,1)S(1)} %collective-permute-done.16.refs_1_, s32[544,128]{1,0:T(8,128)S(1)} %get-tuple-element.39.refs_2_, f32[544,128]{1,0:T(8,128)S(1)} %get-tuple-element.40.refs_3_, ...), custom_call_target="tpu_custom_call" | custom-call | flops 4000000000 | bytes 8000000 | tf_op jit(solution)/shard_map/forward/pallas_call | solution.py:411
  45.6 1.2 %collective-permute-start.17 = (f32[256,128]{1,0:T(8,128)S(1)}, f32[256,128]{1,0:T(8,128)S(1)}, u32[]{:S(2)}, u32[]{:S(2)}) collective-permute-start(f32[256,128]{1,0:T(8,128)S(1)} %forward.11), channel_id=1, source_target_pairs={{0,1},{1,0},{2,3},{3,2},{4,5},{5,4},{6,7},{7,6},{8,9},{9,8},{10,11... | collective-permute-start | bytes 393224 | tf_op jit(solution)/shard_map/ppermute | solution.py:426
  46.8 1.1 %forward.10.projection_ref = f32[256,128]{1,0:T(8,128)S(1)} custom-call(s32[8,128]{1,0:T(8,128)S(4)} %get-tuple-element.43.slots, bf16[384,128]{1,0:T(8,128)(2,1)S(1)} %collective-permute-done.14.refs_0_, bf16[128,128]{1,0:T(8,128)(2,1)S(1)} %collective-permute-done.15.refs_1_, s32[544,128]{1,0:T(8,128)S(1)} %get-tuple-element.44.refs_2_, ...), custom_call_target="tpu_custom_call" | custom-call | flops 4000000000 | bytes 8000000 | tf_op jit(solution)/shard_map/forward/pallas_call | solution.py:411
  48.2 0.9 %backward.10.refs_4_ = f32[512,128]{1,0:T(8,128)S(1)} custom-call(s32[8,128]{1,0:T(8,128)S(4)} %get-tuple-element.43.slots, bf16[256,128]{1,0:T(8,128)(2,1)S(1)} %residual.3.refs_0_, s32[544,128]{1,0:T(8,128)S(1)} %get-tuple-element.54.refs_1_, f32[544,128]{1,0:T(8,128)S(1)} %get-tuple-element.55.refs_2_, f32[544,128]{1,0:T(8,128)S(1)} %get-tuple-element.56.refs_3_), custom_call_target="tpu_custom_call" | custom-call | flops 4000000000 | bytes 8000000 | tf_op jit(solution)/shard_map/backward/pallas_call | solution.py:411
  49.9 1.2 %collective-permute-start.20 = (bf16[256,128]{1,0:T(8,128)(2,1)S(1)}, bf16[256,128]{1,0:T(8,128)(2,1)S(1)}, u32[]{:S(2)}, u32[]{:S(2)}) collective-permute-start(bf16[256,128]{1,0:T(8,128)(2,1)S(1)} %get-tuple-element.67), channel_id=1, source_target_pairs={{0,3},{1,2},{2,1},{3,0},{4,7},{5,6},{6,5},{7,4},{8,11},{9,10},{10,... | collective-permute-start | bytes 196616 | tf_op jit(solution)/shard_map/ppermute | solution.py:426
  51.7 1.4 %backward.9.sum_ref = f32[512,128]{1,0:T(8,128)S(1)} custom-call(s32[8,128]{1,0:T(8,128)S(4)} %get-tuple-element.38.slots, bf16[256,128]{1,0:T(8,128)(2,1)S(1)} %residual.3.refs_0_, bf16[256,128]{1,0:T(8,128)(2,1)S(1)} %collective-permute-done.18.refs_1_.refs_0_, s32[544,128]{1,0:T(8,128)S(1)} %get-tuple-element.51.refs_2_, ...), custom_call_target="tpu_custom_call" | custom-call | flops 4000000000 | bytes 8000000 | tf_op jit(solution)/shard_map/backward/pallas_call | solution.py:411
  53.7 1.7 %collective-permute-start.21 = (bf16[128,128]{1,0:T(8,128)(2,1)S(1)}, bf16[128,128]{1,0:T(8,128)(2,1)S(1)}, u32[]{:S(2)}, u32[]{:S(2)}) collective-permute-start(bf16[128,128]{1,0:T(8,128)(2,1)S(1)} %get-tuple-element.68), channel_id=1, source_target_pairs={{0,9},{1,4},{2,7},{3,10},{4,1},{5,12},{6,15},{7,2},{8,13},{9,0},{1... | collective-permute-start | bytes 98312 | tf_op jit(solution)/shard_map/ppermute | solution.py:426
  55.4 2.5 %collective-permute-start.22 = (bf16[128,128]{1,0:T(8,128)(2,1)S(1)}, bf16[128,128]{1,0:T(8,128)(2,1)S(1)}, u32[]{:S(2)}, u32[]{:S(2)}) collective-permute-start(bf16[128,128]{1,0:T(8,128)(2,1)S(1)} %get-tuple-element.69), channel_id=1, source_target_pairs={{0,12},{1,13},{2,14},{3,15},{4,8},{5,9},{6,10},{7,11},{8,4},{9,5},... | collective-permute-start | bytes 98312 | tf_op jit(solution)/shard_map/ppermute | solution.py:426
  58.0 3.1 %collective-permute-done.22.refs_2_ = bf16[128,128]{1,0:T(8,128)(2,1)S(1)} collective-permute-done((bf16[128,128]{1,0:T(8,128)(2,1)S(1)}, bf16[128,128]{1,0:T(8,128)(2,1)S(1)}, u32[]{:S(2)}, u32[]{:S(2)}) %collective-permute-start.22) | collective-permute-done | bytes 32800 | tf_op jit(solution)/shard_map/ppermute | solution.py:426
  (54 shorter events, 9.6 us)
Async XLA Ops:
  1.0 9.3 %collective-permute-start = (bf16[192,128]{1,0:T(8,128)(2,1)S(1)}, bf16[192,128]{1,0:T(8,128)(2,1)S(1)}, u32[]{:S(2)}, u32[]{:S(2)}) collective-permute-start(bf16[192,128]{1,0:T(8,128)(2,1)S(1)} %pack.1.refs_0_), channel_id=1, source_target_pairs={{0,9},{1,4},{2,7},{3,10},{4,1},{5,12},{6,15},{7,2},{8,13},{9,0},{1... | collective-permute-start | bytes 147464 | tf_op jit(solution)/shard_map/ppermute | solution.py:426
  4.6 5.8 %collective-permute-start.1 = (bf16[192,128]{1,0:T(8,128)(2,1)S(1)}, bf16[192,128]{1,0:T(8,128)(2,1)S(1)}, u32[]{:S(2)}, u32[]{:S(2)}) collective-permute-start(bf16[192,128]{1,0:T(8,128)(2,1)S(1)} %pack.1.refs_0_), channel_id=1, source_target_pairs={{0,5},{1,8},{2,11},{3,6},{4,13},{5,0},{6,3},{7,14},{8,1},{9,12},{1... | collective-permute-start | bytes 147464 | tf_op jit(solution)/shard_map/ppermute | solution.py:426
  6.4 6.0 %collective-permute-start.2 = (bf16[192,128]{1,0:T(8,128)(2,1)S(1)}, bf16[192,128]{1,0:T(8,128)(2,1)S(1)}, u32[]{:S(2)}, u32[]{:S(2)}) collective-permute-start(bf16[192,128]{1,0:T(8,128)(2,1)S(1)} %pack.1.refs_0_), channel_id=1, source_target_pairs={{0,12},{1,13},{2,14},{3,15},{4,8},{5,9},{6,10},{7,11},{8,4},{9,5},... | collective-permute-start | bytes 147464 | tf_op jit(solution)/shard_map/ppermute | solution.py:426
  6.5 9.3 %collective-permute-start.4 = (bf16[192,128]{1,0:T(8,128)(2,1)S(1)}, bf16[192,128]{1,0:T(8,128)(2,1)S(1)}, u32[]{:S(2)}, u32[]{:S(2)}) collective-permute-start(bf16[192,128]{1,0:T(8,128)(2,1)S(1)} %pack.1.refs_0_), channel_id=1, source_target_pairs={{0,15},{1,14},{2,13},{3,12},{4,11},{5,10},{6,9},{7,8},{8,7},{9,6},... | collective-permute-start | bytes 147464 | tf_op jit(solution)/shard_map/ppermute | solution.py:426
  10.4 5.8 %collective-permute-start.3 = (bf16[576,128]{1,0:T(8,128)(2,1)S(1)}, bf16[576,128]{1,0:T(8,128)(2,1)S(1)}, u32[]{:S(2)}, u32[]{:S(2)}) collective-permute-start(bf16[576,128]{1,0:T(8,128)(2,1)S(1)} %join.2.refs_0_), channel_id=1, source_target_pairs={{0,3},{1,2},{2,1},{3,0},{4,7},{5,6},{6,5},{7,4},{8,11},{9,10},{10,... | collective-permute-start | bytes 442376 | tf_op jit(solution)/shard_map/ppermute | solution.py:426
  18.6 2.1 %collective-permute-start.5 = (f32[288,128]{1,0:T(8,128)S(1)}, f32[288,128]{1,0:T(8,128)S(1)}, u32[]{:S(2)}, u32[]{:S(2)}) collective-permute-start(f32[288,128]{1,0:T(8,128)S(1)} %forward.8), channel_id=1, source_target_pairs={{0,1},{1,0},{2,3},{3,2},{4,5},{5,4},{6,7},{7,6},{8,9},{9,8},{10,11... | collective-permute-start | bytes 442376 | tf_op jit(solution)/shard_map/ppermute | solution.py:426
  19.6 1.1 %copy-start.1 = (bf16[32,8,128]{2,1,0:T(8,128)(2,1)S(1)}, bf16[32,8,128]{2,1,0:T(8,128)(2,1)}, u32[]{:S(2)}) copy-start(bf16[32,8,128]{2,1,0:T(8,128)(2,1)} %param.7) | copy-start | bytes 196612
  20.8 1.3 %collective-permute-start.6 = (bf16[256,128]{1,0:T(8,128)(2,1)S(1)}, bf16[256,128]{1,0:T(8,128)(2,1)S(1)}, u32[]{:S(2)}, u32[]{:S(2)}) collective-permute-start(bf16[256,128]{1,0:T(8,128)(2,1)S(1)} %residual.2.refs_0_), channel_id=1, source_target_pairs={{0,1},{1,0},{2,3},{3,2},{4,5},{5,4},{6,7},{7,6},{8,9},{9,8},{10,11... | collective-permute-start | bytes 196616 | tf_op jit(solution)/shard_map/ppermute | solution.py:426
  22.7 3.8 %collective-permute-start.8 = (bf16[256,128]{1,0:T(8,128)(2,1)S(1)}, bf16[256,128]{1,0:T(8,128)(2,1)S(1)}, u32[]{:S(2)}, u32[]{:S(2)}) collective-permute-start(bf16[256,128]{1,0:T(8,128)(2,1)S(1)} %get-tuple-element.59), channel_id=1, source_target_pairs={{0,3},{1,2},{2,1},{3,0},{4,7},{5,6},{6,5},{7,4},{8,11},{9,10},{10,... | collective-permute-start | bytes 196616 | tf_op jit(solution)/shard_map/ppermute | solution.py:426
  23.7 6.1 %collective-permute-start.7 = (bf16[256,128]{1,0:T(8,128)(2,1)S(1)}, bf16[256,128]{1,0:T(8,128)(2,1)S(1)}, u32[]{:S(2)}, u32[]{:S(2)}) collective-permute-start(bf16[256,128]{1,0:T(8,128)(2,1)S(1)} %get-tuple-element.57), channel_id=1, source_target_pairs={{0,3},{1,2},{2,1},{3,0},{4,7},{5,6},{6,5},{7,4},{8,11},{9,10},{10,... | collective-permute-start | bytes 196616 | tf_op jit(solution)/shard_map/ppermute | solution.py:426
  26.5 5.8 %collective-permute-start.10 = (bf16[128,128]{1,0:T(8,128)(2,1)S(1)}, bf16[128,128]{1,0:T(8,128)(2,1)S(1)}, u32[]{:S(2)}, u32[]{:S(2)}) collective-permute-start(bf16[128,128]{1,0:T(8,128)(2,1)S(1)} %get-tuple-element.61), channel_id=1, source_target_pairs={{0,12},{1,13},{2,14},{3,15},{4,8},{5,9},{6,10},{7,11},{8,4},{9,5},... | collective-permute-start | bytes 98312 | tf_op jit(solution)/shard_map/ppermute | solution.py:426
  29.8 1.0 %copy-start.2 = (f32[256,4]{0,1:T(4,128)S(1)}, f32[256,4]{0,1:T(4,128)}, u32[]{:S(2)}) copy-start(f32[256,4]{0,1:T(4,128)} %param.13) | copy-start | bytes 12292
  29.8 1.0 %copy-start.3 = (f32[256,4]{0,1:T(4,128)S(1)}, f32[256,4]{0,1:T(4,128)}, u32[]{:S(2)}) copy-start(f32[256,4]{0,1:T(4,128)} %param.12) | copy-start | bytes 12292
  29.8 1.0 %copy-start.4 = (s32[256,4]{0,1:T(4,128)S(1)}, s32[256,4]{0,1:T(4,128)}, u32[]{:S(2)}) copy-start(s32[256,4]{0,1:T(4,128)} %param.9) | copy-start | bytes 12292
  29.8 4.3 %collective-permute-start.9 = (bf16[128,128]{1,0:T(8,128)(2,1)S(1)}, bf16[128,128]{1,0:T(8,128)(2,1)S(1)}, u32[]{:S(2)}, u32[]{:S(2)}) collective-permute-start(bf16[128,128]{1,0:T(8,128)(2,1)S(1)} %get-tuple-element.60), channel_id=1, source_target_pairs={{0,9},{1,4},{2,7},{3,10},{4,1},{5,12},{6,15},{7,2},{8,13},{9,0},{1... | collective-permute-start | bytes 98312 | tf_op jit(solution)/shard_map/ppermute | solution.py:426
  29.9 0.9 %copy-start.5 = (s32[16]{0:T(128)S(1)}, s32[16]{0:T(128)}, u32[]{:S(2)}) copy-start(s32[16]{0:T(128)} %param.11) | copy-start | bytes 196
  29.9 4.3 %copy-start = (f32[16,8,128]{2,1,0:T(8,128)S(1)}, f32[16,8,128]{2,1,0:T(8,128)}, u32[]{:S(2)}) copy-start(f32[16,8,128]{2,1,0:T(8,128)} %param.8) | copy-start | bytes 196612
  29.9 4.3 %collective-permute-start.11 = (bf16[128,128]{1,0:T(8,128)(2,1)S(1)}, bf16[128,128]{1,0:T(8,128)(2,1)S(1)}, u32[]{:S(2)}, u32[]{:S(2)}) collective-permute-start(bf16[128,128]{1,0:T(8,128)(2,1)S(1)} %get-tuple-element.62), channel_id=1, source_target_pairs={{0,5},{1,8},{2,11},{3,6},{4,13},{5,0},{6,3},{7,14},{8,1},{9,12},{1... | collective-permute-start | bytes 98312 | tf_op jit(solution)/shard_map/ppermute | solution.py:426
  34.2 5.4 %collective-permute-start.12 = (bf16[128,128]{1,0:T(8,128)(2,1)S(1)}, bf16[128,128]{1,0:T(8,128)(2,1)S(1)}, u32[]{:S(2)}, u32[]{:S(2)}) collective-permute-start(bf16[128,128]{1,0:T(8,128)(2,1)S(1)} %get-tuple-element.64.refs_0_), channel_id=1, source_target_pairs={{0,9},{1,4},{2,7},{3,10},{4,1},{5,12},{6,15},{7,2},{8,13},{9,0},{1... | collective-permute-start | bytes 98312 | tf_op jit(solution)/shard_map/ppermute | solution.py:426
  36.1 3.4 %collective-permute-start.13 = (bf16[128,128]{1,0:T(8,128)(2,1)S(1)}, bf16[128,128]{1,0:T(8,128)(2,1)S(1)}, u32[]{:S(2)}, u32[]{:S(2)}) collective-permute-start(bf16[128,128]{1,0:T(8,128)(2,1)S(1)} %get-tuple-element.64.refs_0_), channel_id=1, source_target_pairs={{0,5},{1,8},{2,11},{3,6},{4,13},{5,0},{6,3},{7,14},{8,1},{9,12},{1... | collective-permute-start | bytes 98312 | tf_op jit(solution)/shard_map/ppermute | solution.py:426
  36.6 5.7 %collective-permute-start.16 = (bf16[128,128]{1,0:T(8,128)(2,1)S(1)}, bf16[128,128]{1,0:T(8,128)(2,1)S(1)}, u32[]{:S(2)}, u32[]{:S(2)}) collective-permute-start(bf16[128,128]{1,0:T(8,128)(2,1)S(1)} %get-tuple-element.64.refs_0_), channel_id=1, source_target_pairs={{0,12},{1,13},{2,14},{3,15},{4,8},{5,9},{6,10},{7,11},{8,4},{9,5},... | collective-permute-start | bytes 98312 | tf_op jit(solution)/shard_map/ppermute | solution.py:426
  38.4 6.1 %collective-permute-start.15 = (bf16[128,128]{1,0:T(8,128)(2,1)S(1)}, bf16[128,128]{1,0:T(8,128)(2,1)S(1)}, u32[]{:S(2)}, u32[]{:S(2)}) collective-permute-start(bf16[128,128]{1,0:T(8,128)(2,1)S(1)} %get-tuple-element.64.refs_0_), channel_id=1, source_target_pairs={{0,15},{1,14},{2,13},{3,12},{4,11},{5,10},{6,9},{7,8},{8,7},{9,6},... | collective-permute-start | bytes 98312 | tf_op jit(solution)/shard_map/ppermute | solution.py:426
  39.5 5.3 %collective-permute-start.14 = (bf16[384,128]{1,0:T(8,128)(2,1)S(1)}, bf16[384,128]{1,0:T(8,128)(2,1)S(1)}, u32[]{:S(2)}, u32[]{:S(2)}) collective-permute-start(bf16[384,128]{1,0:T(8,128)(2,1)S(1)} %join.3.refs_0_), channel_id=1, source_target_pairs={{0,3},{1,2},{2,1},{3,0},{4,7},{5,6},{6,5},{7,4},{8,11},{9,10},{10,... | collective-permute-start | bytes 294920 | tf_op jit(solution)/shard_map/ppermute | solution.py:426
  45.6 2.3 %collective-permute-start.17 = (f32[256,128]{1,0:T(8,128)S(1)}, f32[256,128]{1,0:T(8,128)S(1)}, u32[]{:S(2)}, u32[]{:S(2)}) collective-permute-start(f32[256,128]{1,0:T(8,128)S(1)} %forward.11), channel_id=1, source_target_pairs={{0,1},{1,0},{2,3},{3,2},{4,5},{5,4},{6,7},{7,6},{8,9},{9,8},{10,11... | collective-permute-start | bytes 393224 | tf_op jit(solution)/shard_map/ppermute | solution.py:426
  47.9 1.3 %collective-permute-start.18 = (bf16[256,128]{1,0:T(8,128)(2,1)S(1)}, bf16[256,128]{1,0:T(8,128)(2,1)S(1)}, u32[]{:S(2)}, u32[]{:S(2)}) collective-permute-start(bf16[256,128]{1,0:T(8,128)(2,1)S(1)} %residual.3.refs_0_), channel_id=1, source_target_pairs={{0,1},{1,0},{2,3},{3,2},{4,5},{5,4},{6,7},{7,6},{8,9},{9,8},{10,11... | collective-permute-start | bytes 196616 | tf_op jit(solution)/shard_map/ppermute | solution.py:426
  49.9 3.8 %collective-permute-start.20 = (bf16[256,128]{1,0:T(8,128)(2,1)S(1)}, bf16[256,128]{1,0:T(8,128)(2,1)S(1)}, u32[]{:S(2)}, u32[]{:S(2)}) collective-permute-start(bf16[256,128]{1,0:T(8,128)(2,1)S(1)} %get-tuple-element.67), channel_id=1, source_target_pairs={{0,3},{1,2},{2,1},{3,0},{4,7},{5,6},{6,5},{7,4},{8,11},{9,10},{10,... | collective-permute-start | bytes 196616 | tf_op jit(solution)/shard_map/ppermute | solution.py:426
  51.1 6.8 %collective-permute-start.19 = (bf16[256,128]{1,0:T(8,128)(2,1)S(1)}, bf16[256,128]{1,0:T(8,128)(2,1)S(1)}, u32[]{:S(2)}, u32[]{:S(2)}) collective-permute-start(bf16[256,128]{1,0:T(8,128)(2,1)S(1)} %get-tuple-element.65), channel_id=1, source_target_pairs={{0,3},{1,2},{2,1},{3,0},{4,7},{5,6},{6,5},{7,4},{8,11},{9,10},{10,... | collective-permute-start | bytes 196616 | tf_op jit(solution)/shard_map/ppermute | solution.py:426
  53.7 4.3 %collective-permute-start.21 = (bf16[128,128]{1,0:T(8,128)(2,1)S(1)}, bf16[128,128]{1,0:T(8,128)(2,1)S(1)}, u32[]{:S(2)}, u32[]{:S(2)}) collective-permute-start(bf16[128,128]{1,0:T(8,128)(2,1)S(1)} %get-tuple-element.68), channel_id=1, source_target_pairs={{0,9},{1,4},{2,7},{3,10},{4,1},{5,12},{6,15},{7,2},{8,13},{9,0},{1... | collective-permute-start | bytes 98312 | tf_op jit(solution)/shard_map/ppermute | solution.py:426
  55.4 5.7 %collective-permute-start.22 = (bf16[128,128]{1,0:T(8,128)(2,1)S(1)}, bf16[128,128]{1,0:T(8,128)(2,1)S(1)}, u32[]{:S(2)}, u32[]{:S(2)}) collective-permute-start(bf16[128,128]{1,0:T(8,128)(2,1)S(1)} %get-tuple-element.69), channel_id=1, source_target_pairs={{0,12},{1,13},{2,14},{3,15},{4,8},{5,9},{6,10},{7,11},{8,4},{9,5},... | collective-permute-start | bytes 98312 | tf_op jit(solution)/shard_map/ppermute | solution.py:426
  57.9 3.9 %collective-permute-start.23 = (bf16[128,128]{1,0:T(8,128)(2,1)S(1)}, bf16[128,128]{1,0:T(8,128)(2,1)S(1)}, u32[]{:S(2)}, u32[]{:S(2)}) collective-permute-start(bf16[128,128]{1,0:T(8,128)(2,1)S(1)} %get-tuple-element.70), channel_id=1, source_target_pairs={{0,5},{1,8},{2,11},{3,6},{4,13},{5,0},{6,3},{7,14},{8,1},{9,12},{1... | collective-permute-start | bytes 98312 | tf_op jit(solution)/shard_map/ppermute | solution.py:426

commit v23 on v22

--- a/solution.py
+++ b/solution.py
@@ -514,9 +514,9 @@
         last = sweep + 1 == ITERS
         if paired:
             place_1, place_2, place_3, across = [
-                exchange(payload, n_slab, *pair) for pair in ((9, 5), (5, 9), (12, 12), (15, 15))]
+                exchange(payload, n_slab, *pair) for pair in ((9, 3), (5, 9), (12, 10), (15, 15))]
             z_part = join(payload, place_1, place_2)
-            y_part = exchange(z_part, n_slab, 3)
+            y_part = exchange(z_part, n_slab, 3, 5)
             along_z, along_y = (z_part, place_3), (y_part, across)
             if sweep == 0:
                 (z_list,), z_rows, z_forward, z_backward = setup(along_z, 4, (None,))
@@ -535,13 +535,13 @@
             y_sum = backward(own_list, [residual], 4, y_backward, F32)
             far_sum, near_sum = backward(
                 other_list, [other_residual], 4, y_backward, (BF16, BF16), y_sum, ((1, 3), (0, 2)))
-            far_part, near_part = exchange(far_sum, n_slab, 3), exchange(near_sum, n_slab, 3)
+            far_part, near_part = exchange(far_sum, n_slab, 3, 5), exchange(near_sum, n_slab, 3, 5)
             z_sum = backward(z_list, [residual, other_residual], 4, z_backward, F32)
             piece = shape((rows, extent), BF16)
             piece_1, piece_3 = call(
                 functools.partial(combine_kernel, (1, 3)), "combine", 16, [VMEM] * 2,
                 [piece, piece], z_sum, far_part)
-            got = [exchange(piece_1, n_slab, 9, 5), exchange(piece_3, n_slab, 12)]
+            got = [exchange(piece_1, n_slab, 9, 3), exchange(piece_3, n_slab, 12, 10)]
             own_piece, piece_2 = call(
                 functools.partial(combine_kernel, (0, 2)), "combine", 16, [VMEM] * 2,
                 [shape((rows, extent), F32), piece], z_sum, near_part)

time: 62.5 us -> 61.8 us (0.989)
  starting transfers between devices: 32.9 us -> 30.5 us
  Pallas kernels: 18.9 us -> 20.2 us
    ppermute x24, starting transfers between devices: 32.9 us -> 30.5 us  [exchange(): lax.ppermute(values, 'slab', [(device, device ^ far[device.bit_count() %...]
    pallas_call x26, Pallas kernels: 18.9 us -> 20.2 us  [call(): pl.pallas_call(kernel, out_shape=out_shape, in_specs=in_specs, out_specs=...]
  transfers between devices with their start and end apart: 24 -> 24, of which waited for: 13 -> 15; matrix products, arithmetic and copies ran while one was open for 0% -> 0% of each run, Pallas kernels for 20% -> 21%
where the time goes in v23:
time: 61.8 us; the launch traced here: 61.4 us
  starting transfers between devices  30.5 us (49%)
  Pallas kernels  20.2 us (33%)
  waiting for transfers between devices  10.4 us (17%)
    ppermute x24, starting transfers between devices, exchange(): lax.ppermute(values, 'slab', [(device, device ^ far[device.bit_count() %...  30.5 us
    pallas_call x26, Pallas kernels, call(): pl.pallas_call(kernel, out_shape=out_shape, in_specs=in_specs, out_specs=...  20.2 us
    ppermute x24, waiting for transfers between devices, exchange(): lax.ppermute(values, 'slab', [(device, device ^ far[device.bit_count() %...  10.4 us
  transfers between devices with their start and end apart: 24, of which 15 were waited for; matrix products, arithmetic and copies ran while one was open for 0% of the time, Pallas kernels for 21%

profile of v23, /device:TPU:0, one launch (start us, length us, event | category | flops | bytes accessed | tf_op | source)
XLA Modules:
  0.0 61.4 jit_solution(11699398057768561215)
XLA Ops:
  0.0 1.0 %pack.1.refs_0_ = bf16[192,128]{1,0:T(8,128)(2,1)S(1)} custom-call(f32[128,128]{1,0:T(8,128)} %bitcast.8, f32[4,256]{1,0:T(4,128)} %bitcast.12, f32[4,256]{1,0:T(4,128)} %bitcast.14, s32[4,256]{1,0:T(4,128)} %bitcast.16, s32[1,256]{1,0:T(1,128)} %bitcast.20, s32[1,16]{1,0:T(1,128)} %bitcast.18), custom_call_target="tpu_custom_call" | custom-call | flops 4000000000 | bytes 8000000 | tf_op jit(solution)/shard_map/pack/pallas_call | solution.py:411
  1.0 3.5 %collective-permute-start = (bf16[192,128]{1,0:T(8,128)(2,1)S(1)}, bf16[192,128]{1,0:T(8,128)(2,1)S(1)}, u32[]{:S(2)}, u32[]{:S(2)}) collective-permute-start(bf16[192,128]{1,0:T(8,128)(2,1)S(1)} %pack.1.refs_0_), channel_id=1, source_target_pairs={{0,9},{1,2},{2,1},{3,10},{4,7},{5,12},{6,15},{7,4},{8,11},{9,0},{1... | collective-permute-start | bytes 147464 | tf_op jit(solution)/shard_map/ppermute | solution.py:426
  4.6 1.9 %collective-permute-start.1 = (bf16[192,128]{1,0:T(8,128)(2,1)S(1)}, bf16[192,128]{1,0:T(8,128)(2,1)S(1)}, u32[]{:S(2)}, u32[]{:S(2)}) collective-permute-start(bf16[192,128]{1,0:T(8,128)(2,1)S(1)} %pack.1.refs_0_), channel_id=1, source_target_pairs={{0,5},{1,8},{2,11},{3,6},{4,13},{5,0},{6,3},{7,14},{8,1},{9,12},{1... | collective-permute-start | bytes 147464 | tf_op jit(solution)/shard_map/ppermute | solution.py:426
  6.5 3.9 %collective-permute-start.4 = (bf16[192,128]{1,0:T(8,128)(2,1)S(1)}, bf16[192,128]{1,0:T(8,128)(2,1)S(1)}, u32[]{:S(2)}, u32[]{:S(2)}) collective-permute-start(bf16[192,128]{1,0:T(8,128)(2,1)S(1)} %pack.1.refs_0_), channel_id=1, source_target_pairs={{0,15},{1,14},{2,13},{3,12},{4,11},{5,10},{6,9},{7,8},{8,7},{9,6},... | collective-permute-start | bytes 147464 | tf_op jit(solution)/shard_map/ppermute | solution.py:426
  10.4 1.1 %collective-permute-start.3 = (bf16[576,128]{1,0:T(8,128)(2,1)S(1)}, bf16[576,128]{1,0:T(8,128)(2,1)S(1)}, u32[]{:S(2)}, u32[]{:S(2)}) collective-permute-start(bf16[576,128]{1,0:T(8,128)(2,1)S(1)} %join.2.refs_0_), channel_id=1, source_target_pairs={{0,3},{1,4},{2,7},{3,0},{4,1},{5,6},{6,5},{7,2},{8,13},{9,10},{10,... | collective-permute-start | bytes 442376 | tf_op jit(solution)/shard_map/ppermute | solution.py:426
  11.5 0.8 %collective-permute-done.2.refs_1_ = bf16[192,128]{1,0:T(8,128)(2,1)S(1)} collective-permute-done((bf16[192,128]{1,0:T(8,128)(2,1)S(1)}, bf16[192,128]{1,0:T(8,128)(2,1)S(1)}, u32[]{:S(2)}, u32[]{:S(2)}) %collective-permute-start.2) | collective-permute-done | bytes 49184 | tf_op jit(solution)/shard_map/ppermute | solution.py:426
  12.3 1.5 %setup.2 = (s32[8,128]{1,0:T(8,128)S(4)}, f32[64,128]{1,0:T(8,128)S(1)}, s32[544,128]{1,0:T(8,128)S(1)}, f32[544,128]{1,0:T(8,128)S(1)}, f32[544,128]{1,0:T(8,12...) custom-call(bf16[576,128]{1,0:T(8,128)(2,1)S(1)} %join.2.refs_0_, ...), custom_call_target="tpu_custom_call" | custom-call | flops 4000000000 | bytes 8000000 | tf_op jit(solution)/shard_map/setup/pallas_call | solution.py:411
  13.8 2.2 %forward.6.refs_2_.refs_6_ = f32[512,128]{1,0:T(8,128)S(1)} custom-call(s32[8,128]{1,0:T(8,128)S(4)} %get-tuple-element.38.slots, bf16[576,128]{1,0:T(8,128)(2,1)S(1)} %join.2.refs_0_, bf16[192,128]{1,0:T(8,128)(2,1)S(1)} %collective-permute-done.2.refs_1_, s32[544,128]{1,0:T(8,128)S(1)} %get-tuple-element.39.refs_2_, ...), custom_call_target="tpu_custom_call" | custom-call | flops 4000000000 | bytes 8000000 | tf_op jit(solution)/shard_map/forward/pallas_call | solution.py:411
  16.0 1.6 %setup.3 = (s32[8,128]{1,0:T(8,128)S(4)}, s32[8,128]{1,0:T(8,128)S(4)}, f32[64,128]{1,0:T(8,128)S(1)}, s32[544,128]{1,0:T(8,128)S(1)}, f32[544,128]{1,0:T(8,128)...) custom-call(bf16[576,128]{1,0:T(8,128)(2,1)S(1)} %collective-permute, ...), custom_call_target="tpu_custom_call" | custom-call | flops 4000000000 | bytes 8000000 | tf_op jit(solution)/shard_map/setup/pallas_call | solution.py:411
  17.6 1.1 %forward.8 = f32[288,128]{1,0:T(8,128)S(1)} custom-call(s32[8,128]{1,0:T(8,128)S(4)} %get-tuple-element.50.slots, bf16[576,128]{1,0:T(8,128)(2,1)S(1)} %collective-permute-done.3.refs_0_, bf16[192,128]{1,0:T(8,128)(2,1)S(1)} %collective-permute-done.4.refs_1_, s32[544,128]{1,0:T(8,128)S(1)} %get-tuple-element.44.refs_2_, ...), custom_call_target="tpu_custom_call" | custom-call | flops 4000000000 | bytes 8000000 | tf_op jit(solution)/shard_map/forward/pallas_call | solution.py:411
  18.8 0.8 %forward.7.projection_ref = f32[256,128]{1,0:T(8,128)S(1)} custom-call(s32[8,128]{1,0:T(8,128)S(4)} %get-tuple-element.43.slots, bf16[576,128]{1,0:T(8,128)(2,1)S(1)} %collective-permute-done.3.refs_0_, bf16[192,128]{1,0:T(8,128)(2,1)S(1)} %collective-permute-done.4.refs_1_, s32[544,128]{1,0:T(8,128)S(1)} %get-tuple-element.44.refs_2_, ...), custom_call_target="tpu_custom_call" | custom-call | flops 4000000000 | bytes 8000000 | tf_op jit(solution)/shard_map/forward/pallas_call | solution.py:411
  21.6 0.9 %backward.8 = (bf16[256,128]{1,0:T(8,128)(2,1)S(1)}, bf16[256,128]{1,0:T(8,128)(2,1)S(1)}) custom-call(s32[8,128]{1,0:T(8,128)S(4)} %get-tuple-element.50.slots, bf16[256,128]{1,0:T(8,128)(2,1)S(1)} %collective-permute-done.6.refs_1_.refs_0_, s32[544,128]{1,0:T(8,128)S(1)} %get-tuple-element.54.refs_1_, f32[544,128]{1,0:T(8,128)S(1)} %get-tuple-element.55.refs_2_, ...), custom_call_target="tpu_custom_call" | custom-call | flops 4000000000 | bytes 8000000 | tf_op jit(solution)/shard_map/backward/pallas_call | solution.py:411
  22.5 2.4 %collective-permute-start.8 = (bf16[256,128]{1,0:T(8,128)(2,1)S(1)}, bf16[256,128]{1,0:T(8,128)(2,1)S(1)}, u32[]{:S(2)}, u32[]{:S(2)}) collective-permute-start(bf16[256,128]{1,0:T(8,128)(2,1)S(1)} %get-tuple-element.59), channel_id=1, source_target_pairs={{0,3},{1,4},{2,7},{3,0},{4,1},{5,6},{6,5},{7,2},{8,13},{9,10},{10,... | collective-permute-start | bytes 196616 | tf_op jit(solution)/shard_map/ppermute | solution.py:426
  25.0 1.7 %backward.6.sum_ref = f32[512,128]{1,0:T(8,128)S(1)} custom-call(s32[8,128]{1,0:T(8,128)S(4)} %get-tuple-element.38.slots, bf16[256,128]{1,0:T(8,128)(2,1)S(1)} %residual.2.refs_0_, bf16[256,128]{1,0:T(8,128)(2,1)S(1)} %collective-permute-done.6.refs_1_.refs_0_, s32[544,128]{1,0:T(8,128)S(1)} %get-tuple-element.51.refs_2_, ...), custom_call_target="tpu_custom_call" | custom-call | flops 4000000000 | bytes 8000000 | tf_op jit(solution)/shard_map/backward/pallas_call | solution.py:411
  26.9 2.3 %collective-permute-start.10 = (bf16[128,128]{1,0:T(8,128)(2,1)S(1)}, bf16[128,128]{1,0:T(8,128)(2,1)S(1)}, u32[]{:S(2)}, u32[]{:S(2)}) collective-permute-start(bf16[128,128]{1,0:T(8,128)(2,1)S(1)} %get-tuple-element.61), channel_id=1, source_target_pairs={{0,12},{1,11},{2,8},{3,15},{4,14},{5,9},{6,10},{7,13},{8,2},{9,5},... | collective-permute-start | bytes 98312 | tf_op jit(solution)/shard_map/ppermute | solution.py:426
  29.3 1.9 %collective-permute-start.11 = (bf16[128,128]{1,0:T(8,128)(2,1)S(1)}, bf16[128,128]{1,0:T(8,128)(2,1)S(1)}, u32[]{:S(2)}, u32[]{:S(2)}) collective-permute-start(bf16[128,128]{1,0:T(8,128)(2,1)S(1)} %get-tuple-element.62), channel_id=1, source_target_pairs={{0,5},{1,8},{2,11},{3,6},{4,13},{5,0},{6,3},{7,14},{8,1},{9,12},{1... | collective-permute-start | bytes 98312 | tf_op jit(solution)/shard_map/ppermute | solution.py:426
  31.8 0.8 %collective-permute-done.10.refs_2_ = bf16[128,128]{1,0:T(8,128)(2,1)S(1)} collective-permute-done((bf16[128,128]{1,0:T(8,128)(2,1)S(1)}, bf16[128,128]{1,0:T(8,128)(2,1)S(1)}, u32[]{:S(2)}, u32[]{:S(2)}) %collective-permute-start.10) | collective-permute-done | bytes 32800 | tf_op jit(solution)/shard_map/ppermute | solution.py:426
  32.7 1.1 %collective-permute-done.9.refs_1_ = bf16[128,128]{1,0:T(8,128)(2,1)S(1)} collective-permute-done((bf16[128,128]{1,0:T(8,128)(2,1)S(1)}, bf16[128,128]{1,0:T(8,128)(2,1)S(1)}, u32[]{:S(2)}, u32[]{:S(2)}) %collective-permute-start.9) | collective-permute-done | bytes 32800 | tf_op jit(solution)/shard_map/ppermute | solution.py:426
  33.8 1.9 %collective-permute-start.12 = (bf16[128,128]{1,0:T(8,128)(2,1)S(1)}, bf16[128,128]{1,0:T(8,128)(2,1)S(1)}, u32[]{:S(2)}, u32[]{:S(2)}) collective-permute-start(bf16[128,128]{1,0:T(8,128)(2,1)S(1)} %get-tuple-element.64.refs_0_), channel_id=1, source_target_pairs={{0,9},{1,2},{2,1},{3,10},{4,7},{5,12},{6,15},{7,4},{8,11},{9,0},{1... | collective-permute-start | bytes 98312 | tf_op jit(solution)/shard_map/ppermute | solution.py:426
  36.3 1.7 %collective-permute-start.16 = (bf16[128,128]{1,0:T(8,128)(2,1)S(1)}, bf16[128,128]{1,0:T(8,128)(2,1)S(1)}, u32[]{:S(2)}, u32[]{:S(2)}) collective-permute-start(bf16[128,128]{1,0:T(8,128)(2,1)S(1)} %get-tuple-element.64.refs_0_), channel_id=1, source_target_pairs={{0,12},{1,11},{2,8},{3,15},{4,14},{5,9},{6,10},{7,13},{8,2},{9,5},... | collective-permute-start | bytes 98312 | tf_op jit(solution)/shard_map/ppermute | solution.py:426
  38.0 2.1 %collective-permute-start.15 = (bf16[128,128]{1,0:T(8,128)(2,1)S(1)}, bf16[128,128]{1,0:T(8,128)(2,1)S(1)}, u32[]{:S(2)}, u32[]{:S(2)}) collective-permute-start(bf16[128,128]{1,0:T(8,128)(2,1)S(1)} %get-tuple-element.64.refs_0_), channel_id=1, source_target_pairs={{0,15},{1,14},{2,13},{3,12},{4,11},{5,10},{6,9},{7,8},{8,7},{9,6},... | collective-permute-start | bytes 98312 | tf_op jit(solution)/shard_map/ppermute | solution.py:426
  40.1 1.2 %collective-permute-start.14 = (bf16[384,128]{1,0:T(8,128)(2,1)S(1)}, bf16[384,128]{1,0:T(8,128)(2,1)S(1)}, u32[]{:S(2)}, u32[]{:S(2)}) collective-permute-start(bf16[384,128]{1,0:T(8,128)(2,1)S(1)} %join.3.refs_0_), channel_id=1, source_target_pairs={{0,3},{1,4},{2,7},{3,0},{4,1},{5,6},{6,5},{7,2},{8,13},{9,10},{10,... | collective-permute-start | bytes 294920 | tf_op jit(solution)/shard_map/ppermute | solution.py:426
  42.0 2.1 %forward.9.refs_6_ = f32[512,128]{1,0:T(8,128)S(1)} custom-call(s32[8,128]{1,0:T(8,128)S(4)} %get-tuple-element.38.slots, bf16[384,128]{1,0:T(8,128)(2,1)S(1)} %join.3.refs_0_, bf16[128,128]{1,0:T(8,128)(2,1)S(1)} %collective-permute-done.16.refs_1_, s32[544,128]{1,0:T(8,128)S(1)} %get-tuple-element.39.refs_2_, f32[544,128]{1,0:T(8,128)S(1)} %get-tuple-element.40.refs_3_, ...), custom_call_target="tpu_custom_call" | custom-call | flops 4000000000 | bytes 8000000 | tf_op jit(solution)/shard_map/forward/pallas_call | solution.py:411
  45.0 1.1 %forward.11 = f32[256,128]{1,0:T(8,128)S(1)} custom-call(s32[8,128]{1,0:T(8,128)S(4)} %get-tuple-element.50.slots, bf16[384,128]{1,0:T(8,128)(2,1)S(1)} %collective-permute-done.14.refs_0_, bf16[128,128]{1,0:T(8,128)(2,1)S(1)} %collective-permute-done.15.refs_1_, s32[544,128]{1,0:T(8,128)S(1)} %get-tuple-element.44.refs_2_, ...), custom_call_target="tpu_custom_call" | custom-call | flops 4000000000 | bytes 8000000 | tf_op jit(solution)/shard_map/forward/pallas_call | solution.py:411
  46.4 0.7 %forward.10.projection_ref = f32[256,128]{1,0:T(8,128)S(1)} custom-call(s32[8,128]{1,0:T(8,128)S(4)} %get-tuple-element.43.slots, bf16[384,128]{1,0:T(8,128)(2,1)S(1)} %collective-permute-done.14.refs_0_, bf16[128,128]{1,0:T(8,128)(2,1)S(1)} %collective-permute-done.15.refs_1_, s32[544,128]{1,0:T(8,128)S(1)} %get-tuple-element.44.refs_2_, ...), custom_call_target="tpu_custom_call" | custom-call | flops 4000000000 | bytes 8000000 | tf_op jit(solution)/shard_map/forward/pallas_call | solution.py:411
  48.8 0.9 %backward.11 = (bf16[256,128]{1,0:T(8,128)(2,1)S(1)}, bf16[256,128]{1,0:T(8,128)(2,1)S(1)}) custom-call(s32[8,128]{1,0:T(8,128)S(4)} %get-tuple-element.50.slots, bf16[256,128]{1,0:T(8,128)(2,1)S(1)} %collective-permute-done.18.refs_1_.refs_0_, s32[544,128]{1,0:T(8,128)S(1)} %get-tuple-element.54.refs_1_, f32[544,128]{1,0:T(8,128)S(1)} %get-tuple-element.55.refs_2_, ...), custom_call_target="tpu_custom_call" | custom-call | flops 4000000000 | bytes 8000000 | tf_op jit(solution)/shard_map/backward/pallas_call | solution.py:411
  49.7 0.7 %collective-permute-start.20 = (bf16[256,128]{1,0:T(8,128)(2,1)S(1)}, bf16[256,128]{1,0:T(8,128)(2,1)S(1)}, u32[]{:S(2)}, u32[]{:S(2)}) collective-permute-start(bf16[256,128]{1,0:T(8,128)(2,1)S(1)} %get-tuple-element.67), channel_id=1, source_target_pairs={{0,3},{1,4},{2,7},{3,0},{4,1},{5,6},{6,5},{7,2},{8,13},{9,10},{10,... | collective-permute-start | bytes 196616 | tf_op jit(solution)/shard_map/ppermute | solution.py:426
  50.4 1.1 %collective-permute-start.19 = (bf16[256,128]{1,0:T(8,128)(2,1)S(1)}, bf16[256,128]{1,0:T(8,128)(2,1)S(1)}, u32[]{:S(2)}, u32[]{:S(2)}) collective-permute-start(bf16[256,128]{1,0:T(8,128)(2,1)S(1)} %get-tuple-element.65), channel_id=1, source_target_pairs={{0,3},{1,4},{2,7},{3,0},{4,1},{5,6},{6,5},{7,2},{8,13},{9,10},{10,... | collective-permute-start | bytes 196616 | tf_op jit(solution)/shard_map/ppermute | solution.py:426
  51.6 1.7 %backward.9.sum_ref = f32[512,128]{1,0:T(8,128)S(1)} custom-call(s32[8,128]{1,0:T(8,128)S(4)} %get-tuple-element.38.slots, bf16[256,128]{1,0:T(8,128)(2,1)S(1)} %residual.3.refs_0_, bf16[256,128]{1,0:T(8,128)(2,1)S(1)} %collective-permute-done.18.refs_1_.refs_0_, s32[544,128]{1,0:T(8,128)S(1)} %get-tuple-element.51.refs_2_, ...), custom_call_target="tpu_custom_call" | custom-call | flops 4000000000 | bytes 8000000 | tf_op jit(solution)/shard_map/backward/pallas_call | solution.py:411
  54.2 2.1 %collective-permute-start.22 = (bf16[128,128]{1,0:T(8,128)(2,1)S(1)}, bf16[128,128]{1,0:T(8,128)(2,1)S(1)}, u32[]{:S(2)}, u32[]{:S(2)}) collective-permute-start(bf16[128,128]{1,0:T(8,128)(2,1)S(1)} %get-tuple-element.69), channel_id=1, source_target_pairs={{0,12},{1,11},{2,8},{3,15},{4,14},{5,9},{6,10},{7,13},{8,2},{9,5},... | collective-permute-start | bytes 98312 | tf_op jit(solution)/shard_map/ppermute | solution.py:426
  56.6 1.2 %collective-permute-done.21.refs_1_ = bf16[128,128]{1,0:T(8,128)(2,1)S(1)} collective-permute-done((bf16[128,128]{1,0:T(8,128)(2,1)S(1)}, bf16[128,128]{1,0:T(8,128)(2,1)S(1)}, u32[]{:S(2)}, u32[]{:S(2)}) %collective-permute-start.21) | collective-permute-done | bytes 32800 | tf_op jit(solution)/shard_map/ppermute | solution.py:426
  57.8 2.2 %collective-permute-done.22.refs_2_ = bf16[128,128]{1,0:T(8,128)(2,1)S(1)} collective-permute-done((bf16[128,128]{1,0:T(8,128)(2,1)S(1)}, bf16[128,128]{1,0:T(8,128)(2,1)S(1)}, u32[]{:S(2)}, u32[]{:S(2)}) %collective-permute-start.22) | collective-permute-done | bytes 32800 | tf_op jit(solution)/shard_map/ppermute | solution.py:426
  (54 shorter events, 9.5 us)
Async XLA Ops:
  1.0 9.3 %collective-permute-start = (bf16[192,128]{1,0:T(8,128)(2,1)S(1)}, bf16[192,128]{1,0:T(8,128)(2,1)S(1)}, u32[]{:S(2)}, u32[]{:S(2)}) collective-permute-start(bf16[192,128]{1,0:T(8,128)(2,1)S(1)} %pack.1.refs_0_), channel_id=1, source_target_pairs={{0,9},{1,2},{2,1},{3,10},{4,7},{5,12},{6,15},{7,4},{8,11},{9,0},{1... | collective-permute-start | bytes 147464 | tf_op jit(solution)/shard_map/ppermute | solution.py:426
  4.6 5.8 %collective-permute-start.1 = (bf16[192,128]{1,0:T(8,128)(2,1)S(1)}, bf16[192,128]{1,0:T(8,128)(2,1)S(1)}, u32[]{:S(2)}, u32[]{:S(2)}) collective-permute-start(bf16[192,128]{1,0:T(8,128)(2,1)S(1)} %pack.1.refs_0_), channel_id=1, source_target_pairs={{0,5},{1,8},{2,11},{3,6},{4,13},{5,0},{6,3},{7,14},{8,1},{9,12},{1... | collective-permute-start | bytes 147464 | tf_op jit(solution)/shard_map/ppermute | solution.py:426
  6.4 5.9 %collective-permute-start.2 = (bf16[192,128]{1,0:T(8,128)(2,1)S(1)}, bf16[192,128]{1,0:T(8,128)(2,1)S(1)}, u32[]{:S(2)}, u32[]{:S(2)}) collective-permute-start(bf16[192,128]{1,0:T(8,128)(2,1)S(1)} %pack.1.refs_0_), channel_id=1, source_target_pairs={{0,12},{1,11},{2,8},{3,15},{4,14},{5,9},{6,10},{7,13},{8,2},{9,5},... | collective-permute-start | bytes 147464 | tf_op jit(solution)/shard_map/ppermute | solution.py:426
  6.5 9.6 %collective-permute-start.4 = (bf16[192,128]{1,0:T(8,128)(2,1)S(1)}, bf16[192,128]{1,0:T(8,128)(2,1)S(1)}, u32[]{:S(2)}, u32[]{:S(2)}) collective-permute-start(bf16[192,128]{1,0:T(8,128)(2,1)S(1)} %pack.1.refs_0_), channel_id=1, source_target_pairs={{0,15},{1,14},{2,13},{3,12},{4,11},{5,10},{6,9},{7,8},{8,7},{9,6},... | collective-permute-start | bytes 147464 | tf_op jit(solution)/shard_map/ppermute | solution.py:426
  10.4 5.6 %collective-permute-start.3 = (bf16[576,128]{1,0:T(8,128)(2,1)S(1)}, bf16[576,128]{1,0:T(8,128)(2,1)S(1)}, u32[]{:S(2)}, u32[]{:S(2)}) collective-permute-start(bf16[576,128]{1,0:T(8,128)(2,1)S(1)} %join.2.refs_0_), channel_id=1, source_target_pairs={{0,3},{1,4},{2,7},{3,0},{4,1},{5,6},{6,5},{7,2},{8,13},{9,10},{10,... | collective-permute-start | bytes 442376 | tf_op jit(solution)/shard_map/ppermute | solution.py:426
  18.8 1.4 %collective-permute-start.5 = (f32[288,128]{1,0:T(8,128)S(1)}, f32[288,128]{1,0:T(8,128)S(1)}, u32[]{:S(2)}, u32[]{:S(2)}) collective-permute-start(f32[288,128]{1,0:T(8,128)S(1)} %forward.8), channel_id=1, source_target_pairs={{0,1},{1,0},{2,3},{3,2},{4,5},{5,4},{6,7},{7,6},{8,9},{9,8},{10,11... | collective-permute-start | bytes 442376 | tf_op jit(solution)/shard_map/ppermute | solution.py:426
  18.8 1.4 %copy-start.1 = (bf16[32,8,128]{2,1,0:T(8,128)(2,1)S(1)}, bf16[32,8,128]{2,1,0:T(8,128)(2,1)}, u32[]{:S(2)}) copy-start(bf16[32,8,128]{2,1,0:T(8,128)(2,1)} %param.7) | copy-start | bytes 196612
  20.2 1.3 %collective-permute-start.6 = (bf16[256,128]{1,0:T(8,128)(2,1)S(1)}, bf16[256,128]{1,0:T(8,128)(2,1)S(1)}, u32[]{:S(2)}, u32[]{:S(2)}) collective-permute-start(bf16[256,128]{1,0:T(8,128)(2,1)S(1)} %residual.2.refs_0_), channel_id=1, source_target_pairs={{0,1},{1,0},{2,3},{3,2},{4,5},{5,4},{6,7},{7,6},{8,9},{9,8},{10,11... | collective-permute-start | bytes 196616 | tf_op jit(solution)/shard_map/ppermute | solution.py:426
  22.5 4.4 %collective-permute-start.8 = (bf16[256,128]{1,0:T(8,128)(2,1)S(1)}, bf16[256,128]{1,0:T(8,128)(2,1)S(1)}, u32[]{:S(2)}, u32[]{:S(2)}) collective-permute-start(bf16[256,128]{1,0:T(8,128)(2,1)S(1)} %get-tuple-element.59), channel_id=1, source_target_pairs={{0,3},{1,4},{2,7},{3,0},{4,1},{5,6},{6,5},{7,2},{8,13},{9,10},{10,... | collective-permute-start | bytes 196616 | tf_op jit(solution)/shard_map/ppermute | solution.py:426
  24.9 4.3 %collective-permute-start.7 = (bf16[256,128]{1,0:T(8,128)(2,1)S(1)}, bf16[256,128]{1,0:T(8,128)(2,1)S(1)}, u32[]{:S(2)}, u32[]{:S(2)}) collective-permute-start(bf16[256,128]{1,0:T(8,128)(2,1)S(1)} %get-tuple-element.57), channel_id=1, source_target_pairs={{0,3},{1,4},{2,7},{3,0},{4,1},{5,6},{6,5},{7,2},{8,13},{9,10},{10,... | collective-permute-start | bytes 196616 | tf_op jit(solution)/shard_map/ppermute | solution.py:426
  26.9 5.8 %collective-permute-start.10 = (bf16[128,128]{1,0:T(8,128)(2,1)S(1)}, bf16[128,128]{1,0:T(8,128)(2,1)S(1)}, u32[]{:S(2)}, u32[]{:S(2)}) collective-permute-start(bf16[128,128]{1,0:T(8,128)(2,1)S(1)} %get-tuple-element.61), channel_id=1, source_target_pairs={{0,12},{1,11},{2,8},{3,15},{4,14},{5,9},{6,10},{7,13},{8,2},{9,5},... | collective-permute-start | bytes 98312 | tf_op jit(solution)/shard_map/ppermute | solution.py:426
  29.2 2.0 %copy-start.2 = (f32[256,4]{0,1:T(4,128)S(1)}, f32[256,4]{0,1:T(4,128)}, u32[]{:S(2)}) copy-start(f32[256,4]{0,1:T(4,128)} %param.13) | copy-start | bytes 12292
  29.2 2.0 %copy-start.3 = (f32[256,4]{0,1:T(4,128)S(1)}, f32[256,4]{0,1:T(4,128)}, u32[]{:S(2)}) copy-start(f32[256,4]{0,1:T(4,128)} %param.12) | copy-start | bytes 12292
  29.2 2.0 %copy-start.4 = (s32[256,4]{0,1:T(4,128)S(1)}, s32[256,4]{0,1:T(4,128)}, u32[]{:S(2)}) copy-start(s32[256,4]{0,1:T(4,128)} %param.9) | copy-start | bytes 12292
  29.2 4.6 %collective-permute-start.9 = (bf16[128,128]{1,0:T(8,128)(2,1)S(1)}, bf16[128,128]{1,0:T(8,128)(2,1)S(1)}, u32[]{:S(2)}, u32[]{:S(2)}) collective-permute-start(bf16[128,128]{1,0:T(8,128)(2,1)S(1)} %get-tuple-element.60), channel_id=1, source_target_pairs={{0,9},{1,2},{2,1},{3,10},{4,7},{5,12},{6,15},{7,4},{8,11},{9,0},{1... | collective-permute-start | bytes 98312 | tf_op jit(solution)/shard_map/ppermute | solution.py:426
  29.2 1.9 %copy-start.5 = (s32[16]{0:T(128)S(1)}, s32[16]{0:T(128)}, u32[]{:S(2)}) copy-start(s32[16]{0:T(128)} %param.11) | copy-start | bytes 196
  29.3 4.5 %copy-start = (f32[16,8,128]{2,1,0:T(8,128)S(1)}, f32[16,8,128]{2,1,0:T(8,128)}, u32[]{:S(2)}) copy-start(f32[16,8,128]{2,1,0:T(8,128)} %param.8) | copy-start | bytes 196612
  29.3 4.5 %collective-permute-start.11 = (bf16[128,128]{1,0:T(8,128)(2,1)S(1)}, bf16[128,128]{1,0:T(8,128)(2,1)S(1)}, u32[]{:S(2)}, u32[]{:S(2)}) collective-permute-start(bf16[128,128]{1,0:T(8,128)(2,1)S(1)} %get-tuple-element.62), channel_id=1, source_target_pairs={{0,5},{1,8},{2,11},{3,6},{4,13},{5,0},{6,3},{7,14},{8,1},{9,12},{1... | collective-permute-start | bytes 98312 | tf_op jit(solution)/shard_map/ppermute | solution.py:426
  33.8 6.3 %collective-permute-start.12 = (bf16[128,128]{1,0:T(8,128)(2,1)S(1)}, bf16[128,128]{1,0:T(8,128)(2,1)S(1)}, u32[]{:S(2)}, u32[]{:S(2)}) collective-permute-start(bf16[128,128]{1,0:T(8,128)(2,1)S(1)} %get-tuple-element.64.refs_0_), channel_id=1, source_target_pairs={{0,9},{1,2},{2,1},{3,10},{4,7},{5,12},{6,15},{7,4},{8,11},{9,0},{1... | collective-permute-start | bytes 98312 | tf_op jit(solution)/shard_map/ppermute | solution.py:426
  35.7 4.4 %collective-permute-start.13 = (bf16[128,128]{1,0:T(8,128)(2,1)S(1)}, bf16[128,128]{1,0:T(8,128)(2,1)S(1)}, u32[]{:S(2)}, u32[]{:S(2)}) collective-permute-start(bf16[128,128]{1,0:T(8,128)(2,1)S(1)} %get-tuple-element.64.refs_0_), channel_id=1, source_target_pairs={{0,5},{1,8},{2,11},{3,6},{4,13},{5,0},{6,3},{7,14},{8,1},{9,12},{1... | collective-permute-start | bytes 98312 | tf_op jit(solution)/shard_map/ppermute | solution.py:426
  36.3 5.7 %collective-permute-start.16 = (bf16[128,128]{1,0:T(8,128)(2,1)S(1)}, bf16[128,128]{1,0:T(8,128)(2,1)S(1)}, u32[]{:S(2)}, u32[]{:S(2)}) collective-permute-start(bf16[128,128]{1,0:T(8,128)(2,1)S(1)} %get-tuple-element.64.refs_0_), channel_id=1, source_target_pairs={{0,12},{1,11},{2,8},{3,15},{4,14},{5,9},{6,10},{7,13},{8,2},{9,5},... | collective-permute-start | bytes 98312 | tf_op jit(solution)/shard_map/ppermute | solution.py:426
  38.0 6.5 %collective-permute-start.15 = (bf16[128,128]{1,0:T(8,128)(2,1)S(1)}, bf16[128,128]{1,0:T(8,128)(2,1)S(1)}, u32[]{:S(2)}, u32[]{:S(2)}) collective-permute-start(bf16[128,128]{1,0:T(8,128)(2,1)S(1)} %get-tuple-element.64.refs_0_), channel_id=1, source_target_pairs={{0,15},{1,14},{2,13},{3,12},{4,11},{5,10},{6,9},{7,8},{8,7},{9,6},... | collective-permute-start | bytes 98312 | tf_op jit(solution)/shard_map/ppermute | solution.py:426
  40.1 4.8 %collective-permute-start.14 = (bf16[384,128]{1,0:T(8,128)(2,1)S(1)}, bf16[384,128]{1,0:T(8,128)(2,1)S(1)}, u32[]{:S(2)}, u32[]{:S(2)}) collective-permute-start(bf16[384,128]{1,0:T(8,128)(2,1)S(1)} %join.3.refs_0_), channel_id=1, source_target_pairs={{0,3},{1,4},{2,7},{3,0},{4,1},{5,6},{6,5},{7,2},{8,13},{9,10},{10,... | collective-permute-start | bytes 294920 | tf_op jit(solution)/shard_map/ppermute | solution.py:426
  46.1 1.4 %collective-permute-start.17 = (f32[256,128]{1,0:T(8,128)S(1)}, f32[256,128]{1,0:T(8,128)S(1)}, u32[]{:S(2)}, u32[]{:S(2)}) collective-permute-start(f32[256,128]{1,0:T(8,128)S(1)} %forward.11), channel_id=1, source_target_pairs={{0,1},{1,0},{2,3},{3,2},{4,5},{5,4},{6,7},{7,6},{8,9},{9,8},{10,11... | collective-permute-start | bytes 393224 | tf_op jit(solution)/shard_map/ppermute | solution.py:426
  47.5 1.3 %collective-permute-start.18 = (bf16[256,128]{1,0:T(8,128)(2,1)S(1)}, bf16[256,128]{1,0:T(8,128)(2,1)S(1)}, u32[]{:S(2)}, u32[]{:S(2)}) collective-permute-start(bf16[256,128]{1,0:T(8,128)(2,1)S(1)} %residual.3.refs_0_), channel_id=1, source_target_pairs={{0,1},{1,0},{2,3},{3,2},{4,5},{5,4},{6,7},{7,6},{8,9},{9,8},{10,11... | collective-permute-start | bytes 196616 | tf_op jit(solution)/shard_map/ppermute | solution.py:426
  49.7 3.8 %collective-permute-start.20 = (bf16[256,128]{1,0:T(8,128)(2,1)S(1)}, bf16[256,128]{1,0:T(8,128)(2,1)S(1)}, u32[]{:S(2)}, u32[]{:S(2)}) collective-permute-start(bf16[256,128]{1,0:T(8,128)(2,1)S(1)} %get-tuple-element.67), channel_id=1, source_target_pairs={{0,3},{1,4},{2,7},{3,0},{4,1},{5,6},{6,5},{7,2},{8,13},{9,10},{10,... | collective-permute-start | bytes 196616 | tf_op jit(solution)/shard_map/ppermute | solution.py:426
  50.4 5.8 %collective-permute-start.19 = (bf16[256,128]{1,0:T(8,128)(2,1)S(1)}, bf16[256,128]{1,0:T(8,128)(2,1)S(1)}, u32[]{:S(2)}, u32[]{:S(2)}) collective-permute-start(bf16[256,128]{1,0:T(8,128)(2,1)S(1)} %get-tuple-element.65), channel_id=1, source_target_pairs={{0,3},{1,4},{2,7},{3,0},{4,1},{5,6},{6,5},{7,2},{8,13},{9,10},{10,... | collective-permute-start | bytes 196616 | tf_op jit(solution)/shard_map/ppermute | solution.py:426
  53.5 4.3 %collective-permute-start.21 = (bf16[128,128]{1,0:T(8,128)(2,1)S(1)}, bf16[128,128]{1,0:T(8,128)(2,1)S(1)}, u32[]{:S(2)}, u32[]{:S(2)}) collective-permute-start(bf16[128,128]{1,0:T(8,128)(2,1)S(1)} %get-tuple-element.68), channel_id=1, source_target_pairs={{0,9},{1,2},{2,1},{3,10},{4,7},{5,12},{6,15},{7,4},{8,11},{9,0},{1... | collective-permute-start | bytes 98312 | tf_op jit(solution)/shard_map/ppermute | solution.py:426
  54.2 5.8 %collective-permute-start.22 = (bf16[128,128]{1,0:T(8,128)(2,1)S(1)}, bf16[128,128]{1,0:T(8,128)(2,1)S(1)}, u32[]{:S(2)}, u32[]{:S(2)}) collective-permute-start(bf16[128,128]{1,0:T(8,128)(2,1)S(1)} %get-tuple-element.69), channel_id=1, source_target_pairs={{0,12},{1,11},{2,8},{3,15},{4,14},{5,9},{6,10},{7,13},{8,2},{9,5},... | collective-permute-start | bytes 98312 | tf_op jit(solution)/shard_map/ppermute | solution.py:426
  56.3 4.5 %collective-permute-start.23 = (bf16[128,128]{1,0:T(8,128)(2,1)S(1)}, bf16[128,128]{1,0:T(8,128)(2,1)S(1)}, u32[]{:S(2)}, u32[]{:S(2)}) collective-permute-start(bf16[128,128]{1,0:T(8,128)(2,1)S(1)} %get-tuple-element.70), channel_id=1, source_target_pairs={{0,5},{1,8},{2,11},{3,6},{4,13},{5,0},{6,3},{7,14},{8,1},{9,12},{1... | collective-permute-start | bytes 98312 | tf_op jit(solution)/shard_map/ppermute | solution.py:426

commit v24 on v23

--- a/solution.py
+++ b/solution.py
@@ -254,6 +254,10 @@
 
 def for_rows(rows, body):
     step = 128
+    if rows <= 8 * step:
+        for start in range(0, rows, step):
+            body(pl.ds(start, step))
+        return
 
     def some(number, carry):
         body(pl.ds(pl.multiple_of(number * step, step), step))
@@ -277,12 +281,20 @@
     base = 0
     for ref in value_refs:
         def widen(member, carry, ref=ref, base=base):
-            at = pl.ds(pl.multiple_of((base + member) * rows, rows), rows)
-            wide[at, :] = ref[pl.ds(pl.multiple_of(member * stride, 16), rows), :].astype(F32)
+            at = (base + member) * rows
+            start = member * stride
+            if not isinstance(member, int):
+                at, start = pl.multiple_of(at, rows), pl.multiple_of(start, 16)
+            wide[pl.ds(at, rows), :] = ref[pl.ds(start, rows), :].astype(F32)
             return carry
 
-        lax.fori_loop(0, ref.shape[0] // stride, widen, 0)
-        base += ref.shape[0] // stride
+        here = ref.shape[0] // stride
+        if here <= 8:
+            for member in range(here):
+                widen(member, 0)
+        else:
+            lax.fori_loop(0, here, widen, 0)
+        base += here
     second[...] = jnp.zeros_like(second)
     if start_ref is None:
         out_ref[...] = jnp.zeros_like(out_ref)

time: 61.8 us -> 61.1 us (0.989); the launches traced: 61.4 us -> 61.4 us
  Pallas kernels: 20.2 us -> 21.3 us
  starting transfers between devices: 30.5 us -> 29.5 us
    pallas_call x26, Pallas kernels: 20.2 us -> 21.3 us  [call(): pl.pallas_call(kernel, out_shape=out_shape, in_specs=in_specs, out_specs=...]
    ppermute x24, starting transfers between devices: 30.5 us -> 29.5 us  [exchange(): lax.ppermute(values, 'slab', [(device, device ^ far[device.bit_count() %...]
where the time goes in v24:
time: 61.1 us; the launch traced here: 61.4 us
  starting transfers between devices  29.5 us (48%)
  Pallas kernels  21.3 us (35%)
  waiting for transfers between devices  10.4 us (17%)
    ppermute x24, starting transfers between devices, exchange(): lax.ppermute(values, 'slab', [(device, device ^ far[device.bit_count() %...  29.5 us
    pallas_call x26, Pallas kernels, call(): pl.pallas_call(kernel, out_shape=out_shape, in_specs=in_specs, out_specs=...  21.3 us
    ppermute x24, waiting for transfers between devices, exchange(): lax.ppermute(values, 'slab', [(device, device ^ far[device.bit_count() %...  10.4 us
  transfers between devices with their start and end apart: 24, of which 15 were waited for; matrix products, arithmetic and copies ran while one was open for 0% of the time, Pallas kernels for 21%

profile of v24, /device:TPU:0, one launch (start us, length us, event | category | flops | bytes accessed | tf_op | source)
XLA Modules:
  0.0 61.4 jit_solution(15437797571001306969)
XLA Ops:
  0.0 1.0 %pack.1.refs_0_ = bf16[192,128]{1,0:T(8,128)(2,1)S(1)} custom-call(f32[128,128]{1,0:T(8,128)} %bitcast.8, f32[4,256]{1,0:T(4,128)} %bitcast.12, f32[4,256]{1,0:T(4,128)} %bitcast.14, s32[4,256]{1,0:T(4,128)} %bitcast.16, s32[1,256]{1,0:T(1,128)} %bitcast.20, s32[1,16]{1,0:T(1,128)} %bitcast.18), custom_call_target="tpu_custom_call" | custom-call | flops 4000000000 | bytes 8000000 | tf_op jit(solution)/shard_map/pack/pallas_call | solution.py:423
  1.0 3.5 %collective-permute-start = (bf16[192,128]{1,0:T(8,128)(2,1)S(1)}, bf16[192,128]{1,0:T(8,128)(2,1)S(1)}, u32[]{:S(2)}, u32[]{:S(2)}) collective-permute-start(bf16[192,128]{1,0:T(8,128)(2,1)S(1)} %pack.1.refs_0_), channel_id=1, source_target_pairs={{0,9},{1,2},{2,1},{3,10},{4,7},{5,12},{6,15},{7,4},{8,11},{9,0},{1... | collective-permute-start | bytes 147464 | tf_op jit(solution)/shard_map/ppermute | solution.py:438
  4.6 1.9 %collective-permute-start.1 = (bf16[192,128]{1,0:T(8,128)(2,1)S(1)}, bf16[192,128]{1,0:T(8,128)(2,1)S(1)}, u32[]{:S(2)}, u32[]{:S(2)}) collective-permute-start(bf16[192,128]{1,0:T(8,128)(2,1)S(1)} %pack.1.refs_0_), channel_id=1, source_target_pairs={{0,5},{1,8},{2,11},{3,6},{4,13},{5,0},{6,3},{7,14},{8,1},{9,12},{1... | collective-permute-start | bytes 147464 | tf_op jit(solution)/shard_map/ppermute | solution.py:438
  6.5 3.9 %collective-permute-start.4 = (bf16[192,128]{1,0:T(8,128)(2,1)S(1)}, bf16[192,128]{1,0:T(8,128)(2,1)S(1)}, u32[]{:S(2)}, u32[]{:S(2)}) collective-permute-start(bf16[192,128]{1,0:T(8,128)(2,1)S(1)} %pack.1.refs_0_), channel_id=1, source_target_pairs={{0,15},{1,14},{2,13},{3,12},{4,11},{5,10},{6,9},{7,8},{8,7},{9,6},... | collective-permute-start | bytes 147464 | tf_op jit(solution)/shard_map/ppermute | solution.py:438
  10.4 1.1 %collective-permute-start.3 = (bf16[576,128]{1,0:T(8,128)(2,1)S(1)}, bf16[576,128]{1,0:T(8,128)(2,1)S(1)}, u32[]{:S(2)}, u32[]{:S(2)}) collective-permute-start(bf16[576,128]{1,0:T(8,128)(2,1)S(1)} %join.2.refs_0_), channel_id=1, source_target_pairs={{0,3},{1,4},{2,7},{3,0},{4,1},{5,6},{6,5},{7,2},{8,13},{9,10},{10,... | collective-permute-start | bytes 442376 | tf_op jit(solution)/shard_map/ppermute | solution.py:438
  12.3 1.5 %setup.2 = (s32[8,128]{1,0:T(8,128)S(4)}, f32[64,128]{1,0:T(8,128)S(1)}, s32[544,128]{1,0:T(8,128)S(1)}, f32[544,128]{1,0:T(8,128)S(1)}, f32[544,128]{1,0:T(8,12...) custom-call(bf16[576,128]{1,0:T(8,128)(2,1)S(1)} %join.2.refs_0_, ...), custom_call_target="tpu_custom_call" | custom-call | flops 4000000000 | bytes 8000000 | tf_op jit(solution)/shard_map/setup/pallas_call | solution.py:423
  13.8 1.8 %forward.6.refs_2_.refs_6_ = f32[512,128]{1,0:T(8,128)S(1)} custom-call(s32[8,128]{1,0:T(8,128)S(4)} %get-tuple-element.38.slots, bf16[576,128]{1,0:T(8,128)(2,1)S(1)} %join.2.refs_0_, bf16[192,128]{1,0:T(8,128)(2,1)S(1)} %collective-permute-done.2.refs_1_, s32[544,128]{1,0:T(8,128)S(1)} %get-tuple-element.39.refs_2_, ...), custom_call_target="tpu_custom_call" | custom-call | flops 4000000000 | bytes 8000000 | tf_op jit(solution)/shard_map/forward/pallas_call | solution.py:423
  15.7 1.6 %setup.3 = (s32[8,128]{1,0:T(8,128)S(4)}, s32[8,128]{1,0:T(8,128)S(4)}, f32[64,128]{1,0:T(8,128)S(1)}, s32[544,128]{1,0:T(8,128)S(1)}, f32[544,128]{1,0:T(8,128)...) custom-call(bf16[576,128]{1,0:T(8,128)(2,1)S(1)} %collective-permute, ...), custom_call_target="tpu_custom_call" | custom-call | flops 4000000000 | bytes 8000000 | tf_op jit(solution)/shard_map/setup/pallas_call | solution.py:423
  17.3 1.4 %forward.8 = f32[288,128]{1,0:T(8,128)S(1)} custom-call(s32[8,128]{1,0:T(8,128)S(4)} %get-tuple-element.50.slots, bf16[576,128]{1,0:T(8,128)(2,1)S(1)} %collective-permute-done.3.refs_0_, bf16[192,128]{1,0:T(8,128)(2,1)S(1)} %collective-permute-done.4.refs_1_, s32[544,128]{1,0:T(8,128)S(1)} %get-tuple-element.44.refs_2_, ...), custom_call_target="tpu_custom_call" | custom-call | flops 4000000000 | bytes 8000000 | tf_op jit(solution)/shard_map/forward/pallas_call | solution.py:423
  18.8 1.1 %forward.7.projection_ref = f32[256,128]{1,0:T(8,128)S(1)} custom-call(s32[8,128]{1,0:T(8,128)S(4)} %get-tuple-element.43.slots, bf16[576,128]{1,0:T(8,128)(2,1)S(1)} %collective-permute-done.3.refs_0_, bf16[192,128]{1,0:T(8,128)(2,1)S(1)} %collective-permute-done.4.refs_1_, s32[544,128]{1,0:T(8,128)S(1)} %get-tuple-element.44.refs_2_, ...), custom_call_target="tpu_custom_call" | custom-call | flops 4000000000 | bytes 8000000 | tf_op jit(solution)/shard_map/forward/pallas_call | solution.py:423
  20.5 0.9 %backward.7.refs_4_ = f32[512,128]{1,0:T(8,128)S(1)} custom-call(s32[8,128]{1,0:T(8,128)S(4)} %get-tuple-element.43.slots, bf16[256,128]{1,0:T(8,128)(2,1)S(1)} %residual.2.refs_0_, s32[544,128]{1,0:T(8,128)S(1)} %get-tuple-element.54.refs_1_, f32[544,128]{1,0:T(8,128)S(1)} %get-tuple-element.55.refs_2_, f32[544,128]{1,0:T(8,128)S(1)} %get-tuple-element.56.refs_3_), custom_call_target="tpu_custom_call" | custom-call | flops 4000000000 | bytes 8000000 | tf_op jit(solution)/shard_map/backward/pallas_call | solution.py:423
  21.5 1.2 %backward.8 = (bf16[256,128]{1,0:T(8,128)(2,1)S(1)}, bf16[256,128]{1,0:T(8,128)(2,1)S(1)}) custom-call(s32[8,128]{1,0:T(8,128)S(4)} %get-tuple-element.50.slots, bf16[256,128]{1,0:T(8,128)(2,1)S(1)} %collective-permute-done.6.refs_1_.refs_0_, s32[544,128]{1,0:T(8,128)S(1)} %get-tuple-element.54.refs_1_, f32[544,128]{1,0:T(8,128)S(1)} %get-tuple-element.55.refs_2_, ...), custom_call_target="tpu_custom_call" | custom-call | flops 4000000000 | bytes 8000000 | tf_op jit(solution)/shard_map/backward/pallas_call | solution.py:423
  22.7 2.0 %collective-permute-start.8 = (bf16[256,128]{1,0:T(8,128)(2,1)S(1)}, bf16[256,128]{1,0:T(8,128)(2,1)S(1)}, u32[]{:S(2)}, u32[]{:S(2)}) collective-permute-start(bf16[256,128]{1,0:T(8,128)(2,1)S(1)} %get-tuple-element.59), channel_id=1, source_target_pairs={{0,3},{1,4},{2,7},{3,0},{4,1},{5,6},{6,5},{7,2},{8,13},{9,10},{10,... | collective-permute-start | bytes 196616 | tf_op jit(solution)/shard_map/ppermute | solution.py:438
  24.8 1.5 %backward.6.sum_ref = f32[512,128]{1,0:T(8,128)S(1)} custom-call(s32[8,128]{1,0:T(8,128)S(4)} %get-tuple-element.38.slots, bf16[256,128]{1,0:T(8,128)(2,1)S(1)} %residual.2.refs_0_, bf16[256,128]{1,0:T(8,128)(2,1)S(1)} %collective-permute-done.6.refs_1_.refs_0_, s32[544,128]{1,0:T(8,128)S(1)} %get-tuple-element.51.refs_2_, ...), custom_call_target="tpu_custom_call" | custom-call | flops 4000000000 | bytes 8000000 | tf_op jit(solution)/shard_map/backward/pallas_call | solution.py:423
  26.7 1.1 %collective-permute-start.10 = (bf16[128,128]{1,0:T(8,128)(2,1)S(1)}, bf16[128,128]{1,0:T(8,128)(2,1)S(1)}, u32[]{:S(2)}, u32[]{:S(2)}) collective-permute-start(bf16[128,128]{1,0:T(8,128)(2,1)S(1)} %get-tuple-element.61), channel_id=1, source_target_pairs={{0,12},{1,11},{2,8},{3,15},{4,14},{5,9},{6,10},{7,13},{8,2},{9,5},... | collective-permute-start | bytes 98312 | tf_op jit(solution)/shard_map/ppermute | solution.py:438
  27.8 1.0 %collective-permute-start.9 = (bf16[128,128]{1,0:T(8,128)(2,1)S(1)}, bf16[128,128]{1,0:T(8,128)(2,1)S(1)}, u32[]{:S(2)}, u32[]{:S(2)}) collective-permute-start(bf16[128,128]{1,0:T(8,128)(2,1)S(1)} %get-tuple-element.60), channel_id=1, source_target_pairs={{0,9},{1,2},{2,1},{3,10},{4,7},{5,12},{6,15},{7,4},{8,11},{9,0},{1... | collective-permute-start | bytes 98312 | tf_op jit(solution)/shard_map/ppermute | solution.py:438
  28.9 2.1 %collective-permute-start.11 = (bf16[128,128]{1,0:T(8,128)(2,1)S(1)}, bf16[128,128]{1,0:T(8,128)(2,1)S(1)}, u32[]{:S(2)}, u32[]{:S(2)}) collective-permute-start(bf16[128,128]{1,0:T(8,128)(2,1)S(1)} %get-tuple-element.62), channel_id=1, source_target_pairs={{0,5},{1,8},{2,11},{3,6},{4,13},{5,0},{6,3},{7,14},{8,1},{9,12},{1... | collective-permute-start | bytes 98312 | tf_op jit(solution)/shard_map/ppermute | solution.py:438
  31.7 1.1 %collective-permute-done.10.refs_2_ = bf16[128,128]{1,0:T(8,128)(2,1)S(1)} collective-permute-done((bf16[128,128]{1,0:T(8,128)(2,1)S(1)}, bf16[128,128]{1,0:T(8,128)(2,1)S(1)}, u32[]{:S(2)}, u32[]{:S(2)}) %collective-permute-start.10) | collective-permute-done | bytes 32800 | tf_op jit(solution)/shard_map/ppermute | solution.py:438
  33.3 1.0 %collective-permute-start.12 = (bf16[128,128]{1,0:T(8,128)(2,1)S(1)}, bf16[128,128]{1,0:T(8,128)(2,1)S(1)}, u32[]{:S(2)}, u32[]{:S(2)}) collective-permute-start(bf16[128,128]{1,0:T(8,128)(2,1)S(1)} %get-tuple-element.64.refs_0_), channel_id=1, source_target_pairs={{0,9},{1,2},{2,1},{3,10},{4,7},{5,12},{6,15},{7,4},{8,11},{9,0},{1... | collective-permute-start | bytes 98312 | tf_op jit(solution)/shard_map/ppermute | solution.py:438
  34.3 1.0 %collective-permute-start.13 = (bf16[128,128]{1,0:T(8,128)(2,1)S(1)}, bf16[128,128]{1,0:T(8,128)(2,1)S(1)}, u32[]{:S(2)}, u32[]{:S(2)}) collective-permute-start(bf16[128,128]{1,0:T(8,128)(2,1)S(1)} %get-tuple-element.64.refs_0_), channel_id=1, source_target_pairs={{0,5},{1,8},{2,11},{3,6},{4,13},{5,0},{6,3},{7,14},{8,1},{9,12},{1... | collective-permute-start | bytes 98312 | tf_op jit(solution)/shard_map/ppermute | solution.py:438
  35.3 2.2 %collective-permute-start.16 = (bf16[128,128]{1,0:T(8,128)(2,1)S(1)}, bf16[128,128]{1,0:T(8,128)(2,1)S(1)}, u32[]{:S(2)}, u32[]{:S(2)}) collective-permute-start(bf16[128,128]{1,0:T(8,128)(2,1)S(1)} %get-tuple-element.64.refs_0_), channel_id=1, source_target_pairs={{0,12},{1,11},{2,8},{3,15},{4,14},{5,9},{6,10},{7,13},{8,2},{9,5},... | collective-permute-start | bytes 98312 | tf_op jit(solution)/shard_map/ppermute | solution.py:438
  37.5 2.7 %collective-permute-start.15 = (bf16[128,128]{1,0:T(8,128)(2,1)S(1)}, bf16[128,128]{1,0:T(8,128)(2,1)S(1)}, u32[]{:S(2)}, u32[]{:S(2)}) collective-permute-start(bf16[128,128]{1,0:T(8,128)(2,1)S(1)} %get-tuple-element.64.refs_0_), channel_id=1, source_target_pairs={{0,15},{1,14},{2,13},{3,12},{4,11},{5,10},{6,9},{7,8},{8,7},{9,6},... | collective-permute-start | bytes 98312 | tf_op jit(solution)/shard_map/ppermute | solution.py:438
  41.2 1.8 %forward.9.refs_6_ = f32[512,128]{1,0:T(8,128)S(1)} custom-call(s32[8,128]{1,0:T(8,128)S(4)} %get-tuple-element.38.slots, bf16[384,128]{1,0:T(8,128)(2,1)S(1)} %join.3.refs_0_, bf16[128,128]{1,0:T(8,128)(2,1)S(1)} %collective-permute-done.16.refs_1_, s32[544,128]{1,0:T(8,128)S(1)} %get-tuple-element.39.refs_2_, f32[544,128]{1,0:T(8,128)S(1)} %get-tuple-element.40.refs_3_, ...), custom_call_target="tpu_custom_call" | custom-call | flops 4000000000 | bytes 8000000 | tf_op jit(solution)/shard_map/forward/pallas_call | solution.py:423
  43.6 1.4 %collective-permute-done.14.refs_0_ = bf16[384,128]{1,0:T(8,128)(2,1)S(1)} collective-permute-done((bf16[384,128]{1,0:T(8,128)(2,1)S(1)}, bf16[384,128]{1,0:T(8,128)(2,1)S(1)}, u32[]{:S(2)}, u32[]{:S(2)}) %collective-permute-start.14) | collective-permute-done | bytes 98336 | tf_op jit(solution)/shard_map/ppermute | solution.py:438
  44.9 1.4 %forward.11 = f32[256,128]{1,0:T(8,128)S(1)} custom-call(s32[8,128]{1,0:T(8,128)S(4)} %get-tuple-element.50.slots, bf16[384,128]{1,0:T(8,128)(2,1)S(1)} %collective-permute-done.14.refs_0_, bf16[128,128]{1,0:T(8,128)(2,1)S(1)} %collective-permute-done.15.refs_1_, s32[544,128]{1,0:T(8,128)S(1)} %get-tuple-element.44.refs_2_, ...), custom_call_target="tpu_custom_call" | custom-call | flops 4000000000 | bytes 8000000 | tf_op jit(solution)/shard_map/forward/pallas_call | solution.py:423
  46.5 1.1 %forward.10.projection_ref = f32[256,128]{1,0:T(8,128)S(1)} custom-call(s32[8,128]{1,0:T(8,128)S(4)} %get-tuple-element.43.slots, bf16[384,128]{1,0:T(8,128)(2,1)S(1)} %collective-permute-done.14.refs_0_, bf16[128,128]{1,0:T(8,128)(2,1)S(1)} %collective-permute-done.15.refs_1_, s32[544,128]{1,0:T(8,128)S(1)} %get-tuple-element.44.refs_2_, ...), custom_call_target="tpu_custom_call" | custom-call | flops 4000000000 | bytes 8000000 | tf_op jit(solution)/shard_map/forward/pallas_call | solution.py:423
  49.1 1.2 %backward.11 = (bf16[256,128]{1,0:T(8,128)(2,1)S(1)}, bf16[256,128]{1,0:T(8,128)(2,1)S(1)}) custom-call(s32[8,128]{1,0:T(8,128)S(4)} %get-tuple-element.50.slots, bf16[256,128]{1,0:T(8,128)(2,1)S(1)} %collective-permute-done.18.refs_1_.refs_0_, s32[544,128]{1,0:T(8,128)S(1)} %get-tuple-element.54.refs_1_, f32[544,128]{1,0:T(8,128)S(1)} %get-tuple-element.55.refs_2_, ...), custom_call_target="tpu_custom_call" | custom-call | flops 4000000000 | bytes 8000000 | tf_op jit(solution)/shard_map/backward/pallas_call | solution.py:423
  50.4 1.7 %collective-permute-start.19 = (bf16[256,128]{1,0:T(8,128)(2,1)S(1)}, bf16[256,128]{1,0:T(8,128)(2,1)S(1)}, u32[]{:S(2)}, u32[]{:S(2)}) collective-permute-start(bf16[256,128]{1,0:T(8,128)(2,1)S(1)} %get-tuple-element.65), channel_id=1, source_target_pairs={{0,3},{1,4},{2,7},{3,0},{4,1},{5,6},{6,5},{7,2},{8,13},{9,10},{10,... | collective-permute-start | bytes 196616 | tf_op jit(solution)/shard_map/ppermute | solution.py:438
  52.1 1.5 %backward.9.sum_ref = f32[512,128]{1,0:T(8,128)S(1)} custom-call(s32[8,128]{1,0:T(8,128)S(4)} %get-tuple-element.38.slots, bf16[256,128]{1,0:T(8,128)(2,1)S(1)} %residual.3.refs_0_, bf16[256,128]{1,0:T(8,128)(2,1)S(1)} %collective-permute-done.18.refs_1_.refs_0_, s32[544,128]{1,0:T(8,128)S(1)} %get-tuple-element.51.refs_2_, ...), custom_call_target="tpu_custom_call" | custom-call | flops 4000000000 | bytes 8000000 | tf_op jit(solution)/shard_map/backward/pallas_call | solution.py:423
  54.2 2.1 %collective-permute-start.22 = (bf16[128,128]{1,0:T(8,128)(2,1)S(1)}, bf16[128,128]{1,0:T(8,128)(2,1)S(1)}, u32[]{:S(2)}, u32[]{:S(2)}) collective-permute-start(bf16[128,128]{1,0:T(8,128)(2,1)S(1)} %get-tuple-element.69), channel_id=1, source_target_pairs={{0,12},{1,11},{2,8},{3,15},{4,14},{5,9},{6,10},{7,13},{8,2},{9,5},... | collective-permute-start | bytes 98312 | tf_op jit(solution)/shard_map/ppermute | solution.py:438
  57.2 1.4 %collective-permute-done.21.refs_1_ = bf16[128,128]{1,0:T(8,128)(2,1)S(1)} collective-permute-done((bf16[128,128]{1,0:T(8,128)(2,1)S(1)}, bf16[128,128]{1,0:T(8,128)(2,1)S(1)}, u32[]{:S(2)}, u32[]{:S(2)}) %collective-permute-start.21) | collective-permute-done | bytes 32800 | tf_op jit(solution)/shard_map/ppermute | solution.py:438
  58.6 1.5 %collective-permute-done.22.refs_2_ = bf16[128,128]{1,0:T(8,128)(2,1)S(1)} collective-permute-done((bf16[128,128]{1,0:T(8,128)(2,1)S(1)}, bf16[128,128]{1,0:T(8,128)(2,1)S(1)}, u32[]{:S(2)}, u32[]{:S(2)}) %collective-permute-start.22) | collective-permute-done | bytes 32800 | tf_op jit(solution)/shard_map/ppermute | solution.py:438
  (54 shorter events, 9.5 us)
Async XLA Ops:
  1.0 9.3 %collective-permute-start = (bf16[192,128]{1,0:T(8,128)(2,1)S(1)}, bf16[192,128]{1,0:T(8,128)(2,1)S(1)}, u32[]{:S(2)}, u32[]{:S(2)}) collective-permute-start(bf16[192,128]{1,0:T(8,128)(2,1)S(1)} %pack.1.refs_0_), channel_id=1, source_target_pairs={{0,9},{1,2},{2,1},{3,10},{4,7},{5,12},{6,15},{7,4},{8,11},{9,0},{1... | collective-permute-start | bytes 147464 | tf_op jit(solution)/shard_map/ppermute | solution.py:438
  4.6 5.8 %collective-permute-start.1 = (bf16[192,128]{1,0:T(8,128)(2,1)S(1)}, bf16[192,128]{1,0:T(8,128)(2,1)S(1)}, u32[]{:S(2)}, u32[]{:S(2)}) collective-permute-start(bf16[192,128]{1,0:T(8,128)(2,1)S(1)} %pack.1.refs_0_), channel_id=1, source_target_pairs={{0,5},{1,8},{2,11},{3,6},{4,13},{5,0},{6,3},{7,14},{8,1},{9,12},{1... | collective-permute-start | bytes 147464 | tf_op jit(solution)/shard_map/ppermute | solution.py:438
  6.4 5.9 %collective-permute-start.2 = (bf16[192,128]{1,0:T(8,128)(2,1)S(1)}, bf16[192,128]{1,0:T(8,128)(2,1)S(1)}, u32[]{:S(2)}, u32[]{:S(2)}) collective-permute-start(bf16[192,128]{1,0:T(8,128)(2,1)S(1)} %pack.1.refs_0_), channel_id=1, source_target_pairs={{0,12},{1,11},{2,8},{3,15},{4,14},{5,9},{6,10},{7,13},{8,2},{9,5},... | collective-permute-start | bytes 147464 | tf_op jit(solution)/shard_map/ppermute | solution.py:438
  6.5 9.2 %collective-permute-start.4 = (bf16[192,128]{1,0:T(8,128)(2,1)S(1)}, bf16[192,128]{1,0:T(8,128)(2,1)S(1)}, u32[]{:S(2)}, u32[]{:S(2)}) collective-permute-start(bf16[192,128]{1,0:T(8,128)(2,1)S(1)} %pack.1.refs_0_), channel_id=1, source_target_pairs={{0,15},{1,14},{2,13},{3,12},{4,11},{5,10},{6,9},{7,8},{8,7},{9,6},... | collective-permute-start | bytes 147464 | tf_op jit(solution)/shard_map/ppermute | solution.py:438
  10.4 5.3 %collective-permute-start.3 = (bf16[576,128]{1,0:T(8,128)(2,1)S(1)}, bf16[576,128]{1,0:T(8,128)(2,1)S(1)}, u32[]{:S(2)}, u32[]{:S(2)}) collective-permute-start(bf16[576,128]{1,0:T(8,128)(2,1)S(1)} %join.2.refs_0_), channel_id=1, source_target_pairs={{0,3},{1,4},{2,7},{3,0},{4,1},{5,6},{6,5},{7,2},{8,13},{9,10},{10,... | collective-permute-start | bytes 442376 | tf_op jit(solution)/shard_map/ppermute | solution.py:438
  18.7 1.4 %collective-permute-start.5 = (f32[288,128]{1,0:T(8,128)S(1)}, f32[288,128]{1,0:T(8,128)S(1)}, u32[]{:S(2)}, u32[]{:S(2)}) collective-permute-start(f32[288,128]{1,0:T(8,128)S(1)} %forward.8), channel_id=1, source_target_pairs={{0,1},{1,0},{2,3},{3,2},{4,5},{5,4},{6,7},{7,6},{8,9},{9,8},{10,11... | collective-permute-start | bytes 442376 | tf_op jit(solution)/shard_map/ppermute | solution.py:438
  18.8 1.4 %copy-start.1 = (bf16[32,8,128]{2,1,0:T(8,128)(2,1)S(1)}, bf16[32,8,128]{2,1,0:T(8,128)(2,1)}, u32[]{:S(2)}) copy-start(bf16[32,8,128]{2,1,0:T(8,128)(2,1)} %param.7) | copy-start | bytes 196612
  20.2 1.3 %collective-permute-start.6 = (bf16[256,128]{1,0:T(8,128)(2,1)S(1)}, bf16[256,128]{1,0:T(8,128)(2,1)S(1)}, u32[]{:S(2)}, u32[]{:S(2)}) collective-permute-start(bf16[256,128]{1,0:T(8,128)(2,1)S(1)} %residual.2.refs_0_), channel_id=1, source_target_pairs={{0,1},{1,0},{2,3},{3,2},{4,5},{5,4},{6,7},{7,6},{8,9},{9,8},{10,11... | collective-permute-start | bytes 196616 | tf_op jit(solution)/shard_map/ppermute | solution.py:438
  22.7 4.0 %collective-permute-start.8 = (bf16[256,128]{1,0:T(8,128)(2,1)S(1)}, bf16[256,128]{1,0:T(8,128)(2,1)S(1)}, u32[]{:S(2)}, u32[]{:S(2)}) collective-permute-start(bf16[256,128]{1,0:T(8,128)(2,1)S(1)} %get-tuple-element.59), channel_id=1, source_target_pairs={{0,3},{1,4},{2,7},{3,0},{4,1},{5,6},{6,5},{7,2},{8,13},{9,10},{10,... | collective-permute-start | bytes 196616 | tf_op jit(solution)/shard_map/ppermute | solution.py:438
  24.8 4.1 %collective-permute-start.7 = (bf16[256,128]{1,0:T(8,128)(2,1)S(1)}, bf16[256,128]{1,0:T(8,128)(2,1)S(1)}, u32[]{:S(2)}, u32[]{:S(2)}) collective-permute-start(bf16[256,128]{1,0:T(8,128)(2,1)S(1)} %get-tuple-element.57), channel_id=1, source_target_pairs={{0,3},{1,4},{2,7},{3,0},{4,1},{5,6},{6,5},{7,2},{8,13},{9,10},{10,... | collective-permute-start | bytes 196616 | tf_op jit(solution)/shard_map/ppermute | solution.py:438
  26.7 6.0 %collective-permute-start.10 = (bf16[128,128]{1,0:T(8,128)(2,1)S(1)}, bf16[128,128]{1,0:T(8,128)(2,1)S(1)}, u32[]{:S(2)}, u32[]{:S(2)}) collective-permute-start(bf16[128,128]{1,0:T(8,128)(2,1)S(1)} %get-tuple-element.61), channel_id=1, source_target_pairs={{0,12},{1,11},{2,8},{3,15},{4,14},{5,9},{6,10},{7,13},{8,2},{9,5},... | collective-permute-start | bytes 98312 | tf_op jit(solution)/shard_map/ppermute | solution.py:438
  27.8 3.2 %copy-start.2 = (f32[256,4]{0,1:T(4,128)S(1)}, f32[256,4]{0,1:T(4,128)}, u32[]{:S(2)}) copy-start(f32[256,4]{0,1:T(4,128)} %param.13) | copy-start | bytes 12292
  27.8 3.2 %copy-start.3 = (f32[256,4]{0,1:T(4,128)S(1)}, f32[256,4]{0,1:T(4,128)}, u32[]{:S(2)}) copy-start(f32[256,4]{0,1:T(4,128)} %param.12) | copy-start | bytes 12292
  27.8 3.2 %copy-start.4 = (s32[256,4]{0,1:T(4,128)S(1)}, s32[256,4]{0,1:T(4,128)}, u32[]{:S(2)}) copy-start(s32[256,4]{0,1:T(4,128)} %param.9) | copy-start | bytes 12292
  27.8 5.5 %collective-permute-start.9 = (bf16[128,128]{1,0:T(8,128)(2,1)S(1)}, bf16[128,128]{1,0:T(8,128)(2,1)S(1)}, u32[]{:S(2)}, u32[]{:S(2)}) collective-permute-start(bf16[128,128]{1,0:T(8,128)(2,1)S(1)} %get-tuple-element.60), channel_id=1, source_target_pairs={{0,9},{1,2},{2,1},{3,10},{4,7},{5,12},{6,15},{7,4},{8,11},{9,0},{1... | collective-permute-start | bytes 98312 | tf_op jit(solution)/shard_map/ppermute | solution.py:438
  28.8 2.2 %copy-start.5 = (s32[16]{0:T(128)S(1)}, s32[16]{0:T(128)}, u32[]{:S(2)}) copy-start(s32[16]{0:T(128)} %param.11) | copy-start | bytes 196
  28.9 4.4 %copy-start = (f32[16,8,128]{2,1,0:T(8,128)S(1)}, f32[16,8,128]{2,1,0:T(8,128)}, u32[]{:S(2)}) copy-start(f32[16,8,128]{2,1,0:T(8,128)} %param.8) | copy-start | bytes 196612
  28.9 4.4 %collective-permute-start.11 = (bf16[128,128]{1,0:T(8,128)(2,1)S(1)}, bf16[128,128]{1,0:T(8,128)(2,1)S(1)}, u32[]{:S(2)}, u32[]{:S(2)}) collective-permute-start(bf16[128,128]{1,0:T(8,128)(2,1)S(1)} %get-tuple-element.62), channel_id=1, source_target_pairs={{0,5},{1,8},{2,11},{3,6},{4,13},{5,0},{6,3},{7,14},{8,1},{9,12},{1... | collective-permute-start | bytes 98312 | tf_op jit(solution)/shard_map/ppermute | solution.py:438
  33.3 6.8 %collective-permute-start.12 = (bf16[128,128]{1,0:T(8,128)(2,1)S(1)}, bf16[128,128]{1,0:T(8,128)(2,1)S(1)}, u32[]{:S(2)}, u32[]{:S(2)}) collective-permute-start(bf16[128,128]{1,0:T(8,128)(2,1)S(1)} %get-tuple-element.64.refs_0_), channel_id=1, source_target_pairs={{0,9},{1,2},{2,1},{3,10},{4,7},{5,12},{6,15},{7,4},{8,11},{9,0},{1... | collective-permute-start | bytes 98312 | tf_op jit(solution)/shard_map/ppermute | solution.py:438
  34.3 5.9 %collective-permute-start.13 = (bf16[128,128]{1,0:T(8,128)(2,1)S(1)}, bf16[128,128]{1,0:T(8,128)(2,1)S(1)}, u32[]{:S(2)}, u32[]{:S(2)}) collective-permute-start(bf16[128,128]{1,0:T(8,128)(2,1)S(1)} %get-tuple-element.64.refs_0_), channel_id=1, source_target_pairs={{0,5},{1,8},{2,11},{3,6},{4,13},{5,0},{6,3},{7,14},{8,1},{9,12},{1... | collective-permute-start | bytes 98312 | tf_op jit(solution)/shard_map/ppermute | solution.py:438
  35.3 6.0 %collective-permute-start.16 = (bf16[128,128]{1,0:T(8,128)(2,1)S(1)}, bf16[128,128]{1,0:T(8,128)(2,1)S(1)}, u32[]{:S(2)}, u32[]{:S(2)}) collective-permute-start(bf16[128,128]{1,0:T(8,128)(2,1)S(1)} %get-tuple-element.64.refs_0_), channel_id=1, source_target_pairs={{0,12},{1,11},{2,8},{3,15},{4,14},{5,9},{6,10},{7,13},{8,2},{9,5},... | collective-permute-start | bytes 98312 | tf_op jit(solution)/shard_map/ppermute | solution.py:438
  37.5 6.1 %collective-permute-start.15 = (bf16[128,128]{1,0:T(8,128)(2,1)S(1)}, bf16[128,128]{1,0:T(8,128)(2,1)S(1)}, u32[]{:S(2)}, u32[]{:S(2)}) collective-permute-start(bf16[128,128]{1,0:T(8,128)(2,1)S(1)} %get-tuple-element.64.refs_0_), channel_id=1, source_target_pairs={{0,15},{1,14},{2,13},{3,12},{4,11},{5,10},{6,9},{7,8},{8,7},{9,6},... | collective-permute-start | bytes 98312 | tf_op jit(solution)/shard_map/ppermute | solution.py:438
  40.2 4.8 %collective-permute-start.14 = (bf16[384,128]{1,0:T(8,128)(2,1)S(1)}, bf16[384,128]{1,0:T(8,128)(2,1)S(1)}, u32[]{:S(2)}, u32[]{:S(2)}) collective-permute-start(bf16[384,128]{1,0:T(8,128)(2,1)S(1)} %join.3.refs_0_), channel_id=1, source_target_pairs={{0,3},{1,4},{2,7},{3,0},{4,1},{5,6},{6,5},{7,2},{8,13},{9,10},{10,... | collective-permute-start | bytes 294920 | tf_op jit(solution)/shard_map/ppermute | solution.py:438
  46.4 1.4 %collective-permute-start.17 = (f32[256,128]{1,0:T(8,128)S(1)}, f32[256,128]{1,0:T(8,128)S(1)}, u32[]{:S(2)}, u32[]{:S(2)}) collective-permute-start(f32[256,128]{1,0:T(8,128)S(1)} %forward.11), channel_id=1, source_target_pairs={{0,1},{1,0},{2,3},{3,2},{4,5},{5,4},{6,7},{7,6},{8,9},{9,8},{10,11... | collective-permute-start | bytes 393224 | tf_op jit(solution)/shard_map/ppermute | solution.py:438
  47.8 1.3 %collective-permute-start.18 = (bf16[256,128]{1,0:T(8,128)(2,1)S(1)}, bf16[256,128]{1,0:T(8,128)(2,1)S(1)}, u32[]{:S(2)}, u32[]{:S(2)}) collective-permute-start(bf16[256,128]{1,0:T(8,128)(2,1)S(1)} %residual.3.refs_0_), channel_id=1, source_target_pairs={{0,1},{1,0},{2,3},{3,2},{4,5},{5,4},{6,7},{7,6},{8,9},{9,8},{10,11... | collective-permute-start | bytes 196616 | tf_op jit(solution)/shard_map/ppermute | solution.py:438
  50.3 3.8 %collective-permute-start.20 = (bf16[256,128]{1,0:T(8,128)(2,1)S(1)}, bf16[256,128]{1,0:T(8,128)(2,1)S(1)}, u32[]{:S(2)}, u32[]{:S(2)}) collective-permute-start(bf16[256,128]{1,0:T(8,128)(2,1)S(1)} %get-tuple-element.67), channel_id=1, source_target_pairs={{0,3},{1,4},{2,7},{3,0},{4,1},{5,6},{6,5},{7,2},{8,13},{9,10},{10,... | collective-permute-start | bytes 196616 | tf_op jit(solution)/shard_map/ppermute | solution.py:438
  50.4 5.9 %collective-permute-start.19 = (bf16[256,128]{1,0:T(8,128)(2,1)S(1)}, bf16[256,128]{1,0:T(8,128)(2,1)S(1)}, u32[]{:S(2)}, u32[]{:S(2)}) collective-permute-start(bf16[256,128]{1,0:T(8,128)(2,1)S(1)} %get-tuple-element.65), channel_id=1, source_target_pairs={{0,3},{1,4},{2,7},{3,0},{4,1},{5,6},{6,5},{7,2},{8,13},{9,10},{10,... | collective-permute-start | bytes 196616 | tf_op jit(solution)/shard_map/ppermute | solution.py:438
  54.1 4.4 %collective-permute-start.21 = (bf16[128,128]{1,0:T(8,128)(2,1)S(1)}, bf16[128,128]{1,0:T(8,128)(2,1)S(1)}, u32[]{:S(2)}, u32[]{:S(2)}) collective-permute-start(bf16[128,128]{1,0:T(8,128)(2,1)S(1)} %get-tuple-element.68), channel_id=1, source_target_pairs={{0,9},{1,2},{2,1},{3,10},{4,7},{5,12},{6,15},{7,4},{8,11},{9,0},{1... | collective-permute-start | bytes 98312 | tf_op jit(solution)/shard_map/ppermute | solution.py:438
  54.2 5.9 %collective-permute-start.22 = (bf16[128,128]{1,0:T(8,128)(2,1)S(1)}, bf16[128,128]{1,0:T(8,128)(2,1)S(1)}, u32[]{:S(2)}, u32[]{:S(2)}) collective-permute-start(bf16[128,128]{1,0:T(8,128)(2,1)S(1)} %get-tuple-element.69), channel_id=1, source_target_pairs={{0,12},{1,11},{2,8},{3,15},{4,14},{5,9},{6,10},{7,13},{8,2},{9,5},... | collective-permute-start | bytes 98312 | tf_op jit(solution)/shard_map/ppermute | solution.py:438
  56.3 4.5 %collective-permute-start.23 = (bf16[128,128]{1,0:T(8,128)(2,1)S(1)}, bf16[128,128]{1,0:T(8,128)(2,1)S(1)}, u32[]{:S(2)}, u32[]{:S(2)}) collective-permute-start(bf16[128,128]{1,0:T(8,128)(2,1)S(1)} %get-tuple-element.70), channel_id=1, source_target_pairs={{0,5},{1,8},{2,11},{3,6},{4,13},{5,0},{6,3},{7,14},{8,1},{9,12},{1... | collective-permute-start | bytes 98312 | tf_op jit(solution)/shard_map/ppermute | solution.py:438
